TPU v7x, 32 devices: a whole 2x2x4 slice. The times are simulated.
32 devices in a mesh: groups: 2 (over y), hid: 4 (over z), emb: 4 (over x, core).
Axes of the slice: x: 2, y: 2, z: 4, core: 2. Of those that a mesh axis runs over, the one named last changes fastest.
Arguments:
- inputs: float32 [256, 6144], P(('groups', 'hid'), 'emb'), parts along dimension 0, may hold values from -160 to 160
- out_grad: float32 [256, 6144], P(('groups', 'hid'), 'emb'), parts along dimension 0, may hold values from -6 to 6
- in_weight: float32 [6144, 24576], P('emb', 'hid'), may hold values from -0.078125 to 0.078125
- in_bias: float32 [24576], P('hid'), may hold values from -4 to 4
- out_weight: float32 [24576, 6144], P('hid', 'emb'), may hold values from -0.0390625 to 0.0390625
- norm_gain: float32 [6144], P('emb'), may hold values from 0.25 to 2.7
Outputs:
- input_grad: float32 [256, 6144], P(('groups', 'hid'), 'emb'), parts along dimension 0
There are 2 independent parts, one for each index of `groups`. A program takes and returns all parts, laid end to end along the dimension named above; an argument that names none is the same for every part. Nothing has to cross between parts.
All inputs are finite; a program needn't handle non-finite values.
Results may differ from a plain program's by a relative error of at most 0.00018.
Values sent between devices are 32-bit elements; how exact they have to be, the bound alone decides.
No kernel may reach another device: no remote copies, remote signals or barrier semaphores. Data moves between devices by JAX's collectives and lax.ppermute only.
A program may use at most 192 MiB of HBM per device.

v0:
```python
import math

import jax
import jax.numpy as jnp
from jax import lax
from jax.sharding import PartitionSpec as P

D = 6144


def gelu_slope(values):
    cdf = 0.5 * (1.0 + lax.erf(values * (1.0 / math.sqrt(2.0))))
    density = jnp.exp(-0.5 * values * values) * (1.0 / math.sqrt(2.0 * math.pi))
    return cdf + values * density


def times_transposed(left, right):
    return lax.dot_general(
        left,
        right,
        (((1,), (1,)), ((), ())),
        precision=lax.Precision.HIGHEST,
        preferred_element_type=jnp.float32,
    )


def body(inputs, out_grad, in_weight, in_bias, out_weight, norm_gain):
    highest = lax.Precision.HIGHEST
    hidden_local = in_weight.shape[1]
    row_total = lax.psum(jnp.sum(inputs, axis=-1), "emb")
    row_mean = (row_total / D)[:, None]
    centred = inputs - row_mean
    square_total = lax.psum(jnp.sum(centred * centred, axis=-1), "emb")
    variance = (square_total / D)[:, None]
    inv_std = 1.0 / jnp.sqrt(variance + 1e-06)
    normed = centred * inv_std
    scaled = normed * norm_gain
    stacked = jnp.stack([scaled, out_grad], axis=1)
    piece = lax.all_gather(stacked, "hid", axis=0, tiled=True)
    pre_part = jnp.dot(
        piece[:, 0], in_weight, precision=highest, preferred_element_type=jnp.float32
    )
    back_part = times_transposed(piece[:, 1], out_weight)
    partial_sums = jnp.concatenate([pre_part, back_part], axis=1)
    summed = lax.psum_scatter(partial_sums, "emb", scatter_dimension=0, tiled=True)
    act_grad = summed[:, hidden_local:] * gelu_slope(summed[:, :hidden_local] + in_bias)
    scaled_part = times_transposed(lax.all_gather(act_grad, "emb", axis=0, tiled=True), in_weight)
    scaled_grad = lax.psum_scatter(scaled_part, "hid", scatter_dimension=0, tiled=True)
    normed_grad = scaled_grad * norm_gain
    first_total, second_total = lax.psum(
        (jnp.sum(normed_grad, axis=-1), jnp.sum(normed_grad * normed, axis=-1)), "emb"
    )
    first = (first_total / D)[:, None]
    second = (second_total / D)[:, None]
    return inv_std * (normed_grad - first - normed * second)


def solution(mesh):
    return jax.shard_map(
        body,
        mesh=mesh,
        in_specs=(
            P(("groups", "hid"), "emb"),
            P(("groups", "hid"), "emb"),
            P("emb", "hid"),
            P("hid"),
            P("hid", "emb"),
            P("emb"),
        ),
        out_specs=P(("groups", "hid"), "emb"),
        check_vma=False,
    )
```

profile of v0, /device:TPU:0, one launch (start us, length us, event | category | flops | bytes accessed | tf_op | source)
XLA Modules:
  0.0 305.4 jit_solution(7876558549612361955)
XLA Ops:
  6.5 0.0 all-gather.3.cloned.1.call-start
  6.5 1.0 reduce_sum.36
  7.6 8.3 %psum.28 = f32[32]{0:T(128)S(1)} all-reduce(f32[32]{0:T(128)S(1)} %reduce_sum.36), channel_id=1, replica_groups=mesh['groups'=2,'hid'=4,'emb'=4] {'emb'}, use_global_device_ids=true, to_apply=%region_1.0 | all-reduce | flops 32 | bytes 256 | tf_op jit(solution)/shard_map/psum | solution.py:30
  15.9 1.1 multiply_reduce_fusion.1
  17.1 5.8 %psum.29 = f32[32]{0:T(128)S(1)} all-reduce(f32[32]{0:T(128)S(1)} %multiply_reduce_fusion.1), channel_id=1, replica_groups=mesh['groups'=2,'hid'=4,'emb'=4] {'emb'}, use_global_device_ids=true, to_apply=%region_3.0 | all-reduce | flops 32 | bytes 256 | tf_op jit(solution)/shard_map/psum | solution.py:33
  22.8 1.0 multiply_bitcast_fusion
  23.9 1.7 pad_maximum_fusion.1
  25.6 0.0 all-gather.3.cloned.1.call-update
  25.6 0.0 reduce-scatter.3.cloned.1.call-start
  25.6 37.6 %all-gather.3.cloned.1.call-done = f32[128,2,1536]{2,0,1:T(8,128)} async-done(((f32[32,2,1536]{2,0,1:T(8,128)}), f32[128,2,1536]{2,0,1:T(8,128)}) %all-gather.3.cloned.1.call-update) | async-done | bytes 1572880 | tf_op jit(solution)/shard_map/all_gather | solution.py:39
  63.3 42.3 %fusion.5 = f32[128,6144]{1,0:T(8,128)S(1)} fusion(f32[6144,1536]{1,0:T(8,128)} %param.10, f32[128,2,1536]{2,0,1:T(8,128)} %all-gather.3.cloned.1.call-done), kind=kOutput, calls=%fused_computation.9 | convolution fusion | flops 14495514624 | bytes 41680896 | tf_op jit(solution)/shard_map/dot_general | solution.py:18
  105.6 0.0 copy-done.1
  105.6 24.5 %fusion.6 = f32[128,6144]{1,0:T(8,128)S(1)} fusion(f32[1536,6144]{1,0:T(8,128)} %param.8, f32[128,2,1536]{2,0,1:T(8,128)S(1)} %copy-done.1), kind=kOutput, calls=%fused_computation.11 | convolution fusion | flops 14495514624 | bytes 41680896 | tf_op jit(solution)/shard_map/dot_general | solution.py:40
  130.1 3.1 %pad_maximum_fusion = f32[128,12288]{1,0:T(8,128)} fusion(f32[128,6144]{1,0:T(8,128)S(1)} %fusion.5, f32[128,6144]{1,0:T(8,128)S(1)} %fusion.6), kind=kLoop, calls=%fused_computation | loop fusion | flops 1572864 | bytes 12582912 | tf_op jit(solution)/shard_map/concatenate | solution.py:44
  133.2 0.0 reduce-scatter.3.cloned.1.call-update
  133.2 0.0 all-gather.5.cloned.1.call-start
  133.3 57.3 %reduce-scatter.3.cloned.1.call-done = f32[32,12288]{1,0:T(8,128)} async-done(((f32[128,12288]{1,0:T(8,128)}), f32[32,12288]{1,0:T(8,128)}) %reduce-scatter.3.cloned.1.call-update) | async-done | bytes 1572880 | tf_op jit(solution)/shard_map/reduce_scatter | solution.py:45
  190.6 0.0 copy-done.3
  190.6 2.6 fusion.4
  193.2 0.0 all-gather.5.cloned.1.call-update
  193.2 0.0 copy-start
  193.2 0.0 copy-start.2
  193.2 0.0 reduce-scatter.5.cloned.1.call-start
  193.3 28.6 %all-gather.5.cloned.1.call-done = f32[128,6144]{1,0:T(8,128)} async-done(((f32[32,6144]{1,0:T(8,128)}), f32[128,6144]{1,0:T(8,128)}) %all-gather.5.cloned.1.call-update) | async-done | bytes 3145744 | tf_op jit(solution)/shard_map/all_gather | solution.py:47
  221.9 44.9 %fusion.7 = f32[128,1536]{1,0:T(8,128)} fusion(f32[128,6144]{1,0:T(8,128)} %all-gather.5.cloned.1.call-done, f32[1536,6144]{1,0:T(8,128)} %param.8), kind=kOutput, calls=%fused_computation.23 | convolution fusion | flops 14495514624 | bytes 41680896 | tf_op jit(solution)/shard_map/dot_general | solution.py:18
  266.8 0.0 reduce-scatter.5.cloned.1.call-update
  266.9 23.5 %reduce-scatter.5.cloned.1.call-done = f32[32,1536]{1,0:T(8,128)} async-done(((f32[128,1536]{1,0:T(8,128)}), f32[32,1536]{1,0:T(8,128)}) %reduce-scatter.5.cloned.1.call-update) | async-done | bytes 196624 | tf_op jit(solution)/shard_map/reduce_scatter | solution.py:48
  290.3 0.0 copy-done
  290.3 0.0 copy-done.2
  290.3 1.1 multiply_reduce_fusion.2
  291.5 5.7 %all-reduce = (f32[32]{0:T(128)S(1)}, f32[32]{0:T(128)S(1)}) all-reduce(f32[32]{0:T(128)S(1)} %get-tuple-element.6, f32[32]{0:T(128)S(1)} %get-tuple-element.5), channel_id=1, replica_groups=mesh['groups'=2,'hid'=4,'emb'=4] {'emb'}, use_global_device_ids=true, to_apply=%region_9.0 | all-reduce | flops 64 | bytes 512 | tf_op jit(solution)/shard_map/psum | solution.py:50
  297.2 1.7 subtract_multiply_fusion
  (5 shorter events, 0.0 us)
Async XLA Ops:
  6.5 56.7 %all-gather.3.cloned.1.call-start = ((), (), s32[]{:S(2)}) async-start(), calls=%async_computation.2 | async-start | bytes 1966080 | tf_op jit(solution)/shard_map/all_gather | solution.py:39
  25.6 165.0 %reduce-scatter.3.cloned.1.call-start = ((), (), s32[]{:S(2)}) async-start(), calls=%async_computation.3 | async-start | bytes 7864320 | tf_op jit(solution)/shard_map/reduce_scatter | solution.py:45
  63.3 42.4 %copy-start.1 = (f32[128,2,1536]{2,0,1:T(8,128)S(1)}, f32[128,2,1536]{2,0,1:T(8,128)}, u32[]{:S(2)}) copy-start(f32[128,2,1536]{2,0,1:T(8,128)} %all-gather.3.cloned.1.call-done) | copy-start | bytes 4718596
  133.2 57.4 %copy-start.3 = (f32[6144]{0:T(1024)S(1)}, f32[6144]{0:T(1024)}, u32[]{:S(2)}) copy-start(f32[6144]{0:T(1024)} %param.9) | copy-start | bytes 73732
  133.2 88.7 %all-gather.5.cloned.1.call-start = ((), (), s32[]{:S(2)}) async-start(), calls=%async_computation.4 | async-start | bytes 3932160 | tf_op jit(solution)/shard_map/all_gather | solution.py:47
  193.2 97.1 %copy-start = (f32[32,1536]{1,0:T(8,128)S(1)}, f32[32,1536]{1,0:T(8,128)}, u32[]{:S(2)}) copy-start(f32[32,1536]{1,0:T(8,128)} %param.6) | copy-start | bytes 589828
  193.2 97.1 %copy-start.2 = (f32[1536]{0:T(1024)S(1)}, f32[1536]{0:T(1024)}, u32[]{:S(2)}) copy-start(f32[1536]{0:T(1024)} %param.11) | copy-start | bytes 18436
  193.2 97.1 %reduce-scatter.5.cloned.1.call-start = ((), (), s32[]{:S(2)}) async-start(), calls=%async_computation.5 | async-start | bytes 983040 | tf_op jit(solution)/shard_map/reduce_scatter | solution.py:48
Sparse Core Ops, SparseCore 0:
  25.7 37.5 all-gather.2
  133.4 57.1 reduce-scatter.2
  193.3 28.5 all-gather.4
  267.0 23.3 reduce-scatter.4
where the time goes:
time: 306 us; the launch traced here: 305 us
  waiting for transfers between devices  147 us (48%)
  matrix products  112 us (37%)
  blocking collectives  19.8 us (6%)
  other arithmetic  13.4 us (4%)
  between operations  13.2 us (4%)
    dot_general x2, matrix products, times_transposed(): lax.dot_general(left, right, (((1,), (1,)), ((), ())), precision=lax.Prec...  87.3 us
    reduce_scatter x1, waiting for transfers between devices, body(): lax.psum_scatter(partial_sums, 'emb', scatter_dimension=0, tiled=True)  57.3 us
    all_gather x1, waiting for transfers between devices, body(): piece = lax.all_gather(stacked, 'hid', axis=0, tiled=True)  37.6 us
    all_gather x1, waiting for transfers between devices, body(): lax.all_gather(act_grad, 'emb', axis=0, tiled=True)  28.6 us
    dot_general x1, matrix products, body(): jnp.dot(piece[:, 0], in_weight, precision=highest, preferred_element_type...  24.5 us
    reduce_scatter x1, waiting for transfers between devices, body(): lax.psum_scatter(scaled_part, 'hid', scatter_dimension=0, tiled=True)  23.5 us
    psum x1, blocking collectives, body(): row_total = lax.psum(jnp.sum(inputs, axis=-1), 'emb')  8.34 us
  transfers between devices with their start and end apart: 4, of which 4 were waited for; matrix products, arithmetic and copies ran while one was open for 0% of the time, Pallas kernels for 0%

commit v1 on v0

v1 whole, which is shorter than its diff:
```python
import functools
import math

import jax
import jax.numpy as jnp
from jax import lax
from jax.experimental import pallas as pl
from jax.experimental.pallas import tpu as pltpu
from jax.sharding import PartitionSpec as P

VMEM_LIMIT = 40 * 1024 * 1024
CHUNKS = 2


def gelu_slope(values):
    cdf = 0.5 * (1.0 + lax.erf(values * (1.0 / math.sqrt(2.0))))
    density = jnp.exp(-0.5 * values * values) * (1.0 / math.sqrt(2.0 * math.pi))
    return cdf + values * density


def split(values):
    high = values.astype(jnp.bfloat16)
    return high, (values - high.astype(jnp.float32)).astype(jnp.bfloat16)


def divisor(extent, *choices):
    return next(c for c in choices if extent % c == 0)


def three_pass(both, weight, dims):
    rows = both.shape[0] // 2
    high, low = split(weight)
    dot = functools.partial(
        lax.dot_general,
        dimension_numbers=((dims[:1], dims[1:]), ((), ())),
        preferred_element_type=jnp.float32,
    )
    first = dot(both, high)
    return first[:rows] + first[rows:] + dot(both[:rows], low)


def forward_kernel(slots, contract, place_ref, *refs):
    slot_refs, (weight_ref, send_ref, keep_ref, both) = refs[:slots], refs[slots:]
    block = slot_refs[0].shape[0]
    total = block * slots

    @pl.when(pl.program_id(0) == 0)
    def _():
        for b in range(slots):
            high, low = split(slot_refs[b][...])
            row = pl.multiple_of(place_ref[b] * block, block)
            both[pl.ds(row, block), :] = high
            both[pl.ds(total + row, block), :] = low

    result = three_pass(both[...], weight_ref[...], (1, contract))
    keep_ref[...] = result[: total // 2]
    send_ref[...] = result[total // 2 :]


def forward(blocks, weight, place, chunk, chunks, by_column):
    slots, (block, depth) = len(blocks), blocks[0].shape
    hidden = weight.shape[1 if by_column else 0] // chunks
    width = divisor(hidden, 512, 384, 256, 128)
    steps = hidden // width
    whole = pl.BlockSpec((block, depth), lambda i, place: (0, 0))
    if by_column:
        weight_spec = pl.BlockSpec((depth, width), lambda i, place: (0, chunk * steps + i))
    else:
        weight_spec = pl.BlockSpec((width, depth), lambda i, place: (chunk * steps + i, 0))
    half = block * slots // 2
    out = jax.ShapeDtypeStruct((half, hidden), jnp.float32)
    return pl.pallas_call(
        functools.partial(forward_kernel, slots, 0 if by_column else 1),
        out_shape=(out, out),
        grid_spec=pltpu.PrefetchScalarGridSpec(
            num_scalar_prefetch=1,
            grid=(steps,),
            in_specs=[whole] * slots + [weight_spec],
            out_specs=[pl.BlockSpec((half, width), lambda i, place: (0, i))] * 2,
            scratch_shapes=[pltpu.VMEM((2 * block * slots, depth), jnp.bfloat16)],
        ),
        compiler_params=pltpu.CompilerParams(vmem_limit_bytes=VMEM_LIMIT),
        cost_estimate=pl.CostEstimate(
            flops=6 * block * slots * depth * hidden,
            bytes_accessed=4 * depth * hidden + 8 * half * hidden,
            transcendentals=0,
        ),
    )(place, *blocks, weight)


def backward_kernel(slots, earlier, place_ref, *refs):
    act_refs, weight_ref = refs[:slots], refs[slots]
    earlier_refs = refs[slots + 1 : slots + 1 + earlier]
    out_refs = refs[slots + 1 + earlier : -2]
    both, result = refs[-2:]
    block = act_refs[0].shape[0]
    total = block * slots

    @pl.when(pl.program_id(0) == 0)
    def _():
        for p in range(slots):
            high, low = split(act_refs[p][...])
            both[p * block : (p + 1) * block, :] = high
            both[total + p * block : total + (p + 1) * block, :] = low

    result[...] = three_pass(both[...], weight_ref[...], (1, 1))
    for b in range(slots):
        row = pl.multiple_of(place_ref[b] * block, block)
        rows = result[pl.ds(row, block), :]
        out_refs[b][...] = rows + earlier_refs[b][...] if earlier else rows


def backward(acts, weight, place, earlier, chunk):
    slots, (block, hidden) = len(acts), acts[0].shape
    depth = weight.shape[0]
    width = divisor(depth, 256, 128)
    tile = pl.BlockSpec((block, width), lambda i, place: (0, i))
    out = jax.ShapeDtypeStruct((block, depth), jnp.float32)
    return pl.pallas_call(
        functools.partial(backward_kernel, slots, len(earlier)),
        out_shape=[out] * slots,
        grid_spec=pltpu.PrefetchScalarGridSpec(
            num_scalar_prefetch=1,
            grid=(depth // width,),
            in_specs=[pl.BlockSpec((block, hidden), lambda i, place: (0, 0))] * slots
            + [pl.BlockSpec((width, hidden), lambda i, place: (i, chunk))]
            + [tile] * len(earlier),
            out_specs=[tile] * slots,
            scratch_shapes=[
                pltpu.VMEM((2 * block * slots, hidden), jnp.bfloat16),
                pltpu.VMEM((block * slots, width), jnp.float32),
            ],
        ),
        compiler_params=pltpu.CompilerParams(vmem_limit_bytes=VMEM_LIMIT),
        cost_estimate=pl.CostEstimate(
            flops=6 * block * slots * depth * hidden,
            bytes_accessed=4 * depth * hidden + 8 * block * slots * depth,
            transcendentals=0,
        ),
    )(place, *acts, weight, *earlier)


def body(hid_size, emb_size, inputs, out_grad, in_weight, in_bias, out_weight, norm_gain):
    chips = emb_size // 2
    tokens, depth = inputs.shape
    model_width = depth * emb_size
    hidden = in_weight.shape[1]
    me = lax.axis_index("emb")
    chip, core = me // 2, me % 2

    def along_hid(values):
        return lax.ppermute(values, "hid", [(i, (i + 1) % hid_size) for i in range(hid_size)])

    def other_core(values):
        return lax.ppermute(values, "emb", [(i, i ^ 1) for i in range(emb_size)])

    def next_chip(values):
        return lax.ppermute(values, "emb", [(i, (i + 2) % emb_size) for i in range(emb_size)])

    owner = jnp.arange(emb_size, dtype=jnp.int32)
    place = ((owner % 2) ^ core) * chips + (owner // 2 - chip) % chips

    def gathered(values):
        blocks = [values]
        for _ in range(hid_size - 1):
            blocks.append(along_hid(blocks[-1]))
        return blocks

    grads = gathered(out_grad)

    local_mean = jnp.mean(inputs, axis=-1, keepdims=True)
    local_square = jnp.sum(jnp.square(inputs - local_mean), axis=-1)
    stats = lax.all_gather(jnp.stack([local_mean[:, 0], local_square]), "emb")
    row_mean = jnp.mean(stats[:, 0], axis=0)
    spread = jnp.sum(stats[:, 1] + depth * jnp.square(stats[:, 0] - row_mean), axis=0)
    inv_std = (1.0 / jnp.sqrt(spread / model_width + 1e-06))[:, None]
    normed = (inputs - row_mean[:, None]) * inv_std
    scaled = gathered(normed * norm_gain)

    def reduced(partial):
        send, keep = partial
        summed = keep + other_core(send)
        terms = [summed[d * tokens : (d + 1) * tokens] for d in range(chips)]
        running = terms[chips - 1]
        for step in range(1, chips):
            running = next_chip(running) + terms[chips - 1 - step]
        return running

    back_parts = [forward(grads, out_weight, place, c, CHUNKS, False) for c in range(CHUNKS)]
    backs = [reduced(part) for part in back_parts]
    pre_parts = [forward(scaled, in_weight, place, c, CHUNKS, True) for c in range(CHUNKS)]
    pres = [reduced(part) for part in pre_parts]

    sums = ()
    for c in range(CHUNKS):
        piece = hidden // CHUNKS
        act = backs[c] * gelu_slope(pres[c] + in_bias[c * piece : (c + 1) * piece])
        mine = [None] * chips
        mine[0] = act
        for step in range(1, chips):
            act = next_chip(act)
            mine[(chips - step) % chips] = act
        theirs = [other_core(block) for block in mine]
        sums = backward(mine + theirs, in_weight, place, sums, c)

    running = sums[1 % hid_size]
    for step in range(1, hid_size):
        running = along_hid(running) + sums[(step + 1) % hid_size]
    normed_grad = running * norm_gain
    totals = lax.psum(
        jnp.stack([jnp.sum(normed_grad, axis=-1), jnp.sum(normed_grad * normed, axis=-1)]), "emb"
    )
    first, second = (totals / model_width)[:, :, None]
    return inv_std * (normed_grad - first - normed * second)


def solution(mesh):
    hid_size, emb_size = mesh.shape["hid"], mesh.shape["emb"]
    assert hid_size == emb_size and emb_size % 2 == 0
    return jax.shard_map(
        functools.partial(body, hid_size, emb_size),
        mesh=mesh,
        in_specs=(
            P(("groups", "hid"), "emb"),
            P(("groups", "hid"), "emb"),
            P("emb", "hid"),
            P("hid"),
            P("hid", "emb"),
            P("emb"),
        ),
        out_specs=P(("groups", "hid"), "emb"),
        check_vma=False,
    )
```

time: 306 us -> 189 us (0.62)
  matrix products: 112 us -> 0 us
  Pallas kernels: 0 us -> 65.1 us
  waiting for transfers between devices: 147 us -> 91.6 us
  starting transfers between devices: 0.13 us -> 14.2 us
  between operations: 13.2 us -> 0.23 us
  blocking collectives: 19.8 us -> 11.6 us
  other arithmetic: 13.4 us -> 5.31 us
    dot_general x3 -> x0, matrix products: 112 us -> none  [the longest x2 87.3 us: times_transposed(): lax.dot_general(left, right, (((1,), (1,)), ((), ())), precision=lax.Prec...]
    ppermute x0 -> x23, waiting for transfers between devices: none -> 91.6 us  [the longest x9 47.7 us: along_hid(): lax.ppermute(values, 'hid', [(i, (i + 1) % hid_size) for i in range(hid_s...]
    reduce_scatter x2 -> x0, waiting for transfers between devices: 80.8 us -> none  [the longest x1 57.3 us: body(): lax.psum_scatter(partial_sums, 'emb', scatter_dimension=0, tiled=True)]
    all_gather x2 -> x0, waiting for transfers between devices: 66.3 us -> none  [the longest x1 37.6 us: body(): piece = lax.all_gather(stacked, 'hid', axis=0, tiled=True)]
    pallas_call x0 -> x6, Pallas kernels: none -> 65.1 us  [the longest x4 42.9 us: forward(): pl.pallas_call(functools.partial(forward_kernel, slots, 0 if by_column el...]
    ppermute x0 -> x23, starting transfers between devices: none -> 14.2 us  [the longest x6 7.85 us: next_chip(): lax.ppermute(values, 'emb', [(i, (i + 2) % emb_size) for i in range(emb_s...]
    psum x3 -> x1, blocking collectives: 19.8 us -> 5.66 us  [body(): lax.psum(jnp.stack([jnp.sum(normed_grad, axis=-1), jnp.sum(normed_grad *...]
    all_gather x0 -> x1, blocking collectives: none -> 5.98 us  [body(): stats = lax.all_gather(jnp.stack([local_mean[:, 0], local_square]), 'emb')]
  transfers between devices with their start and end apart: 4 -> 23, of which waited for: 4 -> 14; matrix products, arithmetic and copies ran while one was open for 0% -> 1% of each run, Pallas kernels for 0% -> 29%
where the time goes in v1:
time: 189 us; the launch traced here: 188 us
  waiting for transfers between devices  91.6 us (48%)
  Pallas kernels  65.1 us (34%)
  starting transfers between devices  14.2 us (8%)
  blocking collectives  11.6 us (6%)
  other arithmetic  5.31 us (3%)
    ppermute x9, waiting for transfers between devices, along_hid(): lax.ppermute(values, 'hid', [(i, (i + 1) % hid_size) for i in range(hid_s...  47.7 us
    ppermute x6, waiting for transfers between devices, next_chip(): lax.ppermute(values, 'emb', [(i, (i + 2) % emb_size) for i in range(emb_s...  43.9 us
    pallas_call x4, Pallas kernels, forward(): pl.pallas_call(functools.partial(forward_kernel, slots, 0 if by_column el...  42.9 us
    pallas_call x2, Pallas kernels, backward(): pl.pallas_call(functools.partial(backward_kernel, slots, len(earlier)), o...  22.2 us
    ppermute x6, starting transfers between devices, next_chip(): lax.ppermute(values, 'emb', [(i, (i + 2) % emb_size) for i in range(emb_s...  7.85 us
    all_gather x1, blocking collectives, body(): stats = lax.all_gather(jnp.stack([local_mean[:, 0], local_square]), 'emb')  5.98 us
    psum x1, blocking collectives, body(): lax.psum(jnp.stack([jnp.sum(normed_grad, axis=-1), jnp.sum(normed_grad *...  5.66 us
    ppermute x9, starting transfers between devices, along_hid(): lax.ppermute(values, 'hid', [(i, (i + 1) % hid_size) for i in range(hid_s...  4.57 us
  transfers between devices with their start and end apart: 23, of which 14 were waited for; matrix products, arithmetic and copies ran while one was open for 1% of the time, Pallas kernels for 29%

profile of v1, /device:TPU:0, one launch (start us, length us, event | category | flops | bytes accessed | tf_op | source)
XLA Modules:
  0.0 188.2 jit_solution(15766285245281846414)
XLA Ops:
  0.0 1.1 reduce_sum.54
  1.1 1.1 multiply_reduce_fusion.1
  2.2 6.0 %all-gather.1 = f32[4,2,32]{2,1,0:T(2,128)S(1)} all-gather(f32[1,2,32]{2,1,0:T(2,128)S(1)} %maximum_bitcast_fusion), channel_id=2, replica_groups=mesh['groups'=2,'hid'=4,'emb'=4] {'emb'}, dimensions={0}, use_global_device_ids=true | all-gather | bytes 1280 | tf_op jit(solution)/shard_map/all_gather | solution.py:173
  8.3 1.0 fusion.12.refs_0_
  9.3 2.2 %collective-permute-start.5 = (f32[32,1536]{1,0:T(8,128)S(1)}, f32[32,1536]{1,0:T(8,128)S(1)}, u32[]{:S(2)}, u32[]{:S(2)}) collective-permute-start(f32[32,1536]{1,0:T(8,128)S(1)} %fusion.12.refs_0_), channel_id=1, source_target_pairs={{0,4},{4,8},{8,12},{12,0},{1,5},{5,9},{9,13},{13,1},{2,6},{6,10},{... | collective-permute-start | bytes 589832 | tf_op jit(solution)/shard_map/ppermute | solution.py:152
  11.5 1.6 collective-permute-start
  13.1 6.1 %collective-permute-done.5.refs_1_ = f32[32,1536]{1,0:T(8,128)S(1)} collective-permute-done((f32[32,1536]{1,0:T(8,128)S(1)}, f32[32,1536]{1,0:T(8,128)S(1)}, u32[]{:S(2)}, u32[]{:S(2)}) %collective-permute-start.5) | collective-permute-done | bytes 196640 | tf_op jit(solution)/shard_map/ppermute | solution.py:152
  19.2 3.9 %collective-permute-done.refs_1_ = f32[32,1536]{1,0:T(8,128)S(1)} collective-permute-done((f32[32,1536]{1,0:T(8,128)}, f32[32,1536]{1,0:T(8,128)S(1)}, u32[]{:S(2)}, u32[]{:S(2)}) %collective-permute-start) | collective-permute-done | bytes 196640 | tf_op jit(solution)/shard_map/ppermute | solution.py:152
  23.4 3.9 %collective-permute-done.6.refs_2_ = f32[32,1536]{1,0:T(8,128)S(1)} collective-permute-done((f32[32,1536]{1,0:T(8,128)S(1)}, f32[32,1536]{1,0:T(8,128)S(1)}, u32[]{:S(2)}, u32[]{:S(2)}) %collective-permute-start.6) | collective-permute-done | bytes 196640 | tf_op jit(solution)/shard_map/ppermute | solution.py:152
  27.6 5.0 %collective-permute-done.1.refs_2_ = f32[32,1536]{1,0:T(8,128)S(1)} collective-permute-done((f32[32,1536]{1,0:T(8,128)S(1)}, f32[32,1536]{1,0:T(8,128)S(1)}, u32[]{:S(2)}, u32[]{:S(2)}) %collective-permute-start.1) | collective-permute-done | bytes 196640 | tf_op jit(solution)/shard_map/ppermute | solution.py:152
  32.7 3.9 %collective-permute-done.7.refs_3_ = f32[32,1536]{1,0:T(8,128)S(1)} collective-permute-done((f32[32,1536]{1,0:T(8,128)S(1)}, f32[32,1536]{1,0:T(8,128)S(1)}, u32[]{:S(2)}, u32[]{:S(2)}) %collective-permute-start.7) | collective-permute-done | bytes 196640 | tf_op jit(solution)/shard_map/ppermute | solution.py:152
  36.6 10.3 %shard_map.67 = (f32[64,3072]{1,0:T(8,128)S(1)}, f32[64,3072]{1,0:T(8,128)S(1)}) custom-call(s32[4]{0:T(128)S(1)} %fusion.13.place_ref, f32[32,1536]{1,0:T(8,128)S(1)} %fusion.12.refs_0_, f32[32,1536]{1,0:T(8,128)S(1)} %collective-permute-done.5.refs_1_, f32[32,1536]{1,0:T(8,128)S(1)} %collective-permute-done.6.refs_2_, ...), custom_call_target="tpu_custom_call" | custom-call | flops 3623878656 | bytes 20447232 | tf_op jit(solution)/shard_map/pallas_call | solution.py:72
  47.0 11.1 %shard_map.66 = (f32[64,3072]{1,0:T(8,128)S(1)}, f32[64,3072]{1,0:T(8,128)S(1)}) custom-call(s32[4]{0:T(128)S(1)} %fusion.13.place_ref, f32[32,1536]{1,0:T(8,128)S(1)} %copy-done, f32[32,1536]{1,0:T(8,128)S(1)} %collective-permute-done.refs_1_, f32[32,1536]{1,0:T(8,128)S(1)} %collective-permute-done.1.refs_2_, ...), custom_call_target="tpu_custom_call" | custom-call | flops 3623878656 | bytes 20447232 | tf_op jit(solution)/shard_map/pallas_call | solution.py:72
  58.6 10.3 %shard_map.65 = (f32[64,3072]{1,0:T(8,128)S(1)}, f32[64,3072]{1,0:T(8,128)S(1)}) custom-call(s32[4]{0:T(128)S(1)} %fusion.13.place_ref, f32[32,1536]{1,0:T(8,128)S(1)} %fusion.12.refs_0_, f32[32,1536]{1,0:T(8,128)S(1)} %collective-permute-done.5.refs_1_, f32[32,1536]{1,0:T(8,128)S(1)} %collective-permute-done.6.refs_2_, ...), custom_call_target="tpu_custom_call" | custom-call | flops 3623878656 | bytes 20447232 | tf_op jit(solution)/shard_map/pallas_call | solution.py:72
  69.1 11.1 %shard_map.64 = (f32[64,3072]{1,0:T(8,128)S(1)}, f32[64,3072]{1,0:T(8,128)S(1)}) custom-call(s32[4]{0:T(128)S(1)} %fusion.13.place_ref, f32[32,1536]{1,0:T(8,128)S(1)} %copy-done, f32[32,1536]{1,0:T(8,128)S(1)} %collective-permute-done.refs_1_, f32[32,1536]{1,0:T(8,128)S(1)} %collective-permute-done.1.refs_2_, ...), custom_call_target="tpu_custom_call" | custom-call | flops 3623878656 | bytes 20447232 | tf_op jit(solution)/shard_map/pallas_call | solution.py:72
  80.9 1.8 collective-permute-start.16
  83.4 1.8 collective-permute-start.9
  85.7 7.2 %collective-permute-done.16 = f32[32,3072]{1,0:T(8,128)S(1)} collective-permute-done((f32[32,3072]{1,0:T(8,128)S(1)}, f32[32,3072]{1,0:T(8,128)S(1)}, u32[]{:S(2)}, u32[]{:S(2)}) %collective-permute-start.16) | collective-permute-done | bytes 393248 | tf_op jit(solution)/shard_map/ppermute | solution.py:158
  92.9 8.4 %collective-permute-done.14 = f32[32,3072]{1,0:T(8,128)S(1)} collective-permute-done((f32[32,3072]{1,0:T(8,128)S(1)}, f32[32,3072]{1,0:T(8,128)S(1)}, u32[]{:S(2)}, u32[]{:S(2)}) %collective-permute-start.14) | collective-permute-done | bytes 393248 | tf_op jit(solution)/shard_map/ppermute | solution.py:158
  101.6 1.8 collective-permute-start.17
  103.4 6.4 %collective-permute-done.9 = f32[32,3072]{1,0:T(8,128)S(1)} collective-permute-done((f32[32,3072]{1,0:T(8,128)S(1)}, f32[32,3072]{1,0:T(8,128)S(1)}, u32[]{:S(2)}, u32[]{:S(2)}) %collective-permute-start.9) | collective-permute-done | bytes 393248 | tf_op jit(solution)/shard_map/ppermute | solution.py:158
  109.8 8.4 %collective-permute-done.4 = f32[32,3072]{1,0:T(8,128)S(1)} collective-permute-done((f32[32,3072]{1,0:T(8,128)S(1)}, f32[32,3072]{1,0:T(8,128)S(1)}, u32[]{:S(2)}, u32[]{:S(2)}) %collective-permute-start.4) | collective-permute-done | bytes 393248 | tf_op jit(solution)/shard_map/ppermute | solution.py:158
  118.5 1.8 collective-permute-start.10
  120.2 6.4 %collective-permute-done.17.refs_1_ = f32[32,3072]{1,0:T(8,128)S(1)} collective-permute-done((f32[32,3072]{1,0:T(8,128)S(1)}, f32[32,3072]{1,0:T(8,128)S(1)}, u32[]{:S(2)}, u32[]{:S(2)}) %collective-permute-start.17) | collective-permute-done | bytes 393248 | tf_op jit(solution)/shard_map/ppermute | solution.py:158
  127.2 7.0 %collective-permute-done.10.refs_1_ = f32[32,3072]{1,0:T(8,128)S(1)} collective-permute-done((f32[32,3072]{1,0:T(8,128)S(1)}, f32[32,3072]{1,0:T(8,128)S(1)}, u32[]{:S(2)}, u32[]{:S(2)}) %collective-permute-start.10) | collective-permute-done | bytes 393248 | tf_op jit(solution)/shard_map/ppermute | solution.py:158
  134.2 11.1 %shard_map.68 = (f32[32,1536]{1,0:T(8,128)S(1)}, f32[32,1536]{1,0:T(8,128)S(1)}, f32[32,1536]{1,0:T(8,128)S(1)}, f32[32,1536]{1,0:T(8,128)S(1)}) custom-call(s32[4]{0:T(128)S(1)} %fusion.13.place_ref, f32[32,3072]{1,0:T(8,128)S(1)} %fusion.9.refs_0_, f32[32,3072]{1,0:T(8,128)S(1)} %collective-permute-done.17.refs_1_, ...), custom_call_target="tpu_custom_call" | custom-call | flops 3623878656 | bytes 20447232 | tf_op jit(solution)/shard_map/pallas_call | solution.py:119
  145.3 11.2 %shard_map.69 = (f32[32,1536]{1,0:T(8,128)S(1)}, f32[32,1536]{1,0:T(8,128)S(1)}, f32[32,1536]{1,0:T(8,128)S(1)}, f32[32,1536]{1,0:T(8,128)S(1)}) custom-call(s32[4]{0:T(128)S(1)} %fusion.13.place_ref, f32[32,3072]{1,0:T(8,128)S(1)} %fusion.4.refs_0_, f32[32,3072]{1,0:T(8,128)S(1)} %collective-permute-done.10.refs_1_, ...), custom_call_target="tpu_custom_call" | custom-call | flops 3623878656 | bytes 20447232 | tf_op jit(solution)/shard_map/pallas_call | solution.py:119
  156.5 9.1 %collective-permute-done.20 = f32[32,1536]{1,0:T(8,128)S(1)} collective-permute-done((f32[32,1536]{1,0:T(8,128)S(1)}, f32[32,1536]{1,0:T(8,128)S(1)}, u32[]{:S(2)}, u32[]{:S(2)}) %collective-permute-start.20) | collective-permute-done | bytes 196640 | tf_op jit(solution)/shard_map/ppermute | solution.py:152
  165.7 8.3 %collective-permute-done.21 = f32[32,1536]{1,0:T(8,128)S(1)} collective-permute-done((f32[32,1536]{1,0:T(8,128)S(1)}, f32[32,1536]{1,0:T(8,128)S(1)}, u32[]{:S(2)}, u32[]{:S(2)}) %collective-permute-start.21) | collective-permute-done | bytes 196640 | tf_op jit(solution)/shard_map/ppermute | solution.py:152
  174.1 7.5 %collective-permute-done.22 = f32[32,1536]{1,0:T(8,128)S(1)} collective-permute-done((f32[32,1536]{1,0:T(8,128)S(1)}, f32[32,1536]{1,0:T(8,128)S(1)}, u32[]{:S(2)}, u32[]{:S(2)}) %collective-permute-start.22) | collective-permute-done | bytes 196640 | tf_op jit(solution)/shard_map/ppermute | solution.py:152
  181.8 5.7 %psum.7 = f32[2,32]{1,0:T(2,128)S(1)} all-reduce(f32[2,32]{1,0:T(2,128)S(1)} %pad_maximum_fusion), channel_id=1, replica_groups=mesh['groups'=2,'hid'=4,'emb'=4] {'emb'}, use_global_device_ids=true, to_apply=%region_6.7 | all-reduce | flops 64 | bytes 512 | tf_op jit(solution)/shard_map/psum | solution.py:210
  187.4 0.8 subtract_multiply_fusion
  (58 shorter events, 4.8 us)
Async XLA Ops:
  0.0 47.0 %copy-start = (f32[32,1536]{1,0:T(8,128)S(1)}, f32[32,1536]{1,0:T(8,128)}, u32[]{:S(2)}) copy-start(f32[32,1536]{1,0:T(8,128)} %refs_0_.3) | copy-start | bytes 589828
  9.3 9.9 %collective-permute-start.5 = (f32[32,1536]{1,0:T(8,128)S(1)}, f32[32,1536]{1,0:T(8,128)S(1)}, u32[]{:S(2)}, u32[]{:S(2)}) collective-permute-start(f32[32,1536]{1,0:T(8,128)S(1)} %fusion.12.refs_0_), channel_id=1, source_target_pairs={{0,4},{4,8},{8,12},{12,0},{1,5},{5,9},{9,13},{13,1},{2,6},{6,10},{... | collective-permute-start | bytes 589832 | tf_op jit(solution)/shard_map/ppermute | solution.py:152
  11.5 11.6 %collective-permute-start = (f32[32,1536]{1,0:T(8,128)}, f32[32,1536]{1,0:T(8,128)S(1)}, u32[]{:S(2)}, u32[]{:S(2)}) collective-permute-start(f32[32,1536]{1,0:T(8,128)} %refs_0_.3), channel_id=1, source_target_pairs={{0,4},{4,8},{8,12},{12,0},{1,5},{5,9},{9,13},{13,1},{2,6},{6,10},{... | collective-permute-start | bytes 589832 | tf_op jit(solution)/shard_map/ppermute | solution.py:152
  19.2 8.2 %collective-permute-start.6 = (f32[32,1536]{1,0:T(8,128)S(1)}, f32[32,1536]{1,0:T(8,128)S(1)}, u32[]{:S(2)}, u32[]{:S(2)}) collective-permute-start(f32[32,1536]{1,0:T(8,128)S(1)} %collective-permute-done.5.refs_1_), channel_id=1, source_target_pairs={{0,4},{4,8},{8,12},{12,0},{1,5},{5,9},{9,13},{13,1},{2,6},{6,10},{... | collective-permute-start | bytes 589832 | tf_op jit(solution)/shard_map/ppermute | solution.py:152
  23.1 9.6 %collective-permute-start.1 = (f32[32,1536]{1,0:T(8,128)S(1)}, f32[32,1536]{1,0:T(8,128)S(1)}, u32[]{:S(2)}, u32[]{:S(2)}) collective-permute-start(f32[32,1536]{1,0:T(8,128)S(1)} %collective-permute-done.refs_1_), channel_id=1, source_target_pairs={{0,4},{4,8},{8,12},{12,0},{1,5},{5,9},{9,13},{13,1},{2,6},{6,10},{... | collective-permute-start | bytes 589832 | tf_op jit(solution)/shard_map/ppermute | solution.py:152
  27.3 9.2 %collective-permute-start.7 = (f32[32,1536]{1,0:T(8,128)S(1)}, f32[32,1536]{1,0:T(8,128)S(1)}, u32[]{:S(2)}, u32[]{:S(2)}) collective-permute-start(f32[32,1536]{1,0:T(8,128)S(1)} %collective-permute-done.6.refs_2_), channel_id=1, source_target_pairs={{0,4},{4,8},{8,12},{12,0},{1,5},{5,9},{9,13},{13,1},{2,6},{6,10},{... | collective-permute-start | bytes 589832 | tf_op jit(solution)/shard_map/ppermute | solution.py:152
  32.7 14.3 %collective-permute-start.2 = (f32[32,1536]{1,0:T(8,128)S(1)}, f32[32,1536]{1,0:T(8,128)S(1)}, u32[]{:S(2)}, u32[]{:S(2)}) collective-permute-start(f32[32,1536]{1,0:T(8,128)S(1)} %collective-permute-done.1.refs_2_), channel_id=1, source_target_pairs={{0,4},{4,8},{8,12},{12,0},{1,5},{5,9},{9,13},{13,1},{2,6},{6,10},{... | collective-permute-start | bytes 589832 | tf_op jit(solution)/shard_map/ppermute | solution.py:152
  46.9 33.8 %collective-permute-start.15 = (f32[64,3072]{1,0:T(8,128)S(1)}, f32[64,3072]{1,0:T(8,128)S(1)}, u32[]{:S(2)}, u32[]{:S(2)}) collective-permute-start(f32[64,3072]{1,0:T(8,128)S(1)} %get-tuple-element.28), channel_id=1, source_target_pairs={{0,1},{1,0},{2,3},{3,2},{4,5},{5,4},{6,7},{7,6},{8,9},{9,8},{10,11... | collective-permute-start | bytes 2359304 | tf_op jit(solution)/shard_map/ppermute | solution.py:155
  58.1 25.1 %copy-start.3 = (f32[6144]{0:T(1024)S(1)}, f32[6144]{0:T(1024)}, u32[]{:S(2)}) copy-start(f32[6144]{0:T(1024)} %param.9) | copy-start | bytes 73732
  58.1 24.6 %collective-permute-start.13 = (f32[64,3072]{1,0:T(8,128)S(1)}, f32[64,3072]{1,0:T(8,128)S(1)}, u32[]{:S(2)}, u32[]{:S(2)}) collective-permute-start(f32[64,3072]{1,0:T(8,128)S(1)} %get-tuple-element.26), channel_id=1, source_target_pairs={{0,1},{1,0},{2,3},{3,2},{4,5},{5,4},{6,7},{7,6},{8,9},{9,8},{10,11... | collective-permute-start | bytes 2359304 | tf_op jit(solution)/shard_map/ppermute | solution.py:155
  69.0 14.2 %collective-permute-start.8 = (f32[64,3072]{1,0:T(8,128)S(1)}, f32[64,3072]{1,0:T(8,128)S(1)}, u32[]{:S(2)}, u32[]{:S(2)}) collective-permute-start(f32[64,3072]{1,0:T(8,128)S(1)} %get-tuple-element.24), channel_id=1, source_target_pairs={{0,1},{1,0},{2,3},{3,2},{4,5},{5,4},{6,7},{7,6},{8,9},{9,8},{10,11... | collective-permute-start | bytes 2359304 | tf_op jit(solution)/shard_map/ppermute | solution.py:155
  80.2 5.0 %collective-permute-start.3 = (f32[64,3072]{1,0:T(8,128)S(1)}, f32[64,3072]{1,0:T(8,128)S(1)}, u32[]{:S(2)}, u32[]{:S(2)}) collective-permute-start(f32[64,3072]{1,0:T(8,128)S(1)} %get-tuple-element.22), channel_id=1, source_target_pairs={{0,1},{1,0},{2,3},{3,2},{4,5},{5,4},{6,7},{7,6},{8,9},{9,8},{10,11... | collective-permute-start | bytes 2359304 | tf_op jit(solution)/shard_map/ppermute | solution.py:155
  80.9 12.0 %collective-permute-start.16 = (f32[32,3072]{1,0:T(8,128)S(1)}, f32[32,3072]{1,0:T(8,128)S(1)}, u32[]{:S(2)}, u32[]{:S(2)}) collective-permute-start(f32[32,3072]{1,0:T(8,128)S(1)} %slice.59), channel_id=1, source_target_pairs={{0,2},{1,3},{2,0},{3,1},{4,6},{5,7},{6,4},{7,5},{8,10},{9,11},{10,... | collective-permute-start | bytes 1179656 | tf_op jit(solution)/shard_map/ppermute | solution.py:158
  82.8 18.5 %collective-permute-start.14 = (f32[32,3072]{1,0:T(8,128)S(1)}, f32[32,3072]{1,0:T(8,128)S(1)}, u32[]{:S(2)}, u32[]{:S(2)}) collective-permute-start(f32[32,3072]{1,0:T(8,128)S(1)} %slice.57), channel_id=1, source_target_pairs={{0,2},{1,3},{2,0},{3,1},{4,6},{5,7},{6,4},{7,5},{8,10},{9,11},{10,... | collective-permute-start | bytes 1179656 | tf_op jit(solution)/shard_map/ppermute | solution.py:158
  83.4 26.4 %collective-permute-start.9 = (f32[32,3072]{1,0:T(8,128)S(1)}, f32[32,3072]{1,0:T(8,128)S(1)}, u32[]{:S(2)}, u32[]{:S(2)}) collective-permute-start(f32[32,3072]{1,0:T(8,128)S(1)} %slice.55), channel_id=1, source_target_pairs={{0,2},{1,3},{2,0},{3,1},{4,6},{5,7},{6,4},{7,5},{8,10},{9,11},{10,... | collective-permute-start | bytes 1179656 | tf_op jit(solution)/shard_map/ppermute | solution.py:158
  85.3 32.9 %collective-permute-start.4 = (f32[32,3072]{1,0:T(8,128)S(1)}, f32[32,3072]{1,0:T(8,128)S(1)}, u32[]{:S(2)}, u32[]{:S(2)}) collective-permute-start(f32[32,3072]{1,0:T(8,128)S(1)} %slice.53), channel_id=1, source_target_pairs={{0,2},{1,3},{2,0},{3,1},{4,6},{5,7},{6,4},{7,5},{8,10},{9,11},{10,... | collective-permute-start | bytes 1179656 | tf_op jit(solution)/shard_map/ppermute | solution.py:158
  101.6 25.1 %collective-permute-start.17 = (f32[32,3072]{1,0:T(8,128)S(1)}, f32[32,3072]{1,0:T(8,128)S(1)}, u32[]{:S(2)}, u32[]{:S(2)}) collective-permute-start(f32[32,3072]{1,0:T(8,128)S(1)} %fusion.9.refs_0_), channel_id=1, source_target_pairs={{0,2},{1,3},{2,0},{3,1},{4,6},{5,7},{6,4},{7,5},{8,10},{9,11},{10,... | collective-permute-start | bytes 1179656 | tf_op jit(solution)/shard_map/ppermute | solution.py:158
  118.4 63.1 %copy-start.1 = (f32[32,1536]{1,0:T(8,128)S(1)}, f32[32,1536]{1,0:T(8,128)}, u32[]{:S(2)}) copy-start(f32[32,1536]{1,0:T(8,128)} %param.6) | copy-start | bytes 589828
  118.5 63.1 %copy-start.2 = (f32[1536]{0:T(1024)S(1)}, f32[1536]{0:T(1024)}, u32[]{:S(2)}) copy-start(f32[1536]{0:T(1024)} %param.11) | copy-start | bytes 18436
  118.5 15.7 %collective-permute-start.10 = (f32[32,3072]{1,0:T(8,128)S(1)}, f32[32,3072]{1,0:T(8,128)S(1)}, u32[]{:S(2)}, u32[]{:S(2)}) collective-permute-start(f32[32,3072]{1,0:T(8,128)S(1)} %fusion.4.refs_0_), channel_id=1, source_target_pairs={{0,2},{1,3},{2,0},{3,1},{4,6},{5,7},{6,4},{7,5},{8,10},{9,11},{10,... | collective-permute-start | bytes 1179656 | tf_op jit(solution)/shard_map/ppermute | solution.py:158
  120.2 13.9 %collective-permute-start.18 = (f32[32,3072]{1,0:T(8,128)S(1)}, f32[32,3072]{1,0:T(8,128)S(1)}, u32[]{:S(2)}, u32[]{:S(2)}) collective-permute-start(f32[32,3072]{1,0:T(8,128)S(1)} %fusion.9.refs_0_), channel_id=1, source_target_pairs={{0,1},{1,0},{2,3},{3,2},{4,5},{5,4},{6,7},{7,6},{8,9},{9,8},{10,11... | collective-permute-start | bytes 1179656 | tf_op jit(solution)/shard_map/ppermute | solution.py:155
  126.6 7.5 %collective-permute-start.19 = (f32[32,3072]{1,0:T(8,128)S(1)}, f32[32,3072]{1,0:T(8,128)S(1)}, u32[]{:S(2)}, u32[]{:S(2)}) collective-permute-start(f32[32,3072]{1,0:T(8,128)S(1)} %collective-permute-done.17.refs_1_), channel_id=1, source_target_pairs={{0,1},{1,0},{2,3},{3,2},{4,5},{5,4},{6,7},{7,6},{8,9},{9,8},{10,11... | collective-permute-start | bytes 1179656 | tf_op jit(solution)/shard_map/ppermute | solution.py:155
  126.6 18.6 %collective-permute-start.11 = (f32[32,3072]{1,0:T(8,128)S(1)}, f32[32,3072]{1,0:T(8,128)S(1)}, u32[]{:S(2)}, u32[]{:S(2)}) collective-permute-start(f32[32,3072]{1,0:T(8,128)S(1)} %fusion.4.refs_0_), channel_id=1, source_target_pairs={{0,1},{1,0},{2,3},{3,2},{4,5},{5,4},{6,7},{7,6},{8,9},{9,8},{10,11... | collective-permute-start | bytes 1179656 | tf_op jit(solution)/shard_map/ppermute | solution.py:155
  134.2 11.1 %collective-permute-start.12 = (f32[32,3072]{1,0:T(8,128)S(1)}, f32[32,3072]{1,0:T(8,128)S(1)}, u32[]{:S(2)}, u32[]{:S(2)}) collective-permute-start(f32[32,3072]{1,0:T(8,128)S(1)} %collective-permute-done.10.refs_1_), channel_id=1, source_target_pairs={{0,1},{1,0},{2,3},{3,2},{4,5},{5,4},{6,7},{7,6},{8,9},{9,8},{10,11... | collective-permute-start | bytes 1179656 | tf_op jit(solution)/shard_map/ppermute | solution.py:155
  156.4 9.2 %collective-permute-start.20 = (f32[32,1536]{1,0:T(8,128)S(1)}, f32[32,1536]{1,0:T(8,128)S(1)}, u32[]{:S(2)}, u32[]{:S(2)}) collective-permute-start(f32[32,1536]{1,0:T(8,128)S(1)} %get-tuple-element.33), channel_id=1, source_target_pairs={{0,4},{4,8},{8,12},{12,0},{1,5},{5,9},{9,13},{13,1},{2,6},{6,10},{... | collective-permute-start | bytes 589832 | tf_op jit(solution)/shard_map/ppermute | solution.py:152
  165.6 8.4 %collective-permute-start.21 = (f32[32,1536]{1,0:T(8,128)S(1)}, f32[32,1536]{1,0:T(8,128)S(1)}, u32[]{:S(2)}, u32[]{:S(2)}) collective-permute-start(f32[32,1536]{1,0:T(8,128)S(1)} %add.118), channel_id=1, source_target_pairs={{0,4},{4,8},{8,12},{12,0},{1,5},{5,9},{9,13},{13,1},{2,6},{6,10},{... | collective-permute-start | bytes 589832 | tf_op jit(solution)/shard_map/ppermute | solution.py:152
  174.0 7.5 %collective-permute-start.22 = (f32[32,1536]{1,0:T(8,128)S(1)}, f32[32,1536]{1,0:T(8,128)S(1)}, u32[]{:S(2)}, u32[]{:S(2)}) collective-permute-start(f32[32,1536]{1,0:T(8,128)S(1)} %add.119), channel_id=1, source_target_pairs={{0,4},{4,8},{8,12},{12,0},{1,5},{5,9},{9,13},{13,1},{2,6},{6,10},{... | collective-permute-start | bytes 589832 | tf_op jit(solution)/shard_map/ppermute | solution.py:152

commit v2 on v1

--- a/solution.py
+++ b/solution.py
@@ -27,20 +27,53 @@
     return next(c for c in choices if extent % c == 0)
 
 
-def three_pass(both, weight, dims):
+def three_pass(both, weight_ref, contract, tile, streamed):
     rows = both.shape[0] // 2
-    high, low = split(weight)
-    dot = functools.partial(
-        lax.dot_general,
-        dimension_numbers=((dims[:1], dims[1:]), ((), ())),
-        preferred_element_type=jnp.float32,
-    )
-    first = dot(both, high)
-    return first[:rows] + first[rows:] + dot(both[:rows], low)
-
-
-def forward_kernel(slots, contract, place_ref, *refs):
-    slot_refs, (weight_ref, send_ref, keep_ref, both) = refs[:slots], refs[slots:]
+    extent = weight_ref.shape
+    tiles = [
+        (i, j)
+        for i in range(0, extent[0], min(tile[0], extent[0]))
+        for j in range(0, extent[1], min(tile[1], extent[1]))
+    ]
+    tile = tuple(min(t, e) for t, e in zip(tile, extent))
+    sums = {}
+
+    def loaded(at):
+        return split(weight_ref[at[0] : at[0] + tile[0], at[1] : at[1] + tile[1]])
+
+    def multiply(at, parts):
+        high, low = parts
+        start = at[contract]
+        pair = both[:, start : start + tile[contract]]
+        if streamed:
+            dot = functools.partial(
+                lax.dot_general,
+                dimension_numbers=(((contract,), (1,)), ((), ())),
+                preferred_element_type=jnp.float32,
+            )
+            first = dot(high, pair)
+            value = first[:, :rows] + first[:, rows:] + dot(low, pair[:rows])
+        else:
+            dot = functools.partial(
+                lax.dot_general,
+                dimension_numbers=(((1,), (contract,)), ((), ())),
+                preferred_element_type=jnp.float32,
+            )
+            first = dot(pair, high)
+            value = first[:rows] + first[rows:] + dot(pair[:rows], low)
+        key = at[1 - contract]
+        sums[key] = sums[key] + value if key in sums else value
+
+    ready = loaded(tiles[0])
+    for n, at in enumerate(tiles):
+        following = loaded(tiles[n + 1]) if n + 1 < len(tiles) else None
+        multiply(at, ready)
+        ready = following
+    return [sums[key].T if streamed else sums[key] for key in sorted(sums)]
+
+
+def forward_kernel(slots, contract, tile, streamed, place_ref, *refs):
+    slot_refs, weight_ref, (send_ref, keep_ref, both) = refs[:slots], refs[slots], refs[-3:]
     block = slot_refs[0].shape[0]
     total = block * slots
 
@@ -52,12 +85,15 @@
             both[pl.ds(row, block), :] = high
             both[pl.ds(total + row, block), :] = low
 
-    result = three_pass(both[...], weight_ref[...], (1, contract))
-    keep_ref[...] = result[: total // 2]
-    send_ref[...] = result[total // 2 :]
-
-
-def forward(blocks, weight, place, chunk, chunks, by_column):
+    column = 0
+    for part in three_pass(both, weight_ref, contract, tile, streamed):
+        width = part.shape[1]
+        keep_ref[:, column : column + width] = part[: total // 2]
+        send_ref[:, column : column + width] = part[total // 2 :]
+        column += width
+
+
+def forward(blocks, weight, place, chunk, chunks, by_column, tile, streamed, after):
     slots, (block, depth) = len(blocks), blocks[0].shape
     hidden = weight.shape[1 if by_column else 0] // chunks
     width = divisor(hidden, 512, 384, 256, 128)
@@ -70,12 +106,12 @@
     half = block * slots // 2
     out = jax.ShapeDtypeStruct((half, hidden), jnp.float32)
     return pl.pallas_call(
-        functools.partial(forward_kernel, slots, 0 if by_column else 1),
+        functools.partial(forward_kernel, slots, 0 if by_column else 1, tile, streamed),
         out_shape=(out, out),
         grid_spec=pltpu.PrefetchScalarGridSpec(
             num_scalar_prefetch=1,
             grid=(steps,),
-            in_specs=[whole] * slots + [weight_spec],
+            in_specs=[whole] * slots + [weight_spec] + [pl.BlockSpec(memory_space=pl.ANY)] * len(after),
             out_specs=[pl.BlockSpec((half, width), lambda i, place: (0, i))] * 2,
             scratch_shapes=[pltpu.VMEM((2 * block * slots, depth), jnp.bfloat16)],
         ),
@@ -85,13 +121,13 @@
             bytes_accessed=4 * depth * hidden + 8 * half * hidden,
             transcendentals=0,
         ),
-    )(place, *blocks, weight)
-
-
-def backward_kernel(slots, earlier, place_ref, *refs):
+    )(place, *blocks, weight, *after)
+
+
+def backward_kernel(slots, earlier, waits, tile, streamed, place_ref, *refs):
     act_refs, weight_ref = refs[:slots], refs[slots]
     earlier_refs = refs[slots + 1 : slots + 1 + earlier]
-    out_refs = refs[slots + 1 + earlier : -2]
+    out_refs = refs[slots + 1 + earlier + waits : -2]
     both, result = refs[-2:]
     block = act_refs[0].shape[0]
     total = block * slots
@@ -103,29 +139,33 @@
             both[p * block : (p + 1) * block, :] = high
             both[total + p * block : total + (p + 1) * block, :] = low
 
-    result[...] = three_pass(both[...], weight_ref[...], (1, 1))
+    column = 0
+    for part in three_pass(both, weight_ref, 1, tile, streamed):
+        result[:, column : column + part.shape[1]] = part
+        column += part.shape[1]
     for b in range(slots):
         row = pl.multiple_of(place_ref[b] * block, block)
         rows = result[pl.ds(row, block), :]
         out_refs[b][...] = rows + earlier_refs[b][...] if earlier else rows
 
 
-def backward(acts, weight, place, earlier, chunk):
+def backward(acts, weight, place, earlier, chunk, part, parts, tile, streamed, after):
     slots, (block, hidden) = len(acts), acts[0].shape
-    depth = weight.shape[0]
+    depth = weight.shape[0] // parts
     width = divisor(depth, 256, 128)
-    tile = pl.BlockSpec((block, width), lambda i, place: (0, i))
+    steps = depth // width
     out = jax.ShapeDtypeStruct((block, depth), jnp.float32)
     return pl.pallas_call(
-        functools.partial(backward_kernel, slots, len(earlier)),
+        functools.partial(backward_kernel, slots, len(earlier), len(after), tile, streamed),
         out_shape=[out] * slots,
         grid_spec=pltpu.PrefetchScalarGridSpec(
             num_scalar_prefetch=1,
-            grid=(depth // width,),
+            grid=(steps,),
             in_specs=[pl.BlockSpec((block, hidden), lambda i, place: (0, 0))] * slots
-            + [pl.BlockSpec((width, hidden), lambda i, place: (i, chunk))]
-            + [tile] * len(earlier),
-            out_specs=[tile] * slots,
+            + [pl.BlockSpec((width, hidden), lambda i, place: (part * steps + i, chunk))]
+            + [pl.BlockSpec((block, width), lambda i, place: (0, part * steps + i))] * len(earlier)
+            + [pl.BlockSpec(memory_space=pl.ANY)] * len(after),
+            out_specs=[pl.BlockSpec((block, width), lambda i, place: (0, i))] * slots,
             scratch_shapes=[
                 pltpu.VMEM((2 * block * slots, hidden), jnp.bfloat16),
                 pltpu.VMEM((block * slots, width), jnp.float32),
@@ -137,7 +177,7 @@
             bytes_accessed=4 * depth * hidden + 8 * block * slots * depth,
             transcendentals=0,
         ),
-    )(place, *acts, weight, *earlier)
+    )(place, *acts, weight, *earlier, *after)
 
 
 def body(hid_size, emb_size, inputs, out_grad, in_weight, in_bias, out_weight, norm_gain):
@@ -177,35 +217,53 @@
     normed = (inputs - row_mean[:, None]) * inv_std
     scaled = gathered(normed * norm_gain)
 
-    def reduced(partial):
+    def halved(partial):
         send, keep = partial
-        summed = keep + other_core(send)
+        return keep + other_core(send)
+
+    def exchanged(summed):
         terms = [summed[d * tokens : (d + 1) * tokens] for d in range(chips)]
-        running = terms[chips - 1]
-        for step in range(1, chips):
-            running = next_chip(running) + terms[chips - 1 - step]
-        return running
-
-    back_parts = [forward(grads, out_weight, place, c, CHUNKS, False) for c in range(CHUNKS)]
-    backs = [reduced(part) for part in back_parts]
-    pre_parts = [forward(scaled, in_weight, place, c, CHUNKS, True) for c in range(CHUNKS)]
-    pres = [reduced(part) for part in pre_parts]
-
-    sums = ()
-    for c in range(CHUNKS):
+        arrival = next_chip(terms[chips - 1])
+        for step in range(2, chips):
+            arrival = next_chip(arrival + terms[chips - step])
+        return arrival, terms[0]
+
+    tall, wide = (256, depth), (depth, 256)
+    back_0 = forward(grads, out_weight, place, 0, CHUNKS, False, tall, True, [scaled[hid_size // 2]])
+    back_1 = forward(grads, out_weight, place, 1, CHUNKS, False, tall, False, [scaled[-1], back_0[1]])
+    half_0 = halved(back_0)
+    back_0 = exchanged(half_0)
+    pre_0 = forward(scaled, in_weight, place, 0, CHUNKS, True, wide, False, [half_0])
+    half_1 = halved(back_1)
+    back_1 = exchanged(half_1)
+    pre_1 = forward(scaled, in_weight, place, 1, CHUNKS, True, (256, 512), False, [half_1, back_0[0]])
+    backs = [back_0, back_1]
+    pres = [exchanged(halved(pre_0)), exchanged(halved(pre_1))]
+
+    def spread_out(c):
         piece = hidden // CHUNKS
-        act = backs[c] * gelu_slope(pres[c] + in_bias[c * piece : (c + 1) * piece])
+        act = sum(backs[c]) * gelu_slope(sum(pres[c]) + in_bias[c * piece : (c + 1) * piece])
         mine = [None] * chips
         mine[0] = act
         for step in range(1, chips):
             act = next_chip(act)
             mine[(chips - step) % chips] = act
-        theirs = [other_core(block) for block in mine]
-        sums = backward(mine + theirs, in_weight, place, sums, c)
-
-    running = sums[1 % hid_size]
-    for step in range(1, hid_size):
-        running = along_hid(running) + sums[(step + 1) % hid_size]
+        return mine + [other_core(block) for block in mine]
+
+    def summed_along_hid(sums):
+        running = sums[1 % hid_size]
+        for step in range(1, hid_size):
+            running = along_hid(running) + sums[(step + 1) % hid_size]
+        return running
+
+    acts_0, acts_1 = spread_out(0), spread_out(1)
+    sums = backward(acts_0, in_weight, place, (), 0, 0, 1, (256, 768), True, [pre_1[1]])
+    parts = 2 if depth % 512 == 0 else 1
+    ends = []
+    for part in range(parts):
+        form = ((256, 768), (256, 1536))[part]
+        ends.append(backward(acts_1, in_weight, place, sums, 1, part, parts, form, False, [ends[-1][0] if ends else sums[0]]))
+    running = jnp.concatenate([summed_along_hid(end) for end in ends], axis=1)
     normed_grad = running * norm_gain
     totals = lax.psum(
         jnp.stack([jnp.sum(normed_grad, axis=-1), jnp.sum(normed_grad * normed, axis=-1)]), "emb"

time: 189 us -> 180 us (0.952)
  waiting for transfers between devices: 91.6 us -> 79.4 us
  Pallas kernels: 65.1 us -> 68.1 us
    ppermute x9 -> x12, waiting for transfers between devices: 47.7 us -> 39.6 us  [along_hid(): lax.ppermute(values, 'hid', [(i, (i + 1) % hid_size) for i in range(hid_s...]
    ppermute x6, waiting for transfers between devices: 43.9 us -> 39.8 us  [next_chip(): lax.ppermute(values, 'emb', [(i, (i + 2) % emb_size) for i in range(emb_s...]
    ppermute x9 -> x12, starting transfers between devices: 4.57 us -> 7.53 us  [along_hid(): lax.ppermute(values, 'hid', [(i, (i + 1) % hid_size) for i in range(hid_s...]
    pallas_call x2 -> x3, Pallas kernels: 22.2 us -> 25 us  [backward(): pl.pallas_call(functools.partial(backward_kernel, slots, len(earlier), le...]
    ppermute x6, starting transfers between devices: 7.85 us -> 5.45 us  [next_chip(): lax.ppermute(values, 'emb', [(i, (i + 2) % emb_size) for i in range(emb_s...]
  transfers between devices with their start and end apart: 23 -> 26, of which waited for: 14 -> 14; matrix products, arithmetic and copies ran while one was open for 1% -> 2% of each run, Pallas kernels for 29% -> 34%
where the time goes in v2:
time: 180 us
  waiting for transfers between devices  79.4 us (44%)
  Pallas kernels  68.1 us (38%)
  starting transfers between devices  14.7 us (8%)
  blocking collectives  11 us (6%)
  other arithmetic  5.2 us (3%)
    pallas_call x4, Pallas kernels, forward(): pl.pallas_call(functools.partial(forward_kernel, slots, 0 if by_column el...  43 us
    ppermute x6, waiting for transfers between devices, next_chip(): lax.ppermute(values, 'emb', [(i, (i + 2) % emb_size) for i in range(emb_s...  39.8 us
    ppermute x12, waiting for transfers between devices, along_hid(): lax.ppermute(values, 'hid', [(i, (i + 1) % hid_size) for i in range(hid_s...  39.6 us
    pallas_call x3, Pallas kernels, backward(): pl.pallas_call(functools.partial(backward_kernel, slots, len(earlier), le...  25 us
    ppermute x12, starting transfers between devices, along_hid(): lax.ppermute(values, 'hid', [(i, (i + 1) % hid_size) for i in range(hid_s...  7.53 us
    psum x1, blocking collectives, body(): lax.psum(jnp.stack([jnp.sum(normed_grad, axis=-1), jnp.sum(normed_grad *...  5.89 us
    ppermute x6, starting transfers between devices, next_chip(): lax.ppermute(values, 'emb', [(i, (i + 2) % emb_size) for i in range(emb_s...  5.45 us
    all_gather x1, blocking collectives, body(): stats = lax.all_gather(jnp.stack([local_mean[:, 0], local_square]), 'emb')  5.07 us
  transfers between devices with their start and end apart: 26, of which 14 were waited for; matrix products, arithmetic and copies ran while one was open for 2% of the time, Pallas kernels for 34%

profile of v2, /device:TPU:0, one launch (start us, length us, event | category | flops | bytes accessed | tf_op | source)
XLA Modules:
  0.0 179.7 jit_solution(4419253286650371127)
XLA Ops:
  0.0 3.0 %collective-permute-start = (f32[32,1536]{1,0:T(8,128)}, f32[32,1536]{1,0:T(8,128)S(1)}, u32[]{:S(2)}, u32[]{:S(2)}) collective-permute-start(f32[32,1536]{1,0:T(8,128)} %refs_0_.3), channel_id=1, source_target_pairs={{0,4},{4,8},{8,12},{12,0},{1,5},{5,9},{9,13},{13,1},{2,6},{6,10},{... | collective-permute-start | bytes 589832 | tf_op jit(solution)/shard_map/ppermute | solution.py:192
  3.0 1.0 reduce_sum.54
  4.1 1.1 multiply_reduce_fusion.1
  5.2 5.1 %all-gather.1 = f32[4,2,32]{2,1,0:T(2,128)S(1)} all-gather(f32[1,2,32]{2,1,0:T(2,128)S(1)} %maximum_bitcast_fusion), channel_id=2, replica_groups=mesh['groups'=2,'hid'=4,'emb'=4] {'emb'}, dimensions={0}, use_global_device_ids=true | all-gather | bytes 1280 | tf_op jit(solution)/shard_map/all_gather | solution.py:213
  10.4 1.0 fusion.12.refs_0_
  11.4 1.6 collective-permute-start.3
  13.0 1.6 collective-permute-start.1
  14.6 6.4 %collective-permute-done.3.refs_1_ = f32[32,1536]{1,0:T(8,128)S(1)} collective-permute-done((f32[32,1536]{1,0:T(8,128)S(1)}, f32[32,1536]{1,0:T(8,128)S(1)}, u32[]{:S(2)}, u32[]{:S(2)}) %collective-permute-start.3) | collective-permute-done | bytes 196640 | tf_op jit(solution)/shard_map/ppermute | solution.py:192
  21.0 3.9 %collective-permute-done.1.refs_2_ = f32[32,1536]{1,0:T(8,128)S(1)} collective-permute-done((f32[32,1536]{1,0:T(8,128)S(1)}, f32[32,1536]{1,0:T(8,128)S(1)}, u32[]{:S(2)}, u32[]{:S(2)}) %collective-permute-start.1) | collective-permute-done | bytes 196640 | tf_op jit(solution)/shard_map/ppermute | solution.py:192
  25.0 4.1 %collective-permute-done.4.refs_5_.refs_2_ = f32[32,1536]{1,0:T(8,128)S(1)} collective-permute-done((f32[32,1536]{1,0:T(8,128)S(1)}, f32[32,1536]{1,0:T(8,128)S(1)}, u32[]{:S(2)}, u32[]{:S(2)}) %collective-permute-start.4) | collective-permute-done | bytes 196640 | tf_op jit(solution)/shard_map/ppermute | solution.py:192
  29.2 5.3 %collective-permute-done.2.refs_3_ = f32[32,1536]{1,0:T(8,128)S(1)} collective-permute-done((f32[32,1536]{1,0:T(8,128)S(1)}, f32[32,1536]{1,0:T(8,128)S(1)}, u32[]{:S(2)}, u32[]{:S(2)}) %collective-permute-start.2) | collective-permute-done | bytes 196640 | tf_op jit(solution)/shard_map/ppermute | solution.py:192
  34.5 0.9 copy-done
  35.4 11.1 %shard_map.64 = (f32[64,3072]{1,0:T(8,128)S(1)}, f32[64,3072]{1,0:T(8,128)S(1)}) custom-call(s32[4]{0:T(128)S(1)} %fusion.14.place_ref, f32[32,1536]{1,0:T(8,128)S(1)} %copy-done, f32[32,1536]{1,0:T(8,128)S(1)} %collective-permute-done.refs_1_, f32[32,1536]{1,0:T(8,128)S(1)} %collective-permute-done.1.refs_2_, ...), custom_call_target="tpu_custom_call" | custom-call | flops 3623878656 | bytes 20447232 | tf_op jit(solution)/shard_map/pallas_call | solution.py:108
  46.6 11.1 %shard_map.65 = (f32[64,3072]{1,0:T(8,128)S(1)}, f32[64,3072]{1,0:T(8,128)S(1)}) custom-call(s32[4]{0:T(128)S(1)} %fusion.14.place_ref, f32[32,1536]{1,0:T(8,128)S(1)} %copy-done, f32[32,1536]{1,0:T(8,128)S(1)} %collective-permute-done.refs_1_, f32[32,1536]{1,0:T(8,128)S(1)} %collective-permute-done.1.refs_2_, ...), custom_call_target="tpu_custom_call" | custom-call | flops 3623878656 | bytes 20447232 | tf_op jit(solution)/shard_map/pallas_call | solution.py:108
  58.4 1.6 collective-permute-start.9
  60.0 10.3 %shard_map.67 = (f32[64,3072]{1,0:T(8,128)S(1)}, f32[64,3072]{1,0:T(8,128)S(1)}) custom-call(s32[4]{0:T(128)S(1)} %fusion.14.place_ref, f32[32,1536]{1,0:T(8,128)S(1)} %fusion.12.refs_0_, f32[32,1536]{1,0:T(8,128)S(1)} %collective-permute-done.3.refs_1_, f32[32,1536]{1,0:T(8,128)S(1)} %collective-permute-done.4.refs_5_.refs_2_, ...), custom_call_target="tpu_custom_call" | custom-call | flops 3623878656 | bytes 20447232 | tf_op jit(solution)/shard_map/pallas_call | solution.py:108
  70.5 10.4 %shard_map.66 = (f32[64,3072]{1,0:T(8,128)S(1)}, f32[64,3072]{1,0:T(8,128)S(1)}) custom-call(s32[4]{0:T(128)S(1)} %fusion.14.place_ref, f32[32,1536]{1,0:T(8,128)S(1)} %fusion.12.refs_0_, f32[32,1536]{1,0:T(8,128)S(1)} %collective-permute-done.3.refs_1_, f32[32,1536]{1,0:T(8,128)S(1)} %collective-permute-done.4.refs_5_.refs_2_, ...), custom_call_target="tpu_custom_call" | custom-call | flops 3623878656 | bytes 20447232 | tf_op jit(solution)/shard_map/pallas_call | solution.py:108
  82.3 1.6 collective-permute-start.7
  84.6 9.1 %collective-permute-done.16 = f32[32,3072]{1,0:T(8,128)S(1)} collective-permute-done((f32[32,3072]{1,0:T(8,128)S(1)}, f32[32,3072]{1,0:T(8,128)S(1)}, u32[]{:S(2)}, u32[]{:S(2)}) %collective-permute-start.16) | collective-permute-done | bytes 393248 | tf_op jit(solution)/shard_map/ppermute | solution.py:198
  94.5 7.6 %collective-permute-done.7 = f32[32,3072]{1,0:T(8,128)S(1)} collective-permute-done((f32[32,3072]{1,0:T(8,128)S(1)}, f32[32,3072]{1,0:T(8,128)S(1)}, u32[]{:S(2)}, u32[]{:S(2)}) %collective-permute-start.7) | collective-permute-done | bytes 393248 | tf_op jit(solution)/shard_map/ppermute | solution.py:198
  102.2 8.4 %collective-permute-done.11 = f32[32,3072]{1,0:T(8,128)S(1)} collective-permute-done((f32[32,3072]{1,0:T(8,128)S(1)}, f32[32,3072]{1,0:T(8,128)S(1)}, u32[]{:S(2)}, u32[]{:S(2)}) %collective-permute-start.11) | collective-permute-done | bytes 393248 | tf_op jit(solution)/shard_map/ppermute | solution.py:198
  111.4 7.6 %collective-permute-done.17.refs_1_ = f32[32,3072]{1,0:T(8,128)S(1)} collective-permute-done((f32[32,3072]{1,0:T(8,128)S(1)}, f32[32,3072]{1,0:T(8,128)S(1)}, u32[]{:S(2)}, u32[]{:S(2)}) %collective-permute-start.17) | collective-permute-done | bytes 393248 | tf_op jit(solution)/shard_map/ppermute | solution.py:198
  119.5 7.0 %collective-permute-done.12.refs_1_ = f32[32,3072]{1,0:T(8,128)S(1)} collective-permute-done((f32[32,3072]{1,0:T(8,128)S(1)}, f32[32,3072]{1,0:T(8,128)S(1)}, u32[]{:S(2)}, u32[]{:S(2)}) %collective-permute-start.12) | collective-permute-done | bytes 393248 | tf_op jit(solution)/shard_map/ppermute | solution.py:198
  126.5 11.3 %shard_map.68 = (f32[32,1536]{1,0:T(8,128)S(1)}, f32[32,1536]{1,0:T(8,128)S(1)}, f32[32,1536]{1,0:T(8,128)S(1)}, f32[32,1536]{1,0:T(8,128)S(1)}) custom-call(s32[4]{0:T(128)S(1)} %fusion.14.place_ref, f32[32,3072]{1,0:T(8,128)S(1)} %fusion.9.refs_0_, f32[32,3072]{1,0:T(8,128)S(1)} %collective-permute-done.17.refs_1_, ...), custom_call_target="tpu_custom_call" | custom-call | flops 3623878656 | bytes 20447232 | tf_op jit(solution)/shard_map/pallas_call | solution.py:158
  137.9 6.9 %shard_map.69 = (f32[32,768]{1,0:T(8,128)S(1)}, f32[32,768]{1,0:T(8,128)S(1)}, f32[32,768]{1,0:T(8,128)S(1)}, f32[32,768]{1,0:T(8,128)S(1)}) custom-call(s32[4]{0:T(128)S(1)} %fusion.14.place_ref, f32[32,3072]{1,0:T(8,128)S(1)} %fusion.4.refs_0_, f32[32,3072]{1,0:T(8,128)S(1)} %collective-permute-done.12.refs_1_, ...), custom_call_target="tpu_custom_call" | custom-call | flops 1811939328 | bytes 10223616 | tf_op jit(solution)/shard_map/pallas_call | solution.py:158
  144.8 6.9 %shard_map.70 = (f32[32,768]{1,0:T(8,128)S(1)}, f32[32,768]{1,0:T(8,128)S(1)}, f32[32,768]{1,0:T(8,128)S(1)}, f32[32,768]{1,0:T(8,128)S(1)}) custom-call(s32[4]{0:T(128)S(1)} %fusion.14.place_ref, f32[32,3072]{1,0:T(8,128)S(1)} %fusion.4.refs_0_, f32[32,3072]{1,0:T(8,128)S(1)} %collective-permute-done.12.refs_1_, ...), custom_call_target="tpu_custom_call" | custom-call | flops 1811939328 | bytes 10223616 | tf_op jit(solution)/shard_map/pallas_call | solution.py:158
  152.5 6.6 %collective-permute-done.23 = f32[32,768]{1,0:T(8,128)S(1)} collective-permute-done((f32[32,768]{1,0:T(8,128)S(1)}, f32[32,768]{1,0:T(8,128)S(1)}, u32[]{:S(2)}, u32[]{:S(2)}) %collective-permute-start.23) | collective-permute-done | bytes 98336 | tf_op jit(solution)/shard_map/ppermute | solution.py:192
  159.2 1.6 collective-permute-done.21
  160.9 5.3 %collective-permute-done.24 = f32[32,768]{1,0:T(8,128)S(1)} collective-permute-done((f32[32,768]{1,0:T(8,128)S(1)}, f32[32,768]{1,0:T(8,128)S(1)}, u32[]{:S(2)}, u32[]{:S(2)}) %collective-permute-start.24) | collective-permute-done | bytes 98336 | tf_op jit(solution)/shard_map/ppermute | solution.py:192
  166.4 1.4 collective-permute-done.22
  167.8 5.0 %collective-permute-done.25 = f32[32,768]{1,0:T(8,128)S(1)} collective-permute-done((f32[32,768]{1,0:T(8,128)S(1)}, f32[32,768]{1,0:T(8,128)S(1)}, u32[]{:S(2)}, u32[]{:S(2)}) %collective-permute-start.25) | collective-permute-done | bytes 98336 | tf_op jit(solution)/shard_map/ppermute | solution.py:192
  173.0 5.9 %psum.7 = f32[2,32]{1,0:T(2,128)S(1)} all-reduce(f32[2,32]{1,0:T(2,128)S(1)} %pad_maximum_fusion), channel_id=1, replica_groups=mesh['groups'=2,'hid'=4,'emb'=4] {'emb'}, use_global_device_ids=true, to_apply=%region_6.7 | all-reduce | flops 64 | bytes 512 | tf_op jit(solution)/shard_map/psum | solution.py:268
  (69 shorter events, 7.5 us)
Async XLA Ops:
  0.0 13.0 %collective-permute-start = (f32[32,1536]{1,0:T(8,128)}, f32[32,1536]{1,0:T(8,128)S(1)}, u32[]{:S(2)}, u32[]{:S(2)}) collective-permute-start(f32[32,1536]{1,0:T(8,128)} %refs_0_.3), channel_id=1, source_target_pairs={{0,4},{4,8},{8,12},{12,0},{1,5},{5,9},{9,13},{13,1},{2,6},{6,10},{... | collective-permute-start | bytes 589832 | tf_op jit(solution)/shard_map/ppermute | solution.py:192
  11.4 9.6 %collective-permute-start.3 = (f32[32,1536]{1,0:T(8,128)S(1)}, f32[32,1536]{1,0:T(8,128)S(1)}, u32[]{:S(2)}, u32[]{:S(2)}) collective-permute-start(f32[32,1536]{1,0:T(8,128)S(1)} %fusion.12.refs_0_), channel_id=1, source_target_pairs={{0,4},{4,8},{8,12},{12,0},{1,5},{5,9},{9,13},{13,1},{2,6},{6,10},{... | collective-permute-start | bytes 589832 | tf_op jit(solution)/shard_map/ppermute | solution.py:192
  13.0 11.8 %collective-permute-start.1 = (f32[32,1536]{1,0:T(8,128)S(1)}, f32[32,1536]{1,0:T(8,128)S(1)}, u32[]{:S(2)}, u32[]{:S(2)}) collective-permute-start(f32[32,1536]{1,0:T(8,128)S(1)} %collective-permute-done.refs_1_), channel_id=1, source_target_pairs={{0,4},{4,8},{8,12},{12,0},{1,5},{5,9},{9,13},{13,1},{2,6},{6,10},{... | collective-permute-start | bytes 589832 | tf_op jit(solution)/shard_map/ppermute | solution.py:192
  21.0 8.1 %collective-permute-start.4 = (f32[32,1536]{1,0:T(8,128)S(1)}, f32[32,1536]{1,0:T(8,128)S(1)}, u32[]{:S(2)}, u32[]{:S(2)}) collective-permute-start(f32[32,1536]{1,0:T(8,128)S(1)} %collective-permute-done.3.refs_1_), channel_id=1, source_target_pairs={{0,4},{4,8},{8,12},{12,0},{1,5},{5,9},{9,13},{13,1},{2,6},{6,10},{... | collective-permute-start | bytes 589832 | tf_op jit(solution)/shard_map/ppermute | solution.py:192
  24.8 9.6 %collective-permute-start.2 = (f32[32,1536]{1,0:T(8,128)S(1)}, f32[32,1536]{1,0:T(8,128)S(1)}, u32[]{:S(2)}, u32[]{:S(2)}) collective-permute-start(f32[32,1536]{1,0:T(8,128)S(1)} %collective-permute-done.1.refs_2_), channel_id=1, source_target_pairs={{0,4},{4,8},{8,12},{12,0},{1,5},{5,9},{9,13},{13,1},{2,6},{6,10},{... | collective-permute-start | bytes 589832 | tf_op jit(solution)/shard_map/ppermute | solution.py:192
  29.0 17.6 %collective-permute-start.5 = (f32[32,1536]{1,0:T(8,128)S(1)}, f32[32,1536]{1,0:T(8,128)S(1)}, u32[]{:S(2)}, u32[]{:S(2)}) collective-permute-start(f32[32,1536]{1,0:T(8,128)S(1)} %collective-permute-done.4.refs_5_.refs_2_), channel_id=1, source_target_pairs={{0,4},{4,8},{8,12},{12,0},{1,5},{5,9},{9,13},{13,1},{2,6},{6,10},{... | collective-permute-start | bytes 589832 | tf_op jit(solution)/shard_map/ppermute | solution.py:192
  34.5 0.9 copy-start
  46.5 11.8 %collective-permute-start.8 = (f32[64,3072]{1,0:T(8,128)S(1)}, f32[64,3072]{1,0:T(8,128)S(1)}, u32[]{:S(2)}, u32[]{:S(2)}) collective-permute-start(f32[64,3072]{1,0:T(8,128)S(1)} %get-tuple-element.28), channel_id=1, source_target_pairs={{0,1},{1,0},{2,3},{3,2},{4,5},{5,4},{6,7},{7,6},{8,9},{9,8},{10,11... | collective-permute-start | bytes 2359304 | tf_op jit(solution)/shard_map/ppermute | solution.py:195
  57.7 12.7 %collective-permute-start.6 = (f32[64,3072]{1,0:T(8,128)S(1)}, f32[64,3072]{1,0:T(8,128)S(1)}, u32[]{:S(2)}, u32[]{:S(2)}) collective-permute-start(f32[64,3072]{1,0:T(8,128)S(1)} %get-tuple-element.27), channel_id=1, source_target_pairs={{0,1},{1,0},{2,3},{3,2},{4,5},{5,4},{6,7},{7,6},{8,9},{9,8},{10,11... | collective-permute-start | bytes 2359304 | tf_op jit(solution)/shard_map/ppermute | solution.py:195
  58.4 23.9 %copy-start.3 = (f32[6144]{0:T(1024)S(1)}, f32[6144]{0:T(1024)}, u32[]{:S(2)}) copy-start(f32[6144]{0:T(1024)} %param.9) | copy-start | bytes 73732
  58.4 12.1 %collective-permute-start.9 = (f32[32,3072]{1,0:T(8,128)S(1)}, f32[32,3072]{1,0:T(8,128)S(1)}, u32[]{:S(2)}, u32[]{:S(2)}) collective-permute-start(f32[32,3072]{1,0:T(8,128)S(1)} %slice.55), channel_id=1, source_target_pairs={{0,2},{1,3},{2,0},{3,1},{4,6},{5,7},{6,4},{7,5},{8,10},{9,11},{10,... | collective-permute-start | bytes 1179656 | tf_op jit(solution)/shard_map/ppermute | solution.py:198
  70.3 11.2 %collective-permute-start.15 = (f32[64,3072]{1,0:T(8,128)S(1)}, f32[64,3072]{1,0:T(8,128)S(1)}, u32[]{:S(2)}, u32[]{:S(2)}) collective-permute-start(f32[64,3072]{1,0:T(8,128)S(1)} %get-tuple-element.32), channel_id=1, source_target_pairs={{0,1},{1,0},{2,3},{3,2},{4,5},{5,4},{6,7},{7,6},{8,9},{9,8},{10,11... | collective-permute-start | bytes 2359304 | tf_op jit(solution)/shard_map/ppermute | solution.py:195
  81.0 2.9 %collective-permute-start.10 = (f32[64,3072]{1,0:T(8,128)S(1)}, f32[64,3072]{1,0:T(8,128)S(1)}, u32[]{:S(2)}, u32[]{:S(2)}) collective-permute-start(f32[64,3072]{1,0:T(8,128)S(1)} %get-tuple-element.30), channel_id=1, source_target_pairs={{0,1},{1,0},{2,3},{3,2},{4,5},{5,4},{6,7},{7,6},{8,9},{9,8},{10,11... | collective-permute-start | bytes 2359304 | tf_op jit(solution)/shard_map/ppermute | solution.py:195
  81.7 12.1 %collective-permute-start.16 = (f32[32,3072]{1,0:T(8,128)S(1)}, f32[32,3072]{1,0:T(8,128)S(1)}, u32[]{:S(2)}, u32[]{:S(2)}) collective-permute-start(f32[32,3072]{1,0:T(8,128)S(1)} %slice.59), channel_id=1, source_target_pairs={{0,2},{1,3},{2,0},{3,1},{4,6},{5,7},{6,4},{7,5},{8,10},{9,11},{10,... | collective-permute-start | bytes 1179656 | tf_op jit(solution)/shard_map/ppermute | solution.py:198
  82.3 19.9 %collective-permute-start.7 = (f32[32,3072]{1,0:T(8,128)S(1)}, f32[32,3072]{1,0:T(8,128)S(1)}, u32[]{:S(2)}, u32[]{:S(2)}) collective-permute-start(f32[32,3072]{1,0:T(8,128)S(1)} %slice.53), channel_id=1, source_target_pairs={{0,2},{1,3},{2,0},{3,1},{4,6},{5,7},{6,4},{7,5},{8,10},{9,11},{10,... | collective-permute-start | bytes 1179656 | tf_op jit(solution)/shard_map/ppermute | solution.py:198
  84.1 26.6 %collective-permute-start.11 = (f32[32,3072]{1,0:T(8,128)S(1)}, f32[32,3072]{1,0:T(8,128)S(1)}, u32[]{:S(2)}, u32[]{:S(2)}) collective-permute-start(f32[32,3072]{1,0:T(8,128)S(1)} %slice.56), channel_id=1, source_target_pairs={{0,2},{1,3},{2,0},{3,1},{4,6},{5,7},{6,4},{7,5},{8,10},{9,11},{10,... | collective-permute-start | bytes 1179656 | tf_op jit(solution)/shard_map/ppermute | solution.py:198
  94.0 25.1 %collective-permute-start.17 = (f32[32,3072]{1,0:T(8,128)S(1)}, f32[32,3072]{1,0:T(8,128)S(1)}, u32[]{:S(2)}, u32[]{:S(2)}) collective-permute-start(f32[32,3072]{1,0:T(8,128)S(1)} %fusion.9.refs_0_), channel_id=1, source_target_pairs={{0,2},{1,3},{2,0},{3,1},{4,6},{5,7},{6,4},{7,5},{8,10},{9,11},{10,... | collective-permute-start | bytes 1179656 | tf_op jit(solution)/shard_map/ppermute | solution.py:198
  110.8 15.7 %collective-permute-start.12 = (f32[32,3072]{1,0:T(8,128)S(1)}, f32[32,3072]{1,0:T(8,128)S(1)}, u32[]{:S(2)}, u32[]{:S(2)}) collective-permute-start(f32[32,3072]{1,0:T(8,128)S(1)} %fusion.4.refs_0_), channel_id=1, source_target_pairs={{0,2},{1,3},{2,0},{3,1},{4,6},{5,7},{6,4},{7,5},{8,10},{9,11},{10,... | collective-permute-start | bytes 1179656 | tf_op jit(solution)/shard_map/ppermute | solution.py:198
  111.4 15.1 %collective-permute-start.18 = (f32[32,3072]{1,0:T(8,128)S(1)}, f32[32,3072]{1,0:T(8,128)S(1)}, u32[]{:S(2)}, u32[]{:S(2)}) collective-permute-start(f32[32,3072]{1,0:T(8,128)S(1)} %fusion.9.refs_0_), channel_id=1, source_target_pairs={{0,1},{1,0},{2,3},{3,2},{4,5},{5,4},{6,7},{7,6},{8,9},{9,8},{10,11... | collective-permute-start | bytes 1179656 | tf_op jit(solution)/shard_map/ppermute | solution.py:195
  119.0 7.5 %collective-permute-start.19 = (f32[32,3072]{1,0:T(8,128)S(1)}, f32[32,3072]{1,0:T(8,128)S(1)}, u32[]{:S(2)}, u32[]{:S(2)}) collective-permute-start(f32[32,3072]{1,0:T(8,128)S(1)} %collective-permute-done.17.refs_1_), channel_id=1, source_target_pairs={{0,1},{1,0},{2,3},{3,2},{4,5},{5,4},{6,7},{7,6},{8,9},{9,8},{10,11... | collective-permute-start | bytes 1179656 | tf_op jit(solution)/shard_map/ppermute | solution.py:195
  119.0 18.8 %collective-permute-start.13 = (f32[32,3072]{1,0:T(8,128)S(1)}, f32[32,3072]{1,0:T(8,128)S(1)}, u32[]{:S(2)}, u32[]{:S(2)}) collective-permute-start(f32[32,3072]{1,0:T(8,128)S(1)} %fusion.4.refs_0_), channel_id=1, source_target_pairs={{0,1},{1,0},{2,3},{3,2},{4,5},{5,4},{6,7},{7,6},{8,9},{9,8},{10,11... | collective-permute-start | bytes 1179656 | tf_op jit(solution)/shard_map/ppermute | solution.py:195
  126.5 11.4 %collective-permute-start.14 = (f32[32,3072]{1,0:T(8,128)S(1)}, f32[32,3072]{1,0:T(8,128)S(1)}, u32[]{:S(2)}, u32[]{:S(2)}) collective-permute-start(f32[32,3072]{1,0:T(8,128)S(1)} %collective-permute-done.12.refs_1_), channel_id=1, source_target_pairs={{0,1},{1,0},{2,3},{3,2},{4,5},{5,4},{6,7},{7,6},{8,9},{9,8},{10,11... | collective-permute-start | bytes 1179656 | tf_op jit(solution)/shard_map/ppermute | solution.py:195
  137.9 34.9 %copy-start.1 = (f32[32,1536]{1,0:T(8,128)S(1)}, f32[32,1536]{1,0:T(8,128)}, u32[]{:S(2)}) copy-start(f32[32,1536]{1,0:T(8,128)} %param.6) | copy-start | bytes 589828
  137.9 34.9 %copy-start.2 = (f32[1536]{0:T(1024)S(1)}, f32[1536]{0:T(1024)}, u32[]{:S(2)}) copy-start(f32[1536]{0:T(1024)} %param.11) | copy-start | bytes 18436
  144.8 7.5 %collective-permute-start.20 = (f32[32,768]{1,0:T(8,128)S(1)}, f32[32,768]{1,0:T(8,128)S(1)}, u32[]{:S(2)}, u32[]{:S(2)}) collective-permute-start(f32[32,768]{1,0:T(8,128)S(1)} %get-tuple-element.37), channel_id=1, source_target_pairs={{0,4},{4,8},{8,12},{12,0},{1,5},{5,9},{9,13},{13,1},{2,6},{6,10},{... | collective-permute-start | bytes 294920 | tf_op jit(solution)/shard_map/ppermute | solution.py:192
  151.7 7.4 %collective-permute-start.23 = (f32[32,768]{1,0:T(8,128)S(1)}, f32[32,768]{1,0:T(8,128)S(1)}, u32[]{:S(2)}, u32[]{:S(2)}) collective-permute-start(f32[32,768]{1,0:T(8,128)S(1)} %get-tuple-element.41), channel_id=1, source_target_pairs={{0,4},{4,8},{8,12},{12,0},{1,5},{5,9},{9,13},{13,1},{2,6},{6,10},{... | collective-permute-start | bytes 294920 | tf_op jit(solution)/shard_map/ppermute | solution.py:192
  152.3 8.6 %collective-permute-start.21 = (f32[32,768]{1,0:T(8,128)S(1)}, f32[32,768]{1,0:T(8,128)S(1)}, u32[]{:S(2)}, u32[]{:S(2)}) collective-permute-start(f32[32,768]{1,0:T(8,128)S(1)} %add.127), channel_id=1, source_target_pairs={{0,4},{4,8},{8,12},{12,0},{1,5},{5,9},{9,13},{13,1},{2,6},{6,10},{... | collective-permute-start | bytes 294920 | tf_op jit(solution)/shard_map/ppermute | solution.py:192
  159.2 7.1 %collective-permute-start.24 = (f32[32,768]{1,0:T(8,128)S(1)}, f32[32,768]{1,0:T(8,128)S(1)}, u32[]{:S(2)}, u32[]{:S(2)}) collective-permute-start(f32[32,768]{1,0:T(8,128)S(1)} %add.130), channel_id=1, source_target_pairs={{0,4},{4,8},{8,12},{12,0},{1,5},{5,9},{9,13},{13,1},{2,6},{6,10},{... | collective-permute-start | bytes 294920 | tf_op jit(solution)/shard_map/ppermute | solution.py:192
  160.9 6.9 %collective-permute-start.22 = (f32[32,768]{1,0:T(8,128)S(1)}, f32[32,768]{1,0:T(8,128)S(1)}, u32[]{:S(2)}, u32[]{:S(2)}) collective-permute-start(f32[32,768]{1,0:T(8,128)S(1)} %add.128), channel_id=1, source_target_pairs={{0,4},{4,8},{8,12},{12,0},{1,5},{5,9},{9,13},{13,1},{2,6},{6,10},{... | collective-permute-start | bytes 294920 | tf_op jit(solution)/shard_map/ppermute | solution.py:192
  166.3 6.5 %collective-permute-start.25 = (f32[32,768]{1,0:T(8,128)S(1)}, f32[32,768]{1,0:T(8,128)S(1)}, u32[]{:S(2)}, u32[]{:S(2)}) collective-permute-start(f32[32,768]{1,0:T(8,128)S(1)} %add.131), channel_id=1, source_target_pairs={{0,4},{4,8},{8,12},{12,0},{1,5},{5,9},{9,13},{13,1},{2,6},{6,10},{... | collective-permute-start | bytes 294920 | tf_op jit(solution)/shard_map/ppermute | solution.py:192

commit v3 on v2

v3 whole, which is shorter than its diff:
```python
import functools
import math

import jax
import jax.numpy as jnp
from jax import lax
from jax.experimental import pallas as pl
from jax.experimental.pallas import tpu as pltpu
from jax.sharding import PartitionSpec as P

VMEM_LIMIT = 40 * 1024 * 1024
CHUNKS = 2


def gelu_slope(values):
    cdf = 0.5 * (1.0 + lax.erf(values * (1.0 / math.sqrt(2.0))))
    density = jnp.exp(-0.5 * values * values) * (1.0 / math.sqrt(2.0 * math.pi))
    return cdf + values * density


def split(values):
    high = values.astype(jnp.bfloat16)
    return high, (values - high.astype(jnp.float32)).astype(jnp.bfloat16)


def divisor(extent, *choices):
    return next(c for c in choices if extent % c == 0)


def three_pass(both, weight_refs, contract, width):
    rows = both.shape[0] // 2
    deep = weight_refs[0].shape[contract]
    extent = weight_refs[0].shape[1 - contract]
    width = min(width, extent)
    dot = functools.partial(
        lax.dot_general,
        dimension_numbers=(((1,), (contract,)), ((), ())),
        preferred_element_type=jnp.float32,
    )
    for column in range(0, extent, width):
        total = None
        for n, ref in enumerate(weight_refs):
            tile = ref[:, column : column + width] if contract == 0 else ref[column : column + width, :]
            high, low = split(tile)
            pair = both[:, n * deep : (n + 1) * deep]
            first = dot(pair, high)
            value = first[:rows] + first[rows:] + dot(pair[:rows], low)
            total = value if total is None else total + value
        yield column, total


def pieces_of(weight_block, index, contract, pieces):
    shape = list(weight_block)
    shape[contract] //= pieces

    def spec(n):
        def at(i, place):
            row, column = index(i)
            return (row * pieces + n, column) if contract == 0 else (row, column * pieces + n)

        return pl.BlockSpec(tuple(shape), at)

    return [spec(n) for n in range(pieces)]


def forward_kernel(slots, pieces, contract, place_ref, *refs):
    slot_refs, weight_refs, (send_ref, keep_ref, both) = refs[:slots], refs[slots : slots + pieces], refs[-3:]
    block = slot_refs[0].shape[0]
    total = block * slots

    @pl.when(pl.program_id(0) == 0)
    def _():
        for b in range(slots):
            high, low = split(slot_refs[b][...])
            row = pl.multiple_of(place_ref[b] * block, block)
            both[pl.ds(row, block), :] = high
            both[pl.ds(total + row, block), :] = low

    for column, part in three_pass(both, weight_refs, contract, 256):
        width = part.shape[1]
        keep_ref[:, column : column + width] = part[: total // 2]
        send_ref[:, column : column + width] = part[total // 2 :]


def forward(blocks, weight, place, chunk, chunks, by_column, pieces, after):
    slots, (block, depth) = len(blocks), blocks[0].shape
    hidden = weight.shape[1 if by_column else 0] // chunks
    width = divisor(hidden, 512, 384, 256, 128)
    steps = hidden // width
    whole = pl.BlockSpec((block, depth), lambda i, place: (0, 0))
    if by_column:
        weight_specs = pieces_of((depth, width), lambda i: (0, chunk * steps + i), 0, pieces)
    else:
        weight_specs = pieces_of((width, depth), lambda i: (chunk * steps + i, 0), 1, pieces)
    half = block * slots // 2
    out = jax.ShapeDtypeStruct((half, hidden), jnp.float32)
    return pl.pallas_call(
        functools.partial(forward_kernel, slots, pieces, 0 if by_column else 1),
        out_shape=(out, out),
        grid_spec=pltpu.PrefetchScalarGridSpec(
            num_scalar_prefetch=1,
            grid=(steps,),
            in_specs=[whole] * slots + weight_specs + [pl.BlockSpec(memory_space=pl.ANY)] * len(after),
            out_specs=[pl.BlockSpec((half, width), lambda i, place: (0, i))] * 2,
            scratch_shapes=[pltpu.VMEM((2 * block * slots, depth), jnp.bfloat16)],
        ),
        compiler_params=pltpu.CompilerParams(vmem_limit_bytes=VMEM_LIMIT),
        cost_estimate=pl.CostEstimate(
            flops=6 * block * slots * depth * hidden,
            bytes_accessed=4 * depth * hidden + 8 * half * hidden,
            transcendentals=0,
        ),
    )(place, *blocks, *[weight] * pieces, *after)


def backward_kernel(slots, pieces, earlier, place_ref, *refs):
    act_refs, weight_refs = refs[:slots], refs[slots : slots + pieces]
    earlier_refs = refs[slots + pieces : slots + pieces + earlier]
    out_refs = refs[-2 - slots : -2]
    both, result = refs[-2:]
    block = act_refs[0].shape[0]
    total = block * slots

    @pl.when(pl.program_id(0) == 0)
    def _():
        for p in range(slots):
            high, low = split(act_refs[p][...])
            both[p * block : (p + 1) * block, :] = high
            both[total + p * block : total + (p + 1) * block, :] = low

    for column, part in three_pass(both, weight_refs, 1, 256):
        result[:, column : column + part.shape[1]] = part
    for b in range(slots):
        row = pl.multiple_of(place_ref[b] * block, block)
        rows = result[pl.ds(row, block), :]
        out_refs[b][...] = rows + earlier_refs[b][...] if earlier else rows


def backward(acts, weight, place, earlier, chunk, part, parts, pieces, after):
    slots, (block, hidden) = len(acts), acts[0].shape
    depth = weight.shape[0] // parts
    width = divisor(depth, 256, 128)
    steps = depth // width
    out = jax.ShapeDtypeStruct((block, depth), jnp.float32)
    return pl.pallas_call(
        functools.partial(backward_kernel, slots, pieces, len(earlier)),
        out_shape=[out] * slots,
        grid_spec=pltpu.PrefetchScalarGridSpec(
            num_scalar_prefetch=1,
            grid=(steps,),
            in_specs=[pl.BlockSpec((block, hidden), lambda i, place: (0, 0))] * slots
            + pieces_of((width, hidden), lambda i: (part * steps + i, chunk), 1, pieces)
            + [pl.BlockSpec((block, width), lambda i, place: (0, part * steps + i))] * len(earlier)
            + [pl.BlockSpec(memory_space=pl.ANY)] * len(after),
            out_specs=[pl.BlockSpec((block, width), lambda i, place: (0, i))] * slots,
            scratch_shapes=[
                pltpu.VMEM((2 * block * slots, hidden), jnp.bfloat16),
                pltpu.VMEM((block * slots, width), jnp.float32),
            ],
        ),
        compiler_params=pltpu.CompilerParams(vmem_limit_bytes=VMEM_LIMIT),
        cost_estimate=pl.CostEstimate(
            flops=6 * block * slots * depth * hidden,
            bytes_accessed=4 * depth * hidden + 8 * block * slots * depth,
            transcendentals=0,
        ),
    )(place, *acts, *[weight] * pieces, *earlier, *after)


def body(hid_size, emb_size, inputs, out_grad, in_weight, in_bias, out_weight, norm_gain):
    chips = emb_size // 2
    tokens, depth = inputs.shape
    model_width = depth * emb_size
    hidden = in_weight.shape[1]
    me = lax.axis_index("emb")
    chip, core = me // 2, me % 2

    def along_hid(values, steps=1):
        return lax.ppermute(values, "hid", [(i, (i + steps) % hid_size) for i in range(hid_size)])

    def other_core(values):
        return lax.ppermute(values, "emb", [(i, i ^ 1) for i in range(emb_size)])

    def next_chip(values):
        return lax.ppermute(values, "emb", [(i, (i + 2) % emb_size) for i in range(emb_size)])

    owner = jnp.arange(emb_size, dtype=jnp.int32)
    place = ((owner % 2) ^ core) * chips + (owner // 2 - chip) % chips

    def gathered(values):
        blocks = [values]
        for _ in range(hid_size - 1):
            blocks.append(along_hid(blocks[-1]))
        return blocks

    grads = [out_grad] + [along_hid(out_grad, step) for step in range(1, hid_size)]

    local_mean = jnp.mean(inputs, axis=-1, keepdims=True)
    local_square = jnp.sum(jnp.square(inputs - local_mean), axis=-1)
    stats = lax.all_gather(jnp.stack([local_mean[:, 0], local_square]), "emb")
    row_mean = jnp.mean(stats[:, 0], axis=0)
    spread = jnp.sum(stats[:, 1] + depth * jnp.square(stats[:, 0] - row_mean), axis=0)
    inv_std = (1.0 / jnp.sqrt(spread / model_width + 1e-06))[:, None]
    normed = (inputs - row_mean[:, None]) * inv_std
    scaled = gathered(normed * norm_gain)

    def halved(partial):
        send, keep = partial
        return keep + other_core(send)

    def exchanged(summed):
        terms = [summed[d * tokens : (d + 1) * tokens] for d in range(chips)]
        arrival = next_chip(terms[chips - 1])
        for step in range(2, chips):
            arrival = next_chip(arrival + terms[chips - step])
        return arrival, terms[0]

    many = 6 if depth % 768 == 0 else 3
    back_0 = forward(grads, out_weight, place, 0, CHUNKS, False, 3, [scaled[1]])
    half_0 = halved(back_0)
    back_1 = forward(grads, out_weight, place, 1, CHUNKS, False, many, [half_0, scaled[hid_size // 2]])
    half_1 = halved(back_1)
    back_0, back_1 = exchanged(half_0), exchanged(half_1)
    pre_0 = forward(scaled, in_weight, place, 0, CHUNKS, True, 3, [half_1, back_0[0]])
    pre_1 = forward(scaled, in_weight, place, 1, CHUNKS, True, many, [pre_0[1], back_1[0]])
    backs = [back_0, back_1]
    pres = [exchanged(halved(pre_0)), exchanged(halved(pre_1))]

    def spread_out(c):
        piece = hidden // CHUNKS
        act = sum(backs[c]) * gelu_slope(sum(pres[c]) + in_bias[c * piece : (c + 1) * piece])
        mine = [None] * chips
        mine[0] = act
        for step in range(1, chips):
            act = next_chip(act)
            mine[(chips - step) % chips] = act
        return mine + [other_core(block) for block in mine]

    def summed_along_hid(sums):
        return sum([along_hid(sums[step], -step) for step in range(1, hid_size)], start=sums[0])

    acts_0, acts_1 = spread_out(0), spread_out(1)
    sums = backward(acts_0, in_weight, place, (), 0, 0, 1, 6, [pre_1[1]])
    parts = 2 if depth % 512 == 0 else 1
    ends = []
    for part in range(parts):
        ends.append(backward(acts_1, in_weight, place, sums, 1, part, parts, 6, [ends[-1][0] if ends else sums[0]]))
    running = jnp.concatenate([summed_along_hid(end) for end in ends], axis=1)
    normed_grad = running * norm_gain
    totals = lax.psum(
        jnp.stack([jnp.sum(normed_grad, axis=-1), jnp.sum(normed_grad * normed, axis=-1)]), "emb"
    )
    first, second = (totals / model_width)[:, :, None]
    return inv_std * (normed_grad - first - normed * second)


def solution(mesh):
    hid_size, emb_size = mesh.shape["hid"], mesh.shape["emb"]
    assert hid_size == emb_size and emb_size % 2 == 0
    return jax.shard_map(
        functools.partial(body, hid_size, emb_size),
        mesh=mesh,
        in_specs=(
            P(("groups", "hid"), "emb"),
            P(("groups", "hid"), "emb"),
            P("emb", "hid"),
            P("hid"),
            P("hid", "emb"),
            P("emb"),
        ),
        out_specs=P(("groups", "hid"), "emb"),
        check_vma=False,
    )
```

time: 180 us -> 184 us (1.022)
  starting transfers between devices: 14.7 us -> 30.8 us
  waiting for transfers between devices: 79.4 us -> 66.6 us
    ppermute x12, starting transfers between devices: 7.53 us -> 20.2 us  [along_hid(): lax.ppermute(values, 'hid', [(i, (i + steps) % hid_size) for i in range(h...]
    ppermute x6, waiting for transfers between devices: 39.8 us -> 30.5 us  [next_chip(): lax.ppermute(values, 'emb', [(i, (i + 2) % emb_size) for i in range(emb_s...]
    ppermute x6, starting transfers between devices: 5.45 us -> 9.35 us  [next_chip(): lax.ppermute(values, 'emb', [(i, (i + 2) % emb_size) for i in range(emb_s...]
    ppermute x12, waiting for transfers between devices: 39.6 us -> 35.9 us  [along_hid(): lax.ppermute(values, 'hid', [(i, (i + steps) % hid_size) for i in range(h...]
  transfers between devices with their start and end apart: 26 -> 26, of which waited for: 14 -> 13; matrix products, arithmetic and copies ran while one was open for 2% -> 1% of each run, Pallas kernels for 34% -> 21%
where the time goes in v3:
time: 184 us; the launch traced here: 183 us
  Pallas kernels  67.3 us (37%)
  waiting for transfers between devices  66.6 us (36%)
  starting transfers between devices  30.8 us (17%)
  blocking collectives  12.2 us (7%)
  other arithmetic  5.18 us (3%)
    pallas_call x4, Pallas kernels, forward(): pl.pallas_call(functools.partial(forward_kernel, slots, pieces, 0 if by_c...  42.5 us
    ppermute x12, waiting for transfers between devices, along_hid(): lax.ppermute(values, 'hid', [(i, (i + steps) % hid_size) for i in range(h...  35.9 us
    ppermute x6, waiting for transfers between devices, next_chip(): lax.ppermute(values, 'emb', [(i, (i + 2) % emb_size) for i in range(emb_s...  30.5 us
    pallas_call x3, Pallas kernels, backward(): pl.pallas_call(functools.partial(backward_kernel, slots, pieces, len(earl...  24.8 us
    ppermute x12, starting transfers between devices, along_hid(): lax.ppermute(values, 'hid', [(i, (i + steps) % hid_size) for i in range(h...  20.2 us
    ppermute x6, starting transfers between devices, next_chip(): lax.ppermute(values, 'emb', [(i, (i + 2) % emb_size) for i in range(emb_s...  9.35 us
    psum x1, blocking collectives, body(): lax.psum(jnp.stack([jnp.sum(normed_grad, axis=-1), jnp.sum(normed_grad *...  6.17 us
    all_gather x1, blocking collectives, body(): stats = lax.all_gather(jnp.stack([local_mean[:, 0], local_square]), 'emb')  5.98 us
  transfers between devices with their start and end apart: 26, of which 13 were waited for; matrix products, arithmetic and copies ran while one was open for 1% of the time, Pallas kernels for 21%

profile of v3, /device:TPU:0, one launch (start us, length us, event | category | flops | bytes accessed | tf_op | source)
XLA Modules:
  0.0 183.4 jit_solution(1467342739963979003)
XLA Ops:
  2.2 6.0 %all-gather.1 = f32[4,2,32]{2,1,0:T(2,128)S(1)} all-gather(f32[1,2,32]{2,1,0:T(2,128)S(1)} %maximum_bitcast_fusion), channel_id=2, replica_groups=mesh['groups'=2,'hid'=4,'emb'=4] {'emb'}, dimensions={0}, use_global_device_ids=true | all-gather | bytes 1280 | tf_op jit(solution)/shard_map/all_gather | solution.py:200
  9.3 2.2 %collective-permute-start.3 = (f32[32,1536]{1,0:T(8,128)S(1)}, f32[32,1536]{1,0:T(8,128)S(1)}, u32[]{:S(2)}, u32[]{:S(2)}) collective-permute-start(f32[32,1536]{1,0:T(8,128)S(1)} %fusion.12.refs_0_), channel_id=1, source_target_pairs={{0,4},{4,8},{8,12},{12,0},{1,5},{5,9},{9,13},{13,1},{2,6},{6,10},{... | collective-permute-start | bytes 589832 | tf_op jit(solution)/shard_map/ppermute | solution.py:179
  11.5 1.6 collective-permute-start
  14.1 2.9 %collective-permute-start.2 = (f32[32,1536]{1,0:T(8,128)}, f32[32,1536]{1,0:T(8,128)S(1)}, u32[]{:S(2)}, u32[]{:S(2)}) collective-permute-start(f32[32,1536]{1,0:T(8,128)} %refs_0_.3), channel_id=1, source_target_pairs={{0,12},{4,0},{8,4},{12,8},{1,13},{5,1},{9,5},{13,9},{2,14},{6,2},{... | collective-permute-start | bytes 589832 | tf_op jit(solution)/shard_map/ppermute | solution.py:179
  17.0 2.3 %collective-permute-done.3.refs_7_.refs_1_ = f32[32,1536]{1,0:T(8,128)S(1)} collective-permute-done((f32[32,1536]{1,0:T(8,128)S(1)}, f32[32,1536]{1,0:T(8,128)S(1)}, u32[]{:S(2)}, u32[]{:S(2)}) %collective-permute-start.3) | collective-permute-done | bytes 196640 | tf_op jit(solution)/shard_map/ppermute | solution.py:179
  19.3 4.2 %collective-permute-done.refs_1_ = f32[32,1536]{1,0:T(8,128)S(1)} collective-permute-done((f32[32,1536]{1,0:T(8,128)}, f32[32,1536]{1,0:T(8,128)S(1)}, u32[]{:S(2)}, u32[]{:S(2)}) %collective-permute-start) | collective-permute-done | bytes 196640 | tf_op jit(solution)/shard_map/ppermute | solution.py:179
  23.5 8.1 %collective-permute-done.1.refs_2_ = f32[32,1536]{1,0:T(8,128)S(1)} collective-permute-done((f32[32,1536]{1,0:T(8,128)}, f32[32,1536]{1,0:T(8,128)S(1)}, u32[]{:S(2)}, u32[]{:S(2)}) %collective-permute-start.1) | collective-permute-done | bytes 196640 | tf_op jit(solution)/shard_map/ppermute | solution.py:179
  32.6 11.1 %shard_map.64 = (f32[64,3072]{1,0:T(8,128)S(1)}, f32[64,3072]{1,0:T(8,128)S(1)}) custom-call(s32[4]{0:T(128)S(1)} %fusion.14.place_ref, f32[32,1536]{1,0:T(8,128)S(1)} %copy-done, f32[32,1536]{1,0:T(8,128)S(1)} %collective-permute-done.refs_1_, f32[32,1536]{1,0:T(8,128)S(1)} %collective-permute-done.1.refs_2_, ...), custom_call_target="tpu_custom_call" | custom-call | flops 3623878656 | bytes 20447232 | tf_op jit(solution)/shard_map/pallas_call | solution.py:97
  43.7 4.7 %collective-permute-start.5 = (f32[32,1536]{1,0:T(8,128)S(1)}, f32[32,1536]{1,0:T(8,128)S(1)}, u32[]{:S(2)}, u32[]{:S(2)}) collective-permute-start(f32[32,1536]{1,0:T(8,128)S(1)} %collective-permute-done.3.refs_7_.refs_1_), channel_id=1, source_target_pairs={{0,4},{4,8},{8,12},{12,0},{1,5},{5,9},{9,13},{13,1},{2,6},{6,10},{... | collective-permute-start | bytes 589832 | tf_op jit(solution)/shard_map/ppermute | solution.py:179
  48.5 6.4 %collective-permute-done.5.refs_11_.refs_2_ = f32[32,1536]{1,0:T(8,128)S(1)} collective-permute-done((f32[32,1536]{1,0:T(8,128)S(1)}, f32[32,1536]{1,0:T(8,128)S(1)}, u32[]{:S(2)}, u32[]{:S(2)}) %collective-permute-start.5) | collective-permute-done | bytes 196640 | tf_op jit(solution)/shard_map/ppermute | solution.py:179
  55.0 11.1 %shard_map.65 = (f32[64,3072]{1,0:T(8,128)S(1)}, f32[64,3072]{1,0:T(8,128)S(1)}) custom-call(s32[4]{0:T(128)S(1)} %fusion.14.place_ref, f32[32,1536]{1,0:T(8,128)S(1)} %copy-done, f32[32,1536]{1,0:T(8,128)S(1)} %collective-permute-done.refs_1_, f32[32,1536]{1,0:T(8,128)S(1)} %collective-permute-done.1.refs_2_, ...), custom_call_target="tpu_custom_call" | custom-call | flops 3623878656 | bytes 20447232 | tf_op jit(solution)/shard_map/pallas_call | solution.py:97
  66.2 1.6 collective-permute-start.9
  70.2 6.5 %collective-permute-done.8.refs_3_ = f32[32,1536]{1,0:T(8,128)S(1)} collective-permute-done((f32[32,1536]{1,0:T(8,128)S(1)}, f32[32,1536]{1,0:T(8,128)S(1)}, u32[]{:S(2)}, u32[]{:S(2)}) %collective-permute-start.8) | collective-permute-done | bytes 196640 | tf_op jit(solution)/shard_map/ppermute | solution.py:179
  76.6 1.6 collective-permute-done.9.refs_8_
  78.2 10.1 %shard_map.66 = (f32[64,3072]{1,0:T(8,128)S(1)}, f32[64,3072]{1,0:T(8,128)S(1)}) custom-call(s32[4]{0:T(128)S(1)} %fusion.14.place_ref, f32[32,1536]{1,0:T(8,128)S(1)} %fusion.12.refs_0_, f32[32,1536]{1,0:T(8,128)S(1)} %collective-permute-done.3.refs_7_.refs_1_, f32[32,1536]{1,0:T(8,128)S(1)} %collective-permute-done.5.refs_11_.refs_2_, ...), custom_call_target="tpu_custom_call" | custom-call | flops 3623878656 | bytes 20447232 | tf_op jit(solution)/shard_map/pallas_call | solution.py:97
  88.4 10.3 %shard_map.67 = (f32[64,3072]{1,0:T(8,128)S(1)}, f32[64,3072]{1,0:T(8,128)S(1)}) custom-call(s32[4]{0:T(128)S(1)} %fusion.14.place_ref, f32[32,1536]{1,0:T(8,128)S(1)} %fusion.12.refs_0_, f32[32,1536]{1,0:T(8,128)S(1)} %collective-permute-done.3.refs_7_.refs_1_, f32[32,1536]{1,0:T(8,128)S(1)} %collective-permute-done.5.refs_11_.refs_2_, ...), custom_call_target="tpu_custom_call" | custom-call | flops 3623878656 | bytes 20447232 | tf_op jit(solution)/shard_map/pallas_call | solution.py:97
  99.4 1.6 collective-permute-start.16
  101.3 1.6 collective-permute-start.11
  102.9 8.6 %collective-permute-done.16 = f32[32,3072]{1,0:T(8,128)S(1)} collective-permute-done((f32[32,3072]{1,0:T(8,128)S(1)}, f32[32,3072]{1,0:T(8,128)S(1)}, u32[]{:S(2)}, u32[]{:S(2)}) %collective-permute-start.16) | collective-permute-done | bytes 393248 | tf_op jit(solution)/shard_map/ppermute | solution.py:185
  111.6 1.6 collective-permute-start.17
  113.2 6.6 %collective-permute-done.11 = f32[32,3072]{1,0:T(8,128)S(1)} collective-permute-done((f32[32,3072]{1,0:T(8,128)S(1)}, f32[32,3072]{1,0:T(8,128)S(1)}, u32[]{:S(2)}, u32[]{:S(2)}) %collective-permute-start.11) | collective-permute-done | bytes 393248 | tf_op jit(solution)/shard_map/ppermute | solution.py:185
  120.1 1.6 collective-permute-start.12
  121.6 6.6 %collective-permute-done.17.refs_1_ = f32[32,3072]{1,0:T(8,128)S(1)} collective-permute-done((f32[32,3072]{1,0:T(8,128)S(1)}, f32[32,3072]{1,0:T(8,128)S(1)}, u32[]{:S(2)}, u32[]{:S(2)}) %collective-permute-start.17) | collective-permute-done | bytes 393248 | tf_op jit(solution)/shard_map/ppermute | solution.py:185
  128.8 7.0 %collective-permute-done.12.refs_1_ = f32[32,3072]{1,0:T(8,128)S(1)} collective-permute-done((f32[32,3072]{1,0:T(8,128)S(1)}, f32[32,3072]{1,0:T(8,128)S(1)}, u32[]{:S(2)}, u32[]{:S(2)}) %collective-permute-start.12) | collective-permute-done | bytes 393248 | tf_op jit(solution)/shard_map/ppermute | solution.py:185
  135.8 11.2 %shard_map.68 = (f32[32,1536]{1,0:T(8,128)S(1)}, f32[32,1536]{1,0:T(8,128)S(1)}, f32[32,1536]{1,0:T(8,128)S(1)}, f32[32,1536]{1,0:T(8,128)S(1)}) custom-call(s32[4]{0:T(128)S(1)} %fusion.14.place_ref, f32[32,3072]{1,0:T(8,128)S(1)} %fusion.9.refs_0_, f32[32,3072]{1,0:T(8,128)S(1)} %collective-permute-done.17.refs_1_, ...), custom_call_target="tpu_custom_call" | custom-call | flops 3623878656 | bytes 20447232 | tf_op jit(solution)/shard_map/pallas_call | solution.py:145
  147.0 6.8 %shard_map.69 = (f32[32,768]{1,0:T(8,128)S(1)}, f32[32,768]{1,0:T(8,128)S(1)}, f32[32,768]{1,0:T(8,128)S(1)}, f32[32,768]{1,0:T(8,128)S(1)}) custom-call(s32[4]{0:T(128)S(1)} %fusion.14.place_ref, f32[32,3072]{1,0:T(8,128)S(1)} %fusion.4.refs_0_, f32[32,3072]{1,0:T(8,128)S(1)} %collective-permute-done.12.refs_1_, ...), custom_call_target="tpu_custom_call" | custom-call | flops 1811939328 | bytes 10223616 | tf_op jit(solution)/shard_map/pallas_call | solution.py:145
  153.8 1.8 collective-permute-start.20
  156.4 6.8 %shard_map.70 = (f32[32,768]{1,0:T(8,128)S(1)}, f32[32,768]{1,0:T(8,128)S(1)}, f32[32,768]{1,0:T(8,128)S(1)}, f32[32,768]{1,0:T(8,128)S(1)}) custom-call(s32[4]{0:T(128)S(1)} %fusion.14.place_ref, f32[32,3072]{1,0:T(8,128)S(1)} %fusion.4.refs_0_, f32[32,3072]{1,0:T(8,128)S(1)} %collective-permute-done.12.refs_1_, ...), custom_call_target="tpu_custom_call" | custom-call | flops 1811939328 | bytes 10223616 | tf_op jit(solution)/shard_map/pallas_call | solution.py:145
  163.2 3.6 %collective-permute-start.23 = (f32[32,768]{1,0:T(8,128)S(1)}, f32[32,768]{1,0:T(8,128)S(1)}, u32[]{:S(2)}, u32[]{:S(2)}) collective-permute-start(f32[32,768]{1,0:T(8,128)S(1)} %get-tuple-element.42), channel_id=1, source_target_pairs={{0,12},{4,0},{8,4},{12,8},{1,13},{5,1},{9,5},{13,9},{2,14},{6,2},{... | collective-permute-start | bytes 294920 | tf_op jit(solution)/shard_map/ppermute | solution.py:179
  167.8 2.2 %collective-permute-done.23 = f32[32,768]{1,0:T(8,128)S(1)} collective-permute-done((f32[32,768]{1,0:T(8,128)S(1)}, f32[32,768]{1,0:T(8,128)S(1)}, u32[]{:S(2)}, u32[]{:S(2)}) %collective-permute-start.23) | collective-permute-done | bytes 98336 | tf_op jit(solution)/shard_map/ppermute | solution.py:179
  170.0 6.2 %collective-permute-done.24 = f32[32,768]{1,0:T(8,128)S(1)} collective-permute-done((f32[32,768]{1,0:T(8,128)S(1)}, f32[32,768]{1,0:T(8,128)S(1)}, u32[]{:S(2)}, u32[]{:S(2)}) %collective-permute-start.24) | collective-permute-done | bytes 98336 | tf_op jit(solution)/shard_map/ppermute | solution.py:179
  176.5 6.2 %psum.7 = f32[2,32]{1,0:T(2,128)S(1)} all-reduce(f32[2,32]{1,0:T(2,128)S(1)} %pad_maximum_fusion), channel_id=1, replica_groups=mesh['groups'=2,'hid'=4,'emb'=4] {'emb'}, use_global_device_ids=true, to_apply=%region_6.7 | all-reduce | flops 64 | bytes 512 | tf_op jit(solution)/shard_map/psum | solution.py:250
  (73 shorter events, 12.7 us)
Async XLA Ops:
  8.3 5.9 %copy-start.6 = (f32[32]{0:T(128)}, f32[32]{0:T(128)S(1)}, u32[]{:S(2)}) copy-start(f32[32]{0:T(128)S(1)} %add_rsqrt_fusion) | copy-start | bytes 388
  9.3 10.1 %collective-permute-start.3 = (f32[32,1536]{1,0:T(8,128)S(1)}, f32[32,1536]{1,0:T(8,128)S(1)}, u32[]{:S(2)}, u32[]{:S(2)}) collective-permute-start(f32[32,1536]{1,0:T(8,128)S(1)} %fusion.12.refs_0_), channel_id=1, source_target_pairs={{0,4},{4,8},{8,12},{12,0},{1,5},{5,9},{9,13},{13,1},{2,6},{6,10},{... | collective-permute-start | bytes 589832 | tf_op jit(solution)/shard_map/ppermute | solution.py:179
  11.5 12.0 %collective-permute-start = (f32[32,1536]{1,0:T(8,128)}, f32[32,1536]{1,0:T(8,128)S(1)}, u32[]{:S(2)}, u32[]{:S(2)}) collective-permute-start(f32[32,1536]{1,0:T(8,128)} %refs_0_.3), channel_id=1, source_target_pairs={{0,4},{4,8},{8,12},{12,0},{1,5},{5,9},{9,13},{13,1},{2,6},{6,10},{... | collective-permute-start | bytes 589832 | tf_op jit(solution)/shard_map/ppermute | solution.py:179
  13.0 18.6 %collective-permute-start.1 = (f32[32,1536]{1,0:T(8,128)}, f32[32,1536]{1,0:T(8,128)S(1)}, u32[]{:S(2)}, u32[]{:S(2)}) collective-permute-start(f32[32,1536]{1,0:T(8,128)} %refs_0_.3), channel_id=1, source_target_pairs={{0,8},{4,12},{8,0},{12,4},{1,9},{5,13},{9,1},{13,5},{2,10},{6,14},... | collective-permute-start | bytes 589832 | tf_op jit(solution)/shard_map/ppermute | solution.py:179
  14.1 17.5 %collective-permute-start.2 = (f32[32,1536]{1,0:T(8,128)}, f32[32,1536]{1,0:T(8,128)S(1)}, u32[]{:S(2)}, u32[]{:S(2)}) collective-permute-start(f32[32,1536]{1,0:T(8,128)} %refs_0_.3), channel_id=1, source_target_pairs={{0,12},{4,0},{8,4},{12,8},{1,13},{5,1},{9,5},{13,9},{2,14},{6,2},{... | collective-permute-start | bytes 589832 | tf_op jit(solution)/shard_map/ppermute | solution.py:179
  43.6 4.8 %collective-permute-start.4 = (f32[64,3072]{1,0:T(8,128)S(1)}, f32[64,3072]{1,0:T(8,128)S(1)}, u32[]{:S(2)}, u32[]{:S(2)}) collective-permute-start(f32[64,3072]{1,0:T(8,128)S(1)} %get-tuple-element.26), channel_id=1, source_target_pairs={{0,1},{1,0},{2,3},{3,2},{4,5},{5,4},{6,7},{7,6},{8,9},{9,8},{10,11... | collective-permute-start | bytes 2359304 | tf_op jit(solution)/shard_map/ppermute | solution.py:182
  43.7 11.3 %collective-permute-start.5 = (f32[32,1536]{1,0:T(8,128)S(1)}, f32[32,1536]{1,0:T(8,128)S(1)}, u32[]{:S(2)}, u32[]{:S(2)}) collective-permute-start(f32[32,1536]{1,0:T(8,128)S(1)} %collective-permute-done.3.refs_7_.refs_1_), channel_id=1, source_target_pairs={{0,4},{4,8},{8,12},{12,0},{1,5},{5,9},{9,13},{13,1},{2,6},{6,10},{... | collective-permute-start | bytes 589832 | tf_op jit(solution)/shard_map/ppermute | solution.py:179
  66.1 2.4 %collective-permute-start.6 = (f32[64,3072]{1,0:T(8,128)S(1)}, f32[64,3072]{1,0:T(8,128)S(1)}, u32[]{:S(2)}, u32[]{:S(2)}) collective-permute-start(f32[64,3072]{1,0:T(8,128)S(1)} %get-tuple-element.28), channel_id=1, source_target_pairs={{0,1},{1,0},{2,3},{3,2},{4,5},{5,4},{6,7},{7,6},{8,9},{9,8},{10,11... | collective-permute-start | bytes 2359304 | tf_op jit(solution)/shard_map/ppermute | solution.py:182
  66.2 12.0 %collective-permute-start.9 = (f32[32,3072]{1,0:T(8,128)S(1)}, f32[32,3072]{1,0:T(8,128)S(1)}, u32[]{:S(2)}, u32[]{:S(2)}) collective-permute-start(f32[32,3072]{1,0:T(8,128)S(1)} %slice.55), channel_id=1, source_target_pairs={{0,2},{1,3},{2,0},{3,1},{4,6},{5,7},{6,4},{7,5},{8,10},{9,11},{10,... | collective-permute-start | bytes 1179656 | tf_op jit(solution)/shard_map/ppermute | solution.py:185
  67.8 8.8 %collective-permute-start.8 = (f32[32,1536]{1,0:T(8,128)S(1)}, f32[32,1536]{1,0:T(8,128)S(1)}, u32[]{:S(2)}, u32[]{:S(2)}) collective-permute-start(f32[32,1536]{1,0:T(8,128)S(1)} %collective-permute-done.5.refs_11_.refs_2_), channel_id=1, source_target_pairs={{0,4},{4,8},{8,12},{12,0},{1,5},{5,9},{9,13},{13,1},{2,6},{6,10},{... | collective-permute-start | bytes 589832 | tf_op jit(solution)/shard_map/ppermute | solution.py:179
  68.6 19.7 %collective-permute-start.7 = (f32[32,3072]{1,0:T(8,128)S(1)}, f32[32,3072]{1,0:T(8,128)S(1)}, u32[]{:S(2)}, u32[]{:S(2)}) collective-permute-start(f32[32,3072]{1,0:T(8,128)S(1)} %slice.53), channel_id=1, source_target_pairs={{0,2},{1,3},{2,0},{3,1},{4,6},{5,7},{6,4},{7,5},{8,10},{9,11},{10,... | collective-permute-start | bytes 1179656 | tf_op jit(solution)/shard_map/ppermute | solution.py:185
  88.3 10.9 %collective-permute-start.15 = (f32[64,3072]{1,0:T(8,128)S(1)}, f32[64,3072]{1,0:T(8,128)S(1)}, u32[]{:S(2)}, u32[]{:S(2)}) collective-permute-start(f32[64,3072]{1,0:T(8,128)S(1)} %get-tuple-element.32), channel_id=1, source_target_pairs={{0,1},{1,0},{2,3},{3,2},{4,5},{5,4},{6,7},{7,6},{8,9},{9,8},{10,11... | collective-permute-start | bytes 2359304 | tf_op jit(solution)/shard_map/ppermute | solution.py:182
  88.4 12.6 %copy-start.3 = (f32[6144]{0:T(1024)S(1)}, f32[6144]{0:T(1024)}, u32[]{:S(2)}) copy-start(f32[6144]{0:T(1024)} %param.9) | copy-start | bytes 73732
  98.7 2.4 %collective-permute-start.10 = (f32[64,3072]{1,0:T(8,128)S(1)}, f32[64,3072]{1,0:T(8,128)S(1)}, u32[]{:S(2)}, u32[]{:S(2)}) collective-permute-start(f32[64,3072]{1,0:T(8,128)S(1)} %get-tuple-element.31), channel_id=1, source_target_pairs={{0,1},{1,0},{2,3},{3,2},{4,5},{5,4},{6,7},{7,6},{8,9},{9,8},{10,11... | collective-permute-start | bytes 2359304 | tf_op jit(solution)/shard_map/ppermute | solution.py:182
  99.4 12.0 %collective-permute-start.16 = (f32[32,3072]{1,0:T(8,128)S(1)}, f32[32,3072]{1,0:T(8,128)S(1)}, u32[]{:S(2)}, u32[]{:S(2)}) collective-permute-start(f32[32,3072]{1,0:T(8,128)S(1)} %slice.59), channel_id=1, source_target_pairs={{0,2},{1,3},{2,0},{3,1},{4,6},{5,7},{6,4},{7,5},{8,10},{9,11},{10,... | collective-permute-start | bytes 1179656 | tf_op jit(solution)/shard_map/ppermute | solution.py:185
  101.3 18.6 %collective-permute-start.11 = (f32[32,3072]{1,0:T(8,128)S(1)}, f32[32,3072]{1,0:T(8,128)S(1)}, u32[]{:S(2)}, u32[]{:S(2)}) collective-permute-start(f32[32,3072]{1,0:T(8,128)S(1)} %slice.56), channel_id=1, source_target_pairs={{0,2},{1,3},{2,0},{3,1},{4,6},{5,7},{6,4},{7,5},{8,10},{9,11},{10,... | collective-permute-start | bytes 1179656 | tf_op jit(solution)/shard_map/ppermute | solution.py:185
  111.6 16.6 %collective-permute-start.17 = (f32[32,3072]{1,0:T(8,128)S(1)}, f32[32,3072]{1,0:T(8,128)S(1)}, u32[]{:S(2)}, u32[]{:S(2)}) collective-permute-start(f32[32,3072]{1,0:T(8,128)S(1)} %fusion.9.refs_0_), channel_id=1, source_target_pairs={{0,2},{1,3},{2,0},{3,1},{4,6},{5,7},{6,4},{7,5},{8,10},{9,11},{10,... | collective-permute-start | bytes 1179656 | tf_op jit(solution)/shard_map/ppermute | solution.py:185
  120.1 15.7 %collective-permute-start.12 = (f32[32,3072]{1,0:T(8,128)S(1)}, f32[32,3072]{1,0:T(8,128)S(1)}, u32[]{:S(2)}, u32[]{:S(2)}) collective-permute-start(f32[32,3072]{1,0:T(8,128)S(1)} %fusion.4.refs_0_), channel_id=1, source_target_pairs={{0,2},{1,3},{2,0},{3,1},{4,6},{5,7},{6,4},{7,5},{8,10},{9,11},{10,... | collective-permute-start | bytes 1179656 | tf_op jit(solution)/shard_map/ppermute | solution.py:185
  121.6 14.2 %collective-permute-start.18 = (f32[32,3072]{1,0:T(8,128)S(1)}, f32[32,3072]{1,0:T(8,128)S(1)}, u32[]{:S(2)}, u32[]{:S(2)}) collective-permute-start(f32[32,3072]{1,0:T(8,128)S(1)} %fusion.9.refs_0_), channel_id=1, source_target_pairs={{0,1},{1,0},{2,3},{3,2},{4,5},{5,4},{6,7},{7,6},{8,9},{9,8},{10,11... | collective-permute-start | bytes 1179656 | tf_op jit(solution)/shard_map/ppermute | solution.py:182
  128.3 7.5 %collective-permute-start.19 = (f32[32,3072]{1,0:T(8,128)S(1)}, f32[32,3072]{1,0:T(8,128)S(1)}, u32[]{:S(2)}, u32[]{:S(2)}) collective-permute-start(f32[32,3072]{1,0:T(8,128)S(1)} %collective-permute-done.17.refs_1_), channel_id=1, source_target_pairs={{0,1},{1,0},{2,3},{3,2},{4,5},{5,4},{6,7},{7,6},{8,9},{9,8},{10,11... | collective-permute-start | bytes 1179656 | tf_op jit(solution)/shard_map/ppermute | solution.py:182
  128.3 18.7 %collective-permute-start.13 = (f32[32,3072]{1,0:T(8,128)S(1)}, f32[32,3072]{1,0:T(8,128)S(1)}, u32[]{:S(2)}, u32[]{:S(2)}) collective-permute-start(f32[32,3072]{1,0:T(8,128)S(1)} %fusion.4.refs_0_), channel_id=1, source_target_pairs={{0,1},{1,0},{2,3},{3,2},{4,5},{5,4},{6,7},{7,6},{8,9},{9,8},{10,11... | collective-permute-start | bytes 1179656 | tf_op jit(solution)/shard_map/ppermute | solution.py:182
  135.8 11.2 %collective-permute-start.14 = (f32[32,3072]{1,0:T(8,128)S(1)}, f32[32,3072]{1,0:T(8,128)S(1)}, u32[]{:S(2)}, u32[]{:S(2)}) collective-permute-start(f32[32,3072]{1,0:T(8,128)S(1)} %collective-permute-done.12.refs_1_), channel_id=1, source_target_pairs={{0,1},{1,0},{2,3},{3,2},{4,5},{5,4},{6,7},{7,6},{8,9},{9,8},{10,11... | collective-permute-start | bytes 1179656 | tf_op jit(solution)/shard_map/ppermute | solution.py:182
  153.8 13.6 %collective-permute-start.20 = (f32[32,768]{1,0:T(8,128)S(1)}, f32[32,768]{1,0:T(8,128)S(1)}, u32[]{:S(2)}, u32[]{:S(2)}) collective-permute-start(f32[32,768]{1,0:T(8,128)S(1)} %get-tuple-element.38), channel_id=1, source_target_pairs={{0,12},{4,0},{8,4},{12,8},{1,13},{5,1},{9,5},{13,9},{2,14},{6,2},{... | collective-permute-start | bytes 294920 | tf_op jit(solution)/shard_map/ppermute | solution.py:179
  155.6 12.1 %collective-permute-start.21 = (f32[32,768]{1,0:T(8,128)S(1)}, f32[32,768]{1,0:T(8,128)S(1)}, u32[]{:S(2)}, u32[]{:S(2)}) collective-permute-start(f32[32,768]{1,0:T(8,128)S(1)} %get-tuple-element.39), channel_id=1, source_target_pairs={{0,8},{4,12},{8,0},{12,4},{1,9},{5,13},{9,1},{13,5},{2,10},{6,14},... | collective-permute-start | bytes 294920 | tf_op jit(solution)/shard_map/ppermute | solution.py:179
  156.1 11.7 %collective-permute-start.22 = (f32[32,768]{1,0:T(8,128)S(1)}, f32[32,768]{1,0:T(8,128)S(1)}, u32[]{:S(2)}, u32[]{:S(2)}) collective-permute-start(f32[32,768]{1,0:T(8,128)S(1)} %get-tuple-element.40), channel_id=1, source_target_pairs={{0,4},{4,8},{8,12},{12,0},{1,5},{5,9},{9,13},{13,1},{2,6},{6,10},{... | collective-permute-start | bytes 294920 | tf_op jit(solution)/shard_map/ppermute | solution.py:179
  156.4 19.8 %copy-start.1 = (f32[32,1536]{1,0:T(8,128)S(1)}, f32[32,1536]{1,0:T(8,128)}, u32[]{:S(2)}) copy-start(f32[32,1536]{1,0:T(8,128)} %param.6) | copy-start | bytes 589828
  156.4 19.9 %copy-start.2 = (f32[1536]{0:T(1024)S(1)}, f32[1536]{0:T(1024)}, u32[]{:S(2)}) copy-start(f32[1536]{0:T(1024)} %param.11) | copy-start | bytes 18436
  156.4 19.9 %copy-start.5 = (f32[32]{0:T(128)S(1)}, f32[32]{0:T(128)}, u32[]{:S(2)}) copy-start(f32[32]{0:T(128)} %copy-done.4) | copy-start | bytes 388
  156.4 19.9 %copy-start.7 = (f32[32]{0:T(128)S(1)}, f32[32]{0:T(128)}, u32[]{:S(2)}) copy-start(f32[32]{0:T(128)} %copy-done.6) | copy-start | bytes 388
  163.2 6.8 %collective-permute-start.23 = (f32[32,768]{1,0:T(8,128)S(1)}, f32[32,768]{1,0:T(8,128)S(1)}, u32[]{:S(2)}, u32[]{:S(2)}) collective-permute-start(f32[32,768]{1,0:T(8,128)S(1)} %get-tuple-element.42), channel_id=1, source_target_pairs={{0,12},{4,0},{8,4},{12,8},{1,13},{5,1},{9,5},{13,9},{2,14},{6,2},{... | collective-permute-start | bytes 294920 | tf_op jit(solution)/shard_map/ppermute | solution.py:179
  166.8 9.4 %collective-permute-start.24 = (f32[32,768]{1,0:T(8,128)S(1)}, f32[32,768]{1,0:T(8,128)S(1)}, u32[]{:S(2)}, u32[]{:S(2)}) collective-permute-start(f32[32,768]{1,0:T(8,128)S(1)} %get-tuple-element.43), channel_id=1, source_target_pairs={{0,8},{4,12},{8,0},{12,4},{1,9},{5,13},{9,1},{13,5},{2,10},{6,14},... | collective-permute-start | bytes 294920 | tf_op jit(solution)/shard_map/ppermute | solution.py:179
  167.5 8.7 %collective-permute-start.25 = (f32[32,768]{1,0:T(8,128)S(1)}, f32[32,768]{1,0:T(8,128)S(1)}, u32[]{:S(2)}, u32[]{:S(2)}) collective-permute-start(f32[32,768]{1,0:T(8,128)S(1)} %get-tuple-element.44), channel_id=1, source_target_pairs={{0,4},{4,8},{8,12},{12,0},{1,5},{5,9},{9,13},{13,1},{2,6},{6,10},{... | collective-permute-start | bytes 294920 | tf_op jit(solution)/shard_map/ppermute | solution.py:179
  (2 other events, 5.8 us)

commit v4 on v1

v4 whole, which is shorter than its diff:
```python
import functools
import math

import jax
import jax.numpy as jnp
from jax import lax
from jax.experimental import pallas as pl
from jax.experimental.pallas import tpu as pltpu
from jax.sharding import PartitionSpec as P

VMEM_LIMIT = 6 * 1024 * 1024
CHUNKS = 2


def gelu_slope(values):
    cdf = 0.5 * (1.0 + lax.erf(values * (1.0 / math.sqrt(2.0))))
    density = jnp.exp(-0.5 * values * values) * (1.0 / math.sqrt(2.0 * math.pi))
    return cdf + values * density


def split(values):
    high = values.astype(jnp.bfloat16)
    return high, (values - high.astype(jnp.float32)).astype(jnp.bfloat16)


def divisor(extent, *choices):
    return next(c for c in choices if extent % c == 0)


def prepare_kernel(rows, columns, block, depth, weight_ref, *refs):
    high_ref, low_ref, landed, arrived = refs[-4:]
    steps = rows[1] // block

    def fetch(step):
        start = pl.multiple_of(rows[0] + step * block, block)
        slot = lax.rem(step, depth)
        return pltpu.make_async_copy(
            weight_ref.at[pl.ds(start, block), pl.ds(*columns)], landed.at[slot], arrived.at[slot]
        )

    for step in range(min(depth, steps)):
        fetch(step).start()

    @pl.loop(0, steps)
    def _(step):
        fetch(step).wait()
        high, low = split(landed[lax.rem(step, depth)])
        at = pl.ds(pl.multiple_of(step * block, block), block)
        high_ref[at, :] = high
        low_ref[at, :] = low

        @pl.when(step + depth < steps)
        def _():
            fetch(step + depth).start()


def prepare(weight, rows, columns, after):
    block = 128 * 1536 // columns[1]
    block = divisor(rows[1], *[b for b in (256, 128, 64, 32) if b <= max(block, 32)])
    depth = 4
    out = pltpu.VMEM((rows[1], columns[1]), jnp.bfloat16)
    return pl.pallas_call(
        functools.partial(prepare_kernel, rows, columns, block, depth),
        out_shape=(out, out),
        in_specs=[pl.BlockSpec(memory_space=pl.ANY)] * (1 + len(after)),
        out_specs=[pl.BlockSpec(memory_space=pltpu.VMEM)] * 2,
        scratch_shapes=[
            pltpu.VMEM((depth, block, columns[1]), jnp.float32),
            pltpu.SemaphoreType.DMA((depth,)),
        ],
        compiler_params=pltpu.CompilerParams(vmem_limit_bytes=VMEM_LIMIT),
        cost_estimate=pl.CostEstimate(
            flops=0, bytes_accessed=4 * rows[1] * columns[1], transcendentals=0
        ),
    )(weight, *after)


def three_pass(both, high, low, contract):
    rows = both.shape[0] // 2
    dot = functools.partial(
        lax.dot_general,
        dimension_numbers=(((1,), (contract,)), ((), ())),
        preferred_element_type=jnp.float32,
    )
    first = dot(both[...], high)
    return first[:rows] + first[rows:] + dot(both[:rows, :], low)


def forward_kernel(slots, contract, place_ref, *refs):
    slot_refs, (high_ref, low_ref) = refs[:slots], refs[slots : slots + 2]
    send_ref, keep_ref, both = refs[-3:]
    block = slot_refs[0].shape[0]
    total = block * slots
    for b in range(slots):
        high, low = split(slot_refs[b][...])
        row = pl.multiple_of(place_ref[b] * block, block)
        both[pl.ds(row, block), :] = high
        both[pl.ds(total + row, block), :] = low

    hidden = send_ref.shape[1]
    width = divisor(hidden, 256, 128)

    @pl.loop(0, hidden // width)
    def _(step):
        at = pl.ds(pl.multiple_of(step * width, width), width)
        tile = (slice(None), at) if contract == 0 else (at, slice(None))
        part = three_pass(both, high_ref[tile], low_ref[tile], contract)
        keep_ref[:, at] = part[: total // 2]
        send_ref[:, at] = part[total // 2 :]


def forward(blocks, weight, place, by_column, after):
    slots, (block, depth) = len(blocks), blocks[0].shape
    hidden = weight[0].shape[1 if by_column else 0]
    half = block * slots // 2
    out = jax.ShapeDtypeStruct((half, hidden), jnp.float32)
    inside = pl.BlockSpec(memory_space=pltpu.VMEM)
    return pl.pallas_call(
        functools.partial(forward_kernel, slots, 0 if by_column else 1),
        out_shape=(out, out),
        in_specs=[pl.BlockSpec(memory_space=pltpu.SMEM)]
        + [inside] * (slots + 2)
        + [pl.BlockSpec(memory_space=pl.ANY)] * len(after),
        out_specs=[inside] * 2,
        scratch_shapes=[pltpu.VMEM((2 * block * slots, depth), jnp.bfloat16)],
        compiler_params=pltpu.CompilerParams(vmem_limit_bytes=VMEM_LIMIT),
        cost_estimate=pl.CostEstimate(
            flops=6 * block * slots * depth * hidden, bytes_accessed=4 * depth * hidden, transcendentals=0
        ),
    )(place, *blocks, *[pltpu.with_memory_space_constraint(part, pltpu.VMEM) for part in weight], *after)


def backward_kernel(slots, earlier, first_column, place_ref, *refs):
    act_refs, (high_ref, low_ref) = refs[:slots], refs[slots : slots + 2]
    earlier_refs = refs[slots + 2 : slots + 2 + earlier]
    out_refs = refs[-2 - slots : -2]
    both, result = refs[-2:]
    block = act_refs[0].shape[0]
    total = block * slots
    for p in range(slots):
        high, low = split(act_refs[p][...])
        both[p * block : (p + 1) * block, :] = high
        both[total + p * block : total + (p + 1) * block, :] = low

    depth = out_refs[0].shape[1]
    width = result.shape[1]

    @pl.loop(0, depth // width)
    def _(step):
        start = pl.multiple_of(step * width, width)
        tile = (pl.ds(pl.multiple_of(first_column + start, width), width), slice(None))
        result[...] = three_pass(both, high_ref[tile], low_ref[tile], 1)
        for b in range(slots):
            row = pl.multiple_of(place_ref[b] * block, block)
            rows = result[pl.ds(row, block), :]
            if earlier:
                rows = rows + earlier_refs[b][:, pl.ds(pl.multiple_of(first_column + start, width), width)]
            out_refs[b][:, pl.ds(start, width)] = rows


def backward(acts, weight, place, earlier, part, parts, after):
    slots, (block, hidden) = len(acts), acts[0].shape
    depth = weight[0].shape[0] // parts
    width = divisor(depth, 256, 128)
    out = jax.ShapeDtypeStruct((block, depth), jnp.float32)
    inside = pl.BlockSpec(memory_space=pltpu.VMEM)
    return pl.pallas_call(
        functools.partial(backward_kernel, slots, len(earlier), part * depth),
        out_shape=[out] * slots,
        in_specs=[pl.BlockSpec(memory_space=pltpu.SMEM)]
        + [inside] * (slots + 2 + len(earlier))
        + [pl.BlockSpec(memory_space=pl.ANY)] * len(after),
        out_specs=[inside] * slots,
        scratch_shapes=[
            pltpu.VMEM((2 * block * slots, hidden), jnp.bfloat16),
            pltpu.VMEM((block * slots, width), jnp.float32),
        ],
        compiler_params=pltpu.CompilerParams(vmem_limit_bytes=VMEM_LIMIT),
        cost_estimate=pl.CostEstimate(
            flops=6 * block * slots * depth * hidden, bytes_accessed=4 * depth * hidden, transcendentals=0
        ),
    )(place, *acts, *[pltpu.with_memory_space_constraint(part, pltpu.VMEM) for part in weight], *earlier, *after)


def body(hid_size, emb_size, inputs, out_grad, in_weight, in_bias, out_weight, norm_gain):
    chips = emb_size // 2
    tokens, depth = inputs.shape
    model_width = depth * emb_size
    hidden = in_weight.shape[1]
    me = lax.axis_index("emb")
    chip, core = me // 2, me % 2

    def along_hid(values, steps=1):
        return lax.ppermute(values, "hid", [(i, (i + steps) % hid_size) for i in range(hid_size)])

    def other_core(values):
        return lax.ppermute(values, "emb", [(i, i ^ 1) for i in range(emb_size)])

    def next_chip(values):
        return lax.ppermute(values, "emb", [(i, (i + 2) % emb_size) for i in range(emb_size)])

    owner = jnp.arange(emb_size, dtype=jnp.int32)
    place = ((owner % 2) ^ core) * chips + (owner // 2 - chip) % chips

    def gathered(values):
        blocks = [values]
        for _ in range(hid_size - 1):
            blocks.append(along_hid(blocks[-1]))
        return blocks

    grads = [out_grad] + [along_hid(out_grad, step) for step in range(1, hid_size)]

    local_mean = jnp.mean(inputs, axis=-1, keepdims=True)
    local_square = jnp.sum(jnp.square(inputs - local_mean), axis=-1)
    stats = lax.all_gather(jnp.stack([local_mean[:, 0], local_square]), "emb")
    row_mean = jnp.mean(stats[:, 0], axis=0)
    spread = jnp.sum(stats[:, 1] + depth * jnp.square(stats[:, 0] - row_mean), axis=0)
    inv_std = (1.0 / jnp.sqrt(spread / model_width + 1e-06))[:, None]
    normed = (inputs - row_mean[:, None]) * inv_std
    scaled = gathered(normed * norm_gain)

    def halved(partial):
        send, keep = partial
        return keep + other_core(send)

    def exchanged(summed):
        terms = [summed[d * tokens : (d + 1) * tokens] for d in range(chips)]
        arrival = next_chip(terms[chips - 1])
        for step in range(2, chips):
            arrival = next_chip(arrival + terms[chips - step])
        return arrival, terms[0]

    piece = hidden // CHUNKS
    out_parts = [prepare(out_weight, (c * piece, piece), (0, depth), [scaled[0]]) for c in range(CHUNKS)]
    back_0 = forward(grads, out_parts[0], place, False, [scaled[1], out_parts[1][0]])
    half_0 = halved(back_0)
    back_1 = forward(grads, out_parts[1], place, False, [back_0[1]])
    half_1 = halved(back_1)
    back_0, back_1 = exchanged(half_0), exchanged(half_1)
    in_parts_0 = prepare(in_weight, (0, depth), (0, piece), [half_0, scaled[hid_size // 2]])
    pre_0 = forward(scaled, in_parts_0, place, True, [half_1])
    in_parts_1 = prepare(in_weight, (0, depth), (piece, piece), [pre_0[1], back_0[0]])
    pre_1 = forward(scaled, in_parts_1, place, True, [back_1[0]])
    backs = [back_0, back_1]
    pres = [exchanged(halved(pre_0)), exchanged(halved(pre_1))]

    def spread_out(c):
        act = sum(backs[c]) * gelu_slope(sum(pres[c]) + in_bias[c * piece : (c + 1) * piece])
        mine = [None] * chips
        mine[0] = act
        for step in range(1, chips):
            act = next_chip(act)
            mine[(chips - step) % chips] = act
        return mine + [other_core(block) for block in mine]

    def summed_along_hid(sums):
        return sum([along_hid(sums[step], -step) for step in range(1, hid_size)], start=sums[0])

    acts_0, acts_1 = spread_out(0), spread_out(1)
    sums = backward(acts_0, in_parts_0, place, (), 0, 1, [pre_1[1]])
    parts = 2 if depth % 512 == 0 else 1
    ends = []
    for part in range(parts):
        ends.append(backward(acts_1, in_parts_1, place, sums, part, parts, [ends[-1][0] if ends else sums[0]]))
    running = jnp.concatenate([summed_along_hid(end) for end in ends], axis=1)
    normed_grad = running * norm_gain
    totals = lax.psum(
        jnp.stack([jnp.sum(normed_grad, axis=-1), jnp.sum(normed_grad * normed, axis=-1)]), "emb"
    )
    first, second = (totals / model_width)[:, :, None]
    return inv_std * (normed_grad - first - normed * second)


def solution(mesh):
    hid_size, emb_size = mesh.shape["hid"], mesh.shape["emb"]
    assert hid_size == emb_size and emb_size % 2 == 0
    return jax.shard_map(
        functools.partial(body, hid_size, emb_size),
        mesh=mesh,
        in_specs=(
            P(("groups", "hid"), "emb"),
            P(("groups", "hid"), "emb"),
            P("emb", "hid"),
            P("hid"),
            P("hid", "emb"),
            P("emb"),
        ),
        out_specs=P(("groups", "hid"), "emb"),
        check_vma=False,
    )
```

time: 189 us -> 195 us (1.032)
  waiting for transfers between devices: 91.6 us -> 46.1 us
  local copies, waits for them, and re-layouts: 0.14 us -> 25.8 us
  Pallas kernels: 65.1 us -> 78.2 us
  starting transfers between devices: 14.2 us -> 26.8 us
    ppermute x9 -> x12, waiting for transfers between devices: 47.7 us -> 17 us  [along_hid(): lax.ppermute(values, 'hid', [(i, (i + steps) % hid_size) for i in range(h...]
    pallas_call x2 -> x7, Pallas kernels: 22.2 us -> 49.7 us  [the longest x4 35.1 us: prepare(): pl.pallas_call(functools.partial(prepare_kernel, rows, columns, block, de...]
    unnamed x8 -> x24, local copies, waits for them, and re-layouts: 0.02 us -> 25.6 us
    ppermute x6, waiting for transfers between devices: 43.9 us -> 28.9 us  [next_chip(): lax.ppermute(values, 'emb', [(i, (i + 2) % emb_size) for i in range(emb_s...]
    pallas_call x4, Pallas kernels: 42.9 us -> 28.4 us  [forward(): pl.pallas_call(functools.partial(forward_kernel, slots, 0 if by_column el...]
    ppermute x9 -> x12, starting transfers between devices: 4.57 us -> 16.6 us  [along_hid(): lax.ppermute(values, 'hid', [(i, (i + steps) % hid_size) for i in range(h...]
  transfers between devices with their start and end apart: 23 -> 26, of which waited for: 14 -> 9; matrix products, arithmetic and copies ran while one was open for 1% -> 1% of each run, Pallas kernels for 29% -> 34%
where the time goes in v4:
time: 195 us
  Pallas kernels  78.2 us (40%)
  waiting for transfers between devices  46.1 us (24%)
  starting transfers between devices  26.8 us (14%)
  local copies, waits for them, and re-layouts  25.8 us (13%)
  blocking collectives  12.4 us (6%)
  other arithmetic  5.19 us (3%)
    pallas_call x4, Pallas kernels, prepare(): pl.pallas_call(functools.partial(prepare_kernel, rows, columns, block, de...  35.1 us
    ppermute x6, waiting for transfers between devices, next_chip(): lax.ppermute(values, 'emb', [(i, (i + 2) % emb_size) for i in range(emb_s...  28.9 us
    pallas_call x4, Pallas kernels, forward(): pl.pallas_call(functools.partial(forward_kernel, slots, 0 if by_column el...  28.4 us
    unnamed x24, local copies, waits for them, and re-layouts  25.6 us
    ppermute x12, waiting for transfers between devices, along_hid(): lax.ppermute(values, 'hid', [(i, (i + steps) % hid_size) for i in range(h...  17 us
    ppermute x12, starting transfers between devices, along_hid(): lax.ppermute(values, 'hid', [(i, (i + steps) % hid_size) for i in range(h...  16.6 us
    pallas_call x3, Pallas kernels, backward(): pl.pallas_call(functools.partial(backward_kernel, slots, len(earlier), pa...  14.7 us
    ppermute x6, starting transfers between devices, next_chip(): lax.ppermute(values, 'emb', [(i, (i + 2) % emb_size) for i in range(emb_s...  8.39 us
  transfers between devices with their start and end apart: 26, of which 9 were waited for; matrix products, arithmetic and copies ran while one was open for 1% of the time, Pallas kernels for 34%

profile of v4, /device:TPU:0, one launch (start us, length us, event | category | flops | bytes accessed | tf_op | source)
XLA Modules:
  0.0 194.8 jit_solution(3266962414616835126)
XLA Ops:
  2.2 6.0 %all-gather.1 = f32[4,2,32]{2,1,0:T(2,128)S(1)} all-gather(f32[1,2,32]{2,1,0:T(2,128)S(1)} %maximum_bitcast_fusion), channel_id=2, replica_groups=mesh['groups'=2,'hid'=4,'emb'=4] {'emb'}, dimensions={0}, use_global_device_ids=true | all-gather | bytes 1280 | tf_op jit(solution)/shard_map/all_gather | solution.py:215
  9.3 2.2 %collective-permute-start.3 = (f32[32,1536]{1,0:T(8,128)S(1)}, f32[32,1536]{1,0:T(8,128)S(1)}, u32[]{:S(2)}, u32[]{:S(2)}) collective-permute-start(f32[32,1536]{1,0:T(8,128)S(1)} %fusion.12.refs_0_), channel_id=1, source_target_pairs={{0,4},{4,8},{8,12},{12,0},{1,5},{5,9},{9,13},{13,1},{2,6},{6,10},{... | collective-permute-start | bytes 589832 | tf_op jit(solution)/shard_map/ppermute | solution.py:194
  11.4 2.1 %collective-permute-start.2 = (f32[32,1536]{1,0:T(8,128)}, f32[32,1536]{1,0:T(8,128)S(1)}, u32[]{:S(2)}, u32[]{:S(2)}) collective-permute-start(f32[32,1536]{1,0:T(8,128)} %refs_0_.3), channel_id=1, source_target_pairs={{0,12},{4,0},{8,4},{12,8},{1,13},{5,1},{9,5},{13,9},{2,14},{6,2},{... | collective-permute-start | bytes 589832 | tf_op jit(solution)/shard_map/ppermute | solution.py:194
  14.5 1.6 collective-permute-start
  16.1 8.7 %shard_map.65 = (bf16[3072,1536]{1,0:T(8,128)(2,1)S(1)}, bf16[3072,1536]{1,0:T(8,128)(2,1)S(1)}) custom-call(f32[6144,1536]{1,0:T(8,128)} %weight_ref.5, f32[32,1536]{1,0:T(8,128)S(1)} %fusion.12.refs_0_), custom_call_target="tpu_custom_call" | custom-call | bytes 18874368 | tf_op jit(solution)/shard_map/pallas_call | solution.py:62
  24.8 3.6 %copy-done.4 = bf16[3072,1536]{1,0:T(8,128)(2,1)} copy-done((bf16[3072,1536]{1,0:T(8,128)(2,1)}, bf16[3072,1536]{1,0:T(8,128)(2,1)S(1)}, u32[]{:S(2)}) %copy-start.4) | copy-done | bytes 9437208
  28.5 3.6 %copy-done.6 = bf16[3072,1536]{1,0:T(8,128)(2,1)} copy-done((bf16[3072,1536]{1,0:T(8,128)(2,1)}, bf16[3072,1536]{1,0:T(8,128)(2,1)S(1)}, u32[]{:S(2)}) %copy-start.6) | copy-done | bytes 9437208
  32.1 8.8 %shard_map.64 = (bf16[3072,1536]{1,0:T(8,128)(2,1)S(1)}, bf16[3072,1536]{1,0:T(8,128)(2,1)S(1)}) custom-call(f32[6144,1536]{1,0:T(8,128)} %weight_ref.5, f32[32,1536]{1,0:T(8,128)S(1)} %fusion.12.refs_0_), custom_call_target="tpu_custom_call" | custom-call | bytes 18874368 | tf_op jit(solution)/shard_map/pallas_call | solution.py:62
  40.9 3.6 %copy-done = bf16[3072,1536]{1,0:T(8,128)(2,1)} copy-done((bf16[3072,1536]{1,0:T(8,128)(2,1)}, bf16[3072,1536]{1,0:T(8,128)(2,1)S(1)}, u32[]{:S(2)}) %copy-start) | copy-done | bytes 9437208
  44.5 3.7 %copy-done.2 = bf16[3072,1536]{1,0:T(8,128)(2,1)} copy-done((bf16[3072,1536]{1,0:T(8,128)(2,1)}, bf16[3072,1536]{1,0:T(8,128)(2,1)S(1)}, u32[]{:S(2)}) %copy-start.2) | copy-done | bytes 9437208
  48.3 3.7 %copy-done.1 = bf16[3072,1536]{1,0:T(8,128)(2,1)S(1)} copy-done((bf16[3072,1536]{1,0:T(8,128)(2,1)S(1)}, bf16[3072,1536]{1,0:T(8,128)(2,1)}, u32[]{:S(2)}) %copy-start.1) | copy-done | bytes 9437208
  51.9 3.7 %copy-done.5 = bf16[3072,1536]{1,0:T(8,128)(2,1)S(1)} copy-done((bf16[3072,1536]{1,0:T(8,128)(2,1)S(1)}, bf16[3072,1536]{1,0:T(8,128)(2,1)}, u32[]{:S(2)}) %copy-start.5) | copy-done | bytes 9437208
  55.6 3.7 %copy-done.7 = bf16[3072,1536]{1,0:T(8,128)(2,1)S(1)} copy-done((bf16[3072,1536]{1,0:T(8,128)(2,1)S(1)}, bf16[3072,1536]{1,0:T(8,128)(2,1)}, u32[]{:S(2)}) %copy-start.7) | copy-done | bytes 9437208
  59.3 7.6 %shard_map.66 = (f32[64,3072]{1,0:T(8,128)S(1)}, f32[64,3072]{1,0:T(8,128)S(1)}) custom-call(s32[4]{0:T(128)S(1)} %fusion.14.place_ref, f32[32,1536]{1,0:T(8,128)S(1)} %copy-done.8, f32[32,1536]{1,0:T(8,128)S(1)} %collective-permute-done.refs_1_, f32[32,1536]{1,0:T(8,128)S(1)} %collective-permute-done.1.refs_2_, ...), custom_call_target="tpu_custom_call" | custom-call | flops 3623878656 | bytes 18874368 | tf_op jit(solution)/shard_map/pallas_call | solution.py:118
  67.0 7.6 %shard_map.67 = (f32[64,3072]{1,0:T(8,128)S(1)}, f32[64,3072]{1,0:T(8,128)S(1)}) custom-call(s32[4]{0:T(128)S(1)} %fusion.14.place_ref, f32[32,1536]{1,0:T(8,128)S(1)} %copy-done.8, f32[32,1536]{1,0:T(8,128)S(1)} %collective-permute-done.refs_1_, f32[32,1536]{1,0:T(8,128)S(1)} %collective-permute-done.1.refs_2_, ...), custom_call_target="tpu_custom_call" | custom-call | flops 3623878656 | bytes 18874368 | tf_op jit(solution)/shard_map/pallas_call | solution.py:118
  76.2 7.7 %collective-permute-done.6.refs_1_.refs_2_ = f32[32,1536]{1,0:T(8,128)S(1)} collective-permute-done((f32[32,1536]{1,0:T(8,128)S(1)}, f32[32,1536]{1,0:T(8,128)S(1)}, u32[]{:S(2)}, u32[]{:S(2)}) %collective-permute-start.6) | collective-permute-done | bytes 196640 | tf_op jit(solution)/shard_map/ppermute | solution.py:194
  86.3 8.8 %shard_map.68 = (bf16[1536,3072]{1,0:T(8,128)(2,1)S(1)}, bf16[1536,3072]{1,0:T(8,128)(2,1)S(1)}) custom-call(f32[1536,6144]{1,0:T(8,128)} %weight_ref.7, f32[64,3072]{1,0:T(8,128)S(1)} %add.113.refs_0_, f32[32,1536]{1,0:T(8,128)S(1)} %collective-permute-done.6.refs_1_.refs_2_), custom_call_target="tpu_custom_call" | custom-call | bytes 18874368 | tf_op jit(solution)/shard_map/pallas_call | solution.py:62
  95.1 6.6 %shard_map.69 = (f32[64,3072]{1,0:T(8,128)S(1)}, f32[64,3072]{1,0:T(8,128)S(1)}) custom-call(s32[4]{0:T(128)S(1)} %fusion.14.place_ref, f32[32,1536]{1,0:T(8,128)S(1)} %fusion.12.refs_0_, f32[32,1536]{1,0:T(8,128)S(1)} %collective-permute-done.3.refs_6_.refs_1_, f32[32,1536]{1,0:T(8,128)S(1)} %collective-permute-done.6.refs_1_.refs_2_, ...), custom_call_target="tpu_custom_call" | custom-call | flops 3623878656 | bytes 18874368 | tf_op jit(solution)/shard_map/pallas_call | solution.py:118
  101.8 8.8 %shard_map.70 = (bf16[1536,3072]{1,0:T(8,128)(2,1)S(1)}, bf16[1536,3072]{1,0:T(8,128)(2,1)S(1)}) custom-call(f32[1536,6144]{1,0:T(8,128)} %weight_ref.7, f32[64,3072]{1,0:T(8,128)S(1)} %get-tuple-element.43.refs_0_, f32[32,3072]{1,0:T(8,128)S(1)} %collective-permute-done.9.refs_1_), custom_call_target="tpu_custom_call" | custom-call | bytes 18874368 | tf_op jit(solution)/shard_map/pallas_call | solution.py:62
  110.6 6.6 %shard_map.71 = (f32[64,3072]{1,0:T(8,128)S(1)}, f32[64,3072]{1,0:T(8,128)S(1)}) custom-call(s32[4]{0:T(128)S(1)} %fusion.14.place_ref, f32[32,1536]{1,0:T(8,128)S(1)} %fusion.12.refs_0_, f32[32,1536]{1,0:T(8,128)S(1)} %collective-permute-done.3.refs_6_.refs_1_, f32[32,1536]{1,0:T(8,128)S(1)} %collective-permute-done.6.refs_1_.refs_2_, ...), custom_call_target="tpu_custom_call" | custom-call | flops 3623878656 | bytes 18874368 | tf_op jit(solution)/shard_map/pallas_call | solution.py:118
  121.4 8.6 %collective-permute-done.16 = f32[32,3072]{1,0:T(8,128)S(1)} collective-permute-done((f32[32,3072]{1,0:T(8,128)S(1)}, f32[32,3072]{1,0:T(8,128)S(1)}, u32[]{:S(2)}, u32[]{:S(2)}) %collective-permute-start.16) | collective-permute-done | bytes 393248 | tf_op jit(solution)/shard_map/ppermute | solution.py:200
  131.7 6.6 %collective-permute-done.11 = f32[32,3072]{1,0:T(8,128)S(1)} collective-permute-done((f32[32,3072]{1,0:T(8,128)S(1)}, f32[32,3072]{1,0:T(8,128)S(1)}, u32[]{:S(2)}, u32[]{:S(2)}) %collective-permute-start.11) | collective-permute-done | bytes 393248 | tf_op jit(solution)/shard_map/ppermute | solution.py:200
  140.2 6.6 %collective-permute-done.17.refs_1_ = f32[32,3072]{1,0:T(8,128)S(1)} collective-permute-done((f32[32,3072]{1,0:T(8,128)S(1)}, f32[32,3072]{1,0:T(8,128)S(1)}, u32[]{:S(2)}, u32[]{:S(2)}) %collective-permute-start.17) | collective-permute-done | bytes 393248 | tf_op jit(solution)/shard_map/ppermute | solution.py:200
  147.3 7.0 %collective-permute-done.12.refs_1_ = f32[32,3072]{1,0:T(8,128)S(1)} collective-permute-done((f32[32,3072]{1,0:T(8,128)S(1)}, f32[32,3072]{1,0:T(8,128)S(1)}, u32[]{:S(2)}, u32[]{:S(2)}) %collective-permute-start.12) | collective-permute-done | bytes 393248 | tf_op jit(solution)/shard_map/ppermute | solution.py:200
  154.3 6.9 %shard_map.72 = (f32[32,1536]{1,0:T(8,128)S(1)}, f32[32,1536]{1,0:T(8,128)S(1)}, f32[32,1536]{1,0:T(8,128)S(1)}, f32[32,1536]{1,0:T(8,128)S(1)}) custom-call(s32[4]{0:T(128)S(1)} %fusion.14.place_ref, f32[32,3072]{1,0:T(8,128)S(1)} %fusion.9.refs_0_, f32[32,3072]{1,0:T(8,128)S(1)} %collective-permute-done.17.refs_1_, ...), custom_call_target="tpu_custom_call" | custom-call | flops 3623878656 | bytes 18874368 | tf_op jit(solution)/shard_map/pallas_call | solution.py:167
  161.3 3.9 %shard_map.73 = (f32[32,768]{1,0:T(8,128)S(1)}, f32[32,768]{1,0:T(8,128)S(1)}, f32[32,768]{1,0:T(8,128)S(1)}, f32[32,768]{1,0:T(8,128)S(1)}) custom-call(s32[4]{0:T(128)S(1)} %fusion.14.place_ref, f32[32,3072]{1,0:T(8,128)S(1)} %fusion.4.refs_0_, f32[32,3072]{1,0:T(8,128)S(1)} %collective-permute-done.12.refs_1_, ...), custom_call_target="tpu_custom_call" | custom-call | flops 1811939328 | bytes 9437184 | tf_op jit(solution)/shard_map/pallas_call | solution.py:167
  165.2 3.9 %collective-permute-start.20 = (f32[32,768]{1,0:T(8,128)S(1)}, f32[32,768]{1,0:T(8,128)S(1)}, u32[]{:S(2)}, u32[]{:S(2)}) collective-permute-start(f32[32,768]{1,0:T(8,128)S(1)} %get-tuple-element.54), channel_id=1, source_target_pairs={{0,12},{4,0},{8,4},{12,8},{1,13},{5,1},{9,5},{13,9},{2,14},{6,2},{... | collective-permute-start | bytes 294920 | tf_op jit(solution)/shard_map/ppermute | solution.py:194
  169.7 3.9 %shard_map.74 = (f32[32,768]{1,0:T(8,128)S(1)}, f32[32,768]{1,0:T(8,128)S(1)}, f32[32,768]{1,0:T(8,128)S(1)}, f32[32,768]{1,0:T(8,128)S(1)}) custom-call(s32[4]{0:T(128)S(1)} %fusion.14.place_ref, f32[32,3072]{1,0:T(8,128)S(1)} %fusion.4.refs_0_, f32[32,3072]{1,0:T(8,128)S(1)} %collective-permute-done.12.refs_1_, ...), custom_call_target="tpu_custom_call" | custom-call | flops 1811939328 | bytes 9437184 | tf_op jit(solution)/shard_map/pallas_call | solution.py:167
  173.6 3.2 %collective-permute-start.23 = (f32[32,768]{1,0:T(8,128)S(1)}, f32[32,768]{1,0:T(8,128)S(1)}, u32[]{:S(2)}, u32[]{:S(2)}) collective-permute-start(f32[32,768]{1,0:T(8,128)S(1)} %get-tuple-element.58), channel_id=1, source_target_pairs={{0,12},{4,0},{8,4},{12,8},{1,13},{5,1},{9,5},{13,9},{2,14},{6,2},{... | collective-permute-start | bytes 294920 | tf_op jit(solution)/shard_map/ppermute | solution.py:194
  179.0 2.0 %collective-permute-done.23 = f32[32,768]{1,0:T(8,128)S(1)} collective-permute-done((f32[32,768]{1,0:T(8,128)S(1)}, f32[32,768]{1,0:T(8,128)S(1)}, u32[]{:S(2)}, u32[]{:S(2)}) %collective-permute-start.23) | collective-permute-done | bytes 98336 | tf_op jit(solution)/shard_map/ppermute | solution.py:194
  180.9 6.4 %collective-permute-done.24 = f32[32,768]{1,0:T(8,128)S(1)} collective-permute-done((f32[32,768]{1,0:T(8,128)S(1)}, f32[32,768]{1,0:T(8,128)S(1)}, u32[]{:S(2)}, u32[]{:S(2)}) %collective-permute-start.24) | collective-permute-done | bytes 98336 | tf_op jit(solution)/shard_map/ppermute | solution.py:194
  187.6 6.4 %psum.7 = f32[2,32]{1,0:T(2,128)S(1)} all-reduce(f32[2,32]{1,0:T(2,128)S(1)} %pad_maximum_fusion), channel_id=1, replica_groups=mesh['groups'=2,'hid'=4,'emb'=4] {'emb'}, use_global_device_ids=true, to_apply=%region_6.7 | all-reduce | flops 64 | bytes 512 | tf_op jit(solution)/shard_map/psum | solution.py:267
  (85 shorter events, 20.4 us)
Async XLA Ops:
  9.3 38.9 %collective-permute-start.3 = (f32[32,1536]{1,0:T(8,128)S(1)}, f32[32,1536]{1,0:T(8,128)S(1)}, u32[]{:S(2)}, u32[]{:S(2)}) collective-permute-start(f32[32,1536]{1,0:T(8,128)S(1)} %fusion.12.refs_0_), channel_id=1, source_target_pairs={{0,4},{4,8},{8,12},{12,0},{1,5},{5,9},{9,13},{13,1},{2,6},{6,10},{... | collective-permute-start | bytes 589832 | tf_op jit(solution)/shard_map/ppermute | solution.py:194
  11.4 36.8 %collective-permute-start.2 = (f32[32,1536]{1,0:T(8,128)}, f32[32,1536]{1,0:T(8,128)S(1)}, u32[]{:S(2)}, u32[]{:S(2)}) collective-permute-start(f32[32,1536]{1,0:T(8,128)} %refs_0_.3), channel_id=1, source_target_pairs={{0,12},{4,0},{8,4},{12,8},{1,13},{5,1},{9,5},{13,9},{2,14},{6,2},{... | collective-permute-start | bytes 589832 | tf_op jit(solution)/shard_map/ppermute | solution.py:194
  13.5 34.7 %collective-permute-start.1 = (f32[32,1536]{1,0:T(8,128)}, f32[32,1536]{1,0:T(8,128)S(1)}, u32[]{:S(2)}, u32[]{:S(2)}) collective-permute-start(f32[32,1536]{1,0:T(8,128)} %refs_0_.3), channel_id=1, source_target_pairs={{0,8},{4,12},{8,0},{12,4},{1,9},{5,13},{9,1},{13,5},{2,10},{6,14},... | collective-permute-start | bytes 589832 | tf_op jit(solution)/shard_map/ppermute | solution.py:194
  14.5 33.7 %collective-permute-start = (f32[32,1536]{1,0:T(8,128)}, f32[32,1536]{1,0:T(8,128)S(1)}, u32[]{:S(2)}, u32[]{:S(2)}) collective-permute-start(f32[32,1536]{1,0:T(8,128)} %refs_0_.3), channel_id=1, source_target_pairs={{0,4},{4,8},{8,12},{12,0},{1,5},{5,9},{9,13},{13,1},{2,6},{6,10},{... | collective-permute-start | bytes 589832 | tf_op jit(solution)/shard_map/ppermute | solution.py:194
  32.1 16.2 %copy-start.8 = (f32[32,1536]{1,0:T(8,128)S(1)}, f32[32,1536]{1,0:T(8,128)}, u32[]{:S(2)}) copy-start(f32[32,1536]{1,0:T(8,128)} %refs_0_.3) | copy-start | bytes 589828
  48.2 3.7 %copy-start.1 = (bf16[3072,1536]{1,0:T(8,128)(2,1)S(1)}, bf16[3072,1536]{1,0:T(8,128)(2,1)}, u32[]{:S(2)}) copy-start(bf16[3072,1536]{1,0:T(8,128)(2,1)} %copy-done) | copy-start | bytes 28311556
  59.3 7.7 %copy-start.3 = (bf16[3072,1536]{1,0:T(8,128)(2,1)S(1)}, bf16[3072,1536]{1,0:T(8,128)(2,1)}, u32[]{:S(2)}) copy-start(bf16[3072,1536]{1,0:T(8,128)(2,1)} %copy-done.2) | copy-start | bytes 28311556
  66.9 17.0 %collective-permute-start.8 = (f32[64,3072]{1,0:T(8,128)S(1)}, f32[64,3072]{1,0:T(8,128)S(1)}, u32[]{:S(2)}, u32[]{:S(2)}) collective-permute-start(f32[64,3072]{1,0:T(8,128)S(1)} %get-tuple-element.40), channel_id=1, source_target_pairs={{0,1},{1,0},{2,3},{3,2},{4,5},{5,4},{6,7},{7,6},{8,9},{9,8},{10,11... | collective-permute-start | bytes 2359304 | tf_op jit(solution)/shard_map/ppermute | solution.py:197
  74.6 10.9 %collective-permute-start.4 = (f32[64,3072]{1,0:T(8,128)S(1)}, f32[64,3072]{1,0:T(8,128)S(1)}, u32[]{:S(2)}, u32[]{:S(2)}) collective-permute-start(f32[64,3072]{1,0:T(8,128)S(1)} %get-tuple-element.39), channel_id=1, source_target_pairs={{0,1},{1,0},{2,3},{3,2},{4,5},{5,4},{6,7},{7,6},{8,9},{9,8},{10,11... | collective-permute-start | bytes 2359304 | tf_op jit(solution)/shard_map/ppermute | solution.py:197
  75.2 8.7 %collective-permute-start.6 = (f32[32,1536]{1,0:T(8,128)S(1)}, f32[32,1536]{1,0:T(8,128)S(1)}, u32[]{:S(2)}, u32[]{:S(2)}) collective-permute-start(f32[32,1536]{1,0:T(8,128)S(1)} %collective-permute-done.3.refs_6_.refs_1_), channel_id=1, source_target_pairs={{0,4},{4,8},{8,12},{12,0},{1,5},{5,9},{9,13},{13,1},{2,6},{6,10},{... | collective-permute-start | bytes 589832 | tf_op jit(solution)/shard_map/ppermute | solution.py:194
  83.9 11.2 %collective-permute-start.7 = (f32[32,1536]{1,0:T(8,128)S(1)}, f32[32,1536]{1,0:T(8,128)S(1)}, u32[]{:S(2)}, u32[]{:S(2)}) collective-permute-start(f32[32,1536]{1,0:T(8,128)S(1)} %collective-permute-done.6.refs_1_.refs_2_), channel_id=1, source_target_pairs={{0,4},{4,8},{8,12},{12,0},{1,5},{5,9},{9,13},{13,1},{2,6},{6,10},{... | collective-permute-start | bytes 589832 | tf_op jit(solution)/shard_map/ppermute | solution.py:194
  84.0 17.8 %collective-permute-start.9 = (f32[32,3072]{1,0:T(8,128)S(1)}, f32[32,3072]{1,0:T(8,128)S(1)}, u32[]{:S(2)}, u32[]{:S(2)}) collective-permute-start(f32[32,3072]{1,0:T(8,128)S(1)} %slice.55), channel_id=1, source_target_pairs={{0,2},{1,3},{2,0},{3,1},{4,6},{5,7},{6,4},{7,5},{8,10},{9,11},{10,... | collective-permute-start | bytes 1179656 | tf_op jit(solution)/shard_map/ppermute | solution.py:200
  85.7 24.9 %collective-permute-start.5 = (f32[32,3072]{1,0:T(8,128)S(1)}, f32[32,3072]{1,0:T(8,128)S(1)}, u32[]{:S(2)}, u32[]{:S(2)}) collective-permute-start(f32[32,3072]{1,0:T(8,128)S(1)} %slice.53), channel_id=1, source_target_pairs={{0,2},{1,3},{2,0},{3,1},{4,6},{5,7},{6,4},{7,5},{8,10},{9,11},{10,... | collective-permute-start | bytes 1179656 | tf_op jit(solution)/shard_map/ppermute | solution.py:200
  101.7 16.1 %collective-permute-start.15 = (f32[64,3072]{1,0:T(8,128)S(1)}, f32[64,3072]{1,0:T(8,128)S(1)}, u32[]{:S(2)}, u32[]{:S(2)}) collective-permute-start(f32[64,3072]{1,0:T(8,128)S(1)} %get-tuple-element.48), channel_id=1, source_target_pairs={{0,1},{1,0},{2,3},{3,2},{4,5},{5,4},{6,7},{7,6},{8,9},{9,8},{10,11... | collective-permute-start | bytes 2359304 | tf_op jit(solution)/shard_map/ppermute | solution.py:197
  110.6 8.9 %copy-start.11 = (f32[6144]{0:T(1024)S(1)}, f32[6144]{0:T(1024)}, u32[]{:S(2)}) copy-start(f32[6144]{0:T(1024)} %param.9) | copy-start | bytes 73732
  117.2 2.5 %collective-permute-start.10 = (f32[64,3072]{1,0:T(8,128)S(1)}, f32[64,3072]{1,0:T(8,128)S(1)}, u32[]{:S(2)}, u32[]{:S(2)}) collective-permute-start(f32[64,3072]{1,0:T(8,128)S(1)} %get-tuple-element.47), channel_id=1, source_target_pairs={{0,1},{1,0},{2,3},{3,2},{4,5},{5,4},{6,7},{7,6},{8,9},{9,8},{10,11... | collective-permute-start | bytes 2359304 | tf_op jit(solution)/shard_map/ppermute | solution.py:197
  117.9 12.0 %collective-permute-start.16 = (f32[32,3072]{1,0:T(8,128)S(1)}, f32[32,3072]{1,0:T(8,128)S(1)}, u32[]{:S(2)}, u32[]{:S(2)}) collective-permute-start(f32[32,3072]{1,0:T(8,128)S(1)} %slice.59), channel_id=1, source_target_pairs={{0,2},{1,3},{2,0},{3,1},{4,6},{5,7},{6,4},{7,5},{8,10},{9,11},{10,... | collective-permute-start | bytes 1179656 | tf_op jit(solution)/shard_map/ppermute | solution.py:200
  119.8 18.6 %collective-permute-start.11 = (f32[32,3072]{1,0:T(8,128)S(1)}, f32[32,3072]{1,0:T(8,128)S(1)}, u32[]{:S(2)}, u32[]{:S(2)}) collective-permute-start(f32[32,3072]{1,0:T(8,128)S(1)} %slice.56), channel_id=1, source_target_pairs={{0,2},{1,3},{2,0},{3,1},{4,6},{5,7},{6,4},{7,5},{8,10},{9,11},{10,... | collective-permute-start | bytes 1179656 | tf_op jit(solution)/shard_map/ppermute | solution.py:200
  130.2 16.6 %collective-permute-start.17 = (f32[32,3072]{1,0:T(8,128)S(1)}, f32[32,3072]{1,0:T(8,128)S(1)}, u32[]{:S(2)}, u32[]{:S(2)}) collective-permute-start(f32[32,3072]{1,0:T(8,128)S(1)} %fusion.9.refs_0_), channel_id=1, source_target_pairs={{0,2},{1,3},{2,0},{3,1},{4,6},{5,7},{6,4},{7,5},{8,10},{9,11},{10,... | collective-permute-start | bytes 1179656 | tf_op jit(solution)/shard_map/ppermute | solution.py:200
  138.6 15.7 %collective-permute-start.12 = (f32[32,3072]{1,0:T(8,128)S(1)}, f32[32,3072]{1,0:T(8,128)S(1)}, u32[]{:S(2)}, u32[]{:S(2)}) collective-permute-start(f32[32,3072]{1,0:T(8,128)S(1)} %fusion.4.refs_0_), channel_id=1, source_target_pairs={{0,2},{1,3},{2,0},{3,1},{4,6},{5,7},{6,4},{7,5},{8,10},{9,11},{10,... | collective-permute-start | bytes 1179656 | tf_op jit(solution)/shard_map/ppermute | solution.py:200
  140.2 14.2 %collective-permute-start.18 = (f32[32,3072]{1,0:T(8,128)S(1)}, f32[32,3072]{1,0:T(8,128)S(1)}, u32[]{:S(2)}, u32[]{:S(2)}) collective-permute-start(f32[32,3072]{1,0:T(8,128)S(1)} %fusion.9.refs_0_), channel_id=1, source_target_pairs={{0,1},{1,0},{2,3},{3,2},{4,5},{5,4},{6,7},{7,6},{8,9},{9,8},{10,11... | collective-permute-start | bytes 1179656 | tf_op jit(solution)/shard_map/ppermute | solution.py:197
  146.8 7.5 %collective-permute-start.19 = (f32[32,3072]{1,0:T(8,128)S(1)}, f32[32,3072]{1,0:T(8,128)S(1)}, u32[]{:S(2)}, u32[]{:S(2)}) collective-permute-start(f32[32,3072]{1,0:T(8,128)S(1)} %collective-permute-done.17.refs_1_), channel_id=1, source_target_pairs={{0,1},{1,0},{2,3},{3,2},{4,5},{5,4},{6,7},{7,6},{8,9},{9,8},{10,11... | collective-permute-start | bytes 1179656 | tf_op jit(solution)/shard_map/ppermute | solution.py:197
  146.8 14.4 %collective-permute-start.13 = (f32[32,3072]{1,0:T(8,128)S(1)}, f32[32,3072]{1,0:T(8,128)S(1)}, u32[]{:S(2)}, u32[]{:S(2)}) collective-permute-start(f32[32,3072]{1,0:T(8,128)S(1)} %fusion.4.refs_0_), channel_id=1, source_target_pairs={{0,1},{1,0},{2,3},{3,2},{4,5},{5,4},{6,7},{7,6},{8,9},{9,8},{10,11... | collective-permute-start | bytes 1179656 | tf_op jit(solution)/shard_map/ppermute | solution.py:197
  154.3 7.0 %collective-permute-start.14 = (f32[32,3072]{1,0:T(8,128)S(1)}, f32[32,3072]{1,0:T(8,128)S(1)}, u32[]{:S(2)}, u32[]{:S(2)}) collective-permute-start(f32[32,3072]{1,0:T(8,128)S(1)} %collective-permute-done.12.refs_1_), channel_id=1, source_target_pairs={{0,1},{1,0},{2,3},{3,2},{4,5},{5,4},{6,7},{7,6},{8,9},{9,8},{10,11... | collective-permute-start | bytes 1179656 | tf_op jit(solution)/shard_map/ppermute | solution.py:197
  165.2 12.8 %collective-permute-start.20 = (f32[32,768]{1,0:T(8,128)S(1)}, f32[32,768]{1,0:T(8,128)S(1)}, u32[]{:S(2)}, u32[]{:S(2)}) collective-permute-start(f32[32,768]{1,0:T(8,128)S(1)} %get-tuple-element.54), channel_id=1, source_target_pairs={{0,12},{4,0},{8,4},{12,8},{1,13},{5,1},{9,5},{13,9},{2,14},{6,2},{... | collective-permute-start | bytes 294920 | tf_op jit(solution)/shard_map/ppermute | solution.py:194
  169.0 9.9 %collective-permute-start.21 = (f32[32,768]{1,0:T(8,128)S(1)}, f32[32,768]{1,0:T(8,128)S(1)}, u32[]{:S(2)}, u32[]{:S(2)}) collective-permute-start(f32[32,768]{1,0:T(8,128)S(1)} %get-tuple-element.55), channel_id=1, source_target_pairs={{0,8},{4,12},{8,0},{12,4},{1,9},{5,13},{9,1},{13,5},{2,10},{6,14},... | collective-permute-start | bytes 294920 | tf_op jit(solution)/shard_map/ppermute | solution.py:194
  169.1 9.9 %collective-permute-start.22 = (f32[32,768]{1,0:T(8,128)S(1)}, f32[32,768]{1,0:T(8,128)S(1)}, u32[]{:S(2)}, u32[]{:S(2)}) collective-permute-start(f32[32,768]{1,0:T(8,128)S(1)} %get-tuple-element.56), channel_id=1, source_target_pairs={{0,4},{4,8},{8,12},{12,0},{1,5},{5,9},{9,13},{13,1},{2,6},{6,10},{... | collective-permute-start | bytes 294920 | tf_op jit(solution)/shard_map/ppermute | solution.py:194
  169.7 17.6 %copy-start.9 = (f32[32,1536]{1,0:T(8,128)S(1)}, f32[32,1536]{1,0:T(8,128)}, u32[]{:S(2)}) copy-start(f32[32,1536]{1,0:T(8,128)} %param.6) | copy-start | bytes 589828
  169.7 17.6 %copy-start.10 = (f32[1536]{0:T(1024)S(1)}, f32[1536]{0:T(1024)}, u32[]{:S(2)}) copy-start(f32[1536]{0:T(1024)} %param.11) | copy-start | bytes 18436
  173.6 7.4 %collective-permute-start.23 = (f32[32,768]{1,0:T(8,128)S(1)}, f32[32,768]{1,0:T(8,128)S(1)}, u32[]{:S(2)}, u32[]{:S(2)}) collective-permute-start(f32[32,768]{1,0:T(8,128)S(1)} %get-tuple-element.58), channel_id=1, source_target_pairs={{0,12},{4,0},{8,4},{12,8},{1,13},{5,1},{9,5},{13,9},{2,14},{6,2},{... | collective-permute-start | bytes 294920 | tf_op jit(solution)/shard_map/ppermute | solution.py:194
  176.8 10.5 %collective-permute-start.24 = (f32[32,768]{1,0:T(8,128)S(1)}, f32[32,768]{1,0:T(8,128)S(1)}, u32[]{:S(2)}, u32[]{:S(2)}) collective-permute-start(f32[32,768]{1,0:T(8,128)S(1)} %get-tuple-element.59), channel_id=1, source_target_pairs={{0,8},{4,12},{8,0},{12,4},{1,9},{5,13},{9,1},{13,5},{2,10},{6,14},... | collective-permute-start | bytes 294920 | tf_op jit(solution)/shard_map/ppermute | solution.py:194
  177.9 9.3 %collective-permute-start.25 = (f32[32,768]{1,0:T(8,128)S(1)}, f32[32,768]{1,0:T(8,128)S(1)}, u32[]{:S(2)}, u32[]{:S(2)}) collective-permute-start(f32[32,768]{1,0:T(8,128)S(1)} %get-tuple-element.60), channel_id=1, source_target_pairs={{0,4},{4,8},{8,12},{12,0},{1,5},{5,9},{9,13},{13,1},{2,6},{6,10},{... | collective-permute-start | bytes 294920 | tf_op jit(solution)/shard_map/ppermute | solution.py:194
  (6 other events, 22.0 us)

commit v5 on v4

--- a/solution.py
+++ b/solution.py
@@ -8,8 +8,9 @@
 from jax.experimental.pallas import tpu as pltpu
 from jax.sharding import PartitionSpec as P
 
-VMEM_LIMIT = 6 * 1024 * 1024
+VMEM_LIMIT = 5 * 1024 * 1024
 CHUNKS = 2
+SHORT = pl.CostEstimate(flops=1 << 20, bytes_accessed=1 << 18, transcendentals=0)
 
 
 def gelu_slope(values):
@@ -25,6 +26,54 @@
 
 def divisor(extent, *choices):
     return next(c for c in choices if extent % c == 0)
+
+
+def call(kernel, out_shape, operands, after):
+    outs = out_shape if isinstance(out_shape, tuple) else (out_shape,)
+
+    def run(*refs):
+        kernel(*refs[: len(operands)], *refs[len(operands) + len(after) :])
+
+    inside = pl.BlockSpec(memory_space=pltpu.VMEM)
+    result = pl.pallas_call(
+        run,
+        out_shape=tuple(jax.ShapeDtypeStruct(o.shape, o.dtype) for o in outs),
+        in_specs=[inside] * len(operands) + [pl.BlockSpec(memory_space=pl.ANY)] * len(after),
+        out_specs=[inside] * len(outs),
+        compiler_params=pltpu.CompilerParams(vmem_limit_bytes=VMEM_LIMIT),
+        cost_estimate=SHORT,
+    )(*operands, *after)
+    return result if isinstance(out_shape, tuple) else result[0]
+
+
+def moments_kernel(inputs_ref, out_ref):
+    rows, depth = inputs_ref.shape
+    mean = jnp.sum(inputs_ref[...], axis=1, keepdims=True) * (1.0 / depth)
+    square = jnp.sum(jnp.square(inputs_ref[...] - mean), axis=1, keepdims=True)
+    out_ref[:rows] = jnp.broadcast_to(mean, (rows, 128))
+    out_ref[rows:] = jnp.broadcast_to(square, (rows, 128))
+
+
+def merge(moments, count):
+    rows = moments[0].shape[0] // 2
+    mean = sum(part[:rows] for part in moments) * (1.0 / len(moments))
+    square = sum(part[rows:] + count * jnp.square(part[:rows] - mean) for part in moments)
+    return mean, square
+
+
+def merge_kernel(count, first_ref, second_ref, out_ref):
+    rows = out_ref.shape[0] // 2
+    out_ref[:rows], out_ref[rows:] = merge((first_ref[...], second_ref[...]), count)
+
+
+def normalise_kernel(count, inputs_ref, gain_ref, *refs):
+    *moment_refs, normed_ref, scaled_ref, inv_std_ref = refs
+    mean, square = merge([ref[...] for ref in moment_refs], count)
+    inv_std = 1.0 / jnp.sqrt(square * (1.0 / (count * len(moment_refs))) + 1e-06)
+    normed = (inputs_ref[...] - mean[:, :1]) * inv_std[:, :1]
+    normed_ref[...] = normed
+    scaled_ref[...] = normed * gain_ref[...]
+    inv_std_ref[...] = inv_std
 
 
 def prepare_kernel(rows, columns, block, depth, weight_ref, *refs):
@@ -69,26 +118,29 @@
             pltpu.SemaphoreType.DMA((depth,)),
         ],
         compiler_params=pltpu.CompilerParams(vmem_limit_bytes=VMEM_LIMIT),
-        cost_estimate=pl.CostEstimate(
-            flops=0, bytes_accessed=4 * rows[1] * columns[1], transcendentals=0
-        ),
-    )(weight, *after)
-
-
-def three_pass(both, high, low, contract):
+        cost_estimate=SHORT,
+    )(pltpu.with_memory_space_constraint(weight, pltpu.HBM), *after)
+
+
+def three_pass(both, high, low, contract, streamed):
     rows = both.shape[0] // 2
-    dot = functools.partial(
-        lax.dot_general,
-        dimension_numbers=(((1,), (contract,)), ((), ())),
-        preferred_element_type=jnp.float32,
-    )
-    first = dot(both[...], high)
-    return first[:rows] + first[rows:] + dot(both[:rows, :], low)
-
-
-def forward_kernel(slots, contract, place_ref, *refs):
+    dims = ((contract,), (1,)) if streamed else ((1,), (contract,))
+
+    def dot(left, weight):
+        pair = (weight, left) if streamed else (left, weight)
+        return lax.dot_general(*pair, (dims, ((), ())), preferred_element_type=jnp.float32)
+
+    first, second = dot(both[...], high), dot(both[:rows, :], low)
+    if streamed:
+        return (first[:, :rows] + first[:, rows:] + second).T
+    return first[:rows] + first[rows:] + second
+
+
+def forward_kernel(slots, contract, streamed, span, earlier, place_ref, *refs):
     slot_refs, (high_ref, low_ref) = refs[:slots], refs[slots : slots + 2]
     send_ref, keep_ref, both = refs[-3:]
+    for part_ref, whole_ref in zip(refs[slots + 2 : slots + 2 + earlier], (send_ref, keep_ref)):
+        whole_ref[:, : span[0]] = part_ref[...]
     block = slot_refs[0].shape[0]
     total = block * slots
     for b in range(slots):
@@ -97,40 +149,100 @@
         both[pl.ds(row, block), :] = high
         both[pl.ds(total + row, block), :] = low
 
-    hidden = send_ref.shape[1]
-    width = divisor(hidden, 256, 128)
-
-    @pl.loop(0, hidden // width)
+    width = divisor(span[1], *((512,) if streamed else ()), 256, 128)
+
+    @pl.loop(0, span[1] // width, unroll=1 if streamed else 2)
     def _(step):
-        at = pl.ds(pl.multiple_of(step * width, width), width)
-        tile = (slice(None), at) if contract == 0 else (at, slice(None))
-        part = three_pass(both, high_ref[tile], low_ref[tile], contract)
+        at = pl.ds(pl.multiple_of(span[0] + step * width, width), width)
+        tile = pl.ds(pl.multiple_of(step * width, width), width)
+        tile = (slice(None), tile) if contract == 0 else (tile, slice(None))
+        part = three_pass(both, high_ref[tile], low_ref[tile], contract, streamed)
         keep_ref[:, at] = part[: total // 2]
         send_ref[:, at] = part[total // 2 :]
 
 
-def forward(blocks, weight, place, by_column, after):
+def forward(blocks, weight, place, by_column, streamed, span, earlier, after):
     slots, (block, depth) = len(blocks), blocks[0].shape
-    hidden = weight[0].shape[1 if by_column else 0]
     half = block * slots // 2
-    out = jax.ShapeDtypeStruct((half, hidden), jnp.float32)
+    out = jax.ShapeDtypeStruct((half, sum(span)), jnp.float32)
     inside = pl.BlockSpec(memory_space=pltpu.VMEM)
     return pl.pallas_call(
-        functools.partial(forward_kernel, slots, 0 if by_column else 1),
+        functools.partial(forward_kernel, slots, 0 if by_column else 1, streamed, span, len(earlier)),
         out_shape=(out, out),
         in_specs=[pl.BlockSpec(memory_space=pltpu.SMEM)]
-        + [inside] * (slots + 2)
+        + [inside] * (slots + 2 + len(earlier))
         + [pl.BlockSpec(memory_space=pl.ANY)] * len(after),
         out_specs=[inside] * 2,
         scratch_shapes=[pltpu.VMEM((2 * block * slots, depth), jnp.bfloat16)],
         compiler_params=pltpu.CompilerParams(vmem_limit_bytes=VMEM_LIMIT),
-        cost_estimate=pl.CostEstimate(
-            flops=6 * block * slots * depth * hidden, bytes_accessed=4 * depth * hidden, transcendentals=0
-        ),
-    )(place, *blocks, *[pltpu.with_memory_space_constraint(part, pltpu.VMEM) for part in weight], *after)
-
-
-def backward_kernel(slots, earlier, first_column, place_ref, *refs):
+        cost_estimate=SHORT,
+    )(place, *blocks, *[pltpu.with_memory_space_constraint(part, pltpu.VMEM) for part in weight], *earlier, *after)
+
+
+def stream_kernel(slots, first_column, depth, place_ref, *refs):
+    slot_refs, weight_ref = refs[:slots], refs[slots]
+    send_ref, keep_ref, high_ref, low_ref, both, landed, arrived = refs[-7:]
+    block = slot_refs[0].shape[0]
+    total = block * slots
+    width = landed.shape[2]
+    steps = send_ref.shape[1] // width
+
+    def fetch(step):
+        start = pl.multiple_of(first_column + step * width, width)
+        slot = lax.rem(step, depth)
+        return pltpu.make_async_copy(weight_ref.at[:, pl.ds(start, width)], landed.at[slot], arrived.at[slot])
+
+    for step in range(min(depth, steps)):
+        fetch(step).start()
+    for b in range(slots):
+        high, low = split(slot_refs[b][...])
+        row = pl.multiple_of(place_ref[b] * block, block)
+        both[pl.ds(row, block), :] = high
+        both[pl.ds(total + row, block), :] = low
+
+    @pl.loop(0, steps)
+    def _(step):
+        fetch(step).wait()
+        high, low = split(landed[lax.rem(step, depth)])
+        at = pl.ds(pl.multiple_of(step * width, width), width)
+        high_ref[:, at] = high
+        low_ref[:, at] = low
+        part = three_pass(both, high, low, 0, False)
+        keep_ref[:, at] = part[: total // 2]
+        send_ref[:, at] = part[total // 2 :]
+
+        @pl.when(step + depth < steps)
+        def _():
+            fetch(step + depth).start()
+
+
+def stream(blocks, weight, place, columns, after):
+    slots, (block, rows) = len(blocks), blocks[0].shape
+    half, hidden = block * slots // 2, columns[1]
+    width = divisor(hidden, 256, 128)
+    depth = 3
+    out = jax.ShapeDtypeStruct((half, hidden), jnp.float32)
+    kept = pltpu.VMEM((rows, hidden), jnp.bfloat16)
+    inside = pl.BlockSpec(memory_space=pltpu.VMEM)
+    result = pl.pallas_call(
+        functools.partial(stream_kernel, slots, columns[0], depth),
+        out_shape=(out, out, kept, kept),
+        in_specs=[pl.BlockSpec(memory_space=pltpu.SMEM)]
+        + [inside] * slots
+        + [pl.BlockSpec(memory_space=pl.ANY)] * (1 + len(after)),
+        out_specs=[inside] * 4,
+        scratch_shapes=[
+            pltpu.VMEM((2 * block * slots, rows), jnp.bfloat16),
+            pltpu.VMEM((depth, rows, width), jnp.float32),
+            pltpu.SemaphoreType.DMA((depth,)),
+        ],
+        compiler_params=pltpu.CompilerParams(vmem_limit_bytes=2 * VMEM_LIMIT),
+        cost_estimate=SHORT,
+    )(place, *blocks, pltpu.with_memory_space_constraint(weight, pltpu.HBM), *after)
+    return result[:2], result[2:]
+
+
+def backward_kernel(slots, earlier, first_column, streamed, place_ref, *refs):
     act_refs, (high_ref, low_ref) = refs[:slots], refs[slots : slots + 2]
     earlier_refs = refs[slots + 2 : slots + 2 + earlier]
     out_refs = refs[-2 - slots : -2]
@@ -149,7 +261,7 @@
     def _(step):
         start = pl.multiple_of(step * width, width)
         tile = (pl.ds(pl.multiple_of(first_column + start, width), width), slice(None))
-        result[...] = three_pass(both, high_ref[tile], low_ref[tile], 1)
+        result[...] = three_pass(both, high_ref[tile], low_ref[tile], 1, streamed)
         for b in range(slots):
             row = pl.multiple_of(place_ref[b] * block, block)
             rows = result[pl.ds(row, block), :]
@@ -158,14 +270,14 @@
             out_refs[b][:, pl.ds(start, width)] = rows
 
 
-def backward(acts, weight, place, earlier, part, parts, after):
+def backward(acts, weight, place, earlier, part, parts, streamed, after):
     slots, (block, hidden) = len(acts), acts[0].shape
     depth = weight[0].shape[0] // parts
     width = divisor(depth, 256, 128)
     out = jax.ShapeDtypeStruct((block, depth), jnp.float32)
     inside = pl.BlockSpec(memory_space=pltpu.VMEM)
     return pl.pallas_call(
-        functools.partial(backward_kernel, slots, len(earlier), part * depth),
+        functools.partial(backward_kernel, slots, len(earlier), part * depth, streamed),
         out_shape=[out] * slots,
         in_specs=[pl.BlockSpec(memory_space=pltpu.SMEM)]
         + [inside] * (slots + 2 + len(earlier))
@@ -176,9 +288,7 @@
             pltpu.VMEM((block * slots, width), jnp.float32),
         ],
         compiler_params=pltpu.CompilerParams(vmem_limit_bytes=VMEM_LIMIT),
-        cost_estimate=pl.CostEstimate(
-            flops=6 * block * slots * depth * hidden, bytes_accessed=4 * depth * hidden, transcendentals=0
-        ),
+        cost_estimate=SHORT,
     )(place, *acts, *[pltpu.with_memory_space_constraint(part, pltpu.VMEM) for part in weight], *earlier, *after)
 
 
@@ -203,21 +313,30 @@
     place = ((owner % 2) ^ core) * chips + (owner // 2 - chip) % chips
 
     def gathered(values):
-        blocks = [values]
-        for _ in range(hid_size - 1):
-            blocks.append(along_hid(blocks[-1]))
-        return blocks
-
-    grads = [out_grad] + [along_hid(out_grad, step) for step in range(1, hid_size)]
-
-    local_mean = jnp.mean(inputs, axis=-1, keepdims=True)
-    local_square = jnp.sum(jnp.square(inputs - local_mean), axis=-1)
-    stats = lax.all_gather(jnp.stack([local_mean[:, 0], local_square]), "emb")
-    row_mean = jnp.mean(stats[:, 0], axis=0)
-    spread = jnp.sum(stats[:, 1] + depth * jnp.square(stats[:, 0] - row_mean), axis=0)
-    inv_std = (1.0 / jnp.sqrt(spread / model_width + 1e-06))[:, None]
-    normed = (inputs - row_mean[:, None]) * inv_std
-    scaled = gathered(normed * norm_gain)
+        return [values] + [along_hid(values, step) for step in range(1, hid_size)]
+
+    grads = gathered(out_grad)
+    piece = hidden // CHUNKS
+
+    moments = call(moments_kernel, jax.ShapeDtypeStruct((2 * tokens, 128), jnp.float32), (inputs,), ())
+    quarter = piece // 2
+    out_parts = [prepare(out_weight, (0, quarter), (0, depth), [place, moments])]
+    moments = call(
+        functools.partial(merge_kernel, depth), moments, (moments, other_core(moments)), (out_parts[0][0],)
+    )
+    for c in range(1, 4):
+        out_parts.append(prepare(out_weight, (c * quarter, quarter), (0, depth), [moments, out_parts[-1][0]]))
+    parts = [moments]
+    for _ in range(1, chips):
+        parts.append(next_chip(parts[-1]))
+    normed, scaled, inv_std = call(
+        functools.partial(normalise_kernel, 2 * depth),
+        (inputs, inputs, jax.ShapeDtypeStruct((tokens, 128), jnp.float32)),
+        (inputs, norm_gain[None, :], *parts),
+        (out_parts[-1][0],),
+    )
+    inv_std = inv_std[:, :1]
+    scaled = gathered(scaled)
 
     def halved(partial):
         send, keep = partial
@@ -230,17 +349,20 @@
             arrival = next_chip(arrival + terms[chips - step])
         return arrival, terms[0]
 
-    piece = hidden // CHUNKS
-    out_parts = [prepare(out_weight, (c * piece, piece), (0, depth), [scaled[0]]) for c in range(CHUNKS)]
-    back_0 = forward(grads, out_parts[0], place, False, [scaled[1], out_parts[1][0]])
+    def back(c, streamed, earlier, after):
+        span = (c % 2 * quarter, quarter)
+        return forward(grads, out_parts[c], place, False, streamed, span, earlier, after)
+
+    near, far = [scaled[1], scaled[-1]], scaled[2 : hid_size - 1]
+    back_0 = back(0, True, (), [scaled[0]])
+    back_0 = back(1, False, back_0, [])
     half_0 = halved(back_0)
-    back_1 = forward(grads, out_parts[1], place, False, [back_0[1]])
+    back_1 = back(2, True, (), [back_0[1], *near])
+    back_1 = back(3, False, back_1, far)
     half_1 = halved(back_1)
     back_0, back_1 = exchanged(half_0), exchanged(half_1)
-    in_parts_0 = prepare(in_weight, (0, depth), (0, piece), [half_0, scaled[hid_size // 2]])
-    pre_0 = forward(scaled, in_parts_0, place, True, [half_1])
-    in_parts_1 = prepare(in_weight, (0, depth), (piece, piece), [pre_0[1], back_0[0]])
-    pre_1 = forward(scaled, in_parts_1, place, True, [back_1[0]])
+    pre_0, in_parts_0 = stream(scaled, in_weight, place, (0, piece), [half_0, half_1])
+    pre_1, in_parts_1 = stream(scaled, in_weight, place, (piece, piece), [pre_0[1], back_0[0]])
     backs = [back_0, back_1]
     pres = [exchanged(halved(pre_0)), exchanged(halved(pre_1))]
 
@@ -257,11 +379,11 @@
         return sum([along_hid(sums[step], -step) for step in range(1, hid_size)], start=sums[0])
 
     acts_0, acts_1 = spread_out(0), spread_out(1)
-    sums = backward(acts_0, in_parts_0, place, (), 0, 1, [pre_1[1]])
+    sums = backward(acts_0, in_parts_0, place, (), 0, 1, True, [pre_1[1]])
     parts = 2 if depth % 512 == 0 else 1
     ends = []
     for part in range(parts):
-        ends.append(backward(acts_1, in_parts_1, place, sums, part, parts, [ends[-1][0] if ends else sums[0]]))
+        ends.append(backward(acts_1, in_parts_1, place, sums, part, parts, False, [ends[-1][0] if ends else sums[0]]))
     running = jnp.concatenate([summed_along_hid(end) for end in ends], axis=1)
     normed_grad = running * norm_gain
     totals = lax.psum(

time: 195 us -> 158 us (0.81)
  local copies, waits for them, and re-layouts: 25.8 us -> 1.18 us
  Pallas kernels: 78.2 us -> 69 us
  blocking collectives: 12.4 us -> 5.97 us
  waiting for transfers between devices: 46.1 us -> 51.4 us
  other arithmetic: 5.19 us -> 1.79 us
    unnamed x24 -> x10, local copies, waits for them, and re-layouts: 25.6 us -> 0.95 us
    pallas_call x0 -> x5, Pallas kernels: none -> 19.6 us  [the longest x2 19.3 us: stream(): pl.pallas_call(functools.partial(stream_kernel, slots, columns[0], depth)...]
    pallas_call x4, Pallas kernels: 35.1 us -> 18.8 us  [prepare(): pl.pallas_call(functools.partial(prepare_kernel, rows, columns, block, de...]
    pallas_call x4, Pallas kernels: 28.4 us -> 15.4 us  [forward(): pl.pallas_call(functools.partial(forward_kernel, slots, 0 if by_column el...]
    ppermute x6 -> x7, waiting for transfers between devices: 28.9 us -> 38.2 us  [next_chip(): lax.ppermute(values, 'emb', [(i, (i + 2) % emb_size) for i in range(emb_s...]
    all_gather x1 -> x0, blocking collectives: 5.98 us -> none  [body(): stats = lax.all_gather(jnp.stack([local_mean[:, 0], local_square]), 'emb')]
    ppermute x12, waiting for transfers between devices: 17 us -> 12.3 us  [along_hid(): lax.ppermute(values, 'hid', [(i, (i + steps) % hid_size) for i in range(h...]
    reduce_sum x3 -> x0, other arithmetic: 2.2 us -> none  [the longest x1 1.13 us: body(): local_square = jnp.sum(jnp.square(inputs - local_mean), axis=-1)]
  transfers between devices with their start and end apart: 26 -> 28, of which waited for: 9 -> 11; matrix products, arithmetic and copies ran while one was open for 1% -> 1% of each run, Pallas kernels for 34% -> 41%
where the time goes in v5:
time: 158 us; the launch traced here: 157 us
  Pallas kernels  69 us (44%)
  waiting for transfers between devices  51.4 us (33%)
  starting transfers between devices  27.6 us (17%)
  blocking collectives  5.97 us (4%)
  other arithmetic  1.79 us (1%)
    ppermute x7, waiting for transfers between devices, next_chip(): lax.ppermute(values, 'emb', [(i, (i + 2) % emb_size) for i in range(emb_s...  38.2 us
    pallas_call x2, Pallas kernels, stream(): pl.pallas_call(functools.partial(stream_kernel, slots, columns[0], depth)...  19.3 us
    pallas_call x4, Pallas kernels, prepare(): pl.pallas_call(functools.partial(prepare_kernel, rows, columns, block, de...  18.8 us
    ppermute x12, starting transfers between devices, along_hid(): lax.ppermute(values, 'hid', [(i, (i + steps) % hid_size) for i in range(h...  17.9 us
    pallas_call x4, Pallas kernels, forward(): pl.pallas_call(functools.partial(forward_kernel, slots, 0 if by_column el...  15.4 us
    pallas_call x3, Pallas kernels, backward(): pl.pallas_call(functools.partial(backward_kernel, slots, len(earlier), pa...  15.2 us
    ppermute x12, waiting for transfers between devices, along_hid(): lax.ppermute(values, 'hid', [(i, (i + steps) % hid_size) for i in range(h...  12.3 us
    ppermute x7, starting transfers between devices, next_chip(): lax.ppermute(values, 'emb', [(i, (i + 2) % emb_size) for i in range(emb_s...  8.37 us
  transfers between devices with their start and end apart: 28, of which 11 were waited for; matrix products, arithmetic and copies ran while one was open for 1% of the time, Pallas kernels for 41%

profile of v5, /device:TPU:0, one launch (start us, length us, event | category | flops | bytes accessed | tf_op | source)
XLA Modules:
  0.0 157.3 jit_solution(14213957488774241161)
XLA Ops:
  0.0 3.0 %collective-permute-start.2 = (f32[32,1536]{1,0:T(8,128)}, f32[32,1536]{1,0:T(8,128)S(1)}, u32[]{:S(2)}, u32[]{:S(2)}) collective-permute-start(f32[32,1536]{1,0:T(8,128)} %refs_0_.11), channel_id=1, source_target_pairs={{0,4},{4,8},{8,12},{12,0},{1,5},{5,9},{9,13},{13,1},{2,6},{6,10},{... | collective-permute-start | bytes 589832 | tf_op jit(solution)/shard_map/ppermute | solution.py:304
  4.2 4.7 %shard_map.65 = (bf16[1536,1536]{1,0:T(8,128)(2,1)S(1)}, bf16[1536,1536]{1,0:T(8,128)(2,1)S(1)}) custom-call(f32[6144,1536]{1,0:T(8,128)} %weight_ref.7, s32[4]{0:T(128)S(1)} %fusion.13.refs_0_.place_ref, f32[64,128]{1,0:T(8,128)S(1)} %shard_map.64.refs_1_.refs_0_), custom_call_target="tpu_custom_call" | custom-call | flops 1048576 | bytes 262144 | tf_op jit(solution)/shard_map/pallas_call | solution.py:111
  8.9 1.6 collective-permute-start.1
  10.5 2.6 %collective-permute-start.3 = (f32[32,1536]{1,0:T(8,128)S(1)}, f32[32,1536]{1,0:T(8,128)S(1)}, u32[]{:S(2)}, u32[]{:S(2)}) collective-permute-start(f32[32,1536]{1,0:T(8,128)S(1)} %copy-done), channel_id=1, source_target_pairs={{0,8},{4,12},{8,0},{12,4},{1,9},{5,13},{9,1},{13,5},{2,10},{6,14},... | collective-permute-start | bytes 589832 | tf_op jit(solution)/shard_map/ppermute | solution.py:304
  13.1 1.3 collective-permute-start.4
  14.5 4.7 %shard_map.67 = (bf16[1536,1536]{1,0:T(8,128)(2,1)S(1)}, bf16[1536,1536]{1,0:T(8,128)(2,1)S(1)}) custom-call(f32[6144,1536]{1,0:T(8,128)} %weight_ref.7, f32[64,128]{1,0:T(8,128)S(1)} %shard_map.66.refs_0_.refs_2_, bf16[1536,1536]{1,0:T(8,128)(2,1)S(1)} %get-tuple-element.44.refs_2_.refs_1_.refs_4_), custom_call_target="tpu_custom_call" | custom-call | flops 1048576 | bytes 262144 | tf_op jit(solution)/shard_map/pallas_call | solution.py:111
  19.2 4.7 %shard_map.68 = (bf16[1536,1536]{1,0:T(8,128)(2,1)S(1)}, bf16[1536,1536]{1,0:T(8,128)(2,1)S(1)}) custom-call(f32[6144,1536]{1,0:T(8,128)} %weight_ref.7, f32[64,128]{1,0:T(8,128)S(1)} %shard_map.66.refs_0_.refs_2_, bf16[1536,1536]{1,0:T(8,128)(2,1)S(1)} %get-tuple-element.45.refs_1_.refs_4_), custom_call_target="tpu_custom_call" | custom-call | flops 1048576 | bytes 262144 | tf_op jit(solution)/shard_map/pallas_call | solution.py:111
  23.9 4.7 %shard_map.69 = (bf16[1536,1536]{1,0:T(8,128)(2,1)S(1)}, bf16[1536,1536]{1,0:T(8,128)(2,1)S(1)}) custom-call(f32[6144,1536]{1,0:T(8,128)} %weight_ref.7, f32[64,128]{1,0:T(8,128)S(1)} %shard_map.66.refs_0_.refs_2_, bf16[1536,1536]{1,0:T(8,128)(2,1)S(1)} %get-tuple-element.46.refs_1_.refs_4_), custom_call_target="tpu_custom_call" | custom-call | flops 1048576 | bytes 262144 | tf_op jit(solution)/shard_map/pallas_call | solution.py:111
  29.5 3.1 %collective-permute-start.6 = (f32[32,1536]{1,0:T(8,128)S(1)}, f32[32,1536]{1,0:T(8,128)S(1)}, u32[]{:S(2)}, u32[]{:S(2)}) collective-permute-start(f32[32,1536]{1,0:T(8,128)S(1)} %get-tuple-element.53.refs_6_.refs_0_), channel_id=1, source_target_pairs={{0,12},{4,0},{8,4},{12,8},{1,13},{5,1},{9,5},{13,9},{2,14},{6,2},{... | collective-permute-start | bytes 589832 | tf_op jit(solution)/shard_map/ppermute | solution.py:304
  32.7 3.9 %shard_map.71 = (f32[64,1536]{1,0:T(8,128)S(1)}, f32[64,1536]{1,0:T(8,128)S(1)}) custom-call(s32[4]{0:T(128)S(1)} %fusion.13.refs_0_.place_ref, f32[32,1536]{1,0:T(8,128)S(1)} %copy-done, f32[32,1536]{1,0:T(8,128)S(1)} %collective-permute-done.2.refs_1_, f32[32,1536]{1,0:T(8,128)S(1)} %collective-permute-done.3.refs_2_, ...), custom_call_target="tpu_custom_call" | custom-call | flops 1048576 | bytes 262144 | tf_op jit(solution)/shard_map/pallas_call | solution.py:169
  36.5 3.8 %shard_map.72 = (f32[64,3072]{1,0:T(8,128)S(1)}, f32[64,3072]{1,0:T(8,128)S(1)}) custom-call(s32[4]{0:T(128)S(1)} %fusion.13.refs_0_.place_ref, f32[32,1536]{1,0:T(8,128)S(1)} %copy-done, f32[32,1536]{1,0:T(8,128)S(1)} %collective-permute-done.2.refs_1_, f32[32,1536]{1,0:T(8,128)S(1)} %collective-permute-done.3.refs_2_, ...), custom_call_target="tpu_custom_call" | custom-call | flops 1048576 | bytes 262144 | tf_op jit(solution)/shard_map/pallas_call | solution.py:169
  41.1 3.9 %shard_map.73 = (f32[64,1536]{1,0:T(8,128)S(1)}, f32[64,1536]{1,0:T(8,128)S(1)}) custom-call(s32[4]{0:T(128)S(1)} %fusion.13.refs_0_.place_ref, f32[32,1536]{1,0:T(8,128)S(1)} %copy-done, f32[32,1536]{1,0:T(8,128)S(1)} %collective-permute-done.2.refs_1_, f32[32,1536]{1,0:T(8,128)S(1)} %collective-permute-done.3.refs_2_, ...), custom_call_target="tpu_custom_call" | custom-call | flops 1048576 | bytes 262144 | tf_op jit(solution)/shard_map/pallas_call | solution.py:169
  45.0 3.1 %collective-permute-done.7.refs_8_.refs_2_ = f32[32,1536]{1,0:T(8,128)S(1)} collective-permute-done((f32[32,1536]{1,0:T(8,128)S(1)}, f32[32,1536]{1,0:T(8,128)S(1)}, u32[]{:S(2)}, u32[]{:S(2)}) %collective-permute-start.7) | collective-permute-done | bytes 196640 | tf_op jit(solution)/shard_map/ppermute | solution.py:304
  48.1 3.8 %shard_map.74 = (f32[64,3072]{1,0:T(8,128)S(1)}, f32[64,3072]{1,0:T(8,128)S(1)}) custom-call(s32[4]{0:T(128)S(1)} %fusion.13.refs_0_.place_ref, f32[32,1536]{1,0:T(8,128)S(1)} %copy-done, f32[32,1536]{1,0:T(8,128)S(1)} %collective-permute-done.2.refs_1_, f32[32,1536]{1,0:T(8,128)S(1)} %collective-permute-done.3.refs_2_, ...), custom_call_target="tpu_custom_call" | custom-call | flops 1048576 | bytes 262144 | tf_op jit(solution)/shard_map/pallas_call | solution.py:169
  52.2 1.2 collective-permute-start.11
  54.3 9.6 %shard_map.75 = (f32[64,3072]{1,0:T(8,128)S(1)}, f32[64,3072]{1,0:T(8,128)S(1)}, bf16[1536,3072]{1,0:T(8,128)(2,1)S(1)}, bf16[1536,3072]{1,0:T(8,128)(2,1)S(1)}) custom-call(s32[4]{0:T(128)S(1)} %fusion.13.refs_0_.place_ref, f32[32,1536]{1,0:T(8,128)S(1)} %get-tuple-element.53.refs_6_.refs_0_, f32[32,1536]{1,0:T(8,128)S(1)} %collective-permute-done.5.refs_7_.refs_1_, ...), custom_call_target="tpu_custom_call" | custom-call | flops 1048576 | bytes 262144 | tf_op jit(solution)/shard_map/pallas_call | solution.py:227
  64.2 9.6 %shard_map.76 = (f32[64,3072]{1,0:T(8,128)S(1)}, f32[64,3072]{1,0:T(8,128)S(1)}, bf16[1536,3072]{1,0:T(8,128)(2,1)S(1)}, bf16[1536,3072]{1,0:T(8,128)(2,1)S(1)}) custom-call(s32[4]{0:T(128)S(1)} %fusion.13.refs_0_.place_ref, f32[32,1536]{1,0:T(8,128)S(1)} %get-tuple-element.53.refs_6_.refs_0_, f32[32,1536]{1,0:T(8,128)S(1)} %collective-permute-done.5.refs_7_.refs_1_, ...), custom_call_target="tpu_custom_call" | custom-call | flops 1048576 | bytes 262144 | tf_op jit(solution)/shard_map/pallas_call | solution.py:227
  74.4 1.2 collective-permute-start.18
  76.7 1.2 collective-permute-start.13
  77.9 8.5 %collective-permute-done.18 = f32[32,3072]{1,0:T(8,128)S(1)} collective-permute-done((f32[32,3072]{1,0:T(8,128)S(1)}, f32[32,3072]{1,0:T(8,128)S(1)}, u32[]{:S(2)}, u32[]{:S(2)}) %collective-permute-start.18) | collective-permute-done | bytes 393248 | tf_op jit(solution)/shard_map/ppermute | solution.py:310
  86.7 1.2 collective-permute-start.19
  87.8 7.0 %collective-permute-done.9 = f32[32,3072]{1,0:T(8,128)S(1)} collective-permute-done((f32[32,3072]{1,0:T(8,128)S(1)}, f32[32,3072]{1,0:T(8,128)S(1)}, u32[]{:S(2)}, u32[]{:S(2)}) %collective-permute-start.9) | collective-permute-done | bytes 393248 | tf_op jit(solution)/shard_map/ppermute | solution.py:310
  94.9 8.4 %collective-permute-done.13 = f32[32,3072]{1,0:T(8,128)S(1)} collective-permute-done((f32[32,3072]{1,0:T(8,128)S(1)}, f32[32,3072]{1,0:T(8,128)S(1)}, u32[]{:S(2)}, u32[]{:S(2)}) %collective-permute-start.13) | collective-permute-done | bytes 393248 | tf_op jit(solution)/shard_map/ppermute | solution.py:310
  104.7 7.0 %collective-permute-done.19.refs_1_ = f32[32,3072]{1,0:T(8,128)S(1)} collective-permute-done((f32[32,3072]{1,0:T(8,128)S(1)}, f32[32,3072]{1,0:T(8,128)S(1)}, u32[]{:S(2)}, u32[]{:S(2)}) %collective-permute-start.19) | collective-permute-done | bytes 393248 | tf_op jit(solution)/shard_map/ppermute | solution.py:310
  112.2 7.1 %collective-permute-done.14.refs_1_ = f32[32,3072]{1,0:T(8,128)S(1)} collective-permute-done((f32[32,3072]{1,0:T(8,128)S(1)}, f32[32,3072]{1,0:T(8,128)S(1)}, u32[]{:S(2)}, u32[]{:S(2)}) %collective-permute-start.14) | collective-permute-done | bytes 393248 | tf_op jit(solution)/shard_map/ppermute | solution.py:310
  119.4 7.4 %shard_map.77 = (f32[32,1536]{1,0:T(8,128)S(1)}, f32[32,1536]{1,0:T(8,128)S(1)}, f32[32,1536]{1,0:T(8,128)S(1)}, f32[32,1536]{1,0:T(8,128)S(1)}) custom-call(s32[4]{0:T(128)S(1)} %fusion.13.refs_0_.place_ref, f32[32,3072]{1,0:T(8,128)S(1)} %fusion.9.refs_0_, f32[32,3072]{1,0:T(8,128)S(1)} %collective-permute-done.19.refs_1_, ...), custom_call_target="tpu_custom_call" | custom-call | flops 1048576 | bytes 262144 | tf_op jit(solution)/shard_map/pallas_call | solution.py:279
  126.8 3.9 %shard_map.78 = (f32[32,768]{1,0:T(8,128)S(1)}, f32[32,768]{1,0:T(8,128)S(1)}, f32[32,768]{1,0:T(8,128)S(1)}, f32[32,768]{1,0:T(8,128)S(1)}) custom-call(s32[4]{0:T(128)S(1)} %fusion.13.refs_0_.place_ref, f32[32,3072]{1,0:T(8,128)S(1)} %fusion.4.refs_0_, f32[32,3072]{1,0:T(8,128)S(1)} %collective-permute-done.14.refs_1_, ...), custom_call_target="tpu_custom_call" | custom-call | flops 1048576 | bytes 262144 | tf_op jit(solution)/shard_map/pallas_call | solution.py:279
  132.9 3.9 %shard_map.79 = (f32[32,768]{1,0:T(8,128)S(1)}, f32[32,768]{1,0:T(8,128)S(1)}, f32[32,768]{1,0:T(8,128)S(1)}, f32[32,768]{1,0:T(8,128)S(1)}) custom-call(s32[4]{0:T(128)S(1)} %fusion.13.refs_0_.place_ref, f32[32,3072]{1,0:T(8,128)S(1)} %fusion.4.refs_0_, f32[32,3072]{1,0:T(8,128)S(1)} %collective-permute-done.14.refs_1_, ...), custom_call_target="tpu_custom_call" | custom-call | flops 1048576 | bytes 262144 | tf_op jit(solution)/shard_map/pallas_call | solution.py:279
  136.8 2.9 %collective-permute-start.25 = (f32[32,768]{1,0:T(8,128)S(1)}, f32[32,768]{1,0:T(8,128)S(1)}, u32[]{:S(2)}, u32[]{:S(2)}) collective-permute-start(f32[32,768]{1,0:T(8,128)S(1)} %get-tuple-element.79), channel_id=1, source_target_pairs={{0,12},{4,0},{8,4},{12,8},{1,13},{5,1},{9,5},{13,9},{2,14},{6,2},{... | collective-permute-start | bytes 294920 | tf_op jit(solution)/shard_map/ppermute | solution.py:304
  142.4 1.7 %collective-permute-done.25 = f32[32,768]{1,0:T(8,128)S(1)} collective-permute-done((f32[32,768]{1,0:T(8,128)S(1)}, f32[32,768]{1,0:T(8,128)S(1)}, u32[]{:S(2)}, u32[]{:S(2)}) %collective-permute-start.25) | collective-permute-done | bytes 98336 | tf_op jit(solution)/shard_map/ppermute | solution.py:304
  144.0 6.3 %collective-permute-done.26 = f32[32,768]{1,0:T(8,128)S(1)} collective-permute-done((f32[32,768]{1,0:T(8,128)S(1)}, f32[32,768]{1,0:T(8,128)S(1)}, u32[]{:S(2)}, u32[]{:S(2)}) %collective-permute-start.26) | collective-permute-done | bytes 98336 | tf_op jit(solution)/shard_map/ppermute | solution.py:304
  150.6 6.0 %psum.7 = f32[2,32]{1,0:T(2,128)S(1)} all-reduce(f32[2,32]{1,0:T(2,128)S(1)} %pad_maximum_fusion), channel_id=1, replica_groups=mesh['groups'=2,'hid'=4,'emb'=4] {'emb'}, use_global_device_ids=true, to_apply=%region_2.3 | all-reduce | flops 64 | bytes 512 | tf_op jit(solution)/shard_map/psum | solution.py:389
  (72 shorter events, 13.8 us)
Async XLA Ops:
  0.0 32.6 %collective-permute-start.2 = (f32[32,1536]{1,0:T(8,128)}, f32[32,1536]{1,0:T(8,128)S(1)}, u32[]{:S(2)}, u32[]{:S(2)}) collective-permute-start(f32[32,1536]{1,0:T(8,128)} %refs_0_.11), channel_id=1, source_target_pairs={{0,4},{4,8},{8,12},{12,0},{1,5},{5,9},{9,13},{13,1},{2,6},{6,10},{... | collective-permute-start | bytes 589832 | tf_op jit(solution)/shard_map/ppermute | solution.py:304
  4.1 4.8 %collective-permute-start = (f32[64,128]{1,0:T(8,128)S(1)}, f32[64,128]{1,0:T(8,128)S(1)}, u32[]{:S(2)}, u32[]{:S(2)}) collective-permute-start(f32[64,128]{1,0:T(8,128)S(1)} %shard_map.64.refs_1_.refs_0_), channel_id=1, source_target_pairs={{0,1},{1,0},{2,3},{3,2},{4,5},{5,4},{6,7},{7,6},{8,9},{9,8},{10,11... | collective-permute-start | bytes 98312 | tf_op jit(solution)/shard_map/ppermute | solution.py:307
  8.9 1.6 %copy-start = (f32[32,1536]{1,0:T(8,128)S(1)}, f32[32,1536]{1,0:T(8,128)}, u32[]{:S(2)}) copy-start(f32[32,1536]{1,0:T(8,128)} %refs_0_.11) | copy-start | bytes 589828
  8.9 5.5 %copy-start.3 = (f32[1536]{0:T(1024)S(1)}, f32[1536]{0:T(1024)}, u32[]{:S(2)}) copy-start(f32[1536]{0:T(1024)} %param.11) | copy-start | bytes 18436
  8.9 19.7 %collective-permute-start.1 = (f32[64,128]{1,0:T(8,128)S(1)}, f32[64,128]{1,0:T(8,128)S(1)}, u32[]{:S(2)}, u32[]{:S(2)}) collective-permute-start(f32[64,128]{1,0:T(8,128)S(1)} %shard_map.66.refs_0_.refs_2_), channel_id=1, source_target_pairs={{0,2},{1,3},{2,0},{3,1},{4,6},{5,7},{6,4},{7,5},{8,10},{9,11},{10,... | collective-permute-start | bytes 98312 | tf_op jit(solution)/shard_map/ppermute | solution.py:310
  10.5 22.1 %collective-permute-start.3 = (f32[32,1536]{1,0:T(8,128)S(1)}, f32[32,1536]{1,0:T(8,128)S(1)}, u32[]{:S(2)}, u32[]{:S(2)}) collective-permute-start(f32[32,1536]{1,0:T(8,128)S(1)} %copy-done), channel_id=1, source_target_pairs={{0,8},{4,12},{8,0},{12,4},{1,9},{5,13},{9,1},{13,5},{2,10},{6,14},... | collective-permute-start | bytes 589832 | tf_op jit(solution)/shard_map/ppermute | solution.py:304
  13.1 19.6 %collective-permute-start.4 = (f32[32,1536]{1,0:T(8,128)S(1)}, f32[32,1536]{1,0:T(8,128)S(1)}, u32[]{:S(2)}, u32[]{:S(2)}) collective-permute-start(f32[32,1536]{1,0:T(8,128)S(1)} %copy-done), channel_id=1, source_target_pairs={{0,12},{4,0},{8,4},{12,8},{1,13},{5,1},{9,5},{13,9},{2,14},{6,2},{... | collective-permute-start | bytes 589832 | tf_op jit(solution)/shard_map/ppermute | solution.py:304
  23.9 4.8 %copy-start.2 = (f32[32,1536]{1,0:T(8,128)S(1)}, f32[32,1536]{1,0:T(8,128)}, u32[]{:S(2)}) copy-start(f32[32,1536]{1,0:T(8,128)} %refs_0_.7) | copy-start | bytes 589828
  28.8 11.7 %collective-permute-start.5 = (f32[32,1536]{1,0:T(8,128)S(1)}, f32[32,1536]{1,0:T(8,128)S(1)}, u32[]{:S(2)}, u32[]{:S(2)}) collective-permute-start(f32[32,1536]{1,0:T(8,128)S(1)} %get-tuple-element.53.refs_6_.refs_0_), channel_id=1, source_target_pairs={{0,4},{4,8},{8,12},{12,0},{1,5},{5,9},{9,13},{13,1},{2,6},{6,10},{... | collective-permute-start | bytes 589832 | tf_op jit(solution)/shard_map/ppermute | solution.py:304
  29.5 11.6 %collective-permute-start.6 = (f32[32,1536]{1,0:T(8,128)S(1)}, f32[32,1536]{1,0:T(8,128)S(1)}, u32[]{:S(2)}, u32[]{:S(2)}) collective-permute-start(f32[32,1536]{1,0:T(8,128)S(1)} %get-tuple-element.53.refs_6_.refs_0_), channel_id=1, source_target_pairs={{0,12},{4,0},{8,4},{12,8},{1,13},{5,1},{9,5},{13,9},{2,14},{6,2},{... | collective-permute-start | bytes 589832 | tf_op jit(solution)/shard_map/ppermute | solution.py:304
  32.6 15.4 %collective-permute-start.7 = (f32[32,1536]{1,0:T(8,128)S(1)}, f32[32,1536]{1,0:T(8,128)S(1)}, u32[]{:S(2)}, u32[]{:S(2)}) collective-permute-start(f32[32,1536]{1,0:T(8,128)S(1)} %get-tuple-element.53.refs_6_.refs_0_), channel_id=1, source_target_pairs={{0,8},{4,12},{8,0},{12,4},{1,9},{5,13},{9,1},{13,5},{2,10},{6,14},... | collective-permute-start | bytes 589832 | tf_op jit(solution)/shard_map/ppermute | solution.py:304
  40.4 11.6 %collective-permute-start.10 = (f32[64,3072]{1,0:T(8,128)S(1)}, f32[64,3072]{1,0:T(8,128)S(1)}, u32[]{:S(2)}, u32[]{:S(2)}) collective-permute-start(f32[64,3072]{1,0:T(8,128)S(1)} %get-tuple-element.61), channel_id=1, source_target_pairs={{0,1},{1,0},{2,3},{3,2},{4,5},{5,4},{6,7},{7,6},{8,9},{9,8},{10,11... | collective-permute-start | bytes 2359304 | tf_op jit(solution)/shard_map/ppermute | solution.py:307
  51.9 2.4 %collective-permute-start.8 = (f32[64,3072]{1,0:T(8,128)S(1)}, f32[64,3072]{1,0:T(8,128)S(1)}, u32[]{:S(2)}, u32[]{:S(2)}) collective-permute-start(f32[64,3072]{1,0:T(8,128)S(1)} %get-tuple-element.60), channel_id=1, source_target_pairs={{0,1},{1,0},{2,3},{3,2},{4,5},{5,4},{6,7},{7,6},{8,9},{9,8},{10,11... | collective-permute-start | bytes 2359304 | tf_op jit(solution)/shard_map/ppermute | solution.py:307
  52.2 12.0 %collective-permute-start.11 = (f32[32,3072]{1,0:T(8,128)S(1)}, f32[32,3072]{1,0:T(8,128)S(1)}, u32[]{:S(2)}, u32[]{:S(2)}) collective-permute-start(f32[32,3072]{1,0:T(8,128)S(1)} %slice.48), channel_id=1, source_target_pairs={{0,2},{1,3},{2,0},{3,1},{4,6},{5,7},{6,4},{7,5},{8,10},{9,11},{10,... | collective-permute-start | bytes 1179656 | tf_op jit(solution)/shard_map/ppermute | solution.py:310
  64.0 10.3 %collective-permute-start.17 = (f32[64,3072]{1,0:T(8,128)S(1)}, f32[64,3072]{1,0:T(8,128)S(1)}, u32[]{:S(2)}, u32[]{:S(2)}) collective-permute-start(f32[64,3072]{1,0:T(8,128)S(1)} %get-tuple-element.67), channel_id=1, source_target_pairs={{0,1},{1,0},{2,3},{3,2},{4,5},{5,4},{6,7},{7,6},{8,9},{9,8},{10,11... | collective-permute-start | bytes 2359304 | tf_op jit(solution)/shard_map/ppermute | solution.py:307
  64.2 11.4 %copy-start.4 = (f32[6144]{0:T(1024)S(1)}, f32[6144]{0:T(1024)}, u32[]{:S(2)}) copy-start(f32[6144]{0:T(1024)} %param.9) | copy-start | bytes 73732
  73.9 2.8 %collective-permute-start.12 = (f32[64,3072]{1,0:T(8,128)S(1)}, f32[64,3072]{1,0:T(8,128)S(1)}, u32[]{:S(2)}, u32[]{:S(2)}) collective-permute-start(f32[64,3072]{1,0:T(8,128)S(1)} %get-tuple-element.64), channel_id=1, source_target_pairs={{0,1},{1,0},{2,3},{3,2},{4,5},{5,4},{6,7},{7,6},{8,9},{9,8},{10,11... | collective-permute-start | bytes 2359304 | tf_op jit(solution)/shard_map/ppermute | solution.py:307
  74.4 12.0 %collective-permute-start.18 = (f32[32,3072]{1,0:T(8,128)S(1)}, f32[32,3072]{1,0:T(8,128)S(1)}, u32[]{:S(2)}, u32[]{:S(2)}) collective-permute-start(f32[32,3072]{1,0:T(8,128)S(1)} %slice.52), channel_id=1, source_target_pairs={{0,2},{1,3},{2,0},{3,1},{4,6},{5,7},{6,4},{7,5},{8,10},{9,11},{10,... | collective-permute-start | bytes 1179656 | tf_op jit(solution)/shard_map/ppermute | solution.py:310
  75.6 19.3 %collective-permute-start.9 = (f32[32,3072]{1,0:T(8,128)S(1)}, f32[32,3072]{1,0:T(8,128)S(1)}, u32[]{:S(2)}, u32[]{:S(2)}) collective-permute-start(f32[32,3072]{1,0:T(8,128)S(1)} %slice.46), channel_id=1, source_target_pairs={{0,2},{1,3},{2,0},{3,1},{4,6},{5,7},{6,4},{7,5},{8,10},{9,11},{10,... | collective-permute-start | bytes 1179656 | tf_op jit(solution)/shard_map/ppermute | solution.py:310
  76.7 26.6 %collective-permute-start.13 = (f32[32,3072]{1,0:T(8,128)S(1)}, f32[32,3072]{1,0:T(8,128)S(1)}, u32[]{:S(2)}, u32[]{:S(2)}) collective-permute-start(f32[32,3072]{1,0:T(8,128)S(1)} %slice.49), channel_id=1, source_target_pairs={{0,2},{1,3},{2,0},{3,1},{4,6},{5,7},{6,4},{7,5},{8,10},{9,11},{10,... | collective-permute-start | bytes 1179656 | tf_op jit(solution)/shard_map/ppermute | solution.py:310
  86.7 25.1 %collective-permute-start.19 = (f32[32,3072]{1,0:T(8,128)S(1)}, f32[32,3072]{1,0:T(8,128)S(1)}, u32[]{:S(2)}, u32[]{:S(2)}) collective-permute-start(f32[32,3072]{1,0:T(8,128)S(1)} %fusion.9.refs_0_), channel_id=1, source_target_pairs={{0,2},{1,3},{2,0},{3,1},{4,6},{5,7},{6,4},{7,5},{8,10},{9,11},{10,... | collective-permute-start | bytes 1179656 | tf_op jit(solution)/shard_map/ppermute | solution.py:310
  103.5 15.8 %collective-permute-start.14 = (f32[32,3072]{1,0:T(8,128)S(1)}, f32[32,3072]{1,0:T(8,128)S(1)}, u32[]{:S(2)}, u32[]{:S(2)}) collective-permute-start(f32[32,3072]{1,0:T(8,128)S(1)} %fusion.4.refs_0_), channel_id=1, source_target_pairs={{0,2},{1,3},{2,0},{3,1},{4,6},{5,7},{6,4},{7,5},{8,10},{9,11},{10,... | collective-permute-start | bytes 1179656 | tf_op jit(solution)/shard_map/ppermute | solution.py:310
  104.7 14.7 %collective-permute-start.20 = (f32[32,3072]{1,0:T(8,128)S(1)}, f32[32,3072]{1,0:T(8,128)S(1)}, u32[]{:S(2)}, u32[]{:S(2)}) collective-permute-start(f32[32,3072]{1,0:T(8,128)S(1)} %fusion.9.refs_0_), channel_id=1, source_target_pairs={{0,1},{1,0},{2,3},{3,2},{4,5},{5,4},{6,7},{7,6},{8,9},{9,8},{10,11... | collective-permute-start | bytes 1179656 | tf_op jit(solution)/shard_map/ppermute | solution.py:307
  111.7 7.6 %collective-permute-start.21 = (f32[32,3072]{1,0:T(8,128)S(1)}, f32[32,3072]{1,0:T(8,128)S(1)}, u32[]{:S(2)}, u32[]{:S(2)}) collective-permute-start(f32[32,3072]{1,0:T(8,128)S(1)} %collective-permute-done.19.refs_1_), channel_id=1, source_target_pairs={{0,1},{1,0},{2,3},{3,2},{4,5},{5,4},{6,7},{7,6},{8,9},{9,8},{10,11... | collective-permute-start | bytes 1179656 | tf_op jit(solution)/shard_map/ppermute | solution.py:307
  111.7 15.1 %collective-permute-start.15 = (f32[32,3072]{1,0:T(8,128)S(1)}, f32[32,3072]{1,0:T(8,128)S(1)}, u32[]{:S(2)}, u32[]{:S(2)}) collective-permute-start(f32[32,3072]{1,0:T(8,128)S(1)} %fusion.4.refs_0_), channel_id=1, source_target_pairs={{0,1},{1,0},{2,3},{3,2},{4,5},{5,4},{6,7},{7,6},{8,9},{9,8},{10,11... | collective-permute-start | bytes 1179656 | tf_op jit(solution)/shard_map/ppermute | solution.py:307
  119.3 7.5 %collective-permute-start.16 = (f32[32,3072]{1,0:T(8,128)S(1)}, f32[32,3072]{1,0:T(8,128)S(1)}, u32[]{:S(2)}, u32[]{:S(2)}) collective-permute-start(f32[32,3072]{1,0:T(8,128)S(1)} %collective-permute-done.14.refs_1_), channel_id=1, source_target_pairs={{0,1},{1,0},{2,3},{3,2},{4,5},{5,4},{6,7},{7,6},{8,9},{9,8},{10,11... | collective-permute-start | bytes 1179656 | tf_op jit(solution)/shard_map/ppermute | solution.py:307
  130.7 10.1 %collective-permute-start.22 = (f32[32,768]{1,0:T(8,128)S(1)}, f32[32,768]{1,0:T(8,128)S(1)}, u32[]{:S(2)}, u32[]{:S(2)}) collective-permute-start(f32[32,768]{1,0:T(8,128)S(1)} %get-tuple-element.75), channel_id=1, source_target_pairs={{0,12},{4,0},{8,4},{12,8},{1,13},{5,1},{9,5},{13,9},{2,14},{6,2},{... | collective-permute-start | bytes 294920 | tf_op jit(solution)/shard_map/ppermute | solution.py:304
  131.9 10.5 %collective-permute-start.23 = (f32[32,768]{1,0:T(8,128)S(1)}, f32[32,768]{1,0:T(8,128)S(1)}, u32[]{:S(2)}, u32[]{:S(2)}) collective-permute-start(f32[32,768]{1,0:T(8,128)S(1)} %get-tuple-element.76), channel_id=1, source_target_pairs={{0,8},{4,12},{8,0},{12,4},{1,9},{5,13},{9,1},{13,5},{2,10},{6,14},... | collective-permute-start | bytes 294920 | tf_op jit(solution)/shard_map/ppermute | solution.py:304
  131.9 10.5 %collective-permute-start.24 = (f32[32,768]{1,0:T(8,128)S(1)}, f32[32,768]{1,0:T(8,128)S(1)}, u32[]{:S(2)}, u32[]{:S(2)}) collective-permute-start(f32[32,768]{1,0:T(8,128)S(1)} %get-tuple-element.77), channel_id=1, source_target_pairs={{0,4},{4,8},{8,12},{12,0},{1,5},{5,9},{9,13},{13,1},{2,6},{6,10},{... | collective-permute-start | bytes 294920 | tf_op jit(solution)/shard_map/ppermute | solution.py:304
  136.8 7.2 %collective-permute-start.25 = (f32[32,768]{1,0:T(8,128)S(1)}, f32[32,768]{1,0:T(8,128)S(1)}, u32[]{:S(2)}, u32[]{:S(2)}) collective-permute-start(f32[32,768]{1,0:T(8,128)S(1)} %get-tuple-element.79), channel_id=1, source_target_pairs={{0,12},{4,0},{8,4},{12,8},{1,13},{5,1},{9,5},{13,9},{2,14},{6,2},{... | collective-permute-start | bytes 294920 | tf_op jit(solution)/shard_map/ppermute | solution.py:304
  139.8 10.6 %collective-permute-start.26 = (f32[32,768]{1,0:T(8,128)S(1)}, f32[32,768]{1,0:T(8,128)S(1)}, u32[]{:S(2)}, u32[]{:S(2)}) collective-permute-start(f32[32,768]{1,0:T(8,128)S(1)} %get-tuple-element.80), channel_id=1, source_target_pairs={{0,8},{4,12},{8,0},{12,4},{1,9},{5,13},{9,1},{13,5},{2,10},{6,14},... | collective-permute-start | bytes 294920 | tf_op jit(solution)/shard_map/ppermute | solution.py:304
  140.9 9.5 %collective-permute-start.27 = (f32[32,768]{1,0:T(8,128)S(1)}, f32[32,768]{1,0:T(8,128)S(1)}, u32[]{:S(2)}, u32[]{:S(2)}) collective-permute-start(f32[32,768]{1,0:T(8,128)S(1)} %get-tuple-element.81), channel_id=1, source_target_pairs={{0,4},{4,8},{8,12},{12,0},{1,5},{5,9},{9,13},{13,1},{2,6},{6,10},{... | collective-permute-start | bytes 294920 | tf_op jit(solution)/shard_map/ppermute | solution.py:304
  (1 other events, 0.9 us)

commit v6 on v5

--- a/solution.py
+++ b/solution.py
@@ -179,13 +179,15 @@
     )(place, *blocks, *[pltpu.with_memory_space_constraint(part, pltpu.VMEM) for part in weight], *earlier, *after)
 
 
-def stream_kernel(slots, first_column, depth, place_ref, *refs):
+def stream_kernel(slots, first_column, span, earlier, depth, place_ref, *refs):
     slot_refs, weight_ref = refs[:slots], refs[slots]
     send_ref, keep_ref, high_ref, low_ref, both, landed, arrived = refs[-7:]
+    for part_ref, whole_ref in zip(refs[slots + 1 : slots + 1 + earlier], (send_ref, keep_ref)):
+        whole_ref[:, : span[0]] = part_ref[...]
     block = slot_refs[0].shape[0]
     total = block * slots
     width = landed.shape[2]
-    steps = send_ref.shape[1] // width
+    steps = span[1] // width
 
     def fetch(step):
         start = pl.multiple_of(first_column + step * width, width)
@@ -208,6 +210,7 @@
         high_ref[:, at] = high
         low_ref[:, at] = low
         part = three_pass(both, high, low, 0, False)
+        at = pl.ds(pl.multiple_of(span[0] + step * width, width), width)
         keep_ref[:, at] = part[: total // 2]
         send_ref[:, at] = part[total // 2 :]
 
@@ -216,20 +219,22 @@
             fetch(step + depth).start()
 
 
-def stream(blocks, weight, place, columns, after):
+def stream(blocks, weight, place, first_column, span, earlier, after):
     slots, (block, rows) = len(blocks), blocks[0].shape
-    half, hidden = block * slots // 2, columns[1]
-    width = divisor(hidden, 256, 128)
+    half, hidden = block * slots // 2, sum(span)
+    width = divisor(span[1], 256, 128)
     depth = 3
     out = jax.ShapeDtypeStruct((half, hidden), jnp.float32)
-    kept = pltpu.VMEM((rows, hidden), jnp.bfloat16)
+    kept = pltpu.VMEM((rows, span[1]), jnp.bfloat16)
     inside = pl.BlockSpec(memory_space=pltpu.VMEM)
     result = pl.pallas_call(
-        functools.partial(stream_kernel, slots, columns[0], depth),
+        functools.partial(stream_kernel, slots, first_column, span, len(earlier), depth),
         out_shape=(out, out, kept, kept),
         in_specs=[pl.BlockSpec(memory_space=pltpu.SMEM)]
         + [inside] * slots
-        + [pl.BlockSpec(memory_space=pl.ANY)] * (1 + len(after)),
+        + [pl.BlockSpec(memory_space=pl.ANY)]
+        + [inside] * len(earlier)
+        + [pl.BlockSpec(memory_space=pl.ANY)] * len(after),
         out_specs=[inside] * 4,
         scratch_shapes=[
             pltpu.VMEM((2 * block * slots, rows), jnp.bfloat16),
@@ -238,13 +243,13 @@
         ],
         compiler_params=pltpu.CompilerParams(vmem_limit_bytes=2 * VMEM_LIMIT),
         cost_estimate=SHORT,
-    )(place, *blocks, pltpu.with_memory_space_constraint(weight, pltpu.HBM), *after)
+    )(place, *blocks, pltpu.with_memory_space_constraint(weight, pltpu.HBM), *earlier, *after)
     return result[:2], result[2:]
 
 
-def backward_kernel(slots, earlier, first_column, streamed, place_ref, *refs):
-    act_refs, (high_ref, low_ref) = refs[:slots], refs[slots : slots + 2]
-    earlier_refs = refs[slots + 2 : slots + 2 + earlier]
+def backward_kernel(slots, pieces, earlier, first_column, place_ref, *refs):
+    act_refs, weight_refs = refs[:slots], refs[slots : slots + 2 * pieces]
+    earlier_refs = refs[slots + 2 * pieces : slots + 2 * pieces + earlier]
     out_refs = refs[-2 - slots : -2]
     both, result = refs[-2:]
     block = act_refs[0].shape[0]
@@ -261,7 +266,12 @@
     def _(step):
         start = pl.multiple_of(step * width, width)
         tile = (pl.ds(pl.multiple_of(first_column + start, width), width), slice(None))
-        result[...] = three_pass(both, high_ref[tile], low_ref[tile], 1, streamed)
+        total_sum, column = 0.0, 0
+        for high_ref, low_ref in zip(weight_refs[::2], weight_refs[1::2]):
+            columns = slice(column, column + high_ref.shape[1])
+            total_sum += three_pass(both[:, columns], high_ref[tile], low_ref[tile], 1, False)
+            column = columns.stop
+        result[...] = total_sum
         for b in range(slots):
             row = pl.multiple_of(place_ref[b] * block, block)
             rows = result[pl.ds(row, block), :]
@@ -270,17 +280,17 @@
             out_refs[b][:, pl.ds(start, width)] = rows
 
 
-def backward(acts, weight, place, earlier, part, parts, streamed, after):
+def backward(acts, weights, place, earlier, part, parts, after):
     slots, (block, hidden) = len(acts), acts[0].shape
-    depth = weight[0].shape[0] // parts
+    depth = weights[0].shape[0] // parts
     width = divisor(depth, 256, 128)
     out = jax.ShapeDtypeStruct((block, depth), jnp.float32)
     inside = pl.BlockSpec(memory_space=pltpu.VMEM)
     return pl.pallas_call(
-        functools.partial(backward_kernel, slots, len(earlier), part * depth, streamed),
+        functools.partial(backward_kernel, slots, len(weights) // 2, len(earlier), part * depth),
         out_shape=[out] * slots,
         in_specs=[pl.BlockSpec(memory_space=pltpu.SMEM)]
-        + [inside] * (slots + 2 + len(earlier))
+        + [inside] * (slots + len(weights) + len(earlier))
         + [pl.BlockSpec(memory_space=pl.ANY)] * len(after),
         out_specs=[inside] * slots,
         scratch_shapes=[
@@ -289,7 +299,7 @@
         ],
         compiler_params=pltpu.CompilerParams(vmem_limit_bytes=VMEM_LIMIT),
         cost_estimate=SHORT,
-    )(place, *acts, *[pltpu.with_memory_space_constraint(part, pltpu.VMEM) for part in weight], *earlier, *after)
+    )(place, *acts, *[pltpu.with_memory_space_constraint(part, pltpu.VMEM) for part in weights], *earlier, *after)
 
 
 def body(hid_size, emb_size, inputs, out_grad, in_weight, in_bias, out_weight, norm_gain):
@@ -318,14 +328,34 @@
     grads = gathered(out_grad)
     piece = hidden // CHUNKS
 
+    def tied(values, others):
+        return lax.optimization_barrier((values, others))
+
+    def halved(partial, behind=()):
+        send, keep = partial
+        return keep + tied(other_core(send), behind)[0]
+
+    def exchanged(summed):
+        terms = [summed[d * tokens : (d + 1) * tokens] for d in range(chips)]
+        arrival = next_chip(terms[chips - 1])
+        for step in range(2, chips):
+            arrival = next_chip(arrival + terms[chips - step])
+        return arrival, terms[0]
+
+    def prepared(c, after):
+        return prepare(out_weight, (c * quarter, quarter), (0, depth), after)
+
+    def back(c, earlier, after):
+        return forward(grads, out_parts[c], place, False, False, (c % 2 * quarter, quarter), earlier, after)
+
+    quarter = piece // 2
     moments = call(moments_kernel, jax.ShapeDtypeStruct((2 * tokens, 128), jnp.float32), (inputs,), ())
-    quarter = piece // 2
-    out_parts = [prepare(out_weight, (0, quarter), (0, depth), [place, moments])]
-    moments = call(
-        functools.partial(merge_kernel, depth), moments, (moments, other_core(moments)), (out_parts[0][0],)
-    )
-    for c in range(1, 4):
-        out_parts.append(prepare(out_weight, (c * quarter, quarter), (0, depth), [moments, out_parts[-1][0]]))
+    out_parts = [prepared(0, [place, moments])]
+    out_parts.append(prepared(1, [out_parts[0][0]]))
+    out_parts.append(prepared(2, [out_parts[1][0]]))
+    back_0 = back(0, (), [out_parts[2][0]])
+    moments = call(functools.partial(merge_kernel, depth), moments, (moments, other_core(moments)), (back_0[0],))
+    back_0 = back(1, back_0, [moments])
     parts = [moments]
     for _ in range(1, chips):
         parts.append(next_chip(parts[-1]))
@@ -333,38 +363,32 @@
         functools.partial(normalise_kernel, 2 * depth),
         (inputs, inputs, jax.ShapeDtypeStruct((tokens, 128), jnp.float32)),
         (inputs, norm_gain[None, :], *parts),
-        (out_parts[-1][0],),
+        (back_0[1],),
     )
     inv_std = inv_std[:, :1]
     scaled = gathered(scaled)
-
-    def halved(partial):
-        send, keep = partial
-        return keep + other_core(send)
-
-    def exchanged(summed):
-        terms = [summed[d * tokens : (d + 1) * tokens] for d in range(chips)]
-        arrival = next_chip(terms[chips - 1])
-        for step in range(2, chips):
-            arrival = next_chip(arrival + terms[chips - step])
-        return arrival, terms[0]
-
-    def back(c, streamed, earlier, after):
+    back_0, _ = tied(back_0, parts)
+    out_parts.append(prepared(3, [scaled[0]]))
+    half_0 = halved(back_0, (out_parts[3], scaled[1], scaled[-1]))
+    back_1 = back(2, (), [out_parts[3][0], half_0])
+    back_1 = back(3, back_1, [scaled[1], scaled[-1]])
+    back_0 = exchanged(half_0)
+    back_1, (back_0, scaled[2:-1]) = tied(back_1, (back_0, scaled[2:-1]))
+
+    def pre(c, earlier, after):
         span = (c % 2 * quarter, quarter)
-        return forward(grads, out_parts[c], place, False, streamed, span, earlier, after)
-
-    near, far = [scaled[1], scaled[-1]], scaled[2 : hid_size - 1]
-    back_0 = back(0, True, (), [scaled[0]])
-    back_0 = back(1, False, back_0, [])
-    half_0 = halved(back_0)
-    back_1 = back(2, True, (), [back_0[1], *near])
-    back_1 = back(3, False, back_1, far)
-    half_1 = halved(back_1)
-    back_0, back_1 = exchanged(half_0), exchanged(half_1)
-    pre_0, in_parts_0 = stream(scaled, in_weight, place, (0, piece), [half_0, half_1])
-    pre_1, in_parts_1 = stream(scaled, in_weight, place, (piece, piece), [pre_0[1], back_0[0]])
+        return stream(scaled, in_weight, place, c * quarter, span, earlier, after)
+
+    pre_0, in_parts_0 = pre(0, (), [back_1[1]])
+    half_1 = halved(back_1, pre_0)
+    back_1 = exchanged(half_1)
+    pre_0, in_parts_1 = pre(1, pre_0, [half_1])
+    pre_1, in_parts_2 = pre(2, (), [pre_0[1]])
+    half_0 = halved(pre_0, pre_1)
+    pre_1, in_parts_3 = pre(3, pre_1, [half_0])
+    pre_1, back_1 = tied(pre_1, back_1)
     backs = [back_0, back_1]
-    pres = [exchanged(halved(pre_0)), exchanged(halved(pre_1))]
+    pres = [exchanged(half_0), exchanged(halved(pre_1))]
 
     def spread_out(c):
         act = sum(backs[c]) * gelu_slope(sum(pres[c]) + in_bias[c * piece : (c + 1) * piece])
@@ -373,17 +397,22 @@
         for step in range(1, chips):
             act = next_chip(act)
             mine[(chips - step) % chips] = act
+        return mine
+
+    def both_cores(mine):
         return mine + [other_core(block) for block in mine]
 
     def summed_along_hid(sums):
         return sum([along_hid(sums[step], -step) for step in range(1, hid_size)], start=sums[0])
 
     acts_0, acts_1 = spread_out(0), spread_out(1)
-    sums = backward(acts_0, in_parts_0, place, (), 0, 1, True, [pre_1[1]])
+    sums = backward(both_cores(acts_0), in_parts_0 + in_parts_1, place, (), 0, 1, [pre_1[1]])
+    acts_1[1:], sums = tied(acts_1[1:], sums)
+    acts_1, in_parts_1 = both_cores(acts_1), in_parts_2 + in_parts_3
     parts = 2 if depth % 512 == 0 else 1
     ends = []
     for part in range(parts):
-        ends.append(backward(acts_1, in_parts_1, place, sums, part, parts, False, [ends[-1][0] if ends else sums[0]]))
+        ends.append(backward(acts_1, in_parts_1, place, sums, part, parts, [ends[-1][0] if ends else sums[0]]))
     running = jnp.concatenate([summed_along_hid(end) for end in ends], axis=1)
     normed_grad = running * norm_gain
     totals = lax.psum(

time: 158 us -> 148 us (0.937)
  waiting for transfers between devices: 51.4 us -> 35.6 us
  Pallas kernels: 69 us -> 72 us
  starting transfers between devices: 27.6 us -> 30.3 us
    ppermute x7, waiting for transfers between devices: 38.2 us -> 22.9 us  [next_chip(): lax.ppermute(values, 'emb', [(i, (i + 2) % emb_size) for i in range(emb_s...]
    ppermute x12, starting transfers between devices: 17.9 us -> 21.3 us  [along_hid(): lax.ppermute(values, 'hid', [(i, (i + steps) % hid_size) for i in range(h...]
    pallas_call x5 -> x7, Pallas kernels: 34.5 us -> 37.6 us  [the longest x4 22.2 us: stream(): pl.pallas_call(functools.partial(stream_kernel, slots, first_column, span...]
  transfers between devices with their start and end apart: 28 -> 28, of which waited for: 11 -> 10; matrix products, arithmetic and copies ran while one was open for 1% -> 1% of each run, Pallas kernels for 41% -> 42%
where the time goes in v6:
time: 148 us
  Pallas kernels  72 us (49%)
  waiting for transfers between devices  35.6 us (24%)
  starting transfers between devices  30.3 us (20%)
  blocking collectives  6.16 us (4%)
  other arithmetic  1.88 us (1%)
    ppermute x7, waiting for transfers between devices, next_chip(): lax.ppermute(values, 'emb', [(i, (i + 2) % emb_size) for i in range(emb_s...  22.9 us
    pallas_call x4, Pallas kernels, stream(): pl.pallas_call(functools.partial(stream_kernel, slots, first_column, span...  22.2 us
    ppermute x12, starting transfers between devices, along_hid(): lax.ppermute(values, 'hid', [(i, (i + steps) % hid_size) for i in range(h...  21.3 us
    pallas_call x4, Pallas kernels, prepare(): pl.pallas_call(functools.partial(prepare_kernel, rows, columns, block, de...  18.8 us
    pallas_call x3, Pallas kernels, backward(): pl.pallas_call(functools.partial(backward_kernel, slots, len(weights) //...  15.4 us
    pallas_call x4, Pallas kernels, forward(): pl.pallas_call(functools.partial(forward_kernel, slots, 0 if by_column el...  15.3 us
    ppermute x12, waiting for transfers between devices, along_hid(): lax.ppermute(values, 'hid', [(i, (i + steps) % hid_size) for i in range(h...  11.1 us
    ppermute x7, starting transfers between devices, next_chip(): lax.ppermute(values, 'emb', [(i, (i + 2) % emb_size) for i in range(emb_s...  8.02 us
  transfers between devices with their start and end apart: 28, of which 10 were waited for; matrix products, arithmetic and copies ran while one was open for 1% of the time, Pallas kernels for 42%

profile of v6, /device:TPU:0, one launch (start us, length us, event | category | flops | bytes accessed | tf_op | source)
XLA Modules:
  0.0 147.6 jit_solution(535423016252186902)
XLA Ops:
  0.0 3.0 %collective-permute-start.1 = (f32[32,1536]{1,0:T(8,128)}, f32[32,1536]{1,0:T(8,128)S(1)}, u32[]{:S(2)}, u32[]{:S(2)}) collective-permute-start(f32[32,1536]{1,0:T(8,128)} %refs_0_.11), channel_id=1, source_target_pairs={{0,4},{4,8},{8,12},{12,0},{1,5},{5,9},{9,13},{13,1},{2,6},{6,10},{... | collective-permute-start | bytes 589832 | tf_op jit(solution)/shard_map/ppermute | solution.py:314
  3.0 2.6 %collective-permute-start.2 = (f32[32,1536]{1,0:T(8,128)}, f32[32,1536]{1,0:T(8,128)S(1)}, u32[]{:S(2)}, u32[]{:S(2)}) collective-permute-start(f32[32,1536]{1,0:T(8,128)} %refs_0_.11), channel_id=1, source_target_pairs={{0,8},{4,12},{8,0},{12,4},{1,9},{5,13},{9,1},{13,5},{2,10},{6,14},... | collective-permute-start | bytes 589832 | tf_op jit(solution)/shard_map/ppermute | solution.py:314
  8.1 4.7 %shard_map.65 = (bf16[1536,1536]{1,0:T(8,128)(2,1)S(1)}, bf16[1536,1536]{1,0:T(8,128)(2,1)S(1)}) custom-call(f32[6144,1536]{1,0:T(8,128)} %weight_ref.7, s32[4]{0:T(128)S(1)} %fusion.13.refs_0_.place_ref, f32[64,128]{1,0:T(8,128)S(1)} %shard_map.64.refs_1_.refs_0_), custom_call_target="tpu_custom_call" | custom-call | flops 1048576 | bytes 262144 | tf_op jit(solution)/shard_map/pallas_call | solution.py:111
  12.8 4.7 %shard_map.66 = (bf16[1536,1536]{1,0:T(8,128)(2,1)S(1)}, bf16[1536,1536]{1,0:T(8,128)(2,1)S(1)}) custom-call(f32[6144,1536]{1,0:T(8,128)} %weight_ref.7, bf16[1536,1536]{1,0:T(8,128)(2,1)S(1)} %get-tuple-element.71.refs_0_.refs_4_), custom_call_target="tpu_custom_call" | custom-call | flops 1048576 | bytes 262144 | tf_op jit(solution)/shard_map/pallas_call | solution.py:111
  17.5 4.7 %shard_map.67 = (bf16[1536,1536]{1,0:T(8,128)(2,1)S(1)}, bf16[1536,1536]{1,0:T(8,128)(2,1)S(1)}) custom-call(f32[6144,1536]{1,0:T(8,128)} %weight_ref.7, bf16[1536,1536]{1,0:T(8,128)(2,1)S(1)} %get-tuple-element.73.refs_0_.refs_4_), custom_call_target="tpu_custom_call" | custom-call | flops 1048576 | bytes 262144 | tf_op jit(solution)/shard_map/pallas_call | solution.py:111
  22.3 3.8 %shard_map.68 = (f32[64,1536]{1,0:T(8,128)S(1)}, f32[64,1536]{1,0:T(8,128)S(1)}) custom-call(s32[4]{0:T(128)S(1)} %fusion.13.refs_0_.place_ref, f32[32,1536]{1,0:T(8,128)S(1)} %copy-done, f32[32,1536]{1,0:T(8,128)S(1)} %collective-permute-done.1.refs_1_, f32[32,1536]{1,0:T(8,128)S(1)} %collective-permute-done.2.refs_2_, ...), custom_call_target="tpu_custom_call" | custom-call | flops 1048576 | bytes 262144 | tf_op jit(solution)/shard_map/pallas_call | solution.py:169
  26.2 1.6 %collective-permute-start.4 = (f32[64,128]{1,0:T(8,128)S(1)}, f32[64,128]{1,0:T(8,128)S(1)}, u32[]{:S(2)}, u32[]{:S(2)}) collective-permute-start(f32[64,128]{1,0:T(8,128)S(1)} %shard_map.69.refs_8_.refs_2_), channel_id=1, source_target_pairs={{0,2},{1,3},{2,0},{3,1},{4,6},{5,7},{6,4},{7,5},{8,10},{9,11},{10,... | collective-permute-start | bytes 98312 | tf_op jit(solution)/shard_map/ppermute | solution.py:320
  27.7 3.8 %shard_map.70 = (f32[64,3072]{1,0:T(8,128)S(1)}, f32[64,3072]{1,0:T(8,128)S(1)}) custom-call(s32[4]{0:T(128)S(1)} %fusion.13.refs_0_.place_ref, f32[32,1536]{1,0:T(8,128)S(1)} %copy-done, f32[32,1536]{1,0:T(8,128)S(1)} %collective-permute-done.1.refs_1_, f32[32,1536]{1,0:T(8,128)S(1)} %collective-permute-done.2.refs_2_, ...), custom_call_target="tpu_custom_call" | custom-call | flops 1048576 | bytes 262144 | tf_op jit(solution)/shard_map/pallas_call | solution.py:169
  32.9 3.0 %collective-permute-start.7 = (f32[32,1536]{1,0:T(8,128)S(1)}, f32[32,1536]{1,0:T(8,128)S(1)}, u32[]{:S(2)}, u32[]{:S(2)}) collective-permute-start(f32[32,1536]{1,0:T(8,128)S(1)} %get-tuple-element.80.refs_0_), channel_id=1, source_target_pairs={{0,12},{4,0},{8,4},{12,8},{1,13},{5,1},{9,5},{13,9},{2,14},{6,2},{... | collective-permute-start | bytes 589832 | tf_op jit(solution)/shard_map/ppermute | solution.py:314
  35.9 4.7 %shard_map.72 = (bf16[1536,1536]{1,0:T(8,128)(2,1)S(1)}, bf16[1536,1536]{1,0:T(8,128)(2,1)S(1)}) custom-call(f32[6144,1536]{1,0:T(8,128)} %weight_ref.7, f32[32,1536]{1,0:T(8,128)S(1)} %get-tuple-element.80.refs_0_), custom_call_target="tpu_custom_call" | custom-call | flops 1048576 | bytes 262144 | tf_op jit(solution)/shard_map/pallas_call | solution.py:111
  41.6 2.5 %collective-permute-done.7.refs_9_.refs_3_ = f32[32,1536]{1,0:T(8,128)S(1)} collective-permute-done((f32[32,1536]{1,0:T(8,128)S(1)}, f32[32,1536]{1,0:T(8,128)S(1)}, u32[]{:S(2)}, u32[]{:S(2)}) %collective-permute-start.7) | collective-permute-done | bytes 196640 | tf_op jit(solution)/shard_map/ppermute | solution.py:314
  44.9 1.6 %collective-permute-start.9 = (f32[32,1536]{1,0:T(8,128)S(1)}, f32[32,1536]{1,0:T(8,128)S(1)}, u32[]{:S(2)}, u32[]{:S(2)}) collective-permute-start(f32[32,1536]{1,0:T(8,128)S(1)} %get-tuple-element.80.refs_0_), channel_id=1, source_target_pairs={{0,8},{4,12},{8,0},{12,4},{1,9},{5,13},{9,1},{13,5},{2,10},{6,14},... | collective-permute-start | bytes 589832 | tf_op jit(solution)/shard_map/ppermute | solution.py:314
  46.6 3.8 %shard_map.73 = (f32[64,1536]{1,0:T(8,128)S(1)}, f32[64,1536]{1,0:T(8,128)S(1)}) custom-call(s32[4]{0:T(128)S(1)} %fusion.13.refs_0_.place_ref, f32[32,1536]{1,0:T(8,128)S(1)} %copy-done, f32[32,1536]{1,0:T(8,128)S(1)} %collective-permute-done.1.refs_1_, f32[32,1536]{1,0:T(8,128)S(1)} %collective-permute-done.2.refs_2_, ...), custom_call_target="tpu_custom_call" | custom-call | flops 1048576 | bytes 262144 | tf_op jit(solution)/shard_map/pallas_call | solution.py:169
  50.4 3.8 %shard_map.74 = (f32[64,3072]{1,0:T(8,128)S(1)}, f32[64,3072]{1,0:T(8,128)S(1)}) custom-call(s32[4]{0:T(128)S(1)} %fusion.13.refs_0_.place_ref, f32[32,1536]{1,0:T(8,128)S(1)} %copy-done, f32[32,1536]{1,0:T(8,128)S(1)} %collective-permute-done.1.refs_1_, f32[32,1536]{1,0:T(8,128)S(1)} %collective-permute-done.2.refs_2_, ...), custom_call_target="tpu_custom_call" | custom-call | flops 1048576 | bytes 262144 | tf_op jit(solution)/shard_map/pallas_call | solution.py:169
  54.2 1.7 %collective-permute-done.9.refs_2_ = f32[32,1536]{1,0:T(8,128)S(1)} collective-permute-done((f32[32,1536]{1,0:T(8,128)S(1)}, f32[32,1536]{1,0:T(8,128)S(1)}, u32[]{:S(2)}, u32[]{:S(2)}) %collective-permute-start.9) | collective-permute-done | bytes 196640 | tf_op jit(solution)/shard_map/ppermute | solution.py:314
  56.0 5.6 %shard_map.75 = (f32[64,1536]{1,0:T(8,128)S(1)}, f32[64,1536]{1,0:T(8,128)S(1)}, bf16[1536,1536]{1,0:T(8,128)(2,1)S(1)}, bf16[1536,1536]{1,0:T(8,128)(2,1)S(1)}) custom-call(s32[4]{0:T(128)S(1)} %fusion.13.refs_0_.place_ref, f32[32,1536]{1,0:T(8,128)S(1)} %get-tuple-element.80.refs_0_, f32[32,1536]{1,0:T(8,128)S(1)} %collective-permute-done.5.refs_8_.refs_1_, ...), custom_call_target="tpu_custom_call" | custom-call | flops 1048576 | bytes 262144 | tf_op jit(solution)/shard_map/pallas_call | solution.py:230
  61.7 5.5 %shard_map.76 = (f32[64,3072]{1,0:T(8,128)S(1)}, f32[64,3072]{1,0:T(8,128)S(1)}, bf16[1536,1536]{1,0:T(8,128)(2,1)S(1)}, bf16[1536,1536]{1,0:T(8,128)(2,1)S(1)}) custom-call(s32[4]{0:T(128)S(1)} %fusion.13.refs_0_.place_ref, f32[32,1536]{1,0:T(8,128)S(1)} %get-tuple-element.80.refs_0_, f32[32,1536]{1,0:T(8,128)S(1)} %collective-permute-done.5.refs_8_.refs_1_, ...), custom_call_target="tpu_custom_call" | custom-call | flops 1048576 | bytes 262144 | tf_op jit(solution)/shard_map/pallas_call | solution.py:230
  67.8 1.5 %collective-permute-start.12 = (f32[32,3072]{1,0:T(8,128)S(1)}, f32[32,3072]{1,0:T(8,128)S(1)}, u32[]{:S(2)}, u32[]{:S(2)}) collective-permute-start(f32[32,3072]{1,0:T(8,128)S(1)} %get-tuple-element.140), channel_id=1, source_target_pairs={{0,2},{1,3},{2,0},{3,1},{4,6},{5,7},{6,4},{7,5},{8,10},{9,11},{10,... | collective-permute-start | bytes 1179656 | tf_op jit(solution)/shard_map/ppermute | solution.py:320
  69.4 5.5 %shard_map.77 = (f32[64,1536]{1,0:T(8,128)S(1)}, f32[64,1536]{1,0:T(8,128)S(1)}, bf16[1536,1536]{1,0:T(8,128)(2,1)S(1)}, bf16[1536,1536]{1,0:T(8,128)(2,1)S(1)}) custom-call(s32[4]{0:T(128)S(1)} %fusion.13.refs_0_.place_ref, f32[32,1536]{1,0:T(8,128)S(1)} %get-tuple-element.80.refs_0_, f32[32,1536]{1,0:T(8,128)S(1)} %collective-permute-done.5.refs_8_.refs_1_, ...), custom_call_target="tpu_custom_call" | custom-call | flops 1048576 | bytes 262144 | tf_op jit(solution)/shard_map/pallas_call | solution.py:230
  75.7 5.6 %shard_map.78 = (f32[64,3072]{1,0:T(8,128)S(1)}, f32[64,3072]{1,0:T(8,128)S(1)}, bf16[1536,1536]{1,0:T(8,128)(2,1)S(1)}, bf16[1536,1536]{1,0:T(8,128)(2,1)S(1)}) custom-call(s32[4]{0:T(128)S(1)} %fusion.13.refs_0_.place_ref, f32[32,1536]{1,0:T(8,128)S(1)} %get-tuple-element.80.refs_0_, f32[32,1536]{1,0:T(8,128)S(1)} %collective-permute-done.5.refs_8_.refs_1_, ...), custom_call_target="tpu_custom_call" | custom-call | flops 1048576 | bytes 262144 | tf_op jit(solution)/shard_map/pallas_call | solution.py:230
  81.4 6.0 %collective-permute-done.16 = f32[32,3072]{1,0:T(8,128)S(1)} collective-permute-done((f32[32,3072]{1,0:T(8,128)S(1)}, f32[32,3072]{1,0:T(8,128)S(1)}, u32[]{:S(2)}, u32[]{:S(2)}) %collective-permute-start.16) | collective-permute-done | bytes 393248 | tf_op jit(solution)/shard_map/ppermute | solution.py:320
  89.9 9.8 %collective-permute-done.17.refs_1_ = f32[32,3072]{1,0:T(8,128)S(1)} collective-permute-done((f32[32,3072]{1,0:T(8,128)S(1)}, f32[32,3072]{1,0:T(8,128)S(1)}, u32[]{:S(2)}, u32[]{:S(2)}) %collective-permute-start.17) | collective-permute-done | bytes 393248 | tf_op jit(solution)/shard_map/ppermute | solution.py:320
  99.7 6.6 %collective-permute-done.14 = f32[32,3072]{1,0:T(8,128)S(1)} collective-permute-done((f32[32,3072]{1,0:T(8,128)S(1)}, f32[32,3072]{1,0:T(8,128)S(1)}, u32[]{:S(2)}, u32[]{:S(2)}) %collective-permute-start.14) | collective-permute-done | bytes 393248 | tf_op jit(solution)/shard_map/ppermute | solution.py:320
  108.0 7.3 %shard_map.79 = (f32[32,1536]{1,0:T(8,128)S(1)}, f32[32,1536]{1,0:T(8,128)S(1)}, f32[32,1536]{1,0:T(8,128)S(1)}, f32[32,1536]{1,0:T(8,128)S(1)}) custom-call(s32[4]{0:T(128)S(1)} %fusion.13.refs_0_.place_ref, f32[32,3072]{1,0:T(8,128)S(1)} %fusion.9.refs_0_, f32[32,3072]{1,0:T(8,128)S(1)} %collective-permute-done.17.refs_1_, ...), custom_call_target="tpu_custom_call" | custom-call | flops 1048576 | bytes 262144 | tf_op jit(solution)/shard_map/pallas_call | solution.py:289
  115.9 1.7 %collective-permute-done.21.refs_3_ = f32[32,3072]{1,0:T(8,128)S(1)} collective-permute-done((f32[32,3072]{1,0:T(8,128)S(1)}, f32[32,3072]{1,0:T(8,128)S(1)}, u32[]{:S(2)}, u32[]{:S(2)}) %collective-permute-start.21) | collective-permute-done | bytes 393248 | tf_op jit(solution)/shard_map/ppermute | solution.py:317
  117.6 4.0 %shard_map.80 = (f32[32,768]{1,0:T(8,128)S(1)}, f32[32,768]{1,0:T(8,128)S(1)}, f32[32,768]{1,0:T(8,128)S(1)}, f32[32,768]{1,0:T(8,128)S(1)}) custom-call(s32[4]{0:T(128)S(1)} %fusion.13.refs_0_.place_ref, f32[32,3072]{1,0:T(8,128)S(1)} %fusion.4.refs_0_, f32[32,3072]{1,0:T(8,128)S(1)} %collective-permute-done.15.refs_1_, ...), custom_call_target="tpu_custom_call" | custom-call | flops 1048576 | bytes 262144 | tf_op jit(solution)/shard_map/pallas_call | solution.py:289
  121.7 3.0 %collective-permute-start.23 = (f32[32,768]{1,0:T(8,128)S(1)}, f32[32,768]{1,0:T(8,128)S(1)}, u32[]{:S(2)}, u32[]{:S(2)}) collective-permute-start(f32[32,768]{1,0:T(8,128)S(1)} %get-tuple-element.130), channel_id=1, source_target_pairs={{0,8},{4,12},{8,0},{12,4},{1,9},{5,13},{9,1},{13,5},{2,10},{6,14},... | collective-permute-start | bytes 294920 | tf_op jit(solution)/shard_map/ppermute | solution.py:314
  125.6 4.1 %shard_map.81 = (f32[32,768]{1,0:T(8,128)S(1)}, f32[32,768]{1,0:T(8,128)S(1)}, f32[32,768]{1,0:T(8,128)S(1)}, f32[32,768]{1,0:T(8,128)S(1)}) custom-call(s32[4]{0:T(128)S(1)} %fusion.13.refs_0_.place_ref, f32[32,3072]{1,0:T(8,128)S(1)} %fusion.4.refs_0_, f32[32,3072]{1,0:T(8,128)S(1)} %collective-permute-done.15.refs_1_, ...), custom_call_target="tpu_custom_call" | custom-call | flops 1048576 | bytes 262144 | tf_op jit(solution)/shard_map/pallas_call | solution.py:289
  131.8 2.8 %collective-permute-start.25 = (f32[32,768]{1,0:T(8,128)S(1)}, f32[32,768]{1,0:T(8,128)S(1)}, u32[]{:S(2)}, u32[]{:S(2)}) collective-permute-start(f32[32,768]{1,0:T(8,128)S(1)} %get-tuple-element.133), channel_id=1, source_target_pairs={{0,12},{4,0},{8,4},{12,8},{1,13},{5,1},{9,5},{13,9},{2,14},{6,2},{... | collective-permute-start | bytes 294920 | tf_op jit(solution)/shard_map/ppermute | solution.py:314
  134.7 2.5 %collective-permute-done.27 = f32[32,768]{1,0:T(8,128)S(1)} collective-permute-done((f32[32,768]{1,0:T(8,128)S(1)}, f32[32,768]{1,0:T(8,128)S(1)}, u32[]{:S(2)}, u32[]{:S(2)}) %collective-permute-start.27) | collective-permute-done | bytes 98336 | tf_op jit(solution)/shard_map/ppermute | solution.py:314
  137.2 3.2 %collective-permute-done.26 = f32[32,768]{1,0:T(8,128)S(1)} collective-permute-done((f32[32,768]{1,0:T(8,128)S(1)}, f32[32,768]{1,0:T(8,128)S(1)}, u32[]{:S(2)}, u32[]{:S(2)}) %collective-permute-start.26) | collective-permute-done | bytes 98336 | tf_op jit(solution)/shard_map/ppermute | solution.py:314
  140.7 6.2 %psum.7 = f32[2,32]{1,0:T(2,128)S(1)} all-reduce(f32[2,32]{1,0:T(2,128)S(1)} %pad_maximum_fusion), channel_id=1, replica_groups=mesh['groups'=2,'hid'=4,'emb'=4] {'emb'}, use_global_device_ids=true, to_apply=%region_2.3 | all-reduce | flops 64 | bytes 512 | tf_op jit(solution)/shard_map/psum | solution.py:418
  (74 shorter events, 16.3 us)
Async XLA Ops:
  0.0 22.3 %collective-permute-start.1 = (f32[32,1536]{1,0:T(8,128)}, f32[32,1536]{1,0:T(8,128)S(1)}, u32[]{:S(2)}, u32[]{:S(2)}) collective-permute-start(f32[32,1536]{1,0:T(8,128)} %refs_0_.11), channel_id=1, source_target_pairs={{0,4},{4,8},{8,12},{12,0},{1,5},{5,9},{9,13},{13,1},{2,6},{6,10},{... | collective-permute-start | bytes 589832 | tf_op jit(solution)/shard_map/ppermute | solution.py:314
  3.0 19.3 %collective-permute-start.2 = (f32[32,1536]{1,0:T(8,128)}, f32[32,1536]{1,0:T(8,128)S(1)}, u32[]{:S(2)}, u32[]{:S(2)}) collective-permute-start(f32[32,1536]{1,0:T(8,128)} %refs_0_.11), channel_id=1, source_target_pairs={{0,8},{4,12},{8,0},{12,4},{1,9},{5,13},{9,1},{13,5},{2,10},{6,14},... | collective-permute-start | bytes 589832 | tf_op jit(solution)/shard_map/ppermute | solution.py:314
  5.6 16.7 %collective-permute-start.3 = (f32[32,1536]{1,0:T(8,128)}, f32[32,1536]{1,0:T(8,128)S(1)}, u32[]{:S(2)}, u32[]{:S(2)}) collective-permute-start(f32[32,1536]{1,0:T(8,128)} %refs_0_.11), channel_id=1, source_target_pairs={{0,12},{4,0},{8,4},{12,8},{1,13},{5,1},{9,5},{13,9},{2,14},{6,2},{... | collective-permute-start | bytes 589832 | tf_op jit(solution)/shard_map/ppermute | solution.py:314
  8.1 18.1 %collective-permute-start = (f32[64,128]{1,0:T(8,128)S(1)}, f32[64,128]{1,0:T(8,128)S(1)}, u32[]{:S(2)}, u32[]{:S(2)}) collective-permute-start(f32[64,128]{1,0:T(8,128)S(1)} %shard_map.64.refs_1_.refs_0_), channel_id=1, source_target_pairs={{0,1},{1,0},{2,3},{3,2},{4,5},{5,4},{6,7},{7,6},{8,9},{9,8},{10,11... | collective-permute-start | bytes 98312 | tf_op jit(solution)/shard_map/ppermute | solution.py:317
  17.5 4.8 %copy-start = (f32[32,1536]{1,0:T(8,128)S(1)}, f32[32,1536]{1,0:T(8,128)}, u32[]{:S(2)}) copy-start(f32[32,1536]{1,0:T(8,128)} %refs_0_.11) | copy-start | bytes 589828
  26.2 5.4 %collective-permute-start.4 = (f32[64,128]{1,0:T(8,128)S(1)}, f32[64,128]{1,0:T(8,128)S(1)}, u32[]{:S(2)}, u32[]{:S(2)}) collective-permute-start(f32[64,128]{1,0:T(8,128)S(1)} %shard_map.69.refs_8_.refs_2_), channel_id=1, source_target_pairs={{0,2},{1,3},{2,0},{3,1},{4,6},{5,7},{6,4},{7,5},{8,10},{9,11},{10,... | collective-permute-start | bytes 98312 | tf_op jit(solution)/shard_map/ppermute | solution.py:320
  27.7 4.1 %copy-start.3 = (f32[1536]{0:T(1024)S(1)}, f32[1536]{0:T(1024)}, u32[]{:S(2)}) copy-start(f32[1536]{0:T(1024)} %param.11) | copy-start | bytes 18436
  27.7 4.1 %copy-start.2 = (f32[32,1536]{1,0:T(8,128)S(1)}, f32[32,1536]{1,0:T(8,128)}, u32[]{:S(2)}) copy-start(f32[32,1536]{1,0:T(8,128)} %refs_0_.9) | copy-start | bytes 589828
  31.6 12.5 %collective-permute-start.6 = (f32[64,3072]{1,0:T(8,128)S(1)}, f32[64,3072]{1,0:T(8,128)S(1)}, u32[]{:S(2)}, u32[]{:S(2)}) collective-permute-start(f32[64,3072]{1,0:T(8,128)S(1)} %get-tuple-element.86), channel_id=1, source_target_pairs={{0,1},{1,0},{2,3},{3,2},{4,5},{5,4},{6,7},{7,6},{8,9},{9,8},{10,11... | collective-permute-start | bytes 2359304 | tf_op jit(solution)/shard_map/ppermute | solution.py:317
  32.0 9.6 %collective-permute-start.5 = (f32[32,1536]{1,0:T(8,128)S(1)}, f32[32,1536]{1,0:T(8,128)S(1)}, u32[]{:S(2)}, u32[]{:S(2)}) collective-permute-start(f32[32,1536]{1,0:T(8,128)S(1)} %get-tuple-element.80.refs_0_), channel_id=1, source_target_pairs={{0,4},{4,8},{8,12},{12,0},{1,5},{5,9},{9,13},{13,1},{2,6},{6,10},{... | collective-permute-start | bytes 589832 | tf_op jit(solution)/shard_map/ppermute | solution.py:314
  32.9 11.2 %collective-permute-start.7 = (f32[32,1536]{1,0:T(8,128)S(1)}, f32[32,1536]{1,0:T(8,128)S(1)}, u32[]{:S(2)}, u32[]{:S(2)}) collective-permute-start(f32[32,1536]{1,0:T(8,128)S(1)} %get-tuple-element.80.refs_0_), channel_id=1, source_target_pairs={{0,12},{4,0},{8,4},{12,8},{1,13},{5,1},{9,5},{13,9},{2,14},{6,2},{... | collective-permute-start | bytes 589832 | tf_op jit(solution)/shard_map/ppermute | solution.py:314
  44.3 11.7 %collective-permute-start.8 = (f32[32,3072]{1,0:T(8,128)S(1)}, f32[32,3072]{1,0:T(8,128)S(1)}, u32[]{:S(2)}, u32[]{:S(2)}) collective-permute-start(f32[32,3072]{1,0:T(8,128)S(1)} %get-tuple-element.142), channel_id=1, source_target_pairs={{0,2},{1,3},{2,0},{3,1},{4,6},{5,7},{6,4},{7,5},{8,10},{9,11},{10,... | collective-permute-start | bytes 1179656 | tf_op jit(solution)/shard_map/ppermute | solution.py:320
  44.9 11.0 %collective-permute-start.9 = (f32[32,1536]{1,0:T(8,128)S(1)}, f32[32,1536]{1,0:T(8,128)S(1)}, u32[]{:S(2)}, u32[]{:S(2)}) collective-permute-start(f32[32,1536]{1,0:T(8,128)S(1)} %get-tuple-element.80.refs_0_), channel_id=1, source_target_pairs={{0,8},{4,12},{8,0},{12,4},{1,9},{5,13},{9,1},{13,5},{2,10},{6,14},... | collective-permute-start | bytes 589832 | tf_op jit(solution)/shard_map/ppermute | solution.py:314
  56.0 5.6 %collective-permute-start.10 = (f32[64,3072]{1,0:T(8,128)S(1)}, f32[64,3072]{1,0:T(8,128)S(1)}, u32[]{:S(2)}, u32[]{:S(2)}) collective-permute-start(f32[64,3072]{1,0:T(8,128)S(1)} %get-tuple-element.96), channel_id=1, source_target_pairs={{0,1},{1,0},{2,3},{3,2},{4,5},{5,4},{6,7},{7,6},{8,9},{9,8},{10,11... | collective-permute-start | bytes 2359304 | tf_op jit(solution)/shard_map/ppermute | solution.py:317
  67.2 7.7 %collective-permute-start.11 = (f32[64,3072]{1,0:T(8,128)S(1)}, f32[64,3072]{1,0:T(8,128)S(1)}, u32[]{:S(2)}, u32[]{:S(2)}) collective-permute-start(f32[64,3072]{1,0:T(8,128)S(1)} %get-tuple-element.101), channel_id=1, source_target_pairs={{0,1},{1,0},{2,3},{3,2},{4,5},{5,4},{6,7},{7,6},{8,9},{9,8},{10,11... | collective-permute-start | bytes 2359304 | tf_op jit(solution)/shard_map/ppermute | solution.py:317
  67.8 13.4 %collective-permute-start.12 = (f32[32,3072]{1,0:T(8,128)S(1)}, f32[32,3072]{1,0:T(8,128)S(1)}, u32[]{:S(2)}, u32[]{:S(2)}) collective-permute-start(f32[32,3072]{1,0:T(8,128)S(1)} %get-tuple-element.140), channel_id=1, source_target_pairs={{0,2},{1,3},{2,0},{3,1},{4,6},{5,7},{6,4},{7,5},{8,10},{9,11},{10,... | collective-permute-start | bytes 1179656 | tf_op jit(solution)/shard_map/ppermute | solution.py:320
  75.1 6.3 %copy-start.4 = (f32[6144]{0:T(1024)S(1)}, f32[6144]{0:T(1024)}, u32[]{:S(2)}) copy-start(f32[6144]{0:T(1024)} %param.9) | copy-start | bytes 73732
  75.1 12.3 %collective-permute-start.16 = (f32[32,3072]{1,0:T(8,128)S(1)}, f32[32,3072]{1,0:T(8,128)S(1)}, u32[]{:S(2)}, u32[]{:S(2)}) collective-permute-start(f32[32,3072]{1,0:T(8,128)S(1)} %slice.52), channel_id=1, source_target_pairs={{0,2},{1,3},{2,0},{3,1},{4,6},{5,7},{6,4},{7,5},{8,10},{9,11},{10,... | collective-permute-start | bytes 1179656 | tf_op jit(solution)/shard_map/ppermute | solution.py:320
  81.3 7.8 %collective-permute-start.13 = (f32[64,3072]{1,0:T(8,128)S(1)}, f32[64,3072]{1,0:T(8,128)S(1)}, u32[]{:S(2)}, u32[]{:S(2)}) collective-permute-start(f32[64,3072]{1,0:T(8,128)S(1)} %get-tuple-element.108), channel_id=1, source_target_pairs={{0,1},{1,0},{2,3},{3,2},{4,5},{5,4},{6,7},{7,6},{8,9},{9,8},{10,11... | collective-permute-start | bytes 2359304 | tf_op jit(solution)/shard_map/ppermute | solution.py:317
  87.6 12.1 %collective-permute-start.17 = (f32[32,3072]{1,0:T(8,128)S(1)}, f32[32,3072]{1,0:T(8,128)S(1)}, u32[]{:S(2)}, u32[]{:S(2)}) collective-permute-start(f32[32,3072]{1,0:T(8,128)S(1)} %fusion.9.refs_0_), channel_id=1, source_target_pairs={{0,2},{1,3},{2,0},{3,1},{4,6},{5,7},{6,4},{7,5},{8,10},{9,11},{10,... | collective-permute-start | bytes 1179656 | tf_op jit(solution)/shard_map/ppermute | solution.py:320
  89.3 17.0 %collective-permute-start.14 = (f32[32,3072]{1,0:T(8,128)S(1)}, f32[32,3072]{1,0:T(8,128)S(1)}, u32[]{:S(2)}, u32[]{:S(2)}) collective-permute-start(f32[32,3072]{1,0:T(8,128)S(1)} %slice.50), channel_id=1, source_target_pairs={{0,2},{1,3},{2,0},{3,1},{4,6},{5,7},{6,4},{7,5},{8,10},{9,11},{10,... | collective-permute-start | bytes 1179656 | tf_op jit(solution)/shard_map/ppermute | solution.py:320
  89.9 18.1 %collective-permute-start.18 = (f32[32,3072]{1,0:T(8,128)S(1)}, f32[32,3072]{1,0:T(8,128)S(1)}, u32[]{:S(2)}, u32[]{:S(2)}) collective-permute-start(f32[32,3072]{1,0:T(8,128)S(1)} %fusion.9.refs_0_), channel_id=1, source_target_pairs={{0,1},{1,0},{2,3},{3,2},{4,5},{5,4},{6,7},{7,6},{8,9},{9,8},{10,11... | collective-permute-start | bytes 1179656 | tf_op jit(solution)/shard_map/ppermute | solution.py:317
  99.7 8.3 %collective-permute-start.19 = (f32[32,3072]{1,0:T(8,128)S(1)}, f32[32,3072]{1,0:T(8,128)S(1)}, u32[]{:S(2)}, u32[]{:S(2)}) collective-permute-start(f32[32,3072]{1,0:T(8,128)S(1)} %collective-permute-done.17.refs_1_), channel_id=1, source_target_pairs={{0,1},{1,0},{2,3},{3,2},{4,5},{5,4},{6,7},{7,6},{8,9},{9,8},{10,11... | collective-permute-start | bytes 1179656 | tf_op jit(solution)/shard_map/ppermute | solution.py:317
  106.5 9.3 %collective-permute-start.15 = (f32[32,3072]{1,0:T(8,128)S(1)}, f32[32,3072]{1,0:T(8,128)S(1)}, u32[]{:S(2)}, u32[]{:S(2)}) collective-permute-start(f32[32,3072]{1,0:T(8,128)S(1)} %fusion.4.refs_0_), channel_id=1, source_target_pairs={{0,2},{1,3},{2,0},{3,1},{4,6},{5,7},{6,4},{7,5},{8,10},{9,11},{10,... | collective-permute-start | bytes 1179656 | tf_op jit(solution)/shard_map/ppermute | solution.py:320
  108.0 7.9 %collective-permute-start.20 = (f32[32,3072]{1,0:T(8,128)S(1)}, f32[32,3072]{1,0:T(8,128)S(1)}, u32[]{:S(2)}, u32[]{:S(2)}) collective-permute-start(f32[32,3072]{1,0:T(8,128)S(1)} %fusion.4.refs_0_), channel_id=1, source_target_pairs={{0,1},{1,0},{2,3},{3,2},{4,5},{5,4},{6,7},{7,6},{8,9},{9,8},{10,11... | collective-permute-start | bytes 1179656 | tf_op jit(solution)/shard_map/ppermute | solution.py:317
  115.8 1.7 %collective-permute-start.21 = (f32[32,3072]{1,0:T(8,128)S(1)}, f32[32,3072]{1,0:T(8,128)S(1)}, u32[]{:S(2)}, u32[]{:S(2)}) collective-permute-start(f32[32,3072]{1,0:T(8,128)S(1)} %collective-permute-done.15.refs_1_), channel_id=1, source_target_pairs={{0,1},{1,0},{2,3},{3,2},{4,5},{5,4},{6,7},{7,6},{8,9},{9,8},{10,11... | collective-permute-start | bytes 1179656 | tf_op jit(solution)/shard_map/ppermute | solution.py:317
  121.6 10.2 %collective-permute-start.24 = (f32[32,768]{1,0:T(8,128)S(1)}, f32[32,768]{1,0:T(8,128)S(1)}, u32[]{:S(2)}, u32[]{:S(2)}) collective-permute-start(f32[32,768]{1,0:T(8,128)S(1)} %get-tuple-element.131), channel_id=1, source_target_pairs={{0,4},{4,8},{8,12},{12,0},{1,5},{5,9},{9,13},{13,1},{2,6},{6,10},{... | collective-permute-start | bytes 294920 | tf_op jit(solution)/shard_map/ppermute | solution.py:314
  121.7 13.0 %collective-permute-start.23 = (f32[32,768]{1,0:T(8,128)S(1)}, f32[32,768]{1,0:T(8,128)S(1)}, u32[]{:S(2)}, u32[]{:S(2)}) collective-permute-start(f32[32,768]{1,0:T(8,128)S(1)} %get-tuple-element.130), channel_id=1, source_target_pairs={{0,8},{4,12},{8,0},{12,4},{1,9},{5,13},{9,1},{13,5},{2,10},{6,14},... | collective-permute-start | bytes 294920 | tf_op jit(solution)/shard_map/ppermute | solution.py:314
  124.6 10.0 %collective-permute-start.22 = (f32[32,768]{1,0:T(8,128)S(1)}, f32[32,768]{1,0:T(8,128)S(1)}, u32[]{:S(2)}, u32[]{:S(2)}) collective-permute-start(f32[32,768]{1,0:T(8,128)S(1)} %get-tuple-element.129), channel_id=1, source_target_pairs={{0,12},{4,0},{8,4},{12,8},{1,13},{5,1},{9,5},{13,9},{2,14},{6,2},{... | collective-permute-start | bytes 294920 | tf_op jit(solution)/shard_map/ppermute | solution.py:314
  129.7 7.6 %collective-permute-start.27 = (f32[32,768]{1,0:T(8,128)S(1)}, f32[32,768]{1,0:T(8,128)S(1)}, u32[]{:S(2)}, u32[]{:S(2)}) collective-permute-start(f32[32,768]{1,0:T(8,128)S(1)} %get-tuple-element.135), channel_id=1, source_target_pairs={{0,4},{4,8},{8,12},{12,0},{1,5},{5,9},{9,13},{13,1},{2,6},{6,10},{... | collective-permute-start | bytes 294920 | tf_op jit(solution)/shard_map/ppermute | solution.py:314
  130.9 9.6 %collective-permute-start.26 = (f32[32,768]{1,0:T(8,128)S(1)}, f32[32,768]{1,0:T(8,128)S(1)}, u32[]{:S(2)}, u32[]{:S(2)}) collective-permute-start(f32[32,768]{1,0:T(8,128)S(1)} %get-tuple-element.134), channel_id=1, source_target_pairs={{0,8},{4,12},{8,0},{12,4},{1,9},{5,13},{9,1},{13,5},{2,10},{6,14},... | collective-permute-start | bytes 294920 | tf_op jit(solution)/shard_map/ppermute | solution.py:314
  131.8 8.6 %collective-permute-start.25 = (f32[32,768]{1,0:T(8,128)S(1)}, f32[32,768]{1,0:T(8,128)S(1)}, u32[]{:S(2)}, u32[]{:S(2)}) collective-permute-start(f32[32,768]{1,0:T(8,128)S(1)} %get-tuple-element.133), channel_id=1, source_target_pairs={{0,12},{4,0},{8,4},{12,8},{1,13},{5,1},{9,5},{13,9},{2,14},{6,2},{... | collective-permute-start | bytes 294920 | tf_op jit(solution)/shard_map/ppermute | solution.py:314
  (1 other events, 0.9 us)

commit v7 on v6

--- a/solution.py
+++ b/solution.py
@@ -122,129 +122,126 @@
     )(pltpu.with_memory_space_constraint(weight, pltpu.HBM), *after)
 
 
-def three_pass(both, high, low, contract, streamed):
+def three_pass(both, high, low, contract):
     rows = both.shape[0] // 2
-    dims = ((contract,), (1,)) if streamed else ((1,), (contract,))
-
-    def dot(left, weight):
-        pair = (weight, left) if streamed else (left, weight)
-        return lax.dot_general(*pair, (dims, ((), ())), preferred_element_type=jnp.float32)
-
-    first, second = dot(both[...], high), dot(both[:rows, :], low)
-    if streamed:
-        return (first[:, :rows] + first[:, rows:] + second).T
-    return first[:rows] + first[rows:] + second
-
-
-def forward_kernel(slots, contract, streamed, span, earlier, place_ref, *refs):
-    slot_refs, (high_ref, low_ref) = refs[:slots], refs[slots : slots + 2]
-    send_ref, keep_ref, both = refs[-3:]
-    for part_ref, whole_ref in zip(refs[slots + 2 : slots + 2 + earlier], (send_ref, keep_ref)):
-        whole_ref[:, : span[0]] = part_ref[...]
-    block = slot_refs[0].shape[0]
-    total = block * slots
-    for b in range(slots):
-        high, low = split(slot_refs[b][...])
-        row = pl.multiple_of(place_ref[b] * block, block)
-        both[pl.ds(row, block), :] = high
-        both[pl.ds(total + row, block), :] = low
-
-    width = divisor(span[1], *((512,) if streamed else ()), 256, 128)
-
-    @pl.loop(0, span[1] // width, unroll=1 if streamed else 2)
-    def _(step):
-        at = pl.ds(pl.multiple_of(span[0] + step * width, width), width)
-        tile = pl.ds(pl.multiple_of(step * width, width), width)
-        tile = (slice(None), tile) if contract == 0 else (tile, slice(None))
-        part = three_pass(both, high_ref[tile], low_ref[tile], contract, streamed)
-        keep_ref[:, at] = part[: total // 2]
-        send_ref[:, at] = part[total // 2 :]
-
-
-def forward(blocks, weight, place, by_column, streamed, span, earlier, after):
-    slots, (block, depth) = len(blocks), blocks[0].shape
-    half = block * slots // 2
-    out = jax.ShapeDtypeStruct((half, sum(span)), jnp.float32)
-    inside = pl.BlockSpec(memory_space=pltpu.VMEM)
+    dot = functools.partial(
+        lax.dot_general,
+        dimension_numbers=(((1,), (contract,)), ((), ())),
+        preferred_element_type=jnp.float32,
+    )
+    first = dot(both[...], high)
+    return first[:rows] + first[rows:] + dot(both[:rows, :], low)
+
+
+def fill(both, block_refs, place_ref):
+    total = both.shape[0] // 2
+    block = total // place_ref.shape[0]
+    index = 0
+    for ref in block_refs:
+        for start in range(0, ref.shape[0], block):
+            high, low = split(ref[start : start + block, :])
+            row = pl.multiple_of(place_ref[index] * block, block)
+            both[pl.ds(row, block), :] = high
+            both[pl.ds(total + row, block), :] = low
+            index += 1
+
+
+def follow(earlier_refs, out_refs):
+    for earlier_ref, out_ref in zip(earlier_refs, out_refs):
+        out_ref[:, : earlier_ref.shape[1]] = earlier_ref[...]
+    return earlier_refs[0].shape[1] if earlier_refs else 0
+
+
+def forward_kernel(place_ref, slot_refs, weight_refs, earlier_refs, send_ref, keep_ref, both):
+    fill(both, slot_refs, place_ref)
+    half, column = send_ref.shape[0], follow(earlier_refs, (send_ref, keep_ref))
+    for high_ref, low_ref in zip(weight_refs[::2], weight_refs[1::2]):
+        width = divisor(high_ref.shape[1], 256, 128)
+
+        @pl.loop(0, high_ref.shape[1] // width, unroll=2)
+        def _(step):
+            at = pl.ds(pl.multiple_of(step * width, width), width)
+            part = three_pass(both, high_ref[:, at], low_ref[:, at], 0)
+            at = pl.ds(pl.multiple_of(column + step * width, width), width)
+            keep_ref[:, at] = part[:half]
+            send_ref[:, at] = part[half:]
+
+        column += high_ref.shape[1]
+
+
+def forward(slots, weights, place, earlier, after):
+    tokens, depth = slots[0].shape[0] * len(slots), slots[0].shape[1]
+    hidden = sum(w.shape[1] for w in weights[::2]) + (earlier[0].shape[1] if earlier else 0)
+    out = jax.ShapeDtypeStruct((tokens // 2, hidden), jnp.float32)
+    inside, anywhere = pl.BlockSpec(memory_space=pltpu.VMEM), pl.BlockSpec(memory_space=pl.ANY)
+    ends = [1 + len(slots), 1 + len(slots) + len(weights), 1 + len(slots) + len(weights) + len(earlier)]
     return pl.pallas_call(
-        functools.partial(forward_kernel, slots, 0 if by_column else 1, streamed, span, len(earlier)),
+        lambda *refs: forward_kernel(
+            refs[0], refs[1 : ends[0]], refs[ends[0] : ends[1]], refs[ends[1] : ends[2]], *refs[-3:]
+        ),
         out_shape=(out, out),
-        in_specs=[pl.BlockSpec(memory_space=pltpu.SMEM)]
-        + [inside] * (slots + 2 + len(earlier))
-        + [pl.BlockSpec(memory_space=pl.ANY)] * len(after),
+        in_specs=[pl.BlockSpec(memory_space=pltpu.SMEM)] + [inside] * (ends[2] - 1) + [anywhere] * len(after),
         out_specs=[inside] * 2,
-        scratch_shapes=[pltpu.VMEM((2 * block * slots, depth), jnp.bfloat16)],
+        scratch_shapes=[pltpu.VMEM((2 * tokens, depth), jnp.bfloat16)],
         compiler_params=pltpu.CompilerParams(vmem_limit_bytes=VMEM_LIMIT),
         cost_estimate=SHORT,
-    )(place, *blocks, *[pltpu.with_memory_space_constraint(part, pltpu.VMEM) for part in weight], *earlier, *after)
-
-
-def stream_kernel(slots, first_column, span, earlier, depth, place_ref, *refs):
-    slot_refs, weight_ref = refs[:slots], refs[slots]
-    send_ref, keep_ref, high_ref, low_ref, both, landed, arrived = refs[-7:]
-    for part_ref, whole_ref in zip(refs[slots + 1 : slots + 1 + earlier], (send_ref, keep_ref)):
-        whole_ref[:, : span[0]] = part_ref[...]
-    block = slot_refs[0].shape[0]
-    total = block * slots
-    width = landed.shape[2]
-    steps = span[1] // width
+    )(place, *slots, *[pltpu.with_memory_space_constraint(w, pltpu.VMEM) for w in weights], *earlier, *after)
+
+
+def stream_kernel(first, depth, place_ref, slot_refs, weight_ref, earlier_refs, send_ref, keep_ref, both, landed, arrived):
+    half = send_ref.shape[0]
+    width = landed.shape[1]
+    column = follow(earlier_refs, (send_ref, keep_ref))
+    steps = (send_ref.shape[1] - column) // width
 
     def fetch(step):
-        start = pl.multiple_of(first_column + step * width, width)
+        start = pl.multiple_of(first + step * width, width)
         slot = lax.rem(step, depth)
-        return pltpu.make_async_copy(weight_ref.at[:, pl.ds(start, width)], landed.at[slot], arrived.at[slot])
+        return pltpu.make_async_copy(weight_ref.at[pl.ds(start, width), :], landed.at[slot], arrived.at[slot])
 
     for step in range(min(depth, steps)):
         fetch(step).start()
-    for b in range(slots):
-        high, low = split(slot_refs[b][...])
-        row = pl.multiple_of(place_ref[b] * block, block)
-        both[pl.ds(row, block), :] = high
-        both[pl.ds(total + row, block), :] = low
+    fill(both, slot_refs, place_ref)
 
     @pl.loop(0, steps)
     def _(step):
         fetch(step).wait()
         high, low = split(landed[lax.rem(step, depth)])
-        at = pl.ds(pl.multiple_of(step * width, width), width)
-        high_ref[:, at] = high
-        low_ref[:, at] = low
-        part = three_pass(both, high, low, 0, False)
-        at = pl.ds(pl.multiple_of(span[0] + step * width, width), width)
-        keep_ref[:, at] = part[: total // 2]
-        send_ref[:, at] = part[total // 2 :]
+        part = three_pass(both, high, low, 1)
+        at = pl.ds(pl.multiple_of(column + step * width, width), width)
+        keep_ref[:, at] = part[:half]
+        send_ref[:, at] = part[half:]
 
         @pl.when(step + depth < steps)
         def _():
             fetch(step + depth).start()
 
 
-def stream(blocks, weight, place, first_column, span, earlier, after):
-    slots, (block, rows) = len(blocks), blocks[0].shape
-    half, hidden = block * slots // 2, sum(span)
-    width = divisor(span[1], 256, 128)
-    depth = 3
-    out = jax.ShapeDtypeStruct((half, hidden), jnp.float32)
-    kept = pltpu.VMEM((rows, span[1]), jnp.bfloat16)
-    inside = pl.BlockSpec(memory_space=pltpu.VMEM)
-    result = pl.pallas_call(
-        functools.partial(stream_kernel, slots, first_column, span, len(earlier), depth),
-        out_shape=(out, out, kept, kept),
+def stream(slots, weight, place, first, hidden, earlier, after):
+    tokens, columns = slots[0].shape[0] * len(slots), slots[0].shape[1]
+    width, depth = divisor(hidden, 256, 128), 2
+    out = jax.ShapeDtypeStruct((tokens // 2, hidden + (earlier[0].shape[1] if earlier else 0)), jnp.float32)
+    inside, anywhere = pl.BlockSpec(memory_space=pltpu.VMEM), pl.BlockSpec(memory_space=pl.ANY)
+    last = 1 + len(slots)
+    return pl.pallas_call(
+        lambda *refs: stream_kernel(
+            first, depth, refs[0], refs[1:last], refs[last], refs[last + 1 : last + 1 + len(earlier)], *refs[-5:]
+        ),
+        out_shape=(out, out),
         in_specs=[pl.BlockSpec(memory_space=pltpu.SMEM)]
-        + [inside] * slots
-        + [pl.BlockSpec(memory_space=pl.ANY)]
+        + [inside] * len(slots)
+        + [anywhere]
         + [inside] * len(earlier)
-        + [pl.BlockSpec(memory_space=pl.ANY)] * len(after),
-        out_specs=[inside] * 4,
+        + [anywhere] * len(after),
+        out_specs=[inside] * 2,
         scratch_shapes=[
-            pltpu.VMEM((2 * block * slots, rows), jnp.bfloat16),
-            pltpu.VMEM((depth, rows, width), jnp.float32),
+            pltpu.VMEM((2 * tokens, columns), jnp.bfloat16),
+            pltpu.VMEM((depth, width, columns), jnp.float32),
             pltpu.SemaphoreType.DMA((depth,)),
         ],
-        compiler_params=pltpu.CompilerParams(vmem_limit_bytes=2 * VMEM_LIMIT),
+        compiler_params=pltpu.CompilerParams(vmem_limit_bytes=VMEM_LIMIT),
         cost_estimate=SHORT,
-    )(place, *blocks, pltpu.with_memory_space_constraint(weight, pltpu.HBM), *earlier, *after)
-    return result[:2], result[2:]
+    )(place, *slots, pltpu.with_memory_space_constraint(weight, pltpu.HBM), *earlier, *after)
 
 
 def backward_kernel(slots, pieces, earlier, first_column, place_ref, *refs):
@@ -269,7 +266,7 @@
         total_sum, column = 0.0, 0
         for high_ref, low_ref in zip(weight_refs[::2], weight_refs[1::2]):
             columns = slice(column, column + high_ref.shape[1])
-            total_sum += three_pass(both[:, columns], high_ref[tile], low_ref[tile], 1, False)
+            total_sum += three_pass(both[:, columns], high_ref[tile], low_ref[tile], 1)
             column = columns.stop
         result[...] = total_sum
         for b in range(slots):
@@ -327,6 +324,7 @@
 
     grads = gathered(out_grad)
     piece = hidden // CHUNKS
+    quarter = piece // 2
 
     def tied(values, others):
         return lax.optimization_barrier((values, others))
@@ -343,19 +341,16 @@
         return arrival, terms[0]
 
     def prepared(c, after):
-        return prepare(out_weight, (c * quarter, quarter), (0, depth), after)
-
-    def back(c, earlier, after):
-        return forward(grads, out_parts[c], place, False, False, (c % 2 * quarter, quarter), earlier, after)
-
-    quarter = piece // 2
+        return prepare(in_weight, (0, depth), (c * quarter, quarter), after)
+
     moments = call(moments_kernel, jax.ShapeDtypeStruct((2 * tokens, 128), jnp.float32), (inputs,), ())
-    out_parts = [prepared(0, [place, moments])]
-    out_parts.append(prepared(1, [out_parts[0][0]]))
-    out_parts.append(prepared(2, [out_parts[1][0]]))
-    back_0 = back(0, (), [out_parts[2][0]])
-    moments = call(functools.partial(merge_kernel, depth), moments, (moments, other_core(moments)), (back_0[0],))
-    back_0 = back(1, back_0, [moments])
+    in_parts = prepared(0, [place, moments])
+    in_parts += prepared(1, [in_parts[0]])
+    in_parts += prepared(2, [in_parts[2]])
+    moments = call(
+        functools.partial(merge_kernel, depth), moments, (moments, other_core(moments)), (in_parts[4], *grads[1:])
+    )
+    back_0 = stream(grads, out_weight, place, 0, piece, (), [moments])
     parts = [moments]
     for _ in range(1, chips):
         parts.append(next_chip(parts[-1]))
@@ -368,24 +363,18 @@
     inv_std = inv_std[:, :1]
     scaled = gathered(scaled)
     back_0, _ = tied(back_0, parts)
-    out_parts.append(prepared(3, [scaled[0]]))
-    half_0 = halved(back_0, (out_parts[3], scaled[1], scaled[-1]))
-    back_1 = back(2, (), [out_parts[3][0], half_0])
-    back_1 = back(3, back_1, [scaled[1], scaled[-1]])
+    half_0 = halved(back_0, scaled[0])
+    in_parts += prepared(3, [scaled[0], half_0])
+    back_1 = stream(grads, out_weight, place, piece, piece, (), [in_parts[6]])
     back_0 = exchanged(half_0)
-    back_1, (back_0, scaled[2:-1]) = tied(back_1, (back_0, scaled[2:-1]))
-
-    def pre(c, earlier, after):
-        span = (c % 2 * quarter, quarter)
-        return stream(scaled, in_weight, place, c * quarter, span, earlier, after)
-
-    pre_0, in_parts_0 = pre(0, (), [back_1[1]])
+    back_1, (back_0, scaled) = tied(back_1, (back_0, scaled))
+    pre_0 = forward(scaled, in_parts[:2], place, (), [back_1[1]])
     half_1 = halved(back_1, pre_0)
     back_1 = exchanged(half_1)
-    pre_0, in_parts_1 = pre(1, pre_0, [half_1])
-    pre_1, in_parts_2 = pre(2, (), [pre_0[1]])
+    pre_0 = forward(scaled, in_parts[2:4], place, pre_0, [half_1])
+    pre_1 = forward(scaled, in_parts[4:6], place, (), [pre_0[1]])
     half_0 = halved(pre_0, pre_1)
-    pre_1, in_parts_3 = pre(3, pre_1, [half_0])
+    pre_1 = forward(scaled, in_parts[6:], place, pre_1, [half_0])
     pre_1, back_1 = tied(pre_1, back_1)
     backs = [back_0, back_1]
     pres = [exchanged(half_0), exchanged(halved(pre_1))]
@@ -406,13 +395,13 @@
         return sum([along_hid(sums[step], -step) for step in range(1, hid_size)], start=sums[0])
 
     acts_0, acts_1 = spread_out(0), spread_out(1)
-    sums = backward(both_cores(acts_0), in_parts_0 + in_parts_1, place, (), 0, 1, [pre_1[1]])
+    sums = backward(both_cores(acts_0), in_parts[:4], place, (), 0, 1, [pre_1[1]])
     acts_1[1:], sums = tied(acts_1[1:], sums)
-    acts_1, in_parts_1 = both_cores(acts_1), in_parts_2 + in_parts_3
+    acts_1 = both_cores(acts_1)
     parts = 2 if depth % 512 == 0 else 1
     ends = []
     for part in range(parts):
-        ends.append(backward(acts_1, in_parts_1, place, sums, part, parts, [ends[-1][0] if ends else sums[0]]))
+        ends.append(backward(acts_1, in_parts[4:], place, sums, part, parts, [ends[-1][0] if ends else sums[0]]))
     running = jnp.concatenate([summed_along_hid(end) for end in ends], axis=1)
     normed_grad = running * norm_gain
     totals = lax.psum(

time: 148 us -> 149 us (level)
  waiting for transfers between devices: 35.6 us -> 38.4 us
  starting transfers between devices: 30.3 us -> 28.6 us
    ppermute x7, waiting for transfers between devices: 22.9 us -> 28.4 us  [next_chip(): lax.ppermute(values, 'emb', [(i, (i + 2) % emb_size) for i in range(emb_s...]
    ppermute x12, waiting for transfers between devices: 11.1 us -> 6.38 us  [along_hid(): lax.ppermute(values, 'hid', [(i, (i + steps) % hid_size) for i in range(h...]
    ppermute x9, waiting for transfers between devices: 1.69 us -> 3.68 us  [other_core(): return lax.ppermute(values, 'emb', [(i, i ^ 1) for i in range(emb_size)])]
    ppermute x12, starting transfers between devices: 21.3 us -> 19.7 us  [along_hid(): lax.ppermute(values, 'hid', [(i, (i + steps) % hid_size) for i in range(h...]
    pallas_call x8 -> x6, Pallas kernels: 37.5 us -> 37.9 us  [the longest x2 25.8 us: stream(): pl.pallas_call(lambda *refs: stream_kernel(first, depth, refs[0], refs[1:...]
  transfers between devices with their start and end apart: 28 -> 28, of which waited for: 10 -> 9; matrix products, arithmetic and copies ran while one was open for 1% -> 1% of each run, Pallas kernels for 42% -> 44%
where the time goes in v7:
time: 149 us; the launch traced here: 148 us
  Pallas kernels  72.3 us (49%)
  waiting for transfers between devices  38.4 us (26%)
  starting transfers between devices  28.6 us (19%)
  blocking collectives  5.73 us (4%)
  other arithmetic  1.78 us (1%)
    ppermute x7, waiting for transfers between devices, next_chip(): lax.ppermute(values, 'emb', [(i, (i + 2) % emb_size) for i in range(emb_s...  28.4 us
    pallas_call x2, Pallas kernels, stream(): pl.pallas_call(lambda *refs: stream_kernel(first, depth, refs[0], refs[1:...  25.8 us
    ppermute x12, starting transfers between devices, along_hid(): lax.ppermute(values, 'hid', [(i, (i + steps) % hid_size) for i in range(h...  19.7 us
    pallas_call x4, Pallas kernels, prepare(): pl.pallas_call(functools.partial(prepare_kernel, rows, columns, block, de...  18.8 us
    pallas_call x3, Pallas kernels, backward(): pl.pallas_call(functools.partial(backward_kernel, slots, len(weights) //...  15.4 us
    pallas_call x4, Pallas kernels, forward(): pl.pallas_call(lambda *refs: forward_kernel(refs[0], refs[1:ends[0]], ref...  12.1 us
    ppermute x7, starting transfers between devices, next_chip(): lax.ppermute(values, 'emb', [(i, (i + 2) % emb_size) for i in range(emb_s...  8.02 us
    ppermute x12, waiting for transfers between devices, along_hid(): lax.ppermute(values, 'hid', [(i, (i + steps) % hid_size) for i in range(h...  6.38 us
  transfers between devices with their start and end apart: 28, of which 9 were waited for; matrix products, arithmetic and copies ran while one was open for 1% of the time, Pallas kernels for 44%

profile of v7, /device:TPU:0, one launch (start us, length us, event | category | flops | bytes accessed | tf_op | source)
XLA Modules:
  0.0 148.5 jit_solution(12861482861939045646)
XLA Ops:
  0.0 3.0 %collective-permute-start.1 = (f32[32,1536]{1,0:T(8,128)}, f32[32,1536]{1,0:T(8,128)S(1)}, u32[]{:S(2)}, u32[]{:S(2)}) collective-permute-start(f32[32,1536]{1,0:T(8,128)} %refs_1_.3), channel_id=1, source_target_pairs={{0,4},{4,8},{8,12},{12,0},{1,5},{5,9},{9,13},{13,1},{2,6},{6,10},{... | collective-permute-start | bytes 589832 | tf_op jit(solution)/shard_map/ppermute | solution.py:311
  3.0 2.6 %collective-permute-start.2 = (f32[32,1536]{1,0:T(8,128)}, f32[32,1536]{1,0:T(8,128)S(1)}, u32[]{:S(2)}, u32[]{:S(2)}) collective-permute-start(f32[32,1536]{1,0:T(8,128)} %refs_1_.3), channel_id=1, source_target_pairs={{0,8},{4,12},{8,0},{12,4},{1,9},{5,13},{9,1},{13,5},{2,10},{6,14},... | collective-permute-start | bytes 589832 | tf_op jit(solution)/shard_map/ppermute | solution.py:311
  5.6 1.3 collective-permute-start.3
  8.1 4.7 %shard_map.65 = (bf16[1536,1536]{1,0:T(8,128)(2,1)S(1)}, bf16[1536,1536]{1,0:T(8,128)(2,1)S(1)}) custom-call(f32[1536,6144]{1,0:T(8,128)} %weight_ref.7, s32[4]{0:T(128)S(1)} %fusion.13.refs_0_.place_ref, f32[64,128]{1,0:T(8,128)S(1)} %shard_map.64.refs_1_.refs_0_), custom_call_target="tpu_custom_call" | custom-call | flops 1048576 | bytes 262144 | tf_op jit(solution)/shard_map/pallas_call | solution.py:111
  12.8 4.7 %shard_map.66 = (bf16[1536,1536]{1,0:T(8,128)(2,1)S(1)}, bf16[1536,1536]{1,0:T(8,128)(2,1)S(1)}) custom-call(f32[1536,6144]{1,0:T(8,128)} %weight_ref.7, bf16[1536,1536]{1,0:T(8,128)(2,1)S(1)} %get-tuple-element.62.refs_0_.refs_5_.refs_4_), custom_call_target="tpu_custom_call" | custom-call | flops 1048576 | bytes 262144 | tf_op jit(solution)/shard_map/pallas_call | solution.py:111
  17.5 4.7 %shard_map.67 = (bf16[1536,1536]{1,0:T(8,128)(2,1)S(1)}, bf16[1536,1536]{1,0:T(8,128)(2,1)S(1)}) custom-call(f32[1536,6144]{1,0:T(8,128)} %weight_ref.7, bf16[1536,1536]{1,0:T(8,128)(2,1)S(1)} %get-tuple-element.63.refs_0_.refs_5_.refs_6_), custom_call_target="tpu_custom_call" | custom-call | flops 1048576 | bytes 262144 | tf_op jit(solution)/shard_map/pallas_call | solution.py:111
  22.3 1.6 %collective-permute-start.4 = (f32[64,128]{1,0:T(8,128)S(1)}, f32[64,128]{1,0:T(8,128)S(1)}, u32[]{:S(2)}, u32[]{:S(2)}) collective-permute-start(f32[64,128]{1,0:T(8,128)S(1)} %shard_map.68.refs_6_.refs_2_), channel_id=1, source_target_pairs={{0,2},{1,3},{2,0},{3,1},{4,6},{5,7},{6,4},{7,5},{8,10},{9,11},{10,... | collective-permute-start | bytes 98312 | tf_op jit(solution)/shard_map/ppermute | solution.py:317
  23.9 12.9 %shard_map.69 = (f32[64,3072]{1,0:T(8,128)S(1)}, f32[64,3072]{1,0:T(8,128)S(1)}) custom-call(s32[4]{0:T(128)S(1)} %fusion.13.refs_0_.place_ref, f32[32,1536]{1,0:T(8,128)S(1)} %copy-done, f32[32,1536]{1,0:T(8,128)S(1)} %collective-permute-done.1.refs_3_.refs_2_, f32[32,1536]{1,0:T(8,128)S(1)} %collective-permute-done.2.refs_4_.refs_3_, ...), custom_call_target="tpu_custom_call" | custom-call | flops 1048576 | bytes 262144 | tf_op jit(solution)/shard_map/pallas_call | solution.py:226
  37.2 1.9 %collective-permute-done.5 = f32[64,3072]{1,0:T(8,128)S(1)} collective-permute-done((f32[64,3072]{1,0:T(8,128)S(1)}, f32[64,3072]{1,0:T(8,128)S(1)}, u32[]{:S(2)}, u32[]{:S(2)}) %collective-permute-start.5) | collective-permute-done | bytes 786464 | tf_op jit(solution)/shard_map/ppermute | solution.py:314
  41.0 1.6 %collective-permute-start.8 = (f32[32,1536]{1,0:T(8,128)S(1)}, f32[32,1536]{1,0:T(8,128)S(1)}, u32[]{:S(2)}, u32[]{:S(2)}) collective-permute-start(f32[32,1536]{1,0:T(8,128)S(1)} %get-tuple-element.75.refs_0_.refs_1_), channel_id=1, source_target_pairs={{0,8},{4,12},{8,0},{12,4},{1,9},{5,13},{9,1},{13,5},{2,10},{6,14},... | collective-permute-start | bytes 589832 | tf_op jit(solution)/shard_map/ppermute | solution.py:311
  42.6 1.5 collective-permute-start.9
  44.1 4.7 %shard_map.71 = (bf16[1536,1536]{1,0:T(8,128)(2,1)S(1)}, bf16[1536,1536]{1,0:T(8,128)(2,1)S(1)}) custom-call(f32[1536,6144]{1,0:T(8,128)} %weight_ref.7, f32[32,1536]{1,0:T(8,128)S(1)} %get-tuple-element.75.refs_0_.refs_1_, f32[64,3072]{1,0:T(8,128)S(1)} %add.95.refs_1_), custom_call_target="tpu_custom_call" | custom-call | flops 1048576 | bytes 262144 | tf_op jit(solution)/shard_map/pallas_call | solution.py:111
  48.8 12.9 %shard_map.72 = (f32[64,3072]{1,0:T(8,128)S(1)}, f32[64,3072]{1,0:T(8,128)S(1)}) custom-call(s32[4]{0:T(128)S(1)} %fusion.13.refs_0_.place_ref, f32[32,1536]{1,0:T(8,128)S(1)} %copy-done, f32[32,1536]{1,0:T(8,128)S(1)} %collective-permute-done.1.refs_3_.refs_2_, f32[32,1536]{1,0:T(8,128)S(1)} %collective-permute-done.2.refs_4_.refs_3_, ...), custom_call_target="tpu_custom_call" | custom-call | flops 1048576 | bytes 262144 | tf_op jit(solution)/shard_map/pallas_call | solution.py:226
  61.8 3.0 %shard_map.73 = (f32[64,1536]{1,0:T(8,128)S(1)}, f32[64,1536]{1,0:T(8,128)S(1)}) custom-call(s32[4]{0:T(128)S(1)} %fusion.13.refs_0_.place_ref, f32[32,1536]{1,0:T(8,128)S(1)} %get-tuple-element.75.refs_0_.refs_1_, f32[32,1536]{1,0:T(8,128)S(1)} %collective-permute-done.7.refs_2_, f32[32,1536]{1,0:T(8,128)S(1)} %collective-permute-done.8.refs_3_, ...), custom_call_target="tpu_custom_call" | custom-call | flops 1048576 | bytes 262144 | tf_op jit(solution)/shard_map/pallas_call | solution.py:178
  64.9 3.0 %shard_map.74 = (f32[64,3072]{1,0:T(8,128)S(1)}, f32[64,3072]{1,0:T(8,128)S(1)}) custom-call(s32[4]{0:T(128)S(1)} %fusion.13.refs_0_.place_ref, f32[32,1536]{1,0:T(8,128)S(1)} %get-tuple-element.75.refs_0_.refs_1_, f32[32,1536]{1,0:T(8,128)S(1)} %collective-permute-done.7.refs_2_, f32[32,1536]{1,0:T(8,128)S(1)} %collective-permute-done.8.refs_3_, ...), custom_call_target="tpu_custom_call" | custom-call | flops 1048576 | bytes 262144 | tf_op jit(solution)/shard_map/pallas_call | solution.py:178
  68.6 1.2 collective-permute-start.12
  69.8 3.0 %shard_map.75 = (f32[64,1536]{1,0:T(8,128)S(1)}, f32[64,1536]{1,0:T(8,128)S(1)}) custom-call(s32[4]{0:T(128)S(1)} %fusion.13.refs_0_.place_ref, f32[32,1536]{1,0:T(8,128)S(1)} %get-tuple-element.75.refs_0_.refs_1_, f32[32,1536]{1,0:T(8,128)S(1)} %collective-permute-done.7.refs_2_, f32[32,1536]{1,0:T(8,128)S(1)} %collective-permute-done.8.refs_3_, ...), custom_call_target="tpu_custom_call" | custom-call | flops 1048576 | bytes 262144 | tf_op jit(solution)/shard_map/pallas_call | solution.py:178
  73.9 3.0 %shard_map.76 = (f32[64,3072]{1,0:T(8,128)S(1)}, f32[64,3072]{1,0:T(8,128)S(1)}) custom-call(s32[4]{0:T(128)S(1)} %fusion.13.refs_0_.place_ref, f32[32,1536]{1,0:T(8,128)S(1)} %get-tuple-element.75.refs_0_.refs_1_, f32[32,1536]{1,0:T(8,128)S(1)} %collective-permute-done.7.refs_2_, f32[32,1536]{1,0:T(8,128)S(1)} %collective-permute-done.8.refs_3_, ...), custom_call_target="tpu_custom_call" | custom-call | flops 1048576 | bytes 262144 | tf_op jit(solution)/shard_map/pallas_call | solution.py:178
  77.0 3.6 %collective-permute-done.12 = f32[32,3072]{1,0:T(8,128)S(1)} collective-permute-done((f32[32,3072]{1,0:T(8,128)S(1)}, f32[32,3072]{1,0:T(8,128)S(1)}, u32[]{:S(2)}, u32[]{:S(2)}) %collective-permute-start.12) | collective-permute-done | bytes 393248 | tf_op jit(solution)/shard_map/ppermute | solution.py:317
  80.6 7.5 %collective-permute-done.16 = f32[32,3072]{1,0:T(8,128)S(1)} collective-permute-done((f32[32,3072]{1,0:T(8,128)S(1)}, f32[32,3072]{1,0:T(8,128)S(1)}, u32[]{:S(2)}, u32[]{:S(2)}) %collective-permute-start.16) | collective-permute-done | bytes 393248 | tf_op jit(solution)/shard_map/ppermute | solution.py:317
  90.6 9.8 %collective-permute-done.17.refs_1_ = f32[32,3072]{1,0:T(8,128)S(1)} collective-permute-done((f32[32,3072]{1,0:T(8,128)S(1)}, f32[32,3072]{1,0:T(8,128)S(1)}, u32[]{:S(2)}, u32[]{:S(2)}) %collective-permute-start.17) | collective-permute-done | bytes 393248 | tf_op jit(solution)/shard_map/ppermute | solution.py:317
  100.4 6.6 %collective-permute-done.14 = f32[32,3072]{1,0:T(8,128)S(1)} collective-permute-done((f32[32,3072]{1,0:T(8,128)S(1)}, f32[32,3072]{1,0:T(8,128)S(1)}, u32[]{:S(2)}, u32[]{:S(2)}) %collective-permute-start.14) | collective-permute-done | bytes 393248 | tf_op jit(solution)/shard_map/ppermute | solution.py:317
  108.4 7.3 %shard_map.77 = (f32[32,1536]{1,0:T(8,128)S(1)}, f32[32,1536]{1,0:T(8,128)S(1)}, f32[32,1536]{1,0:T(8,128)S(1)}, f32[32,1536]{1,0:T(8,128)S(1)}) custom-call(s32[4]{0:T(128)S(1)} %fusion.13.refs_0_.place_ref, f32[32,3072]{1,0:T(8,128)S(1)} %fusion.9.refs_0_, f32[32,3072]{1,0:T(8,128)S(1)} %collective-permute-done.17.refs_1_, ...), custom_call_target="tpu_custom_call" | custom-call | flops 1048576 | bytes 262144 | tf_op jit(solution)/shard_map/pallas_call | solution.py:286
  116.6 1.7 %collective-permute-done.21.refs_3_ = f32[32,3072]{1,0:T(8,128)S(1)} collective-permute-done((f32[32,3072]{1,0:T(8,128)S(1)}, f32[32,3072]{1,0:T(8,128)S(1)}, u32[]{:S(2)}, u32[]{:S(2)}) %collective-permute-start.21) | collective-permute-done | bytes 393248 | tf_op jit(solution)/shard_map/ppermute | solution.py:314
  118.3 4.0 %shard_map.78 = (f32[32,768]{1,0:T(8,128)S(1)}, f32[32,768]{1,0:T(8,128)S(1)}, f32[32,768]{1,0:T(8,128)S(1)}, f32[32,768]{1,0:T(8,128)S(1)}) custom-call(s32[4]{0:T(128)S(1)} %fusion.13.refs_0_.place_ref, f32[32,3072]{1,0:T(8,128)S(1)} %fusion.4.refs_0_, f32[32,3072]{1,0:T(8,128)S(1)} %collective-permute-done.15.refs_1_, ...), custom_call_target="tpu_custom_call" | custom-call | flops 1048576 | bytes 262144 | tf_op jit(solution)/shard_map/pallas_call | solution.py:286
  123.0 1.5 %collective-permute-start.23 = (f32[32,768]{1,0:T(8,128)S(1)}, f32[32,768]{1,0:T(8,128)S(1)}, u32[]{:S(2)}, u32[]{:S(2)}) collective-permute-start(f32[32,768]{1,0:T(8,128)S(1)} %get-tuple-element.112), channel_id=1, source_target_pairs={{0,8},{4,12},{8,0},{12,4},{1,9},{5,13},{9,1},{13,5},{2,10},{6,14},... | collective-permute-start | bytes 294920 | tf_op jit(solution)/shard_map/ppermute | solution.py:311
  124.5 2.8 %collective-permute-start.22 = (f32[32,768]{1,0:T(8,128)S(1)}, f32[32,768]{1,0:T(8,128)S(1)}, u32[]{:S(2)}, u32[]{:S(2)}) collective-permute-start(f32[32,768]{1,0:T(8,128)S(1)} %get-tuple-element.111), channel_id=1, source_target_pairs={{0,12},{4,0},{8,4},{12,8},{1,13},{5,1},{9,5},{13,9},{2,14},{6,2},{... | collective-permute-start | bytes 294920 | tf_op jit(solution)/shard_map/ppermute | solution.py:311
  127.5 4.0 %shard_map.79 = (f32[32,768]{1,0:T(8,128)S(1)}, f32[32,768]{1,0:T(8,128)S(1)}, f32[32,768]{1,0:T(8,128)S(1)}, f32[32,768]{1,0:T(8,128)S(1)}) custom-call(s32[4]{0:T(128)S(1)} %fusion.13.refs_0_.place_ref, f32[32,3072]{1,0:T(8,128)S(1)} %fusion.4.refs_0_, f32[32,3072]{1,0:T(8,128)S(1)} %collective-permute-done.15.refs_1_, ...), custom_call_target="tpu_custom_call" | custom-call | flops 1048576 | bytes 262144 | tf_op jit(solution)/shard_map/pallas_call | solution.py:286
  132.5 2.9 %collective-permute-start.25 = (f32[32,768]{1,0:T(8,128)S(1)}, f32[32,768]{1,0:T(8,128)S(1)}, u32[]{:S(2)}, u32[]{:S(2)}) collective-permute-start(f32[32,768]{1,0:T(8,128)S(1)} %get-tuple-element.115), channel_id=1, source_target_pairs={{0,12},{4,0},{8,4},{12,8},{1,13},{5,1},{9,5},{13,9},{2,14},{6,2},{... | collective-permute-start | bytes 294920 | tf_op jit(solution)/shard_map/ppermute | solution.py:311
  135.4 3.7 %collective-permute-done.27 = f32[32,768]{1,0:T(8,128)S(1)} collective-permute-done((f32[32,768]{1,0:T(8,128)S(1)}, f32[32,768]{1,0:T(8,128)S(1)}, u32[]{:S(2)}, u32[]{:S(2)}) %collective-permute-start.27) | collective-permute-done | bytes 98336 | tf_op jit(solution)/shard_map/ppermute | solution.py:311
  139.2 2.6 %collective-permute-done.26 = f32[32,768]{1,0:T(8,128)S(1)} collective-permute-done((f32[32,768]{1,0:T(8,128)S(1)}, f32[32,768]{1,0:T(8,128)S(1)}, u32[]{:S(2)}, u32[]{:S(2)}) %collective-permute-start.26) | collective-permute-done | bytes 98336 | tf_op jit(solution)/shard_map/ppermute | solution.py:311
  142.0 5.7 %psum.7 = f32[2,32]{1,0:T(2,128)S(1)} all-reduce(f32[2,32]{1,0:T(2,128)S(1)} %pad_maximum_fusion), channel_id=1, replica_groups=mesh['groups'=2,'hid'=4,'emb'=4] {'emb'}, use_global_device_ids=true, to_apply=%region_2.3 | all-reduce | flops 64 | bytes 512 | tf_op jit(solution)/shard_map/psum | solution.py:407
  (72 shorter events, 12.8 us)
Async XLA Ops:
  0.0 22.3 %collective-permute-start.1 = (f32[32,1536]{1,0:T(8,128)}, f32[32,1536]{1,0:T(8,128)S(1)}, u32[]{:S(2)}, u32[]{:S(2)}) collective-permute-start(f32[32,1536]{1,0:T(8,128)} %refs_1_.3), channel_id=1, source_target_pairs={{0,4},{4,8},{8,12},{12,0},{1,5},{5,9},{9,13},{13,1},{2,6},{6,10},{... | collective-permute-start | bytes 589832 | tf_op jit(solution)/shard_map/ppermute | solution.py:311
  3.0 19.3 %collective-permute-start.2 = (f32[32,1536]{1,0:T(8,128)}, f32[32,1536]{1,0:T(8,128)S(1)}, u32[]{:S(2)}, u32[]{:S(2)}) collective-permute-start(f32[32,1536]{1,0:T(8,128)} %refs_1_.3), channel_id=1, source_target_pairs={{0,8},{4,12},{8,0},{12,4},{1,9},{5,13},{9,1},{13,5},{2,10},{6,14},... | collective-permute-start | bytes 589832 | tf_op jit(solution)/shard_map/ppermute | solution.py:311
  5.6 16.7 %collective-permute-start.3 = (f32[32,1536]{1,0:T(8,128)}, f32[32,1536]{1,0:T(8,128)S(1)}, u32[]{:S(2)}, u32[]{:S(2)}) collective-permute-start(f32[32,1536]{1,0:T(8,128)} %refs_1_.3), channel_id=1, source_target_pairs={{0,12},{4,0},{8,4},{12,8},{1,13},{5,1},{9,5},{13,9},{2,14},{6,2},{... | collective-permute-start | bytes 589832 | tf_op jit(solution)/shard_map/ppermute | solution.py:311
  8.1 14.2 %collective-permute-start = (f32[64,128]{1,0:T(8,128)S(1)}, f32[64,128]{1,0:T(8,128)S(1)}, u32[]{:S(2)}, u32[]{:S(2)}) collective-permute-start(f32[64,128]{1,0:T(8,128)S(1)} %shard_map.64.refs_1_.refs_0_), channel_id=1, source_target_pairs={{0,1},{1,0},{2,3},{3,2},{4,5},{5,4},{6,7},{7,6},{8,9},{9,8},{10,11... | collective-permute-start | bytes 98312 | tf_op jit(solution)/shard_map/ppermute | solution.py:314
  22.2 1.7 %copy-start = (f32[32,1536]{1,0:T(8,128)S(1)}, f32[32,1536]{1,0:T(8,128)}, u32[]{:S(2)}) copy-start(f32[32,1536]{1,0:T(8,128)} %refs_1_.3) | copy-start | bytes 589828
  22.3 14.8 %copy-start.3 = (f32[1536]{0:T(1024)S(1)}, f32[1536]{0:T(1024)}, u32[]{:S(2)}) copy-start(f32[1536]{0:T(1024)} %param.11) | copy-start | bytes 18436
  22.3 14.7 %copy-start.2 = (f32[32,1536]{1,0:T(8,128)S(1)}, f32[32,1536]{1,0:T(8,128)}, u32[]{:S(2)}) copy-start(f32[32,1536]{1,0:T(8,128)} %refs_0_.3) | copy-start | bytes 589828
  22.3 14.5 %collective-permute-start.4 = (f32[64,128]{1,0:T(8,128)S(1)}, f32[64,128]{1,0:T(8,128)S(1)}, u32[]{:S(2)}, u32[]{:S(2)}) collective-permute-start(f32[64,128]{1,0:T(8,128)S(1)} %shard_map.68.refs_6_.refs_2_), channel_id=1, source_target_pairs={{0,2},{1,3},{2,0},{3,1},{4,6},{5,7},{6,4},{7,5},{8,10},{9,11},{10,... | collective-permute-start | bytes 98312 | tf_op jit(solution)/shard_map/ppermute | solution.py:317
  36.8 2.4 %collective-permute-start.5 = (f32[64,3072]{1,0:T(8,128)S(1)}, f32[64,3072]{1,0:T(8,128)S(1)}, u32[]{:S(2)}, u32[]{:S(2)}) collective-permute-start(f32[64,3072]{1,0:T(8,128)S(1)} %get-tuple-element.70), channel_id=1, source_target_pairs={{0,1},{1,0},{2,3},{3,2},{4,5},{5,4},{6,7},{7,6},{8,9},{9,8},{10,11... | collective-permute-start | bytes 2359304 | tf_op jit(solution)/shard_map/ppermute | solution.py:314
  39.3 22.4 %collective-permute-start.6 = (f32[32,3072]{1,0:T(8,128)S(1)}, f32[32,3072]{1,0:T(8,128)S(1)}, u32[]{:S(2)}, u32[]{:S(2)}) collective-permute-start(f32[32,3072]{1,0:T(8,128)S(1)} %get-tuple-element.124), channel_id=1, source_target_pairs={{0,2},{1,3},{2,0},{3,1},{4,6},{5,7},{6,4},{7,5},{8,10},{9,11},{10,... | collective-permute-start | bytes 1179656 | tf_op jit(solution)/shard_map/ppermute | solution.py:317
  40.2 21.4 %collective-permute-start.7 = (f32[32,1536]{1,0:T(8,128)S(1)}, f32[32,1536]{1,0:T(8,128)S(1)}, u32[]{:S(2)}, u32[]{:S(2)}) collective-permute-start(f32[32,1536]{1,0:T(8,128)S(1)} %get-tuple-element.75.refs_0_.refs_1_), channel_id=1, source_target_pairs={{0,4},{4,8},{8,12},{12,0},{1,5},{5,9},{9,13},{13,1},{2,6},{6,10},{... | collective-permute-start | bytes 589832 | tf_op jit(solution)/shard_map/ppermute | solution.py:311
  41.0 20.7 %collective-permute-start.8 = (f32[32,1536]{1,0:T(8,128)S(1)}, f32[32,1536]{1,0:T(8,128)S(1)}, u32[]{:S(2)}, u32[]{:S(2)}) collective-permute-start(f32[32,1536]{1,0:T(8,128)S(1)} %get-tuple-element.75.refs_0_.refs_1_), channel_id=1, source_target_pairs={{0,8},{4,12},{8,0},{12,4},{1,9},{5,13},{9,1},{13,5},{2,10},{6,14},... | collective-permute-start | bytes 589832 | tf_op jit(solution)/shard_map/ppermute | solution.py:311
  42.6 19.1 %collective-permute-start.9 = (f32[32,1536]{1,0:T(8,128)S(1)}, f32[32,1536]{1,0:T(8,128)S(1)}, u32[]{:S(2)}, u32[]{:S(2)}) collective-permute-start(f32[32,1536]{1,0:T(8,128)S(1)} %get-tuple-element.75.refs_0_.refs_1_), channel_id=1, source_target_pairs={{0,12},{4,0},{8,4},{12,8},{1,13},{5,1},{9,5},{13,9},{2,14},{6,2},{... | collective-permute-start | bytes 589832 | tf_op jit(solution)/shard_map/ppermute | solution.py:311
  61.7 3.1 %collective-permute-start.10 = (f32[64,3072]{1,0:T(8,128)S(1)}, f32[64,3072]{1,0:T(8,128)S(1)}, u32[]{:S(2)}, u32[]{:S(2)}) collective-permute-start(f32[64,3072]{1,0:T(8,128)S(1)} %get-tuple-element.86), channel_id=1, source_target_pairs={{0,1},{1,0},{2,3},{3,2},{4,5},{5,4},{6,7},{7,6},{8,9},{9,8},{10,11... | collective-permute-start | bytes 2359304 | tf_op jit(solution)/shard_map/ppermute | solution.py:314
  68.0 4.8 %collective-permute-start.11 = (f32[64,3072]{1,0:T(8,128)S(1)}, f32[64,3072]{1,0:T(8,128)S(1)}, u32[]{:S(2)}, u32[]{:S(2)}) collective-permute-start(f32[64,3072]{1,0:T(8,128)S(1)} %get-tuple-element.91), channel_id=1, source_target_pairs={{0,1},{1,0},{2,3},{3,2},{4,5},{5,4},{6,7},{7,6},{8,9},{9,8},{10,11... | collective-permute-start | bytes 2359304 | tf_op jit(solution)/shard_map/ppermute | solution.py:314
  68.6 12.0 %collective-permute-start.12 = (f32[32,3072]{1,0:T(8,128)S(1)}, f32[32,3072]{1,0:T(8,128)S(1)}, u32[]{:S(2)}, u32[]{:S(2)}) collective-permute-start(f32[32,3072]{1,0:T(8,128)S(1)} %get-tuple-element.122), channel_id=1, source_target_pairs={{0,2},{1,3},{2,0},{3,1},{4,6},{5,7},{6,4},{7,5},{8,10},{9,11},{10,... | collective-permute-start | bytes 1179656 | tf_op jit(solution)/shard_map/ppermute | solution.py:317
  73.0 15.1 %collective-permute-start.16 = (f32[32,3072]{1,0:T(8,128)S(1)}, f32[32,3072]{1,0:T(8,128)S(1)}, u32[]{:S(2)}, u32[]{:S(2)}) collective-permute-start(f32[32,3072]{1,0:T(8,128)S(1)} %slice.52), channel_id=1, source_target_pairs={{0,2},{1,3},{2,0},{3,1},{4,6},{5,7},{6,4},{7,5},{8,10},{9,11},{10,... | collective-permute-start | bytes 1179656 | tf_op jit(solution)/shard_map/ppermute | solution.py:317
  73.9 6.7 %copy-start.4 = (f32[6144]{0:T(1024)S(1)}, f32[6144]{0:T(1024)}, u32[]{:S(2)}) copy-start(f32[6144]{0:T(1024)} %param.9) | copy-start | bytes 73732
  80.6 8.9 %collective-permute-start.13 = (f32[64,3072]{1,0:T(8,128)S(1)}, f32[64,3072]{1,0:T(8,128)S(1)}, u32[]{:S(2)}, u32[]{:S(2)}) collective-permute-start(f32[64,3072]{1,0:T(8,128)S(1)} %get-tuple-element.98), channel_id=1, source_target_pairs={{0,1},{1,0},{2,3},{3,2},{4,5},{5,4},{6,7},{7,6},{8,9},{9,8},{10,11... | collective-permute-start | bytes 2359304 | tf_op jit(solution)/shard_map/ppermute | solution.py:314
  88.3 12.1 %collective-permute-start.17 = (f32[32,3072]{1,0:T(8,128)S(1)}, f32[32,3072]{1,0:T(8,128)S(1)}, u32[]{:S(2)}, u32[]{:S(2)}) collective-permute-start(f32[32,3072]{1,0:T(8,128)S(1)} %fusion.9.refs_0_), channel_id=1, source_target_pairs={{0,2},{1,3},{2,0},{3,1},{4,6},{5,7},{6,4},{7,5},{8,10},{9,11},{10,... | collective-permute-start | bytes 1179656 | tf_op jit(solution)/shard_map/ppermute | solution.py:317
  89.7 17.3 %collective-permute-start.14 = (f32[32,3072]{1,0:T(8,128)S(1)}, f32[32,3072]{1,0:T(8,128)S(1)}, u32[]{:S(2)}, u32[]{:S(2)}) collective-permute-start(f32[32,3072]{1,0:T(8,128)S(1)} %slice.50), channel_id=1, source_target_pairs={{0,2},{1,3},{2,0},{3,1},{4,6},{5,7},{6,4},{7,5},{8,10},{9,11},{10,... | collective-permute-start | bytes 1179656 | tf_op jit(solution)/shard_map/ppermute | solution.py:317
  90.6 17.8 %collective-permute-start.18 = (f32[32,3072]{1,0:T(8,128)S(1)}, f32[32,3072]{1,0:T(8,128)S(1)}, u32[]{:S(2)}, u32[]{:S(2)}) collective-permute-start(f32[32,3072]{1,0:T(8,128)S(1)} %fusion.9.refs_0_), channel_id=1, source_target_pairs={{0,1},{1,0},{2,3},{3,2},{4,5},{5,4},{6,7},{7,6},{8,9},{9,8},{10,11... | collective-permute-start | bytes 1179656 | tf_op jit(solution)/shard_map/ppermute | solution.py:314
  100.4 8.0 %collective-permute-start.19 = (f32[32,3072]{1,0:T(8,128)S(1)}, f32[32,3072]{1,0:T(8,128)S(1)}, u32[]{:S(2)}, u32[]{:S(2)}) collective-permute-start(f32[32,3072]{1,0:T(8,128)S(1)} %collective-permute-done.17.refs_1_), channel_id=1, source_target_pairs={{0,1},{1,0},{2,3},{3,2},{4,5},{5,4},{6,7},{7,6},{8,9},{9,8},{10,11... | collective-permute-start | bytes 1179656 | tf_op jit(solution)/shard_map/ppermute | solution.py:314
  107.2 9.3 %collective-permute-start.15 = (f32[32,3072]{1,0:T(8,128)S(1)}, f32[32,3072]{1,0:T(8,128)S(1)}, u32[]{:S(2)}, u32[]{:S(2)}) collective-permute-start(f32[32,3072]{1,0:T(8,128)S(1)} %fusion.4.refs_0_), channel_id=1, source_target_pairs={{0,2},{1,3},{2,0},{3,1},{4,6},{5,7},{6,4},{7,5},{8,10},{9,11},{10,... | collective-permute-start | bytes 1179656 | tf_op jit(solution)/shard_map/ppermute | solution.py:317
  108.4 8.1 %collective-permute-start.20 = (f32[32,3072]{1,0:T(8,128)S(1)}, f32[32,3072]{1,0:T(8,128)S(1)}, u32[]{:S(2)}, u32[]{:S(2)}) collective-permute-start(f32[32,3072]{1,0:T(8,128)S(1)} %fusion.4.refs_0_), channel_id=1, source_target_pairs={{0,1},{1,0},{2,3},{3,2},{4,5},{5,4},{6,7},{7,6},{8,9},{9,8},{10,11... | collective-permute-start | bytes 1179656 | tf_op jit(solution)/shard_map/ppermute | solution.py:314
  116.6 1.7 %collective-permute-start.21 = (f32[32,3072]{1,0:T(8,128)S(1)}, f32[32,3072]{1,0:T(8,128)S(1)}, u32[]{:S(2)}, u32[]{:S(2)}) collective-permute-start(f32[32,3072]{1,0:T(8,128)S(1)} %collective-permute-done.15.refs_1_), channel_id=1, source_target_pairs={{0,1},{1,0},{2,3},{3,2},{4,5},{5,4},{6,7},{7,6},{8,9},{9,8},{10,11... | collective-permute-start | bytes 1179656 | tf_op jit(solution)/shard_map/ppermute | solution.py:314
  122.3 10.2 %collective-permute-start.24 = (f32[32,768]{1,0:T(8,128)S(1)}, f32[32,768]{1,0:T(8,128)S(1)}, u32[]{:S(2)}, u32[]{:S(2)}) collective-permute-start(f32[32,768]{1,0:T(8,128)S(1)} %get-tuple-element.113), channel_id=1, source_target_pairs={{0,4},{4,8},{8,12},{12,0},{1,5},{5,9},{9,13},{13,1},{2,6},{6,10},{... | collective-permute-start | bytes 294920 | tf_op jit(solution)/shard_map/ppermute | solution.py:311
  123.0 12.4 %collective-permute-start.23 = (f32[32,768]{1,0:T(8,128)S(1)}, f32[32,768]{1,0:T(8,128)S(1)}, u32[]{:S(2)}, u32[]{:S(2)}) collective-permute-start(f32[32,768]{1,0:T(8,128)S(1)} %get-tuple-element.112), channel_id=1, source_target_pairs={{0,8},{4,12},{8,0},{12,4},{1,9},{5,13},{9,1},{13,5},{2,10},{6,14},... | collective-permute-start | bytes 294920 | tf_op jit(solution)/shard_map/ppermute | solution.py:311
  124.5 10.9 %collective-permute-start.22 = (f32[32,768]{1,0:T(8,128)S(1)}, f32[32,768]{1,0:T(8,128)S(1)}, u32[]{:S(2)}, u32[]{:S(2)}) collective-permute-start(f32[32,768]{1,0:T(8,128)S(1)} %get-tuple-element.111), channel_id=1, source_target_pairs={{0,12},{4,0},{8,4},{12,8},{1,13},{5,1},{9,5},{13,9},{2,14},{6,2},{... | collective-permute-start | bytes 294920 | tf_op jit(solution)/shard_map/ppermute | solution.py:311
  131.5 7.6 %collective-permute-start.27 = (f32[32,768]{1,0:T(8,128)S(1)}, f32[32,768]{1,0:T(8,128)S(1)}, u32[]{:S(2)}, u32[]{:S(2)}) collective-permute-start(f32[32,768]{1,0:T(8,128)S(1)} %get-tuple-element.117), channel_id=1, source_target_pairs={{0,4},{4,8},{8,12},{12,0},{1,5},{5,9},{9,13},{13,1},{2,6},{6,10},{... | collective-permute-start | bytes 294920 | tf_op jit(solution)/shard_map/ppermute | solution.py:311
  131.6 10.2 %collective-permute-start.26 = (f32[32,768]{1,0:T(8,128)S(1)}, f32[32,768]{1,0:T(8,128)S(1)}, u32[]{:S(2)}, u32[]{:S(2)}) collective-permute-start(f32[32,768]{1,0:T(8,128)S(1)} %get-tuple-element.116), channel_id=1, source_target_pairs={{0,8},{4,12},{8,0},{12,4},{1,9},{5,13},{9,1},{13,5},{2,10},{6,14},... | collective-permute-start | bytes 294920 | tf_op jit(solution)/shard_map/ppermute | solution.py:311
  132.5 9.2 %collective-permute-start.25 = (f32[32,768]{1,0:T(8,128)S(1)}, f32[32,768]{1,0:T(8,128)S(1)}, u32[]{:S(2)}, u32[]{:S(2)}) collective-permute-start(f32[32,768]{1,0:T(8,128)S(1)} %get-tuple-element.115), channel_id=1, source_target_pairs={{0,12},{4,0},{8,4},{12,8},{1,13},{5,1},{9,5},{13,9},{2,14},{6,2},{... | collective-permute-start | bytes 294920 | tf_op jit(solution)/shard_map/ppermute | solution.py:311
  (1 other events, 0.9 us)

commit v8 on v7

--- a/solution.py
+++ b/solution.py
@@ -104,7 +104,7 @@
 
 
 def prepare(weight, rows, columns, after):
-    block = 128 * 1536 // columns[1]
+    block = 256 * 1536 // columns[1]
     block = divisor(rows[1], *[b for b in (256, 128, 64, 32) if b <= max(block, 32)])
     depth = 4
     out = pltpu.VMEM((rows[1], columns[1]), jnp.bfloat16)
@@ -117,7 +117,7 @@
             pltpu.VMEM((depth, block, columns[1]), jnp.float32),
             pltpu.SemaphoreType.DMA((depth,)),
         ],
-        compiler_params=pltpu.CompilerParams(vmem_limit_bytes=VMEM_LIMIT),
+        compiler_params=pltpu.CompilerParams(vmem_limit_bytes=2 * VMEM_LIMIT),
         cost_estimate=SHORT,
     )(pltpu.with_memory_space_constraint(weight, pltpu.HBM), *after)
 
@@ -219,7 +219,7 @@
 
 def stream(slots, weight, place, first, hidden, earlier, after):
     tokens, columns = slots[0].shape[0] * len(slots), slots[0].shape[1]
-    width, depth = divisor(hidden, 256, 128), 2
+    width, depth = divisor(hidden, 256, 128), 4
     out = jax.ShapeDtypeStruct((tokens // 2, hidden + (earlier[0].shape[1] if earlier else 0)), jnp.float32)
     inside, anywhere = pl.BlockSpec(memory_space=pltpu.VMEM), pl.BlockSpec(memory_space=pl.ANY)
     last = 1 + len(slots)
@@ -239,7 +239,7 @@
             pltpu.VMEM((depth, width, columns), jnp.float32),
             pltpu.SemaphoreType.DMA((depth,)),
         ],
-        compiler_params=pltpu.CompilerParams(vmem_limit_bytes=VMEM_LIMIT),
+        compiler_params=pltpu.CompilerParams(vmem_limit_bytes=2 * VMEM_LIMIT),
         cost_estimate=SHORT,
     )(place, *slots, pltpu.with_memory_space_constraint(weight, pltpu.HBM), *earlier, *after)
 
@@ -346,11 +346,10 @@
     moments = call(moments_kernel, jax.ShapeDtypeStruct((2 * tokens, 128), jnp.float32), (inputs,), ())
     in_parts = prepared(0, [place, moments])
     in_parts += prepared(1, [in_parts[0]])
-    in_parts += prepared(2, [in_parts[2]])
     moments = call(
-        functools.partial(merge_kernel, depth), moments, (moments, other_core(moments)), (in_parts[4], *grads[1:])
+        functools.partial(merge_kernel, depth), moments, (moments, other_core(moments)), (in_parts[2], *grads[1:])
     )
-    back_0 = stream(grads, out_weight, place, 0, piece, (), [moments])
+    in_parts += prepared(2, [moments])
     parts = [moments]
     for _ in range(1, chips):
         parts.append(next_chip(parts[-1]))
@@ -358,24 +357,24 @@
         functools.partial(normalise_kernel, 2 * depth),
         (inputs, inputs, jax.ShapeDtypeStruct((tokens, 128), jnp.float32)),
         (inputs, norm_gain[None, :], *parts),
-        (back_0[1],),
+        (in_parts[4],),
     )
     inv_std = inv_std[:, :1]
     scaled = gathered(scaled)
-    back_0, _ = tied(back_0, parts)
-    half_0 = halved(back_0, scaled[0])
-    in_parts += prepared(3, [scaled[0], half_0])
-    back_1 = stream(grads, out_weight, place, piece, piece, (), [in_parts[6]])
+    back_0 = stream(grads, out_weight, place, 0, piece, (), [scaled[0]])
+    back_0, (scaled[1], scaled[-1]) = tied(back_0, (scaled[1], scaled[-1]))
+    half_0 = halved(back_0)
+    back_1 = stream(grads, out_weight, place, piece, piece, (), [half_0])
     back_0 = exchanged(half_0)
     back_1, (back_0, scaled) = tied(back_1, (back_0, scaled))
-    pre_0 = forward(scaled, in_parts[:2], place, (), [back_1[1]])
-    half_1 = halved(back_1, pre_0)
+    in_parts += prepared(3, [back_1[0]])
+    half_1 = halved(back_1, in_parts[6])
     back_1 = exchanged(half_1)
-    pre_0 = forward(scaled, in_parts[2:4], place, pre_0, [half_1])
+    pre_0 = forward(scaled, in_parts[:4], place, (), [half_1])
+    pre_0, back_1 = tied(pre_0, back_1)
     pre_1 = forward(scaled, in_parts[4:6], place, (), [pre_0[1]])
     half_0 = halved(pre_0, pre_1)
     pre_1 = forward(scaled, in_parts[6:], place, pre_1, [half_0])
-    pre_1, back_1 = tied(pre_1, back_1)
     backs = [back_0, back_1]
     pres = [exchanged(half_0), exchanged(halved(pre_1))]
 

time: 149 us -> 147 us (0.987)
  Pallas kernels: 72.3 us -> 62.2 us
  waiting for transfers between devices: 38.4 us -> 43.7 us
  starting transfers between devices: 28.6 us -> 31.6 us
    pallas_call x2, Pallas kernels: 25.8 us -> 18.3 us  [stream(): pl.pallas_call(lambda *refs: stream_kernel(first, depth, refs[0], refs[1:...]
    ppermute x12, waiting for transfers between devices: 6.38 us -> 10.4 us  [along_hid(): lax.ppermute(values, 'hid', [(i, (i + steps) % hid_size) for i in range(h...]
    ppermute x12, starting transfers between devices: 19.7 us -> 22.2 us  [along_hid(): lax.ppermute(values, 'hid', [(i, (i + steps) % hid_size) for i in range(h...]
    pallas_call x4, Pallas kernels: 18.8 us -> 16.8 us  [prepare(): pl.pallas_call(functools.partial(prepare_kernel, rows, columns, block, de...]
    pallas_call x4 -> x3, Pallas kernels: 12.1 us -> 11.4 us  [forward(): pl.pallas_call(lambda *refs: forward_kernel(refs[0], refs[1:ends[0]], ref...]
  transfers between devices with their start and end apart: 28 -> 28, of which waited for: 9 -> 11; matrix products, arithmetic and copies ran while one was open for 1% -> 0% of each run, Pallas kernels for 44% -> 40%
where the time goes in v8:
time: 147 us; the launch traced here: 146 us
  Pallas kernels  62.2 us (42%)
  waiting for transfers between devices  43.7 us (30%)
  starting transfers between devices  31.6 us (21%)
  blocking collectives  5.67 us (4%)
  other arithmetic  1.79 us (1%)
    ppermute x7, waiting for transfers between devices, next_chip(): lax.ppermute(values, 'emb', [(i, (i + 2) % emb_size) for i in range(emb_s...  29.3 us
    ppermute x12, starting transfers between devices, along_hid(): lax.ppermute(values, 'hid', [(i, (i + steps) % hid_size) for i in range(h...  22.2 us
    pallas_call x2, Pallas kernels, stream(): pl.pallas_call(lambda *refs: stream_kernel(first, depth, refs[0], refs[1:...  18.3 us
    pallas_call x4, Pallas kernels, prepare(): pl.pallas_call(functools.partial(prepare_kernel, rows, columns, block, de...  16.8 us
    pallas_call x3, Pallas kernels, backward(): pl.pallas_call(functools.partial(backward_kernel, slots, len(weights) //...  15.4 us
    pallas_call x3, Pallas kernels, forward(): pl.pallas_call(lambda *refs: forward_kernel(refs[0], refs[1:ends[0]], ref...  11.4 us
    ppermute x12, waiting for transfers between devices, along_hid(): lax.ppermute(values, 'hid', [(i, (i + steps) % hid_size) for i in range(h...  10.4 us
    ppermute x7, starting transfers between devices, next_chip(): lax.ppermute(values, 'emb', [(i, (i + 2) % emb_size) for i in range(emb_s...  8.98 us
  transfers between devices with their start and end apart: 28, of which 11 were waited for; matrix products, arithmetic and copies ran while one was open for 0% of the time, Pallas kernels for 40%

profile of v8, /device:TPU:0, one launch (start us, length us, event | category | flops | bytes accessed | tf_op | source)
XLA Modules:
  0.0 146.5 jit_solution(15675471750786684195)
XLA Ops:
  0.0 3.0 %collective-permute-start.1 = (f32[32,1536]{1,0:T(8,128)}, f32[32,1536]{1,0:T(8,128)S(1)}, u32[]{:S(2)}, u32[]{:S(2)}) collective-permute-start(f32[32,1536]{1,0:T(8,128)} %refs_1_.3), channel_id=1, source_target_pairs={{0,4},{4,8},{8,12},{12,0},{1,5},{5,9},{9,13},{13,1},{2,6},{6,10},{... | collective-permute-start | bytes 589832 | tf_op jit(solution)/shard_map/ppermute | solution.py:311
  3.0 2.6 %collective-permute-start.2 = (f32[32,1536]{1,0:T(8,128)}, f32[32,1536]{1,0:T(8,128)S(1)}, u32[]{:S(2)}, u32[]{:S(2)}) collective-permute-start(f32[32,1536]{1,0:T(8,128)} %refs_1_.3), channel_id=1, source_target_pairs={{0,8},{4,12},{8,0},{12,4},{1,9},{5,13},{9,1},{13,5},{2,10},{6,14},... | collective-permute-start | bytes 589832 | tf_op jit(solution)/shard_map/ppermute | solution.py:311
  8.1 4.2 %shard_map.65 = (bf16[1536,1536]{1,0:T(8,128)(2,1)S(1)}, bf16[1536,1536]{1,0:T(8,128)(2,1)S(1)}) custom-call(f32[1536,6144]{1,0:T(8,128)} %weight_ref.7, s32[4]{0:T(128)S(1)} %fusion.13.refs_0_.place_ref, f32[64,128]{1,0:T(8,128)S(1)} %shard_map.64.refs_1_.refs_0_), custom_call_target="tpu_custom_call" | custom-call | flops 1048576 | bytes 262144 | tf_op jit(solution)/shard_map/pallas_call | solution.py:111
  12.3 4.2 %shard_map.66 = (bf16[1536,1536]{1,0:T(8,128)(2,1)S(1)}, bf16[1536,1536]{1,0:T(8,128)(2,1)S(1)}) custom-call(f32[1536,6144]{1,0:T(8,128)} %weight_ref.7, bf16[1536,1536]{1,0:T(8,128)(2,1)S(1)} %get-tuple-element.61.refs_0_.refs_5_.refs_4_), custom_call_target="tpu_custom_call" | custom-call | flops 1048576 | bytes 262144 | tf_op jit(solution)/shard_map/pallas_call | solution.py:111
  16.6 2.1 %collective-permute-done.2.refs_4_.refs_3_ = f32[32,1536]{1,0:T(8,128)S(1)} collective-permute-done((f32[32,1536]{1,0:T(8,128)}, f32[32,1536]{1,0:T(8,128)S(1)}, u32[]{:S(2)}, u32[]{:S(2)}) %collective-permute-start.2) | collective-permute-done | bytes 196640 | tf_op jit(solution)/shard_map/ppermute | solution.py:311
  20.3 4.2 %shard_map.68 = (bf16[1536,1536]{1,0:T(8,128)(2,1)S(1)}, bf16[1536,1536]{1,0:T(8,128)(2,1)S(1)}) custom-call(f32[1536,6144]{1,0:T(8,128)} %weight_ref.7, f32[64,128]{1,0:T(8,128)S(1)} %shard_map.67.refs_0_.refs_2_), custom_call_target="tpu_custom_call" | custom-call | flops 1048576 | bytes 262144 | tf_op jit(solution)/shard_map/pallas_call | solution.py:111
  24.7 4.7 %collective-permute-start.5 = (f32[32,1536]{1,0:T(8,128)S(1)}, f32[32,1536]{1,0:T(8,128)S(1)}, u32[]{:S(2)}, u32[]{:S(2)}) collective-permute-start(f32[32,1536]{1,0:T(8,128)S(1)} %get-tuple-element.74.refs_6_.refs_1_), channel_id=1, source_target_pairs={{0,4},{4,8},{8,12},{12,0},{1,5},{5,9},{9,13},{13,1},{2,6},{6,10},{... | collective-permute-start | bytes 589832 | tf_op jit(solution)/shard_map/ppermute | solution.py:311
  30.5 9.2 %shard_map.70 = (f32[64,3072]{1,0:T(8,128)S(1)}, f32[64,3072]{1,0:T(8,128)S(1)}) custom-call(s32[4]{0:T(128)S(1)} %fusion.13.refs_0_.place_ref, f32[32,1536]{1,0:T(8,128)S(1)} %copy-done, f32[32,1536]{1,0:T(8,128)S(1)} %collective-permute-done.1.refs_3_.refs_2_, f32[32,1536]{1,0:T(8,128)S(1)} %collective-permute-done.2.refs_4_.refs_3_, ...), custom_call_target="tpu_custom_call" | custom-call | flops 1048576 | bytes 262144 | tf_op jit(solution)/shard_map/pallas_call | solution.py:226
  39.8 2.3 %collective-permute-done.7 = f32[64,3072]{1,0:T(8,128)S(1)} collective-permute-done((f32[64,3072]{1,0:T(8,128)S(1)}, f32[64,3072]{1,0:T(8,128)S(1)}, u32[]{:S(2)}, u32[]{:S(2)}) %collective-permute-start.7) | collective-permute-done | bytes 786464 | tf_op jit(solution)/shard_map/ppermute | solution.py:314
  43.3 9.1 %shard_map.71 = (f32[64,3072]{1,0:T(8,128)S(1)}, f32[64,3072]{1,0:T(8,128)S(1)}) custom-call(s32[4]{0:T(128)S(1)} %fusion.13.refs_0_.place_ref, f32[32,1536]{1,0:T(8,128)S(1)} %copy-done, f32[32,1536]{1,0:T(8,128)S(1)} %collective-permute-done.1.refs_3_.refs_2_, f32[32,1536]{1,0:T(8,128)S(1)} %collective-permute-done.2.refs_4_.refs_3_, ...), custom_call_target="tpu_custom_call" | custom-call | flops 1048576 | bytes 262144 | tf_op jit(solution)/shard_map/pallas_call | solution.py:226
  52.5 2.1 %collective-permute-done.9.refs_3_ = f32[32,1536]{1,0:T(8,128)S(1)} collective-permute-done((f32[32,1536]{1,0:T(8,128)S(1)}, f32[32,1536]{1,0:T(8,128)S(1)}, u32[]{:S(2)}, u32[]{:S(2)}) %collective-permute-start.9) | collective-permute-done | bytes 196640 | tf_op jit(solution)/shard_map/ppermute | solution.py:311
  54.6 4.2 %shard_map.72 = (bf16[1536,1536]{1,0:T(8,128)(2,1)S(1)}, bf16[1536,1536]{1,0:T(8,128)(2,1)S(1)}) custom-call(f32[1536,6144]{1,0:T(8,128)} %weight_ref.7, f32[64,3072]{1,0:T(8,128)S(1)} %get-tuple-element.81.refs_0_), custom_call_target="tpu_custom_call" | custom-call | flops 1048576 | bytes 262144 | tf_op jit(solution)/shard_map/pallas_call | solution.py:111
  59.0 1.6 %collective-permute-start.11 = (f32[32,3072]{1,0:T(8,128)S(1)}, f32[32,3072]{1,0:T(8,128)S(1)}, u32[]{:S(2)}, u32[]{:S(2)}) collective-permute-start(f32[32,3072]{1,0:T(8,128)S(1)} %get-tuple-element.120), channel_id=1, source_target_pairs={{0,2},{1,3},{2,0},{3,1},{4,6},{5,7},{6,4},{7,5},{8,10},{9,11},{10,... | collective-permute-start | bytes 1179656 | tf_op jit(solution)/shard_map/ppermute | solution.py:317
  60.5 5.4 %shard_map.73 = (f32[64,3072]{1,0:T(8,128)S(1)}, f32[64,3072]{1,0:T(8,128)S(1)}) custom-call(s32[4]{0:T(128)S(1)} %fusion.13.refs_0_.place_ref, f32[32,1536]{1,0:T(8,128)S(1)} %get-tuple-element.74.refs_6_.refs_1_, f32[32,1536]{1,0:T(8,128)S(1)} %collective-permute-done.5.refs_2_, f32[32,1536]{1,0:T(8,128)S(1)} %collective-permute-done.9.refs_3_, ...), custom_call_target="tpu_custom_call" | custom-call | flops 1048576 | bytes 262144 | tf_op jit(solution)/shard_map/pallas_call | solution.py:178
  65.9 4.6 %collective-permute-done.11 = f32[32,3072]{1,0:T(8,128)S(1)} collective-permute-done((f32[32,3072]{1,0:T(8,128)S(1)}, f32[32,3072]{1,0:T(8,128)S(1)}, u32[]{:S(2)}, u32[]{:S(2)}) %collective-permute-start.11) | collective-permute-done | bytes 393248 | tf_op jit(solution)/shard_map/ppermute | solution.py:317
  70.6 3.0 %shard_map.74 = (f32[64,1536]{1,0:T(8,128)S(1)}, f32[64,1536]{1,0:T(8,128)S(1)}) custom-call(s32[4]{0:T(128)S(1)} %fusion.13.refs_0_.place_ref, f32[32,1536]{1,0:T(8,128)S(1)} %get-tuple-element.74.refs_6_.refs_1_, f32[32,1536]{1,0:T(8,128)S(1)} %collective-permute-done.5.refs_2_, f32[32,1536]{1,0:T(8,128)S(1)} %collective-permute-done.9.refs_3_, ...), custom_call_target="tpu_custom_call" | custom-call | flops 1048576 | bytes 262144 | tf_op jit(solution)/shard_map/pallas_call | solution.py:178
  75.3 3.0 %shard_map.75 = (f32[64,3072]{1,0:T(8,128)S(1)}, f32[64,3072]{1,0:T(8,128)S(1)}) custom-call(s32[4]{0:T(128)S(1)} %fusion.13.refs_0_.place_ref, f32[32,1536]{1,0:T(8,128)S(1)} %get-tuple-element.74.refs_6_.refs_1_, f32[32,1536]{1,0:T(8,128)S(1)} %collective-permute-done.5.refs_2_, f32[32,1536]{1,0:T(8,128)S(1)} %collective-permute-done.9.refs_3_, ...), custom_call_target="tpu_custom_call" | custom-call | flops 1048576 | bytes 262144 | tf_op jit(solution)/shard_map/pallas_call | solution.py:178
  78.7 6.7 %collective-permute-done.16 = f32[32,3072]{1,0:T(8,128)S(1)} collective-permute-done((f32[32,3072]{1,0:T(8,128)S(1)}, f32[32,3072]{1,0:T(8,128)S(1)}, u32[]{:S(2)}, u32[]{:S(2)}) %collective-permute-start.16) | collective-permute-done | bytes 393248 | tf_op jit(solution)/shard_map/ppermute | solution.py:317
  85.5 1.6 %collective-permute-start.17 = (f32[32,3072]{1,0:T(8,128)S(1)}, f32[32,3072]{1,0:T(8,128)S(1)}, u32[]{:S(2)}, u32[]{:S(2)}) collective-permute-start(f32[32,3072]{1,0:T(8,128)S(1)} %fusion.9.refs_0_), channel_id=1, source_target_pairs={{0,2},{1,3},{2,0},{3,1},{4,6},{5,7},{6,4},{7,5},{8,10},{9,11},{10,... | collective-permute-start | bytes 1179656 | tf_op jit(solution)/shard_map/ppermute | solution.py:317
  87.8 9.8 %collective-permute-done.17.refs_1_ = f32[32,3072]{1,0:T(8,128)S(1)} collective-permute-done((f32[32,3072]{1,0:T(8,128)S(1)}, f32[32,3072]{1,0:T(8,128)S(1)}, u32[]{:S(2)}, u32[]{:S(2)}) %collective-permute-start.17) | collective-permute-done | bytes 393248 | tf_op jit(solution)/shard_map/ppermute | solution.py:317
  97.6 7.1 %collective-permute-done.14 = f32[32,3072]{1,0:T(8,128)S(1)} collective-permute-done((f32[32,3072]{1,0:T(8,128)S(1)}, f32[32,3072]{1,0:T(8,128)S(1)}, u32[]{:S(2)}, u32[]{:S(2)}) %collective-permute-start.14) | collective-permute-done | bytes 393248 | tf_op jit(solution)/shard_map/ppermute | solution.py:317
  105.0 1.6 %collective-permute-start.15 = (f32[32,3072]{1,0:T(8,128)S(1)}, f32[32,3072]{1,0:T(8,128)S(1)}, u32[]{:S(2)}, u32[]{:S(2)}) collective-permute-start(f32[32,3072]{1,0:T(8,128)S(1)} %fusion.4.refs_0_), channel_id=1, source_target_pairs={{0,2},{1,3},{2,0},{3,1},{4,6},{5,7},{6,4},{7,5},{8,10},{9,11},{10,... | collective-permute-start | bytes 1179656 | tf_op jit(solution)/shard_map/ppermute | solution.py:317
  106.6 7.3 %shard_map.76 = (f32[32,1536]{1,0:T(8,128)S(1)}, f32[32,1536]{1,0:T(8,128)S(1)}, f32[32,1536]{1,0:T(8,128)S(1)}, f32[32,1536]{1,0:T(8,128)S(1)}) custom-call(s32[4]{0:T(128)S(1)} %fusion.13.refs_0_.place_ref, f32[32,3072]{1,0:T(8,128)S(1)} %fusion.9.refs_0_, f32[32,3072]{1,0:T(8,128)S(1)} %collective-permute-done.17.refs_1_, ...), custom_call_target="tpu_custom_call" | custom-call | flops 1048576 | bytes 262144 | tf_op jit(solution)/shard_map/pallas_call | solution.py:286
  114.9 1.7 %collective-permute-done.21.refs_3_ = f32[32,3072]{1,0:T(8,128)S(1)} collective-permute-done((f32[32,3072]{1,0:T(8,128)S(1)}, f32[32,3072]{1,0:T(8,128)S(1)}, u32[]{:S(2)}, u32[]{:S(2)}) %collective-permute-start.21) | collective-permute-done | bytes 393248 | tf_op jit(solution)/shard_map/ppermute | solution.py:314
  116.6 4.0 %shard_map.77 = (f32[32,768]{1,0:T(8,128)S(1)}, f32[32,768]{1,0:T(8,128)S(1)}, f32[32,768]{1,0:T(8,128)S(1)}, f32[32,768]{1,0:T(8,128)S(1)}) custom-call(s32[4]{0:T(128)S(1)} %fusion.13.refs_0_.place_ref, f32[32,3072]{1,0:T(8,128)S(1)} %fusion.4.refs_0_, f32[32,3072]{1,0:T(8,128)S(1)} %collective-permute-done.15.refs_1_, ...), custom_call_target="tpu_custom_call" | custom-call | flops 1048576 | bytes 262144 | tf_op jit(solution)/shard_map/pallas_call | solution.py:286
  121.0 1.8 %collective-permute-start.23 = (f32[32,768]{1,0:T(8,128)S(1)}, f32[32,768]{1,0:T(8,128)S(1)}, u32[]{:S(2)}, u32[]{:S(2)}) collective-permute-start(f32[32,768]{1,0:T(8,128)S(1)} %get-tuple-element.110), channel_id=1, source_target_pairs={{0,8},{4,12},{8,0},{12,4},{1,9},{5,13},{9,1},{13,5},{2,10},{6,14},... | collective-permute-start | bytes 294920 | tf_op jit(solution)/shard_map/ppermute | solution.py:311
  122.7 1.9 %collective-permute-start.22 = (f32[32,768]{1,0:T(8,128)S(1)}, f32[32,768]{1,0:T(8,128)S(1)}, u32[]{:S(2)}, u32[]{:S(2)}) collective-permute-start(f32[32,768]{1,0:T(8,128)S(1)} %get-tuple-element.109), channel_id=1, source_target_pairs={{0,12},{4,0},{8,4},{12,8},{1,13},{5,1},{9,5},{13,9},{2,14},{6,2},{... | collective-permute-start | bytes 294920 | tf_op jit(solution)/shard_map/ppermute | solution.py:311
  124.7 4.1 %shard_map.78 = (f32[32,768]{1,0:T(8,128)S(1)}, f32[32,768]{1,0:T(8,128)S(1)}, f32[32,768]{1,0:T(8,128)S(1)}, f32[32,768]{1,0:T(8,128)S(1)}) custom-call(s32[4]{0:T(128)S(1)} %fusion.13.refs_0_.place_ref, f32[32,3072]{1,0:T(8,128)S(1)} %fusion.4.refs_0_, f32[32,3072]{1,0:T(8,128)S(1)} %collective-permute-done.15.refs_1_, ...), custom_call_target="tpu_custom_call" | custom-call | flops 1048576 | bytes 262144 | tf_op jit(solution)/shard_map/pallas_call | solution.py:286
  130.9 2.8 %collective-permute-start.25 = (f32[32,768]{1,0:T(8,128)S(1)}, f32[32,768]{1,0:T(8,128)S(1)}, u32[]{:S(2)}, u32[]{:S(2)}) collective-permute-start(f32[32,768]{1,0:T(8,128)S(1)} %get-tuple-element.113), channel_id=1, source_target_pairs={{0,12},{4,0},{8,4},{12,8},{1,13},{5,1},{9,5},{13,9},{2,14},{6,2},{... | collective-permute-start | bytes 294920 | tf_op jit(solution)/shard_map/ppermute | solution.py:311
  133.8 2.5 %collective-permute-done.27 = f32[32,768]{1,0:T(8,128)S(1)} collective-permute-done((f32[32,768]{1,0:T(8,128)S(1)}, f32[32,768]{1,0:T(8,128)S(1)}, u32[]{:S(2)}, u32[]{:S(2)}) %collective-permute-start.27) | collective-permute-done | bytes 98336 | tf_op jit(solution)/shard_map/ppermute | solution.py:311
  136.3 3.5 %collective-permute-done.26 = f32[32,768]{1,0:T(8,128)S(1)} collective-permute-done((f32[32,768]{1,0:T(8,128)S(1)}, f32[32,768]{1,0:T(8,128)S(1)}, u32[]{:S(2)}, u32[]{:S(2)}) %collective-permute-start.26) | collective-permute-done | bytes 98336 | tf_op jit(solution)/shard_map/ppermute | solution.py:311
  140.0 5.7 %psum.7 = f32[2,32]{1,0:T(2,128)S(1)} all-reduce(f32[2,32]{1,0:T(2,128)S(1)} %pad_maximum_fusion), channel_id=1, replica_groups=mesh['groups'=2,'hid'=4,'emb'=4] {'emb'}, use_global_device_ids=true, to_apply=%region_2.3 | all-reduce | flops 64 | bytes 512 | tf_op jit(solution)/shard_map/psum | solution.py:406
  (71 shorter events, 14.5 us)
Async XLA Ops:
  0.0 16.5 %collective-permute-start.1 = (f32[32,1536]{1,0:T(8,128)}, f32[32,1536]{1,0:T(8,128)S(1)}, u32[]{:S(2)}, u32[]{:S(2)}) collective-permute-start(f32[32,1536]{1,0:T(8,128)} %refs_1_.3), channel_id=1, source_target_pairs={{0,4},{4,8},{8,12},{12,0},{1,5},{5,9},{9,13},{13,1},{2,6},{6,10},{... | collective-permute-start | bytes 589832 | tf_op jit(solution)/shard_map/ppermute | solution.py:311
  3.0 15.7 %collective-permute-start.2 = (f32[32,1536]{1,0:T(8,128)}, f32[32,1536]{1,0:T(8,128)S(1)}, u32[]{:S(2)}, u32[]{:S(2)}) collective-permute-start(f32[32,1536]{1,0:T(8,128)} %refs_1_.3), channel_id=1, source_target_pairs={{0,8},{4,12},{8,0},{12,4},{1,9},{5,13},{9,1},{13,5},{2,10},{6,14},... | collective-permute-start | bytes 589832 | tf_op jit(solution)/shard_map/ppermute | solution.py:311
  5.6 13.1 %collective-permute-start.3 = (f32[32,1536]{1,0:T(8,128)}, f32[32,1536]{1,0:T(8,128)S(1)}, u32[]{:S(2)}, u32[]{:S(2)}) collective-permute-start(f32[32,1536]{1,0:T(8,128)} %refs_1_.3), channel_id=1, source_target_pairs={{0,12},{4,0},{8,4},{12,8},{1,13},{5,1},{9,5},{13,9},{2,14},{6,2},{... | collective-permute-start | bytes 589832 | tf_op jit(solution)/shard_map/ppermute | solution.py:311
  8.1 8.5 %collective-permute-start = (f32[64,128]{1,0:T(8,128)S(1)}, f32[64,128]{1,0:T(8,128)S(1)}, u32[]{:S(2)}, u32[]{:S(2)}) collective-permute-start(f32[64,128]{1,0:T(8,128)S(1)} %shard_map.64.refs_1_.refs_0_), channel_id=1, source_target_pairs={{0,1},{1,0},{2,3},{3,2},{4,5},{5,4},{6,7},{7,6},{8,9},{9,8},{10,11... | collective-permute-start | bytes 98312 | tf_op jit(solution)/shard_map/ppermute | solution.py:314
  16.5 3.7 %copy-start.3 = (f32[1536]{0:T(1024)S(1)}, f32[1536]{0:T(1024)}, u32[]{:S(2)}) copy-start(f32[1536]{0:T(1024)} %param.11) | copy-start | bytes 18436
  18.7 5.8 %collective-permute-start.4 = (f32[64,128]{1,0:T(8,128)S(1)}, f32[64,128]{1,0:T(8,128)S(1)}, u32[]{:S(2)}, u32[]{:S(2)}) collective-permute-start(f32[64,128]{1,0:T(8,128)S(1)} %shard_map.67.refs_0_.refs_2_), channel_id=1, source_target_pairs={{0,2},{1,3},{2,0},{3,1},{4,6},{5,7},{6,4},{7,5},{8,10},{9,11},{10,... | collective-permute-start | bytes 98312 | tf_op jit(solution)/shard_map/ppermute | solution.py:317
  20.3 4.3 %copy-start.2 = (f32[32,1536]{1,0:T(8,128)S(1)}, f32[32,1536]{1,0:T(8,128)}, u32[]{:S(2)}) copy-start(f32[32,1536]{1,0:T(8,128)} %refs_0_.3) | copy-start | bytes 589828
  24.5 6.0 %copy-start = (f32[32,1536]{1,0:T(8,128)S(1)}, f32[32,1536]{1,0:T(8,128)}, u32[]{:S(2)}) copy-start(f32[32,1536]{1,0:T(8,128)} %refs_1_.3) | copy-start | bytes 589828
  24.7 15.0 %collective-permute-start.5 = (f32[32,1536]{1,0:T(8,128)S(1)}, f32[32,1536]{1,0:T(8,128)S(1)}, u32[]{:S(2)}, u32[]{:S(2)}) collective-permute-start(f32[32,1536]{1,0:T(8,128)S(1)} %get-tuple-element.74.refs_6_.refs_1_), channel_id=1, source_target_pairs={{0,4},{4,8},{8,12},{12,0},{1,5},{5,9},{9,13},{13,1},{2,6},{6,10},{... | collective-permute-start | bytes 589832 | tf_op jit(solution)/shard_map/ppermute | solution.py:311
  29.4 10.3 %collective-permute-start.6 = (f32[32,1536]{1,0:T(8,128)S(1)}, f32[32,1536]{1,0:T(8,128)S(1)}, u32[]{:S(2)}, u32[]{:S(2)}) collective-permute-start(f32[32,1536]{1,0:T(8,128)S(1)} %get-tuple-element.74.refs_6_.refs_1_), channel_id=1, source_target_pairs={{0,12},{4,0},{8,4},{12,8},{1,13},{5,1},{9,5},{13,9},{2,14},{6,2},{... | collective-permute-start | bytes 589832 | tf_op jit(solution)/shard_map/ppermute | solution.py:311
  39.7 2.4 %collective-permute-start.7 = (f32[64,3072]{1,0:T(8,128)S(1)}, f32[64,3072]{1,0:T(8,128)S(1)}, u32[]{:S(2)}, u32[]{:S(2)}) collective-permute-start(f32[64,3072]{1,0:T(8,128)S(1)} %get-tuple-element.69), channel_id=1, source_target_pairs={{0,1},{1,0},{2,3},{3,2},{4,5},{5,4},{6,7},{7,6},{8,9},{9,8},{10,11... | collective-permute-start | bytes 2359304 | tf_op jit(solution)/shard_map/ppermute | solution.py:314
  42.2 12.4 %collective-permute-start.8 = (f32[32,3072]{1,0:T(8,128)S(1)}, f32[32,3072]{1,0:T(8,128)S(1)}, u32[]{:S(2)}, u32[]{:S(2)}) collective-permute-start(f32[32,3072]{1,0:T(8,128)S(1)} %get-tuple-element.122), channel_id=1, source_target_pairs={{0,2},{1,3},{2,0},{3,1},{4,6},{5,7},{6,4},{7,5},{8,10},{9,11},{10,... | collective-permute-start | bytes 1179656 | tf_op jit(solution)/shard_map/ppermute | solution.py:317
  42.8 11.8 %collective-permute-start.9 = (f32[32,1536]{1,0:T(8,128)S(1)}, f32[32,1536]{1,0:T(8,128)S(1)}, u32[]{:S(2)}, u32[]{:S(2)}) collective-permute-start(f32[32,1536]{1,0:T(8,128)S(1)} %get-tuple-element.74.refs_6_.refs_1_), channel_id=1, source_target_pairs={{0,8},{4,12},{8,0},{12,4},{1,9},{5,13},{9,1},{13,5},{2,10},{6,14},... | collective-permute-start | bytes 589832 | tf_op jit(solution)/shard_map/ppermute | solution.py:311
  54.6 4.2 %collective-permute-start.10 = (f32[64,3072]{1,0:T(8,128)S(1)}, f32[64,3072]{1,0:T(8,128)S(1)}, u32[]{:S(2)}, u32[]{:S(2)}) collective-permute-start(f32[64,3072]{1,0:T(8,128)S(1)} %get-tuple-element.81.refs_0_), channel_id=1, source_target_pairs={{0,1},{1,0},{2,3},{3,2},{4,5},{5,4},{6,7},{7,6},{8,9},{9,8},{10,11... | collective-permute-start | bytes 2359304 | tf_op jit(solution)/shard_map/ppermute | solution.py:314
  59.0 11.6 %collective-permute-start.11 = (f32[32,3072]{1,0:T(8,128)S(1)}, f32[32,3072]{1,0:T(8,128)S(1)}, u32[]{:S(2)}, u32[]{:S(2)}) collective-permute-start(f32[32,3072]{1,0:T(8,128)S(1)} %get-tuple-element.120), channel_id=1, source_target_pairs={{0,2},{1,3},{2,0},{3,1},{4,6},{5,7},{6,4},{7,5},{8,10},{9,11},{10,... | collective-permute-start | bytes 1179656 | tf_op jit(solution)/shard_map/ppermute | solution.py:317
  70.6 3.0 %collective-permute-start.12 = (f32[64,3072]{1,0:T(8,128)S(1)}, f32[64,3072]{1,0:T(8,128)S(1)}, u32[]{:S(2)}, u32[]{:S(2)}) collective-permute-start(f32[64,3072]{1,0:T(8,128)S(1)} %get-tuple-element.93), channel_id=1, source_target_pairs={{0,1},{1,0},{2,3},{3,2},{4,5},{5,4},{6,7},{7,6},{8,9},{9,8},{10,11... | collective-permute-start | bytes 2359304 | tf_op jit(solution)/shard_map/ppermute | solution.py:314
  73.7 11.6 %collective-permute-start.16 = (f32[32,3072]{1,0:T(8,128)S(1)}, f32[32,3072]{1,0:T(8,128)S(1)}, u32[]{:S(2)}, u32[]{:S(2)}) collective-permute-start(f32[32,3072]{1,0:T(8,128)S(1)} %slice.52), channel_id=1, source_target_pairs={{0,2},{1,3},{2,0},{3,1},{4,6},{5,7},{6,4},{7,5},{8,10},{9,11},{10,... | collective-permute-start | bytes 1179656 | tf_op jit(solution)/shard_map/ppermute | solution.py:317
  75.3 3.4 %copy-start.4 = (f32[6144]{0:T(1024)S(1)}, f32[6144]{0:T(1024)}, u32[]{:S(2)}) copy-start(f32[6144]{0:T(1024)} %param.9) | copy-start | bytes 73732
  78.3 8.8 %collective-permute-start.13 = (f32[64,3072]{1,0:T(8,128)S(1)}, f32[64,3072]{1,0:T(8,128)S(1)}, u32[]{:S(2)}, u32[]{:S(2)}) collective-permute-start(f32[64,3072]{1,0:T(8,128)S(1)} %get-tuple-element.96), channel_id=1, source_target_pairs={{0,1},{1,0},{2,3},{3,2},{4,5},{5,4},{6,7},{7,6},{8,9},{9,8},{10,11... | collective-permute-start | bytes 2359304 | tf_op jit(solution)/shard_map/ppermute | solution.py:314
  85.5 12.1 %collective-permute-start.17 = (f32[32,3072]{1,0:T(8,128)S(1)}, f32[32,3072]{1,0:T(8,128)S(1)}, u32[]{:S(2)}, u32[]{:S(2)}) collective-permute-start(f32[32,3072]{1,0:T(8,128)S(1)} %fusion.9.refs_0_), channel_id=1, source_target_pairs={{0,2},{1,3},{2,0},{3,1},{4,6},{5,7},{6,4},{7,5},{8,10},{9,11},{10,... | collective-permute-start | bytes 1179656 | tf_op jit(solution)/shard_map/ppermute | solution.py:317
  87.2 17.5 %collective-permute-start.14 = (f32[32,3072]{1,0:T(8,128)S(1)}, f32[32,3072]{1,0:T(8,128)S(1)}, u32[]{:S(2)}, u32[]{:S(2)}) collective-permute-start(f32[32,3072]{1,0:T(8,128)S(1)} %slice.50), channel_id=1, source_target_pairs={{0,2},{1,3},{2,0},{3,1},{4,6},{5,7},{6,4},{7,5},{8,10},{9,11},{10,... | collective-permute-start | bytes 1179656 | tf_op jit(solution)/shard_map/ppermute | solution.py:317
  87.8 18.8 %collective-permute-start.18 = (f32[32,3072]{1,0:T(8,128)S(1)}, f32[32,3072]{1,0:T(8,128)S(1)}, u32[]{:S(2)}, u32[]{:S(2)}) collective-permute-start(f32[32,3072]{1,0:T(8,128)S(1)} %fusion.9.refs_0_), channel_id=1, source_target_pairs={{0,1},{1,0},{2,3},{3,2},{4,5},{5,4},{6,7},{7,6},{8,9},{9,8},{10,11... | collective-permute-start | bytes 1179656 | tf_op jit(solution)/shard_map/ppermute | solution.py:314
  97.6 9.0 %collective-permute-start.19 = (f32[32,3072]{1,0:T(8,128)S(1)}, f32[32,3072]{1,0:T(8,128)S(1)}, u32[]{:S(2)}, u32[]{:S(2)}) collective-permute-start(f32[32,3072]{1,0:T(8,128)S(1)} %collective-permute-done.17.refs_1_), channel_id=1, source_target_pairs={{0,1},{1,0},{2,3},{3,2},{4,5},{5,4},{6,7},{7,6},{8,9},{9,8},{10,11... | collective-permute-start | bytes 1179656 | tf_op jit(solution)/shard_map/ppermute | solution.py:314
  105.0 9.9 %collective-permute-start.15 = (f32[32,3072]{1,0:T(8,128)S(1)}, f32[32,3072]{1,0:T(8,128)S(1)}, u32[]{:S(2)}, u32[]{:S(2)}) collective-permute-start(f32[32,3072]{1,0:T(8,128)S(1)} %fusion.4.refs_0_), channel_id=1, source_target_pairs={{0,2},{1,3},{2,0},{3,1},{4,6},{5,7},{6,4},{7,5},{8,10},{9,11},{10,... | collective-permute-start | bytes 1179656 | tf_op jit(solution)/shard_map/ppermute | solution.py:317
  106.6 8.3 %collective-permute-start.20 = (f32[32,3072]{1,0:T(8,128)S(1)}, f32[32,3072]{1,0:T(8,128)S(1)}, u32[]{:S(2)}, u32[]{:S(2)}) collective-permute-start(f32[32,3072]{1,0:T(8,128)S(1)} %fusion.4.refs_0_), channel_id=1, source_target_pairs={{0,1},{1,0},{2,3},{3,2},{4,5},{5,4},{6,7},{7,6},{8,9},{9,8},{10,11... | collective-permute-start | bytes 1179656 | tf_op jit(solution)/shard_map/ppermute | solution.py:314
  114.9 1.7 %collective-permute-start.21 = (f32[32,3072]{1,0:T(8,128)S(1)}, f32[32,3072]{1,0:T(8,128)S(1)}, u32[]{:S(2)}, u32[]{:S(2)}) collective-permute-start(f32[32,3072]{1,0:T(8,128)S(1)} %collective-permute-done.15.refs_1_), channel_id=1, source_target_pairs={{0,1},{1,0},{2,3},{3,2},{4,5},{5,4},{6,7},{7,6},{8,9},{9,8},{10,11... | collective-permute-start | bytes 1179656 | tf_op jit(solution)/shard_map/ppermute | solution.py:314
  120.7 10.2 %collective-permute-start.24 = (f32[32,768]{1,0:T(8,128)S(1)}, f32[32,768]{1,0:T(8,128)S(1)}, u32[]{:S(2)}, u32[]{:S(2)}) collective-permute-start(f32[32,768]{1,0:T(8,128)S(1)} %get-tuple-element.111), channel_id=1, source_target_pairs={{0,4},{4,8},{8,12},{12,0},{1,5},{5,9},{9,13},{13,1},{2,6},{6,10},{... | collective-permute-start | bytes 294920 | tf_op jit(solution)/shard_map/ppermute | solution.py:311
  121.0 12.8 %collective-permute-start.23 = (f32[32,768]{1,0:T(8,128)S(1)}, f32[32,768]{1,0:T(8,128)S(1)}, u32[]{:S(2)}, u32[]{:S(2)}) collective-permute-start(f32[32,768]{1,0:T(8,128)S(1)} %get-tuple-element.110), channel_id=1, source_target_pairs={{0,8},{4,12},{8,0},{12,4},{1,9},{5,13},{9,1},{13,5},{2,10},{6,14},... | collective-permute-start | bytes 294920 | tf_op jit(solution)/shard_map/ppermute | solution.py:311
  122.7 11.0 %collective-permute-start.22 = (f32[32,768]{1,0:T(8,128)S(1)}, f32[32,768]{1,0:T(8,128)S(1)}, u32[]{:S(2)}, u32[]{:S(2)}) collective-permute-start(f32[32,768]{1,0:T(8,128)S(1)} %get-tuple-element.109), channel_id=1, source_target_pairs={{0,12},{4,0},{8,4},{12,8},{1,13},{5,1},{9,5},{13,9},{2,14},{6,2},{... | collective-permute-start | bytes 294920 | tf_op jit(solution)/shard_map/ppermute | solution.py:311
  128.7 7.6 %collective-permute-start.27 = (f32[32,768]{1,0:T(8,128)S(1)}, f32[32,768]{1,0:T(8,128)S(1)}, u32[]{:S(2)}, u32[]{:S(2)}) collective-permute-start(f32[32,768]{1,0:T(8,128)S(1)} %get-tuple-element.115), channel_id=1, source_target_pairs={{0,4},{4,8},{8,12},{12,0},{1,5},{5,9},{9,13},{13,1},{2,6},{6,10},{... | collective-permute-start | bytes 294920 | tf_op jit(solution)/shard_map/ppermute | solution.py:311
  129.3 10.5 %collective-permute-start.26 = (f32[32,768]{1,0:T(8,128)S(1)}, f32[32,768]{1,0:T(8,128)S(1)}, u32[]{:S(2)}, u32[]{:S(2)}) collective-permute-start(f32[32,768]{1,0:T(8,128)S(1)} %get-tuple-element.114), channel_id=1, source_target_pairs={{0,8},{4,12},{8,0},{12,4},{1,9},{5,13},{9,1},{13,5},{2,10},{6,14},... | collective-permute-start | bytes 294920 | tf_op jit(solution)/shard_map/ppermute | solution.py:311
  130.9 9.0 %collective-permute-start.25 = (f32[32,768]{1,0:T(8,128)S(1)}, f32[32,768]{1,0:T(8,128)S(1)}, u32[]{:S(2)}, u32[]{:S(2)}) collective-permute-start(f32[32,768]{1,0:T(8,128)S(1)} %get-tuple-element.113), channel_id=1, source_target_pairs={{0,12},{4,0},{8,4},{12,8},{1,13},{5,1},{9,5},{13,9},{2,14},{6,2},{... | collective-permute-start | bytes 294920 | tf_op jit(solution)/shard_map/ppermute | solution.py:311
  (1 other events, 0.9 us)

commit v9 on v8

--- a/solution.py
+++ b/solution.py
@@ -330,15 +330,16 @@
         return lax.optimization_barrier((values, others))
 
     def halved(partial, behind=()):
-        send, keep = partial
-        return keep + tied(other_core(send), behind)[0]
-
-    def exchanged(summed):
-        terms = [summed[d * tokens : (d + 1) * tokens] for d in range(chips)]
-        arrival = next_chip(terms[chips - 1])
-        for step in range(2, chips):
-            arrival = next_chip(arrival + terms[chips - step])
-        return arrival, terms[0]
+        (send_own, send), (keep_own, keep) = [(rows[:tokens], rows[tokens:]) for rows in partial]
+        return keep + tied(other_core(send), behind)[0], (keep_own, other_core(send_own))
+
+    def exchanged(half):
+        summed, own = half
+        terms = [summed[d * tokens : (d + 1) * tokens] for d in range(chips - 1)]
+        arrival = next_chip(terms[chips - 2])
+        for step in range(chips - 3, -1, -1):
+            arrival = next_chip(arrival + terms[step])
+        return arrival, *own
 
     def prepared(c, after):
         return prepare(in_weight, (0, depth), (c * quarter, quarter), after)
@@ -364,22 +365,22 @@
     back_0 = stream(grads, out_weight, place, 0, piece, (), [scaled[0]])
     back_0, (scaled[1], scaled[-1]) = tied(back_0, (scaled[1], scaled[-1]))
     half_0 = halved(back_0)
-    back_1 = stream(grads, out_weight, place, piece, piece, (), [half_0])
+    back_1 = stream(grads, out_weight, place, piece, piece, (), [half_0[0]])
     back_0 = exchanged(half_0)
     back_1, (back_0, scaled) = tied(back_1, (back_0, scaled))
     in_parts += prepared(3, [back_1[0]])
     half_1 = halved(back_1, in_parts[6])
     back_1 = exchanged(half_1)
-    pre_0 = forward(scaled, in_parts[:4], place, (), [half_1])
-    pre_0, back_1 = tied(pre_0, back_1)
-    pre_1 = forward(scaled, in_parts[4:6], place, (), [pre_0[1]])
+    pre_0 = forward(scaled, in_parts[:4], place, (), [half_1[0]])
+    pre_1 = forward(scaled, in_parts[4:6], place, (), [pre_0[1], back_1[0]])
     half_0 = halved(pre_0, pre_1)
-    pre_1 = forward(scaled, in_parts[6:], place, pre_1, [half_0])
-    backs = [back_0, back_1]
-    pres = [exchanged(half_0), exchanged(halved(pre_1))]
-
-    def spread_out(c):
-        act = sum(backs[c]) * gelu_slope(sum(pres[c]) + in_bias[c * piece : (c + 1) * piece])
+    pre_1 = forward(scaled, in_parts[6:], place, pre_1, [half_0[0]])
+    pre_0 = exchanged(half_0)
+
+    def slope_product(c, back, pre):
+        return sum(back) * gelu_slope(sum(pre) + in_bias[c * piece : (c + 1) * piece])
+
+    def spread_out(act):
         mine = [None] * chips
         mine[0] = act
         for step in range(1, chips):
@@ -387,13 +388,17 @@
             mine[(chips - step) % chips] = act
         return mine
 
+    act_0 = slope_product(0, back_0, pre_0)
+    pre_1 = exchanged(halved(pre_1, act_0))
+    act_1 = slope_product(1, back_1, pre_1)
+
     def both_cores(mine):
         return mine + [other_core(block) for block in mine]
 
     def summed_along_hid(sums):
         return sum([along_hid(sums[step], -step) for step in range(1, hid_size)], start=sums[0])
 
-    acts_0, acts_1 = spread_out(0), spread_out(1)
+    acts_0, acts_1 = spread_out(act_0), spread_out(act_1)
     sums = backward(both_cores(acts_0), in_parts[:4], place, (), 0, 1, [pre_1[1]])
     acts_1[1:], sums = tied(acts_1[1:], sums)
     acts_1 = both_cores(acts_1)

time: 147 us -> 144 us (0.980)
  waiting for transfers between devices: 43.7 us -> 40.9 us
    ppermute x7, waiting for transfers between devices: 29.3 us -> 25.5 us  [next_chip(): lax.ppermute(values, 'emb', [(i, (i + 2) % emb_size) for i in range(emb_s...]
    ppermute x12, waiting for transfers between devices: 10.4 us -> 12.8 us  [along_hid(): lax.ppermute(values, 'hid', [(i, (i + steps) % hid_size) for i in range(h...]
    ppermute x9 -> x13, starting transfers between devices: 0.39 us -> 2.47 us  [other_core(): return lax.ppermute(values, 'emb', [(i, i ^ 1) for i in range(emb_size)])]
    ppermute x12, starting transfers between devices: 22.2 us -> 20.4 us  [along_hid(): lax.ppermute(values, 'hid', [(i, (i + steps) % hid_size) for i in range(h...]
    ppermute x9 -> x13, waiting for transfers between devices: 4.01 us -> 2.59 us  [other_core(): return lax.ppermute(values, 'emb', [(i, i ^ 1) for i in range(emb_size)])]
  transfers between devices with their start and end apart: 28 -> 32, of which waited for: 11 -> 12; matrix products, arithmetic and copies ran while one was open for 0% -> 1% of each run, Pallas kernels for 40% -> 40%
where the time goes in v9:
time: 144 us
  Pallas kernels  62.2 us (43%)
  waiting for transfers between devices  40.9 us (28%)
  starting transfers between devices  31.8 us (22%)
  blocking collectives  5.93 us (4%)
  other arithmetic  1.74 us (1%)
    ppermute x7, waiting for transfers between devices, next_chip(): lax.ppermute(values, 'emb', [(i, (i + 2) % emb_size) for i in range(emb_s...  25.5 us
    ppermute x12, starting transfers between devices, along_hid(): lax.ppermute(values, 'hid', [(i, (i + steps) % hid_size) for i in range(h...  20.4 us
    pallas_call x2, Pallas kernels, stream(): pl.pallas_call(lambda *refs: stream_kernel(first, depth, refs[0], refs[1:...  18.3 us
    pallas_call x4, Pallas kernels, prepare(): pl.pallas_call(functools.partial(prepare_kernel, rows, columns, block, de...  16.8 us
    pallas_call x3, Pallas kernels, backward(): pl.pallas_call(functools.partial(backward_kernel, slots, len(weights) //...  15.4 us
    ppermute x12, waiting for transfers between devices, along_hid(): lax.ppermute(values, 'hid', [(i, (i + steps) % hid_size) for i in range(h...  12.8 us
    pallas_call x3, Pallas kernels, forward(): pl.pallas_call(lambda *refs: forward_kernel(refs[0], refs[1:ends[0]], ref...  11.4 us
    ppermute x7, starting transfers between devices, next_chip(): lax.ppermute(values, 'emb', [(i, (i + 2) % emb_size) for i in range(emb_s...  8.95 us
  transfers between devices with their start and end apart: 32, of which 12 were waited for; matrix products, arithmetic and copies ran while one was open for 1% of the time, Pallas kernels for 40%

profile of v9, /device:TPU:0, one launch (start us, length us, event | category | flops | bytes accessed | tf_op | source)
XLA Modules:
  0.0 144.3 jit_solution(3591187868895113381)
XLA Ops:
  0.0 3.0 %collective-permute-start.1 = (f32[32,1536]{1,0:T(8,128)}, f32[32,1536]{1,0:T(8,128)S(1)}, u32[]{:S(2)}, u32[]{:S(2)}) collective-permute-start(f32[32,1536]{1,0:T(8,128)} %refs_1_.3), channel_id=1, source_target_pairs={{0,4},{4,8},{8,12},{12,0},{1,5},{5,9},{9,13},{13,1},{2,6},{6,10},{... | collective-permute-start | bytes 589832 | tf_op jit(solution)/shard_map/ppermute | solution.py:311
  3.0 2.6 %collective-permute-start.2 = (f32[32,1536]{1,0:T(8,128)}, f32[32,1536]{1,0:T(8,128)S(1)}, u32[]{:S(2)}, u32[]{:S(2)}) collective-permute-start(f32[32,1536]{1,0:T(8,128)} %refs_1_.3), channel_id=1, source_target_pairs={{0,8},{4,12},{8,0},{12,4},{1,9},{5,13},{9,1},{13,5},{2,10},{6,14},... | collective-permute-start | bytes 589832 | tf_op jit(solution)/shard_map/ppermute | solution.py:311
  5.6 1.3 collective-permute-start.3
  8.1 4.2 %shard_map.65 = (bf16[1536,1536]{1,0:T(8,128)(2,1)S(1)}, bf16[1536,1536]{1,0:T(8,128)(2,1)S(1)}) custom-call(f32[1536,6144]{1,0:T(8,128)} %weight_ref.7, s32[4]{0:T(128)S(1)} %fusion.11.refs_0_.place_ref, f32[64,128]{1,0:T(8,128)S(1)} %shard_map.64.refs_1_.refs_0_), custom_call_target="tpu_custom_call" | custom-call | flops 1048576 | bytes 262144 | tf_op jit(solution)/shard_map/pallas_call | solution.py:111
  12.3 4.2 %shard_map.66 = (bf16[1536,1536]{1,0:T(8,128)(2,1)S(1)}, bf16[1536,1536]{1,0:T(8,128)(2,1)S(1)}) custom-call(f32[1536,6144]{1,0:T(8,128)} %weight_ref.7, bf16[1536,1536]{1,0:T(8,128)(2,1)S(1)} %get-tuple-element.59.refs_0_.refs_5_.refs_4_), custom_call_target="tpu_custom_call" | custom-call | flops 1048576 | bytes 262144 | tf_op jit(solution)/shard_map/pallas_call | solution.py:111
  16.6 2.1 %collective-permute-done.2.refs_4_.refs_3_ = f32[32,1536]{1,0:T(8,128)S(1)} collective-permute-done((f32[32,1536]{1,0:T(8,128)}, f32[32,1536]{1,0:T(8,128)S(1)}, u32[]{:S(2)}, u32[]{:S(2)}) %collective-permute-start.2) | collective-permute-done | bytes 196640 | tf_op jit(solution)/shard_map/ppermute | solution.py:311
  18.7 1.5 %collective-permute-start.4 = (f32[64,128]{1,0:T(8,128)S(1)}, f32[64,128]{1,0:T(8,128)S(1)}, u32[]{:S(2)}, u32[]{:S(2)}) collective-permute-start(f32[64,128]{1,0:T(8,128)S(1)} %shard_map.67.refs_0_.refs_2_), channel_id=1, source_target_pairs={{0,2},{1,3},{2,0},{3,1},{4,6},{5,7},{6,4},{7,5},{8,10},{9,11},{10,... | collective-permute-start | bytes 98312 | tf_op jit(solution)/shard_map/ppermute | solution.py:317
  20.3 4.2 %shard_map.68 = (bf16[1536,1536]{1,0:T(8,128)(2,1)S(1)}, bf16[1536,1536]{1,0:T(8,128)(2,1)S(1)}) custom-call(f32[1536,6144]{1,0:T(8,128)} %weight_ref.7, f32[64,128]{1,0:T(8,128)S(1)} %shard_map.67.refs_0_.refs_2_), custom_call_target="tpu_custom_call" | custom-call | flops 1048576 | bytes 262144 | tf_op jit(solution)/shard_map/pallas_call | solution.py:111
  24.7 4.7 %collective-permute-start.5 = (f32[32,1536]{1,0:T(8,128)S(1)}, f32[32,1536]{1,0:T(8,128)S(1)}, u32[]{:S(2)}, u32[]{:S(2)}) collective-permute-start(f32[32,1536]{1,0:T(8,128)S(1)} %get-tuple-element.76.refs_6_.refs_1_), channel_id=1, source_target_pairs={{0,4},{4,8},{8,12},{12,0},{1,5},{5,9},{9,13},{13,1},{2,6},{6,10},{... | collective-permute-start | bytes 589832 | tf_op jit(solution)/shard_map/ppermute | solution.py:311
  30.5 9.2 %shard_map.70 = (f32[64,3072]{1,0:T(8,128)S(1)}, f32[64,3072]{1,0:T(8,128)S(1)}) custom-call(s32[4]{0:T(128)S(1)} %fusion.11.refs_0_.place_ref, f32[32,1536]{1,0:T(8,128)S(1)} %copy-done, f32[32,1536]{1,0:T(8,128)S(1)} %collective-permute-done.1.refs_3_.refs_2_, f32[32,1536]{1,0:T(8,128)S(1)} %collective-permute-done.2.refs_4_.refs_3_, ...), custom_call_target="tpu_custom_call" | custom-call | flops 1048576 | bytes 262144 | tf_op jit(solution)/shard_map/pallas_call | solution.py:226
  42.7 9.2 %shard_map.71 = (f32[64,3072]{1,0:T(8,128)S(1)}, f32[64,3072]{1,0:T(8,128)S(1)}) custom-call(s32[4]{0:T(128)S(1)} %fusion.11.refs_0_.place_ref, f32[32,1536]{1,0:T(8,128)S(1)} %copy-done, f32[32,1536]{1,0:T(8,128)S(1)} %collective-permute-done.1.refs_3_.refs_2_, f32[32,1536]{1,0:T(8,128)S(1)} %collective-permute-done.2.refs_4_.refs_3_, ...), custom_call_target="tpu_custom_call" | custom-call | flops 1048576 | bytes 262144 | tf_op jit(solution)/shard_map/pallas_call | solution.py:226
  51.9 2.1 %collective-permute-done.10.refs_3_ = f32[32,1536]{1,0:T(8,128)S(1)} collective-permute-done((f32[32,1536]{1,0:T(8,128)S(1)}, f32[32,1536]{1,0:T(8,128)S(1)}, u32[]{:S(2)}, u32[]{:S(2)}) %collective-permute-start.10) | collective-permute-done | bytes 196640 | tf_op jit(solution)/shard_map/ppermute | solution.py:311
  54.2 4.2 %shard_map.72 = (bf16[1536,1536]{1,0:T(8,128)(2,1)S(1)}, bf16[1536,1536]{1,0:T(8,128)(2,1)S(1)}) custom-call(f32[1536,6144]{1,0:T(8,128)} %weight_ref.7, f32[64,3072]{1,0:T(8,128)S(1)} %get-tuple-element.73.refs_0_), custom_call_target="tpu_custom_call" | custom-call | flops 1048576 | bytes 262144 | tf_op jit(solution)/shard_map/pallas_call | solution.py:111
  58.4 1.6 %collective-permute-start.12 = (f32[32,3072]{1,0:T(8,128)S(1)}, f32[32,3072]{1,0:T(8,128)S(1)}, u32[]{:S(2)}, u32[]{:S(2)}) collective-permute-start(f32[32,3072]{1,0:T(8,128)S(1)} %slice_add_fusion.2.refs_9_), channel_id=1, source_target_pairs={{0,2},{1,3},{2,0},{3,1},{4,6},{5,7},{6,4},{7,5},{8,10},{9,11},{10,... | collective-permute-start | bytes 1179656 | tf_op jit(solution)/shard_map/ppermute | solution.py:317
  60.0 5.4 %shard_map.73 = (f32[64,3072]{1,0:T(8,128)S(1)}, f32[64,3072]{1,0:T(8,128)S(1)}) custom-call(s32[4]{0:T(128)S(1)} %fusion.11.refs_0_.place_ref, f32[32,1536]{1,0:T(8,128)S(1)} %get-tuple-element.76.refs_6_.refs_1_, f32[32,1536]{1,0:T(8,128)S(1)} %collective-permute-done.5.refs_2_, f32[32,1536]{1,0:T(8,128)S(1)} %collective-permute-done.10.refs_3_, ...), custom_call_target="tpu_custom_call" | custom-call | flops 1048576 | bytes 262144 | tf_op jit(solution)/shard_map/pallas_call | solution.py:178
  66.2 3.8 %collective-permute-done.12.refs_8_ = f32[32,3072]{1,0:T(8,128)S(1)} collective-permute-done((f32[32,3072]{1,0:T(8,128)S(1)}, f32[32,3072]{1,0:T(8,128)S(1)}, u32[]{:S(2)}, u32[]{:S(2)}) %collective-permute-start.12) | collective-permute-done | bytes 393248 | tf_op jit(solution)/shard_map/ppermute | solution.py:317
  70.0 3.0 %shard_map.74 = (f32[64,1536]{1,0:T(8,128)S(1)}, f32[64,1536]{1,0:T(8,128)S(1)}) custom-call(s32[4]{0:T(128)S(1)} %fusion.11.refs_0_.place_ref, f32[32,1536]{1,0:T(8,128)S(1)} %get-tuple-element.76.refs_6_.refs_1_, f32[32,1536]{1,0:T(8,128)S(1)} %collective-permute-done.5.refs_2_, f32[32,1536]{1,0:T(8,128)S(1)} %collective-permute-done.10.refs_3_, ...), custom_call_target="tpu_custom_call" | custom-call | flops 1048576 | bytes 262144 | tf_op jit(solution)/shard_map/pallas_call | solution.py:178
  73.1 1.5 %collective-permute-start.16 = (f32[32,3072]{1,0:T(8,128)S(1)}, f32[32,3072]{1,0:T(8,128)S(1)}, u32[]{:S(2)}, u32[]{:S(2)}) collective-permute-start(f32[32,3072]{1,0:T(8,128)S(1)} %slice_add_fusion.1.refs_9_), channel_id=1, source_target_pairs={{0,2},{1,3},{2,0},{3,1},{4,6},{5,7},{6,4},{7,5},{8,10},{9,11},{10,... | collective-permute-start | bytes 1179656 | tf_op jit(solution)/shard_map/ppermute | solution.py:317
  74.6 3.0 %shard_map.75 = (f32[64,3072]{1,0:T(8,128)S(1)}, f32[64,3072]{1,0:T(8,128)S(1)}) custom-call(s32[4]{0:T(128)S(1)} %fusion.11.refs_0_.place_ref, f32[32,1536]{1,0:T(8,128)S(1)} %get-tuple-element.76.refs_6_.refs_1_, f32[32,1536]{1,0:T(8,128)S(1)} %collective-permute-done.5.refs_2_, f32[32,1536]{1,0:T(8,128)S(1)} %collective-permute-done.10.refs_3_, ...), custom_call_target="tpu_custom_call" | custom-call | flops 1048576 | bytes 262144 | tf_op jit(solution)/shard_map/pallas_call | solution.py:178
  78.3 5.5 %collective-permute-done.16 = f32[32,3072]{1,0:T(8,128)S(1)} collective-permute-done((f32[32,3072]{1,0:T(8,128)S(1)}, f32[32,3072]{1,0:T(8,128)S(1)}, u32[]{:S(2)}, u32[]{:S(2)}) %collective-permute-start.16) | collective-permute-done | bytes 393248 | tf_op jit(solution)/shard_map/ppermute | solution.py:317
  84.1 1.6 %collective-permute-start.21 = (f32[32,3072]{1,0:T(8,128)S(1)}, f32[32,3072]{1,0:T(8,128)S(1)}, u32[]{:S(2)}, u32[]{:S(2)}) collective-permute-start(f32[32,3072]{1,0:T(8,128)S(1)} %fusion.4.refs_0_), channel_id=1, source_target_pairs={{0,2},{1,3},{2,0},{3,1},{4,6},{5,7},{6,4},{7,5},{8,10},{9,11},{10,... | collective-permute-start | bytes 1179656 | tf_op jit(solution)/shard_map/ppermute | solution.py:317
  86.4 9.9 %collective-permute-done.21.refs_1_ = f32[32,3072]{1,0:T(8,128)S(1)} collective-permute-done((f32[32,3072]{1,0:T(8,128)S(1)}, f32[32,3072]{1,0:T(8,128)S(1)}, u32[]{:S(2)}, u32[]{:S(2)}) %collective-permute-start.21) | collective-permute-done | bytes 393248 | tf_op jit(solution)/shard_map/ppermute | solution.py:317
  96.3 6.2 %collective-permute-done.18 = f32[32,3072]{1,0:T(8,128)S(1)} collective-permute-done((f32[32,3072]{1,0:T(8,128)S(1)}, f32[32,3072]{1,0:T(8,128)S(1)}, u32[]{:S(2)}, u32[]{:S(2)}) %collective-permute-start.18) | collective-permute-done | bytes 393248 | tf_op jit(solution)/shard_map/ppermute | solution.py:317
  102.7 1.6 %collective-permute-start.20 = (f32[32,3072]{1,0:T(8,128)S(1)}, f32[32,3072]{1,0:T(8,128)S(1)}, u32[]{:S(2)}, u32[]{:S(2)}) collective-permute-start(f32[32,3072]{1,0:T(8,128)S(1)} %get-tuple-element.116.refs_0_), channel_id=1, source_target_pairs={{0,2},{1,3},{2,0},{3,1},{4,6},{5,7},{6,4},{7,5},{8,10},{9,11},{10,... | collective-permute-start | bytes 1179656 | tf_op jit(solution)/shard_map/ppermute | solution.py:317
  104.3 7.3 %shard_map.76 = (f32[32,1536]{1,0:T(8,128)S(1)}, f32[32,1536]{1,0:T(8,128)S(1)}, f32[32,1536]{1,0:T(8,128)S(1)}, f32[32,1536]{1,0:T(8,128)S(1)}) custom-call(s32[4]{0:T(128)S(1)} %fusion.11.refs_0_.place_ref, f32[32,3072]{1,0:T(8,128)S(1)} %fusion.4.refs_0_, f32[32,3072]{1,0:T(8,128)S(1)} %collective-permute-done.21.refs_1_, ...), custom_call_target="tpu_custom_call" | custom-call | flops 1048576 | bytes 262144 | tf_op jit(solution)/shard_map/pallas_call | solution.py:286
  113.5 4.1 %shard_map.77 = (f32[32,768]{1,0:T(8,128)S(1)}, f32[32,768]{1,0:T(8,128)S(1)}, f32[32,768]{1,0:T(8,128)S(1)}, f32[32,768]{1,0:T(8,128)S(1)}) custom-call(s32[4]{0:T(128)S(1)} %fusion.11.refs_0_.place_ref, f32[32,3072]{1,0:T(8,128)S(1)} %get-tuple-element.116.refs_0_, f32[32,3072]{1,0:T(8,128)S(1)} %collective-permute-done.20.refs_1_, ...), custom_call_target="tpu_custom_call" | custom-call | flops 1048576 | bytes 262144 | tf_op jit(solution)/shard_map/pallas_call | solution.py:286
  117.6 1.5 %collective-permute-start.26 = (f32[32,768]{1,0:T(8,128)S(1)}, f32[32,768]{1,0:T(8,128)S(1)}, u32[]{:S(2)}, u32[]{:S(2)}) collective-permute-start(f32[32,768]{1,0:T(8,128)S(1)} %get-tuple-element.105), channel_id=1, source_target_pairs={{0,12},{4,0},{8,4},{12,8},{1,13},{5,1},{9,5},{13,9},{2,14},{6,2},{... | collective-permute-start | bytes 294920 | tf_op jit(solution)/shard_map/ppermute | solution.py:311
  120.1 4.1 %shard_map.78 = (f32[32,768]{1,0:T(8,128)S(1)}, f32[32,768]{1,0:T(8,128)S(1)}, f32[32,768]{1,0:T(8,128)S(1)}, f32[32,768]{1,0:T(8,128)S(1)}) custom-call(s32[4]{0:T(128)S(1)} %fusion.11.refs_0_.place_ref, f32[32,3072]{1,0:T(8,128)S(1)} %get-tuple-element.116.refs_0_, f32[32,3072]{1,0:T(8,128)S(1)} %collective-permute-done.20.refs_1_, ...), custom_call_target="tpu_custom_call" | custom-call | flops 1048576 | bytes 262144 | tf_op jit(solution)/shard_map/pallas_call | solution.py:286
  124.2 3.2 %collective-permute-start.29 = (f32[32,768]{1,0:T(8,128)S(1)}, f32[32,768]{1,0:T(8,128)S(1)}, u32[]{:S(2)}, u32[]{:S(2)}) collective-permute-start(f32[32,768]{1,0:T(8,128)S(1)} %get-tuple-element.109), channel_id=1, source_target_pairs={{0,12},{4,0},{8,4},{12,8},{1,13},{5,1},{9,5},{13,9},{2,14},{6,2},{... | collective-permute-start | bytes 294920 | tf_op jit(solution)/shard_map/ppermute | solution.py:311
  129.1 1.9 %collective-permute-done.29 = f32[32,768]{1,0:T(8,128)S(1)} collective-permute-done((f32[32,768]{1,0:T(8,128)S(1)}, f32[32,768]{1,0:T(8,128)S(1)}, u32[]{:S(2)}, u32[]{:S(2)}) %collective-permute-start.29) | collective-permute-done | bytes 98336 | tf_op jit(solution)/shard_map/ppermute | solution.py:311
  131.0 6.3 %collective-permute-done.30 = f32[32,768]{1,0:T(8,128)S(1)} collective-permute-done((f32[32,768]{1,0:T(8,128)S(1)}, f32[32,768]{1,0:T(8,128)S(1)}, u32[]{:S(2)}, u32[]{:S(2)}) %collective-permute-start.30) | collective-permute-done | bytes 98336 | tf_op jit(solution)/shard_map/ppermute | solution.py:311
  137.6 5.9 %psum.7 = f32[2,32]{1,0:T(2,128)S(1)} all-reduce(f32[2,32]{1,0:T(2,128)S(1)} %pad_maximum_fusion), channel_id=1, replica_groups=mesh['groups'=2,'hid'=4,'emb'=4] {'emb'}, use_global_device_ids=true, to_apply=%region_2.3 | all-reduce | flops 64 | bytes 512 | tf_op jit(solution)/shard_map/psum | solution.py:411
  (79 shorter events, 14.1 us)
Async XLA Ops:
  0.0 16.5 %collective-permute-start.1 = (f32[32,1536]{1,0:T(8,128)}, f32[32,1536]{1,0:T(8,128)S(1)}, u32[]{:S(2)}, u32[]{:S(2)}) collective-permute-start(f32[32,1536]{1,0:T(8,128)} %refs_1_.3), channel_id=1, source_target_pairs={{0,4},{4,8},{8,12},{12,0},{1,5},{5,9},{9,13},{13,1},{2,6},{6,10},{... | collective-permute-start | bytes 589832 | tf_op jit(solution)/shard_map/ppermute | solution.py:311
  3.0 15.7 %collective-permute-start.2 = (f32[32,1536]{1,0:T(8,128)}, f32[32,1536]{1,0:T(8,128)S(1)}, u32[]{:S(2)}, u32[]{:S(2)}) collective-permute-start(f32[32,1536]{1,0:T(8,128)} %refs_1_.3), channel_id=1, source_target_pairs={{0,8},{4,12},{8,0},{12,4},{1,9},{5,13},{9,1},{13,5},{2,10},{6,14},... | collective-permute-start | bytes 589832 | tf_op jit(solution)/shard_map/ppermute | solution.py:311
  5.6 13.1 %collective-permute-start.3 = (f32[32,1536]{1,0:T(8,128)}, f32[32,1536]{1,0:T(8,128)S(1)}, u32[]{:S(2)}, u32[]{:S(2)}) collective-permute-start(f32[32,1536]{1,0:T(8,128)} %refs_1_.3), channel_id=1, source_target_pairs={{0,12},{4,0},{8,4},{12,8},{1,13},{5,1},{9,5},{13,9},{2,14},{6,2},{... | collective-permute-start | bytes 589832 | tf_op jit(solution)/shard_map/ppermute | solution.py:311
  8.1 8.5 %collective-permute-start = (f32[64,128]{1,0:T(8,128)S(1)}, f32[64,128]{1,0:T(8,128)S(1)}, u32[]{:S(2)}, u32[]{:S(2)}) collective-permute-start(f32[64,128]{1,0:T(8,128)S(1)} %shard_map.64.refs_1_.refs_0_), channel_id=1, source_target_pairs={{0,1},{1,0},{2,3},{3,2},{4,5},{5,4},{6,7},{7,6},{8,9},{9,8},{10,11... | collective-permute-start | bytes 98312 | tf_op jit(solution)/shard_map/ppermute | solution.py:314
  18.7 5.8 %collective-permute-start.4 = (f32[64,128]{1,0:T(8,128)S(1)}, f32[64,128]{1,0:T(8,128)S(1)}, u32[]{:S(2)}, u32[]{:S(2)}) collective-permute-start(f32[64,128]{1,0:T(8,128)S(1)} %shard_map.67.refs_0_.refs_2_), channel_id=1, source_target_pairs={{0,2},{1,3},{2,0},{3,1},{4,6},{5,7},{6,4},{7,5},{8,10},{9,11},{10,... | collective-permute-start | bytes 98312 | tf_op jit(solution)/shard_map/ppermute | solution.py:317
  24.7 15.0 %collective-permute-start.5 = (f32[32,1536]{1,0:T(8,128)S(1)}, f32[32,1536]{1,0:T(8,128)S(1)}, u32[]{:S(2)}, u32[]{:S(2)}) collective-permute-start(f32[32,1536]{1,0:T(8,128)S(1)} %get-tuple-element.76.refs_6_.refs_1_), channel_id=1, source_target_pairs={{0,4},{4,8},{8,12},{12,0},{1,5},{5,9},{9,13},{13,1},{2,6},{6,10},{... | collective-permute-start | bytes 589832 | tf_op jit(solution)/shard_map/ppermute | solution.py:311
  29.4 10.3 %collective-permute-start.6 = (f32[32,1536]{1,0:T(8,128)S(1)}, f32[32,1536]{1,0:T(8,128)S(1)}, u32[]{:S(2)}, u32[]{:S(2)}) collective-permute-start(f32[32,1536]{1,0:T(8,128)S(1)} %get-tuple-element.76.refs_6_.refs_1_), channel_id=1, source_target_pairs={{0,12},{4,0},{8,4},{12,8},{1,13},{5,1},{9,5},{13,9},{2,14},{6,2},{... | collective-permute-start | bytes 589832 | tf_op jit(solution)/shard_map/ppermute | solution.py:311
  39.8 1.8 %collective-permute-start.7 = (f32[32,3072]{1,0:T(8,128)S(1)}, f32[32,3072]{1,0:T(8,128)S(1)}, u32[]{:S(2)}, u32[]{:S(2)}) collective-permute-start(f32[32,3072]{1,0:T(8,128)S(1)} %get-tuple-element.124), channel_id=1, source_target_pairs={{0,1},{1,0},{2,3},{3,2},{4,5},{5,4},{6,7},{7,6},{8,9},{9,8},{10,11... | collective-permute-start | bytes 1179656 | tf_op jit(solution)/shard_map/ppermute | solution.py:314
  39.9 14.2 %collective-permute-start.9 = (f32[32,3072]{1,0:T(8,128)S(1)}, f32[32,3072]{1,0:T(8,128)S(1)}, u32[]{:S(2)}, u32[]{:S(2)}) collective-permute-start(f32[32,3072]{1,0:T(8,128)S(1)} %get-tuple-element.123), channel_id=1, source_target_pairs={{0,1},{1,0},{2,3},{3,2},{4,5},{5,4},{6,7},{7,6},{8,9},{9,8},{10,11... | collective-permute-start | bytes 1179656 | tf_op jit(solution)/shard_map/ppermute | solution.py:314
  41.6 12.4 %collective-permute-start.8 = (f32[32,3072]{1,0:T(8,128)S(1)}, f32[32,3072]{1,0:T(8,128)S(1)}, u32[]{:S(2)}, u32[]{:S(2)}) collective-permute-start(f32[32,3072]{1,0:T(8,128)S(1)} %get-tuple-element.126.refs_6_), channel_id=1, source_target_pairs={{0,2},{1,3},{2,0},{3,1},{4,6},{5,7},{6,4},{7,5},{8,10},{9,11},{10,... | collective-permute-start | bytes 1179656 | tf_op jit(solution)/shard_map/ppermute | solution.py:317
  42.3 11.8 %collective-permute-start.10 = (f32[32,1536]{1,0:T(8,128)S(1)}, f32[32,1536]{1,0:T(8,128)S(1)}, u32[]{:S(2)}, u32[]{:S(2)}) collective-permute-start(f32[32,1536]{1,0:T(8,128)S(1)} %get-tuple-element.76.refs_6_.refs_1_), channel_id=1, source_target_pairs={{0,8},{4,12},{8,0},{12,4},{1,9},{5,13},{9,1},{13,5},{2,10},{6,14},... | collective-permute-start | bytes 589832 | tf_op jit(solution)/shard_map/ppermute | solution.py:311
  54.1 4.3 %collective-permute-start.11 = (f32[32,3072]{1,0:T(8,128)S(1)}, f32[32,3072]{1,0:T(8,128)S(1)}, u32[]{:S(2)}, u32[]{:S(2)}) collective-permute-start(f32[32,3072]{1,0:T(8,128)S(1)} %get-tuple-element.118), channel_id=1, source_target_pairs={{0,1},{1,0},{2,3},{3,2},{4,5},{5,4},{6,7},{7,6},{8,9},{9,8},{10,11... | collective-permute-start | bytes 1179656 | tf_op jit(solution)/shard_map/ppermute | solution.py:314
  58.4 11.6 %collective-permute-start.12 = (f32[32,3072]{1,0:T(8,128)S(1)}, f32[32,3072]{1,0:T(8,128)S(1)}, u32[]{:S(2)}, u32[]{:S(2)}) collective-permute-start(f32[32,3072]{1,0:T(8,128)S(1)} %slice_add_fusion.2.refs_9_), channel_id=1, source_target_pairs={{0,2},{1,3},{2,0},{3,1},{4,6},{5,7},{6,4},{7,5},{8,10},{9,11},{10,... | collective-permute-start | bytes 1179656 | tf_op jit(solution)/shard_map/ppermute | solution.py:317
  65.4 7.6 %collective-permute-start.14 = (f32[32,3072]{1,0:T(8,128)S(1)}, f32[32,3072]{1,0:T(8,128)S(1)}, u32[]{:S(2)}, u32[]{:S(2)}) collective-permute-start(f32[32,3072]{1,0:T(8,128)S(1)} %get-tuple-element.120), channel_id=1, source_target_pairs={{0,1},{1,0},{2,3},{3,2},{4,5},{5,4},{6,7},{7,6},{8,9},{9,8},{10,11... | collective-permute-start | bytes 1179656 | tf_op jit(solution)/shard_map/ppermute | solution.py:314
  65.7 30.6 %collective-permute-start.13 = (f32[32,3072]{1,0:T(8,128)S(1)}, f32[32,3072]{1,0:T(8,128)S(1)}, u32[]{:S(2)}, u32[]{:S(2)}) collective-permute-start(f32[32,3072]{1,0:T(8,128)S(1)} %get-tuple-element.117), channel_id=1, source_target_pairs={{0,1},{1,0},{2,3},{3,2},{4,5},{5,4},{6,7},{7,6},{8,9},{9,8},{10,11... | collective-permute-start | bytes 1179656 | tf_op jit(solution)/shard_map/ppermute | solution.py:314
  66.0 12.3 %collective-permute-start.17 = (f32[32,3072]{1,0:T(8,128)S(1)}, f32[32,3072]{1,0:T(8,128)S(1)}, u32[]{:S(2)}, u32[]{:S(2)}) collective-permute-start(f32[32,3072]{1,0:T(8,128)S(1)} %get-tuple-element.119), channel_id=1, source_target_pairs={{0,1},{1,0},{2,3},{3,2},{4,5},{5,4},{6,7},{7,6},{8,9},{9,8},{10,11... | collective-permute-start | bytes 1179656 | tf_op jit(solution)/shard_map/ppermute | solution.py:314
  73.1 10.8 %collective-permute-start.16 = (f32[32,3072]{1,0:T(8,128)S(1)}, f32[32,3072]{1,0:T(8,128)S(1)}, u32[]{:S(2)}, u32[]{:S(2)}) collective-permute-start(f32[32,3072]{1,0:T(8,128)S(1)} %slice_add_fusion.1.refs_9_), channel_id=1, source_target_pairs={{0,2},{1,3},{2,0},{3,1},{4,6},{5,7},{6,4},{7,5},{8,10},{9,11},{10,... | collective-permute-start | bytes 1179656 | tf_op jit(solution)/shard_map/ppermute | solution.py:317
  77.7 7.9 %collective-permute-start.15 = (f32[32,3072]{1,0:T(8,128)S(1)}, f32[32,3072]{1,0:T(8,128)S(1)}, u32[]{:S(2)}, u32[]{:S(2)}) collective-permute-start(f32[32,3072]{1,0:T(8,128)S(1)} %get-tuple-element.121), channel_id=1, source_target_pairs={{0,1},{1,0},{2,3},{3,2},{4,5},{5,4},{6,7},{7,6},{8,9},{9,8},{10,11... | collective-permute-start | bytes 1179656 | tf_op jit(solution)/shard_map/ppermute | solution.py:314
  77.8 18.4 %collective-permute-start.19 = (f32[32,3072]{1,0:T(8,128)S(1)}, f32[32,3072]{1,0:T(8,128)S(1)}, u32[]{:S(2)}, u32[]{:S(2)}) collective-permute-start(f32[32,3072]{1,0:T(8,128)S(1)} %get-tuple-element.122), channel_id=1, source_target_pairs={{0,1},{1,0},{2,3},{3,2},{4,5},{5,4},{6,7},{7,6},{8,9},{9,8},{10,11... | collective-permute-start | bytes 1179656 | tf_op jit(solution)/shard_map/ppermute | solution.py:314
  84.1 12.1 %collective-permute-start.21 = (f32[32,3072]{1,0:T(8,128)S(1)}, f32[32,3072]{1,0:T(8,128)S(1)}, u32[]{:S(2)}, u32[]{:S(2)}) collective-permute-start(f32[32,3072]{1,0:T(8,128)S(1)} %fusion.4.refs_0_), channel_id=1, source_target_pairs={{0,2},{1,3},{2,0},{3,1},{4,6},{5,7},{6,4},{7,5},{8,10},{9,11},{10,... | collective-permute-start | bytes 1179656 | tf_op jit(solution)/shard_map/ppermute | solution.py:317
  85.8 16.7 %collective-permute-start.18 = (f32[32,3072]{1,0:T(8,128)S(1)}, f32[32,3072]{1,0:T(8,128)S(1)}, u32[]{:S(2)}, u32[]{:S(2)}) collective-permute-start(f32[32,3072]{1,0:T(8,128)S(1)} %slice_add_fusion), channel_id=1, source_target_pairs={{0,2},{1,3},{2,0},{3,1},{4,6},{5,7},{6,4},{7,5},{8,10},{9,11},{10,... | collective-permute-start | bytes 1179656 | tf_op jit(solution)/shard_map/ppermute | solution.py:317
  86.4 17.9 %collective-permute-start.22 = (f32[32,3072]{1,0:T(8,128)S(1)}, f32[32,3072]{1,0:T(8,128)S(1)}, u32[]{:S(2)}, u32[]{:S(2)}) collective-permute-start(f32[32,3072]{1,0:T(8,128)S(1)} %fusion.4.refs_0_), channel_id=1, source_target_pairs={{0,1},{1,0},{2,3},{3,2},{4,5},{5,4},{6,7},{7,6},{8,9},{9,8},{10,11... | collective-permute-start | bytes 1179656 | tf_op jit(solution)/shard_map/ppermute | solution.py:314
  96.3 8.0 %collective-permute-start.23 = (f32[32,3072]{1,0:T(8,128)S(1)}, f32[32,3072]{1,0:T(8,128)S(1)}, u32[]{:S(2)}, u32[]{:S(2)}) collective-permute-start(f32[32,3072]{1,0:T(8,128)S(1)} %collective-permute-done.21.refs_1_), channel_id=1, source_target_pairs={{0,1},{1,0},{2,3},{3,2},{4,5},{5,4},{6,7},{7,6},{8,9},{9,8},{10,11... | collective-permute-start | bytes 1179656 | tf_op jit(solution)/shard_map/ppermute | solution.py:314
  102.7 9.0 %collective-permute-start.20 = (f32[32,3072]{1,0:T(8,128)S(1)}, f32[32,3072]{1,0:T(8,128)S(1)}, u32[]{:S(2)}, u32[]{:S(2)}) collective-permute-start(f32[32,3072]{1,0:T(8,128)S(1)} %get-tuple-element.116.refs_0_), channel_id=1, source_target_pairs={{0,2},{1,3},{2,0},{3,1},{4,6},{5,7},{6,4},{7,5},{8,10},{9,11},{10,... | collective-permute-start | bytes 1179656 | tf_op jit(solution)/shard_map/ppermute | solution.py:317
  104.3 7.9 %collective-permute-start.24 = (f32[32,3072]{1,0:T(8,128)S(1)}, f32[32,3072]{1,0:T(8,128)S(1)}, u32[]{:S(2)}, u32[]{:S(2)}) collective-permute-start(f32[32,3072]{1,0:T(8,128)S(1)} %get-tuple-element.116.refs_0_), channel_id=1, source_target_pairs={{0,1},{1,0},{2,3},{3,2},{4,5},{5,4},{6,7},{7,6},{8,9},{9,8},{10,11... | collective-permute-start | bytes 1179656 | tf_op jit(solution)/shard_map/ppermute | solution.py:314
  111.7 1.8 %collective-permute-start.25 = (f32[32,3072]{1,0:T(8,128)S(1)}, f32[32,3072]{1,0:T(8,128)S(1)}, u32[]{:S(2)}, u32[]{:S(2)}) collective-permute-start(f32[32,3072]{1,0:T(8,128)S(1)} %collective-permute-done.20.refs_1_), channel_id=1, source_target_pairs={{0,1},{1,0},{2,3},{3,2},{4,5},{5,4},{6,7},{7,6},{8,9},{9,8},{10,11... | collective-permute-start | bytes 1179656 | tf_op jit(solution)/shard_map/ppermute | solution.py:314
  117.6 10.6 %collective-permute-start.26 = (f32[32,768]{1,0:T(8,128)S(1)}, f32[32,768]{1,0:T(8,128)S(1)}, u32[]{:S(2)}, u32[]{:S(2)}) collective-permute-start(f32[32,768]{1,0:T(8,128)S(1)} %get-tuple-element.105), channel_id=1, source_target_pairs={{0,12},{4,0},{8,4},{12,8},{1,13},{5,1},{9,5},{13,9},{2,14},{6,2},{... | collective-permute-start | bytes 294920 | tf_op jit(solution)/shard_map/ppermute | solution.py:311
  119.0 10.1 %collective-permute-start.27 = (f32[32,768]{1,0:T(8,128)S(1)}, f32[32,768]{1,0:T(8,128)S(1)}, u32[]{:S(2)}, u32[]{:S(2)}) collective-permute-start(f32[32,768]{1,0:T(8,128)S(1)} %get-tuple-element.106), channel_id=1, source_target_pairs={{0,8},{4,12},{8,0},{12,4},{1,9},{5,13},{9,1},{13,5},{2,10},{6,14},... | collective-permute-start | bytes 294920 | tf_op jit(solution)/shard_map/ppermute | solution.py:311
  119.3 9.8 %collective-permute-start.28 = (f32[32,768]{1,0:T(8,128)S(1)}, f32[32,768]{1,0:T(8,128)S(1)}, u32[]{:S(2)}, u32[]{:S(2)}) collective-permute-start(f32[32,768]{1,0:T(8,128)S(1)} %get-tuple-element.107), channel_id=1, source_target_pairs={{0,4},{4,8},{8,12},{12,0},{1,5},{5,9},{9,13},{13,1},{2,6},{6,10},{... | collective-permute-start | bytes 294920 | tf_op jit(solution)/shard_map/ppermute | solution.py:311
  124.2 6.8 %collective-permute-start.29 = (f32[32,768]{1,0:T(8,128)S(1)}, f32[32,768]{1,0:T(8,128)S(1)}, u32[]{:S(2)}, u32[]{:S(2)}) collective-permute-start(f32[32,768]{1,0:T(8,128)S(1)} %get-tuple-element.109), channel_id=1, source_target_pairs={{0,12},{4,0},{8,4},{12,8},{1,13},{5,1},{9,5},{13,9},{2,14},{6,2},{... | collective-permute-start | bytes 294920 | tf_op jit(solution)/shard_map/ppermute | solution.py:311
  127.4 10.0 %collective-permute-start.30 = (f32[32,768]{1,0:T(8,128)S(1)}, f32[32,768]{1,0:T(8,128)S(1)}, u32[]{:S(2)}, u32[]{:S(2)}) collective-permute-start(f32[32,768]{1,0:T(8,128)S(1)} %get-tuple-element.110), channel_id=1, source_target_pairs={{0,8},{4,12},{8,0},{12,4},{1,9},{5,13},{9,1},{13,5},{2,10},{6,14},... | collective-permute-start | bytes 294920 | tf_op jit(solution)/shard_map/ppermute | solution.py:311
  128.2 9.2 %collective-permute-start.31 = (f32[32,768]{1,0:T(8,128)S(1)}, f32[32,768]{1,0:T(8,128)S(1)}, u32[]{:S(2)}, u32[]{:S(2)}) collective-permute-start(f32[32,768]{1,0:T(8,128)S(1)} %get-tuple-element.111), channel_id=1, source_target_pairs={{0,4},{4,8},{8,12},{12,0},{1,5},{5,9},{9,13},{13,1},{2,6},{6,10},{... | collective-permute-start | bytes 294920 | tf_op jit(solution)/shard_map/ppermute | solution.py:311
  (5 other events, 20.7 us)

commit v10 on v9

--- a/solution.py
+++ b/solution.py
@@ -350,7 +350,6 @@
     moments = call(
         functools.partial(merge_kernel, depth), moments, (moments, other_core(moments)), (in_parts[2], *grads[1:])
     )
-    in_parts += prepared(2, [moments])
     parts = [moments]
     for _ in range(1, chips):
         parts.append(next_chip(parts[-1]))
@@ -358,7 +357,7 @@
         functools.partial(normalise_kernel, 2 * depth),
         (inputs, inputs, jax.ShapeDtypeStruct((tokens, 128), jnp.float32)),
         (inputs, norm_gain[None, :], *parts),
-        (in_parts[4],),
+        (),
     )
     inv_std = inv_std[:, :1]
     scaled = gathered(scaled)
@@ -368,13 +367,13 @@
     back_1 = stream(grads, out_weight, place, piece, piece, (), [half_0[0]])
     back_0 = exchanged(half_0)
     back_1, (back_0, scaled) = tied(back_1, (back_0, scaled))
-    in_parts += prepared(3, [back_1[0]])
-    half_1 = halved(back_1, in_parts[6])
+    in_parts += prepared(2, [back_1[0]])
+    half_1 = halved(back_1, in_parts[4])
     back_1 = exchanged(half_1)
     pre_0 = forward(scaled, in_parts[:4], place, (), [half_1[0]])
-    pre_1 = forward(scaled, in_parts[4:6], place, (), [pre_0[1], back_1[0]])
-    half_0 = halved(pre_0, pre_1)
-    pre_1 = forward(scaled, in_parts[6:], place, pre_1, [half_0[0]])
+    in_parts += prepared(3, [pre_0[1]])
+    half_0 = halved(pre_0, (in_parts[6], back_1[0]))
+    pre_1 = forward(scaled, in_parts[4:], place, (), [half_0[0]])
     pre_0 = exchanged(half_0)
 
     def slope_product(c, back, pre):

time: 144 us -> 142 us (0.986)
  starting transfers between devices: 31.8 us -> 28.6 us
    ppermute x12, starting transfers between devices: 20.4 us -> 17.9 us  [along_hid(): lax.ppermute(values, 'hid', [(i, (i + steps) % hid_size) for i in range(h...]
    ppermute x12, waiting for transfers between devices: 12.8 us -> 15.1 us  [along_hid(): lax.ppermute(values, 'hid', [(i, (i + steps) % hid_size) for i in range(h...]
    ppermute x7, waiting for transfers between devices: 25.5 us -> 23.9 us  [next_chip(): lax.ppermute(values, 'emb', [(i, (i + 2) % emb_size) for i in range(emb_s...]
    pallas_call x3 -> x2, Pallas kernels: 11.4 us -> 10.8 us  [forward(): pl.pallas_call(lambda *refs: forward_kernel(refs[0], refs[1:ends[0]], ref...]
  transfers between devices with their start and end apart: 32 -> 32, of which waited for: 12 -> 13; matrix products, arithmetic and copies ran while one was open for 1% -> 1% of each run, Pallas kernels for 40% -> 40%
where the time goes in v10:
time: 142 us
  Pallas kernels  61.5 us (43%)
  waiting for transfers between devices  42 us (30%)
  starting transfers between devices  28.6 us (20%)
  blocking collectives  6.04 us (4%)
  other arithmetic  1.79 us (1%)
    ppermute x7, waiting for transfers between devices, next_chip(): lax.ppermute(values, 'emb', [(i, (i + 2) % emb_size) for i in range(emb_s...  23.9 us
    pallas_call x2, Pallas kernels, stream(): pl.pallas_call(lambda *refs: stream_kernel(first, depth, refs[0], refs[1:...  18.3 us
    ppermute x12, starting transfers between devices, along_hid(): lax.ppermute(values, 'hid', [(i, (i + steps) % hid_size) for i in range(h...  17.9 us
    pallas_call x4, Pallas kernels, prepare(): pl.pallas_call(functools.partial(prepare_kernel, rows, columns, block, de...  16.8 us
    pallas_call x3, Pallas kernels, backward(): pl.pallas_call(functools.partial(backward_kernel, slots, len(weights) //...  15.4 us
    ppermute x12, waiting for transfers between devices, along_hid(): lax.ppermute(values, 'hid', [(i, (i + steps) % hid_size) for i in range(h...  15.1 us
    pallas_call x2, Pallas kernels, forward(): pl.pallas_call(lambda *refs: forward_kernel(refs[0], refs[1:ends[0]], ref...  10.8 us
    ppermute x7, starting transfers between devices, next_chip(): lax.ppermute(values, 'emb', [(i, (i + 2) % emb_size) for i in range(emb_s...  8.68 us
  transfers between devices with their start and end apart: 32, of which 13 were waited for; matrix products, arithmetic and copies ran while one was open for 1% of the time, Pallas kernels for 40%

profile of v10, /device:TPU:0, one launch (start us, length us, event | category | flops | bytes accessed | tf_op | source)
XLA Modules:
  0.0 141.6 jit_solution(13565844487259072501)
XLA Ops:
  0.0 5.0 %collective-permute-start.3 = (f32[32,1536]{1,0:T(8,128)}, f32[32,1536]{1,0:T(8,128)S(1)}, u32[]{:S(2)}, u32[]{:S(2)}) collective-permute-start(f32[32,1536]{1,0:T(8,128)} %refs_1_.3), channel_id=1, source_target_pairs={{0,12},{4,0},{8,4},{12,8},{1,13},{5,1},{9,5},{13,9},{2,14},{6,2},{... | collective-permute-start | bytes 589832 | tf_op jit(solution)/shard_map/ppermute | solution.py:311
  7.2 4.2 %shard_map.65 = (bf16[1536,1536]{1,0:T(8,128)(2,1)S(1)}, bf16[1536,1536]{1,0:T(8,128)(2,1)S(1)}) custom-call(f32[1536,6144]{1,0:T(8,128)} %weight_ref.7, s32[4]{0:T(128)S(1)} %fusion.11.refs_0_.place_ref, f32[64,128]{1,0:T(8,128)S(1)} %shard_map.64.refs_1_.refs_0_), custom_call_target="tpu_custom_call" | custom-call | flops 1048576 | bytes 262144 | tf_op jit(solution)/shard_map/pallas_call | solution.py:111
  11.4 4.2 %shard_map.66 = (bf16[1536,1536]{1,0:T(8,128)(2,1)S(1)}, bf16[1536,1536]{1,0:T(8,128)(2,1)S(1)}) custom-call(f32[1536,6144]{1,0:T(8,128)} %weight_ref.7, bf16[1536,1536]{1,0:T(8,128)(2,1)S(1)} %get-tuple-element.57.refs_0_.refs_5_.refs_4_), custom_call_target="tpu_custom_call" | custom-call | flops 1048576 | bytes 262144 | tf_op jit(solution)/shard_map/pallas_call | solution.py:111
  15.7 6.3 %collective-permute-done.2.refs_4_.refs_3_ = f32[32,1536]{1,0:T(8,128)S(1)} collective-permute-done((f32[32,1536]{1,0:T(8,128)}, f32[32,1536]{1,0:T(8,128)S(1)}, u32[]{:S(2)}, u32[]{:S(2)}) %collective-permute-start.2) | collective-permute-done | bytes 196640 | tf_op jit(solution)/shard_map/ppermute | solution.py:311
  22.0 1.6 %collective-permute-start.4 = (f32[64,128]{1,0:T(8,128)S(1)}, f32[64,128]{1,0:T(8,128)S(1)}, u32[]{:S(2)}, u32[]{:S(2)}) collective-permute-start(f32[64,128]{1,0:T(8,128)S(1)} %shard_map.67.refs_2_), channel_id=1, source_target_pairs={{0,2},{1,3},{2,0},{3,1},{4,6},{5,7},{6,4},{7,5},{8,10},{9,11},{10,... | collective-permute-start | bytes 98312 | tf_op jit(solution)/shard_map/ppermute | solution.py:317
  23.5 2.4 %collective-permute-done.4.refs_3_ = f32[64,128]{1,0:T(8,128)S(1)} collective-permute-done((f32[64,128]{1,0:T(8,128)S(1)}, f32[64,128]{1,0:T(8,128)S(1)}, u32[]{:S(2)}, u32[]{:S(2)}) %collective-permute-start.4) | collective-permute-done | bytes 32800 | tf_op jit(solution)/shard_map/ppermute | solution.py:317
  26.5 1.7 %collective-permute-start.5 = (f32[32,1536]{1,0:T(8,128)S(1)}, f32[32,1536]{1,0:T(8,128)S(1)}, u32[]{:S(2)}, u32[]{:S(2)}) collective-permute-start(f32[32,1536]{1,0:T(8,128)S(1)} %get-tuple-element.73.refs_6_.refs_1_), channel_id=1, source_target_pairs={{0,4},{4,8},{8,12},{12,0},{1,5},{5,9},{9,13},{13,1},{2,6},{6,10},{... | collective-permute-start | bytes 589832 | tf_op jit(solution)/shard_map/ppermute | solution.py:311
  28.2 9.2 %shard_map.69 = (f32[64,3072]{1,0:T(8,128)S(1)}, f32[64,3072]{1,0:T(8,128)S(1)}) custom-call(s32[4]{0:T(128)S(1)} %fusion.11.refs_0_.place_ref, f32[32,1536]{1,0:T(8,128)S(1)} %copy-done, f32[32,1536]{1,0:T(8,128)S(1)} %collective-permute-done.1.refs_3_.refs_2_, f32[32,1536]{1,0:T(8,128)S(1)} %collective-permute-done.2.refs_4_.refs_3_, ...), custom_call_target="tpu_custom_call" | custom-call | flops 1048576 | bytes 262144 | tf_op jit(solution)/shard_map/pallas_call | solution.py:226
  38.1 1.2 collective-permute-done.7
  39.4 1.6 %collective-permute-start.8 = (f32[32,3072]{1,0:T(8,128)S(1)}, f32[32,3072]{1,0:T(8,128)S(1)}, u32[]{:S(2)}, u32[]{:S(2)}) collective-permute-start(f32[32,3072]{1,0:T(8,128)S(1)} %get-tuple-element.122.refs_6_), channel_id=1, source_target_pairs={{0,2},{1,3},{2,0},{3,1},{4,6},{5,7},{6,4},{7,5},{8,10},{9,11},{10,... | collective-permute-start | bytes 1179656 | tf_op jit(solution)/shard_map/ppermute | solution.py:317
  40.9 2.7 %collective-permute-start.10 = (f32[32,1536]{1,0:T(8,128)S(1)}, f32[32,1536]{1,0:T(8,128)S(1)}, u32[]{:S(2)}, u32[]{:S(2)}) collective-permute-start(f32[32,1536]{1,0:T(8,128)S(1)} %get-tuple-element.73.refs_6_.refs_1_), channel_id=1, source_target_pairs={{0,8},{4,12},{8,0},{12,4},{1,9},{5,13},{9,1},{13,5},{2,10},{6,14},... | collective-permute-start | bytes 589832 | tf_op jit(solution)/shard_map/ppermute | solution.py:311
  43.6 9.2 %shard_map.70 = (f32[64,3072]{1,0:T(8,128)S(1)}, f32[64,3072]{1,0:T(8,128)S(1)}) custom-call(s32[4]{0:T(128)S(1)} %fusion.11.refs_0_.place_ref, f32[32,1536]{1,0:T(8,128)S(1)} %copy-done, f32[32,1536]{1,0:T(8,128)S(1)} %collective-permute-done.1.refs_3_.refs_2_, f32[32,1536]{1,0:T(8,128)S(1)} %collective-permute-done.2.refs_4_.refs_3_, ...), custom_call_target="tpu_custom_call" | custom-call | flops 1048576 | bytes 262144 | tf_op jit(solution)/shard_map/pallas_call | solution.py:226
  53.0 4.2 %shard_map.71 = (bf16[1536,1536]{1,0:T(8,128)(2,1)S(1)}, bf16[1536,1536]{1,0:T(8,128)(2,1)S(1)}) custom-call(f32[1536,6144]{1,0:T(8,128)} %weight_ref.7, f32[64,3072]{1,0:T(8,128)S(1)} %get-tuple-element.70.refs_0_), custom_call_target="tpu_custom_call" | custom-call | flops 1048576 | bytes 262144 | tf_op jit(solution)/shard_map/pallas_call | solution.py:111
  57.8 5.4 %shard_map.72 = (f32[64,3072]{1,0:T(8,128)S(1)}, f32[64,3072]{1,0:T(8,128)S(1)}) custom-call(s32[4]{0:T(128)S(1)} %fusion.11.refs_0_.place_ref, f32[32,1536]{1,0:T(8,128)S(1)} %get-tuple-element.73.refs_6_.refs_1_, f32[32,1536]{1,0:T(8,128)S(1)} %collective-permute-done.5.refs_2_, f32[32,1536]{1,0:T(8,128)S(1)} %collective-permute-done.10.refs_3_, ...), custom_call_target="tpu_custom_call" | custom-call | flops 1048576 | bytes 262144 | tf_op jit(solution)/shard_map/pallas_call | solution.py:178
  64.0 4.2 %shard_map.73 = (bf16[1536,1536]{1,0:T(8,128)(2,1)S(1)}, bf16[1536,1536]{1,0:T(8,128)(2,1)S(1)}) custom-call(f32[1536,6144]{1,0:T(8,128)} %weight_ref.7, f32[64,3072]{1,0:T(8,128)S(1)} %get-tuple-element.80.refs_0_), custom_call_target="tpu_custom_call" | custom-call | flops 1048576 | bytes 262144 | tf_op jit(solution)/shard_map/pallas_call | solution.py:111
  69.9 5.4 %shard_map.74 = (f32[64,3072]{1,0:T(8,128)S(1)}, f32[64,3072]{1,0:T(8,128)S(1)}) custom-call(s32[4]{0:T(128)S(1)} %fusion.11.refs_0_.place_ref, f32[32,1536]{1,0:T(8,128)S(1)} %get-tuple-element.73.refs_6_.refs_1_, f32[32,1536]{1,0:T(8,128)S(1)} %collective-permute-done.5.refs_2_, f32[32,1536]{1,0:T(8,128)S(1)} %collective-permute-done.10.refs_3_, ...), custom_call_target="tpu_custom_call" | custom-call | flops 1048576 | bytes 262144 | tf_op jit(solution)/shard_map/pallas_call | solution.py:178
  75.9 3.8 %collective-permute-done.16 = f32[32,3072]{1,0:T(8,128)S(1)} collective-permute-done((f32[32,3072]{1,0:T(8,128)S(1)}, f32[32,3072]{1,0:T(8,128)S(1)}, u32[]{:S(2)}, u32[]{:S(2)}) %collective-permute-start.16) | collective-permute-done | bytes 393248 | tf_op jit(solution)/shard_map/ppermute | solution.py:317
  80.0 1.6 %collective-permute-start.21 = (f32[32,3072]{1,0:T(8,128)S(1)}, f32[32,3072]{1,0:T(8,128)S(1)}, u32[]{:S(2)}, u32[]{:S(2)}) collective-permute-start(f32[32,3072]{1,0:T(8,128)S(1)} %fusion.4.refs_0_), channel_id=1, source_target_pairs={{0,2},{1,3},{2,0},{3,1},{4,6},{5,7},{6,4},{7,5},{8,10},{9,11},{10,... | collective-permute-start | bytes 1179656 | tf_op jit(solution)/shard_map/ppermute | solution.py:317
  82.2 9.9 %collective-permute-done.21.refs_1_ = f32[32,3072]{1,0:T(8,128)S(1)} collective-permute-done((f32[32,3072]{1,0:T(8,128)S(1)}, f32[32,3072]{1,0:T(8,128)S(1)}, u32[]{:S(2)}, u32[]{:S(2)}) %collective-permute-start.21) | collective-permute-done | bytes 393248 | tf_op jit(solution)/shard_map/ppermute | solution.py:317
  92.1 6.6 %collective-permute-done.18 = f32[32,3072]{1,0:T(8,128)S(1)} collective-permute-done((f32[32,3072]{1,0:T(8,128)S(1)}, f32[32,3072]{1,0:T(8,128)S(1)}, u32[]{:S(2)}, u32[]{:S(2)}) %collective-permute-start.18) | collective-permute-done | bytes 393248 | tf_op jit(solution)/shard_map/ppermute | solution.py:317
  99.0 1.8 %collective-permute-start.20 = (f32[32,3072]{1,0:T(8,128)S(1)}, f32[32,3072]{1,0:T(8,128)S(1)}, u32[]{:S(2)}, u32[]{:S(2)}) collective-permute-start(f32[32,3072]{1,0:T(8,128)S(1)} %get-tuple-element.112.refs_0_), channel_id=1, source_target_pairs={{0,2},{1,3},{2,0},{3,1},{4,6},{5,7},{6,4},{7,5},{8,10},{9,11},{10,... | collective-permute-start | bytes 1179656 | tf_op jit(solution)/shard_map/ppermute | solution.py:317
  100.9 7.3 %shard_map.75 = (f32[32,1536]{1,0:T(8,128)S(1)}, f32[32,1536]{1,0:T(8,128)S(1)}, f32[32,1536]{1,0:T(8,128)S(1)}, f32[32,1536]{1,0:T(8,128)S(1)}) custom-call(s32[4]{0:T(128)S(1)} %fusion.11.refs_0_.place_ref, f32[32,3072]{1,0:T(8,128)S(1)} %fusion.4.refs_0_, f32[32,3072]{1,0:T(8,128)S(1)} %collective-permute-done.21.refs_1_, ...), custom_call_target="tpu_custom_call" | custom-call | flops 1048576 | bytes 262144 | tf_op jit(solution)/shard_map/pallas_call | solution.py:286
  108.7 1.7 %collective-permute-done.25.refs_3_ = f32[32,3072]{1,0:T(8,128)S(1)} collective-permute-done((f32[32,3072]{1,0:T(8,128)S(1)}, f32[32,3072]{1,0:T(8,128)S(1)}, u32[]{:S(2)}, u32[]{:S(2)}) %collective-permute-start.25) | collective-permute-done | bytes 393248 | tf_op jit(solution)/shard_map/ppermute | solution.py:314
  110.5 4.1 %shard_map.76 = (f32[32,768]{1,0:T(8,128)S(1)}, f32[32,768]{1,0:T(8,128)S(1)}, f32[32,768]{1,0:T(8,128)S(1)}, f32[32,768]{1,0:T(8,128)S(1)}) custom-call(s32[4]{0:T(128)S(1)} %fusion.11.refs_0_.place_ref, f32[32,3072]{1,0:T(8,128)S(1)} %get-tuple-element.112.refs_0_, f32[32,3072]{1,0:T(8,128)S(1)} %collective-permute-done.20.refs_1_, ...), custom_call_target="tpu_custom_call" | custom-call | flops 1048576 | bytes 262144 | tf_op jit(solution)/shard_map/pallas_call | solution.py:286
  114.5 2.0 %collective-permute-start.26 = (f32[32,768]{1,0:T(8,128)S(1)}, f32[32,768]{1,0:T(8,128)S(1)}, u32[]{:S(2)}, u32[]{:S(2)}) collective-permute-start(f32[32,768]{1,0:T(8,128)S(1)} %get-tuple-element.101), channel_id=1, source_target_pairs={{0,12},{4,0},{8,4},{12,8},{1,13},{5,1},{9,5},{13,9},{2,14},{6,2},{... | collective-permute-start | bytes 294920 | tf_op jit(solution)/shard_map/ppermute | solution.py:311
  116.6 1.7 %collective-permute-start.28 = (f32[32,768]{1,0:T(8,128)S(1)}, f32[32,768]{1,0:T(8,128)S(1)}, u32[]{:S(2)}, u32[]{:S(2)}) collective-permute-start(f32[32,768]{1,0:T(8,128)S(1)} %get-tuple-element.103), channel_id=1, source_target_pairs={{0,4},{4,8},{8,12},{12,0},{1,5},{5,9},{9,13},{13,1},{2,6},{6,10},{... | collective-permute-start | bytes 294920 | tf_op jit(solution)/shard_map/ppermute | solution.py:311
  118.3 4.1 %shard_map.77 = (f32[32,768]{1,0:T(8,128)S(1)}, f32[32,768]{1,0:T(8,128)S(1)}, f32[32,768]{1,0:T(8,128)S(1)}, f32[32,768]{1,0:T(8,128)S(1)}) custom-call(s32[4]{0:T(128)S(1)} %fusion.11.refs_0_.place_ref, f32[32,3072]{1,0:T(8,128)S(1)} %get-tuple-element.112.refs_0_, f32[32,3072]{1,0:T(8,128)S(1)} %collective-permute-done.20.refs_1_, ...), custom_call_target="tpu_custom_call" | custom-call | flops 1048576 | bytes 262144 | tf_op jit(solution)/shard_map/pallas_call | solution.py:286
  122.4 2.2 %collective-permute-start.29 = (f32[32,768]{1,0:T(8,128)S(1)}, f32[32,768]{1,0:T(8,128)S(1)}, u32[]{:S(2)}, u32[]{:S(2)}) collective-permute-start(f32[32,768]{1,0:T(8,128)S(1)} %get-tuple-element.105), channel_id=1, source_target_pairs={{0,12},{4,0},{8,4},{12,8},{1,13},{5,1},{9,5},{13,9},{2,14},{6,2},{... | collective-permute-start | bytes 294920 | tf_op jit(solution)/shard_map/ppermute | solution.py:311
  124.6 1.1 collective-permute-start.30
  126.6 1.6 %collective-permute-done.29 = f32[32,768]{1,0:T(8,128)S(1)} collective-permute-done((f32[32,768]{1,0:T(8,128)S(1)}, f32[32,768]{1,0:T(8,128)S(1)}, u32[]{:S(2)}, u32[]{:S(2)}) %collective-permute-start.29) | collective-permute-done | bytes 98336 | tf_op jit(solution)/shard_map/ppermute | solution.py:311
  128.2 6.3 %collective-permute-done.30 = f32[32,768]{1,0:T(8,128)S(1)} collective-permute-done((f32[32,768]{1,0:T(8,128)S(1)}, f32[32,768]{1,0:T(8,128)S(1)}, u32[]{:S(2)}, u32[]{:S(2)}) %collective-permute-start.30) | collective-permute-done | bytes 98336 | tf_op jit(solution)/shard_map/ppermute | solution.py:311
  134.7 6.0 %psum.7 = f32[2,32]{1,0:T(2,128)S(1)} all-reduce(f32[2,32]{1,0:T(2,128)S(1)} %pad_maximum_fusion), channel_id=1, replica_groups=mesh['groups'=2,'hid'=4,'emb'=4] {'emb'}, use_global_device_ids=true, to_apply=%region_2.3 | all-reduce | flops 64 | bytes 512 | tf_op jit(solution)/shard_map/psum | solution.py:410
  (78 shorter events, 11.2 us)
Async XLA Ops:
  0.0 15.7 %collective-permute-start.3 = (f32[32,1536]{1,0:T(8,128)}, f32[32,1536]{1,0:T(8,128)S(1)}, u32[]{:S(2)}, u32[]{:S(2)}) collective-permute-start(f32[32,1536]{1,0:T(8,128)} %refs_1_.3), channel_id=1, source_target_pairs={{0,12},{4,0},{8,4},{12,8},{1,13},{5,1},{9,5},{13,9},{2,14},{6,2},{... | collective-permute-start | bytes 589832 | tf_op jit(solution)/shard_map/ppermute | solution.py:311
  5.0 16.9 %collective-permute-start.2 = (f32[32,1536]{1,0:T(8,128)}, f32[32,1536]{1,0:T(8,128)S(1)}, u32[]{:S(2)}, u32[]{:S(2)}) collective-permute-start(f32[32,1536]{1,0:T(8,128)} %refs_1_.3), channel_id=1, source_target_pairs={{0,8},{4,12},{8,0},{12,4},{1,9},{5,13},{9,1},{13,5},{2,10},{6,14},... | collective-permute-start | bytes 589832 | tf_op jit(solution)/shard_map/ppermute | solution.py:311
  5.1 16.9 %collective-permute-start.1 = (f32[32,1536]{1,0:T(8,128)}, f32[32,1536]{1,0:T(8,128)S(1)}, u32[]{:S(2)}, u32[]{:S(2)}) collective-permute-start(f32[32,1536]{1,0:T(8,128)} %refs_1_.3), channel_id=1, source_target_pairs={{0,4},{4,8},{8,12},{12,0},{1,5},{5,9},{9,13},{13,1},{2,6},{6,10},{... | collective-permute-start | bytes 589832 | tf_op jit(solution)/shard_map/ppermute | solution.py:311
  7.2 8.5 %collective-permute-start = (f32[64,128]{1,0:T(8,128)S(1)}, f32[64,128]{1,0:T(8,128)S(1)}, u32[]{:S(2)}, u32[]{:S(2)}) collective-permute-start(f32[64,128]{1,0:T(8,128)S(1)} %shard_map.64.refs_1_.refs_0_), channel_id=1, source_target_pairs={{0,1},{1,0},{2,3},{3,2},{4,5},{5,4},{6,7},{7,6},{8,9},{9,8},{10,11... | collective-permute-start | bytes 98312 | tf_op jit(solution)/shard_map/ppermute | solution.py:314
  22.0 4.0 %collective-permute-start.4 = (f32[64,128]{1,0:T(8,128)S(1)}, f32[64,128]{1,0:T(8,128)S(1)}, u32[]{:S(2)}, u32[]{:S(2)}) collective-permute-start(f32[64,128]{1,0:T(8,128)S(1)} %shard_map.67.refs_2_), channel_id=1, source_target_pairs={{0,2},{1,3},{2,0},{3,1},{4,6},{5,7},{6,4},{7,5},{8,10},{9,11},{10,... | collective-permute-start | bytes 98312 | tf_op jit(solution)/shard_map/ppermute | solution.py:317
  26.1 11.2 %collective-permute-start.6 = (f32[32,1536]{1,0:T(8,128)S(1)}, f32[32,1536]{1,0:T(8,128)S(1)}, u32[]{:S(2)}, u32[]{:S(2)}) collective-permute-start(f32[32,1536]{1,0:T(8,128)S(1)} %get-tuple-element.73.refs_6_.refs_1_), channel_id=1, source_target_pairs={{0,12},{4,0},{8,4},{12,8},{1,13},{5,1},{9,5},{13,9},{2,14},{6,2},{... | collective-permute-start | bytes 589832 | tf_op jit(solution)/shard_map/ppermute | solution.py:311
  26.5 11.0 %collective-permute-start.5 = (f32[32,1536]{1,0:T(8,128)S(1)}, f32[32,1536]{1,0:T(8,128)S(1)}, u32[]{:S(2)}, u32[]{:S(2)}) collective-permute-start(f32[32,1536]{1,0:T(8,128)S(1)} %get-tuple-element.73.refs_6_.refs_1_), channel_id=1, source_target_pairs={{0,4},{4,8},{8,12},{12,0},{1,5},{5,9},{9,13},{13,1},{2,6},{6,10},{... | collective-permute-start | bytes 589832 | tf_op jit(solution)/shard_map/ppermute | solution.py:311
  37.5 1.8 %collective-permute-start.7 = (f32[32,3072]{1,0:T(8,128)S(1)}, f32[32,3072]{1,0:T(8,128)S(1)}, u32[]{:S(2)}, u32[]{:S(2)}) collective-permute-start(f32[32,3072]{1,0:T(8,128)S(1)} %get-tuple-element.120), channel_id=1, source_target_pairs={{0,1},{1,0},{2,3},{3,2},{4,5},{5,4},{6,7},{7,6},{8,9},{9,8},{10,11... | collective-permute-start | bytes 1179656 | tf_op jit(solution)/shard_map/ppermute | solution.py:314
  37.6 15.2 %collective-permute-start.9 = (f32[32,3072]{1,0:T(8,128)S(1)}, f32[32,3072]{1,0:T(8,128)S(1)}, u32[]{:S(2)}, u32[]{:S(2)}) collective-permute-start(f32[32,3072]{1,0:T(8,128)S(1)} %get-tuple-element.119), channel_id=1, source_target_pairs={{0,1},{1,0},{2,3},{3,2},{4,5},{5,4},{6,7},{7,6},{8,9},{9,8},{10,11... | collective-permute-start | bytes 1179656 | tf_op jit(solution)/shard_map/ppermute | solution.py:314
  39.4 13.4 %collective-permute-start.8 = (f32[32,3072]{1,0:T(8,128)S(1)}, f32[32,3072]{1,0:T(8,128)S(1)}, u32[]{:S(2)}, u32[]{:S(2)}) collective-permute-start(f32[32,3072]{1,0:T(8,128)S(1)} %get-tuple-element.122.refs_6_), channel_id=1, source_target_pairs={{0,2},{1,3},{2,0},{3,1},{4,6},{5,7},{6,4},{7,5},{8,10},{9,11},{10,... | collective-permute-start | bytes 1179656 | tf_op jit(solution)/shard_map/ppermute | solution.py:317
  40.9 11.8 %collective-permute-start.10 = (f32[32,1536]{1,0:T(8,128)S(1)}, f32[32,1536]{1,0:T(8,128)S(1)}, u32[]{:S(2)}, u32[]{:S(2)}) collective-permute-start(f32[32,1536]{1,0:T(8,128)S(1)} %get-tuple-element.73.refs_6_.refs_1_), channel_id=1, source_target_pairs={{0,8},{4,12},{8,0},{12,4},{1,9},{5,13},{9,1},{13,5},{2,10},{6,14},... | collective-permute-start | bytes 589832 | tf_op jit(solution)/shard_map/ppermute | solution.py:311
  52.9 4.3 %collective-permute-start.11 = (f32[32,3072]{1,0:T(8,128)S(1)}, f32[32,3072]{1,0:T(8,128)S(1)}, u32[]{:S(2)}, u32[]{:S(2)}) collective-permute-start(f32[32,3072]{1,0:T(8,128)S(1)} %get-tuple-element.114), channel_id=1, source_target_pairs={{0,1},{1,0},{2,3},{3,2},{4,5},{5,4},{6,7},{7,6},{8,9},{9,8},{10,11... | collective-permute-start | bytes 1179656 | tf_op jit(solution)/shard_map/ppermute | solution.py:314
  57.2 11.6 %collective-permute-start.12 = (f32[32,3072]{1,0:T(8,128)S(1)}, f32[32,3072]{1,0:T(8,128)S(1)}, u32[]{:S(2)}, u32[]{:S(2)}) collective-permute-start(f32[32,3072]{1,0:T(8,128)S(1)} %slice_add_fusion.2.refs_9_), channel_id=1, source_target_pairs={{0,2},{1,3},{2,0},{3,1},{4,6},{5,7},{6,4},{7,5},{8,10},{9,11},{10,... | collective-permute-start | bytes 1179656 | tf_op jit(solution)/shard_map/ppermute | solution.py:317
  63.3 5.5 %collective-permute-start.14 = (f32[32,3072]{1,0:T(8,128)S(1)}, f32[32,3072]{1,0:T(8,128)S(1)}, u32[]{:S(2)}, u32[]{:S(2)}) collective-permute-start(f32[32,3072]{1,0:T(8,128)S(1)} %get-tuple-element.116), channel_id=1, source_target_pairs={{0,1},{1,0},{2,3},{3,2},{4,5},{5,4},{6,7},{7,6},{8,9},{9,8},{10,11... | collective-permute-start | bytes 1179656 | tf_op jit(solution)/shard_map/ppermute | solution.py:314
  63.5 28.6 %collective-permute-start.13 = (f32[32,3072]{1,0:T(8,128)S(1)}, f32[32,3072]{1,0:T(8,128)S(1)}, u32[]{:S(2)}, u32[]{:S(2)}) collective-permute-start(f32[32,3072]{1,0:T(8,128)S(1)} %get-tuple-element.113), channel_id=1, source_target_pairs={{0,1},{1,0},{2,3},{3,2},{4,5},{5,4},{6,7},{7,6},{8,9},{9,8},{10,11... | collective-permute-start | bytes 1179656 | tf_op jit(solution)/shard_map/ppermute | solution.py:314
  63.8 12.1 %collective-permute-start.17 = (f32[32,3072]{1,0:T(8,128)S(1)}, f32[32,3072]{1,0:T(8,128)S(1)}, u32[]{:S(2)}, u32[]{:S(2)}) collective-permute-start(f32[32,3072]{1,0:T(8,128)S(1)} %get-tuple-element.115), channel_id=1, source_target_pairs={{0,1},{1,0},{2,3},{3,2},{4,5},{5,4},{6,7},{7,6},{8,9},{9,8},{10,11... | collective-permute-start | bytes 1179656 | tf_op jit(solution)/shard_map/ppermute | solution.py:314
  68.9 10.9 %collective-permute-start.16 = (f32[32,3072]{1,0:T(8,128)S(1)}, f32[32,3072]{1,0:T(8,128)S(1)}, u32[]{:S(2)}, u32[]{:S(2)}) collective-permute-start(f32[32,3072]{1,0:T(8,128)S(1)} %slice_add_fusion.1.refs_9_), channel_id=1, source_target_pairs={{0,2},{1,3},{2,0},{3,1},{4,6},{5,7},{6,4},{7,5},{8,10},{9,11},{10,... | collective-permute-start | bytes 1179656 | tf_op jit(solution)/shard_map/ppermute | solution.py:317
  75.3 6.2 %collective-permute-start.15 = (f32[32,3072]{1,0:T(8,128)S(1)}, f32[32,3072]{1,0:T(8,128)S(1)}, u32[]{:S(2)}, u32[]{:S(2)}) collective-permute-start(f32[32,3072]{1,0:T(8,128)S(1)} %get-tuple-element.117), channel_id=1, source_target_pairs={{0,1},{1,0},{2,3},{3,2},{4,5},{5,4},{6,7},{7,6},{8,9},{9,8},{10,11... | collective-permute-start | bytes 1179656 | tf_op jit(solution)/shard_map/ppermute | solution.py:314
  75.4 16.7 %collective-permute-start.19 = (f32[32,3072]{1,0:T(8,128)S(1)}, f32[32,3072]{1,0:T(8,128)S(1)}, u32[]{:S(2)}, u32[]{:S(2)}) collective-permute-start(f32[32,3072]{1,0:T(8,128)S(1)} %get-tuple-element.118), channel_id=1, source_target_pairs={{0,1},{1,0},{2,3},{3,2},{4,5},{5,4},{6,7},{7,6},{8,9},{9,8},{10,11... | collective-permute-start | bytes 1179656 | tf_op jit(solution)/shard_map/ppermute | solution.py:314
  80.0 12.1 %collective-permute-start.21 = (f32[32,3072]{1,0:T(8,128)S(1)}, f32[32,3072]{1,0:T(8,128)S(1)}, u32[]{:S(2)}, u32[]{:S(2)}) collective-permute-start(f32[32,3072]{1,0:T(8,128)S(1)} %fusion.4.refs_0_), channel_id=1, source_target_pairs={{0,2},{1,3},{2,0},{3,1},{4,6},{5,7},{6,4},{7,5},{8,10},{9,11},{10,... | collective-permute-start | bytes 1179656 | tf_op jit(solution)/shard_map/ppermute | solution.py:317
  81.6 17.2 %collective-permute-start.18 = (f32[32,3072]{1,0:T(8,128)S(1)}, f32[32,3072]{1,0:T(8,128)S(1)}, u32[]{:S(2)}, u32[]{:S(2)}) collective-permute-start(f32[32,3072]{1,0:T(8,128)S(1)} %slice_add_fusion), channel_id=1, source_target_pairs={{0,2},{1,3},{2,0},{3,1},{4,6},{5,7},{6,4},{7,5},{8,10},{9,11},{10,... | collective-permute-start | bytes 1179656 | tf_op jit(solution)/shard_map/ppermute | solution.py:317
  82.2 18.7 %collective-permute-start.22 = (f32[32,3072]{1,0:T(8,128)S(1)}, f32[32,3072]{1,0:T(8,128)S(1)}, u32[]{:S(2)}, u32[]{:S(2)}) collective-permute-start(f32[32,3072]{1,0:T(8,128)S(1)} %fusion.4.refs_0_), channel_id=1, source_target_pairs={{0,1},{1,0},{2,3},{3,2},{4,5},{5,4},{6,7},{7,6},{8,9},{9,8},{10,11... | collective-permute-start | bytes 1179656 | tf_op jit(solution)/shard_map/ppermute | solution.py:314
  92.1 8.8 %collective-permute-start.23 = (f32[32,3072]{1,0:T(8,128)S(1)}, f32[32,3072]{1,0:T(8,128)S(1)}, u32[]{:S(2)}, u32[]{:S(2)}) collective-permute-start(f32[32,3072]{1,0:T(8,128)S(1)} %collective-permute-done.21.refs_1_), channel_id=1, source_target_pairs={{0,1},{1,0},{2,3},{3,2},{4,5},{5,4},{6,7},{7,6},{8,9},{9,8},{10,11... | collective-permute-start | bytes 1179656 | tf_op jit(solution)/shard_map/ppermute | solution.py:314
  99.0 9.7 %collective-permute-start.20 = (f32[32,3072]{1,0:T(8,128)S(1)}, f32[32,3072]{1,0:T(8,128)S(1)}, u32[]{:S(2)}, u32[]{:S(2)}) collective-permute-start(f32[32,3072]{1,0:T(8,128)S(1)} %get-tuple-element.112.refs_0_), channel_id=1, source_target_pairs={{0,2},{1,3},{2,0},{3,1},{4,6},{5,7},{6,4},{7,5},{8,10},{9,11},{10,... | collective-permute-start | bytes 1179656 | tf_op jit(solution)/shard_map/ppermute | solution.py:317
  100.9 7.9 %collective-permute-start.24 = (f32[32,3072]{1,0:T(8,128)S(1)}, f32[32,3072]{1,0:T(8,128)S(1)}, u32[]{:S(2)}, u32[]{:S(2)}) collective-permute-start(f32[32,3072]{1,0:T(8,128)S(1)} %get-tuple-element.112.refs_0_), channel_id=1, source_target_pairs={{0,1},{1,0},{2,3},{3,2},{4,5},{5,4},{6,7},{7,6},{8,9},{9,8},{10,11... | collective-permute-start | bytes 1179656 | tf_op jit(solution)/shard_map/ppermute | solution.py:314
  108.7 1.7 %collective-permute-start.25 = (f32[32,3072]{1,0:T(8,128)S(1)}, f32[32,3072]{1,0:T(8,128)S(1)}, u32[]{:S(2)}, u32[]{:S(2)}) collective-permute-start(f32[32,3072]{1,0:T(8,128)S(1)} %collective-permute-done.20.refs_1_), channel_id=1, source_target_pairs={{0,1},{1,0},{2,3},{3,2},{4,5},{5,4},{6,7},{7,6},{8,9},{9,8},{10,11... | collective-permute-start | bytes 1179656 | tf_op jit(solution)/shard_map/ppermute | solution.py:314
  114.5 11.2 %collective-permute-start.26 = (f32[32,768]{1,0:T(8,128)S(1)}, f32[32,768]{1,0:T(8,128)S(1)}, u32[]{:S(2)}, u32[]{:S(2)}) collective-permute-start(f32[32,768]{1,0:T(8,128)S(1)} %get-tuple-element.101), channel_id=1, source_target_pairs={{0,12},{4,0},{8,4},{12,8},{1,13},{5,1},{9,5},{13,9},{2,14},{6,2},{... | collective-permute-start | bytes 294920 | tf_op jit(solution)/shard_map/ppermute | solution.py:311
  116.5 10.0 %collective-permute-start.27 = (f32[32,768]{1,0:T(8,128)S(1)}, f32[32,768]{1,0:T(8,128)S(1)}, u32[]{:S(2)}, u32[]{:S(2)}) collective-permute-start(f32[32,768]{1,0:T(8,128)S(1)} %get-tuple-element.102), channel_id=1, source_target_pairs={{0,8},{4,12},{8,0},{12,4},{1,9},{5,13},{9,1},{13,5},{2,10},{6,14},... | collective-permute-start | bytes 294920 | tf_op jit(solution)/shard_map/ppermute | solution.py:311
  116.6 10.0 %collective-permute-start.28 = (f32[32,768]{1,0:T(8,128)S(1)}, f32[32,768]{1,0:T(8,128)S(1)}, u32[]{:S(2)}, u32[]{:S(2)}) collective-permute-start(f32[32,768]{1,0:T(8,128)S(1)} %get-tuple-element.103), channel_id=1, source_target_pairs={{0,4},{4,8},{8,12},{12,0},{1,5},{5,9},{9,13},{13,1},{2,6},{6,10},{... | collective-permute-start | bytes 294920 | tf_op jit(solution)/shard_map/ppermute | solution.py:311
  122.4 5.8 %collective-permute-start.29 = (f32[32,768]{1,0:T(8,128)S(1)}, f32[32,768]{1,0:T(8,128)S(1)}, u32[]{:S(2)}, u32[]{:S(2)}) collective-permute-start(f32[32,768]{1,0:T(8,128)S(1)} %get-tuple-element.105), channel_id=1, source_target_pairs={{0,12},{4,0},{8,4},{12,8},{1,13},{5,1},{9,5},{13,9},{2,14},{6,2},{... | collective-permute-start | bytes 294920 | tf_op jit(solution)/shard_map/ppermute | solution.py:311
  124.6 9.9 %collective-permute-start.30 = (f32[32,768]{1,0:T(8,128)S(1)}, f32[32,768]{1,0:T(8,128)S(1)}, u32[]{:S(2)}, u32[]{:S(2)}) collective-permute-start(f32[32,768]{1,0:T(8,128)S(1)} %get-tuple-element.106), channel_id=1, source_target_pairs={{0,8},{4,12},{8,0},{12,4},{1,9},{5,13},{9,1},{13,5},{2,10},{6,14},... | collective-permute-start | bytes 294920 | tf_op jit(solution)/shard_map/ppermute | solution.py:311
  125.7 8.8 %collective-permute-start.31 = (f32[32,768]{1,0:T(8,128)S(1)}, f32[32,768]{1,0:T(8,128)S(1)}, u32[]{:S(2)}, u32[]{:S(2)}) collective-permute-start(f32[32,768]{1,0:T(8,128)S(1)} %get-tuple-element.107), channel_id=1, source_target_pairs={{0,4},{4,8},{8,12},{12,0},{1,5},{5,9},{9,13},{13,1},{2,6},{6,10},{... | collective-permute-start | bytes 294920 | tf_op jit(solution)/shard_map/ppermute | solution.py:311
  (5 other events, 37.4 us)

commit v11 on v10

--- a/solution.py
+++ b/solution.py
@@ -9,7 +9,6 @@
 from jax.sharding import PartitionSpec as P
 
 VMEM_LIMIT = 5 * 1024 * 1024
-CHUNKS = 2
 SHORT = pl.CostEstimate(flops=1 << 20, bytes_accessed=1 << 18, transcendentals=0)
 
 
@@ -77,7 +76,8 @@
 
 
 def prepare_kernel(rows, columns, block, depth, weight_ref, *refs):
-    high_ref, low_ref, landed, arrived = refs[-4:]
+    *part_refs, landed, arrived = refs
+    width = part_refs[0].shape[1]
     steps = rows[1] // block
 
     def fetch(step):
@@ -95,8 +95,8 @@
         fetch(step).wait()
         high, low = split(landed[lax.rem(step, depth)])
         at = pl.ds(pl.multiple_of(step * block, block), block)
-        high_ref[at, :] = high
-        low_ref[at, :] = low
+        for n, part_ref in enumerate(part_refs):
+            part_ref[at, :] = (low if n % 2 else high)[:, n // 2 * width : (n // 2 + 1) * width]
 
         @pl.when(step + depth < steps)
         def _():
@@ -104,20 +104,20 @@
 
 
 def prepare(weight, rows, columns, after):
-    block = 256 * 1536 // columns[1]
-    block = divisor(rows[1], *[b for b in (256, 128, 64, 32) if b <= max(block, 32)])
+    block = divisor(rows[1], *[b for b in (256, 128, 64, 32) if b <= max(256 * 1536 // columns[1], 32)])
     depth = 4
-    out = pltpu.VMEM((rows[1], columns[1]), jnp.bfloat16)
+    outs = (pltpu.VMEM((rows[1], columns[1] // 2), jnp.bfloat16),) * 4
+    anywhere = pl.BlockSpec(memory_space=pl.ANY)
     return pl.pallas_call(
-        functools.partial(prepare_kernel, rows, columns, block, depth),
-        out_shape=(out, out),
-        in_specs=[pl.BlockSpec(memory_space=pl.ANY)] * (1 + len(after)),
-        out_specs=[pl.BlockSpec(memory_space=pltpu.VMEM)] * 2,
+        lambda weight_ref, *refs: prepare_kernel(rows, columns, block, depth, weight_ref, *refs[len(after) :]),
+        out_shape=outs,
+        in_specs=[anywhere] * (1 + len(after)),
+        out_specs=[pl.BlockSpec(memory_space=pltpu.VMEM)] * 4,
         scratch_shapes=[
             pltpu.VMEM((depth, block, columns[1]), jnp.float32),
             pltpu.SemaphoreType.DMA((depth,)),
         ],
-        compiler_params=pltpu.CompilerParams(vmem_limit_bytes=2 * VMEM_LIMIT),
+        compiler_params=pltpu.CompilerParams(vmem_limit_bytes=VMEM_LIMIT),
         cost_estimate=SHORT,
     )(pltpu.with_memory_space_constraint(weight, pltpu.HBM), *after)
 
@@ -239,7 +239,7 @@
             pltpu.VMEM((depth, width, columns), jnp.float32),
             pltpu.SemaphoreType.DMA((depth,)),
         ],
-        compiler_params=pltpu.CompilerParams(vmem_limit_bytes=2 * VMEM_LIMIT),
+        compiler_params=pltpu.CompilerParams(vmem_limit_bytes=8 * 1024 * 1024),
         cost_estimate=SHORT,
     )(place, *slots, pltpu.with_memory_space_constraint(weight, pltpu.HBM), *earlier, *after)
 
@@ -322,9 +322,16 @@
     def gathered(values):
         return [values] + [along_hid(values, step) for step in range(1, hid_size)]
 
+    def relayed(values):
+        blocks = [values] + [None] * (hid_size - 1)
+        for step in range(1, hid_size // 2 + 1):
+            blocks[step] = along_hid(blocks[step - 1], 1)
+        for step in range(1, hid_size - hid_size // 2):
+            blocks[-step] = along_hid(blocks[(1 - step) % hid_size], -1)
+        return blocks
+
     grads = gathered(out_grad)
-    piece = hidden // CHUNKS
-    quarter = piece // 2
+    third = hidden // 3
 
     def tied(values, others):
         return lax.optimization_barrier((values, others))
@@ -342,13 +349,13 @@
         return arrival, *own
 
     def prepared(c, after):
-        return prepare(in_weight, (0, depth), (c * quarter, quarter), after)
+        return prepare(in_weight, (0, depth), (c * third, third), after)
 
     moments = call(moments_kernel, jax.ShapeDtypeStruct((2 * tokens, 128), jnp.float32), (inputs,), ())
     in_parts = prepared(0, [place, moments])
     in_parts += prepared(1, [in_parts[0]])
     moments = call(
-        functools.partial(merge_kernel, depth), moments, (moments, other_core(moments)), (in_parts[2], *grads[1:])
+        functools.partial(merge_kernel, depth), moments, (moments, other_core(moments)), (in_parts[4], *grads[:0:-1])
     )
     parts = [moments]
     for _ in range(1, chips):
@@ -360,24 +367,23 @@
         (),
     )
     inv_std = inv_std[:, :1]
-    scaled = gathered(scaled)
-    back_0 = stream(grads, out_weight, place, 0, piece, (), [scaled[0]])
+    scaled = relayed(scaled)
+    back_0 = stream(grads, out_weight, place, 0, 2 * third, (), [scaled[0]])
     back_0, (scaled[1], scaled[-1]) = tied(back_0, (scaled[1], scaled[-1]))
     half_0 = halved(back_0)
-    back_1 = stream(grads, out_weight, place, piece, piece, (), [half_0[0]])
+    back_1 = stream(grads, out_weight, place, 2 * third, third, (), [half_0[0]])
     back_0 = exchanged(half_0)
-    back_1, (back_0, scaled) = tied(back_1, (back_0, scaled))
-    in_parts += prepared(2, [back_1[0]])
-    half_1 = halved(back_1, in_parts[4])
+    back_1, scaled = tied(back_1, scaled)
+    pre_0 = forward(scaled, in_parts[:8], place, (), [back_1[0]])
+    half_1 = halved(back_1, (pre_0, back_0[0]))
     back_1 = exchanged(half_1)
-    pre_0 = forward(scaled, in_parts[:4], place, (), [half_1[0]])
-    in_parts += prepared(3, [pre_0[1]])
-    half_0 = halved(pre_0, (in_parts[6], back_1[0]))
-    pre_1 = forward(scaled, in_parts[4:], place, (), [half_0[0]])
+    in_parts += prepared(2, [pre_0[1], half_1[0]])
+    half_0 = halved(pre_0, (in_parts[8], back_1[0]))
+    pre_1 = forward(scaled, in_parts[8:], place, (), [half_0[0]])
     pre_0 = exchanged(half_0)
 
-    def slope_product(c, back, pre):
-        return sum(back) * gelu_slope(sum(pre) + in_bias[c * piece : (c + 1) * piece])
+    def slope_product(bias, back, pre):
+        return sum(back) * gelu_slope(sum(pre) + bias)
 
     def spread_out(act):
         mine = [None] * chips
@@ -387,9 +393,9 @@
             mine[(chips - step) % chips] = act
         return mine
 
-    act_0 = slope_product(0, back_0, pre_0)
+    act_0 = slope_product(in_bias[: 2 * third], back_0, pre_0)
     pre_1 = exchanged(halved(pre_1, act_0))
-    act_1 = slope_product(1, back_1, pre_1)
+    act_1 = slope_product(in_bias[2 * third :], back_1, pre_1)
 
     def both_cores(mine):
         return mine + [other_core(block) for block in mine]
@@ -398,13 +404,13 @@
         return sum([along_hid(sums[step], -step) for step in range(1, hid_size)], start=sums[0])
 
     acts_0, acts_1 = spread_out(act_0), spread_out(act_1)
-    sums = backward(both_cores(acts_0), in_parts[:4], place, (), 0, 1, [pre_1[1]])
+    sums = backward(both_cores(acts_0), in_parts[:8], place, (), 0, 1, [pre_1[1]])
     acts_1[1:], sums = tied(acts_1[1:], sums)
     acts_1 = both_cores(acts_1)
     parts = 2 if depth % 512 == 0 else 1
     ends = []
     for part in range(parts):
-        ends.append(backward(acts_1, in_parts[4:], place, sums, part, parts, [ends[-1][0] if ends else sums[0]]))
+        ends.append(backward(acts_1, in_parts[8:], place, sums, part, parts, [ends[-1][0] if ends else sums[0]]))
     running = jnp.concatenate([summed_along_hid(end) for end in ends], axis=1)
     normed_grad = running * norm_gain
     totals = lax.psum(

time: 142 us -> 141 us (level)
    ppermute x12, waiting for transfers between devices: 15.1 us -> 11.1 us  [along_hid(): lax.ppermute(values, 'hid', [(i, (i + steps) % hid_size) for i in range(h...]
    ppermute x7, waiting for transfers between devices: 23.9 us -> 27.6 us  [next_chip(): lax.ppermute(values, 'emb', [(i, (i + 2) % emb_size) for i in range(emb_s...]
    ppermute x7, starting transfers between devices: 8.68 us -> 7.11 us  [next_chip(): lax.ppermute(values, 'emb', [(i, (i + 2) % emb_size) for i in range(emb_s...]
    pallas_call x4 -> x3, Pallas kernels: 16.8 us -> 16.3 us  [prepare(): pl.pallas_call(lambda weight_ref, *refs: prepare_kernel(rows, columns, bl...]
  transfers between devices with their start and end apart: 32 -> 32, of which waited for: 13 -> 10; matrix products, arithmetic and copies ran while one was open for 1% -> 1% of each run, Pallas kernels for 40% -> 41%
where the time goes in v11:
time: 141 us; the launch traced here: 140 us
  Pallas kernels  61.3 us (43%)
  waiting for transfers between devices  41.6 us (30%)
  starting transfers between devices  28.4 us (20%)
  blocking collectives  5.74 us (4%)
  other arithmetic  1.72 us (1%)
    ppermute x7, waiting for transfers between devices, next_chip(): lax.ppermute(values, 'emb', [(i, (i + 2) % emb_size) for i in range(emb_s...  27.6 us
    ppermute x12, starting transfers between devices, along_hid(): lax.ppermute(values, 'hid', [(i, (i + steps) % hid_size) for i in range(h...  18.9 us
    pallas_call x2, Pallas kernels, stream(): pl.pallas_call(lambda *refs: stream_kernel(first, depth, refs[0], refs[1:...  18.3 us
    pallas_call x3, Pallas kernels, prepare(): pl.pallas_call(lambda weight_ref, *refs: prepare_kernel(rows, columns, bl...  16.3 us
    pallas_call x3, Pallas kernels, backward(): pl.pallas_call(functools.partial(backward_kernel, slots, len(weights) //...  15.3 us
    pallas_call x2, Pallas kernels, forward(): pl.pallas_call(lambda *refs: forward_kernel(refs[0], refs[1:ends[0]], ref...  11.2 us
    ppermute x12, waiting for transfers between devices, along_hid(): lax.ppermute(values, 'hid', [(i, (i + steps) % hid_size) for i in range(h...  11.1 us
    ppermute x7, starting transfers between devices, next_chip(): lax.ppermute(values, 'emb', [(i, (i + 2) % emb_size) for i in range(emb_s...  7.11 us
  transfers between devices with their start and end apart: 32, of which 10 were waited for; matrix products, arithmetic and copies ran while one was open for 1% of the time, Pallas kernels for 41%

profile of v11, /device:TPU:0, one launch (start us, length us, event | category | flops | bytes accessed | tf_op | source)
XLA Modules:
  0.0 140.5 jit_solution(15482789684173776221)
XLA Ops:
  0.0 5.0 %collective-permute-start.1 = (f32[32,1536]{1,0:T(8,128)}, f32[32,1536]{1,0:T(8,128)S(1)}, u32[]{:S(2)}, u32[]{:S(2)}) collective-permute-start(f32[32,1536]{1,0:T(8,128)} %refs_1_.3), channel_id=1, source_target_pairs={{0,12},{4,0},{8,4},{12,8},{1,13},{5,1},{9,5},{13,9},{2,14},{6,2},{... | collective-permute-start | bytes 589832 | tf_op jit(solution)/shard_map/ppermute | solution.py:311
  5.1 1.0 collective-permute-start.3
  7.2 5.4 %shard_map.65 = (bf16[1536,1024]{1,0:T(8,128)(2,1)S(1)}, bf16[1536,1024]{1,0:T(8,128)(2,1)S(1)}, bf16[1536,1024]{1,0:T(8,128)(2,1)S(1)}, bf16[1536,1024]{1,0:T(8,128)(2,1)S(1)}) custom-call(f32[1536,6144]{1,0:T(8,128)} %weight_ref.5, s32[4]{0:T(128)S(1)} %fusion.11.refs_0_.place_ref, f32[64,128]{1,0:T(8,128)S(1)} %shard_map.64.refs_1_.refs_0_), custom_call_target="tpu_custom_call" | custom-call | flops 1048576 | bytes 262144 | tf_op jit(solution)/shard_map/pallas_call | solution.py:111
  12.7 5.4 %shard_map.66 = (bf16[1536,1024]{1,0:T(8,128)(2,1)S(1)}, bf16[1536,1024]{1,0:T(8,128)(2,1)S(1)}, bf16[1536,1024]{1,0:T(8,128)(2,1)S(1)}, bf16[1536,1024]{1,0:T(8,128)(2,1)S(1)}) custom-call(f32[1536,6144]{1,0:T(8,128)} %weight_ref.5, bf16[1536,1024]{1,0:T(8,128)(2,1)S(1)} %get-tuple-element.58.refs_0_.refs_5_.refs_4_), custom_call_target="tpu_custom_call" | custom-call | flops 1048576 | bytes 262144 | tf_op jit(solution)/shard_map/pallas_call | solution.py:111
  18.1 3.8 %collective-permute-done.2.refs_4_.refs_3_ = f32[32,1536]{1,0:T(8,128)S(1)} collective-permute-done((f32[32,1536]{1,0:T(8,128)}, f32[32,1536]{1,0:T(8,128)S(1)}, u32[]{:S(2)}, u32[]{:S(2)}) %collective-permute-start.2) | collective-permute-done | bytes 196640 | tf_op jit(solution)/shard_map/ppermute | solution.py:311
  22.0 1.6 %collective-permute-start.4 = (f32[64,128]{1,0:T(8,128)S(1)}, f32[64,128]{1,0:T(8,128)S(1)}, u32[]{:S(2)}, u32[]{:S(2)}) collective-permute-start(f32[64,128]{1,0:T(8,128)S(1)} %shard_map.67.refs_2_), channel_id=1, source_target_pairs={{0,2},{1,3},{2,0},{3,1},{4,6},{5,7},{6,4},{7,5},{8,10},{9,11},{10,... | collective-permute-start | bytes 98312 | tf_op jit(solution)/shard_map/ppermute | solution.py:317
  23.5 2.4 %collective-permute-done.4.refs_3_ = f32[64,128]{1,0:T(8,128)S(1)} collective-permute-done((f32[64,128]{1,0:T(8,128)S(1)}, f32[64,128]{1,0:T(8,128)S(1)}, u32[]{:S(2)}, u32[]{:S(2)}) %collective-permute-start.4) | collective-permute-done | bytes 32800 | tf_op jit(solution)/shard_map/ppermute | solution.py:317
  26.1 1.0 collective-permute-start.5
  27.1 2.8 %collective-permute-start.6 = (f32[32,1536]{1,0:T(8,128)S(1)}, f32[32,1536]{1,0:T(8,128)S(1)}, u32[]{:S(2)}, u32[]{:S(2)}) collective-permute-start(f32[32,1536]{1,0:T(8,128)S(1)} %get-tuple-element.72.refs_6_.refs_1_), channel_id=1, source_target_pairs={{0,12},{4,0},{8,4},{12,8},{1,13},{5,1},{9,5},{13,9},{2,14},{6,2},{... | collective-permute-start | bytes 589832 | tf_op jit(solution)/shard_map/ppermute | solution.py:311
  30.0 11.5 %shard_map.69 = (f32[64,4096]{1,0:T(8,128)S(1)}, f32[64,4096]{1,0:T(8,128)S(1)}) custom-call(s32[4]{0:T(128)S(1)} %fusion.11.refs_0_.place_ref, f32[32,1536]{1,0:T(8,128)S(1)} %copy-done.2, f32[32,1536]{1,0:T(8,128)S(1)} %collective-permute-done.3.refs_5_.refs_2_, f32[32,1536]{1,0:T(8,128)S(1)} %collective-permute-done.2.refs_4_.refs_3_, ...), custom_call_target="tpu_custom_call" | custom-call | flops 1048576 | bytes 262144 | tf_op jit(solution)/shard_map/pallas_call | solution.py:226
  41.8 1.8 %collective-permute-done.7 = f32[32,4096]{1,0:T(8,128)S(1)} collective-permute-done((f32[32,4096]{1,0:T(8,128)S(1)}, f32[32,4096]{1,0:T(8,128)S(1)}, u32[]{:S(2)}, u32[]{:S(2)}) %collective-permute-start.7) | collective-permute-done | bytes 524320 | tf_op jit(solution)/shard_map/ppermute | solution.py:314
  43.7 1.6 %collective-permute-start.10 = (f32[32,4096]{1,0:T(8,128)S(1)}, f32[32,4096]{1,0:T(8,128)S(1)}, u32[]{:S(2)}, u32[]{:S(2)}) collective-permute-start(f32[32,4096]{1,0:T(8,128)S(1)} %slice_add_fusion.1.refs_6_), channel_id=1, source_target_pairs={{0,2},{1,3},{2,0},{3,1},{4,6},{5,7},{6,4},{7,5},{8,10},{9,11},{10,... | collective-permute-start | bytes 1572872 | tf_op jit(solution)/shard_map/ppermute | solution.py:317
  45.2 6.8 %shard_map.70 = (f32[64,2048]{1,0:T(8,128)S(1)}, f32[64,2048]{1,0:T(8,128)S(1)}) custom-call(s32[4]{0:T(128)S(1)} %fusion.11.refs_0_.place_ref, f32[32,1536]{1,0:T(8,128)S(1)} %copy-done.2, f32[32,1536]{1,0:T(8,128)S(1)} %collective-permute-done.3.refs_5_.refs_2_, f32[32,1536]{1,0:T(8,128)S(1)} %collective-permute-done.2.refs_4_.refs_3_, ...), custom_call_target="tpu_custom_call" | custom-call | flops 1048576 | bytes 262144 | tf_op jit(solution)/shard_map/pallas_call | solution.py:226
  52.1 7.3 %shard_map.71 = (f32[64,4096]{1,0:T(8,128)S(1)}, f32[64,4096]{1,0:T(8,128)S(1)}) custom-call(s32[4]{0:T(128)S(1)} %fusion.11.refs_0_.place_ref, f32[32,1536]{1,0:T(8,128)S(1)} %get-tuple-element.72.refs_6_.refs_1_, f32[32,1536]{1,0:T(8,128)S(1)} %collective-permute-done.5.refs_2_, f32[32,1536]{1,0:T(8,128)S(1)} %collective-permute-done.8.refs_3_, ...), custom_call_target="tpu_custom_call" | custom-call | flops 1048576 | bytes 262144 | tf_op jit(solution)/shard_map/pallas_call | solution.py:178
  61.2 5.4 %shard_map.72 = (bf16[1536,1024]{1,0:T(8,128)(2,1)S(1)}, bf16[1536,1024]{1,0:T(8,128)(2,1)S(1)}, bf16[1536,1024]{1,0:T(8,128)(2,1)S(1)}, bf16[1536,1024]{1,0:T(8,128)(2,1)S(1)}) custom-call(f32[1536,6144]{1,0:T(8,128)} %weight_ref.5, f32[64,4096]{1,0:T(8,128)S(1)} %get-tuple-element.83.refs_0_, f32[32,2048]{1,0:T(8,128)S(1)} %slice_add_fusion.3.refs_1_), custom_call_target="tpu_custom_call" | custom-call | flops 1048576 | bytes 262144 | tf_op jit(solution)/shard_map/pallas_call | solution.py:111
  66.6 1.8 %collective-permute-done.11 = f32[32,2048]{1,0:T(8,128)S(1)} collective-permute-done((f32[32,2048]{1,0:T(8,128)S(1)}, f32[32,2048]{1,0:T(8,128)S(1)}, u32[]{:S(2)}, u32[]{:S(2)}) %collective-permute-start.11) | collective-permute-done | bytes 262176 | tf_op jit(solution)/shard_map/ppermute | solution.py:317
  69.0 3.9 %shard_map.73 = (f32[64,2048]{1,0:T(8,128)S(1)}, f32[64,2048]{1,0:T(8,128)S(1)}) custom-call(s32[4]{0:T(128)S(1)} %fusion.11.refs_0_.place_ref, f32[32,1536]{1,0:T(8,128)S(1)} %get-tuple-element.72.refs_6_.refs_1_, f32[32,1536]{1,0:T(8,128)S(1)} %collective-permute-done.5.refs_2_, f32[32,1536]{1,0:T(8,128)S(1)} %collective-permute-done.8.refs_3_, ...), custom_call_target="tpu_custom_call" | custom-call | flops 1048576 | bytes 262144 | tf_op jit(solution)/shard_map/pallas_call | solution.py:178
  73.7 7.8 %collective-permute-done.16 = f32[32,4096]{1,0:T(8,128)S(1)} collective-permute-done((f32[32,4096]{1,0:T(8,128)S(1)}, f32[32,4096]{1,0:T(8,128)S(1)}, u32[]{:S(2)}, u32[]{:S(2)}) %collective-permute-start.16) | collective-permute-done | bytes 524320 | tf_op jit(solution)/shard_map/ppermute | solution.py:317
  82.5 1.5 %collective-permute-start.18 = (f32[32,2048]{1,0:T(8,128)S(1)}, f32[32,2048]{1,0:T(8,128)S(1)}, u32[]{:S(2)}, u32[]{:S(2)}) collective-permute-start(f32[32,2048]{1,0:T(8,128)S(1)} %slice_add_fusion.2), channel_id=1, source_target_pairs={{0,2},{1,3},{2,0},{3,1},{4,6},{5,7},{6,4},{7,5},{8,10},{9,11},{10,... | collective-permute-start | bytes 786440 | tf_op jit(solution)/shard_map/ppermute | solution.py:317
  84.0 12.7 %collective-permute-done.21.refs_1_ = f32[32,4096]{1,0:T(8,128)S(1)} collective-permute-done((f32[32,4096]{1,0:T(8,128)S(1)}, f32[32,4096]{1,0:T(8,128)S(1)}, u32[]{:S(2)}, u32[]{:S(2)}) %collective-permute-start.21) | collective-permute-done | bytes 524320 | tf_op jit(solution)/shard_map/ppermute | solution.py:317
  96.8 2.8 %collective-permute-done.18 = f32[32,2048]{1,0:T(8,128)S(1)} collective-permute-done((f32[32,2048]{1,0:T(8,128)S(1)}, f32[32,2048]{1,0:T(8,128)S(1)}, u32[]{:S(2)}, u32[]{:S(2)}) %collective-permute-start.18) | collective-permute-done | bytes 262176 | tf_op jit(solution)/shard_map/ppermute | solution.py:317
  100.5 9.2 %shard_map.74 = (f32[32,1536]{1,0:T(8,128)S(1)}, f32[32,1536]{1,0:T(8,128)S(1)}, f32[32,1536]{1,0:T(8,128)S(1)}, f32[32,1536]{1,0:T(8,128)S(1)}) custom-call(s32[4]{0:T(128)S(1)} %fusion.11.refs_0_.place_ref, f32[32,4096]{1,0:T(8,128)S(1)} %fusion.4.refs_0_, f32[32,4096]{1,0:T(8,128)S(1)} %collective-permute-done.21.refs_1_, ...), custom_call_target="tpu_custom_call" | custom-call | flops 1048576 | bytes 262144 | tf_op jit(solution)/shard_map/pallas_call | solution.py:286
  110.3 1.2 collective-permute-done.25.refs_3_
  111.4 3.0 %shard_map.75 = (f32[32,768]{1,0:T(8,128)S(1)}, f32[32,768]{1,0:T(8,128)S(1)}, f32[32,768]{1,0:T(8,128)S(1)}, f32[32,768]{1,0:T(8,128)S(1)}) custom-call(s32[4]{0:T(128)S(1)} %fusion.11.refs_0_.place_ref, f32[32,2048]{1,0:T(8,128)S(1)} %get-tuple-element.118.refs_0_, f32[32,2048]{1,0:T(8,128)S(1)} %collective-permute-done.20.refs_1_, ...), custom_call_target="tpu_custom_call" | custom-call | flops 1048576 | bytes 262144 | tf_op jit(solution)/shard_map/pallas_call | solution.py:286
  114.5 2.6 %collective-permute-start.27 = (f32[32,768]{1,0:T(8,128)S(1)}, f32[32,768]{1,0:T(8,128)S(1)}, u32[]{:S(2)}, u32[]{:S(2)}) collective-permute-start(f32[32,768]{1,0:T(8,128)S(1)} %get-tuple-element.104), channel_id=1, source_target_pairs={{0,8},{4,12},{8,0},{12,4},{1,9},{5,13},{9,1},{13,5},{2,10},{6,14},... | collective-permute-start | bytes 294920 | tf_op jit(solution)/shard_map/ppermute | solution.py:311
  117.1 1.4 collective-permute-start.26
  118.6 3.0 %shard_map.76 = (f32[32,768]{1,0:T(8,128)S(1)}, f32[32,768]{1,0:T(8,128)S(1)}, f32[32,768]{1,0:T(8,128)S(1)}, f32[32,768]{1,0:T(8,128)S(1)}) custom-call(s32[4]{0:T(128)S(1)} %fusion.11.refs_0_.place_ref, f32[32,2048]{1,0:T(8,128)S(1)} %get-tuple-element.118.refs_0_, f32[32,2048]{1,0:T(8,128)S(1)} %collective-permute-done.20.refs_1_, ...), custom_call_target="tpu_custom_call" | custom-call | flops 1048576 | bytes 262144 | tf_op jit(solution)/shard_map/pallas_call | solution.py:286
  122.3 1.4 collective-permute-start.30
  123.6 2.8 %collective-permute-start.29 = (f32[32,768]{1,0:T(8,128)S(1)}, f32[32,768]{1,0:T(8,128)S(1)}, u32[]{:S(2)}, u32[]{:S(2)}) collective-permute-start(f32[32,768]{1,0:T(8,128)S(1)} %get-tuple-element.107), channel_id=1, source_target_pairs={{0,12},{4,0},{8,4},{12,8},{1,13},{5,1},{9,5},{13,9},{2,14},{6,2},{... | collective-permute-start | bytes 294920 | tf_op jit(solution)/shard_map/ppermute | solution.py:311
  126.5 2.6 %collective-permute-done.31 = f32[32,768]{1,0:T(8,128)S(1)} collective-permute-done((f32[32,768]{1,0:T(8,128)S(1)}, f32[32,768]{1,0:T(8,128)S(1)}, u32[]{:S(2)}, u32[]{:S(2)}) %collective-permute-start.31) | collective-permute-done | bytes 98336 | tf_op jit(solution)/shard_map/ppermute | solution.py:311
  129.1 4.6 %collective-permute-done.30 = f32[32,768]{1,0:T(8,128)S(1)} collective-permute-done((f32[32,768]{1,0:T(8,128)S(1)}, f32[32,768]{1,0:T(8,128)S(1)}, u32[]{:S(2)}, u32[]{:S(2)}) %collective-permute-start.30) | collective-permute-done | bytes 98336 | tf_op jit(solution)/shard_map/ppermute | solution.py:311
  133.9 5.7 %psum.7 = f32[2,32]{1,0:T(2,128)S(1)} all-reduce(f32[2,32]{1,0:T(2,128)S(1)} %pad_maximum_fusion), channel_id=1, replica_groups=mesh['groups'=2,'hid'=4,'emb'=4] {'emb'}, use_global_device_ids=true, to_apply=%region_2.3 | all-reduce | flops 64 | bytes 512 | tf_op jit(solution)/shard_map/psum | solution.py:416
  (78 shorter events, 9.1 us)
Async XLA Ops:
  0.0 18.1 %collective-permute-start.1 = (f32[32,1536]{1,0:T(8,128)}, f32[32,1536]{1,0:T(8,128)S(1)}, u32[]{:S(2)}, u32[]{:S(2)}) collective-permute-start(f32[32,1536]{1,0:T(8,128)} %refs_1_.3), channel_id=1, source_target_pairs={{0,12},{4,0},{8,4},{12,8},{1,13},{5,1},{9,5},{13,9},{2,14},{6,2},{... | collective-permute-start | bytes 589832 | tf_op jit(solution)/shard_map/ppermute | solution.py:311
  5.0 16.9 %collective-permute-start.2 = (f32[32,1536]{1,0:T(8,128)}, f32[32,1536]{1,0:T(8,128)S(1)}, u32[]{:S(2)}, u32[]{:S(2)}) collective-permute-start(f32[32,1536]{1,0:T(8,128)} %refs_1_.3), channel_id=1, source_target_pairs={{0,8},{4,12},{8,0},{12,4},{1,9},{5,13},{9,1},{13,5},{2,10},{6,14},... | collective-permute-start | bytes 589832 | tf_op jit(solution)/shard_map/ppermute | solution.py:311
  5.1 16.9 %collective-permute-start.3 = (f32[32,1536]{1,0:T(8,128)}, f32[32,1536]{1,0:T(8,128)S(1)}, u32[]{:S(2)}, u32[]{:S(2)}) collective-permute-start(f32[32,1536]{1,0:T(8,128)} %refs_1_.3), channel_id=1, source_target_pairs={{0,4},{4,8},{8,12},{12,0},{1,5},{5,9},{9,13},{13,1},{2,6},{6,10},{... | collective-permute-start | bytes 589832 | tf_op jit(solution)/shard_map/ppermute | solution.py:311
  7.2 10.9 %collective-permute-start = (f32[64,128]{1,0:T(8,128)S(1)}, f32[64,128]{1,0:T(8,128)S(1)}, u32[]{:S(2)}, u32[]{:S(2)}) collective-permute-start(f32[64,128]{1,0:T(8,128)S(1)} %shard_map.64.refs_1_.refs_0_), channel_id=1, source_target_pairs={{0,1},{1,0},{2,3},{3,2},{4,5},{5,4},{6,7},{7,6},{8,9},{9,8},{10,11... | collective-permute-start | bytes 98312 | tf_op jit(solution)/shard_map/ppermute | solution.py:314
  22.0 4.0 %collective-permute-start.4 = (f32[64,128]{1,0:T(8,128)S(1)}, f32[64,128]{1,0:T(8,128)S(1)}, u32[]{:S(2)}, u32[]{:S(2)}) collective-permute-start(f32[64,128]{1,0:T(8,128)S(1)} %shard_map.67.refs_2_), channel_id=1, source_target_pairs={{0,2},{1,3},{2,0},{3,1},{4,6},{5,7},{6,4},{7,5},{8,10},{9,11},{10,... | collective-permute-start | bytes 98312 | tf_op jit(solution)/shard_map/ppermute | solution.py:317
  26.1 15.4 %collective-permute-start.5 = (f32[32,1536]{1,0:T(8,128)S(1)}, f32[32,1536]{1,0:T(8,128)S(1)}, u32[]{:S(2)}, u32[]{:S(2)}) collective-permute-start(f32[32,1536]{1,0:T(8,128)S(1)} %get-tuple-element.72.refs_6_.refs_1_), channel_id=1, source_target_pairs={{0,4},{4,8},{8,12},{12,0},{1,5},{5,9},{9,13},{13,1},{2,6},{6,10},{... | collective-permute-start | bytes 589832 | tf_op jit(solution)/shard_map/ppermute | solution.py:311
  27.1 14.4 %collective-permute-start.6 = (f32[32,1536]{1,0:T(8,128)S(1)}, f32[32,1536]{1,0:T(8,128)S(1)}, u32[]{:S(2)}, u32[]{:S(2)}) collective-permute-start(f32[32,1536]{1,0:T(8,128)S(1)} %get-tuple-element.72.refs_6_.refs_1_), channel_id=1, source_target_pairs={{0,12},{4,0},{8,4},{12,8},{1,13},{5,1},{9,5},{13,9},{2,14},{6,2},{... | collective-permute-start | bytes 589832 | tf_op jit(solution)/shard_map/ppermute | solution.py:311
  41.6 2.0 %collective-permute-start.7 = (f32[32,4096]{1,0:T(8,128)S(1)}, f32[32,4096]{1,0:T(8,128)S(1)}, u32[]{:S(2)}, u32[]{:S(2)}) collective-permute-start(f32[32,4096]{1,0:T(8,128)S(1)} %get-tuple-element.114), channel_id=1, source_target_pairs={{0,1},{1,0},{2,3},{3,2},{4,5},{5,4},{6,7},{7,6},{8,9},{9,8},{10,11... | collective-permute-start | bytes 1572872 | tf_op jit(solution)/shard_map/ppermute | solution.py:314
  41.7 10.3 %collective-permute-start.8 = (f32[32,1536]{1,0:T(8,128)S(1)}, f32[32,1536]{1,0:T(8,128)S(1)}, u32[]{:S(2)}, u32[]{:S(2)}) collective-permute-start(f32[32,1536]{1,0:T(8,128)S(1)} %collective-permute-done.5.refs_2_), channel_id=1, source_target_pairs={{0,4},{4,8},{8,12},{12,0},{1,5},{5,9},{9,13},{13,1},{2,6},{6,10},{... | collective-permute-start | bytes 589832 | tf_op jit(solution)/shard_map/ppermute | solution.py:311
  43.7 16.4 %collective-permute-start.10 = (f32[32,4096]{1,0:T(8,128)S(1)}, f32[32,4096]{1,0:T(8,128)S(1)}, u32[]{:S(2)}, u32[]{:S(2)}) collective-permute-start(f32[32,4096]{1,0:T(8,128)S(1)} %slice_add_fusion.1.refs_6_), channel_id=1, source_target_pairs={{0,2},{1,3},{2,0},{3,1},{4,6},{5,7},{6,4},{7,5},{8,10},{9,11},{10,... | collective-permute-start | bytes 1572872 | tf_op jit(solution)/shard_map/ppermute | solution.py:317
  52.0 8.0 %collective-permute-start.9 = (f32[32,2048]{1,0:T(8,128)S(1)}, f32[32,2048]{1,0:T(8,128)S(1)}, u32[]{:S(2)}, u32[]{:S(2)}) collective-permute-start(f32[32,2048]{1,0:T(8,128)S(1)} %get-tuple-element.120), channel_id=1, source_target_pairs={{0,1},{1,0},{2,3},{3,2},{4,5},{5,4},{6,7},{7,6},{8,9},{9,8},{10,11... | collective-permute-start | bytes 786440 | tf_op jit(solution)/shard_map/ppermute | solution.py:314
  59.5 7.1 %collective-permute-start.13 = (f32[32,4096]{1,0:T(8,128)S(1)}, f32[32,4096]{1,0:T(8,128)S(1)}, u32[]{:S(2)}, u32[]{:S(2)}) collective-permute-start(f32[32,4096]{1,0:T(8,128)S(1)} %get-tuple-element.116), channel_id=1, source_target_pairs={{0,1},{1,0},{2,3},{3,2},{4,5},{5,4},{6,7},{7,6},{8,9},{9,8},{10,11... | collective-permute-start | bytes 1572872 | tf_op jit(solution)/shard_map/ppermute | solution.py:314
  60.1 8.3 %collective-permute-start.11 = (f32[32,2048]{1,0:T(8,128)S(1)}, f32[32,2048]{1,0:T(8,128)S(1)}, u32[]{:S(2)}, u32[]{:S(2)}) collective-permute-start(f32[32,2048]{1,0:T(8,128)S(1)} %slice_add_fusion.3.refs_1_), channel_id=1, source_target_pairs={{0,2},{1,3},{2,0},{3,1},{4,6},{5,7},{6,4},{7,5},{8,10},{9,11},{10,... | collective-permute-start | bytes 786440 | tf_op jit(solution)/shard_map/ppermute | solution.py:317
  60.7 12.9 %collective-permute-start.15 = (f32[32,4096]{1,0:T(8,128)S(1)}, f32[32,4096]{1,0:T(8,128)S(1)}, u32[]{:S(2)}, u32[]{:S(2)}) collective-permute-start(f32[32,4096]{1,0:T(8,128)S(1)} %get-tuple-element.113), channel_id=1, source_target_pairs={{0,1},{1,0},{2,3},{3,2},{4,5},{5,4},{6,7},{7,6},{8,9},{9,8},{10,11... | collective-permute-start | bytes 1572872 | tf_op jit(solution)/shard_map/ppermute | solution.py:314
  60.7 13.0 %collective-permute-start.17 = (f32[32,4096]{1,0:T(8,128)S(1)}, f32[32,4096]{1,0:T(8,128)S(1)}, u32[]{:S(2)}, u32[]{:S(2)}) collective-permute-start(f32[32,4096]{1,0:T(8,128)S(1)} %get-tuple-element.115), channel_id=1, source_target_pairs={{0,1},{1,0},{2,3},{3,2},{4,5},{5,4},{6,7},{7,6},{8,9},{9,8},{10,11... | collective-permute-start | bytes 1572872 | tf_op jit(solution)/shard_map/ppermute | solution.py:314
  68.4 13.1 %collective-permute-start.16 = (f32[32,4096]{1,0:T(8,128)S(1)}, f32[32,4096]{1,0:T(8,128)S(1)}, u32[]{:S(2)}, u32[]{:S(2)}) collective-permute-start(f32[32,4096]{1,0:T(8,128)S(1)} %slice_add_fusion.refs_9_), channel_id=1, source_target_pairs={{0,2},{1,3},{2,0},{3,1},{4,6},{5,7},{6,4},{7,5},{8,10},{9,11},{10,... | collective-permute-start | bytes 1572872 | tf_op jit(solution)/shard_map/ppermute | solution.py:317
  69.0 27.7 %collective-permute-start.12 = (f32[32,2048]{1,0:T(8,128)S(1)}, f32[32,2048]{1,0:T(8,128)S(1)}, u32[]{:S(2)}, u32[]{:S(2)}) collective-permute-start(f32[32,2048]{1,0:T(8,128)S(1)} %get-tuple-element.119), channel_id=1, source_target_pairs={{0,1},{1,0},{2,3},{3,2},{4,5},{5,4},{6,7},{7,6},{8,9},{9,8},{10,11... | collective-permute-start | bytes 786440 | tf_op jit(solution)/shard_map/ppermute | solution.py:314
  73.0 23.7 %collective-permute-start.19 = (f32[32,2048]{1,0:T(8,128)S(1)}, f32[32,2048]{1,0:T(8,128)S(1)}, u32[]{:S(2)}, u32[]{:S(2)}) collective-permute-start(f32[32,2048]{1,0:T(8,128)S(1)} %get-tuple-element.122), channel_id=1, source_target_pairs={{0,1},{1,0},{2,3},{3,2},{4,5},{5,4},{6,7},{7,6},{8,9},{9,8},{10,11... | collective-permute-start | bytes 786440 | tf_op jit(solution)/shard_map/ppermute | solution.py:314
  73.6 8.8 %collective-permute-start.14 = (f32[32,2048]{1,0:T(8,128)S(1)}, f32[32,2048]{1,0:T(8,128)S(1)}, u32[]{:S(2)}, u32[]{:S(2)}) collective-permute-start(f32[32,2048]{1,0:T(8,128)S(1)} %get-tuple-element.121), channel_id=1, source_target_pairs={{0,1},{1,0},{2,3},{3,2},{4,5},{5,4},{6,7},{7,6},{8,9},{9,8},{10,11... | collective-permute-start | bytes 786440 | tf_op jit(solution)/shard_map/ppermute | solution.py:314
  81.8 14.9 %collective-permute-start.21 = (f32[32,4096]{1,0:T(8,128)S(1)}, f32[32,4096]{1,0:T(8,128)S(1)}, u32[]{:S(2)}, u32[]{:S(2)}) collective-permute-start(f32[32,4096]{1,0:T(8,128)S(1)} %fusion.4.refs_0_), channel_id=1, source_target_pairs={{0,2},{1,3},{2,0},{3,1},{4,6},{5,7},{6,4},{7,5},{8,10},{9,11},{10,... | collective-permute-start | bytes 1572872 | tf_op jit(solution)/shard_map/ppermute | solution.py:317
  82.5 17.1 %collective-permute-start.18 = (f32[32,2048]{1,0:T(8,128)S(1)}, f32[32,2048]{1,0:T(8,128)S(1)}, u32[]{:S(2)}, u32[]{:S(2)}) collective-permute-start(f32[32,2048]{1,0:T(8,128)S(1)} %slice_add_fusion.2), channel_id=1, source_target_pairs={{0,2},{1,3},{2,0},{3,1},{4,6},{5,7},{6,4},{7,5},{8,10},{9,11},{10,... | collective-permute-start | bytes 786440 | tf_op jit(solution)/shard_map/ppermute | solution.py:317
  84.0 16.4 %collective-permute-start.22 = (f32[32,4096]{1,0:T(8,128)S(1)}, f32[32,4096]{1,0:T(8,128)S(1)}, u32[]{:S(2)}, u32[]{:S(2)}) collective-permute-start(f32[32,4096]{1,0:T(8,128)S(1)} %fusion.4.refs_0_), channel_id=1, source_target_pairs={{0,1},{1,0},{2,3},{3,2},{4,5},{5,4},{6,7},{7,6},{8,9},{9,8},{10,11... | collective-permute-start | bytes 1572872 | tf_op jit(solution)/shard_map/ppermute | solution.py:314
  96.8 3.7 %collective-permute-start.23 = (f32[32,4096]{1,0:T(8,128)S(1)}, f32[32,4096]{1,0:T(8,128)S(1)}, u32[]{:S(2)}, u32[]{:S(2)}) collective-permute-start(f32[32,4096]{1,0:T(8,128)S(1)} %collective-permute-done.21.refs_1_), channel_id=1, source_target_pairs={{0,1},{1,0},{2,3},{3,2},{4,5},{5,4},{6,7},{7,6},{8,9},{9,8},{10,11... | collective-permute-start | bytes 1572872 | tf_op jit(solution)/shard_map/ppermute | solution.py:314
  99.8 9.9 %collective-permute-start.20 = (f32[32,2048]{1,0:T(8,128)S(1)}, f32[32,2048]{1,0:T(8,128)S(1)}, u32[]{:S(2)}, u32[]{:S(2)}) collective-permute-start(f32[32,2048]{1,0:T(8,128)S(1)} %get-tuple-element.118.refs_0_), channel_id=1, source_target_pairs={{0,2},{1,3},{2,0},{3,1},{4,6},{5,7},{6,4},{7,5},{8,10},{9,11},{10,... | collective-permute-start | bytes 786440 | tf_op jit(solution)/shard_map/ppermute | solution.py:317
  100.4 9.8 %collective-permute-start.24 = (f32[32,2048]{1,0:T(8,128)S(1)}, f32[32,2048]{1,0:T(8,128)S(1)}, u32[]{:S(2)}, u32[]{:S(2)}) collective-permute-start(f32[32,2048]{1,0:T(8,128)S(1)} %get-tuple-element.118.refs_0_), channel_id=1, source_target_pairs={{0,1},{1,0},{2,3},{3,2},{4,5},{5,4},{6,7},{7,6},{8,9},{9,8},{10,11... | collective-permute-start | bytes 786440 | tf_op jit(solution)/shard_map/ppermute | solution.py:314
  109.7 1.7 %collective-permute-start.25 = (f32[32,2048]{1,0:T(8,128)S(1)}, f32[32,2048]{1,0:T(8,128)S(1)}, u32[]{:S(2)}, u32[]{:S(2)}) collective-permute-start(f32[32,2048]{1,0:T(8,128)S(1)} %collective-permute-done.20.refs_1_), channel_id=1, source_target_pairs={{0,1},{1,0},{2,3},{3,2},{4,5},{5,4},{6,7},{7,6},{8,9},{9,8},{10,11... | collective-permute-start | bytes 786440 | tf_op jit(solution)/shard_map/ppermute | solution.py:314
  114.4 9.2 %collective-permute-start.28 = (f32[32,768]{1,0:T(8,128)S(1)}, f32[32,768]{1,0:T(8,128)S(1)}, u32[]{:S(2)}, u32[]{:S(2)}) collective-permute-start(f32[32,768]{1,0:T(8,128)S(1)} %get-tuple-element.105), channel_id=1, source_target_pairs={{0,4},{4,8},{8,12},{12,0},{1,5},{5,9},{9,13},{13,1},{2,6},{6,10},{... | collective-permute-start | bytes 294920 | tf_op jit(solution)/shard_map/ppermute | solution.py:311
  114.5 12.0 %collective-permute-start.27 = (f32[32,768]{1,0:T(8,128)S(1)}, f32[32,768]{1,0:T(8,128)S(1)}, u32[]{:S(2)}, u32[]{:S(2)}) collective-permute-start(f32[32,768]{1,0:T(8,128)S(1)} %get-tuple-element.104), channel_id=1, source_target_pairs={{0,8},{4,12},{8,0},{12,4},{1,9},{5,13},{9,1},{13,5},{2,10},{6,14},... | collective-permute-start | bytes 294920 | tf_op jit(solution)/shard_map/ppermute | solution.py:311
  117.1 9.4 %collective-permute-start.26 = (f32[32,768]{1,0:T(8,128)S(1)}, f32[32,768]{1,0:T(8,128)S(1)}, u32[]{:S(2)}, u32[]{:S(2)}) collective-permute-start(f32[32,768]{1,0:T(8,128)S(1)} %get-tuple-element.103), channel_id=1, source_target_pairs={{0,12},{4,0},{8,4},{12,8},{1,13},{5,1},{9,5},{13,9},{2,14},{6,2},{... | collective-permute-start | bytes 294920 | tf_op jit(solution)/shard_map/ppermute | solution.py:311
  121.6 7.6 %collective-permute-start.31 = (f32[32,768]{1,0:T(8,128)S(1)}, f32[32,768]{1,0:T(8,128)S(1)}, u32[]{:S(2)}, u32[]{:S(2)}) collective-permute-start(f32[32,768]{1,0:T(8,128)S(1)} %get-tuple-element.109), channel_id=1, source_target_pairs={{0,4},{4,8},{8,12},{12,0},{1,5},{5,9},{9,13},{13,1},{2,6},{6,10},{... | collective-permute-start | bytes 294920 | tf_op jit(solution)/shard_map/ppermute | solution.py:311
  122.3 11.5 %collective-permute-start.30 = (f32[32,768]{1,0:T(8,128)S(1)}, f32[32,768]{1,0:T(8,128)S(1)}, u32[]{:S(2)}, u32[]{:S(2)}) collective-permute-start(f32[32,768]{1,0:T(8,128)S(1)} %get-tuple-element.108), channel_id=1, source_target_pairs={{0,8},{4,12},{8,0},{12,4},{1,9},{5,13},{9,1},{13,5},{2,10},{6,14},... | collective-permute-start | bytes 294920 | tf_op jit(solution)/shard_map/ppermute | solution.py:311
  123.6 10.1 %collective-permute-start.29 = (f32[32,768]{1,0:T(8,128)S(1)}, f32[32,768]{1,0:T(8,128)S(1)}, u32[]{:S(2)}, u32[]{:S(2)}) collective-permute-start(f32[32,768]{1,0:T(8,128)S(1)} %get-tuple-element.107), channel_id=1, source_target_pairs={{0,12},{4,0},{8,4},{12,8},{1,13},{5,1},{9,5},{13,9},{2,14},{6,2},{... | collective-permute-start | bytes 294920 | tf_op jit(solution)/shard_map/ppermute | solution.py:311
  (6 other events, 65.2 us)

commit v12 on v11

--- a/solution.py
+++ b/solution.py
@@ -133,17 +133,14 @@
     return first[:rows] + first[rows:] + dot(both[:rows, :], low)
 
 
-def fill(both, block_refs, place_ref):
+def fill(both, block_refs, place_ref, rows):
+    first, count = rows
     total = both.shape[0] // 2
-    block = total // place_ref.shape[0]
-    index = 0
-    for ref in block_refs:
-        for start in range(0, ref.shape[0], block):
-            high, low = split(ref[start : start + block, :])
-            row = pl.multiple_of(place_ref[index] * block, block)
-            both[pl.ds(row, block), :] = high
-            both[pl.ds(total + row, block), :] = low
-            index += 1
+    for index, ref in enumerate(block_refs):
+        high, low = split(ref[first : first + count, :])
+        row = pl.multiple_of(place_ref[index] * count, count)
+        both[pl.ds(row, count), :] = high
+        both[pl.ds(total + row, count), :] = low
 
 
 def follow(earlier_refs, out_refs):
@@ -152,9 +149,21 @@
     return earlier_refs[0].shape[1] if earlier_refs else 0
 
 
-def forward_kernel(place_ref, slot_refs, weight_refs, earlier_refs, send_ref, keep_ref, both):
-    fill(both, slot_refs, place_ref)
-    half, column = send_ref.shape[0], follow(earlier_refs, (send_ref, keep_ref))
+def put(out_refs, at, value):
+    row = 0
+    for out_ref in out_refs:
+        out_ref[:, at] = value[row : row + out_ref.shape[0]]
+        row += out_ref.shape[0]
+
+
+def parts_of(tokens, chips, hidden):
+    block = tokens // (2 * chips)
+    return [jax.ShapeDtypeStruct((n, hidden), jnp.float32) for n in (block, block * (chips - 1))] * 2
+
+
+def forward_kernel(rows, place_ref, slot_refs, weight_refs, earlier_refs, out_refs, both):
+    fill(both, slot_refs, place_ref, rows)
+    column = follow(earlier_refs, out_refs)
     for high_ref, low_ref in zip(weight_refs[::2], weight_refs[1::2]):
         width = divisor(high_ref.shape[1], 256, 128)
 
@@ -162,37 +171,32 @@
         def _(step):
             at = pl.ds(pl.multiple_of(step * width, width), width)
             part = three_pass(both, high_ref[:, at], low_ref[:, at], 0)
-            at = pl.ds(pl.multiple_of(column + step * width, width), width)
-            keep_ref[:, at] = part[:half]
-            send_ref[:, at] = part[half:]
+            put(out_refs, pl.ds(pl.multiple_of(column + step * width, width), width), part)
 
         column += high_ref.shape[1]
 
 
-def forward(slots, weights, place, earlier, after):
-    tokens, depth = slots[0].shape[0] * len(slots), slots[0].shape[1]
+def forward(slots, rows, weights, place, earlier, after):
+    tokens, depth = rows[1] * len(slots), slots[0].shape[1]
     hidden = sum(w.shape[1] for w in weights[::2]) + (earlier[0].shape[1] if earlier else 0)
-    out = jax.ShapeDtypeStruct((tokens // 2, hidden), jnp.float32)
     inside, anywhere = pl.BlockSpec(memory_space=pltpu.VMEM), pl.BlockSpec(memory_space=pl.ANY)
     ends = [1 + len(slots), 1 + len(slots) + len(weights), 1 + len(slots) + len(weights) + len(earlier)]
     return pl.pallas_call(
         lambda *refs: forward_kernel(
-            refs[0], refs[1 : ends[0]], refs[ends[0] : ends[1]], refs[ends[1] : ends[2]], *refs[-3:]
+            rows, refs[0], refs[1 : ends[0]], refs[ends[0] : ends[1]], refs[ends[1] : ends[2]], refs[-5:-1], refs[-1]
         ),
-        out_shape=(out, out),
+        out_shape=parts_of(tokens, len(slots) // 2, hidden),
         in_specs=[pl.BlockSpec(memory_space=pltpu.SMEM)] + [inside] * (ends[2] - 1) + [anywhere] * len(after),
-        out_specs=[inside] * 2,
+        out_specs=[inside] * 4,
         scratch_shapes=[pltpu.VMEM((2 * tokens, depth), jnp.bfloat16)],
         compiler_params=pltpu.CompilerParams(vmem_limit_bytes=VMEM_LIMIT),
         cost_estimate=SHORT,
     )(place, *slots, *[pltpu.with_memory_space_constraint(w, pltpu.VMEM) for w in weights], *earlier, *after)
 
 
-def stream_kernel(first, depth, place_ref, slot_refs, weight_ref, earlier_refs, send_ref, keep_ref, both, landed, arrived):
-    half = send_ref.shape[0]
+def stream_kernel(first, depth, place_ref, slot_refs, weight_ref, out_refs, both, landed, arrived):
     width = landed.shape[1]
-    column = follow(earlier_refs, (send_ref, keep_ref))
-    steps = (send_ref.shape[1] - column) // width
+    steps = out_refs[0].shape[1] // width
 
     def fetch(step):
         start = pl.multiple_of(first + step * width, width)
@@ -201,39 +205,29 @@
 
     for step in range(min(depth, steps)):
         fetch(step).start()
-    fill(both, slot_refs, place_ref)
+    fill(both, slot_refs, place_ref, (0, slot_refs[0].shape[0]))
 
     @pl.loop(0, steps)
     def _(step):
         fetch(step).wait()
         high, low = split(landed[lax.rem(step, depth)])
-        part = three_pass(both, high, low, 1)
-        at = pl.ds(pl.multiple_of(column + step * width, width), width)
-        keep_ref[:, at] = part[:half]
-        send_ref[:, at] = part[half:]
+        put(out_refs, pl.ds(pl.multiple_of(step * width, width), width), three_pass(both, high, low, 1))
 
         @pl.when(step + depth < steps)
         def _():
             fetch(step + depth).start()
 
 
-def stream(slots, weight, place, first, hidden, earlier, after):
+def stream(slots, weight, place, first, hidden, after):
     tokens, columns = slots[0].shape[0] * len(slots), slots[0].shape[1]
     width, depth = divisor(hidden, 256, 128), 4
-    out = jax.ShapeDtypeStruct((tokens // 2, hidden + (earlier[0].shape[1] if earlier else 0)), jnp.float32)
     inside, anywhere = pl.BlockSpec(memory_space=pltpu.VMEM), pl.BlockSpec(memory_space=pl.ANY)
     last = 1 + len(slots)
     return pl.pallas_call(
-        lambda *refs: stream_kernel(
-            first, depth, refs[0], refs[1:last], refs[last], refs[last + 1 : last + 1 + len(earlier)], *refs[-5:]
-        ),
-        out_shape=(out, out),
-        in_specs=[pl.BlockSpec(memory_space=pltpu.SMEM)]
-        + [inside] * len(slots)
-        + [anywhere]
-        + [inside] * len(earlier)
-        + [anywhere] * len(after),
-        out_specs=[inside] * 2,
+        lambda *refs: stream_kernel(first, depth, refs[0], refs[1:last], refs[last], refs[-7:-3], *refs[-3:]),
+        out_shape=parts_of(tokens, len(slots) // 2, hidden),
+        in_specs=[pl.BlockSpec(memory_space=pltpu.SMEM)] + [inside] * len(slots) + [anywhere] * (1 + len(after)),
+        out_specs=[inside] * 4,
         scratch_shapes=[
             pltpu.VMEM((2 * tokens, columns), jnp.bfloat16),
             pltpu.VMEM((depth, width, columns), jnp.float32),
@@ -241,54 +235,45 @@
         ],
         compiler_params=pltpu.CompilerParams(vmem_limit_bytes=8 * 1024 * 1024),
         cost_estimate=SHORT,
-    )(place, *slots, pltpu.with_memory_space_constraint(weight, pltpu.HBM), *earlier, *after)
-
-
-def backward_kernel(slots, pieces, earlier, first_column, place_ref, *refs):
-    act_refs, weight_refs = refs[:slots], refs[slots : slots + 2 * pieces]
-    earlier_refs = refs[slots + 2 * pieces : slots + 2 * pieces + earlier]
-    out_refs = refs[-2 - slots : -2]
-    both, result = refs[-2:]
+    )(place, *slots, pltpu.with_memory_space_constraint(weight, pltpu.HBM), *after)
+
+
+def backward_kernel(place_ref, act_refs, weight_refs, out_refs, both, result):
     block = act_refs[0].shape[0]
-    total = block * slots
-    for p in range(slots):
-        high, low = split(act_refs[p][...])
+    total = block * len(act_refs)
+    for p, act_ref in enumerate(act_refs):
+        high, low = split(act_ref[...])
         both[p * block : (p + 1) * block, :] = high
         both[total + p * block : total + (p + 1) * block, :] = low
-
-    depth = out_refs[0].shape[1]
     width = result.shape[1]
 
-    @pl.loop(0, depth // width)
+    @pl.loop(0, out_refs[0].shape[1] // width)
     def _(step):
-        start = pl.multiple_of(step * width, width)
-        tile = (pl.ds(pl.multiple_of(first_column + start, width), width), slice(None))
-        total_sum, column = 0.0, 0
+        at = pl.ds(pl.multiple_of(step * width, width), width)
+        value, column = 0.0, 0
         for high_ref, low_ref in zip(weight_refs[::2], weight_refs[1::2]):
             columns = slice(column, column + high_ref.shape[1])
-            total_sum += three_pass(both[:, columns], high_ref[tile], low_ref[tile], 1)
+            value += three_pass(both[:, columns], high_ref[at, :], low_ref[at, :], 1)
             column = columns.stop
-        result[...] = total_sum
-        for b in range(slots):
+        result[...] = value
+        for b, out_ref in enumerate(out_refs):
             row = pl.multiple_of(place_ref[b] * block, block)
-            rows = result[pl.ds(row, block), :]
-            if earlier:
-                rows = rows + earlier_refs[b][:, pl.ds(pl.multiple_of(first_column + start, width), width)]
-            out_refs[b][:, pl.ds(start, width)] = rows
-
-
-def backward(acts, weights, place, earlier, part, parts, after):
+            out_ref[:, at] = result[pl.ds(row, block), :]
+
+
+def backward(acts, weights, place, after):
     slots, (block, hidden) = len(acts), acts[0].shape
-    depth = weights[0].shape[0] // parts
+    depth = weights[0].shape[0]
     width = divisor(depth, 256, 128)
     out = jax.ShapeDtypeStruct((block, depth), jnp.float32)
-    inside = pl.BlockSpec(memory_space=pltpu.VMEM)
+    inside, anywhere = pl.BlockSpec(memory_space=pltpu.VMEM), pl.BlockSpec(memory_space=pl.ANY)
+    last = 1 + slots + len(weights)
     return pl.pallas_call(
-        functools.partial(backward_kernel, slots, len(weights) // 2, len(earlier), part * depth),
+        lambda *refs: backward_kernel(
+            refs[0], refs[1 : 1 + slots], refs[1 + slots : last], refs[-2 - slots : -2], *refs[-2:]
+        ),
         out_shape=[out] * slots,
-        in_specs=[pl.BlockSpec(memory_space=pltpu.SMEM)]
-        + [inside] * (slots + len(weights) + len(earlier))
-        + [pl.BlockSpec(memory_space=pl.ANY)] * len(after),
+        in_specs=[pl.BlockSpec(memory_space=pltpu.SMEM)] + [inside] * (last - 1) + [anywhere] * len(after),
         out_specs=[inside] * slots,
         scratch_shapes=[
             pltpu.VMEM((2 * block * slots, hidden), jnp.bfloat16),
@@ -296,7 +281,7 @@
         ],
         compiler_params=pltpu.CompilerParams(vmem_limit_bytes=VMEM_LIMIT),
         cost_estimate=SHORT,
-    )(place, *acts, *[pltpu.with_memory_space_constraint(part, pltpu.VMEM) for part in weights], *earlier, *after)
+    )(place, *acts, *[pltpu.with_memory_space_constraint(w, pltpu.VMEM) for w in weights], *after)
 
 
 def body(hid_size, emb_size, inputs, out_grad, in_weight, in_bias, out_weight, norm_gain):
@@ -337,12 +322,12 @@
         return lax.optimization_barrier((values, others))
 
     def halved(partial, behind=()):
-        (send_own, send), (keep_own, keep) = [(rows[:tokens], rows[tokens:]) for rows in partial]
+        keep_own, keep, send_own, send = partial
         return keep + tied(other_core(send), behind)[0], (keep_own, other_core(send_own))
 
     def exchanged(half):
         summed, own = half
-        terms = [summed[d * tokens : (d + 1) * tokens] for d in range(chips - 1)]
+        terms = jnp.split(summed, chips - 1)
         arrival = next_chip(terms[chips - 2])
         for step in range(chips - 3, -1, -1):
             arrival = next_chip(arrival + terms[step])
@@ -368,22 +353,25 @@
     )
     inv_std = inv_std[:, :1]
     scaled = relayed(scaled)
-    back_0 = stream(grads, out_weight, place, 0, 2 * third, (), [scaled[0]])
+    back_0 = stream(grads, out_weight, place, 0, 2 * third, [scaled[0]])
     back_0, (scaled[1], scaled[-1]) = tied(back_0, (scaled[1], scaled[-1]))
     half_0 = halved(back_0)
-    back_1 = stream(grads, out_weight, place, 2 * third, third, (), [half_0[0]])
+    back_1 = stream(grads, out_weight, place, 2 * third, third, [half_0[0]])
     back_0 = exchanged(half_0)
     back_1, scaled = tied(back_1, scaled)
-    pre_0 = forward(scaled, in_parts[:8], place, (), [back_1[0]])
-    half_1 = halved(back_1, (pre_0, back_0[0]))
+    in_parts += prepared(2, [back_1[0]])
+    half_1 = halved(back_1, (in_parts[8], back_0[0]))
     back_1 = exchanged(half_1)
-    in_parts += prepared(2, [pre_0[1], half_1[0]])
-    half_0 = halved(pre_0, (in_parts[8], back_1[0]))
-    pre_1 = forward(scaled, in_parts[8:], place, (), [half_0[0]])
+    early, late = (0, tokens // 2), (tokens // 2, tokens // 2)
+    pre_0 = forward(scaled, early, in_parts, place, (), [half_1[0]])
+    pre_1 = forward(scaled, late, in_parts[:8], place, (), [pre_0[0]])
+    half_0 = halved(pre_0, (pre_1, back_1[0]))
+    pre_1 = forward(scaled, late, in_parts[8:], place, pre_1, [half_0[0]])
     pre_0 = exchanged(half_0)
-
-    def slope_product(bias, back, pre):
-        return sum(back) * gelu_slope(sum(pre) + bias)
+    back_sum = jnp.concatenate([sum(back_0), sum(back_1)], axis=1)
+
+    def slope_product(rows, pre):
+        return back_sum[rows[0] : sum(rows)] * gelu_slope(sum(pre) + in_bias)
 
     def spread_out(act):
         mine = [None] * chips
@@ -393,9 +381,9 @@
             mine[(chips - step) % chips] = act
         return mine
 
-    act_0 = slope_product(in_bias[: 2 * third], back_0, pre_0)
+    act_0 = slope_product(early, pre_0)
     pre_1 = exchanged(halved(pre_1, act_0))
-    act_1 = slope_product(in_bias[2 * third :], back_1, pre_1)
+    act_1 = slope_product(late, pre_1)
 
     def both_cores(mine):
         return mine + [other_core(block) for block in mine]
@@ -404,14 +392,10 @@
         return sum([along_hid(sums[step], -step) for step in range(1, hid_size)], start=sums[0])
 
     acts_0, acts_1 = spread_out(act_0), spread_out(act_1)
-    sums = backward(both_cores(acts_0), in_parts[:8], place, (), 0, 1, [pre_1[1]])
-    acts_1[1:], sums = tied(acts_1[1:], sums)
-    acts_1 = both_cores(acts_1)
-    parts = 2 if depth % 512 == 0 else 1
-    ends = []
-    for part in range(parts):
-        ends.append(backward(acts_1, in_parts[8:], place, sums, part, parts, [ends[-1][0] if ends else sums[0]]))
-    running = jnp.concatenate([summed_along_hid(end) for end in ends], axis=1)
+    sums_0 = backward(both_cores(acts_0), in_parts, place, [])
+    acts_1[1:], sums_0 = tied(acts_1[1:], sums_0)
+    sums_1 = backward(both_cores(acts_1), in_parts, place, [])
+    running = jnp.concatenate([summed_along_hid(sums_0), summed_along_hid(sums_1)])
     normed_grad = running * norm_gain
     totals = lax.psum(
         jnp.stack([jnp.sum(normed_grad, axis=-1), jnp.sum(normed_grad * normed, axis=-1)]), "emb"

time: 141 us -> 157 us (1.11)
  Pallas kernels: 61.3 us -> 79.3 us
  waiting for transfers between devices: 41.6 us -> 36.5 us
  starting transfers between devices: 28.4 us -> 31.6 us
    pallas_call x5, Pallas kernels: 26.5 us -> 44.4 us  [the longest x2 27.1 us: backward(): pl.pallas_call(lambda *refs: backward_kernel(refs[0], refs[1:1 + slots],...]
    ppermute x7, waiting for transfers between devices: 27.6 us -> 24.6 us  [next_chip(): lax.ppermute(values, 'emb', [(i, (i + 2) % emb_size) for i in range(emb_s...]
    ppermute x7, starting transfers between devices: 7.11 us -> 8.99 us  [next_chip(): lax.ppermute(values, 'emb', [(i, (i + 2) % emb_size) for i in range(emb_s...]
  transfers between devices with their start and end apart: 32 -> 32, of which waited for: 10 -> 8; matrix products, arithmetic and copies ran while one was open for 1% -> 1% of each run, Pallas kernels for 41% -> 51%
where the time goes in v12:
time: 157 us
  Pallas kernels  79.3 us (51%)
  waiting for transfers between devices  36.5 us (23%)
  starting transfers between devices  31.6 us (20%)
  blocking collectives  5.98 us (4%)
  other arithmetic  1.71 us (1%)
    pallas_call x2, Pallas kernels, backward(): pl.pallas_call(lambda *refs: backward_kernel(refs[0], refs[1:1 + slots],...  27.1 us
    ppermute x7, waiting for transfers between devices, next_chip(): lax.ppermute(values, 'emb', [(i, (i + 2) % emb_size) for i in range(emb_s...  24.6 us
    ppermute x12, starting transfers between devices, along_hid(): lax.ppermute(values, 'hid', [(i, (i + steps) % hid_size) for i in range(h...  20.3 us
    pallas_call x2, Pallas kernels, stream(): pl.pallas_call(lambda *refs: stream_kernel(first, depth, refs[0], refs[1:...  18.3 us
    pallas_call x3, Pallas kernels, forward(): pl.pallas_call(lambda *refs: forward_kernel(rows, refs[0], refs[1:ends[0]...  17.3 us
    pallas_call x3, Pallas kernels, prepare(): pl.pallas_call(lambda weight_ref, *refs: prepare_kernel(rows, columns, bl...  16.3 us
    ppermute x12, waiting for transfers between devices, along_hid(): lax.ppermute(values, 'hid', [(i, (i + steps) % hid_size) for i in range(h...  9.96 us
    ppermute x7, starting transfers between devices, next_chip(): lax.ppermute(values, 'emb', [(i, (i + 2) % emb_size) for i in range(emb_s...  8.99 us
  transfers between devices with their start and end apart: 32, of which 8 were waited for; matrix products, arithmetic and copies ran while one was open for 1% of the time, Pallas kernels for 51%

profile of v12, /device:TPU:0, one launch (start us, length us, event | category | flops | bytes accessed | tf_op | source)
XLA Modules:
  0.0 156.6 jit_solution(11671825796648691840)
XLA Ops:
  0.0 3.0 %collective-permute-start.3 = (f32[32,1536]{1,0:T(8,128)}, f32[32,1536]{1,0:T(8,128)S(1)}, u32[]{:S(2)}, u32[]{:S(2)}) collective-permute-start(f32[32,1536]{1,0:T(8,128)} %refs_1_.3), channel_id=1, source_target_pairs={{0,4},{4,8},{8,12},{12,0},{1,5},{5,9},{9,13},{13,1},{2,6},{6,10},{... | collective-permute-start | bytes 589832 | tf_op jit(solution)/shard_map/ppermute | solution.py:296
  3.0 2.6 %collective-permute-start.2 = (f32[32,1536]{1,0:T(8,128)}, f32[32,1536]{1,0:T(8,128)S(1)}, u32[]{:S(2)}, u32[]{:S(2)}) collective-permute-start(f32[32,1536]{1,0:T(8,128)} %refs_1_.3), channel_id=1, source_target_pairs={{0,8},{4,12},{8,0},{12,4},{1,9},{5,13},{9,1},{13,5},{2,10},{6,14},... | collective-permute-start | bytes 589832 | tf_op jit(solution)/shard_map/ppermute | solution.py:296
  5.6 1.3 collective-permute-start.1
  8.1 5.4 %shard_map.65 = (bf16[1536,1024]{1,0:T(8,128)(2,1)S(1)}, bf16[1536,1024]{1,0:T(8,128)(2,1)S(1)}, bf16[1536,1024]{1,0:T(8,128)(2,1)S(1)}, bf16[1536,1024]{1,0:T(8,128)(2,1)S(1)}) custom-call(f32[1536,6144]{1,0:T(8,128)} %weight_ref.5, s32[4]{0:T(128)S(1)} %fusion.12.refs_0_, f32[64,128]{1,0:T(8,128)S(1)} %shard_map.64.refs_1_.refs_0_), custom_call_target="tpu_custom_call" | custom-call | flops 1048576 | bytes 262144 | tf_op jit(solution)/shard_map/pallas_call | solution.py:111
  13.6 5.4 %shard_map.66 = (bf16[1536,1024]{1,0:T(8,128)(2,1)S(1)}, bf16[1536,1024]{1,0:T(8,128)(2,1)S(1)}, bf16[1536,1024]{1,0:T(8,128)(2,1)S(1)}, bf16[1536,1024]{1,0:T(8,128)(2,1)S(1)}) custom-call(f32[1536,6144]{1,0:T(8,128)} %weight_ref.5, bf16[1536,1024]{1,0:T(8,128)(2,1)S(1)} %get-tuple-element.70.refs_0_.refs_5_), custom_call_target="tpu_custom_call" | custom-call | flops 1048576 | bytes 262144 | tf_op jit(solution)/shard_map/pallas_call | solution.py:111
  19.1 1.6 collective-permute-start.4
  20.7 2.4 %collective-permute-done.4.refs_3_ = f32[64,128]{1,0:T(8,128)S(1)} collective-permute-done((f32[64,128]{1,0:T(8,128)S(1)}, f32[64,128]{1,0:T(8,128)S(1)}, u32[]{:S(2)}, u32[]{:S(2)}) %collective-permute-start.4) | collective-permute-done | bytes 32800 | tf_op jit(solution)/shard_map/ppermute | solution.py:302
  23.2 5.4 %collective-permute-start.6 = (f32[32,1536]{1,0:T(8,128)S(1)}, f32[32,1536]{1,0:T(8,128)S(1)}, u32[]{:S(2)}, u32[]{:S(2)}) collective-permute-start(f32[32,1536]{1,0:T(8,128)S(1)} %get-tuple-element.94.refs_6_.refs_1_), channel_id=1, source_target_pairs={{0,12},{4,0},{8,4},{12,8},{1,13},{5,1},{9,5},{13,9},{2,14},{6,2},{... | collective-permute-start | bytes 589832 | tf_op jit(solution)/shard_map/ppermute | solution.py:296
  28.6 11.5 %shard_map.69 = (f32[32,4096]{1,0:T(8,128)S(1)}, f32[32,4096]{1,0:T(8,128)S(1)}, f32[32,4096]{1,0:T(8,128)S(1)}, f32[32,4096]{1,0:T(8,128)S(1)}) custom-call(s32[4]{0:T(128)S(1)} %fusion.12.refs_0_, f32[32,1536]{1,0:T(8,128)S(1)} %copy-done.8, f32[32,1536]{1,0:T(8,128)S(1)} %collective-permute-done.3.refs_5_.refs_2_, ...), custom_call_target="tpu_custom_call" | custom-call | flops 1048576 | bytes 262144 | tf_op jit(solution)/shard_map/pallas_call | solution.py:226
  40.3 1.9 %collective-permute-done.7 = f32[32,4096]{1,0:T(8,128)S(1)} collective-permute-done((f32[32,4096]{1,0:T(8,128)S(1)}, f32[32,4096]{1,0:T(8,128)S(1)}, u32[]{:S(2)}, u32[]{:S(2)}) %collective-permute-start.7) | collective-permute-done | bytes 524320 | tf_op jit(solution)/shard_map/ppermute | solution.py:299
  42.2 1.6 collective-permute-start.8
  44.7 6.8 %shard_map.70 = (f32[32,2048]{1,0:T(8,128)S(1)}, f32[32,2048]{1,0:T(8,128)S(1)}, f32[32,2048]{1,0:T(8,128)S(1)}, f32[32,2048]{1,0:T(8,128)S(1)}) custom-call(s32[4]{0:T(128)S(1)} %fusion.12.refs_0_, f32[32,1536]{1,0:T(8,128)S(1)} %copy-done.8, f32[32,1536]{1,0:T(8,128)S(1)} %collective-permute-done.3.refs_5_.refs_2_, ...), custom_call_target="tpu_custom_call" | custom-call | flops 1048576 | bytes 262144 | tf_op jit(solution)/shard_map/pallas_call | solution.py:226
  51.5 1.7 %collective-permute-done.10.refs_3_ = f32[32,1536]{1,0:T(8,128)S(1)} collective-permute-done((f32[32,1536]{1,0:T(8,128)S(1)}, f32[32,1536]{1,0:T(8,128)S(1)}, u32[]{:S(2)}, u32[]{:S(2)}) %collective-permute-start.10) | collective-permute-done | bytes 196640 | tf_op jit(solution)/shard_map/ppermute | solution.py:296
  53.7 5.4 %shard_map.71 = (bf16[1536,1024]{1,0:T(8,128)(2,1)S(1)}, bf16[1536,1024]{1,0:T(8,128)(2,1)S(1)}, bf16[1536,1024]{1,0:T(8,128)(2,1)S(1)}, bf16[1536,1024]{1,0:T(8,128)(2,1)S(1)}) custom-call(f32[1536,6144]{1,0:T(8,128)} %weight_ref.5, f32[32,2048]{1,0:T(8,128)S(1)} %get-tuple-element.90.refs_0_), custom_call_target="tpu_custom_call" | custom-call | flops 1048576 | bytes 262144 | tf_op jit(solution)/shard_map/pallas_call | solution.py:111
  59.8 8.3 %shard_map.72 = (f32[16,6144]{1,0:T(8,128)S(1)}, f32[16,6144]{1,0:T(8,128)S(1)}, f32[16,6144]{1,0:T(8,128)S(1)}, f32[16,6144]{1,0:T(8,128)S(1)}) custom-call(s32[4]{0:T(128)S(1)} %fusion.12.refs_0_, f32[32,1536]{1,0:T(8,128)S(1)} %get-tuple-element.94.refs_6_.refs_1_, f32[32,1536]{1,0:T(8,128)S(1)} %collective-permute-done.5.refs_2_, ...), custom_call_target="tpu_custom_call" | custom-call | flops 1048576 | bytes 262144 | tf_op jit(solution)/shard_map/pallas_call | solution.py:184
  68.8 5.7 %shard_map.73 = (f32[16,4096]{1,0:T(8,128)S(1)}, f32[16,4096]{1,0:T(8,128)S(1)}, f32[16,4096]{1,0:T(8,128)S(1)}, f32[16,4096]{1,0:T(8,128)S(1)}) custom-call(s32[4]{0:T(128)S(1)} %fusion.12.refs_0_, f32[32,1536]{1,0:T(8,128)S(1)} %get-tuple-element.94.refs_6_.refs_1_, f32[32,1536]{1,0:T(8,128)S(1)} %collective-permute-done.5.refs_2_, ...), custom_call_target="tpu_custom_call" | custom-call | flops 1048576 | bytes 262144 | tf_op jit(solution)/shard_map/pallas_call | solution.py:184
  74.6 1.6 collective-permute-start.16
  76.2 3.2 %shard_map.74 = (f32[16,6144]{1,0:T(8,128)S(1)}, f32[16,6144]{1,0:T(8,128)S(1)}, f32[16,6144]{1,0:T(8,128)S(1)}, f32[16,6144]{1,0:T(8,128)S(1)}) custom-call(s32[4]{0:T(128)S(1)} %fusion.12.refs_0_, f32[32,1536]{1,0:T(8,128)S(1)} %get-tuple-element.94.refs_6_.refs_1_, f32[32,1536]{1,0:T(8,128)S(1)} %collective-permute-done.5.refs_2_, ...), custom_call_target="tpu_custom_call" | custom-call | flops 1048576 | bytes 262144 | tf_op jit(solution)/shard_map/pallas_call | solution.py:184
  80.1 5.7 %collective-permute-done.16 = f32[16,6144]{1,0:T(8,128)S(1)} collective-permute-done((f32[16,6144]{1,0:T(8,128)S(1)}, f32[16,6144]{1,0:T(8,128)S(1)}, u32[]{:S(2)}, u32[]{:S(2)}) %collective-permute-start.16) | collective-permute-done | bytes 393248 | tf_op jit(solution)/shard_map/ppermute | solution.py:302
  86.0 1.6 collective-permute-start.21
  88.2 9.9 %collective-permute-done.21.refs_2_ = f32[16,6144]{1,0:T(8,128)S(1)} collective-permute-done((f32[16,6144]{1,0:T(8,128)S(1)}, f32[16,6144]{1,0:T(8,128)S(1)}, u32[]{:S(2)}, u32[]{:S(2)}) %collective-permute-start.21) | collective-permute-done | bytes 393248 | tf_op jit(solution)/shard_map/ppermute | solution.py:302
  98.1 6.6 %collective-permute-done.18 = f32[16,6144]{1,0:T(8,128)S(1)} collective-permute-done((f32[16,6144]{1,0:T(8,128)S(1)}, f32[16,6144]{1,0:T(8,128)S(1)}, u32[]{:S(2)}, u32[]{:S(2)}) %collective-permute-start.18) | collective-permute-done | bytes 393248 | tf_op jit(solution)/shard_map/ppermute | solution.py:302
  104.9 1.6 collective-permute-start.20
  106.5 13.6 %shard_map.75 = (f32[16,1536]{1,0:T(8,128)S(1)}, f32[16,1536]{1,0:T(8,128)S(1)}, f32[16,1536]{1,0:T(8,128)S(1)}, f32[16,1536]{1,0:T(8,128)S(1)}) custom-call(s32[4]{0:T(128)S(1)} %fusion.12.refs_0_, f32[16,6144]{1,0:T(8,128)S(1)} %fusion.4.refs_1_, f32[16,6144]{1,0:T(8,128)S(1)} %collective-permute-done.21.refs_2_, ...), custom_call_target="tpu_custom_call" | custom-call | flops 1048576 | bytes 262144 | tf_op jit(solution)/shard_map/pallas_call | solution.py:271
  120.7 1.7 %collective-permute-start.24 = (f32[16,1536]{1,0:T(8,128)S(1)}, f32[16,1536]{1,0:T(8,128)S(1)}, u32[]{:S(2)}, u32[]{:S(2)}) collective-permute-start(f32[16,1536]{1,0:T(8,128)S(1)} %get-tuple-element.126), channel_id=1, source_target_pairs={{0,12},{4,0},{8,4},{12,8},{1,13},{5,1},{9,5},{13,9},{2,14},{6,2},{... | collective-permute-start | bytes 294920 | tf_op jit(solution)/shard_map/ppermute | solution.py:296
  122.5 2.0 %collective-permute-start.26 = (f32[16,1536]{1,0:T(8,128)S(1)}, f32[16,1536]{1,0:T(8,128)S(1)}, u32[]{:S(2)}, u32[]{:S(2)}) collective-permute-start(f32[16,1536]{1,0:T(8,128)S(1)} %get-tuple-element.128), channel_id=1, source_target_pairs={{0,4},{4,8},{8,12},{12,0},{1,5},{5,9},{9,13},{13,1},{2,6},{6,10},{... | collective-permute-start | bytes 294920 | tf_op jit(solution)/shard_map/ppermute | solution.py:296
  124.7 13.6 %shard_map.76 = (f32[16,1536]{1,0:T(8,128)S(1)}, f32[16,1536]{1,0:T(8,128)S(1)}, f32[16,1536]{1,0:T(8,128)S(1)}, f32[16,1536]{1,0:T(8,128)S(1)}) custom-call(s32[4]{0:T(128)S(1)} %fusion.12.refs_0_, f32[16,6144]{1,0:T(8,128)S(1)} %fusion.9.refs_1_, f32[16,6144]{1,0:T(8,128)S(1)} %collective-permute-done.20.refs_2_, ...), custom_call_target="tpu_custom_call" | custom-call | flops 1048576 | bytes 262144 | tf_op jit(solution)/shard_map/pallas_call | solution.py:271
  138.2 1.9 %collective-permute-start.29 = (f32[16,1536]{1,0:T(8,128)S(1)}, f32[16,1536]{1,0:T(8,128)S(1)}, u32[]{:S(2)}, u32[]{:S(2)}) collective-permute-start(f32[16,1536]{1,0:T(8,128)S(1)} %get-tuple-element.131), channel_id=1, source_target_pairs={{0,12},{4,0},{8,4},{12,8},{1,13},{5,1},{9,5},{13,9},{2,14},{6,2},{... | collective-permute-start | bytes 294920 | tf_op jit(solution)/shard_map/ppermute | solution.py:296
  140.1 1.0 collective-permute-start.30
  141.4 1.9 %collective-permute-done.29 = f32[16,1536]{1,0:T(8,128)S(1)} collective-permute-done((f32[16,1536]{1,0:T(8,128)S(1)}, f32[16,1536]{1,0:T(8,128)S(1)}, u32[]{:S(2)}, u32[]{:S(2)}) %collective-permute-start.29) | collective-permute-done | bytes 98336 | tf_op jit(solution)/shard_map/ppermute | solution.py:296
  143.3 6.4 %collective-permute-done.30 = f32[16,1536]{1,0:T(8,128)S(1)} collective-permute-done((f32[16,1536]{1,0:T(8,128)S(1)}, f32[16,1536]{1,0:T(8,128)S(1)}, u32[]{:S(2)}, u32[]{:S(2)}) %collective-permute-start.30) | collective-permute-done | bytes 98336 | tf_op jit(solution)/shard_map/ppermute | solution.py:296
  149.9 6.0 %psum.7 = f32[2,32]{1,0:T(2,128)S(1)} all-reduce(f32[2,32]{1,0:T(2,128)S(1)} %pad_maximum_fusion.1), channel_id=1, replica_groups=mesh['groups'=2,'hid'=4,'emb'=4] {'emb'}, use_global_device_ids=true, to_apply=%region_2.3 | all-reduce | flops 64 | bytes 512 | tf_op jit(solution)/shard_map/psum | solution.py:400
  (86 shorter events, 8.0 us)
Async XLA Ops:
  0.0 19.1 %collective-permute-start.3 = (f32[32,1536]{1,0:T(8,128)}, f32[32,1536]{1,0:T(8,128)S(1)}, u32[]{:S(2)}, u32[]{:S(2)}) collective-permute-start(f32[32,1536]{1,0:T(8,128)} %refs_1_.3), channel_id=1, source_target_pairs={{0,4},{4,8},{8,12},{12,0},{1,5},{5,9},{9,13},{13,1},{2,6},{6,10},{... | collective-permute-start | bytes 589832 | tf_op jit(solution)/shard_map/ppermute | solution.py:296
  3.0 16.0 %collective-permute-start.2 = (f32[32,1536]{1,0:T(8,128)}, f32[32,1536]{1,0:T(8,128)S(1)}, u32[]{:S(2)}, u32[]{:S(2)}) collective-permute-start(f32[32,1536]{1,0:T(8,128)} %refs_1_.3), channel_id=1, source_target_pairs={{0,8},{4,12},{8,0},{12,4},{1,9},{5,13},{9,1},{13,5},{2,10},{6,14},... | collective-permute-start | bytes 589832 | tf_op jit(solution)/shard_map/ppermute | solution.py:296
  5.6 13.5 %collective-permute-start.1 = (f32[32,1536]{1,0:T(8,128)}, f32[32,1536]{1,0:T(8,128)S(1)}, u32[]{:S(2)}, u32[]{:S(2)}) collective-permute-start(f32[32,1536]{1,0:T(8,128)} %refs_1_.3), channel_id=1, source_target_pairs={{0,12},{4,0},{8,4},{12,8},{1,13},{5,1},{9,5},{13,9},{2,14},{6,2},{... | collective-permute-start | bytes 589832 | tf_op jit(solution)/shard_map/ppermute | solution.py:296
  8.1 11.0 %collective-permute-start = (f32[64,128]{1,0:T(8,128)S(1)}, f32[64,128]{1,0:T(8,128)S(1)}, u32[]{:S(2)}, u32[]{:S(2)}) collective-permute-start(f32[64,128]{1,0:T(8,128)S(1)} %shard_map.64.refs_1_.refs_0_), channel_id=1, source_target_pairs={{0,1},{1,0},{2,3},{3,2},{4,5},{5,4},{6,7},{7,6},{8,9},{9,8},{10,11... | collective-permute-start | bytes 98312 | tf_op jit(solution)/shard_map/ppermute | solution.py:299
  19.1 4.0 %collective-permute-start.4 = (f32[64,128]{1,0:T(8,128)S(1)}, f32[64,128]{1,0:T(8,128)S(1)}, u32[]{:S(2)}, u32[]{:S(2)}) collective-permute-start(f32[64,128]{1,0:T(8,128)S(1)} %shard_map.67.refs_2_), channel_id=1, source_target_pairs={{0,2},{1,3},{2,0},{3,1},{4,6},{5,7},{6,4},{7,5},{8,10},{9,11},{10,... | collective-permute-start | bytes 98312 | tf_op jit(solution)/shard_map/ppermute | solution.py:302
  23.2 17.0 %collective-permute-start.6 = (f32[32,1536]{1,0:T(8,128)S(1)}, f32[32,1536]{1,0:T(8,128)S(1)}, u32[]{:S(2)}, u32[]{:S(2)}) collective-permute-start(f32[32,1536]{1,0:T(8,128)S(1)} %get-tuple-element.94.refs_6_.refs_1_), channel_id=1, source_target_pairs={{0,12},{4,0},{8,4},{12,8},{1,13},{5,1},{9,5},{13,9},{2,14},{6,2},{... | collective-permute-start | bytes 589832 | tf_op jit(solution)/shard_map/ppermute | solution.py:296
  28.6 11.6 %collective-permute-start.5 = (f32[32,1536]{1,0:T(8,128)S(1)}, f32[32,1536]{1,0:T(8,128)S(1)}, u32[]{:S(2)}, u32[]{:S(2)}) collective-permute-start(f32[32,1536]{1,0:T(8,128)S(1)} %get-tuple-element.94.refs_6_.refs_1_), channel_id=1, source_target_pairs={{0,4},{4,8},{8,12},{12,0},{1,5},{5,9},{9,13},{13,1},{2,6},{6,10},{... | collective-permute-start | bytes 589832 | tf_op jit(solution)/shard_map/ppermute | solution.py:296
  40.2 2.0 %collective-permute-start.7 = (f32[32,4096]{1,0:T(8,128)S(1)}, f32[32,4096]{1,0:T(8,128)S(1)}, u32[]{:S(2)}, u32[]{:S(2)}) collective-permute-start(f32[32,4096]{1,0:T(8,128)S(1)} %get-tuple-element.79), channel_id=1, source_target_pairs={{0,1},{1,0},{2,3},{3,2},{4,5},{5,4},{6,7},{7,6},{8,9},{9,8},{10,11... | collective-permute-start | bytes 1572872 | tf_op jit(solution)/shard_map/ppermute | solution.py:299
  42.2 16.9 %collective-permute-start.8 = (f32[32,4096]{1,0:T(8,128)S(1)}, f32[32,4096]{1,0:T(8,128)S(1)}, u32[]{:S(2)}, u32[]{:S(2)}) collective-permute-start(f32[32,4096]{1,0:T(8,128)S(1)} %add.105.refs_6_), channel_id=1, source_target_pairs={{0,2},{1,3},{2,0},{3,1},{4,6},{5,7},{6,4},{7,5},{8,10},{9,11},{10,... | collective-permute-start | bytes 1572872 | tf_op jit(solution)/shard_map/ppermute | solution.py:302
  43.8 24.9 %collective-permute-start.9 = (f32[32,4096]{1,0:T(8,128)S(1)}, f32[32,4096]{1,0:T(8,128)S(1)}, u32[]{:S(2)}, u32[]{:S(2)}) collective-permute-start(f32[32,4096]{1,0:T(8,128)S(1)} %get-tuple-element.81), channel_id=1, source_target_pairs={{0,1},{1,0},{2,3},{3,2},{4,5},{5,4},{6,7},{7,6},{8,9},{9,8},{10,11... | collective-permute-start | bytes 1572872 | tf_op jit(solution)/shard_map/ppermute | solution.py:299
  43.8 9.4 %collective-permute-start.10 = (f32[32,1536]{1,0:T(8,128)S(1)}, f32[32,1536]{1,0:T(8,128)S(1)}, u32[]{:S(2)}, u32[]{:S(2)}) collective-permute-start(f32[32,1536]{1,0:T(8,128)S(1)} %collective-permute-done.5.refs_2_), channel_id=1, source_target_pairs={{0,4},{4,8},{8,12},{12,0},{1,5},{5,9},{9,13},{13,1},{2,6},{6,10},{... | collective-permute-start | bytes 589832 | tf_op jit(solution)/shard_map/ppermute | solution.py:296
  53.2 5.9 %collective-permute-start.11 = (f32[32,2048]{1,0:T(8,128)S(1)}, f32[32,2048]{1,0:T(8,128)S(1)}, u32[]{:S(2)}, u32[]{:S(2)}) collective-permute-start(f32[32,2048]{1,0:T(8,128)S(1)} %get-tuple-element.89), channel_id=1, source_target_pairs={{0,1},{1,0},{2,3},{3,2},{4,5},{5,4},{6,7},{7,6},{8,9},{9,8},{10,11... | collective-permute-start | bytes 786440 | tf_op jit(solution)/shard_map/ppermute | solution.py:299
  53.2 23.0 %collective-permute-start.13 = (f32[32,2048]{1,0:T(8,128)S(1)}, f32[32,2048]{1,0:T(8,128)S(1)}, u32[]{:S(2)}, u32[]{:S(2)}) collective-permute-start(f32[32,2048]{1,0:T(8,128)S(1)} %get-tuple-element.93), channel_id=1, source_target_pairs={{0,1},{1,0},{2,3},{3,2},{4,5},{5,4},{6,7},{7,6},{8,9},{9,8},{10,11... | collective-permute-start | bytes 786440 | tf_op jit(solution)/shard_map/ppermute | solution.py:299
  59.2 15.4 %collective-permute-start.12 = (f32[32,2048]{1,0:T(8,128)S(1)}, f32[32,2048]{1,0:T(8,128)S(1)}, u32[]{:S(2)}, u32[]{:S(2)}) collective-permute-start(f32[32,2048]{1,0:T(8,128)S(1)} %add.108.refs_17_), channel_id=1, source_target_pairs={{0,2},{1,3},{2,0},{3,1},{4,6},{5,7},{6,4},{7,5},{8,10},{9,11},{10,... | collective-permute-start | bytes 786440 | tf_op jit(solution)/shard_map/ppermute | solution.py:302
  68.1 6.5 %collective-permute-start.14 = (f32[16,6144]{1,0:T(8,128)S(1)}, f32[16,6144]{1,0:T(8,128)S(1)}, u32[]{:S(2)}, u32[]{:S(2)}) collective-permute-start(f32[16,6144]{1,0:T(8,128)S(1)} %get-tuple-element.113), channel_id=1, source_target_pairs={{0,1},{1,0},{2,3},{3,2},{4,5},{5,4},{6,7},{7,6},{8,9},{9,8},{10,11... | collective-permute-start | bytes 1179656 | tf_op jit(solution)/shard_map/ppermute | solution.py:299
  68.2 11.9 %collective-permute-start.17 = (f32[16,6144]{1,0:T(8,128)S(1)}, f32[16,6144]{1,0:T(8,128)S(1)}, u32[]{:S(2)}, u32[]{:S(2)}) collective-permute-start(f32[16,6144]{1,0:T(8,128)S(1)} %get-tuple-element.117), channel_id=1, source_target_pairs={{0,1},{1,0},{2,3},{3,2},{4,5},{5,4},{6,7},{7,6},{8,9},{9,8},{10,11... | collective-permute-start | bytes 1179656 | tf_op jit(solution)/shard_map/ppermute | solution.py:299
  74.6 11.2 %collective-permute-start.16 = (f32[16,6144]{1,0:T(8,128)S(1)}, f32[16,6144]{1,0:T(8,128)S(1)}, u32[]{:S(2)}, u32[]{:S(2)}) collective-permute-start(f32[16,6144]{1,0:T(8,128)S(1)} %add.111.refs_13_), channel_id=1, source_target_pairs={{0,2},{1,3},{2,0},{3,1},{4,6},{5,7},{6,4},{7,5},{8,10},{9,11},{10,... | collective-permute-start | bytes 1179656 | tf_op jit(solution)/shard_map/ppermute | solution.py:302
  79.5 8.0 %collective-permute-start.15 = (f32[16,6144]{1,0:T(8,128)S(1)}, f32[16,6144]{1,0:T(8,128)S(1)}, u32[]{:S(2)}, u32[]{:S(2)}) collective-permute-start(f32[16,6144]{1,0:T(8,128)S(1)} %get-tuple-element.116), channel_id=1, source_target_pairs={{0,1},{1,0},{2,3},{3,2},{4,5},{5,4},{6,7},{7,6},{8,9},{9,8},{10,11... | collective-permute-start | bytes 1179656 | tf_op jit(solution)/shard_map/ppermute | solution.py:299
  79.6 18.5 %collective-permute-start.19 = (f32[16,6144]{1,0:T(8,128)S(1)}, f32[16,6144]{1,0:T(8,128)S(1)}, u32[]{:S(2)}, u32[]{:S(2)}) collective-permute-start(f32[16,6144]{1,0:T(8,128)S(1)} %get-tuple-element.120), channel_id=1, source_target_pairs={{0,1},{1,0},{2,3},{3,2},{4,5},{5,4},{6,7},{7,6},{8,9},{9,8},{10,11... | collective-permute-start | bytes 1179656 | tf_op jit(solution)/shard_map/ppermute | solution.py:299
  86.0 12.1 %collective-permute-start.21 = (f32[16,6144]{1,0:T(8,128)S(1)}, f32[16,6144]{1,0:T(8,128)S(1)}, u32[]{:S(2)}, u32[]{:S(2)}) collective-permute-start(f32[16,6144]{1,0:T(8,128)S(1)} %fusion.4.refs_1_), channel_id=1, source_target_pairs={{0,2},{1,3},{2,0},{3,1},{4,6},{5,7},{6,4},{7,5},{8,10},{9,11},{10,... | collective-permute-start | bytes 1179656 | tf_op jit(solution)/shard_map/ppermute | solution.py:302
  87.6 17.1 %collective-permute-start.18 = (f32[16,6144]{1,0:T(8,128)S(1)}, f32[16,6144]{1,0:T(8,128)S(1)}, u32[]{:S(2)}, u32[]{:S(2)}) collective-permute-start(f32[16,6144]{1,0:T(8,128)S(1)} %add.118), channel_id=1, source_target_pairs={{0,2},{1,3},{2,0},{3,1},{4,6},{5,7},{6,4},{7,5},{8,10},{9,11},{10,... | collective-permute-start | bytes 1179656 | tf_op jit(solution)/shard_map/ppermute | solution.py:302
  88.2 18.3 %collective-permute-start.22 = (f32[16,6144]{1,0:T(8,128)S(1)}, f32[16,6144]{1,0:T(8,128)S(1)}, u32[]{:S(2)}, u32[]{:S(2)}) collective-permute-start(f32[16,6144]{1,0:T(8,128)S(1)} %fusion.4.refs_1_), channel_id=1, source_target_pairs={{0,1},{1,0},{2,3},{3,2},{4,5},{5,4},{6,7},{7,6},{8,9},{9,8},{10,11... | collective-permute-start | bytes 1179656 | tf_op jit(solution)/shard_map/ppermute | solution.py:299
  98.1 8.4 %collective-permute-start.23 = (f32[16,6144]{1,0:T(8,128)S(1)}, f32[16,6144]{1,0:T(8,128)S(1)}, u32[]{:S(2)}, u32[]{:S(2)}) collective-permute-start(f32[16,6144]{1,0:T(8,128)S(1)} %collective-permute-done.21.refs_2_), channel_id=1, source_target_pairs={{0,1},{1,0},{2,3},{3,2},{4,5},{5,4},{6,7},{7,6},{8,9},{9,8},{10,11... | collective-permute-start | bytes 1179656 | tf_op jit(solution)/shard_map/ppermute | solution.py:299
  104.9 15.2 %collective-permute-start.20 = (f32[16,6144]{1,0:T(8,128)S(1)}, f32[16,6144]{1,0:T(8,128)S(1)}, u32[]{:S(2)}, u32[]{:S(2)}) collective-permute-start(f32[16,6144]{1,0:T(8,128)S(1)} %fusion.9.refs_1_), channel_id=1, source_target_pairs={{0,2},{1,3},{2,0},{3,1},{4,6},{5,7},{6,4},{7,5},{8,10},{9,11},{10,... | collective-permute-start | bytes 1179656 | tf_op jit(solution)/shard_map/ppermute | solution.py:302
  106.5 18.2 %collective-permute-start.27 = (f32[16,6144]{1,0:T(8,128)S(1)}, f32[16,6144]{1,0:T(8,128)S(1)}, u32[]{:S(2)}, u32[]{:S(2)}) collective-permute-start(f32[16,6144]{1,0:T(8,128)S(1)} %fusion.9.refs_1_), channel_id=1, source_target_pairs={{0,1},{1,0},{2,3},{3,2},{4,5},{5,4},{6,7},{7,6},{8,9},{9,8},{10,11... | collective-permute-start | bytes 1179656 | tf_op jit(solution)/shard_map/ppermute | solution.py:299
  120.1 4.6 %collective-permute-start.28 = (f32[16,6144]{1,0:T(8,128)S(1)}, f32[16,6144]{1,0:T(8,128)S(1)}, u32[]{:S(2)}, u32[]{:S(2)}) collective-permute-start(f32[16,6144]{1,0:T(8,128)S(1)} %collective-permute-done.20.refs_2_), channel_id=1, source_target_pairs={{0,1},{1,0},{2,3},{3,2},{4,5},{5,4},{6,7},{7,6},{8,9},{9,8},{10,11... | collective-permute-start | bytes 1179656 | tf_op jit(solution)/shard_map/ppermute | solution.py:299
  120.7 20.4 %collective-permute-start.24 = (f32[16,1536]{1,0:T(8,128)S(1)}, f32[16,1536]{1,0:T(8,128)S(1)}, u32[]{:S(2)}, u32[]{:S(2)}) collective-permute-start(f32[16,1536]{1,0:T(8,128)S(1)} %get-tuple-element.126), channel_id=1, source_target_pairs={{0,12},{4,0},{8,4},{12,8},{1,13},{5,1},{9,5},{13,9},{2,14},{6,2},{... | collective-permute-start | bytes 294920 | tf_op jit(solution)/shard_map/ppermute | solution.py:296
  122.4 19.0 %collective-permute-start.25 = (f32[16,1536]{1,0:T(8,128)S(1)}, f32[16,1536]{1,0:T(8,128)S(1)}, u32[]{:S(2)}, u32[]{:S(2)}) collective-permute-start(f32[16,1536]{1,0:T(8,128)S(1)} %get-tuple-element.127), channel_id=1, source_target_pairs={{0,8},{4,12},{8,0},{12,4},{1,9},{5,13},{9,1},{13,5},{2,10},{6,14},... | collective-permute-start | bytes 294920 | tf_op jit(solution)/shard_map/ppermute | solution.py:296
  122.5 18.9 %collective-permute-start.26 = (f32[16,1536]{1,0:T(8,128)S(1)}, f32[16,1536]{1,0:T(8,128)S(1)}, u32[]{:S(2)}, u32[]{:S(2)}) collective-permute-start(f32[16,1536]{1,0:T(8,128)S(1)} %get-tuple-element.128), channel_id=1, source_target_pairs={{0,4},{4,8},{8,12},{12,0},{1,5},{5,9},{9,13},{13,1},{2,6},{6,10},{... | collective-permute-start | bytes 294920 | tf_op jit(solution)/shard_map/ppermute | solution.py:296
  138.2 5.1 %collective-permute-start.29 = (f32[16,1536]{1,0:T(8,128)S(1)}, f32[16,1536]{1,0:T(8,128)S(1)}, u32[]{:S(2)}, u32[]{:S(2)}) collective-permute-start(f32[16,1536]{1,0:T(8,128)S(1)} %get-tuple-element.131), channel_id=1, source_target_pairs={{0,12},{4,0},{8,4},{12,8},{1,13},{5,1},{9,5},{13,9},{2,14},{6,2},{... | collective-permute-start | bytes 294920 | tf_op jit(solution)/shard_map/ppermute | solution.py:296
  140.1 9.6 %collective-permute-start.30 = (f32[16,1536]{1,0:T(8,128)S(1)}, f32[16,1536]{1,0:T(8,128)S(1)}, u32[]{:S(2)}, u32[]{:S(2)}) collective-permute-start(f32[16,1536]{1,0:T(8,128)S(1)} %get-tuple-element.132), channel_id=1, source_target_pairs={{0,8},{4,12},{8,0},{12,4},{1,9},{5,13},{9,1},{13,5},{2,10},{6,14},... | collective-permute-start | bytes 294920 | tf_op jit(solution)/shard_map/ppermute | solution.py:296
  141.1 8.6 %collective-permute-start.31 = (f32[16,1536]{1,0:T(8,128)S(1)}, f32[16,1536]{1,0:T(8,128)S(1)}, u32[]{:S(2)}, u32[]{:S(2)}) collective-permute-start(f32[16,1536]{1,0:T(8,128)S(1)} %get-tuple-element.133), channel_id=1, source_target_pairs={{0,4},{4,8},{8,12},{12,0},{1,5},{5,9},{9,13},{13,1},{2,6},{6,10},{... | collective-permute-start | bytes 294920 | tf_op jit(solution)/shard_map/ppermute | solution.py:296
  (11 other events, 262.7 us)

commit v13 on v12

--- a/solution.py
+++ b/solution.py
@@ -75,8 +75,25 @@
     inv_std_ref[...] = inv_std
 
 
-def prepare_kernel(rows, columns, block, depth, weight_ref, *refs):
-    *part_refs, landed, arrived = refs
+def slope_kernel(terms, *refs):
+    back_refs, pre_refs, (bias_ref, weight_ref) = refs[:terms], refs[terms : 2 * terms], refs[2 * terms : 2 * terms + 2]
+    *sums_refs, act_ref, out_sums_ref = refs[2 * terms + 2 :]
+    hidden = bias_ref.shape[1]
+    product = sum(ref[...] for ref in pre_refs)
+    act = sum(ref[...] for ref in back_refs) * gelu_slope(product + bias_ref[...])
+    act_ref[:, :hidden] = act
+    lane = lax.broadcasted_iota(jnp.int32, out_sums_ref.shape, 1)
+    first = jnp.sum(act * weight_ref[...], axis=1, keepdims=True)
+    second = jnp.sum(act * product, axis=1, keepdims=True)
+    sums = jnp.where(lane == 0, first, jnp.where(lane == 1, second, 0.0)) + sum(ref[...] for ref in sums_refs)
+    out_sums_ref[...] = sums
+    if act_ref.shape[1] > hidden:
+        act_ref[:, hidden:] = sums
+
+
+def prepare_kernel(rows, columns, block, depth, weight_ref, gain_ref, *refs):
+    *part_refs, sums_ref, landed, arrived, totals = refs
+    totals[...] = jnp.zeros_like(totals)
     width = part_refs[0].shape[1]
     steps = rows[1] // block
 
@@ -93,8 +110,10 @@
     @pl.loop(0, steps)
     def _(step):
         fetch(step).wait()
-        high, low = split(landed[lax.rem(step, depth)])
+        tile = landed[lax.rem(step, depth)]
+        high, low = split(tile)
         at = pl.ds(pl.multiple_of(step * block, block), block)
+        totals[...] += jnp.sum((tile * gain_ref[at, :]).reshape(block // 8, 8, columns[1]), axis=0)
         for n, part_ref in enumerate(part_refs):
             part_ref[at, :] = (low if n % 2 else high)[:, n // 2 * width : (n // 2 + 1) * width]
 
@@ -102,24 +121,30 @@
         def _():
             fetch(step + depth).start()
 
-
-def prepare(weight, rows, columns, after):
+    sums_ref[...] = jnp.sum(totals[...], axis=0, keepdims=True)
+
+
+def prepare(weight, gain, rows, columns, after):
     block = divisor(rows[1], *[b for b in (256, 128, 64, 32) if b <= max(256 * 1536 // columns[1], 32)])
     depth = 4
     outs = (pltpu.VMEM((rows[1], columns[1] // 2), jnp.bfloat16),) * 4
-    anywhere = pl.BlockSpec(memory_space=pl.ANY)
-    return pl.pallas_call(
-        lambda weight_ref, *refs: prepare_kernel(rows, columns, block, depth, weight_ref, *refs[len(after) :]),
-        out_shape=outs,
-        in_specs=[anywhere] * (1 + len(after)),
-        out_specs=[pl.BlockSpec(memory_space=pltpu.VMEM)] * 4,
+    inside, anywhere = pl.BlockSpec(memory_space=pltpu.VMEM), pl.BlockSpec(memory_space=pl.ANY)
+    result = pl.pallas_call(
+        lambda weight_ref, gain_ref, *refs: prepare_kernel(
+            rows, columns, block, depth, weight_ref, gain_ref, *refs[len(after) :]
+        ),
+        out_shape=outs + (jax.ShapeDtypeStruct((1, columns[1]), jnp.float32),),
+        in_specs=[anywhere, inside] + [anywhere] * len(after),
+        out_specs=[inside] * 5,
         scratch_shapes=[
             pltpu.VMEM((depth, block, columns[1]), jnp.float32),
             pltpu.SemaphoreType.DMA((depth,)),
+            pltpu.VMEM((8, columns[1]), jnp.float32),
         ],
         compiler_params=pltpu.CompilerParams(vmem_limit_bytes=VMEM_LIMIT),
         cost_estimate=SHORT,
-    )(pltpu.with_memory_space_constraint(weight, pltpu.HBM), *after)
+    )(pltpu.with_memory_space_constraint(weight, pltpu.HBM), gain, *after)
+    return list(result[:4]), result[4]
 
 
 def three_pass(both, high, low, contract):
@@ -133,11 +158,11 @@
     return first[:rows] + first[rows:] + dot(both[:rows, :], low)
 
 
-def fill(both, block_refs, place_ref, rows):
-    first, count = rows
+def fill(both, block_refs, place_ref):
+    count = block_refs[0].shape[0]
     total = both.shape[0] // 2
     for index, ref in enumerate(block_refs):
-        high, low = split(ref[first : first + count, :])
+        high, low = split(ref[...])
         row = pl.multiple_of(place_ref[index] * count, count)
         both[pl.ds(row, count), :] = high
         both[pl.ds(total + row, count), :] = low
@@ -161,8 +186,8 @@
     return [jax.ShapeDtypeStruct((n, hidden), jnp.float32) for n in (block, block * (chips - 1))] * 2
 
 
-def forward_kernel(rows, place_ref, slot_refs, weight_refs, earlier_refs, out_refs, both):
-    fill(both, slot_refs, place_ref, rows)
+def forward_kernel(place_ref, slot_refs, weight_refs, earlier_refs, out_refs, both):
+    fill(both, slot_refs, place_ref)
     column = follow(earlier_refs, out_refs)
     for high_ref, low_ref in zip(weight_refs[::2], weight_refs[1::2]):
         width = divisor(high_ref.shape[1], 256, 128)
@@ -176,14 +201,14 @@
         column += high_ref.shape[1]
 
 
-def forward(slots, rows, weights, place, earlier, after):
-    tokens, depth = rows[1] * len(slots), slots[0].shape[1]
+def forward(slots, weights, place, earlier, after):
+    tokens, depth = slots[0].shape[0] * len(slots), slots[0].shape[1]
     hidden = sum(w.shape[1] for w in weights[::2]) + (earlier[0].shape[1] if earlier else 0)
     inside, anywhere = pl.BlockSpec(memory_space=pltpu.VMEM), pl.BlockSpec(memory_space=pl.ANY)
     ends = [1 + len(slots), 1 + len(slots) + len(weights), 1 + len(slots) + len(weights) + len(earlier)]
     return pl.pallas_call(
         lambda *refs: forward_kernel(
-            rows, refs[0], refs[1 : ends[0]], refs[ends[0] : ends[1]], refs[ends[1] : ends[2]], refs[-5:-1], refs[-1]
+            refs[0], refs[1 : ends[0]], refs[ends[0] : ends[1]], refs[ends[1] : ends[2]], refs[-5:-1], refs[-1]
         ),
         out_shape=parts_of(tokens, len(slots) // 2, hidden),
         in_specs=[pl.BlockSpec(memory_space=pltpu.SMEM)] + [inside] * (ends[2] - 1) + [anywhere] * len(after),
@@ -205,7 +230,7 @@
 
     for step in range(min(depth, steps)):
         fetch(step).start()
-    fill(both, slot_refs, place_ref, (0, slot_refs[0].shape[0]))
+    fill(both, slot_refs, place_ref)
 
     @pl.loop(0, steps)
     def _(step):
@@ -238,18 +263,25 @@
     )(place, *slots, pltpu.with_memory_space_constraint(weight, pltpu.HBM), *after)
 
 
-def backward_kernel(place_ref, act_refs, weight_refs, out_refs, both, result):
+def backward_kernel(first, depth, place_ref, act_refs, weight_refs, earlier_refs, out_refs, both, result, riders):
     block = act_refs[0].shape[0]
     total = block * len(act_refs)
+    hidden = both.shape[1]
     for p, act_ref in enumerate(act_refs):
-        high, low = split(act_ref[...])
+        if act_ref.shape[1] > hidden:
+            riders[p * block : (p + 1) * block, :] = act_ref[:, hidden:]
+        high, low = split(act_ref[:, :hidden])
         both[p * block : (p + 1) * block, :] = high
         both[total + p * block : total + (p + 1) * block, :] = low
     width = result.shape[1]
 
-    @pl.loop(0, out_refs[0].shape[1] // width)
+    if out_refs[0].shape[1] > depth:
+        for b, out_ref in enumerate(out_refs):
+            out_ref[:, depth:] = riders[pl.ds(pl.multiple_of(place_ref[b] * block, block), block), :]
+
+    @pl.loop(0, depth // width)
     def _(step):
-        at = pl.ds(pl.multiple_of(step * width, width), width)
+        at = pl.ds(pl.multiple_of(first + step * width, width), width)
         value, column = 0.0, 0
         for high_ref, low_ref in zip(weight_refs[::2], weight_refs[1::2]):
             columns = slice(column, column + high_ref.shape[1])
@@ -257,31 +289,42 @@
             column = columns.stop
         result[...] = value
         for b, out_ref in enumerate(out_refs):
-            row = pl.multiple_of(place_ref[b] * block, block)
-            out_ref[:, at] = result[pl.ds(row, block), :]
-
-
-def backward(acts, weights, place, after):
-    slots, (block, hidden) = len(acts), acts[0].shape
-    depth = weights[0].shape[0]
+            rows = result[pl.ds(pl.multiple_of(place_ref[b] * block, block), block), :]
+            if earlier_refs:
+                rows = rows + earlier_refs[b][:, at]
+            out_ref[:, pl.ds(pl.multiple_of(step * width, width), width)] = rows
+
+
+def backward(acts, weights, place, earlier, part, parts, after):
+    slots, block, hidden = len(acts), acts[0].shape[0], sum(w.shape[1] for w in weights[::2])
+    riding = acts[0].shape[1] - hidden if part == parts - 1 else 0
+    depth = weights[0].shape[0] // parts
     width = divisor(depth, 256, 128)
-    out = jax.ShapeDtypeStruct((block, depth), jnp.float32)
+    out = jax.ShapeDtypeStruct((block, depth + riding), jnp.float32)
     inside, anywhere = pl.BlockSpec(memory_space=pltpu.VMEM), pl.BlockSpec(memory_space=pl.ANY)
-    last = 1 + slots + len(weights)
+    ends = [1 + slots, 1 + slots + len(weights), 1 + slots + len(weights) + len(earlier)]
     return pl.pallas_call(
         lambda *refs: backward_kernel(
-            refs[0], refs[1 : 1 + slots], refs[1 + slots : last], refs[-2 - slots : -2], *refs[-2:]
+            part * depth,
+            depth,
+            refs[0],
+            refs[1 : ends[0]],
+            refs[ends[0] : ends[1]],
+            refs[ends[1] : ends[2]],
+            refs[-3 - slots : -3],
+            *refs[-3:],
         ),
         out_shape=[out] * slots,
-        in_specs=[pl.BlockSpec(memory_space=pltpu.SMEM)] + [inside] * (last - 1) + [anywhere] * len(after),
+        in_specs=[pl.BlockSpec(memory_space=pltpu.SMEM)] + [inside] * (ends[2] - 1) + [anywhere] * len(after),
         out_specs=[inside] * slots,
         scratch_shapes=[
             pltpu.VMEM((2 * block * slots, hidden), jnp.bfloat16),
             pltpu.VMEM((block * slots, width), jnp.float32),
+            pltpu.VMEM((block * slots, 128), jnp.float32),
         ],
         compiler_params=pltpu.CompilerParams(vmem_limit_bytes=VMEM_LIMIT),
         cost_estimate=SHORT,
-    )(place, *acts, *[pltpu.with_memory_space_constraint(w, pltpu.VMEM) for w in weights], *after)
+    )(place, *acts, *[pltpu.with_memory_space_constraint(w, pltpu.VMEM) for w in weights], *earlier, *after)
 
 
 def body(hid_size, emb_size, inputs, out_grad, in_weight, in_bias, out_weight, norm_gain):
@@ -334,13 +377,14 @@
         return arrival, *own
 
     def prepared(c, after):
-        return prepare(in_weight, (0, depth), (c * third, third), after)
+        return prepare(in_weight, norm_gain[:, None], (0, depth), (c * third, third), after)
 
     moments = call(moments_kernel, jax.ShapeDtypeStruct((2 * tokens, 128), jnp.float32), (inputs,), ())
-    in_parts = prepared(0, [place, moments])
-    in_parts += prepared(1, [in_parts[0]])
+    in_parts, sums_0 = prepared(0, [place, moments])
+    parts, sums_1 = prepared(1, [in_parts[0]])
+    in_parts += parts
     moments = call(
-        functools.partial(merge_kernel, depth), moments, (moments, other_core(moments)), (in_parts[4], *grads[:0:-1])
+        functools.partial(merge_kernel, depth), moments, (moments, other_core(moments)), (in_parts[4], *grads[1:])
     )
     parts = [moments]
     for _ in range(1, chips):
@@ -359,19 +403,31 @@
     back_1 = stream(grads, out_weight, place, 2 * third, third, [half_0[0]])
     back_0 = exchanged(half_0)
     back_1, scaled = tied(back_1, scaled)
-    in_parts += prepared(2, [back_1[0]])
-    half_1 = halved(back_1, (in_parts[8], back_0[0]))
+    pre_0 = forward(scaled, in_parts[:8], place, (), [back_1[0]])
+    half_1 = halved(back_1, (pre_0, back_0[0]))
     back_1 = exchanged(half_1)
-    early, late = (0, tokens // 2), (tokens // 2, tokens // 2)
-    pre_0 = forward(scaled, early, in_parts, place, (), [half_1[0]])
-    pre_1 = forward(scaled, late, in_parts[:8], place, (), [pre_0[0]])
-    half_0 = halved(pre_0, (pre_1, back_1[0]))
-    pre_1 = forward(scaled, late, in_parts[8:], place, pre_1, [half_0[0]])
+    parts, sums_2 = prepared(2, [pre_0[0], half_1[0]])
+    in_parts += parts
+    half_0 = halved(pre_0, (parts, back_1[0]))
+    pre_1 = forward(scaled, in_parts[8:], place, (), [half_0[0]])
     pre_0 = exchanged(half_0)
-    back_sum = jnp.concatenate([sum(back_0), sum(back_1)], axis=1)
-
-    def slope_product(rows, pre):
-        return back_sum[rows[0] : sum(rows)] * gelu_slope(sum(pre) + in_bias)
+
+    gain_sums, _ = tied(jnp.concatenate([sums_0, sums_1, sums_2], axis=1), pre_1)
+    gain_sums = passing = gain_sums + other_core(gain_sums)
+    for _ in range(1, chips):
+        passing = next_chip(passing)
+        gain_sums = gain_sums + passing
+
+    def slope_product(span, back, pre, sums):
+        width = span.stop - span.start
+        return call(
+            functools.partial(slope_kernel, len(back)),
+            tuple(
+                jax.ShapeDtypeStruct((tokens, n), jnp.float32) for n in (width + 128 * len(sums), 128)
+            ),
+            (*back, *pre, in_bias[None, span], gain_sums[:, span], *sums),
+            (),
+        )
 
     def spread_out(act):
         mine = [None] * chips
@@ -381,26 +437,27 @@
             mine[(chips - step) % chips] = act
         return mine
 
-    act_0 = slope_product(early, pre_0)
-    pre_1 = exchanged(halved(pre_1, act_0))
-    act_1 = slope_product(late, pre_1)
-
     def both_cores(mine):
         return mine + [other_core(block) for block in mine]
 
     def summed_along_hid(sums):
         return sum([along_hid(sums[step], -step) for step in range(1, hid_size)], start=sums[0])
 
+    act_0, sums_0 = slope_product(slice(0, 2 * third), back_0, pre_0, ())
+    pre_1 = exchanged(halved(pre_1, pre_0[0]))
+    act_1, _ = slope_product(slice(2 * third, hidden), back_1, pre_1, (sums_0,))
     acts_0, acts_1 = spread_out(act_0), spread_out(act_1)
-    sums_0 = backward(both_cores(acts_0), in_parts, place, [])
-    acts_1[1:], sums_0 = tied(acts_1[1:], sums_0)
-    sums_1 = backward(both_cores(acts_1), in_parts, place, [])
-    running = jnp.concatenate([summed_along_hid(sums_0), summed_along_hid(sums_1)])
-    normed_grad = running * norm_gain
-    totals = lax.psum(
-        jnp.stack([jnp.sum(normed_grad, axis=-1), jnp.sum(normed_grad * normed, axis=-1)]), "emb"
-    )
-    first, second = (totals / model_width)[:, :, None]
+    sums = backward(both_cores(acts_0), in_parts[:8], place, (), 0, 1, [])
+    acts_1[1:], sums = tied(acts_1[1:], sums)
+    acts_1 = both_cores(acts_1)
+    parts = 2 if depth % 512 == 0 else 1
+    ends = []
+    for part in range(parts):
+        ends.append(backward(acts_1, in_parts[8:], place, sums, part, parts, [ends[-1][0]] if ends else []))
+    *columns, last = [summed_along_hid(end) for end in ends]
+    width = depth // parts
+    normed_grad = jnp.concatenate([*columns, last[:, :width]], axis=1) * norm_gain
+    first, second = last[:, width : width + 1] / model_width, last[:, width + 1 : width + 2] / model_width
     return inv_std * (normed_grad - first - normed * second)
 
 

time: 157 us -> 140 us (0.89)
  Pallas kernels: 79.3 us -> 63.7 us
  blocking collectives: 5.98 us -> 0 us
  waiting for transfers between devices: 36.5 us -> 41.4 us
    pallas_call x8, Pallas kernels: 60.7 us -> 43.6 us  [the longest x3 17.2 us: prepare(): pl.pallas_call(lambda weight_ref, gain_ref, *refs: prepare_kernel(rows, c...]
    psum x1 -> x0, blocking collectives: 5.98 us -> none  [body(): lax.psum(jnp.stack([jnp.sum(normed_grad, axis=-1), jnp.sum(normed_grad *...]
    ppermute x13 -> x14, waiting for transfers between devices: 1.93 us -> 5.31 us  [other_core(): return lax.ppermute(values, 'emb', [(i, i ^ 1) for i in range(emb_size)])]
    ppermute x12, waiting for transfers between devices: 9.96 us -> 12 us  [along_hid(): lax.ppermute(values, 'hid', [(i, (i + steps) % hid_size) for i in range(h...]
    ppermute x7 -> x8, waiting for transfers between devices: 24.6 us -> 24.1 us  [next_chip(): lax.ppermute(values, 'emb', [(i, (i + 2) % emb_size) for i in range(emb_s...]
    ppermute x7 -> x8, starting transfers between devices: 8.99 us -> 9.15 us  [next_chip(): lax.ppermute(values, 'emb', [(i, (i + 2) % emb_size) for i in range(emb_s...]
  transfers between devices with their start and end apart: 32 -> 34, of which waited for: 8 -> 13; matrix products, arithmetic and copies ran while one was open for 1% -> 1% of each run, Pallas kernels for 51% -> 43%
where the time goes in v13:
time: 140 us; the launch traced here: 139 us
  Pallas kernels  63.7 us (46%)
  waiting for transfers between devices  41.4 us (30%)
  starting transfers between devices  30.5 us (22%)
  local copies, waits for them, and re-layouts  2.04 us (1%)
    ppermute x8, waiting for transfers between devices, next_chip(): lax.ppermute(values, 'emb', [(i, (i + 2) % emb_size) for i in range(emb_s...  24.1 us
    ppermute x12, starting transfers between devices, along_hid(): lax.ppermute(values, 'hid', [(i, (i + steps) % hid_size) for i in range(h...  19 us
    pallas_call x2, Pallas kernels, stream(): pl.pallas_call(lambda *refs: stream_kernel(first, depth, refs[0], refs[1:...  18.3 us
    pallas_call x3, Pallas kernels, prepare(): pl.pallas_call(lambda weight_ref, gain_ref, *refs: prepare_kernel(rows, c...  17.2 us
    pallas_call x3, Pallas kernels, backward(): pl.pallas_call(lambda *refs: backward_kernel(part * depth, depth, refs[0]...  15.3 us
    ppermute x12, waiting for transfers between devices, along_hid(): lax.ppermute(values, 'hid', [(i, (i + steps) % hid_size) for i in range(h...  12 us
    pallas_call x2, Pallas kernels, forward(): pl.pallas_call(lambda *refs: forward_kernel(refs[0], refs[1:ends[0]], ref...  11.1 us
    ppermute x8, starting transfers between devices, next_chip(): lax.ppermute(values, 'emb', [(i, (i + 2) % emb_size) for i in range(emb_s...  9.15 us
  transfers between devices with their start and end apart: 34, of which 13 were waited for; matrix products, arithmetic and copies ran while one was open for 1% of the time, Pallas kernels for 43%

profile of v13, /device:TPU:0, one launch (start us, length us, event | category | flops | bytes accessed | tf_op | source)
XLA Modules:
  0.0 139.4 jit_solution(13051085275138035803)
XLA Ops:
  0.0 3.0 %collective-permute-start.1 = (f32[32,1536]{1,0:T(8,128)}, f32[32,1536]{1,0:T(8,128)S(1)}, u32[]{:S(2)}, u32[]{:S(2)}) collective-permute-start(f32[32,1536]{1,0:T(8,128)} %refs_1_.3), channel_id=1, source_target_pairs={{0,4},{4,8},{8,12},{12,0},{1,5},{5,9},{9,13},{13,1},{2,6},{6,10},{... | collective-permute-start | bytes 589832 | tf_op jit(solution)/shard_map/ppermute | solution.py:339
  3.0 2.6 %collective-permute-start.2 = (f32[32,1536]{1,0:T(8,128)}, f32[32,1536]{1,0:T(8,128)S(1)}, u32[]{:S(2)}, u32[]{:S(2)}) collective-permute-start(f32[32,1536]{1,0:T(8,128)} %refs_1_.3), channel_id=1, source_target_pairs={{0,8},{4,12},{8,0},{12,4},{1,9},{5,13},{9,1},{13,5},{2,10},{6,14},... | collective-permute-start | bytes 589832 | tf_op jit(solution)/shard_map/ppermute | solution.py:339
  5.6 1.3 collective-permute-start.3
  9.1 5.7 %shard_map.65 = (bf16[1536,1024]{1,0:T(8,128)(2,1)S(1)}, bf16[1536,1024]{1,0:T(8,128)(2,1)S(1)}, bf16[1536,1024]{1,0:T(8,128)(2,1)S(1)}, bf16[1536,1024]{1,0:T(8,128)(2,1)S(1)}, f32[1,2048]{1,0:T(1,128)S(1)}) custom-call(f32[1536,6144]{1,0:T(8,128)} %weight_ref.5, f32[1536,1]{1,0:T(8,128)S(1)} %broadcast_in_dim.19.gain_ref, s32[4]{0:T(128)S(1)} %fusion.5.refs_0_, ...), custom_call_target="tpu_custom_call" | custom-call | flops 1048576 | bytes 262144 | tf_op jit(solution)/shard_map/pallas_call | solution.py:132
  14.8 5.7 %shard_map.66 = (bf16[1536,1024]{1,0:T(8,128)(2,1)S(1)}, bf16[1536,1024]{1,0:T(8,128)(2,1)S(1)}, bf16[1536,1024]{1,0:T(8,128)(2,1)S(1)}, bf16[1536,1024]{1,0:T(8,128)(2,1)S(1)}, f32[1,2048]{1,0:T(1,128)S(1)}) custom-call(f32[1536,6144]{1,0:T(8,128)} %weight_ref.5, f32[1536,1]{1,0:T(8,128)S(1)} %broadcast_in_dim.19.gain_ref, ...), custom_call_target="tpu_custom_call" | custom-call | flops 1048576 | bytes 262144 | tf_op jit(solution)/shard_map/pallas_call | solution.py:132
  20.6 1.6 %collective-permute-start.4 = (f32[64,128]{1,0:T(8,128)S(1)}, f32[64,128]{1,0:T(8,128)S(1)}, u32[]{:S(2)}, u32[]{:S(2)}) collective-permute-start(f32[64,128]{1,0:T(8,128)S(1)} %shard_map.67.refs_2_), channel_id=1, source_target_pairs={{0,2},{1,3},{2,0},{3,1},{4,6},{5,7},{6,4},{7,5},{8,10},{9,11},{10,... | collective-permute-start | bytes 98312 | tf_op jit(solution)/shard_map/ppermute | solution.py:345
  22.2 2.4 %collective-permute-done.4.refs_3_ = f32[64,128]{1,0:T(8,128)S(1)} collective-permute-done((f32[64,128]{1,0:T(8,128)S(1)}, f32[64,128]{1,0:T(8,128)S(1)}, u32[]{:S(2)}, u32[]{:S(2)}) %collective-permute-start.4) | collective-permute-done | bytes 32800 | tf_op jit(solution)/shard_map/ppermute | solution.py:345
  24.8 2.8 %collective-permute-start.5 = (f32[32,1536]{1,0:T(8,128)S(1)}, f32[32,1536]{1,0:T(8,128)S(1)}, u32[]{:S(2)}, u32[]{:S(2)}) collective-permute-start(f32[32,1536]{1,0:T(8,128)S(1)} %get-tuple-element.95.refs_6_.refs_1_), channel_id=1, source_target_pairs={{0,4},{4,8},{8,12},{12,0},{1,5},{5,9},{9,13},{13,1},{2,6},{6,10},{... | collective-permute-start | bytes 589832 | tf_op jit(solution)/shard_map/ppermute | solution.py:339
  28.7 11.5 %shard_map.69 = (f32[32,4096]{1,0:T(8,128)S(1)}, f32[32,4096]{1,0:T(8,128)S(1)}, f32[32,4096]{1,0:T(8,128)S(1)}, f32[32,4096]{1,0:T(8,128)S(1)}) custom-call(s32[4]{0:T(128)S(1)} %fusion.5.refs_0_, f32[32,1536]{1,0:T(8,128)S(1)} %copy-done.2, f32[32,1536]{1,0:T(8,128)S(1)} %collective-permute-done.1.refs_3_.refs_2_, ...), custom_call_target="tpu_custom_call" | custom-call | flops 1048576 | bytes 262144 | tf_op jit(solution)/shard_map/pallas_call | solution.py:251
  40.3 1.9 %collective-permute-done.7 = f32[32,4096]{1,0:T(8,128)S(1)} collective-permute-done((f32[32,4096]{1,0:T(8,128)S(1)}, f32[32,4096]{1,0:T(8,128)S(1)}, u32[]{:S(2)}, u32[]{:S(2)}) %collective-permute-start.7) | collective-permute-done | bytes 524320 | tf_op jit(solution)/shard_map/ppermute | solution.py:342
  42.3 1.6 %collective-permute-start.10 = (f32[32,4096]{1,0:T(8,128)S(1)}, f32[32,4096]{1,0:T(8,128)S(1)}, u32[]{:S(2)}, u32[]{:S(2)}) collective-permute-start(f32[32,4096]{1,0:T(8,128)S(1)} %add.59.refs_6_), channel_id=1, source_target_pairs={{0,2},{1,3},{2,0},{3,1},{4,6},{5,7},{6,4},{7,5},{8,10},{9,11},{10,... | collective-permute-start | bytes 1572872 | tf_op jit(solution)/shard_map/ppermute | solution.py:345
  44.8 6.8 %shard_map.70 = (f32[32,2048]{1,0:T(8,128)S(1)}, f32[32,2048]{1,0:T(8,128)S(1)}, f32[32,2048]{1,0:T(8,128)S(1)}, f32[32,2048]{1,0:T(8,128)S(1)}) custom-call(s32[4]{0:T(128)S(1)} %fusion.5.refs_0_, f32[32,1536]{1,0:T(8,128)S(1)} %copy-done.2, f32[32,1536]{1,0:T(8,128)S(1)} %collective-permute-done.1.refs_3_.refs_2_, ...), custom_call_target="tpu_custom_call" | custom-call | flops 1048576 | bytes 262144 | tf_op jit(solution)/shard_map/pallas_call | solution.py:251
  52.3 7.2 %shard_map.71 = (f32[32,4096]{1,0:T(8,128)S(1)}, f32[32,4096]{1,0:T(8,128)S(1)}, f32[32,4096]{1,0:T(8,128)S(1)}, f32[32,4096]{1,0:T(8,128)S(1)}) custom-call(s32[4]{0:T(128)S(1)} %fusion.5.refs_0_, f32[32,1536]{1,0:T(8,128)S(1)} %get-tuple-element.95.refs_6_.refs_1_, f32[32,1536]{1,0:T(8,128)S(1)} %collective-permute-done.5.refs_2_, ...), custom_call_target="tpu_custom_call" | custom-call | flops 1048576 | bytes 262144 | tf_op jit(solution)/shard_map/pallas_call | solution.py:209
  61.3 5.7 %shard_map.72 = (bf16[1536,1024]{1,0:T(8,128)(2,1)S(1)}, bf16[1536,1024]{1,0:T(8,128)(2,1)S(1)}, bf16[1536,1024]{1,0:T(8,128)(2,1)S(1)}, bf16[1536,1024]{1,0:T(8,128)(2,1)S(1)}, f32[1,2048]{1,0:T(1,128)S(1)}) custom-call(f32[1536,6144]{1,0:T(8,128)} %weight_ref.5, f32[1536,1]{1,0:T(8,128)S(1)} %broadcast_in_dim.19.gain_ref, ...), custom_call_target="tpu_custom_call" | custom-call | flops 1048576 | bytes 262144 | tf_op jit(solution)/shard_map/pallas_call | solution.py:132
  67.0 1.5 %collective-permute-done.11.refs_0_ = f32[32,2048]{1,0:T(8,128)S(1)} collective-permute-done((f32[32,2048]{1,0:T(8,128)S(1)}, f32[32,2048]{1,0:T(8,128)S(1)}, u32[]{:S(2)}, u32[]{:S(2)}) %collective-permute-start.11) | collective-permute-done | bytes 262176 | tf_op jit(solution)/shard_map/ppermute | solution.py:345
  69.2 3.9 %shard_map.73 = (f32[32,2048]{1,0:T(8,128)S(1)}, f32[32,2048]{1,0:T(8,128)S(1)}, f32[32,2048]{1,0:T(8,128)S(1)}, f32[32,2048]{1,0:T(8,128)S(1)}) custom-call(s32[4]{0:T(128)S(1)} %fusion.5.refs_0_, f32[32,1536]{1,0:T(8,128)S(1)} %get-tuple-element.95.refs_6_.refs_1_, f32[32,1536]{1,0:T(8,128)S(1)} %collective-permute-done.5.refs_2_, ...), custom_call_target="tpu_custom_call" | custom-call | flops 1048576 | bytes 262144 | tf_op jit(solution)/shard_map/pallas_call | solution.py:209
  73.2 1.2 collective-permute-done.18
  74.4 1.6 %collective-permute-start.19 = (f32[1,6144]{1,0:T(1,128)S(1)}, f32[1,6144]{1,0:T(1,128)S(1)}, u32[]{:S(2)}, u32[]{:S(2)}) collective-permute-start(f32[1,6144]{1,0:T(1,128)S(1)} %add.63), channel_id=1, source_target_pairs={{0,2},{1,3},{2,0},{3,1},{4,6},{5,7},{6,4},{7,5},{8,10},{9,11},{10,... | collective-permute-start | bytes 73736 | tf_op jit(solution)/shard_map/ppermute | solution.py:345
  76.0 6.2 %collective-permute-done.19 = f32[1,6144]{1,0:T(1,128)S(1)} collective-permute-done((f32[1,6144]{1,0:T(1,128)S(1)}, f32[1,6144]{1,0:T(1,128)S(1)}, u32[]{:S(2)}, u32[]{:S(2)}) %collective-permute-start.19) | collective-permute-done | bytes 24608 | tf_op jit(solution)/shard_map/ppermute | solution.py:345
  85.3 1.2 collective-permute-start.16
  86.5 11.2 %collective-permute-done.23.refs_2_ = f32[32,4096]{1,0:T(8,128)S(1)} collective-permute-done((f32[32,4096]{1,0:T(8,128)S(1)}, f32[32,4096]{1,0:T(8,128)S(1)}, u32[]{:S(2)}, u32[]{:S(2)}) %collective-permute-start.23) | collective-permute-done | bytes 524320 | tf_op jit(solution)/shard_map/ppermute | solution.py:345
  97.7 2.8 %collective-permute-done.16.refs_3_ = f32[32,2048]{1,0:T(8,128)S(1)} collective-permute-done((f32[32,2048]{1,0:T(8,128)S(1)}, f32[32,2048]{1,0:T(8,128)S(1)}, u32[]{:S(2)}, u32[]{:S(2)}) %collective-permute-start.16) | collective-permute-done | bytes 262176 | tf_op jit(solution)/shard_map/ppermute | solution.py:345
  101.5 1.2 collective-permute-start.22
  102.7 9.2 %shard_map.76 = (f32[32,1536]{1,0:T(8,128)S(1)}, f32[32,1536]{1,0:T(8,128)S(1)}, f32[32,1536]{1,0:T(8,128)S(1)}, f32[32,1536]{1,0:T(8,128)S(1)}) custom-call(s32[4]{0:T(128)S(1)} %fusion.5.refs_0_, f32[32,4096]{1,0:T(8,128)S(1)} %get-tuple-element.130.refs_1_, f32[32,4096]{1,0:T(8,128)S(1)} %collective-permute-done.23.refs_2_, ...), custom_call_target="tpu_custom_call" | custom-call | flops 1048576 | bytes 262144 | tf_op jit(solution)/shard_map/pallas_call | solution.py:306
  112.5 1.2 collective-permute-done.27.refs_4_
  113.7 3.0 %shard_map.77 = (f32[32,768]{1,0:T(8,128)S(1)}, f32[32,768]{1,0:T(8,128)S(1)}, f32[32,768]{1,0:T(8,128)S(1)}, f32[32,768]{1,0:T(8,128)S(1)}) custom-call(s32[4]{0:T(128)S(1)} %fusion.5.refs_0_, f32[32,2176]{1,0:T(8,128)S(1)} %get-tuple-element.129.refs_1_, f32[32,2176]{1,0:T(8,128)S(1)} %collective-permute-done.22.refs_2_, ...), custom_call_target="tpu_custom_call" | custom-call | flops 1048576 | bytes 262144 | tf_op jit(solution)/shard_map/pallas_call | solution.py:306
  116.7 2.3 %collective-permute-start.28 = (f32[32,768]{1,0:T(8,128)S(1)}, f32[32,768]{1,0:T(8,128)S(1)}, u32[]{:S(2)}, u32[]{:S(2)}) collective-permute-start(f32[32,768]{1,0:T(8,128)S(1)} %get-tuple-element.141), channel_id=1, source_target_pairs={{0,12},{4,0},{8,4},{12,8},{1,13},{5,1},{9,5},{13,9},{2,14},{6,2},{... | collective-permute-start | bytes 294920 | tf_op jit(solution)/shard_map/ppermute | solution.py:339
  119.8 3.1 %shard_map.78 = (f32[32,896]{1,0:T(8,128)S(1)}, f32[32,896]{1,0:T(8,128)S(1)}, f32[32,896]{1,0:T(8,128)S(1)}, f32[32,896]{1,0:T(8,128)S(1)}) custom-call(s32[4]{0:T(128)S(1)} %fusion.5.refs_0_, f32[32,2176]{1,0:T(8,128)S(1)} %get-tuple-element.129.refs_1_, f32[32,2176]{1,0:T(8,128)S(1)} %collective-permute-done.22.refs_2_, ...), custom_call_target="tpu_custom_call" | custom-call | flops 1048576 | bytes 262144 | tf_op jit(solution)/shard_map/pallas_call | solution.py:306
  122.9 3.2 %collective-permute-start.31 = (f32[32,896]{1,0:T(8,128)S(1)}, f32[32,896]{1,0:T(8,128)S(1)}, u32[]{:S(2)}, u32[]{:S(2)}) collective-permute-start(f32[32,896]{1,0:T(8,128)S(1)} %get-tuple-element.145), channel_id=1, source_target_pairs={{0,12},{4,0},{8,4},{12,8},{1,13},{5,1},{9,5},{13,9},{2,14},{6,2},{... | collective-permute-start | bytes 344072 | tf_op jit(solution)/shard_map/ppermute | solution.py:339
  127.1 2.1 %collective-permute-done.29 = f32[32,768]{1,0:T(8,128)S(1)} collective-permute-done((f32[32,768]{1,0:T(8,128)S(1)}, f32[32,768]{1,0:T(8,128)S(1)}, u32[]{:S(2)}, u32[]{:S(2)}) %collective-permute-start.29) | collective-permute-done | bytes 98336 | tf_op jit(solution)/shard_map/ppermute | solution.py:339
  129.3 1.9 %collective-permute-done.31 = f32[32,896]{1,0:T(8,128)S(1)} collective-permute-done((f32[32,896]{1,0:T(8,128)S(1)}, f32[32,896]{1,0:T(8,128)S(1)}, u32[]{:S(2)}, u32[]{:S(2)}) %collective-permute-start.31) | collective-permute-done | bytes 114720 | tf_op jit(solution)/shard_map/ppermute | solution.py:339
  131.2 7.2 %collective-permute-done.32 = f32[32,896]{1,0:T(8,128)S(1)} collective-permute-done((f32[32,896]{1,0:T(8,128)S(1)}, f32[32,896]{1,0:T(8,128)S(1)}, u32[]{:S(2)}, u32[]{:S(2)}) %collective-permute-start.32) | collective-permute-done | bytes 114720 | tf_op jit(solution)/shard_map/ppermute | solution.py:339
  (81 shorter events, 15.3 us)
Async XLA Ops:
  0.0 20.6 %collective-permute-start.1 = (f32[32,1536]{1,0:T(8,128)}, f32[32,1536]{1,0:T(8,128)S(1)}, u32[]{:S(2)}, u32[]{:S(2)}) collective-permute-start(f32[32,1536]{1,0:T(8,128)} %refs_1_.3), channel_id=1, source_target_pairs={{0,4},{4,8},{8,12},{12,0},{1,5},{5,9},{9,13},{13,1},{2,6},{6,10},{... | collective-permute-start | bytes 589832 | tf_op jit(solution)/shard_map/ppermute | solution.py:339
  3.0 17.6 %collective-permute-start.2 = (f32[32,1536]{1,0:T(8,128)}, f32[32,1536]{1,0:T(8,128)S(1)}, u32[]{:S(2)}, u32[]{:S(2)}) collective-permute-start(f32[32,1536]{1,0:T(8,128)} %refs_1_.3), channel_id=1, source_target_pairs={{0,8},{4,12},{8,0},{12,4},{1,9},{5,13},{9,1},{13,5},{2,10},{6,14},... | collective-permute-start | bytes 589832 | tf_op jit(solution)/shard_map/ppermute | solution.py:339
  5.6 15.0 %collective-permute-start.3 = (f32[32,1536]{1,0:T(8,128)}, f32[32,1536]{1,0:T(8,128)S(1)}, u32[]{:S(2)}, u32[]{:S(2)}) collective-permute-start(f32[32,1536]{1,0:T(8,128)} %refs_1_.3), channel_id=1, source_target_pairs={{0,12},{4,0},{8,4},{12,8},{1,13},{5,1},{9,5},{13,9},{2,14},{6,2},{... | collective-permute-start | bytes 589832 | tf_op jit(solution)/shard_map/ppermute | solution.py:339
  8.1 12.5 %collective-permute-start = (f32[64,128]{1,0:T(8,128)S(1)}, f32[64,128]{1,0:T(8,128)S(1)}, u32[]{:S(2)}, u32[]{:S(2)}) collective-permute-start(f32[64,128]{1,0:T(8,128)S(1)} %shard_map.64.refs_1_.refs_0_), channel_id=1, source_target_pairs={{0,1},{1,0},{2,3},{3,2},{4,5},{5,4},{6,7},{7,6},{8,9},{9,8},{10,11... | collective-permute-start | bytes 98312 | tf_op jit(solution)/shard_map/ppermute | solution.py:342
  20.6 4.0 %collective-permute-start.4 = (f32[64,128]{1,0:T(8,128)S(1)}, f32[64,128]{1,0:T(8,128)S(1)}, u32[]{:S(2)}, u32[]{:S(2)}) collective-permute-start(f32[64,128]{1,0:T(8,128)S(1)} %shard_map.67.refs_2_), channel_id=1, source_target_pairs={{0,2},{1,3},{2,0},{3,1},{4,6},{5,7},{6,4},{7,5},{8,10},{9,11},{10,... | collective-permute-start | bytes 98312 | tf_op jit(solution)/shard_map/ppermute | solution.py:345
  24.8 15.5 %collective-permute-start.5 = (f32[32,1536]{1,0:T(8,128)S(1)}, f32[32,1536]{1,0:T(8,128)S(1)}, u32[]{:S(2)}, u32[]{:S(2)}) collective-permute-start(f32[32,1536]{1,0:T(8,128)S(1)} %get-tuple-element.95.refs_6_.refs_1_), channel_id=1, source_target_pairs={{0,4},{4,8},{8,12},{12,0},{1,5},{5,9},{9,13},{13,1},{2,6},{6,10},{... | collective-permute-start | bytes 589832 | tf_op jit(solution)/shard_map/ppermute | solution.py:339
  27.6 12.7 %collective-permute-start.6 = (f32[32,1536]{1,0:T(8,128)S(1)}, f32[32,1536]{1,0:T(8,128)S(1)}, u32[]{:S(2)}, u32[]{:S(2)}) collective-permute-start(f32[32,1536]{1,0:T(8,128)S(1)} %get-tuple-element.95.refs_6_.refs_1_), channel_id=1, source_target_pairs={{0,12},{4,0},{8,4},{12,8},{1,13},{5,1},{9,5},{13,9},{2,14},{6,2},{... | collective-permute-start | bytes 589832 | tf_op jit(solution)/shard_map/ppermute | solution.py:339
  40.2 2.0 %collective-permute-start.7 = (f32[32,4096]{1,0:T(8,128)S(1)}, f32[32,4096]{1,0:T(8,128)S(1)}, u32[]{:S(2)}, u32[]{:S(2)}) collective-permute-start(f32[32,4096]{1,0:T(8,128)S(1)} %get-tuple-element.86), channel_id=1, source_target_pairs={{0,1},{1,0},{2,3},{3,2},{4,5},{5,4},{6,7},{7,6},{8,9},{9,8},{10,11... | collective-permute-start | bytes 1572872 | tf_op jit(solution)/shard_map/ppermute | solution.py:342
  42.3 17.8 %collective-permute-start.10 = (f32[32,4096]{1,0:T(8,128)S(1)}, f32[32,4096]{1,0:T(8,128)S(1)}, u32[]{:S(2)}, u32[]{:S(2)}) collective-permute-start(f32[32,4096]{1,0:T(8,128)S(1)} %add.59.refs_6_), channel_id=1, source_target_pairs={{0,2},{1,3},{2,0},{3,1},{4,6},{5,7},{6,4},{7,5},{8,10},{9,11},{10,... | collective-permute-start | bytes 1572872 | tf_op jit(solution)/shard_map/ppermute | solution.py:345
  43.9 8.5 %collective-permute-start.8 = (f32[32,1536]{1,0:T(8,128)S(1)}, f32[32,1536]{1,0:T(8,128)S(1)}, u32[]{:S(2)}, u32[]{:S(2)}) collective-permute-start(f32[32,1536]{1,0:T(8,128)S(1)} %collective-permute-done.5.refs_2_), channel_id=1, source_target_pairs={{0,4},{4,8},{8,12},{12,0},{1,5},{5,9},{9,13},{13,1},{2,6},{6,10},{... | collective-permute-start | bytes 589832 | tf_op jit(solution)/shard_map/ppermute | solution.py:339
  52.3 7.8 %collective-permute-start.9 = (f32[32,2048]{1,0:T(8,128)S(1)}, f32[32,2048]{1,0:T(8,128)S(1)}, u32[]{:S(2)}, u32[]{:S(2)}) collective-permute-start(f32[32,2048]{1,0:T(8,128)S(1)} %get-tuple-element.94), channel_id=1, source_target_pairs={{0,1},{1,0},{2,3},{3,2},{4,5},{5,4},{6,7},{7,6},{8,9},{9,8},{10,11... | collective-permute-start | bytes 786440 | tf_op jit(solution)/shard_map/ppermute | solution.py:342
  59.5 7.5 %collective-permute-start.13 = (f32[32,4096]{1,0:T(8,128)S(1)}, f32[32,4096]{1,0:T(8,128)S(1)}, u32[]{:S(2)}, u32[]{:S(2)}) collective-permute-start(f32[32,4096]{1,0:T(8,128)S(1)} %get-tuple-element.109), channel_id=1, source_target_pairs={{0,1},{1,0},{2,3},{3,2},{4,5},{5,4},{6,7},{7,6},{8,9},{9,8},{10,11... | collective-permute-start | bytes 1572872 | tf_op jit(solution)/shard_map/ppermute | solution.py:342
  60.2 8.3 %collective-permute-start.11 = (f32[32,2048]{1,0:T(8,128)S(1)}, f32[32,2048]{1,0:T(8,128)S(1)}, u32[]{:S(2)}, u32[]{:S(2)}) collective-permute-start(f32[32,2048]{1,0:T(8,128)S(1)} %add.60.refs_1_), channel_id=1, source_target_pairs={{0,2},{1,3},{2,0},{3,1},{4,6},{5,7},{6,4},{7,5},{8,10},{9,11},{10,... | collective-permute-start | bytes 786440 | tf_op jit(solution)/shard_map/ppermute | solution.py:345
  60.8 21.4 %collective-permute-start.20 = (f32[32,4096]{1,0:T(8,128)S(1)}, f32[32,4096]{1,0:T(8,128)S(1)}, u32[]{:S(2)}, u32[]{:S(2)}) collective-permute-start(f32[32,4096]{1,0:T(8,128)S(1)} %get-tuple-element.127), channel_id=1, source_target_pairs={{0,1},{1,0},{2,3},{3,2},{4,5},{5,4},{6,7},{7,6},{8,9},{9,8},{10,11... | collective-permute-start | bytes 1572872 | tf_op jit(solution)/shard_map/ppermute | solution.py:342
  60.8 21.5 %collective-permute-start.21 = (f32[32,4096]{1,0:T(8,128)S(1)}, f32[32,4096]{1,0:T(8,128)S(1)}, u32[]{:S(2)}, u32[]{:S(2)}) collective-permute-start(f32[32,4096]{1,0:T(8,128)S(1)} %get-tuple-element.108), channel_id=1, source_target_pairs={{0,1},{1,0},{2,3},{3,2},{4,5},{5,4},{6,7},{7,6},{8,9},{9,8},{10,11... | collective-permute-start | bytes 1572872 | tf_op jit(solution)/shard_map/ppermute | solution.py:342
  68.6 13.7 %collective-permute-start.15 = (f32[32,4096]{1,0:T(8,128)S(1)}, f32[32,4096]{1,0:T(8,128)S(1)}, u32[]{:S(2)}, u32[]{:S(2)}) collective-permute-start(f32[32,4096]{1,0:T(8,128)S(1)} %add.61.refs_9_), channel_id=1, source_target_pairs={{0,2},{1,3},{2,0},{3,1},{4,6},{5,7},{6,4},{7,5},{8,10},{9,11},{10,... | collective-permute-start | bytes 1572872 | tf_op jit(solution)/shard_map/ppermute | solution.py:345
  74.4 7.7 %collective-permute-start.19 = (f32[1,6144]{1,0:T(1,128)S(1)}, f32[1,6144]{1,0:T(1,128)S(1)}, u32[]{:S(2)}, u32[]{:S(2)}) collective-permute-start(f32[1,6144]{1,0:T(1,128)S(1)} %add.63), channel_id=1, source_target_pairs={{0,2},{1,3},{2,0},{3,1},{4,6},{5,7},{6,4},{7,5},{8,10},{9,11},{10,... | collective-permute-start | bytes 73736 | tf_op jit(solution)/shard_map/ppermute | solution.py:345
  82.8 14.9 %collective-permute-start.23 = (f32[32,4096]{1,0:T(8,128)S(1)}, f32[32,4096]{1,0:T(8,128)S(1)}, u32[]{:S(2)}, u32[]{:S(2)}) collective-permute-start(f32[32,4096]{1,0:T(8,128)S(1)} %get-tuple-element.130.refs_1_), channel_id=1, source_target_pairs={{0,2},{1,3},{2,0},{3,1},{4,6},{5,7},{6,4},{7,5},{8,10},{9,11},{10,... | collective-permute-start | bytes 1572872 | tf_op jit(solution)/shard_map/ppermute | solution.py:345
  83.7 14.0 %collective-permute-start.12 = (f32[32,2048]{1,0:T(8,128)S(1)}, f32[32,2048]{1,0:T(8,128)S(1)}, u32[]{:S(2)}, u32[]{:S(2)}) collective-permute-start(f32[32,2048]{1,0:T(8,128)S(1)} %get-tuple-element.111), channel_id=1, source_target_pairs={{0,1},{1,0},{2,3},{3,2},{4,5},{5,4},{6,7},{7,6},{8,9},{9,8},{10,11... | collective-permute-start | bytes 786440 | tf_op jit(solution)/shard_map/ppermute | solution.py:342
  84.2 13.5 %collective-permute-start.17 = (f32[32,2048]{1,0:T(8,128)S(1)}, f32[32,2048]{1,0:T(8,128)S(1)}, u32[]{:S(2)}, u32[]{:S(2)}) collective-permute-start(f32[32,2048]{1,0:T(8,128)S(1)} %get-tuple-element.121), channel_id=1, source_target_pairs={{0,1},{1,0},{2,3},{3,2},{4,5},{5,4},{6,7},{7,6},{8,9},{9,8},{10,11... | collective-permute-start | bytes 786440 | tf_op jit(solution)/shard_map/ppermute | solution.py:342
  85.3 15.3 %collective-permute-start.16 = (f32[32,2048]{1,0:T(8,128)S(1)}, f32[32,2048]{1,0:T(8,128)S(1)}, u32[]{:S(2)}, u32[]{:S(2)}) collective-permute-start(f32[32,2048]{1,0:T(8,128)S(1)} %add.62), channel_id=1, source_target_pairs={{0,2},{1,3},{2,0},{3,1},{4,6},{5,7},{6,4},{7,5},{8,10},{9,11},{10,... | collective-permute-start | bytes 786440 | tf_op jit(solution)/shard_map/ppermute | solution.py:345
  86.5 16.1 %collective-permute-start.24 = (f32[32,4096]{1,0:T(8,128)S(1)}, f32[32,4096]{1,0:T(8,128)S(1)}, u32[]{:S(2)}, u32[]{:S(2)}) collective-permute-start(f32[32,4096]{1,0:T(8,128)S(1)} %get-tuple-element.130.refs_1_), channel_id=1, source_target_pairs={{0,1},{1,0},{2,3},{3,2},{4,5},{5,4},{6,7},{7,6},{8,9},{9,8},{10,11... | collective-permute-start | bytes 1572872 | tf_op jit(solution)/shard_map/ppermute | solution.py:342
  97.7 5.0 %collective-permute-start.25 = (f32[32,4096]{1,0:T(8,128)S(1)}, f32[32,4096]{1,0:T(8,128)S(1)}, u32[]{:S(2)}, u32[]{:S(2)}) collective-permute-start(f32[32,4096]{1,0:T(8,128)S(1)} %collective-permute-done.23.refs_2_), channel_id=1, source_target_pairs={{0,1},{1,0},{2,3},{3,2},{4,5},{5,4},{6,7},{7,6},{8,9},{9,8},{10,11... | collective-permute-start | bytes 1572872 | tf_op jit(solution)/shard_map/ppermute | solution.py:342
  101.5 10.4 %collective-permute-start.22 = (f32[32,2176]{1,0:T(8,128)S(1)}, f32[32,2176]{1,0:T(8,128)S(1)}, u32[]{:S(2)}, u32[]{:S(2)}) collective-permute-start(f32[32,2176]{1,0:T(8,128)S(1)} %get-tuple-element.129.refs_1_), channel_id=1, source_target_pairs={{0,2},{1,3},{2,0},{3,1},{4,6},{5,7},{6,4},{7,5},{8,10},{9,11},{10,... | collective-permute-start | bytes 835592 | tf_op jit(solution)/shard_map/ppermute | solution.py:345
  102.7 9.8 %collective-permute-start.26 = (f32[32,2176]{1,0:T(8,128)S(1)}, f32[32,2176]{1,0:T(8,128)S(1)}, u32[]{:S(2)}, u32[]{:S(2)}) collective-permute-start(f32[32,2176]{1,0:T(8,128)S(1)} %get-tuple-element.129.refs_1_), channel_id=1, source_target_pairs={{0,1},{1,0},{2,3},{3,2},{4,5},{5,4},{6,7},{7,6},{8,9},{9,8},{10,11... | collective-permute-start | bytes 835592 | tf_op jit(solution)/shard_map/ppermute | solution.py:342
  111.9 1.7 %collective-permute-start.27 = (f32[32,2176]{1,0:T(8,128)S(1)}, f32[32,2176]{1,0:T(8,128)S(1)}, u32[]{:S(2)}, u32[]{:S(2)}) collective-permute-start(f32[32,2176]{1,0:T(8,128)S(1)} %collective-permute-done.22.refs_2_), channel_id=1, source_target_pairs={{0,1},{1,0},{2,3},{3,2},{4,5},{5,4},{6,7},{7,6},{8,9},{9,8},{10,11... | collective-permute-start | bytes 835592 | tf_op jit(solution)/shard_map/ppermute | solution.py:342
  116.7 10.5 %collective-permute-start.28 = (f32[32,768]{1,0:T(8,128)S(1)}, f32[32,768]{1,0:T(8,128)S(1)}, u32[]{:S(2)}, u32[]{:S(2)}) collective-permute-start(f32[32,768]{1,0:T(8,128)S(1)} %get-tuple-element.141), channel_id=1, source_target_pairs={{0,12},{4,0},{8,4},{12,8},{1,13},{5,1},{9,5},{13,9},{2,14},{6,2},{... | collective-permute-start | bytes 294920 | tf_op jit(solution)/shard_map/ppermute | solution.py:339
  118.9 10.3 %collective-permute-start.29 = (f32[32,768]{1,0:T(8,128)S(1)}, f32[32,768]{1,0:T(8,128)S(1)}, u32[]{:S(2)}, u32[]{:S(2)}) collective-permute-start(f32[32,768]{1,0:T(8,128)S(1)} %get-tuple-element.142), channel_id=1, source_target_pairs={{0,8},{4,12},{8,0},{12,4},{1,9},{5,13},{9,1},{13,5},{2,10},{6,14},... | collective-permute-start | bytes 294920 | tf_op jit(solution)/shard_map/ppermute | solution.py:339
  118.9 10.3 %collective-permute-start.30 = (f32[32,768]{1,0:T(8,128)S(1)}, f32[32,768]{1,0:T(8,128)S(1)}, u32[]{:S(2)}, u32[]{:S(2)}) collective-permute-start(f32[32,768]{1,0:T(8,128)S(1)} %get-tuple-element.143), channel_id=1, source_target_pairs={{0,4},{4,8},{8,12},{12,0},{1,5},{5,9},{9,13},{13,1},{2,6},{6,10},{... | collective-permute-start | bytes 294920 | tf_op jit(solution)/shard_map/ppermute | solution.py:339
  122.9 8.3 %collective-permute-start.31 = (f32[32,896]{1,0:T(8,128)S(1)}, f32[32,896]{1,0:T(8,128)S(1)}, u32[]{:S(2)}, u32[]{:S(2)}) collective-permute-start(f32[32,896]{1,0:T(8,128)S(1)} %get-tuple-element.145), channel_id=1, source_target_pairs={{0,12},{4,0},{8,4},{12,8},{1,13},{5,1},{9,5},{13,9},{2,14},{6,2},{... | collective-permute-start | bytes 344072 | tf_op jit(solution)/shard_map/ppermute | solution.py:339
  126.0 12.4 %collective-permute-start.32 = (f32[32,896]{1,0:T(8,128)S(1)}, f32[32,896]{1,0:T(8,128)S(1)}, u32[]{:S(2)}, u32[]{:S(2)}) collective-permute-start(f32[32,896]{1,0:T(8,128)S(1)} %get-tuple-element.146), channel_id=1, source_target_pairs={{0,8},{4,12},{8,0},{12,4},{1,9},{5,13},{9,1},{13,5},{2,10},{6,14},... | collective-permute-start | bytes 344072 | tf_op jit(solution)/shard_map/ppermute | solution.py:339
  127.1 11.2 %collective-permute-start.33 = (f32[32,896]{1,0:T(8,128)S(1)}, f32[32,896]{1,0:T(8,128)S(1)}, u32[]{:S(2)}, u32[]{:S(2)}) collective-permute-start(f32[32,896]{1,0:T(8,128)S(1)} %get-tuple-element.147), channel_id=1, source_target_pairs={{0,4},{4,8},{8,12},{12,0},{1,5},{5,9},{9,13},{13,1},{2,6},{6,10},{... | collective-permute-start | bytes 344072 | tf_op jit(solution)/shard_map/ppermute | solution.py:339
  (7 other events, 24.3 us)

commit v14 on v13

--- a/solution.py
+++ b/solution.py
@@ -297,7 +297,7 @@
 
 def backward(acts, weights, place, earlier, part, parts, after):
     slots, block, hidden = len(acts), acts[0].shape[0], sum(w.shape[1] for w in weights[::2])
-    riding = acts[0].shape[1] - hidden if part == parts - 1 else 0
+    riding = acts[0].shape[1] - hidden if part == 0 else 0
     depth = weights[0].shape[0] // parts
     width = divisor(depth, 256, 128)
     out = jax.ShapeDtypeStruct((block, depth + riding), jnp.float32)
@@ -406,10 +406,10 @@
     pre_0 = forward(scaled, in_parts[:8], place, (), [back_1[0]])
     half_1 = halved(back_1, (pre_0, back_0[0]))
     back_1 = exchanged(half_1)
-    parts, sums_2 = prepared(2, [pre_0[0], half_1[0]])
+    half_0 = halved(pre_0)
+    parts, sums_2 = prepared(2, [half_0[0], half_1[0]])
     in_parts += parts
-    half_0 = halved(pre_0, (parts, back_1[0]))
-    pre_1 = forward(scaled, in_parts[8:], place, (), [half_0[0]])
+    pre_1 = forward(scaled, in_parts[8:], place, (), [half_0[0], back_1[0]])
     pre_0 = exchanged(half_0)
 
     gain_sums, _ = tied(jnp.concatenate([sums_0, sums_1, sums_2], axis=1), pre_1)
@@ -440,11 +440,14 @@
     def both_cores(mine):
         return mine + [other_core(block) for block in mine]
 
-    def summed_along_hid(sums):
-        return sum([along_hid(sums[step], -step) for step in range(1, hid_size)], start=sums[0])
-
+    def summed_along_hid(sums, behind=()):
+        arrivals = [along_hid(sums[step], -step) for step in range(1, hid_size)]
+        return sum(tied(arrivals, behind)[0], start=sums[0])
+
+    half_1 = halved(pre_1, pre_0[0])
+    pre_0 = tied(pre_0, half_1[0])[0]
     act_0, sums_0 = slope_product(slice(0, 2 * third), back_0, pre_0, ())
-    pre_1 = exchanged(halved(pre_1, pre_0[0]))
+    pre_1 = exchanged(half_1)
     act_1, _ = slope_product(slice(2 * third, hidden), back_1, pre_1, (sums_0,))
     acts_0, acts_1 = spread_out(act_0), spread_out(act_1)
     sums = backward(both_cores(acts_0), in_parts[:8], place, (), 0, 1, [])
@@ -454,11 +457,12 @@
     ends = []
     for part in range(parts):
         ends.append(backward(acts_1, in_parts[8:], place, sums, part, parts, [ends[-1][0]] if ends else []))
-    *columns, last = [summed_along_hid(end) for end in ends]
+    first = summed_along_hid(ends[0])
+    others = [summed_along_hid(end, first) for end in ends[1:]]
     width = depth // parts
-    normed_grad = jnp.concatenate([*columns, last[:, :width]], axis=1) * norm_gain
-    first, second = last[:, width : width + 1] / model_width, last[:, width + 1 : width + 2] / model_width
-    return inv_std * (normed_grad - first - normed * second)
+    normed_grad = jnp.concatenate([first[:, :width], *others], axis=1) * norm_gain
+    mean, slope = first[:, width : width + 1] / model_width, first[:, width + 1 : width + 2] / model_width
+    return inv_std * (normed_grad - mean - normed * slope)
 
 
 def solution(mesh):

time: 140 us -> 138 us (0.986)
  transfers between devices with their start and end apart: 34 -> 34, of which waited for: 13 -> 12; matrix products, arithmetic and copies ran while one was open for 1% -> 1% of each run, Pallas kernels for 43% -> 44%
where the time goes in v14:
time: 138 us; the launch traced here: 137 us
  Pallas kernels  63.8 us (46%)
  waiting for transfers between devices  40 us (29%)
  starting transfers between devices  30 us (22%)
  local copies, waits for them, and re-layouts  2.04 us (1%)
    ppermute x8, waiting for transfers between devices, next_chip(): lax.ppermute(values, 'emb', [(i, (i + 2) % emb_size) for i in range(emb_s...  23.8 us
    ppermute x12, starting transfers between devices, along_hid(): lax.ppermute(values, 'hid', [(i, (i + steps) % hid_size) for i in range(h...  19.1 us
    pallas_call x2, Pallas kernels, stream(): pl.pallas_call(lambda *refs: stream_kernel(first, depth, refs[0], refs[1:...  18.3 us
    pallas_call x3, Pallas kernels, prepare(): pl.pallas_call(lambda weight_ref, gain_ref, *refs: prepare_kernel(rows, c...  17.2 us
    pallas_call x3, Pallas kernels, backward(): pl.pallas_call(lambda *refs: backward_kernel(part * depth, depth, refs[0]...  15.3 us
    ppermute x12, waiting for transfers between devices, along_hid(): lax.ppermute(values, 'hid', [(i, (i + steps) % hid_size) for i in range(h...  11.7 us
    pallas_call x2, Pallas kernels, forward(): pl.pallas_call(lambda *refs: forward_kernel(refs[0], refs[1:ends[0]], ref...  11.2 us
    ppermute x8, starting transfers between devices, next_chip(): lax.ppermute(values, 'emb', [(i, (i + 2) % emb_size) for i in range(emb_s...  8.1 us
  transfers between devices with their start and end apart: 34, of which 12 were waited for; matrix products, arithmetic and copies ran while one was open for 1% of the time, Pallas kernels for 44%

profile of v14, /device:TPU:0, one launch (start us, length us, event | category | flops | bytes accessed | tf_op | source)
XLA Modules:
  0.0 137.4 jit_solution(12951157850499461661)
XLA Ops:
  0.0 3.0 %collective-permute-start.1 = (f32[32,1536]{1,0:T(8,128)}, f32[32,1536]{1,0:T(8,128)S(1)}, u32[]{:S(2)}, u32[]{:S(2)}) collective-permute-start(f32[32,1536]{1,0:T(8,128)} %refs_1_.3), channel_id=1, source_target_pairs={{0,4},{4,8},{8,12},{12,0},{1,5},{5,9},{9,13},{13,1},{2,6},{6,10},{... | collective-permute-start | bytes 589832 | tf_op jit(solution)/shard_map/ppermute | solution.py:339
  3.0 2.6 %collective-permute-start.2 = (f32[32,1536]{1,0:T(8,128)}, f32[32,1536]{1,0:T(8,128)S(1)}, u32[]{:S(2)}, u32[]{:S(2)}) collective-permute-start(f32[32,1536]{1,0:T(8,128)} %refs_1_.3), channel_id=1, source_target_pairs={{0,8},{4,12},{8,0},{12,4},{1,9},{5,13},{9,1},{13,5},{2,10},{6,14},... | collective-permute-start | bytes 589832 | tf_op jit(solution)/shard_map/ppermute | solution.py:339
  5.6 1.3 collective-permute-start.3
  8.1 1.0 broadcast_in_dim.19.gain_ref
  9.1 5.7 %shard_map.65 = (bf16[1536,1024]{1,0:T(8,128)(2,1)S(1)}, bf16[1536,1024]{1,0:T(8,128)(2,1)S(1)}, bf16[1536,1024]{1,0:T(8,128)(2,1)S(1)}, bf16[1536,1024]{1,0:T(8,128)(2,1)S(1)}, f32[1,2048]{1,0:T(1,128)S(1)}) custom-call(f32[1536,6144]{1,0:T(8,128)} %weight_ref.5, f32[1536,1]{1,0:T(8,128)S(1)} %broadcast_in_dim.19.gain_ref, s32[4]{0:T(128)S(1)} %fusion.5.refs_0_, ...), custom_call_target="tpu_custom_call" | custom-call | flops 1048576 | bytes 262144 | tf_op jit(solution)/shard_map/pallas_call | solution.py:132
  14.8 5.7 %shard_map.66 = (bf16[1536,1024]{1,0:T(8,128)(2,1)S(1)}, bf16[1536,1024]{1,0:T(8,128)(2,1)S(1)}, bf16[1536,1024]{1,0:T(8,128)(2,1)S(1)}, bf16[1536,1024]{1,0:T(8,128)(2,1)S(1)}, f32[1,2048]{1,0:T(1,128)S(1)}) custom-call(f32[1536,6144]{1,0:T(8,128)} %weight_ref.5, f32[1536,1]{1,0:T(8,128)S(1)} %broadcast_in_dim.19.gain_ref, ...), custom_call_target="tpu_custom_call" | custom-call | flops 1048576 | bytes 262144 | tf_op jit(solution)/shard_map/pallas_call | solution.py:132
  20.6 1.6 %collective-permute-start.4 = (f32[64,128]{1,0:T(8,128)S(1)}, f32[64,128]{1,0:T(8,128)S(1)}, u32[]{:S(2)}, u32[]{:S(2)}) collective-permute-start(f32[64,128]{1,0:T(8,128)S(1)} %shard_map.67.refs_2_), channel_id=1, source_target_pairs={{0,2},{1,3},{2,0},{3,1},{4,6},{5,7},{6,4},{7,5},{8,10},{9,11},{10,... | collective-permute-start | bytes 98312 | tf_op jit(solution)/shard_map/ppermute | solution.py:345
  22.2 2.4 %collective-permute-done.4.refs_3_ = f32[64,128]{1,0:T(8,128)S(1)} collective-permute-done((f32[64,128]{1,0:T(8,128)S(1)}, f32[64,128]{1,0:T(8,128)S(1)}, u32[]{:S(2)}, u32[]{:S(2)}) %collective-permute-start.4) | collective-permute-done | bytes 32800 | tf_op jit(solution)/shard_map/ppermute | solution.py:345
  24.8 2.8 %collective-permute-start.5 = (f32[32,1536]{1,0:T(8,128)S(1)}, f32[32,1536]{1,0:T(8,128)S(1)}, u32[]{:S(2)}, u32[]{:S(2)}) collective-permute-start(f32[32,1536]{1,0:T(8,128)S(1)} %get-tuple-element.103.refs_6_.refs_1_), channel_id=1, source_target_pairs={{0,4},{4,8},{8,12},{12,0},{1,5},{5,9},{9,13},{13,1},{2,6},{6,10},{... | collective-permute-start | bytes 589832 | tf_op jit(solution)/shard_map/ppermute | solution.py:339
  27.6 1.1 collective-permute-start.6
  28.7 11.5 %shard_map.69 = (f32[32,4096]{1,0:T(8,128)S(1)}, f32[32,4096]{1,0:T(8,128)S(1)}, f32[32,4096]{1,0:T(8,128)S(1)}, f32[32,4096]{1,0:T(8,128)S(1)}) custom-call(s32[4]{0:T(128)S(1)} %fusion.5.refs_0_, f32[32,1536]{1,0:T(8,128)S(1)} %copy-done.2, f32[32,1536]{1,0:T(8,128)S(1)} %collective-permute-done.1.refs_3_.refs_2_, ...), custom_call_target="tpu_custom_call" | custom-call | flops 1048576 | bytes 262144 | tf_op jit(solution)/shard_map/pallas_call | solution.py:251
  40.3 1.9 %collective-permute-done.7 = f32[32,4096]{1,0:T(8,128)S(1)} collective-permute-done((f32[32,4096]{1,0:T(8,128)S(1)}, f32[32,4096]{1,0:T(8,128)S(1)}, u32[]{:S(2)}, u32[]{:S(2)}) %collective-permute-start.7) | collective-permute-done | bytes 524320 | tf_op jit(solution)/shard_map/ppermute | solution.py:342
  42.3 1.6 %collective-permute-start.10 = (f32[32,4096]{1,0:T(8,128)S(1)}, f32[32,4096]{1,0:T(8,128)S(1)}, u32[]{:S(2)}, u32[]{:S(2)}) collective-permute-start(f32[32,4096]{1,0:T(8,128)S(1)} %add.59.refs_6_), channel_id=1, source_target_pairs={{0,2},{1,3},{2,0},{3,1},{4,6},{5,7},{6,4},{7,5},{8,10},{9,11},{10,... | collective-permute-start | bytes 1572872 | tf_op jit(solution)/shard_map/ppermute | solution.py:345
  44.7 6.8 %shard_map.70 = (f32[32,2048]{1,0:T(8,128)S(1)}, f32[32,2048]{1,0:T(8,128)S(1)}, f32[32,2048]{1,0:T(8,128)S(1)}, f32[32,2048]{1,0:T(8,128)S(1)}) custom-call(s32[4]{0:T(128)S(1)} %fusion.5.refs_0_, f32[32,1536]{1,0:T(8,128)S(1)} %copy-done.2, f32[32,1536]{1,0:T(8,128)S(1)} %collective-permute-done.1.refs_3_.refs_2_, ...), custom_call_target="tpu_custom_call" | custom-call | flops 1048576 | bytes 262144 | tf_op jit(solution)/shard_map/pallas_call | solution.py:251
  52.3 7.2 %shard_map.71 = (f32[32,4096]{1,0:T(8,128)S(1)}, f32[32,4096]{1,0:T(8,128)S(1)}, f32[32,4096]{1,0:T(8,128)S(1)}, f32[32,4096]{1,0:T(8,128)S(1)}) custom-call(s32[4]{0:T(128)S(1)} %fusion.5.refs_0_, f32[32,1536]{1,0:T(8,128)S(1)} %get-tuple-element.103.refs_6_.refs_1_, f32[32,1536]{1,0:T(8,128)S(1)} %collective-permute-done.5.refs_2_, ...), custom_call_target="tpu_custom_call" | custom-call | flops 1048576 | bytes 262144 | tf_op jit(solution)/shard_map/pallas_call | solution.py:209
  61.7 1.2 collective-permute-start.15
  62.9 5.7 %shard_map.72 = (bf16[1536,1024]{1,0:T(8,128)(2,1)S(1)}, bf16[1536,1024]{1,0:T(8,128)(2,1)S(1)}, bf16[1536,1024]{1,0:T(8,128)(2,1)S(1)}, bf16[1536,1024]{1,0:T(8,128)(2,1)S(1)}, f32[1,2048]{1,0:T(1,128)S(1)}) custom-call(f32[1536,6144]{1,0:T(8,128)} %weight_ref.5, f32[1536,1]{1,0:T(8,128)S(1)} %broadcast_in_dim.19.gain_ref, ...), custom_call_target="tpu_custom_call" | custom-call | flops 1048576 | bytes 262144 | tf_op jit(solution)/shard_map/pallas_call | solution.py:132
  69.4 3.9 %shard_map.73 = (f32[32,2048]{1,0:T(8,128)S(1)}, f32[32,2048]{1,0:T(8,128)S(1)}, f32[32,2048]{1,0:T(8,128)S(1)}, f32[32,2048]{1,0:T(8,128)S(1)}) custom-call(s32[4]{0:T(128)S(1)} %fusion.5.refs_0_, f32[32,1536]{1,0:T(8,128)S(1)} %get-tuple-element.103.refs_6_.refs_1_, f32[32,1536]{1,0:T(8,128)S(1)} %collective-permute-done.5.refs_2_, ...), custom_call_target="tpu_custom_call" | custom-call | flops 1048576 | bytes 262144 | tf_op jit(solution)/shard_map/pallas_call | solution.py:209
  74.0 1.0 collective-permute-done.18
  75.6 4.6 %collective-permute-done.19 = f32[1,6144]{1,0:T(1,128)S(1)} collective-permute-done((f32[1,6144]{1,0:T(1,128)S(1)}, f32[1,6144]{1,0:T(1,128)S(1)}, u32[]{:S(2)}, u32[]{:S(2)}) %collective-permute-start.19) | collective-permute-done | bytes 24608 | tf_op jit(solution)/shard_map/ppermute | solution.py:345
  82.0 1.5 %collective-permute-start.16 = (f32[32,2048]{1,0:T(8,128)S(1)}, f32[32,2048]{1,0:T(8,128)S(1)}, u32[]{:S(2)}, u32[]{:S(2)}) collective-permute-start(f32[32,2048]{1,0:T(8,128)S(1)} %add.62), channel_id=1, source_target_pairs={{0,2},{1,3},{2,0},{3,1},{4,6},{5,7},{6,4},{7,5},{8,10},{9,11},{10,... | collective-permute-start | bytes 786440 | tf_op jit(solution)/shard_map/ppermute | solution.py:345
  83.5 12.3 %collective-permute-done.23.refs_2_ = f32[32,4096]{1,0:T(8,128)S(1)} collective-permute-done((f32[32,4096]{1,0:T(8,128)S(1)}, f32[32,4096]{1,0:T(8,128)S(1)}, u32[]{:S(2)}, u32[]{:S(2)}) %collective-permute-start.23) | collective-permute-done | bytes 524320 | tf_op jit(solution)/shard_map/ppermute | solution.py:345
  95.8 3.7 %collective-permute-done.16.refs_3_ = f32[32,2048]{1,0:T(8,128)S(1)} collective-permute-done((f32[32,2048]{1,0:T(8,128)S(1)}, f32[32,2048]{1,0:T(8,128)S(1)}, u32[]{:S(2)}, u32[]{:S(2)}) %collective-permute-start.16) | collective-permute-done | bytes 262176 | tf_op jit(solution)/shard_map/ppermute | solution.py:345
  101.0 9.2 %shard_map.76 = (f32[32,1536]{1,0:T(8,128)S(1)}, f32[32,1536]{1,0:T(8,128)S(1)}, f32[32,1536]{1,0:T(8,128)S(1)}, f32[32,1536]{1,0:T(8,128)S(1)}) custom-call(s32[4]{0:T(128)S(1)} %fusion.5.refs_0_, f32[32,4096]{1,0:T(8,128)S(1)} %get-tuple-element.140.refs_1_, f32[32,4096]{1,0:T(8,128)S(1)} %collective-permute-done.23.refs_2_, ...), custom_call_target="tpu_custom_call" | custom-call | flops 1048576 | bytes 262144 | tf_op jit(solution)/shard_map/pallas_call | solution.py:306
  110.9 1.2 collective-permute-done.27.refs_4_
  112.0 3.1 %shard_map.77 = (f32[32,896]{1,0:T(8,128)S(1)}, f32[32,896]{1,0:T(8,128)S(1)}, f32[32,896]{1,0:T(8,128)S(1)}, f32[32,896]{1,0:T(8,128)S(1)}) custom-call(s32[4]{0:T(128)S(1)} %fusion.5.refs_0_, f32[32,2176]{1,0:T(8,128)S(1)} %get-tuple-element.139.refs_1_, f32[32,2176]{1,0:T(8,128)S(1)} %collective-permute-done.22.refs_2_, ...), custom_call_target="tpu_custom_call" | custom-call | flops 1048576 | bytes 262144 | tf_op jit(solution)/shard_map/pallas_call | solution.py:306
  115.1 2.3 %collective-permute-start.28 = (f32[32,896]{1,0:T(8,128)S(1)}, f32[32,896]{1,0:T(8,128)S(1)}, u32[]{:S(2)}, u32[]{:S(2)}) collective-permute-start(f32[32,896]{1,0:T(8,128)S(1)} %get-tuple-element.151), channel_id=1, source_target_pairs={{0,12},{4,0},{8,4},{12,8},{1,13},{5,1},{9,5},{13,9},{2,14},{6,2},{... | collective-permute-start | bytes 344072 | tf_op jit(solution)/shard_map/ppermute | solution.py:339
  118.2 3.0 %shard_map.78 = (f32[32,768]{1,0:T(8,128)S(1)}, f32[32,768]{1,0:T(8,128)S(1)}, f32[32,768]{1,0:T(8,128)S(1)}, f32[32,768]{1,0:T(8,128)S(1)}) custom-call(s32[4]{0:T(128)S(1)} %fusion.5.refs_0_, f32[32,2176]{1,0:T(8,128)S(1)} %get-tuple-element.139.refs_1_, f32[32,2176]{1,0:T(8,128)S(1)} %collective-permute-done.22.refs_2_, ...), custom_call_target="tpu_custom_call" | custom-call | flops 1048576 | bytes 262144 | tf_op jit(solution)/shard_map/pallas_call | solution.py:306
  121.3 3.1 %collective-permute-start.31 = (f32[32,768]{1,0:T(8,128)S(1)}, f32[32,768]{1,0:T(8,128)S(1)}, u32[]{:S(2)}, u32[]{:S(2)}) collective-permute-start(f32[32,768]{1,0:T(8,128)S(1)} %get-tuple-element.158), channel_id=1, source_target_pairs={{0,12},{4,0},{8,4},{12,8},{1,13},{5,1},{9,5},{13,9},{2,14},{6,2},{... | collective-permute-start | bytes 294920 | tf_op jit(solution)/shard_map/ppermute | solution.py:339
  124.4 1.1 collective-permute-start.32
  125.5 7.2 %collective-permute-done.29 = f32[32,896]{1,0:T(8,128)S(1)} collective-permute-done((f32[32,896]{1,0:T(8,128)S(1)}, f32[32,896]{1,0:T(8,128)S(1)}, u32[]{:S(2)}, u32[]{:S(2)}) %collective-permute-start.29) | collective-permute-done | bytes 114720 | tf_op jit(solution)/shard_map/ppermute | solution.py:339
  133.0 3.6 %collective-permute-done.32 = f32[32,768]{1,0:T(8,128)S(1)} collective-permute-done((f32[32,768]{1,0:T(8,128)S(1)}, f32[32,768]{1,0:T(8,128)S(1)}, u32[]{:S(2)}, u32[]{:S(2)}) %collective-permute-start.32) | collective-permute-done | bytes 98336 | tf_op jit(solution)/shard_map/ppermute | solution.py:339
  (81 shorter events, 13.0 us)
Async XLA Ops:
  0.0 20.6 %collective-permute-start.1 = (f32[32,1536]{1,0:T(8,128)}, f32[32,1536]{1,0:T(8,128)S(1)}, u32[]{:S(2)}, u32[]{:S(2)}) collective-permute-start(f32[32,1536]{1,0:T(8,128)} %refs_1_.3), channel_id=1, source_target_pairs={{0,4},{4,8},{8,12},{12,0},{1,5},{5,9},{9,13},{13,1},{2,6},{6,10},{... | collective-permute-start | bytes 589832 | tf_op jit(solution)/shard_map/ppermute | solution.py:339
  3.0 17.6 %collective-permute-start.2 = (f32[32,1536]{1,0:T(8,128)}, f32[32,1536]{1,0:T(8,128)S(1)}, u32[]{:S(2)}, u32[]{:S(2)}) collective-permute-start(f32[32,1536]{1,0:T(8,128)} %refs_1_.3), channel_id=1, source_target_pairs={{0,8},{4,12},{8,0},{12,4},{1,9},{5,13},{9,1},{13,5},{2,10},{6,14},... | collective-permute-start | bytes 589832 | tf_op jit(solution)/shard_map/ppermute | solution.py:339
  5.6 15.0 %collective-permute-start.3 = (f32[32,1536]{1,0:T(8,128)}, f32[32,1536]{1,0:T(8,128)S(1)}, u32[]{:S(2)}, u32[]{:S(2)}) collective-permute-start(f32[32,1536]{1,0:T(8,128)} %refs_1_.3), channel_id=1, source_target_pairs={{0,12},{4,0},{8,4},{12,8},{1,13},{5,1},{9,5},{13,9},{2,14},{6,2},{... | collective-permute-start | bytes 589832 | tf_op jit(solution)/shard_map/ppermute | solution.py:339
  8.1 12.5 %collective-permute-start = (f32[64,128]{1,0:T(8,128)S(1)}, f32[64,128]{1,0:T(8,128)S(1)}, u32[]{:S(2)}, u32[]{:S(2)}) collective-permute-start(f32[64,128]{1,0:T(8,128)S(1)} %shard_map.64.refs_1_.refs_0_), channel_id=1, source_target_pairs={{0,1},{1,0},{2,3},{3,2},{4,5},{5,4},{6,7},{7,6},{8,9},{9,8},{10,11... | collective-permute-start | bytes 98312 | tf_op jit(solution)/shard_map/ppermute | solution.py:342
  20.6 4.0 %collective-permute-start.4 = (f32[64,128]{1,0:T(8,128)S(1)}, f32[64,128]{1,0:T(8,128)S(1)}, u32[]{:S(2)}, u32[]{:S(2)}) collective-permute-start(f32[64,128]{1,0:T(8,128)S(1)} %shard_map.67.refs_2_), channel_id=1, source_target_pairs={{0,2},{1,3},{2,0},{3,1},{4,6},{5,7},{6,4},{7,5},{8,10},{9,11},{10,... | collective-permute-start | bytes 98312 | tf_op jit(solution)/shard_map/ppermute | solution.py:345
  24.8 15.5 %collective-permute-start.5 = (f32[32,1536]{1,0:T(8,128)S(1)}, f32[32,1536]{1,0:T(8,128)S(1)}, u32[]{:S(2)}, u32[]{:S(2)}) collective-permute-start(f32[32,1536]{1,0:T(8,128)S(1)} %get-tuple-element.103.refs_6_.refs_1_), channel_id=1, source_target_pairs={{0,4},{4,8},{8,12},{12,0},{1,5},{5,9},{9,13},{13,1},{2,6},{6,10},{... | collective-permute-start | bytes 589832 | tf_op jit(solution)/shard_map/ppermute | solution.py:339
  27.6 12.7 %collective-permute-start.6 = (f32[32,1536]{1,0:T(8,128)S(1)}, f32[32,1536]{1,0:T(8,128)S(1)}, u32[]{:S(2)}, u32[]{:S(2)}) collective-permute-start(f32[32,1536]{1,0:T(8,128)S(1)} %get-tuple-element.103.refs_6_.refs_1_), channel_id=1, source_target_pairs={{0,12},{4,0},{8,4},{12,8},{1,13},{5,1},{9,5},{13,9},{2,14},{6,2},{... | collective-permute-start | bytes 589832 | tf_op jit(solution)/shard_map/ppermute | solution.py:339
  40.2 2.0 %collective-permute-start.7 = (f32[32,4096]{1,0:T(8,128)S(1)}, f32[32,4096]{1,0:T(8,128)S(1)}, u32[]{:S(2)}, u32[]{:S(2)}) collective-permute-start(f32[32,4096]{1,0:T(8,128)S(1)} %get-tuple-element.94), channel_id=1, source_target_pairs={{0,1},{1,0},{2,3},{3,2},{4,5},{5,4},{6,7},{7,6},{8,9},{9,8},{10,11... | collective-permute-start | bytes 1572872 | tf_op jit(solution)/shard_map/ppermute | solution.py:342
  42.3 17.8 %collective-permute-start.10 = (f32[32,4096]{1,0:T(8,128)S(1)}, f32[32,4096]{1,0:T(8,128)S(1)}, u32[]{:S(2)}, u32[]{:S(2)}) collective-permute-start(f32[32,4096]{1,0:T(8,128)S(1)} %add.59.refs_6_), channel_id=1, source_target_pairs={{0,2},{1,3},{2,0},{3,1},{4,6},{5,7},{6,4},{7,5},{8,10},{9,11},{10,... | collective-permute-start | bytes 1572872 | tf_op jit(solution)/shard_map/ppermute | solution.py:345
  43.8 8.5 %collective-permute-start.8 = (f32[32,1536]{1,0:T(8,128)S(1)}, f32[32,1536]{1,0:T(8,128)S(1)}, u32[]{:S(2)}, u32[]{:S(2)}) collective-permute-start(f32[32,1536]{1,0:T(8,128)S(1)} %collective-permute-done.5.refs_2_), channel_id=1, source_target_pairs={{0,4},{4,8},{8,12},{12,0},{1,5},{5,9},{9,13},{13,1},{2,6},{6,10},{... | collective-permute-start | bytes 589832 | tf_op jit(solution)/shard_map/ppermute | solution.py:339
  52.3 7.8 %collective-permute-start.9 = (f32[32,2048]{1,0:T(8,128)S(1)}, f32[32,2048]{1,0:T(8,128)S(1)}, u32[]{:S(2)}, u32[]{:S(2)}) collective-permute-start(f32[32,2048]{1,0:T(8,128)S(1)} %get-tuple-element.102), channel_id=1, source_target_pairs={{0,1},{1,0},{2,3},{3,2},{4,5},{5,4},{6,7},{7,6},{8,9},{9,8},{10,11... | collective-permute-start | bytes 786440 | tf_op jit(solution)/shard_map/ppermute | solution.py:342
  59.5 2.1 %collective-permute-start.13 = (f32[32,4096]{1,0:T(8,128)S(1)}, f32[32,4096]{1,0:T(8,128)S(1)}, u32[]{:S(2)}, u32[]{:S(2)}) collective-permute-start(f32[32,4096]{1,0:T(8,128)S(1)} %get-tuple-element.117), channel_id=1, source_target_pairs={{0,1},{1,0},{2,3},{3,2},{4,5},{5,4},{6,7},{7,6},{8,9},{9,8},{10,11... | collective-permute-start | bytes 1572872 | tf_op jit(solution)/shard_map/ppermute | solution.py:342
  60.1 9.2 %collective-permute-start.11 = (f32[32,2048]{1,0:T(8,128)S(1)}, f32[32,2048]{1,0:T(8,128)S(1)}, u32[]{:S(2)}, u32[]{:S(2)}) collective-permute-start(f32[32,2048]{1,0:T(8,128)S(1)} %add.60.refs_1_), channel_id=1, source_target_pairs={{0,2},{1,3},{2,0},{3,1},{4,6},{5,7},{6,4},{7,5},{8,10},{9,11},{10,... | collective-permute-start | bytes 786440 | tf_op jit(solution)/shard_map/ppermute | solution.py:345
  60.8 19.6 %collective-permute-start.20 = (f32[32,4096]{1,0:T(8,128)S(1)}, f32[32,4096]{1,0:T(8,128)S(1)}, u32[]{:S(2)}, u32[]{:S(2)}) collective-permute-start(f32[32,4096]{1,0:T(8,128)S(1)} %get-tuple-element.134), channel_id=1, source_target_pairs={{0,1},{1,0},{2,3},{3,2},{4,5},{5,4},{6,7},{7,6},{8,9},{9,8},{10,11... | collective-permute-start | bytes 1572872 | tf_op jit(solution)/shard_map/ppermute | solution.py:342
  60.8 19.6 %collective-permute-start.21 = (f32[32,4096]{1,0:T(8,128)S(1)}, f32[32,4096]{1,0:T(8,128)S(1)}, u32[]{:S(2)}, u32[]{:S(2)}) collective-permute-start(f32[32,4096]{1,0:T(8,128)S(1)} %get-tuple-element.116), channel_id=1, source_target_pairs={{0,1},{1,0},{2,3},{3,2},{4,5},{5,4},{6,7},{7,6},{8,9},{9,8},{10,11... | collective-permute-start | bytes 1572872 | tf_op jit(solution)/shard_map/ppermute | solution.py:342
  61.7 18.5 %collective-permute-start.15 = (f32[32,4096]{1,0:T(8,128)S(1)}, f32[32,4096]{1,0:T(8,128)S(1)}, u32[]{:S(2)}, u32[]{:S(2)}) collective-permute-start(f32[32,4096]{1,0:T(8,128)S(1)} %add.61.refs_0_.refs_9_), channel_id=1, source_target_pairs={{0,2},{1,3},{2,0},{3,1},{4,6},{5,7},{6,4},{7,5},{8,10},{9,11},{10,... | collective-permute-start | bytes 1572872 | tf_op jit(solution)/shard_map/ppermute | solution.py:345
  73.3 6.9 %collective-permute-start.14 = (f32[32,2048]{1,0:T(8,128)S(1)}, f32[32,2048]{1,0:T(8,128)S(1)}, u32[]{:S(2)}, u32[]{:S(2)}) collective-permute-start(f32[32,2048]{1,0:T(8,128)S(1)} %get-tuple-element.125), channel_id=1, source_target_pairs={{0,1},{1,0},{2,3},{3,2},{4,5},{5,4},{6,7},{7,6},{8,9},{9,8},{10,11... | collective-permute-start | bytes 786440 | tf_op jit(solution)/shard_map/ppermute | solution.py:342
  75.0 5.2 %collective-permute-start.19 = (f32[1,6144]{1,0:T(1,128)S(1)}, f32[1,6144]{1,0:T(1,128)S(1)}, u32[]{:S(2)}, u32[]{:S(2)}) collective-permute-start(f32[1,6144]{1,0:T(1,128)S(1)} %add.63), channel_id=1, source_target_pairs={{0,2},{1,3},{2,0},{3,1},{4,6},{5,7},{6,4},{7,5},{8,10},{9,11},{10,... | collective-permute-start | bytes 73736 | tf_op jit(solution)/shard_map/ppermute | solution.py:345
  80.9 14.9 %collective-permute-start.23 = (f32[32,4096]{1,0:T(8,128)S(1)}, f32[32,4096]{1,0:T(8,128)S(1)}, u32[]{:S(2)}, u32[]{:S(2)}) collective-permute-start(f32[32,4096]{1,0:T(8,128)S(1)} %get-tuple-element.140.refs_1_), channel_id=1, source_target_pairs={{0,2},{1,3},{2,0},{3,1},{4,6},{5,7},{6,4},{7,5},{8,10},{9,11},{10,... | collective-permute-start | bytes 1572872 | tf_op jit(solution)/shard_map/ppermute | solution.py:345
  81.5 14.3 %collective-permute-start.12 = (f32[32,2048]{1,0:T(8,128)S(1)}, f32[32,2048]{1,0:T(8,128)S(1)}, u32[]{:S(2)}, u32[]{:S(2)}) collective-permute-start(f32[32,2048]{1,0:T(8,128)S(1)} %get-tuple-element.119), channel_id=1, source_target_pairs={{0,1},{1,0},{2,3},{3,2},{4,5},{5,4},{6,7},{7,6},{8,9},{9,8},{10,11... | collective-permute-start | bytes 786440 | tf_op jit(solution)/shard_map/ppermute | solution.py:342
  81.5 14.3 %collective-permute-start.17 = (f32[32,2048]{1,0:T(8,128)S(1)}, f32[32,2048]{1,0:T(8,128)S(1)}, u32[]{:S(2)}, u32[]{:S(2)}) collective-permute-start(f32[32,2048]{1,0:T(8,128)S(1)} %get-tuple-element.128), channel_id=1, source_target_pairs={{0,1},{1,0},{2,3},{3,2},{4,5},{5,4},{6,7},{7,6},{8,9},{9,8},{10,11... | collective-permute-start | bytes 786440 | tf_op jit(solution)/shard_map/ppermute | solution.py:342
  82.0 17.6 %collective-permute-start.16 = (f32[32,2048]{1,0:T(8,128)S(1)}, f32[32,2048]{1,0:T(8,128)S(1)}, u32[]{:S(2)}, u32[]{:S(2)}) collective-permute-start(f32[32,2048]{1,0:T(8,128)S(1)} %add.62), channel_id=1, source_target_pairs={{0,2},{1,3},{2,0},{3,1},{4,6},{5,7},{6,4},{7,5},{8,10},{9,11},{10,... | collective-permute-start | bytes 786440 | tf_op jit(solution)/shard_map/ppermute | solution.py:345
  83.5 17.6 %collective-permute-start.24 = (f32[32,4096]{1,0:T(8,128)S(1)}, f32[32,4096]{1,0:T(8,128)S(1)}, u32[]{:S(2)}, u32[]{:S(2)}) collective-permute-start(f32[32,4096]{1,0:T(8,128)S(1)} %get-tuple-element.140.refs_1_), channel_id=1, source_target_pairs={{0,1},{1,0},{2,3},{3,2},{4,5},{5,4},{6,7},{7,6},{8,9},{9,8},{10,11... | collective-permute-start | bytes 1572872 | tf_op jit(solution)/shard_map/ppermute | solution.py:342
  95.8 5.2 %collective-permute-start.25 = (f32[32,4096]{1,0:T(8,128)S(1)}, f32[32,4096]{1,0:T(8,128)S(1)}, u32[]{:S(2)}, u32[]{:S(2)}) collective-permute-start(f32[32,4096]{1,0:T(8,128)S(1)} %collective-permute-done.23.refs_2_), channel_id=1, source_target_pairs={{0,1},{1,0},{2,3},{3,2},{4,5},{5,4},{6,7},{7,6},{8,9},{9,8},{10,11... | collective-permute-start | bytes 1572872 | tf_op jit(solution)/shard_map/ppermute | solution.py:342
  100.5 9.8 %collective-permute-start.22 = (f32[32,2176]{1,0:T(8,128)S(1)}, f32[32,2176]{1,0:T(8,128)S(1)}, u32[]{:S(2)}, u32[]{:S(2)}) collective-permute-start(f32[32,2176]{1,0:T(8,128)S(1)} %get-tuple-element.139.refs_1_), channel_id=1, source_target_pairs={{0,2},{1,3},{2,0},{3,1},{4,6},{5,7},{6,4},{7,5},{8,10},{9,11},{10,... | collective-permute-start | bytes 835592 | tf_op jit(solution)/shard_map/ppermute | solution.py:345
  101.0 9.8 %collective-permute-start.26 = (f32[32,2176]{1,0:T(8,128)S(1)}, f32[32,2176]{1,0:T(8,128)S(1)}, u32[]{:S(2)}, u32[]{:S(2)}) collective-permute-start(f32[32,2176]{1,0:T(8,128)S(1)} %get-tuple-element.139.refs_1_), channel_id=1, source_target_pairs={{0,1},{1,0},{2,3},{3,2},{4,5},{5,4},{6,7},{7,6},{8,9},{9,8},{10,11... | collective-permute-start | bytes 835592 | tf_op jit(solution)/shard_map/ppermute | solution.py:342
  115.1 10.4 %collective-permute-start.28 = (f32[32,896]{1,0:T(8,128)S(1)}, f32[32,896]{1,0:T(8,128)S(1)}, u32[]{:S(2)}, u32[]{:S(2)}) collective-permute-start(f32[32,896]{1,0:T(8,128)S(1)} %get-tuple-element.151), channel_id=1, source_target_pairs={{0,12},{4,0},{8,4},{12,8},{1,13},{5,1},{9,5},{13,9},{2,14},{6,2},{... | collective-permute-start | bytes 344072 | tf_op jit(solution)/shard_map/ppermute | solution.py:339
  117.4 15.4 %collective-permute-start.29 = (f32[32,896]{1,0:T(8,128)S(1)}, f32[32,896]{1,0:T(8,128)S(1)}, u32[]{:S(2)}, u32[]{:S(2)}) collective-permute-start(f32[32,896]{1,0:T(8,128)S(1)} %get-tuple-element.152), channel_id=1, source_target_pairs={{0,8},{4,12},{8,0},{12,4},{1,9},{5,13},{9,1},{13,5},{2,10},{6,14},... | collective-permute-start | bytes 344072 | tf_op jit(solution)/shard_map/ppermute | solution.py:339
  117.4 15.4 %collective-permute-start.30 = (f32[32,896]{1,0:T(8,128)S(1)}, f32[32,896]{1,0:T(8,128)S(1)}, u32[]{:S(2)}, u32[]{:S(2)}) collective-permute-start(f32[32,896]{1,0:T(8,128)S(1)} %get-tuple-element.153), channel_id=1, source_target_pairs={{0,4},{4,8},{8,12},{12,0},{1,5},{5,9},{9,13},{13,1},{2,6},{6,10},{... | collective-permute-start | bytes 344072 | tf_op jit(solution)/shard_map/ppermute | solution.py:339
  121.3 11.7 %collective-permute-start.31 = (f32[32,768]{1,0:T(8,128)S(1)}, f32[32,768]{1,0:T(8,128)S(1)}, u32[]{:S(2)}, u32[]{:S(2)}) collective-permute-start(f32[32,768]{1,0:T(8,128)S(1)} %get-tuple-element.158), channel_id=1, source_target_pairs={{0,12},{4,0},{8,4},{12,8},{1,13},{5,1},{9,5},{13,9},{2,14},{6,2},{... | collective-permute-start | bytes 294920 | tf_op jit(solution)/shard_map/ppermute | solution.py:339
  124.4 12.2 %collective-permute-start.32 = (f32[32,768]{1,0:T(8,128)S(1)}, f32[32,768]{1,0:T(8,128)S(1)}, u32[]{:S(2)}, u32[]{:S(2)}) collective-permute-start(f32[32,768]{1,0:T(8,128)S(1)} %get-tuple-element.159), channel_id=1, source_target_pairs={{0,8},{4,12},{8,0},{12,4},{1,9},{5,13},{9,1},{13,5},{2,10},{6,14},... | collective-permute-start | bytes 294920 | tf_op jit(solution)/shard_map/ppermute | solution.py:339
  125.5 11.1 %collective-permute-start.33 = (f32[32,768]{1,0:T(8,128)S(1)}, f32[32,768]{1,0:T(8,128)S(1)}, u32[]{:S(2)}, u32[]{:S(2)}) collective-permute-start(f32[32,768]{1,0:T(8,128)S(1)} %get-tuple-element.160), channel_id=1, source_target_pairs={{0,4},{4,8},{8,12},{12,0},{1,5},{5,9},{9,13},{13,1},{2,6},{6,10},{... | collective-permute-start | bytes 294920 | tf_op jit(solution)/shard_map/ppermute | solution.py:339
  (7 other events, 24.3 us)

commit v15 on v14

--- a/solution.py
+++ b/solution.py
@@ -76,19 +76,21 @@
 
 
 def slope_kernel(terms, *refs):
-    back_refs, pre_refs, (bias_ref, weight_ref) = refs[:terms], refs[terms : 2 * terms], refs[2 * terms : 2 * terms + 2]
-    *sums_refs, act_ref, out_sums_ref = refs[2 * terms + 2 :]
+    back_refs, pre_refs, bias_ref = refs[:terms], refs[terms : 2 * terms], refs[2 * terms]
+    *others, act_ref, sums_ref = refs[2 * terms + 1 :]
     hidden = bias_ref.shape[1]
     product = sum(ref[...] for ref in pre_refs)
     act = sum(ref[...] for ref in back_refs) * gelu_slope(product + bias_ref[...])
     act_ref[:, :hidden] = act
-    lane = lax.broadcasted_iota(jnp.int32, out_sums_ref.shape, 1)
-    first = jnp.sum(act * weight_ref[...], axis=1, keepdims=True)
-    second = jnp.sum(act * product, axis=1, keepdims=True)
-    sums = jnp.where(lane == 0, first, jnp.where(lane == 1, second, 0.0)) + sum(ref[...] for ref in sums_refs)
-    out_sums_ref[...] = sums
-    if act_ref.shape[1] > hidden:
+    lane = lax.broadcasted_iota(jnp.int32, sums_ref.shape, 1)
+    sums = jnp.where(lane == 1, jnp.sum(act * product, axis=1, keepdims=True), 0.0)
+    if others:
+        weight_ref, earlier_ref, earlier_weight_ref, earlier_sums_ref = others
+        first = jnp.sum(act * weight_ref[...], axis=1, keepdims=True)
+        first = first + jnp.sum(earlier_ref[...] * earlier_weight_ref[...], axis=1, keepdims=True)
+        sums = sums + earlier_sums_ref[...] + jnp.where(lane == 0, first, 0.0)
         act_ref[:, hidden:] = sums
+    sums_ref[...] = sums
 
 
 def prepare_kernel(rows, columns, block, depth, weight_ref, gain_ref, *refs):
@@ -290,9 +292,8 @@
         result[...] = value
         for b, out_ref in enumerate(out_refs):
             rows = result[pl.ds(pl.multiple_of(place_ref[b] * block, block), block), :]
-            if earlier_refs:
-                rows = rows + earlier_refs[b][:, at]
-            out_ref[:, pl.ds(pl.multiple_of(step * width, width), width)] = rows
+            local = pl.ds(pl.multiple_of(step * width, width), width)
+            out_ref[:, local] = rows + earlier_refs[b][:, local] if earlier_refs else rows
 
 
 def backward(acts, weights, place, earlier, part, parts, after):
@@ -400,34 +401,38 @@
     back_0 = stream(grads, out_weight, place, 0, 2 * third, [scaled[0]])
     back_0, (scaled[1], scaled[-1]) = tied(back_0, (scaled[1], scaled[-1]))
     half_0 = halved(back_0)
+    back_0 = exchanged(half_0)
+    pre_0 = forward(scaled, in_parts, place, (), [half_0[0]])
+    pre_0, back_0 = tied(pre_0, back_0)
+    half_0 = halved(pre_0)
+    pre_0 = exchanged(half_0)
     back_1 = stream(grads, out_weight, place, 2 * third, third, [half_0[0]])
-    back_0 = exchanged(half_0)
-    back_1, scaled = tied(back_1, scaled)
-    pre_0 = forward(scaled, in_parts[:8], place, (), [back_1[0]])
-    half_1 = halved(back_1, (pre_0, back_0[0]))
+    parts, sums_2 = prepared(2, [back_1[0]])
+    in_parts += parts
+    half_1 = halved(back_1, parts)
     back_1 = exchanged(half_1)
-    half_0 = halved(pre_0)
-    parts, sums_2 = prepared(2, [half_0[0], half_1[0]])
-    in_parts += parts
-    pre_1 = forward(scaled, in_parts[8:], place, (), [half_0[0], back_1[0]])
-    pre_0 = exchanged(half_0)
+
+    def slope_product(span, back, pre, others, after):
+        width = span.stop - span.start
+        return call(
+            functools.partial(slope_kernel, len(back)),
+            tuple(
+                jax.ShapeDtypeStruct((tokens, n), jnp.float32) for n in (width + 128 * bool(others), 128)
+            ),
+            (*back, *pre, in_bias[None, span], *others),
+            after,
+        )
+
+    act_0, sums_act = slope_product(slice(0, 2 * third), back_0, pre_0, (), (parts[0],))
+    pre_1 = forward(scaled, in_parts[8:], place, (), [act_0, half_1[0]])
 
     gain_sums, _ = tied(jnp.concatenate([sums_0, sums_1, sums_2], axis=1), pre_1)
     gain_sums = passing = gain_sums + other_core(gain_sums)
     for _ in range(1, chips):
         passing = next_chip(passing)
         gain_sums = gain_sums + passing
-
-    def slope_product(span, back, pre, sums):
-        width = span.stop - span.start
-        return call(
-            functools.partial(slope_kernel, len(back)),
-            tuple(
-                jax.ShapeDtypeStruct((tokens, n), jnp.float32) for n in (width + 128 * len(sums), 128)
-            ),
-            (*back, *pre, in_bias[None, span], gain_sums[:, span], *sums),
-            (),
-        )
+    half_1 = halved(pre_1, back_1[0])
+    pre_1 = exchanged(half_1)
 
     def spread_out(act):
         mine = [None] * chips
@@ -444,19 +449,24 @@
         arrivals = [along_hid(sums[step], -step) for step in range(1, hid_size)]
         return sum(tied(arrivals, behind)[0], start=sums[0])
 
-    half_1 = halved(pre_1, pre_0[0])
-    pre_0 = tied(pre_0, half_1[0])[0]
-    act_0, sums_0 = slope_product(slice(0, 2 * third), back_0, pre_0, ())
-    pre_1 = exchanged(half_1)
-    act_1, _ = slope_product(slice(2 * third, hidden), back_1, pre_1, (sums_0,))
+    act_1, _ = slope_product(
+        slice(2 * third, hidden),
+        back_1,
+        pre_1,
+        (gain_sums[:, 2 * third :], act_0, gain_sums[:, : 2 * third], sums_act),
+        (),
+    )
     acts_0, acts_1 = spread_out(act_0), spread_out(act_1)
-    sums = backward(both_cores(acts_0), in_parts[:8], place, (), 0, 1, [])
+    acts_0[1:] = tied(acts_0[1:], act_1)[0]
+    acts_0 = both_cores(acts_0)
+    parts = 2 if depth % 512 == 0 else 1
+    sums = [backward(acts_0, in_parts[:8], place, (), part, parts, ()) for part in range(parts)]
     acts_1[1:], sums = tied(acts_1[1:], sums)
     acts_1 = both_cores(acts_1)
-    parts = 2 if depth % 512 == 0 else 1
     ends = []
     for part in range(parts):
-        ends.append(backward(acts_1, in_parts[8:], place, sums, part, parts, [ends[-1][0]] if ends else []))
+        after = [ends[-1][0]] if ends else []
+        ends.append(backward(acts_1, in_parts[8:], place, sums[part], part, parts, after))
     first = summed_along_hid(ends[0])
     others = [summed_along_hid(end, first) for end in ends[1:]]
     width = depth // parts

time: 138 us -> 141 us (1.022)
    ppermute x12, waiting for transfers between devices: 11.7 us -> 17 us  [along_hid(): lax.ppermute(values, 'hid', [(i, (i + steps) % hid_size) for i in range(h...]
    ppermute x8, waiting for transfers between devices: 23.8 us -> 18.5 us  [next_chip(): lax.ppermute(values, 'emb', [(i, (i + 2) % emb_size) for i in range(emb_s...]
    ppermute x14, waiting for transfers between devices: 4.44 us -> 5.86 us  [other_core(): return lax.ppermute(values, 'emb', [(i, i ^ 1) for i in range(emb_size)])]
    pallas_call x3 -> x4, Pallas kernels: 15.3 us -> 16.3 us  [backward(): pl.pallas_call(lambda *refs: backward_kernel(part * depth, depth, refs[0]...]
  transfers between devices with their start and end apart: 34 -> 34, of which waited for: 12 -> 11; matrix products, arithmetic and copies ran while one was open for 1% -> 1% of each run, Pallas kernels for 44% -> 44%
where the time goes in v15:
time: 141 us; the launch traced here: 140 us
  Pallas kernels  64.7 us (46%)
  waiting for transfers between devices  41.4 us (29%)
  starting transfers between devices  30.5 us (22%)
  local copies, waits for them, and re-layouts  2.04 us (1%)
    ppermute x12, starting transfers between devices, along_hid(): lax.ppermute(values, 'hid', [(i, (i + steps) % hid_size) for i in range(h...  18.9 us
    ppermute x8, waiting for transfers between devices, next_chip(): lax.ppermute(values, 'emb', [(i, (i + 2) % emb_size) for i in range(emb_s...  18.5 us
    pallas_call x2, Pallas kernels, stream(): pl.pallas_call(lambda *refs: stream_kernel(first, depth, refs[0], refs[1:...  18.3 us
    pallas_call x3, Pallas kernels, prepare(): pl.pallas_call(lambda weight_ref, gain_ref, *refs: prepare_kernel(rows, c...  17.2 us
    ppermute x12, waiting for transfers between devices, along_hid(): lax.ppermute(values, 'hid', [(i, (i + steps) % hid_size) for i in range(h...  17 us
    pallas_call x4, Pallas kernels, backward(): pl.pallas_call(lambda *refs: backward_kernel(part * depth, depth, refs[0]...  16.3 us
    pallas_call x2, Pallas kernels, forward(): pl.pallas_call(lambda *refs: forward_kernel(refs[0], refs[1:ends[0]], ref...  11.1 us
    ppermute x8, starting transfers between devices, next_chip(): lax.ppermute(values, 'emb', [(i, (i + 2) % emb_size) for i in range(emb_s...  8.8 us
  transfers between devices with their start and end apart: 34, of which 11 were waited for; matrix products, arithmetic and copies ran while one was open for 1% of the time, Pallas kernels for 44%

profile of v15, /device:TPU:0, one launch (start us, length us, event | category | flops | bytes accessed | tf_op | source)
XLA Modules:
  0.0 140.4 jit_solution(16018227462137255799)
XLA Ops:
  0.0 3.0 %collective-permute-start.1 = (f32[32,1536]{1,0:T(8,128)}, f32[32,1536]{1,0:T(8,128)S(1)}, u32[]{:S(2)}, u32[]{:S(2)}) collective-permute-start(f32[32,1536]{1,0:T(8,128)} %refs_1_.3), channel_id=1, source_target_pairs={{0,4},{4,8},{8,12},{12,0},{1,5},{5,9},{9,13},{13,1},{2,6},{6,10},{... | collective-permute-start | bytes 589832 | tf_op jit(solution)/shard_map/ppermute | solution.py:340
  3.0 2.6 %collective-permute-start.2 = (f32[32,1536]{1,0:T(8,128)}, f32[32,1536]{1,0:T(8,128)S(1)}, u32[]{:S(2)}, u32[]{:S(2)}) collective-permute-start(f32[32,1536]{1,0:T(8,128)} %refs_1_.3), channel_id=1, source_target_pairs={{0,8},{4,12},{8,0},{12,4},{1,9},{5,13},{9,1},{13,5},{2,10},{6,14},... | collective-permute-start | bytes 589832 | tf_op jit(solution)/shard_map/ppermute | solution.py:340
  5.6 1.3 collective-permute-start.3
  9.1 5.7 %shard_map.65 = (bf16[1536,1024]{1,0:T(8,128)(2,1)S(1)}, bf16[1536,1024]{1,0:T(8,128)(2,1)S(1)}, bf16[1536,1024]{1,0:T(8,128)(2,1)S(1)}, bf16[1536,1024]{1,0:T(8,128)(2,1)S(1)}, f32[1,2048]{1,0:T(1,128)S(1)}) custom-call(f32[1536,6144]{1,0:T(8,128)} %weight_ref.5, f32[1536,1]{1,0:T(8,128)S(1)} %broadcast_in_dim.19.gain_ref, s32[4]{0:T(128)S(1)} %fusion.5.refs_0_, ...), custom_call_target="tpu_custom_call" | custom-call | flops 1048576 | bytes 262144 | tf_op jit(solution)/shard_map/pallas_call | solution.py:134
  14.8 5.7 %shard_map.66 = (bf16[1536,1024]{1,0:T(8,128)(2,1)S(1)}, bf16[1536,1024]{1,0:T(8,128)(2,1)S(1)}, bf16[1536,1024]{1,0:T(8,128)(2,1)S(1)}, bf16[1536,1024]{1,0:T(8,128)(2,1)S(1)}, f32[1,2048]{1,0:T(1,128)S(1)}) custom-call(f32[1536,6144]{1,0:T(8,128)} %weight_ref.5, f32[1536,1]{1,0:T(8,128)S(1)} %broadcast_in_dim.19.gain_ref, ...), custom_call_target="tpu_custom_call" | custom-call | flops 1048576 | bytes 262144 | tf_op jit(solution)/shard_map/pallas_call | solution.py:134
  20.6 1.6 %collective-permute-start.4 = (f32[64,128]{1,0:T(8,128)S(1)}, f32[64,128]{1,0:T(8,128)S(1)}, u32[]{:S(2)}, u32[]{:S(2)}) collective-permute-start(f32[64,128]{1,0:T(8,128)S(1)} %shard_map.67.refs_2_), channel_id=1, source_target_pairs={{0,2},{1,3},{2,0},{3,1},{4,6},{5,7},{6,4},{7,5},{8,10},{9,11},{10,... | collective-permute-start | bytes 98312 | tf_op jit(solution)/shard_map/ppermute | solution.py:346
  22.2 2.4 %collective-permute-done.4.refs_3_ = f32[64,128]{1,0:T(8,128)S(1)} collective-permute-done((f32[64,128]{1,0:T(8,128)S(1)}, f32[64,128]{1,0:T(8,128)S(1)}, u32[]{:S(2)}, u32[]{:S(2)}) %collective-permute-start.4) | collective-permute-done | bytes 32800 | tf_op jit(solution)/shard_map/ppermute | solution.py:346
  24.8 2.8 %collective-permute-start.5 = (f32[32,1536]{1,0:T(8,128)S(1)}, f32[32,1536]{1,0:T(8,128)S(1)}, u32[]{:S(2)}, u32[]{:S(2)}) collective-permute-start(f32[32,1536]{1,0:T(8,128)S(1)} %get-tuple-element.93.refs_6_.refs_1_), channel_id=1, source_target_pairs={{0,4},{4,8},{8,12},{12,0},{1,5},{5,9},{9,13},{13,1},{2,6},{6,10},{... | collective-permute-start | bytes 589832 | tf_op jit(solution)/shard_map/ppermute | solution.py:340
  28.7 11.5 %shard_map.69 = (f32[32,4096]{1,0:T(8,128)S(1)}, f32[32,4096]{1,0:T(8,128)S(1)}, f32[32,4096]{1,0:T(8,128)S(1)}, f32[32,4096]{1,0:T(8,128)S(1)}) custom-call(s32[4]{0:T(128)S(1)} %fusion.5.refs_0_, f32[32,1536]{1,0:T(8,128)S(1)} %copy-done.2, f32[32,1536]{1,0:T(8,128)S(1)} %collective-permute-done.1.refs_3_.refs_2_, ...), custom_call_target="tpu_custom_call" | custom-call | flops 1048576 | bytes 262144 | tf_op jit(solution)/shard_map/pallas_call | solution.py:253
  40.8 1.4 collective-permute-done.8
  42.3 1.6 %collective-permute-start.9 = (f32[32,4096]{1,0:T(8,128)S(1)}, f32[32,4096]{1,0:T(8,128)S(1)}, u32[]{:S(2)}, u32[]{:S(2)}) collective-permute-start(f32[32,4096]{1,0:T(8,128)S(1)} %add.59.refs_13_), channel_id=1, source_target_pairs={{0,2},{1,3},{2,0},{3,1},{4,6},{5,7},{6,4},{7,5},{8,10},{9,11},{10,... | collective-permute-start | bytes 1572872 | tf_op jit(solution)/shard_map/ppermute | solution.py:346
  44.7 7.6 %collective-permute-done.7.refs_3_ = f32[32,1536]{1,0:T(8,128)S(1)} collective-permute-done((f32[32,1536]{1,0:T(8,128)S(1)}, f32[32,1536]{1,0:T(8,128)S(1)}, u32[]{:S(2)}, u32[]{:S(2)}) %collective-permute-start.7) | collective-permute-done | bytes 196640 | tf_op jit(solution)/shard_map/ppermute | solution.py:340
  52.3 7.2 %shard_map.70 = (f32[32,4096]{1,0:T(8,128)S(1)}, f32[32,4096]{1,0:T(8,128)S(1)}, f32[32,4096]{1,0:T(8,128)S(1)}, f32[32,4096]{1,0:T(8,128)S(1)}) custom-call(s32[4]{0:T(128)S(1)} %fusion.5.refs_0_, f32[32,1536]{1,0:T(8,128)S(1)} %get-tuple-element.93.refs_6_.refs_1_, f32[32,1536]{1,0:T(8,128)S(1)} %collective-permute-done.5.refs_2_, ...), custom_call_target="tpu_custom_call" | custom-call | flops 1048576 | bytes 262144 | tf_op jit(solution)/shard_map/pallas_call | solution.py:211
  60.1 1.4 collective-permute-done.11
  62.2 6.8 %shard_map.71 = (f32[32,2048]{1,0:T(8,128)S(1)}, f32[32,2048]{1,0:T(8,128)S(1)}, f32[32,2048]{1,0:T(8,128)S(1)}, f32[32,2048]{1,0:T(8,128)S(1)}) custom-call(s32[4]{0:T(128)S(1)} %fusion.5.refs_0_, f32[32,1536]{1,0:T(8,128)S(1)} %copy-done.2, f32[32,1536]{1,0:T(8,128)S(1)} %collective-permute-done.1.refs_3_.refs_2_, ...), custom_call_target="tpu_custom_call" | custom-call | flops 1048576 | bytes 262144 | tf_op jit(solution)/shard_map/pallas_call | solution.py:253
  69.1 5.7 %shard_map.72 = (bf16[1536,1024]{1,0:T(8,128)(2,1)S(1)}, bf16[1536,1024]{1,0:T(8,128)(2,1)S(1)}, bf16[1536,1024]{1,0:T(8,128)(2,1)S(1)}, bf16[1536,1024]{1,0:T(8,128)(2,1)S(1)}, f32[1,2048]{1,0:T(1,128)S(1)}) custom-call(f32[1536,6144]{1,0:T(8,128)} %weight_ref.5, f32[1536,1]{1,0:T(8,128)S(1)} %broadcast_in_dim.19.gain_ref, ...), custom_call_target="tpu_custom_call" | custom-call | flops 1048576 | bytes 262144 | tf_op jit(solution)/shard_map/pallas_call | solution.py:134
  74.9 1.6 %collective-permute-start.13 = (f32[32,2048]{1,0:T(8,128)S(1)}, f32[32,2048]{1,0:T(8,128)S(1)}, u32[]{:S(2)}, u32[]{:S(2)}) collective-permute-start(f32[32,2048]{1,0:T(8,128)S(1)} %add.61.refs_10_), channel_id=1, source_target_pairs={{0,2},{1,3},{2,0},{3,1},{4,6},{5,7},{6,4},{7,5},{8,10},{9,11},{10,... | collective-permute-start | bytes 786440 | tf_op jit(solution)/shard_map/ppermute | solution.py:346
  77.0 3.9 %shard_map.74 = (f32[32,2048]{1,0:T(8,128)S(1)}, f32[32,2048]{1,0:T(8,128)S(1)}, f32[32,2048]{1,0:T(8,128)S(1)}, f32[32,2048]{1,0:T(8,128)S(1)}) custom-call(s32[4]{0:T(128)S(1)} %fusion.5.refs_0_, f32[32,1536]{1,0:T(8,128)S(1)} %get-tuple-element.93.refs_6_.refs_1_, f32[32,1536]{1,0:T(8,128)S(1)} %collective-permute-done.5.refs_2_, ...), custom_call_target="tpu_custom_call" | custom-call | flops 1048576 | bytes 262144 | tf_op jit(solution)/shard_map/pallas_call | solution.py:211
  82.0 1.6 %collective-permute-done.13.refs_0_ = f32[32,2048]{1,0:T(8,128)S(1)} collective-permute-done((f32[32,2048]{1,0:T(8,128)S(1)}, f32[32,2048]{1,0:T(8,128)S(1)}, u32[]{:S(2)}, u32[]{:S(2)}) %collective-permute-start.13) | collective-permute-done | bytes 262176 | tf_op jit(solution)/shard_map/ppermute | solution.py:346
  83.6 1.8 %collective-permute-start.18 = (f32[32,2048]{1,0:T(8,128)S(1)}, f32[32,2048]{1,0:T(8,128)S(1)}, u32[]{:S(2)}, u32[]{:S(2)}) collective-permute-start(f32[32,2048]{1,0:T(8,128)S(1)} %add.62), channel_id=1, source_target_pairs={{0,2},{1,3},{2,0},{3,1},{4,6},{5,7},{6,4},{7,5},{8,10},{9,11},{10,... | collective-permute-start | bytes 786440 | tf_op jit(solution)/shard_map/ppermute | solution.py:346
  85.6 1.2 collective-permute-done.20
  87.1 14.5 %collective-permute-done.21 = f32[1,6144]{1,0:T(1,128)S(1)} collective-permute-done((f32[1,6144]{1,0:T(1,128)S(1)}, f32[1,6144]{1,0:T(1,128)S(1)}, u32[]{:S(2)}, u32[]{:S(2)}) %collective-permute-start.21) | collective-permute-done | bytes 24608 | tf_op jit(solution)/shard_map/ppermute | solution.py:346
  104.7 5.1 %shard_map.77 = (f32[32,768]{1,0:T(8,128)S(1)}, f32[32,768]{1,0:T(8,128)S(1)}, f32[32,768]{1,0:T(8,128)S(1)}, f32[32,768]{1,0:T(8,128)S(1)}) custom-call(s32[4]{0:T(128)S(1)} %fusion.5.refs_0_, f32[32,4096]{1,0:T(8,128)S(1)} %get-tuple-element.130.refs_9_.refs_8_.refs_1_, f32[32,4096]{1,0:T(8,128)S(1)} %collective-permute-done.23.refs_2_, ...), custom_call_target="tpu_custom_call" | custom-call | flops 1048576 | bytes 262144 | tf_op jit(solution)/shard_map/pallas_call | solution.py:307
  109.8 5.1 %shard_map.76 = (f32[32,768]{1,0:T(8,128)S(1)}, f32[32,768]{1,0:T(8,128)S(1)}, f32[32,768]{1,0:T(8,128)S(1)}, f32[32,768]{1,0:T(8,128)S(1)}) custom-call(s32[4]{0:T(128)S(1)} %fusion.5.refs_0_, f32[32,4096]{1,0:T(8,128)S(1)} %get-tuple-element.130.refs_9_.refs_8_.refs_1_, f32[32,4096]{1,0:T(8,128)S(1)} %collective-permute-done.23.refs_2_, ...), custom_call_target="tpu_custom_call" | custom-call | flops 1048576 | bytes 262144 | tf_op jit(solution)/shard_map/pallas_call | solution.py:307
  115.4 1.2 collective-permute-done.27.refs_4_
  116.6 3.1 %shard_map.78 = (f32[32,896]{1,0:T(8,128)S(1)}, f32[32,896]{1,0:T(8,128)S(1)}, f32[32,896]{1,0:T(8,128)S(1)}, f32[32,896]{1,0:T(8,128)S(1)}) custom-call(s32[4]{0:T(128)S(1)} %fusion.5.refs_0_, f32[32,2176]{1,0:T(8,128)S(1)} %get-tuple-element.141.refs_1_, f32[32,2176]{1,0:T(8,128)S(1)} %collective-permute-done.22.refs_2_, ...), custom_call_target="tpu_custom_call" | custom-call | flops 1048576 | bytes 262144 | tf_op jit(solution)/shard_map/pallas_call | solution.py:307
  120.3 1.4 %collective-permute-start.30 = (f32[32,896]{1,0:T(8,128)S(1)}, f32[32,896]{1,0:T(8,128)S(1)}, u32[]{:S(2)}, u32[]{:S(2)}) collective-permute-start(f32[32,896]{1,0:T(8,128)S(1)} %get-tuple-element.159), channel_id=1, source_target_pairs={{0,4},{4,8},{8,12},{12,0},{1,5},{5,9},{9,13},{13,1},{2,6},{6,10},{... | collective-permute-start | bytes 344072 | tf_op jit(solution)/shard_map/ppermute | solution.py:340
  121.8 3.0 %shard_map.79 = (f32[32,768]{1,0:T(8,128)S(1)}, f32[32,768]{1,0:T(8,128)S(1)}, f32[32,768]{1,0:T(8,128)S(1)}, f32[32,768]{1,0:T(8,128)S(1)}) custom-call(s32[4]{0:T(128)S(1)} %fusion.5.refs_0_, f32[32,2176]{1,0:T(8,128)S(1)} %get-tuple-element.141.refs_1_, f32[32,2176]{1,0:T(8,128)S(1)} %collective-permute-done.22.refs_2_, ...), custom_call_target="tpu_custom_call" | custom-call | flops 1048576 | bytes 262144 | tf_op jit(solution)/shard_map/pallas_call | solution.py:307
  124.9 2.4 %collective-permute-start.31 = (f32[32,768]{1,0:T(8,128)S(1)}, f32[32,768]{1,0:T(8,128)S(1)}, u32[]{:S(2)}, u32[]{:S(2)}) collective-permute-start(f32[32,768]{1,0:T(8,128)S(1)} %get-tuple-element.168), channel_id=1, source_target_pairs={{0,12},{4,0},{8,4},{12,8},{1,13},{5,1},{9,5},{13,9},{2,14},{6,2},{... | collective-permute-start | bytes 294920 | tf_op jit(solution)/shard_map/ppermute | solution.py:340
  128.0 1.8 %collective-permute-start.33 = (f32[32,768]{1,0:T(8,128)S(1)}, f32[32,768]{1,0:T(8,128)S(1)}, u32[]{:S(2)}, u32[]{:S(2)}) collective-permute-start(f32[32,768]{1,0:T(8,128)S(1)} %get-tuple-element.170), channel_id=1, source_target_pairs={{0,4},{4,8},{8,12},{12,0},{1,5},{5,9},{9,13},{13,1},{2,6},{6,10},{... | collective-permute-start | bytes 294920 | tf_op jit(solution)/shard_map/ppermute | solution.py:340
  129.9 3.1 %collective-permute-done.29 = f32[32,896]{1,0:T(8,128)S(1)} collective-permute-done((f32[32,896]{1,0:T(8,128)S(1)}, f32[32,896]{1,0:T(8,128)S(1)}, u32[]{:S(2)}, u32[]{:S(2)}) %collective-permute-start.29) | collective-permute-done | bytes 114720 | tf_op jit(solution)/shard_map/ppermute | solution.py:340
  133.2 6.4 %collective-permute-done.32 = f32[32,768]{1,0:T(8,128)S(1)} collective-permute-done((f32[32,768]{1,0:T(8,128)S(1)}, f32[32,768]{1,0:T(8,128)S(1)}, u32[]{:S(2)}, u32[]{:S(2)}) %collective-permute-start.32) | collective-permute-done | bytes 98336 | tf_op jit(solution)/shard_map/ppermute | solution.py:340
  (82 shorter events, 14.4 us)
Async XLA Ops:
  0.0 20.6 %collective-permute-start.1 = (f32[32,1536]{1,0:T(8,128)}, f32[32,1536]{1,0:T(8,128)S(1)}, u32[]{:S(2)}, u32[]{:S(2)}) collective-permute-start(f32[32,1536]{1,0:T(8,128)} %refs_1_.3), channel_id=1, source_target_pairs={{0,4},{4,8},{8,12},{12,0},{1,5},{5,9},{9,13},{13,1},{2,6},{6,10},{... | collective-permute-start | bytes 589832 | tf_op jit(solution)/shard_map/ppermute | solution.py:340
  3.0 17.6 %collective-permute-start.2 = (f32[32,1536]{1,0:T(8,128)}, f32[32,1536]{1,0:T(8,128)S(1)}, u32[]{:S(2)}, u32[]{:S(2)}) collective-permute-start(f32[32,1536]{1,0:T(8,128)} %refs_1_.3), channel_id=1, source_target_pairs={{0,8},{4,12},{8,0},{12,4},{1,9},{5,13},{9,1},{13,5},{2,10},{6,14},... | collective-permute-start | bytes 589832 | tf_op jit(solution)/shard_map/ppermute | solution.py:340
  5.6 15.0 %collective-permute-start.3 = (f32[32,1536]{1,0:T(8,128)}, f32[32,1536]{1,0:T(8,128)S(1)}, u32[]{:S(2)}, u32[]{:S(2)}) collective-permute-start(f32[32,1536]{1,0:T(8,128)} %refs_1_.3), channel_id=1, source_target_pairs={{0,12},{4,0},{8,4},{12,8},{1,13},{5,1},{9,5},{13,9},{2,14},{6,2},{... | collective-permute-start | bytes 589832 | tf_op jit(solution)/shard_map/ppermute | solution.py:340
  8.1 12.5 %collective-permute-start = (f32[64,128]{1,0:T(8,128)S(1)}, f32[64,128]{1,0:T(8,128)S(1)}, u32[]{:S(2)}, u32[]{:S(2)}) collective-permute-start(f32[64,128]{1,0:T(8,128)S(1)} %shard_map.64.refs_1_.refs_0_), channel_id=1, source_target_pairs={{0,1},{1,0},{2,3},{3,2},{4,5},{5,4},{6,7},{7,6},{8,9},{9,8},{10,11... | collective-permute-start | bytes 98312 | tf_op jit(solution)/shard_map/ppermute | solution.py:343
  20.6 4.0 %collective-permute-start.4 = (f32[64,128]{1,0:T(8,128)S(1)}, f32[64,128]{1,0:T(8,128)S(1)}, u32[]{:S(2)}, u32[]{:S(2)}) collective-permute-start(f32[64,128]{1,0:T(8,128)S(1)} %shard_map.67.refs_2_), channel_id=1, source_target_pairs={{0,2},{1,3},{2,0},{3,1},{4,6},{5,7},{6,4},{7,5},{8,10},{9,11},{10,... | collective-permute-start | bytes 98312 | tf_op jit(solution)/shard_map/ppermute | solution.py:346
  24.8 15.5 %collective-permute-start.5 = (f32[32,1536]{1,0:T(8,128)S(1)}, f32[32,1536]{1,0:T(8,128)S(1)}, u32[]{:S(2)}, u32[]{:S(2)}) collective-permute-start(f32[32,1536]{1,0:T(8,128)S(1)} %get-tuple-element.93.refs_6_.refs_1_), channel_id=1, source_target_pairs={{0,4},{4,8},{8,12},{12,0},{1,5},{5,9},{9,13},{13,1},{2,6},{6,10},{... | collective-permute-start | bytes 589832 | tf_op jit(solution)/shard_map/ppermute | solution.py:340
  27.6 12.7 %collective-permute-start.6 = (f32[32,1536]{1,0:T(8,128)S(1)}, f32[32,1536]{1,0:T(8,128)S(1)}, u32[]{:S(2)}, u32[]{:S(2)}) collective-permute-start(f32[32,1536]{1,0:T(8,128)S(1)} %get-tuple-element.93.refs_6_.refs_1_), channel_id=1, source_target_pairs={{0,12},{4,0},{8,4},{12,8},{1,13},{5,1},{9,5},{13,9},{2,14},{6,2},{... | collective-permute-start | bytes 589832 | tf_op jit(solution)/shard_map/ppermute | solution.py:340
  40.2 2.0 %collective-permute-start.8 = (f32[32,4096]{1,0:T(8,128)S(1)}, f32[32,4096]{1,0:T(8,128)S(1)}, u32[]{:S(2)}, u32[]{:S(2)}) collective-permute-start(f32[32,4096]{1,0:T(8,128)S(1)} %get-tuple-element.107), channel_id=1, source_target_pairs={{0,1},{1,0},{2,3},{3,2},{4,5},{5,4},{6,7},{7,6},{8,9},{9,8},{10,11... | collective-permute-start | bytes 1572872 | tf_op jit(solution)/shard_map/ppermute | solution.py:343
  40.3 19.2 %collective-permute-start.10 = (f32[32,4096]{1,0:T(8,128)S(1)}, f32[32,4096]{1,0:T(8,128)S(1)}, u32[]{:S(2)}, u32[]{:S(2)}) collective-permute-start(f32[32,4096]{1,0:T(8,128)S(1)} %get-tuple-element.113), channel_id=1, source_target_pairs={{0,1},{1,0},{2,3},{3,2},{4,5},{5,4},{6,7},{7,6},{8,9},{9,8},{10,11... | collective-permute-start | bytes 1572872 | tf_op jit(solution)/shard_map/ppermute | solution.py:343
  42.3 17.2 %collective-permute-start.9 = (f32[32,4096]{1,0:T(8,128)S(1)}, f32[32,4096]{1,0:T(8,128)S(1)}, u32[]{:S(2)}, u32[]{:S(2)}) collective-permute-start(f32[32,4096]{1,0:T(8,128)S(1)} %add.59.refs_13_), channel_id=1, source_target_pairs={{0,2},{1,3},{2,0},{3,1},{4,6},{5,7},{6,4},{7,5},{8,10},{9,11},{10,... | collective-permute-start | bytes 1572872 | tf_op jit(solution)/shard_map/ppermute | solution.py:346
  43.8 8.5 %collective-permute-start.7 = (f32[32,1536]{1,0:T(8,128)S(1)}, f32[32,1536]{1,0:T(8,128)S(1)}, u32[]{:S(2)}, u32[]{:S(2)}) collective-permute-start(f32[32,1536]{1,0:T(8,128)S(1)} %collective-permute-done.5.refs_2_), channel_id=1, source_target_pairs={{0,4},{4,8},{8,12},{12,0},{1,5},{5,9},{9,13},{13,1},{2,6},{6,10},{... | collective-permute-start | bytes 589832 | tf_op jit(solution)/shard_map/ppermute | solution.py:340
  59.5 2.0 %collective-permute-start.11 = (f32[32,4096]{1,0:T(8,128)S(1)}, f32[32,4096]{1,0:T(8,128)S(1)}, u32[]{:S(2)}, u32[]{:S(2)}) collective-permute-start(f32[32,4096]{1,0:T(8,128)S(1)} %get-tuple-element.115), channel_id=1, source_target_pairs={{0,1},{1,0},{2,3},{3,2},{4,5},{5,4},{6,7},{7,6},{8,9},{9,8},{10,11... | collective-permute-start | bytes 1572872 | tf_op jit(solution)/shard_map/ppermute | solution.py:343
  59.6 16.8 %collective-permute-start.16 = (f32[32,4096]{1,0:T(8,128)S(1)}, f32[32,4096]{1,0:T(8,128)S(1)}, u32[]{:S(2)}, u32[]{:S(2)}) collective-permute-start(f32[32,4096]{1,0:T(8,128)S(1)} %get-tuple-element.129), channel_id=1, source_target_pairs={{0,1},{1,0},{2,3},{3,2},{4,5},{5,4},{6,7},{7,6},{8,9},{9,8},{10,11... | collective-permute-start | bytes 1572872 | tf_op jit(solution)/shard_map/ppermute | solution.py:343
  61.6 14.8 %collective-permute-start.15 = (f32[32,4096]{1,0:T(8,128)S(1)}, f32[32,4096]{1,0:T(8,128)S(1)}, u32[]{:S(2)}, u32[]{:S(2)}) collective-permute-start(f32[32,4096]{1,0:T(8,128)S(1)} %add.60.refs_6_), channel_id=1, source_target_pairs={{0,2},{1,3},{2,0},{3,1},{4,6},{5,7},{6,4},{7,5},{8,10},{9,11},{10,... | collective-permute-start | bytes 1572872 | tf_op jit(solution)/shard_map/ppermute | solution.py:346
  69.0 5.8 %collective-permute-start.12 = (f32[32,2048]{1,0:T(8,128)S(1)}, f32[32,2048]{1,0:T(8,128)S(1)}, u32[]{:S(2)}, u32[]{:S(2)}) collective-permute-start(f32[32,2048]{1,0:T(8,128)S(1)} %get-tuple-element.117), channel_id=1, source_target_pairs={{0,1},{1,0},{2,3},{3,2},{4,5},{5,4},{6,7},{7,6},{8,9},{9,8},{10,11... | collective-permute-start | bytes 786440 | tf_op jit(solution)/shard_map/ppermute | solution.py:343
  74.9 8.8 %collective-permute-start.13 = (f32[32,2048]{1,0:T(8,128)S(1)}, f32[32,2048]{1,0:T(8,128)S(1)}, u32[]{:S(2)}, u32[]{:S(2)}) collective-permute-start(f32[32,2048]{1,0:T(8,128)S(1)} %add.61.refs_10_), channel_id=1, source_target_pairs={{0,2},{1,3},{2,0},{3,1},{4,6},{5,7},{6,4},{7,5},{8,10},{9,11},{10,... | collective-permute-start | bytes 786440 | tf_op jit(solution)/shard_map/ppermute | solution.py:346
  80.9 2.7 %collective-permute-start.17 = (f32[32,2048]{1,0:T(8,128)S(1)}, f32[32,2048]{1,0:T(8,128)S(1)}, u32[]{:S(2)}, u32[]{:S(2)}) collective-permute-start(f32[32,2048]{1,0:T(8,128)S(1)} %get-tuple-element.132), channel_id=1, source_target_pairs={{0,1},{1,0},{2,3},{3,2},{4,5},{5,4},{6,7},{7,6},{8,9},{9,8},{10,11... | collective-permute-start | bytes 786440 | tf_op jit(solution)/shard_map/ppermute | solution.py:343
  81.1 20.5 %collective-permute-start.14 = (f32[32,2048]{1,0:T(8,128)S(1)}, f32[32,2048]{1,0:T(8,128)S(1)}, u32[]{:S(2)}, u32[]{:S(2)}) collective-permute-start(f32[32,2048]{1,0:T(8,128)S(1)} %get-tuple-element.124), channel_id=1, source_target_pairs={{0,1},{1,0},{2,3},{3,2},{4,5},{5,4},{6,7},{7,6},{8,9},{9,8},{10,11... | collective-permute-start | bytes 786440 | tf_op jit(solution)/shard_map/ppermute | solution.py:343
  81.5 21.2 %collective-permute-start.23 = (f32[32,4096]{1,0:T(8,128)S(1)}, f32[32,4096]{1,0:T(8,128)S(1)}, u32[]{:S(2)}, u32[]{:S(2)}) collective-permute-start(f32[32,4096]{1,0:T(8,128)S(1)} %get-tuple-element.130.refs_9_.refs_8_.refs_1_), channel_id=1, source_target_pairs={{0,2},{1,3},{2,0},{3,1},{4,6},{5,7},{6,4},{7,5},{8,10},{9,11},{10,... | collective-permute-start | bytes 1572872 | tf_op jit(solution)/shard_map/ppermute | solution.py:346
  82.0 19.7 %collective-permute-start.19 = (f32[32,2048]{1,0:T(8,128)S(1)}, f32[32,2048]{1,0:T(8,128)S(1)}, u32[]{:S(2)}, u32[]{:S(2)}) collective-permute-start(f32[32,2048]{1,0:T(8,128)S(1)} %get-tuple-element.135), channel_id=1, source_target_pairs={{0,1},{1,0},{2,3},{3,2},{4,5},{5,4},{6,7},{7,6},{8,9},{9,8},{10,11... | collective-permute-start | bytes 786440 | tf_op jit(solution)/shard_map/ppermute | solution.py:343
  83.6 18.1 %collective-permute-start.18 = (f32[32,2048]{1,0:T(8,128)S(1)}, f32[32,2048]{1,0:T(8,128)S(1)}, u32[]{:S(2)}, u32[]{:S(2)}) collective-permute-start(f32[32,2048]{1,0:T(8,128)S(1)} %add.62), channel_id=1, source_target_pairs={{0,2},{1,3},{2,0},{3,1},{4,6},{5,7},{6,4},{7,5},{8,10},{9,11},{10,... | collective-permute-start | bytes 786440 | tf_op jit(solution)/shard_map/ppermute | solution.py:346
  86.8 14.8 %collective-permute-start.21 = (f32[1,6144]{1,0:T(1,128)S(1)}, f32[1,6144]{1,0:T(1,128)S(1)}, u32[]{:S(2)}, u32[]{:S(2)}) collective-permute-start(f32[1,6144]{1,0:T(1,128)S(1)} %add.63), channel_id=1, source_target_pairs={{0,2},{1,3},{2,0},{3,1},{4,6},{5,7},{6,4},{7,5},{8,10},{9,11},{10,... | collective-permute-start | bytes 73736 | tf_op jit(solution)/shard_map/ppermute | solution.py:346
  101.6 2.4 %collective-permute-start.24 = (f32[32,4096]{1,0:T(8,128)S(1)}, f32[32,4096]{1,0:T(8,128)S(1)}, u32[]{:S(2)}, u32[]{:S(2)}) collective-permute-start(f32[32,4096]{1,0:T(8,128)S(1)} %get-tuple-element.130.refs_9_.refs_8_.refs_1_), channel_id=1, source_target_pairs={{0,1},{1,0},{2,3},{3,2},{4,5},{5,4},{6,7},{7,6},{8,9},{9,8},{10,11... | collective-permute-start | bytes 1572872 | tf_op jit(solution)/shard_map/ppermute | solution.py:343
  102.7 2.0 %collective-permute-start.25 = (f32[32,4096]{1,0:T(8,128)S(1)}, f32[32,4096]{1,0:T(8,128)S(1)}, u32[]{:S(2)}, u32[]{:S(2)}) collective-permute-start(f32[32,4096]{1,0:T(8,128)S(1)} %collective-permute-done.23.refs_2_), channel_id=1, source_target_pairs={{0,1},{1,0},{2,3},{3,2},{4,5},{5,4},{6,7},{7,6},{8,9},{9,8},{10,11... | collective-permute-start | bytes 1572872 | tf_op jit(solution)/shard_map/ppermute | solution.py:343
  103.2 11.7 %collective-permute-start.22 = (f32[32,2176]{1,0:T(8,128)S(1)}, f32[32,2176]{1,0:T(8,128)S(1)}, u32[]{:S(2)}, u32[]{:S(2)}) collective-permute-start(f32[32,2176]{1,0:T(8,128)S(1)} %get-tuple-element.141.refs_1_), channel_id=1, source_target_pairs={{0,2},{1,3},{2,0},{3,1},{4,6},{5,7},{6,4},{7,5},{8,10},{9,11},{10,... | collective-permute-start | bytes 835592 | tf_op jit(solution)/shard_map/ppermute | solution.py:346
  104.1 11.3 %collective-permute-start.26 = (f32[32,2176]{1,0:T(8,128)S(1)}, f32[32,2176]{1,0:T(8,128)S(1)}, u32[]{:S(2)}, u32[]{:S(2)}) collective-permute-start(f32[32,2176]{1,0:T(8,128)S(1)} %get-tuple-element.141.refs_1_), channel_id=1, source_target_pairs={{0,1},{1,0},{2,3},{3,2},{4,5},{5,4},{6,7},{7,6},{8,9},{9,8},{10,11... | collective-permute-start | bytes 835592 | tf_op jit(solution)/shard_map/ppermute | solution.py:343
  119.6 8.4 %collective-permute-start.28 = (f32[32,896]{1,0:T(8,128)S(1)}, f32[32,896]{1,0:T(8,128)S(1)}, u32[]{:S(2)}, u32[]{:S(2)}) collective-permute-start(f32[32,896]{1,0:T(8,128)S(1)} %get-tuple-element.157), channel_id=1, source_target_pairs={{0,12},{4,0},{8,4},{12,8},{1,13},{5,1},{9,5},{13,9},{2,14},{6,2},{... | collective-permute-start | bytes 344072 | tf_op jit(solution)/shard_map/ppermute | solution.py:340
  119.9 13.1 %collective-permute-start.29 = (f32[32,896]{1,0:T(8,128)S(1)}, f32[32,896]{1,0:T(8,128)S(1)}, u32[]{:S(2)}, u32[]{:S(2)}) collective-permute-start(f32[32,896]{1,0:T(8,128)S(1)} %get-tuple-element.158), channel_id=1, source_target_pairs={{0,8},{4,12},{8,0},{12,4},{1,9},{5,13},{9,1},{13,5},{2,10},{6,14},... | collective-permute-start | bytes 344072 | tf_op jit(solution)/shard_map/ppermute | solution.py:340
  120.3 12.7 %collective-permute-start.30 = (f32[32,896]{1,0:T(8,128)S(1)}, f32[32,896]{1,0:T(8,128)S(1)}, u32[]{:S(2)}, u32[]{:S(2)}) collective-permute-start(f32[32,896]{1,0:T(8,128)S(1)} %get-tuple-element.159), channel_id=1, source_target_pairs={{0,4},{4,8},{8,12},{12,0},{1,5},{5,9},{9,13},{13,1},{2,6},{6,10},{... | collective-permute-start | bytes 344072 | tf_op jit(solution)/shard_map/ppermute | solution.py:340
  124.9 8.3 %collective-permute-start.31 = (f32[32,768]{1,0:T(8,128)S(1)}, f32[32,768]{1,0:T(8,128)S(1)}, u32[]{:S(2)}, u32[]{:S(2)}) collective-permute-start(f32[32,768]{1,0:T(8,128)S(1)} %get-tuple-element.168), channel_id=1, source_target_pairs={{0,12},{4,0},{8,4},{12,8},{1,13},{5,1},{9,5},{13,9},{2,14},{6,2},{... | collective-permute-start | bytes 294920 | tf_op jit(solution)/shard_map/ppermute | solution.py:340
  127.3 12.3 %collective-permute-start.32 = (f32[32,768]{1,0:T(8,128)S(1)}, f32[32,768]{1,0:T(8,128)S(1)}, u32[]{:S(2)}, u32[]{:S(2)}) collective-permute-start(f32[32,768]{1,0:T(8,128)S(1)} %get-tuple-element.169), channel_id=1, source_target_pairs={{0,8},{4,12},{8,0},{12,4},{1,9},{5,13},{9,1},{13,5},{2,10},{6,14},... | collective-permute-start | bytes 294920 | tf_op jit(solution)/shard_map/ppermute | solution.py:340
  128.0 11.5 %collective-permute-start.33 = (f32[32,768]{1,0:T(8,128)S(1)}, f32[32,768]{1,0:T(8,128)S(1)}, u32[]{:S(2)}, u32[]{:S(2)}) collective-permute-start(f32[32,768]{1,0:T(8,128)S(1)} %get-tuple-element.170), channel_id=1, source_target_pairs={{0,4},{4,8},{8,12},{12,0},{1,5},{5,9},{9,13},{13,1},{2,6},{6,10},{... | collective-permute-start | bytes 294920 | tf_op jit(solution)/shard_map/ppermute | solution.py:340
  (7 other events, 25.1 us)

commit v16 on v15

--- a/solution.py
+++ b/solution.py
@@ -402,14 +402,22 @@
     back_0, (scaled[1], scaled[-1]) = tied(back_0, (scaled[1], scaled[-1]))
     half_0 = halved(back_0)
     back_0 = exchanged(half_0)
-    pre_0 = forward(scaled, in_parts, place, (), [half_0[0]])
-    pre_0, back_0 = tied(pre_0, back_0)
+    parts, sums_2 = prepared(2, [half_0[0]])
+    in_parts += parts
+
+    gain_sums = jnp.concatenate([sums_0, sums_1, sums_2], axis=1)
+    gain_sums = passing = gain_sums + other_core(gain_sums)
+    for _ in range(1, chips):
+        passing = next_chip(passing)
+        gain_sums = gain_sums + passing
+
+    pre_0 = forward(scaled, in_parts[:8], place, (), [parts[0]])
+    pre_0, (back_0, gain_sums) = tied(pre_0, (back_0, gain_sums))
     half_0 = halved(pre_0)
     pre_0 = exchanged(half_0)
     back_1 = stream(grads, out_weight, place, 2 * third, third, [half_0[0]])
-    parts, sums_2 = prepared(2, [back_1[0]])
-    in_parts += parts
-    half_1 = halved(back_1, parts)
+    pre_1 = forward(scaled, in_parts[8:], place, (), [back_1[0]])
+    half_1 = halved(back_1, pre_1)
     back_1 = exchanged(half_1)
 
     def slope_product(span, back, pre, others, after):
@@ -423,14 +431,7 @@
             after,
         )
 
-    act_0, sums_act = slope_product(slice(0, 2 * third), back_0, pre_0, (), (parts[0],))
-    pre_1 = forward(scaled, in_parts[8:], place, (), [act_0, half_1[0]])
-
-    gain_sums, _ = tied(jnp.concatenate([sums_0, sums_1, sums_2], axis=1), pre_1)
-    gain_sums = passing = gain_sums + other_core(gain_sums)
-    for _ in range(1, chips):
-        passing = next_chip(passing)
-        gain_sums = gain_sums + passing
+    act_0, sums_act = slope_product(slice(0, 2 * third), back_0, pre_0, (), (half_1[0],))
     half_1 = halved(pre_1, back_1[0])
     pre_1 = exchanged(half_1)
 

time: 141 us -> 141 us (level)
    ppermute x12, waiting for transfers between devices: 17 us -> 10.5 us  [along_hid(): lax.ppermute(values, 'hid', [(i, (i + steps) % hid_size) for i in range(h...]
    ppermute x8, waiting for transfers between devices: 18.5 us -> 23.7 us  [next_chip(): lax.ppermute(values, 'emb', [(i, (i + 2) % emb_size) for i in range(emb_s...]
where the time goes in v16:
time: 141 us; the launch traced here: 140 us
  Pallas kernels  64.7 us (46%)
  waiting for transfers between devices  40.8 us (29%)
  starting transfers between devices  31.1 us (22%)
  local copies, waits for them, and re-layouts  2.06 us (1%)
    ppermute x8, waiting for transfers between devices, next_chip(): lax.ppermute(values, 'emb', [(i, (i + 2) % emb_size) for i in range(emb_s...  23.7 us
    ppermute x12, starting transfers between devices, along_hid(): lax.ppermute(values, 'hid', [(i, (i + steps) % hid_size) for i in range(h...  19.8 us
    pallas_call x2, Pallas kernels, stream(): pl.pallas_call(lambda *refs: stream_kernel(first, depth, refs[0], refs[1:...  18.3 us
    pallas_call x3, Pallas kernels, prepare(): pl.pallas_call(lambda weight_ref, gain_ref, *refs: prepare_kernel(rows, c...  17.2 us
    pallas_call x4, Pallas kernels, backward(): pl.pallas_call(lambda *refs: backward_kernel(part * depth, depth, refs[0]...  16.3 us
    pallas_call x2, Pallas kernels, forward(): pl.pallas_call(lambda *refs: forward_kernel(refs[0], refs[1:ends[0]], ref...  11.1 us
    ppermute x12, waiting for transfers between devices, along_hid(): lax.ppermute(values, 'hid', [(i, (i + steps) % hid_size) for i in range(h...  10.5 us
    ppermute x8, starting transfers between devices, next_chip(): lax.ppermute(values, 'emb', [(i, (i + 2) % emb_size) for i in range(emb_s...  8.56 us
  transfers between devices with their start and end apart: 34, of which 11 were waited for; matrix products, arithmetic and copies ran while one was open for 1% of the time, Pallas kernels for 44%

profile of v16, /device:TPU:0, one launch (start us, length us, event | category | flops | bytes accessed | tf_op | source)
XLA Modules:
  0.0 140.3 jit_solution(650141485364568142)
XLA Ops:
  0.0 3.0 %collective-permute-start.1 = (f32[32,1536]{1,0:T(8,128)}, f32[32,1536]{1,0:T(8,128)S(1)}, u32[]{:S(2)}, u32[]{:S(2)}) collective-permute-start(f32[32,1536]{1,0:T(8,128)} %refs_1_.3), channel_id=1, source_target_pairs={{0,4},{4,8},{8,12},{12,0},{1,5},{5,9},{9,13},{13,1},{2,6},{6,10},{... | collective-permute-start | bytes 589832 | tf_op jit(solution)/shard_map/ppermute | solution.py:340
  3.0 2.6 %collective-permute-start.2 = (f32[32,1536]{1,0:T(8,128)}, f32[32,1536]{1,0:T(8,128)S(1)}, u32[]{:S(2)}, u32[]{:S(2)}) collective-permute-start(f32[32,1536]{1,0:T(8,128)} %refs_1_.3), channel_id=1, source_target_pairs={{0,8},{4,12},{8,0},{12,4},{1,9},{5,13},{9,1},{13,5},{2,10},{6,14},... | collective-permute-start | bytes 589832 | tf_op jit(solution)/shard_map/ppermute | solution.py:340
  5.6 1.3 collective-permute-start.3
  9.1 5.7 %shard_map.65 = (bf16[1536,1024]{1,0:T(8,128)(2,1)S(1)}, bf16[1536,1024]{1,0:T(8,128)(2,1)S(1)}, bf16[1536,1024]{1,0:T(8,128)(2,1)S(1)}, bf16[1536,1024]{1,0:T(8,128)(2,1)S(1)}, f32[1,2048]{1,0:T(1,128)S(1)}) custom-call(f32[1536,6144]{1,0:T(8,128)} %weight_ref.5, f32[1536,1]{1,0:T(8,128)S(1)} %broadcast_in_dim.19.gain_ref, s32[4]{0:T(128)S(1)} %fusion.5.refs_0_, ...), custom_call_target="tpu_custom_call" | custom-call | flops 1048576 | bytes 262144 | tf_op jit(solution)/shard_map/pallas_call | solution.py:134
  14.8 5.7 %shard_map.66 = (bf16[1536,1024]{1,0:T(8,128)(2,1)S(1)}, bf16[1536,1024]{1,0:T(8,128)(2,1)S(1)}, bf16[1536,1024]{1,0:T(8,128)(2,1)S(1)}, bf16[1536,1024]{1,0:T(8,128)(2,1)S(1)}, f32[1,2048]{1,0:T(1,128)S(1)}) custom-call(f32[1536,6144]{1,0:T(8,128)} %weight_ref.5, f32[1536,1]{1,0:T(8,128)S(1)} %broadcast_in_dim.19.gain_ref, ...), custom_call_target="tpu_custom_call" | custom-call | flops 1048576 | bytes 262144 | tf_op jit(solution)/shard_map/pallas_call | solution.py:134
  20.6 1.6 %collective-permute-start.4 = (f32[64,128]{1,0:T(8,128)S(1)}, f32[64,128]{1,0:T(8,128)S(1)}, u32[]{:S(2)}, u32[]{:S(2)}) collective-permute-start(f32[64,128]{1,0:T(8,128)S(1)} %shard_map.67.refs_2_), channel_id=1, source_target_pairs={{0,2},{1,3},{2,0},{3,1},{4,6},{5,7},{6,4},{7,5},{8,10},{9,11},{10,... | collective-permute-start | bytes 98312 | tf_op jit(solution)/shard_map/ppermute | solution.py:346
  22.2 2.4 %collective-permute-done.4.refs_3_ = f32[64,128]{1,0:T(8,128)S(1)} collective-permute-done((f32[64,128]{1,0:T(8,128)S(1)}, f32[64,128]{1,0:T(8,128)S(1)}, u32[]{:S(2)}, u32[]{:S(2)}) %collective-permute-start.4) | collective-permute-done | bytes 32800 | tf_op jit(solution)/shard_map/ppermute | solution.py:346
  24.8 2.8 %collective-permute-start.5 = (f32[32,1536]{1,0:T(8,128)S(1)}, f32[32,1536]{1,0:T(8,128)S(1)}, u32[]{:S(2)}, u32[]{:S(2)}) collective-permute-start(f32[32,1536]{1,0:T(8,128)S(1)} %get-tuple-element.93.refs_6_.refs_1_), channel_id=1, source_target_pairs={{0,4},{4,8},{8,12},{12,0},{1,5},{5,9},{9,13},{13,1},{2,6},{6,10},{... | collective-permute-start | bytes 589832 | tf_op jit(solution)/shard_map/ppermute | solution.py:340
  28.7 11.5 %shard_map.69 = (f32[32,4096]{1,0:T(8,128)S(1)}, f32[32,4096]{1,0:T(8,128)S(1)}, f32[32,4096]{1,0:T(8,128)S(1)}, f32[32,4096]{1,0:T(8,128)S(1)}) custom-call(s32[4]{0:T(128)S(1)} %fusion.5.refs_0_, f32[32,1536]{1,0:T(8,128)S(1)} %copy-done.4, f32[32,1536]{1,0:T(8,128)S(1)} %collective-permute-done.1.refs_3_.refs_2_, ...), custom_call_target="tpu_custom_call" | custom-call | flops 1048576 | bytes 262144 | tf_op jit(solution)/shard_map/pallas_call | solution.py:253
  40.8 1.4 collective-permute-done.8
  42.3 1.6 %collective-permute-start.9 = (f32[32,4096]{1,0:T(8,128)S(1)}, f32[32,4096]{1,0:T(8,128)S(1)}, u32[]{:S(2)}, u32[]{:S(2)}) collective-permute-start(f32[32,4096]{1,0:T(8,128)S(1)} %add.59.refs_0_), channel_id=1, source_target_pairs={{0,2},{1,3},{2,0},{3,1},{4,6},{5,7},{6,4},{7,5},{8,10},{9,11},{10,... | collective-permute-start | bytes 1572872 | tf_op jit(solution)/shard_map/ppermute | solution.py:346
  44.7 5.7 %shard_map.70 = (bf16[1536,1024]{1,0:T(8,128)(2,1)S(1)}, bf16[1536,1024]{1,0:T(8,128)(2,1)S(1)}, bf16[1536,1024]{1,0:T(8,128)(2,1)S(1)}, bf16[1536,1024]{1,0:T(8,128)(2,1)S(1)}, f32[1,2048]{1,0:T(1,128)S(1)}) custom-call(f32[1536,6144]{1,0:T(8,128)} %weight_ref.5, f32[1536,1]{1,0:T(8,128)S(1)} %broadcast_in_dim.19.gain_ref, f32[32,4096]{1,0:T(8,128)S(1)} %add.59.refs_0_), custom_call_target="tpu_custom_call" | custom-call | flops 1048576 | bytes 262144 | tf_op jit(solution)/shard_map/pallas_call | solution.py:134
  50.6 1.2 collective-permute-done.11
  52.4 7.2 %shard_map.71 = (f32[32,4096]{1,0:T(8,128)S(1)}, f32[32,4096]{1,0:T(8,128)S(1)}, f32[32,4096]{1,0:T(8,128)S(1)}, f32[32,4096]{1,0:T(8,128)S(1)}) custom-call(s32[4]{0:T(128)S(1)} %fusion.5.refs_0_, f32[32,1536]{1,0:T(8,128)S(1)} %get-tuple-element.93.refs_6_.refs_1_, f32[32,1536]{1,0:T(8,128)S(1)} %collective-permute-done.5.refs_2_, ...), custom_call_target="tpu_custom_call" | custom-call | flops 1048576 | bytes 262144 | tf_op jit(solution)/shard_map/pallas_call | solution.py:211
  60.3 1.4 collective-permute-done.13
  61.7 1.5 %collective-permute-start.20 = (f32[32,4096]{1,0:T(8,128)S(1)}, f32[32,4096]{1,0:T(8,128)S(1)}, u32[]{:S(2)}, u32[]{:S(2)}) collective-permute-start(f32[32,4096]{1,0:T(8,128)S(1)} %add.62.refs_6_), channel_id=1, source_target_pairs={{0,2},{1,3},{2,0},{3,1},{4,6},{5,7},{6,4},{7,5},{8,10},{9,11},{10,... | collective-permute-start | bytes 1572872 | tf_op jit(solution)/shard_map/ppermute | solution.py:346
  63.3 6.8 %shard_map.72 = (f32[32,2048]{1,0:T(8,128)S(1)}, f32[32,2048]{1,0:T(8,128)S(1)}, f32[32,2048]{1,0:T(8,128)S(1)}, f32[32,2048]{1,0:T(8,128)S(1)}) custom-call(s32[4]{0:T(128)S(1)} %fusion.5.refs_0_, f32[32,1536]{1,0:T(8,128)S(1)} %copy-done.4, f32[32,1536]{1,0:T(8,128)S(1)} %collective-permute-done.1.refs_3_.refs_2_, ...), custom_call_target="tpu_custom_call" | custom-call | flops 1048576 | bytes 262144 | tf_op jit(solution)/shard_map/pallas_call | solution.py:253
  70.1 3.9 %shard_map.73 = (f32[32,2048]{1,0:T(8,128)S(1)}, f32[32,2048]{1,0:T(8,128)S(1)}, f32[32,2048]{1,0:T(8,128)S(1)}, f32[32,2048]{1,0:T(8,128)S(1)}) custom-call(s32[4]{0:T(128)S(1)} %fusion.5.refs_0_, f32[32,1536]{1,0:T(8,128)S(1)} %get-tuple-element.93.refs_6_.refs_1_, f32[32,1536]{1,0:T(8,128)S(1)} %collective-permute-done.5.refs_2_, ...), custom_call_target="tpu_custom_call" | custom-call | flops 1048576 | bytes 262144 | tf_op jit(solution)/shard_map/pallas_call | solution.py:211
  76.3 1.5 %collective-permute-start.23 = (f32[32,4096]{1,0:T(8,128)S(1)}, f32[32,4096]{1,0:T(8,128)S(1)}, u32[]{:S(2)}, u32[]{:S(2)}) collective-permute-start(f32[32,4096]{1,0:T(8,128)S(1)} %get-tuple-element.139.refs_8_.refs_1_), channel_id=1, source_target_pairs={{0,2},{1,3},{2,0},{3,1},{4,6},{5,7},{6,4},{7,5},{8,10},{9,11},{10,... | collective-permute-start | bytes 1572872 | tf_op jit(solution)/shard_map/ppermute | solution.py:346
  78.3 5.6 %collective-permute-done.15.refs_0_ = f32[32,2048]{1,0:T(8,128)S(1)} collective-permute-done((f32[32,2048]{1,0:T(8,128)S(1)}, f32[32,2048]{1,0:T(8,128)S(1)}, u32[]{:S(2)}, u32[]{:S(2)}) %collective-permute-start.15) | collective-permute-done | bytes 262176 | tf_op jit(solution)/shard_map/ppermute | solution.py:346
  84.6 15.2 %collective-permute-done.18.refs_3_ = f32[32,2048]{1,0:T(8,128)S(1)} collective-permute-done((f32[32,2048]{1,0:T(8,128)S(1)}, f32[32,2048]{1,0:T(8,128)S(1)}, u32[]{:S(2)}, u32[]{:S(2)}) %collective-permute-start.18) | collective-permute-done | bytes 262176 | tf_op jit(solution)/shard_map/ppermute | solution.py:346
  101.6 1.1 collective-permute-done.25.refs_4_
  102.7 5.1 %shard_map.77 = (f32[32,768]{1,0:T(8,128)S(1)}, f32[32,768]{1,0:T(8,128)S(1)}, f32[32,768]{1,0:T(8,128)S(1)}, f32[32,768]{1,0:T(8,128)S(1)}) custom-call(s32[4]{0:T(128)S(1)} %fusion.5.refs_0_, f32[32,4096]{1,0:T(8,128)S(1)} %get-tuple-element.139.refs_8_.refs_1_, f32[32,4096]{1,0:T(8,128)S(1)} %collective-permute-done.23.refs_2_, ...), custom_call_target="tpu_custom_call" | custom-call | flops 1048576 | bytes 262144 | tf_op jit(solution)/shard_map/pallas_call | solution.py:307
  107.8 5.1 %shard_map.76 = (f32[32,768]{1,0:T(8,128)S(1)}, f32[32,768]{1,0:T(8,128)S(1)}, f32[32,768]{1,0:T(8,128)S(1)}, f32[32,768]{1,0:T(8,128)S(1)}) custom-call(s32[4]{0:T(128)S(1)} %fusion.5.refs_0_, f32[32,4096]{1,0:T(8,128)S(1)} %get-tuple-element.139.refs_8_.refs_1_, f32[32,4096]{1,0:T(8,128)S(1)} %collective-permute-done.23.refs_2_, ...), custom_call_target="tpu_custom_call" | custom-call | flops 1048576 | bytes 262144 | tf_op jit(solution)/shard_map/pallas_call | solution.py:307
  113.1 1.4 %collective-permute-done.27.refs_4_ = f32[32,2176]{1,0:T(8,128)S(1)} collective-permute-done((f32[32,2176]{1,0:T(8,128)S(1)}, f32[32,2176]{1,0:T(8,128)S(1)}, u32[]{:S(2)}, u32[]{:S(2)}) %collective-permute-start.27) | collective-permute-done | bytes 278560 | tf_op jit(solution)/shard_map/ppermute | solution.py:343
  114.5 3.1 %shard_map.78 = (f32[32,896]{1,0:T(8,128)S(1)}, f32[32,896]{1,0:T(8,128)S(1)}, f32[32,896]{1,0:T(8,128)S(1)}, f32[32,896]{1,0:T(8,128)S(1)}) custom-call(s32[4]{0:T(128)S(1)} %fusion.5.refs_0_, f32[32,2176]{1,0:T(8,128)S(1)} %get-tuple-element.141.refs_1_, f32[32,2176]{1,0:T(8,128)S(1)} %collective-permute-done.22.refs_2_, ...), custom_call_target="tpu_custom_call" | custom-call | flops 1048576 | bytes 262144 | tf_op jit(solution)/shard_map/pallas_call | solution.py:307
  117.6 3.0 %collective-permute-start.28 = (f32[32,896]{1,0:T(8,128)S(1)}, f32[32,896]{1,0:T(8,128)S(1)}, u32[]{:S(2)}, u32[]{:S(2)}) collective-permute-start(f32[32,896]{1,0:T(8,128)S(1)} %get-tuple-element.157), channel_id=1, source_target_pairs={{0,12},{4,0},{8,4},{12,8},{1,13},{5,1},{9,5},{13,9},{2,14},{6,2},{... | collective-permute-start | bytes 344072 | tf_op jit(solution)/shard_map/ppermute | solution.py:340
  121.4 3.0 %shard_map.79 = (f32[32,768]{1,0:T(8,128)S(1)}, f32[32,768]{1,0:T(8,128)S(1)}, f32[32,768]{1,0:T(8,128)S(1)}, f32[32,768]{1,0:T(8,128)S(1)}) custom-call(s32[4]{0:T(128)S(1)} %fusion.5.refs_0_, f32[32,2176]{1,0:T(8,128)S(1)} %get-tuple-element.141.refs_1_, f32[32,2176]{1,0:T(8,128)S(1)} %collective-permute-done.22.refs_2_, ...), custom_call_target="tpu_custom_call" | custom-call | flops 1048576 | bytes 262144 | tf_op jit(solution)/shard_map/pallas_call | solution.py:307
  124.5 3.2 %collective-permute-start.31 = (f32[32,768]{1,0:T(8,128)S(1)}, f32[32,768]{1,0:T(8,128)S(1)}, u32[]{:S(2)}, u32[]{:S(2)}) collective-permute-start(f32[32,768]{1,0:T(8,128)S(1)} %get-tuple-element.168), channel_id=1, source_target_pairs={{0,12},{4,0},{8,4},{12,8},{1,13},{5,1},{9,5},{13,9},{2,14},{6,2},{... | collective-permute-start | bytes 294920 | tf_op jit(solution)/shard_map/ppermute | solution.py:340
  127.6 1.1 collective-permute-start.32
  128.8 7.0 %collective-permute-done.29 = f32[32,896]{1,0:T(8,128)S(1)} collective-permute-done((f32[32,896]{1,0:T(8,128)S(1)}, f32[32,896]{1,0:T(8,128)S(1)}, u32[]{:S(2)}, u32[]{:S(2)}) %collective-permute-start.29) | collective-permute-done | bytes 114720 | tf_op jit(solution)/shard_map/ppermute | solution.py:340
  136.0 3.5 %collective-permute-done.32 = f32[32,768]{1,0:T(8,128)S(1)} collective-permute-done((f32[32,768]{1,0:T(8,128)S(1)}, f32[32,768]{1,0:T(8,128)S(1)}, u32[]{:S(2)}, u32[]{:S(2)}) %collective-permute-start.32) | collective-permute-done | bytes 98336 | tf_op jit(solution)/shard_map/ppermute | solution.py:340
  (88 shorter events, 13.6 us)
Async XLA Ops:
  0.0 20.6 %collective-permute-start.1 = (f32[32,1536]{1,0:T(8,128)}, f32[32,1536]{1,0:T(8,128)S(1)}, u32[]{:S(2)}, u32[]{:S(2)}) collective-permute-start(f32[32,1536]{1,0:T(8,128)} %refs_1_.3), channel_id=1, source_target_pairs={{0,4},{4,8},{8,12},{12,0},{1,5},{5,9},{9,13},{13,1},{2,6},{6,10},{... | collective-permute-start | bytes 589832 | tf_op jit(solution)/shard_map/ppermute | solution.py:340
  3.0 17.6 %collective-permute-start.2 = (f32[32,1536]{1,0:T(8,128)}, f32[32,1536]{1,0:T(8,128)S(1)}, u32[]{:S(2)}, u32[]{:S(2)}) collective-permute-start(f32[32,1536]{1,0:T(8,128)} %refs_1_.3), channel_id=1, source_target_pairs={{0,8},{4,12},{8,0},{12,4},{1,9},{5,13},{9,1},{13,5},{2,10},{6,14},... | collective-permute-start | bytes 589832 | tf_op jit(solution)/shard_map/ppermute | solution.py:340
  5.6 15.0 %collective-permute-start.3 = (f32[32,1536]{1,0:T(8,128)}, f32[32,1536]{1,0:T(8,128)S(1)}, u32[]{:S(2)}, u32[]{:S(2)}) collective-permute-start(f32[32,1536]{1,0:T(8,128)} %refs_1_.3), channel_id=1, source_target_pairs={{0,12},{4,0},{8,4},{12,8},{1,13},{5,1},{9,5},{13,9},{2,14},{6,2},{... | collective-permute-start | bytes 589832 | tf_op jit(solution)/shard_map/ppermute | solution.py:340
  8.1 12.5 %collective-permute-start = (f32[64,128]{1,0:T(8,128)S(1)}, f32[64,128]{1,0:T(8,128)S(1)}, u32[]{:S(2)}, u32[]{:S(2)}) collective-permute-start(f32[64,128]{1,0:T(8,128)S(1)} %shard_map.64.refs_1_.refs_0_), channel_id=1, source_target_pairs={{0,1},{1,0},{2,3},{3,2},{4,5},{5,4},{6,7},{7,6},{8,9},{9,8},{10,11... | collective-permute-start | bytes 98312 | tf_op jit(solution)/shard_map/ppermute | solution.py:343
  20.6 4.0 %collective-permute-start.4 = (f32[64,128]{1,0:T(8,128)S(1)}, f32[64,128]{1,0:T(8,128)S(1)}, u32[]{:S(2)}, u32[]{:S(2)}) collective-permute-start(f32[64,128]{1,0:T(8,128)S(1)} %shard_map.67.refs_2_), channel_id=1, source_target_pairs={{0,2},{1,3},{2,0},{3,1},{4,6},{5,7},{6,4},{7,5},{8,10},{9,11},{10,... | collective-permute-start | bytes 98312 | tf_op jit(solution)/shard_map/ppermute | solution.py:346
  24.8 15.5 %collective-permute-start.5 = (f32[32,1536]{1,0:T(8,128)S(1)}, f32[32,1536]{1,0:T(8,128)S(1)}, u32[]{:S(2)}, u32[]{:S(2)}) collective-permute-start(f32[32,1536]{1,0:T(8,128)S(1)} %get-tuple-element.93.refs_6_.refs_1_), channel_id=1, source_target_pairs={{0,4},{4,8},{8,12},{12,0},{1,5},{5,9},{9,13},{13,1},{2,6},{6,10},{... | collective-permute-start | bytes 589832 | tf_op jit(solution)/shard_map/ppermute | solution.py:340
  27.6 12.7 %collective-permute-start.6 = (f32[32,1536]{1,0:T(8,128)S(1)}, f32[32,1536]{1,0:T(8,128)S(1)}, u32[]{:S(2)}, u32[]{:S(2)}) collective-permute-start(f32[32,1536]{1,0:T(8,128)S(1)} %get-tuple-element.93.refs_6_.refs_1_), channel_id=1, source_target_pairs={{0,12},{4,0},{8,4},{12,8},{1,13},{5,1},{9,5},{13,9},{2,14},{6,2},{... | collective-permute-start | bytes 589832 | tf_op jit(solution)/shard_map/ppermute | solution.py:340
  40.2 2.0 %collective-permute-start.8 = (f32[32,4096]{1,0:T(8,128)S(1)}, f32[32,4096]{1,0:T(8,128)S(1)}, u32[]{:S(2)}, u32[]{:S(2)}) collective-permute-start(f32[32,4096]{1,0:T(8,128)S(1)} %get-tuple-element.107), channel_id=1, source_target_pairs={{0,1},{1,0},{2,3},{3,2},{4,5},{5,4},{6,7},{7,6},{8,9},{9,8},{10,11... | collective-permute-start | bytes 1572872 | tf_op jit(solution)/shard_map/ppermute | solution.py:343
  40.3 19.4 %collective-permute-start.10 = (f32[32,4096]{1,0:T(8,128)S(1)}, f32[32,4096]{1,0:T(8,128)S(1)}, u32[]{:S(2)}, u32[]{:S(2)}) collective-permute-start(f32[32,4096]{1,0:T(8,128)S(1)} %get-tuple-element.114), channel_id=1, source_target_pairs={{0,1},{1,0},{2,3},{3,2},{4,5},{5,4},{6,7},{7,6},{8,9},{9,8},{10,11... | collective-permute-start | bytes 1572872 | tf_op jit(solution)/shard_map/ppermute | solution.py:343
  42.3 17.4 %collective-permute-start.9 = (f32[32,4096]{1,0:T(8,128)S(1)}, f32[32,4096]{1,0:T(8,128)S(1)}, u32[]{:S(2)}, u32[]{:S(2)}) collective-permute-start(f32[32,4096]{1,0:T(8,128)S(1)} %add.59.refs_0_), channel_id=1, source_target_pairs={{0,2},{1,3},{2,0},{3,1},{4,6},{5,7},{6,4},{7,5},{8,10},{9,11},{10,... | collective-permute-start | bytes 1572872 | tf_op jit(solution)/shard_map/ppermute | solution.py:346
  43.8 8.6 %collective-permute-start.7 = (f32[32,1536]{1,0:T(8,128)S(1)}, f32[32,1536]{1,0:T(8,128)S(1)}, u32[]{:S(2)}, u32[]{:S(2)}) collective-permute-start(f32[32,1536]{1,0:T(8,128)S(1)} %collective-permute-done.5.refs_2_), channel_id=1, source_target_pairs={{0,4},{4,8},{8,12},{12,0},{1,5},{5,9},{9,13},{13,1},{2,6},{6,10},{... | collective-permute-start | bytes 589832 | tf_op jit(solution)/shard_map/ppermute | solution.py:340
  51.8 7.8 %collective-permute-start.12 = (f32[1,6144]{1,0:T(1,128)S(1)}, f32[1,6144]{1,0:T(1,128)S(1)}, u32[]{:S(2)}, u32[]{:S(2)}) collective-permute-start(f32[1,6144]{1,0:T(1,128)S(1)} %add.60), channel_id=1, source_target_pairs={{0,2},{1,3},{2,0},{3,1},{4,6},{5,7},{6,4},{7,5},{8,10},{9,11},{10,... | collective-permute-start | bytes 73736 | tf_op jit(solution)/shard_map/ppermute | solution.py:346
  59.7 2.0 %collective-permute-start.13 = (f32[32,4096]{1,0:T(8,128)S(1)}, f32[32,4096]{1,0:T(8,128)S(1)}, u32[]{:S(2)}, u32[]{:S(2)}) collective-permute-start(f32[32,4096]{1,0:T(8,128)S(1)} %get-tuple-element.119), channel_id=1, source_target_pairs={{0,1},{1,0},{2,3},{3,2},{4,5},{5,4},{6,7},{7,6},{8,9},{9,8},{10,11... | collective-permute-start | bytes 1572872 | tf_op jit(solution)/shard_map/ppermute | solution.py:343
  59.8 15.5 %collective-permute-start.21 = (f32[32,4096]{1,0:T(8,128)S(1)}, f32[32,4096]{1,0:T(8,128)S(1)}, u32[]{:S(2)}, u32[]{:S(2)}) collective-permute-start(f32[32,4096]{1,0:T(8,128)S(1)} %get-tuple-element.138), channel_id=1, source_target_pairs={{0,1},{1,0},{2,3},{3,2},{4,5},{5,4},{6,7},{7,6},{8,9},{9,8},{10,11... | collective-permute-start | bytes 1572872 | tf_op jit(solution)/shard_map/ppermute | solution.py:343
  61.7 14.0 %collective-permute-start.20 = (f32[32,4096]{1,0:T(8,128)S(1)}, f32[32,4096]{1,0:T(8,128)S(1)}, u32[]{:S(2)}, u32[]{:S(2)}) collective-permute-start(f32[32,4096]{1,0:T(8,128)S(1)} %add.62.refs_6_), channel_id=1, source_target_pairs={{0,2},{1,3},{2,0},{3,1},{4,6},{5,7},{6,4},{7,5},{8,10},{9,11},{10,... | collective-permute-start | bytes 1572872 | tf_op jit(solution)/shard_map/ppermute | solution.py:346
  70.0 4.6 %collective-permute-start.14 = (f32[32,2048]{1,0:T(8,128)S(1)}, f32[32,2048]{1,0:T(8,128)S(1)}, u32[]{:S(2)}, u32[]{:S(2)}) collective-permute-start(f32[32,2048]{1,0:T(8,128)S(1)} %get-tuple-element.121), channel_id=1, source_target_pairs={{0,1},{1,0},{2,3},{3,2},{4,5},{5,4},{6,7},{7,6},{8,9},{9,8},{10,11... | collective-permute-start | bytes 786440 | tf_op jit(solution)/shard_map/ppermute | solution.py:343
  74.1 4.2 %collective-permute-start.17 = (f32[32,2048]{1,0:T(8,128)S(1)}, f32[32,2048]{1,0:T(8,128)S(1)}, u32[]{:S(2)}, u32[]{:S(2)}) collective-permute-start(f32[32,2048]{1,0:T(8,128)S(1)} %get-tuple-element.129), channel_id=1, source_target_pairs={{0,1},{1,0},{2,3},{3,2},{4,5},{5,4},{6,7},{7,6},{8,9},{9,8},{10,11... | collective-permute-start | bytes 786440 | tf_op jit(solution)/shard_map/ppermute | solution.py:343
  74.7 9.2 %collective-permute-start.15 = (f32[32,2048]{1,0:T(8,128)S(1)}, f32[32,2048]{1,0:T(8,128)S(1)}, u32[]{:S(2)}, u32[]{:S(2)}) collective-permute-start(f32[32,2048]{1,0:T(8,128)S(1)} %add.63.refs_7_), channel_id=1, source_target_pairs={{0,2},{1,3},{2,0},{3,1},{4,6},{5,7},{6,4},{7,5},{8,10},{9,11},{10,... | collective-permute-start | bytes 786440 | tf_op jit(solution)/shard_map/ppermute | solution.py:346
  76.3 24.5 %collective-permute-start.23 = (f32[32,4096]{1,0:T(8,128)S(1)}, f32[32,4096]{1,0:T(8,128)S(1)}, u32[]{:S(2)}, u32[]{:S(2)}) collective-permute-start(f32[32,4096]{1,0:T(8,128)S(1)} %get-tuple-element.139.refs_8_.refs_1_), channel_id=1, source_target_pairs={{0,2},{1,3},{2,0},{3,1},{4,6},{5,7},{6,4},{7,5},{8,10},{9,11},{10,... | collective-permute-start | bytes 1572872 | tf_op jit(solution)/shard_map/ppermute | solution.py:346
  77.8 6.8 %collective-permute-start.19 = (f32[32,2048]{1,0:T(8,128)S(1)}, f32[32,2048]{1,0:T(8,128)S(1)}, u32[]{:S(2)}, u32[]{:S(2)}) collective-permute-start(f32[32,2048]{1,0:T(8,128)S(1)} %get-tuple-element.128), channel_id=1, source_target_pairs={{0,1},{1,0},{2,3},{3,2},{4,5},{5,4},{6,7},{7,6},{8,9},{9,8},{10,11... | collective-permute-start | bytes 786440 | tf_op jit(solution)/shard_map/ppermute | solution.py:343
  77.8 6.8 %collective-permute-start.16 = (f32[32,2048]{1,0:T(8,128)S(1)}, f32[32,2048]{1,0:T(8,128)S(1)}, u32[]{:S(2)}, u32[]{:S(2)}) collective-permute-start(f32[32,2048]{1,0:T(8,128)S(1)} %get-tuple-element.131), channel_id=1, source_target_pairs={{0,1},{1,0},{2,3},{3,2},{4,5},{5,4},{6,7},{7,6},{8,9},{9,8},{10,11... | collective-permute-start | bytes 786440 | tf_op jit(solution)/shard_map/ppermute | solution.py:343
  84.0 15.9 %collective-permute-start.18 = (f32[32,2048]{1,0:T(8,128)S(1)}, f32[32,2048]{1,0:T(8,128)S(1)}, u32[]{:S(2)}, u32[]{:S(2)}) collective-permute-start(f32[32,2048]{1,0:T(8,128)S(1)} %add.64), channel_id=1, source_target_pairs={{0,2},{1,3},{2,0},{3,1},{4,6},{5,7},{6,4},{7,5},{8,10},{9,11},{10,... | collective-permute-start | bytes 786440 | tf_op jit(solution)/shard_map/ppermute | solution.py:346
  84.6 17.0 %collective-permute-start.24 = (f32[32,4096]{1,0:T(8,128)S(1)}, f32[32,4096]{1,0:T(8,128)S(1)}, u32[]{:S(2)}, u32[]{:S(2)}) collective-permute-start(f32[32,4096]{1,0:T(8,128)S(1)} %get-tuple-element.139.refs_8_.refs_1_), channel_id=1, source_target_pairs={{0,1},{1,0},{2,3},{3,2},{4,5},{5,4},{6,7},{7,6},{8,9},{9,8},{10,11... | collective-permute-start | bytes 1572872 | tf_op jit(solution)/shard_map/ppermute | solution.py:343
  100.8 1.9 %collective-permute-start.25 = (f32[32,4096]{1,0:T(8,128)S(1)}, f32[32,4096]{1,0:T(8,128)S(1)}, u32[]{:S(2)}, u32[]{:S(2)}) collective-permute-start(f32[32,4096]{1,0:T(8,128)S(1)} %collective-permute-done.23.refs_2_), channel_id=1, source_target_pairs={{0,1},{1,0},{2,3},{3,2},{4,5},{5,4},{6,7},{7,6},{8,9},{9,8},{10,11... | collective-permute-start | bytes 1572872 | tf_op jit(solution)/shard_map/ppermute | solution.py:343
  100.8 12.1 %collective-permute-start.22 = (f32[32,2176]{1,0:T(8,128)S(1)}, f32[32,2176]{1,0:T(8,128)S(1)}, u32[]{:S(2)}, u32[]{:S(2)}) collective-permute-start(f32[32,2176]{1,0:T(8,128)S(1)} %get-tuple-element.141.refs_1_), channel_id=1, source_target_pairs={{0,2},{1,3},{2,0},{3,1},{4,6},{5,7},{6,4},{7,5},{8,10},{9,11},{10,... | collective-permute-start | bytes 835592 | tf_op jit(solution)/shard_map/ppermute | solution.py:346
  101.4 11.7 %collective-permute-start.26 = (f32[32,2176]{1,0:T(8,128)S(1)}, f32[32,2176]{1,0:T(8,128)S(1)}, u32[]{:S(2)}, u32[]{:S(2)}) collective-permute-start(f32[32,2176]{1,0:T(8,128)S(1)} %get-tuple-element.141.refs_1_), channel_id=1, source_target_pairs={{0,1},{1,0},{2,3},{3,2},{4,5},{5,4},{6,7},{7,6},{8,9},{9,8},{10,11... | collective-permute-start | bytes 835592 | tf_op jit(solution)/shard_map/ppermute | solution.py:343
  117.6 11.1 %collective-permute-start.28 = (f32[32,896]{1,0:T(8,128)S(1)}, f32[32,896]{1,0:T(8,128)S(1)}, u32[]{:S(2)}, u32[]{:S(2)}) collective-permute-start(f32[32,896]{1,0:T(8,128)S(1)} %get-tuple-element.157), channel_id=1, source_target_pairs={{0,12},{4,0},{8,4},{12,8},{1,13},{5,1},{9,5},{13,9},{2,14},{6,2},{... | collective-permute-start | bytes 344072 | tf_op jit(solution)/shard_map/ppermute | solution.py:340
  120.6 15.2 %collective-permute-start.29 = (f32[32,896]{1,0:T(8,128)S(1)}, f32[32,896]{1,0:T(8,128)S(1)}, u32[]{:S(2)}, u32[]{:S(2)}) collective-permute-start(f32[32,896]{1,0:T(8,128)S(1)} %get-tuple-element.158), channel_id=1, source_target_pairs={{0,8},{4,12},{8,0},{12,4},{1,9},{5,13},{9,1},{13,5},{2,10},{6,14},... | collective-permute-start | bytes 344072 | tf_op jit(solution)/shard_map/ppermute | solution.py:340
  120.6 15.2 %collective-permute-start.30 = (f32[32,896]{1,0:T(8,128)S(1)}, f32[32,896]{1,0:T(8,128)S(1)}, u32[]{:S(2)}, u32[]{:S(2)}) collective-permute-start(f32[32,896]{1,0:T(8,128)S(1)} %get-tuple-element.159), channel_id=1, source_target_pairs={{0,4},{4,8},{8,12},{12,0},{1,5},{5,9},{9,13},{13,1},{2,6},{6,10},{... | collective-permute-start | bytes 344072 | tf_op jit(solution)/shard_map/ppermute | solution.py:340
  124.5 11.6 %collective-permute-start.31 = (f32[32,768]{1,0:T(8,128)S(1)}, f32[32,768]{1,0:T(8,128)S(1)}, u32[]{:S(2)}, u32[]{:S(2)}) collective-permute-start(f32[32,768]{1,0:T(8,128)S(1)} %get-tuple-element.168), channel_id=1, source_target_pairs={{0,12},{4,0},{8,4},{12,8},{1,13},{5,1},{9,5},{13,9},{2,14},{6,2},{... | collective-permute-start | bytes 294920 | tf_op jit(solution)/shard_map/ppermute | solution.py:340
  127.6 11.9 %collective-permute-start.32 = (f32[32,768]{1,0:T(8,128)S(1)}, f32[32,768]{1,0:T(8,128)S(1)}, u32[]{:S(2)}, u32[]{:S(2)}) collective-permute-start(f32[32,768]{1,0:T(8,128)S(1)} %get-tuple-element.169), channel_id=1, source_target_pairs={{0,8},{4,12},{8,0},{12,4},{1,9},{5,13},{9,1},{13,5},{2,10},{6,14},... | collective-permute-start | bytes 294920 | tf_op jit(solution)/shard_map/ppermute | solution.py:340
  128.8 10.8 %collective-permute-start.33 = (f32[32,768]{1,0:T(8,128)S(1)}, f32[32,768]{1,0:T(8,128)S(1)}, u32[]{:S(2)}, u32[]{:S(2)}) collective-permute-start(f32[32,768]{1,0:T(8,128)S(1)} %get-tuple-element.170), channel_id=1, source_target_pairs={{0,4},{4,8},{8,12},{12,0},{1,5},{5,9},{9,13},{13,1},{2,6},{6,10},{... | collective-permute-start | bytes 294920 | tf_op jit(solution)/shard_map/ppermute | solution.py:340
  (9 other events, 52.4 us)

commit v17 on v16

--- a/solution.py
+++ b/solution.py
@@ -293,7 +293,7 @@
         for b, out_ref in enumerate(out_refs):
             rows = result[pl.ds(pl.multiple_of(place_ref[b] * block, block), block), :]
             local = pl.ds(pl.multiple_of(step * width, width), width)
-            out_ref[:, local] = rows + earlier_refs[b][:, local] if earlier_refs else rows
+            out_ref[:, local] = rows + earlier_refs[b][:, at] if earlier_refs else rows
 
 
 def backward(acts, weights, place, earlier, part, parts, after):
@@ -402,23 +402,24 @@
     back_0, (scaled[1], scaled[-1]) = tied(back_0, (scaled[1], scaled[-1]))
     half_0 = halved(back_0)
     back_0 = exchanged(half_0)
+    back_1 = stream(grads, out_weight, place, 2 * third, third, [half_0[0]])
+    back_1, scaled = tied(back_1, scaled)
+    half_1 = halved(back_1, back_0[0])
+    back_1 = exchanged(half_1)
+    pre_0 = forward(scaled, in_parts, place, (), [half_1[0]])
+    pre_0, back_1 = tied(pre_0, back_1)
+    half_0 = halved(pre_0)
+    pre_0 = exchanged(half_0)
     parts, sums_2 = prepared(2, [half_0[0]])
     in_parts += parts
+    pre_1 = forward(scaled, parts, place, (), [])
 
     gain_sums = jnp.concatenate([sums_0, sums_1, sums_2], axis=1)
     gain_sums = passing = gain_sums + other_core(gain_sums)
     for _ in range(1, chips):
         passing = next_chip(passing)
         gain_sums = gain_sums + passing
-
-    pre_0 = forward(scaled, in_parts[:8], place, (), [parts[0]])
-    pre_0, (back_0, gain_sums) = tied(pre_0, (back_0, gain_sums))
-    half_0 = halved(pre_0)
-    pre_0 = exchanged(half_0)
-    back_1 = stream(grads, out_weight, place, 2 * third, third, [half_0[0]])
-    pre_1 = forward(scaled, in_parts[8:], place, (), [back_1[0]])
-    half_1 = halved(back_1, pre_1)
-    back_1 = exchanged(half_1)
+    pre_1, gain_sums = tied(pre_1, gain_sums)
 
     def slope_product(span, back, pre, others, after):
         width = span.stop - span.start
@@ -431,9 +432,8 @@
             after,
         )
 
-    act_0, sums_act = slope_product(slice(0, 2 * third), back_0, pre_0, (), (half_1[0],))
-    half_1 = halved(pre_1, back_1[0])
-    pre_1 = exchanged(half_1)
+    act_0, sums_act = slope_product(slice(0, 2 * third), back_0, pre_0, (), (pre_1[0],))
+    pre_1 = exchanged(halved(pre_1))
 
     def spread_out(act):
         mine = [None] * chips
@@ -461,13 +461,13 @@
     acts_0[1:] = tied(acts_0[1:], act_1)[0]
     acts_0 = both_cores(acts_0)
     parts = 2 if depth % 512 == 0 else 1
-    sums = [backward(acts_0, in_parts[:8], place, (), part, parts, ()) for part in range(parts)]
+    sums = backward(acts_0, in_parts[:8], place, (), 0, 1, ())
     acts_1[1:], sums = tied(acts_1[1:], sums)
     acts_1 = both_cores(acts_1)
     ends = []
     for part in range(parts):
         after = [ends[-1][0]] if ends else []
-        ends.append(backward(acts_1, in_parts[8:], place, sums[part], part, parts, after))
+        ends.append(backward(acts_1, in_parts[8:], place, sums, part, parts, after))
     first = summed_along_hid(ends[0])
     others = [summed_along_hid(end, first) for end in ends[1:]]
     width = depth // parts

time: 141 us -> 142 us (level)
  waiting for transfers between devices: 40.8 us -> 42.7 us
    ppermute x14, waiting for transfers between devices: 6.54 us -> 8.12 us  [other_core(): return lax.ppermute(values, 'emb', [(i, i ^ 1) for i in range(emb_size)])]
    pallas_call x4 -> x3, Pallas kernels: 16.3 us -> 15.3 us  [backward(): pl.pallas_call(lambda *refs: backward_kernel(part * depth, depth, refs[0]...]
  transfers between devices with their start and end apart: 34 -> 34, of which waited for: 11 -> 14; matrix products, arithmetic and copies ran while one was open for 1% -> 1% of each run, Pallas kernels for 44% -> 43%
where the time goes in v17:
time: 142 us; the launch traced here: 141 us
  Pallas kernels  63.7 us (45%)
  waiting for transfers between devices  42.7 us (30%)
  starting transfers between devices  31.2 us (22%)
  local copies, waits for them, and re-layouts  2.05 us (1%)
    ppermute x8, waiting for transfers between devices, next_chip(): lax.ppermute(values, 'emb', [(i, (i + 2) % emb_size) for i in range(emb_s...  23.9 us
    ppermute x12, starting transfers between devices, along_hid(): lax.ppermute(values, 'hid', [(i, (i + steps) % hid_size) for i in range(h...  19.9 us
    pallas_call x2, Pallas kernels, stream(): pl.pallas_call(lambda *refs: stream_kernel(first, depth, refs[0], refs[1:...  18.3 us
    pallas_call x3, Pallas kernels, prepare(): pl.pallas_call(lambda weight_ref, gain_ref, *refs: prepare_kernel(rows, c...  17.2 us
    pallas_call x3, Pallas kernels, backward(): pl.pallas_call(lambda *refs: backward_kernel(part * depth, depth, refs[0]...  15.3 us
    pallas_call x2, Pallas kernels, forward(): pl.pallas_call(lambda *refs: forward_kernel(refs[0], refs[1:ends[0]], ref...  11.1 us
    ppermute x12, waiting for transfers between devices, along_hid(): lax.ppermute(values, 'hid', [(i, (i + steps) % hid_size) for i in range(h...  10.7 us
    ppermute x8, starting transfers between devices, next_chip(): lax.ppermute(values, 'emb', [(i, (i + 2) % emb_size) for i in range(emb_s...  9.33 us
  transfers between devices with their start and end apart: 34, of which 14 were waited for; matrix products, arithmetic and copies ran while one was open for 1% of the time, Pallas kernels for 43%

profile of v17, /device:TPU:0, one launch (start us, length us, event | category | flops | bytes accessed | tf_op | source)
XLA Modules:
  0.0 141.4 jit_solution(1681488554127647671)
XLA Ops:
  0.0 3.0 %collective-permute-start.1 = (f32[32,1536]{1,0:T(8,128)}, f32[32,1536]{1,0:T(8,128)S(1)}, u32[]{:S(2)}, u32[]{:S(2)}) collective-permute-start(f32[32,1536]{1,0:T(8,128)} %refs_1_.3), channel_id=1, source_target_pairs={{0,4},{4,8},{8,12},{12,0},{1,5},{5,9},{9,13},{13,1},{2,6},{6,10},{... | collective-permute-start | bytes 589832 | tf_op jit(solution)/shard_map/ppermute | solution.py:340
  3.0 2.6 %collective-permute-start.2 = (f32[32,1536]{1,0:T(8,128)}, f32[32,1536]{1,0:T(8,128)S(1)}, u32[]{:S(2)}, u32[]{:S(2)}) collective-permute-start(f32[32,1536]{1,0:T(8,128)} %refs_1_.3), channel_id=1, source_target_pairs={{0,8},{4,12},{8,0},{12,4},{1,9},{5,13},{9,1},{13,5},{2,10},{6,14},... | collective-permute-start | bytes 589832 | tf_op jit(solution)/shard_map/ppermute | solution.py:340
  5.6 1.3 collective-permute-start.3
  9.1 5.7 %shard_map.65 = (bf16[1536,1024]{1,0:T(8,128)(2,1)S(1)}, bf16[1536,1024]{1,0:T(8,128)(2,1)S(1)}, bf16[1536,1024]{1,0:T(8,128)(2,1)S(1)}, bf16[1536,1024]{1,0:T(8,128)(2,1)S(1)}, f32[1,2048]{1,0:T(1,128)S(1)}) custom-call(f32[1536,6144]{1,0:T(8,128)} %weight_ref.5, f32[1536,1]{1,0:T(8,128)S(1)} %broadcast_in_dim.19.gain_ref, s32[4]{0:T(128)S(1)} %fusion.5.refs_0_, ...), custom_call_target="tpu_custom_call" | custom-call | flops 1048576 | bytes 262144 | tf_op jit(solution)/shard_map/pallas_call | solution.py:134
  14.8 5.7 %shard_map.66 = (bf16[1536,1024]{1,0:T(8,128)(2,1)S(1)}, bf16[1536,1024]{1,0:T(8,128)(2,1)S(1)}, bf16[1536,1024]{1,0:T(8,128)(2,1)S(1)}, bf16[1536,1024]{1,0:T(8,128)(2,1)S(1)}, f32[1,2048]{1,0:T(1,128)S(1)}) custom-call(f32[1536,6144]{1,0:T(8,128)} %weight_ref.5, f32[1536,1]{1,0:T(8,128)S(1)} %broadcast_in_dim.19.gain_ref, ...), custom_call_target="tpu_custom_call" | custom-call | flops 1048576 | bytes 262144 | tf_op jit(solution)/shard_map/pallas_call | solution.py:134
  20.6 1.6 %collective-permute-start.4 = (f32[64,128]{1,0:T(8,128)S(1)}, f32[64,128]{1,0:T(8,128)S(1)}, u32[]{:S(2)}, u32[]{:S(2)}) collective-permute-start(f32[64,128]{1,0:T(8,128)S(1)} %shard_map.67.refs_2_), channel_id=1, source_target_pairs={{0,2},{1,3},{2,0},{3,1},{4,6},{5,7},{6,4},{7,5},{8,10},{9,11},{10,... | collective-permute-start | bytes 98312 | tf_op jit(solution)/shard_map/ppermute | solution.py:346
  22.2 2.4 %collective-permute-done.4.refs_3_ = f32[64,128]{1,0:T(8,128)S(1)} collective-permute-done((f32[64,128]{1,0:T(8,128)S(1)}, f32[64,128]{1,0:T(8,128)S(1)}, u32[]{:S(2)}, u32[]{:S(2)}) %collective-permute-start.4) | collective-permute-done | bytes 32800 | tf_op jit(solution)/shard_map/ppermute | solution.py:346
  24.8 2.8 %collective-permute-start.5 = (f32[32,1536]{1,0:T(8,128)S(1)}, f32[32,1536]{1,0:T(8,128)S(1)}, u32[]{:S(2)}, u32[]{:S(2)}) collective-permute-start(f32[32,1536]{1,0:T(8,128)S(1)} %get-tuple-element.109.refs_6_.refs_1_), channel_id=1, source_target_pairs={{0,4},{4,8},{8,12},{12,0},{1,5},{5,9},{9,13},{13,1},{2,6},{6,10},{... | collective-permute-start | bytes 589832 | tf_op jit(solution)/shard_map/ppermute | solution.py:340
  27.6 1.1 collective-permute-start.6
  28.7 11.5 %shard_map.69 = (f32[32,4096]{1,0:T(8,128)S(1)}, f32[32,4096]{1,0:T(8,128)S(1)}, f32[32,4096]{1,0:T(8,128)S(1)}, f32[32,4096]{1,0:T(8,128)S(1)}) custom-call(s32[4]{0:T(128)S(1)} %fusion.5.refs_0_, f32[32,1536]{1,0:T(8,128)S(1)} %copy-done.2, f32[32,1536]{1,0:T(8,128)S(1)} %collective-permute-done.1.refs_3_.refs_2_, ...), custom_call_target="tpu_custom_call" | custom-call | flops 1048576 | bytes 262144 | tf_op jit(solution)/shard_map/pallas_call | solution.py:253
  40.3 1.9 %collective-permute-done.7 = f32[32,4096]{1,0:T(8,128)S(1)} collective-permute-done((f32[32,4096]{1,0:T(8,128)S(1)}, f32[32,4096]{1,0:T(8,128)S(1)}, u32[]{:S(2)}, u32[]{:S(2)}) %collective-permute-start.7) | collective-permute-done | bytes 524320 | tf_op jit(solution)/shard_map/ppermute | solution.py:343
  42.3 1.6 %collective-permute-start.10 = (f32[32,4096]{1,0:T(8,128)S(1)}, f32[32,4096]{1,0:T(8,128)S(1)}, u32[]{:S(2)}, u32[]{:S(2)}) collective-permute-start(f32[32,4096]{1,0:T(8,128)S(1)} %add.59.refs_6_), channel_id=1, source_target_pairs={{0,2},{1,3},{2,0},{3,1},{4,6},{5,7},{6,4},{7,5},{8,10},{9,11},{10,... | collective-permute-start | bytes 1572872 | tf_op jit(solution)/shard_map/ppermute | solution.py:346
  44.8 6.8 %shard_map.70 = (f32[32,2048]{1,0:T(8,128)S(1)}, f32[32,2048]{1,0:T(8,128)S(1)}, f32[32,2048]{1,0:T(8,128)S(1)}, f32[32,2048]{1,0:T(8,128)S(1)}) custom-call(s32[4]{0:T(128)S(1)} %fusion.5.refs_0_, f32[32,1536]{1,0:T(8,128)S(1)} %copy-done.2, f32[32,1536]{1,0:T(8,128)S(1)} %collective-permute-done.1.refs_3_.refs_2_, ...), custom_call_target="tpu_custom_call" | custom-call | flops 1048576 | bytes 262144 | tf_op jit(solution)/shard_map/pallas_call | solution.py:253
  53.9 2.5 %collective-permute-done.10.refs_0_ = f32[32,4096]{1,0:T(8,128)S(1)} collective-permute-done((f32[32,4096]{1,0:T(8,128)S(1)}, f32[32,4096]{1,0:T(8,128)S(1)}, u32[]{:S(2)}, u32[]{:S(2)}) %collective-permute-start.10) | collective-permute-done | bytes 524320 | tf_op jit(solution)/shard_map/ppermute | solution.py:346
  56.4 1.6 %collective-permute-start.11 = (f32[32,2048]{1,0:T(8,128)S(1)}, f32[32,2048]{1,0:T(8,128)S(1)}, u32[]{:S(2)}, u32[]{:S(2)}) collective-permute-start(f32[32,2048]{1,0:T(8,128)S(1)} %add.60.refs_13_), channel_id=1, source_target_pairs={{0,2},{1,3},{2,0},{3,1},{4,6},{5,7},{6,4},{7,5},{8,10},{9,11},{10,... | collective-permute-start | bytes 786440 | tf_op jit(solution)/shard_map/ppermute | solution.py:346
  57.9 7.2 %shard_map.71 = (f32[32,4096]{1,0:T(8,128)S(1)}, f32[32,4096]{1,0:T(8,128)S(1)}, f32[32,4096]{1,0:T(8,128)S(1)}, f32[32,4096]{1,0:T(8,128)S(1)}) custom-call(s32[4]{0:T(128)S(1)} %fusion.5.refs_0_, f32[32,1536]{1,0:T(8,128)S(1)} %get-tuple-element.109.refs_6_.refs_1_, f32[32,1536]{1,0:T(8,128)S(1)} %collective-permute-done.5.refs_2_, ...), custom_call_target="tpu_custom_call" | custom-call | flops 1048576 | bytes 262144 | tf_op jit(solution)/shard_map/pallas_call | solution.py:211
  65.8 1.3 collective-permute-done.13
  67.9 5.7 %shard_map.72 = (bf16[1536,1024]{1,0:T(8,128)(2,1)S(1)}, bf16[1536,1024]{1,0:T(8,128)(2,1)S(1)}, bf16[1536,1024]{1,0:T(8,128)(2,1)S(1)}, bf16[1536,1024]{1,0:T(8,128)(2,1)S(1)}, f32[1,2048]{1,0:T(1,128)S(1)}) custom-call(f32[1536,6144]{1,0:T(8,128)} %weight_ref.5, f32[1536,1]{1,0:T(8,128)S(1)} %broadcast_in_dim.19.gain_ref, f32[32,4096]{1,0:T(8,128)S(1)} %add.61.refs_0_), custom_call_target="tpu_custom_call" | custom-call | flops 1048576 | bytes 262144 | tf_op jit(solution)/shard_map/pallas_call | solution.py:134
  73.7 1.2 collective-permute-done.14
  74.9 1.5 %collective-permute-start.15 = (f32[1,6144]{1,0:T(1,128)S(1)}, f32[1,6144]{1,0:T(1,128)S(1)}, u32[]{:S(2)}, u32[]{:S(2)}) collective-permute-start(f32[1,6144]{1,0:T(1,128)S(1)} %add.62), channel_id=1, source_target_pairs={{0,2},{1,3},{2,0},{3,1},{4,6},{5,7},{6,4},{7,5},{8,10},{9,11},{10,... | collective-permute-start | bytes 73736 | tf_op jit(solution)/shard_map/ppermute | solution.py:346
  76.4 3.9 %shard_map.73 = (f32[32,2048]{1,0:T(8,128)S(1)}, f32[32,2048]{1,0:T(8,128)S(1)}, f32[32,2048]{1,0:T(8,128)S(1)}, f32[32,2048]{1,0:T(8,128)S(1)}) custom-call(s32[4]{0:T(128)S(1)} %fusion.5.refs_0_, f32[32,1536]{1,0:T(8,128)S(1)} %get-tuple-element.109.refs_6_.refs_1_, f32[32,1536]{1,0:T(8,128)S(1)} %collective-permute-done.5.refs_2_, ...), custom_call_target="tpu_custom_call" | custom-call | flops 1048576 | bytes 262144 | tf_op jit(solution)/shard_map/pallas_call | solution.py:211
  80.4 1.4 %collective-permute-done.15 = f32[1,6144]{1,0:T(1,128)S(1)} collective-permute-done((f32[1,6144]{1,0:T(1,128)S(1)}, f32[1,6144]{1,0:T(1,128)S(1)}, u32[]{:S(2)}, u32[]{:S(2)}) %collective-permute-start.15) | collective-permute-done | bytes 24608 | tf_op jit(solution)/shard_map/ppermute | solution.py:346
  83.5 1.4 collective-permute-start.17
  84.9 17.6 %collective-permute-done.17.refs_3_ = f32[32,2048]{1,0:T(8,128)S(1)} collective-permute-done((f32[32,2048]{1,0:T(8,128)S(1)}, f32[32,2048]{1,0:T(8,128)S(1)}, u32[]{:S(2)}, u32[]{:S(2)}) %collective-permute-start.17) | collective-permute-done | bytes 262176 | tf_op jit(solution)/shard_map/ppermute | solution.py:346
  105.3 9.2 %shard_map.76 = (f32[32,1536]{1,0:T(8,128)S(1)}, f32[32,1536]{1,0:T(8,128)S(1)}, f32[32,1536]{1,0:T(8,128)S(1)}, f32[32,1536]{1,0:T(8,128)S(1)}) custom-call(s32[4]{0:T(128)S(1)} %fusion.5.refs_0_, f32[32,4096]{1,0:T(8,128)S(1)} %get-tuple-element.153.refs_8_.refs_1_, f32[32,4096]{1,0:T(8,128)S(1)} %collective-permute-done.23.refs_2_, ...), custom_call_target="tpu_custom_call" | custom-call | flops 1048576 | bytes 262144 | tf_op jit(solution)/shard_map/pallas_call | solution.py:307
  114.7 1.4 %collective-permute-done.27.refs_4_ = f32[32,2176]{1,0:T(8,128)S(1)} collective-permute-done((f32[32,2176]{1,0:T(8,128)S(1)}, f32[32,2176]{1,0:T(8,128)S(1)}, u32[]{:S(2)}, u32[]{:S(2)}) %collective-permute-start.27) | collective-permute-done | bytes 278560 | tf_op jit(solution)/shard_map/ppermute | solution.py:343
  116.1 3.1 %shard_map.77 = (f32[32,896]{1,0:T(8,128)S(1)}, f32[32,896]{1,0:T(8,128)S(1)}, f32[32,896]{1,0:T(8,128)S(1)}, f32[32,896]{1,0:T(8,128)S(1)}) custom-call(s32[4]{0:T(128)S(1)} %fusion.5.refs_0_, f32[32,2176]{1,0:T(8,128)S(1)} %get-tuple-element.155.refs_1_, f32[32,2176]{1,0:T(8,128)S(1)} %collective-permute-done.22.refs_2_, ...), custom_call_target="tpu_custom_call" | custom-call | flops 1048576 | bytes 262144 | tf_op jit(solution)/shard_map/pallas_call | solution.py:307
  119.2 2.0 %collective-permute-start.28 = (f32[32,896]{1,0:T(8,128)S(1)}, f32[32,896]{1,0:T(8,128)S(1)}, u32[]{:S(2)}, u32[]{:S(2)}) collective-permute-start(f32[32,896]{1,0:T(8,128)S(1)} %get-tuple-element.167), channel_id=1, source_target_pairs={{0,12},{4,0},{8,4},{12,8},{1,13},{5,1},{9,5},{13,9},{2,14},{6,2},{... | collective-permute-start | bytes 344072 | tf_op jit(solution)/shard_map/ppermute | solution.py:340
  122.0 3.0 %shard_map.78 = (f32[32,768]{1,0:T(8,128)S(1)}, f32[32,768]{1,0:T(8,128)S(1)}, f32[32,768]{1,0:T(8,128)S(1)}, f32[32,768]{1,0:T(8,128)S(1)}) custom-call(s32[4]{0:T(128)S(1)} %fusion.5.refs_0_, f32[32,2176]{1,0:T(8,128)S(1)} %get-tuple-element.155.refs_1_, f32[32,2176]{1,0:T(8,128)S(1)} %collective-permute-done.22.refs_2_, ...), custom_call_target="tpu_custom_call" | custom-call | flops 1048576 | bytes 262144 | tf_op jit(solution)/shard_map/pallas_call | solution.py:307
  125.0 3.6 %collective-permute-start.31 = (f32[32,768]{1,0:T(8,128)S(1)}, f32[32,768]{1,0:T(8,128)S(1)}, u32[]{:S(2)}, u32[]{:S(2)}) collective-permute-start(f32[32,768]{1,0:T(8,128)S(1)} %get-tuple-element.174), channel_id=1, source_target_pairs={{0,12},{4,0},{8,4},{12,8},{1,13},{5,1},{9,5},{13,9},{2,14},{6,2},{... | collective-permute-start | bytes 294920 | tf_op jit(solution)/shard_map/ppermute | solution.py:340
  130.4 6.3 %collective-permute-done.29 = f32[32,896]{1,0:T(8,128)S(1)} collective-permute-done((f32[32,896]{1,0:T(8,128)S(1)}, f32[32,896]{1,0:T(8,128)S(1)}, u32[]{:S(2)}, u32[]{:S(2)}) %collective-permute-start.29) | collective-permute-done | bytes 114720 | tf_op jit(solution)/shard_map/ppermute | solution.py:340
  136.9 3.6 %collective-permute-done.32 = f32[32,768]{1,0:T(8,128)S(1)} collective-permute-done((f32[32,768]{1,0:T(8,128)S(1)}, f32[32,768]{1,0:T(8,128)S(1)}, u32[]{:S(2)}, u32[]{:S(2)}) %collective-permute-start.32) | collective-permute-done | bytes 98336 | tf_op jit(solution)/shard_map/ppermute | solution.py:340
  (83 shorter events, 15.5 us)
Async XLA Ops:
  0.0 20.6 %collective-permute-start.1 = (f32[32,1536]{1,0:T(8,128)}, f32[32,1536]{1,0:T(8,128)S(1)}, u32[]{:S(2)}, u32[]{:S(2)}) collective-permute-start(f32[32,1536]{1,0:T(8,128)} %refs_1_.3), channel_id=1, source_target_pairs={{0,4},{4,8},{8,12},{12,0},{1,5},{5,9},{9,13},{13,1},{2,6},{6,10},{... | collective-permute-start | bytes 589832 | tf_op jit(solution)/shard_map/ppermute | solution.py:340
  3.0 17.6 %collective-permute-start.2 = (f32[32,1536]{1,0:T(8,128)}, f32[32,1536]{1,0:T(8,128)S(1)}, u32[]{:S(2)}, u32[]{:S(2)}) collective-permute-start(f32[32,1536]{1,0:T(8,128)} %refs_1_.3), channel_id=1, source_target_pairs={{0,8},{4,12},{8,0},{12,4},{1,9},{5,13},{9,1},{13,5},{2,10},{6,14},... | collective-permute-start | bytes 589832 | tf_op jit(solution)/shard_map/ppermute | solution.py:340
  5.6 15.0 %collective-permute-start.3 = (f32[32,1536]{1,0:T(8,128)}, f32[32,1536]{1,0:T(8,128)S(1)}, u32[]{:S(2)}, u32[]{:S(2)}) collective-permute-start(f32[32,1536]{1,0:T(8,128)} %refs_1_.3), channel_id=1, source_target_pairs={{0,12},{4,0},{8,4},{12,8},{1,13},{5,1},{9,5},{13,9},{2,14},{6,2},{... | collective-permute-start | bytes 589832 | tf_op jit(solution)/shard_map/ppermute | solution.py:340
  8.1 12.5 %collective-permute-start = (f32[64,128]{1,0:T(8,128)S(1)}, f32[64,128]{1,0:T(8,128)S(1)}, u32[]{:S(2)}, u32[]{:S(2)}) collective-permute-start(f32[64,128]{1,0:T(8,128)S(1)} %shard_map.64.refs_1_.refs_0_), channel_id=1, source_target_pairs={{0,1},{1,0},{2,3},{3,2},{4,5},{5,4},{6,7},{7,6},{8,9},{9,8},{10,11... | collective-permute-start | bytes 98312 | tf_op jit(solution)/shard_map/ppermute | solution.py:343
  20.6 4.0 %collective-permute-start.4 = (f32[64,128]{1,0:T(8,128)S(1)}, f32[64,128]{1,0:T(8,128)S(1)}, u32[]{:S(2)}, u32[]{:S(2)}) collective-permute-start(f32[64,128]{1,0:T(8,128)S(1)} %shard_map.67.refs_2_), channel_id=1, source_target_pairs={{0,2},{1,3},{2,0},{3,1},{4,6},{5,7},{6,4},{7,5},{8,10},{9,11},{10,... | collective-permute-start | bytes 98312 | tf_op jit(solution)/shard_map/ppermute | solution.py:346
  24.8 15.5 %collective-permute-start.5 = (f32[32,1536]{1,0:T(8,128)S(1)}, f32[32,1536]{1,0:T(8,128)S(1)}, u32[]{:S(2)}, u32[]{:S(2)}) collective-permute-start(f32[32,1536]{1,0:T(8,128)S(1)} %get-tuple-element.109.refs_6_.refs_1_), channel_id=1, source_target_pairs={{0,4},{4,8},{8,12},{12,0},{1,5},{5,9},{9,13},{13,1},{2,6},{6,10},{... | collective-permute-start | bytes 589832 | tf_op jit(solution)/shard_map/ppermute | solution.py:340
  27.6 12.7 %collective-permute-start.6 = (f32[32,1536]{1,0:T(8,128)S(1)}, f32[32,1536]{1,0:T(8,128)S(1)}, u32[]{:S(2)}, u32[]{:S(2)}) collective-permute-start(f32[32,1536]{1,0:T(8,128)S(1)} %get-tuple-element.109.refs_6_.refs_1_), channel_id=1, source_target_pairs={{0,12},{4,0},{8,4},{12,8},{1,13},{5,1},{9,5},{13,9},{2,14},{6,2},{... | collective-permute-start | bytes 589832 | tf_op jit(solution)/shard_map/ppermute | solution.py:340
  40.2 2.0 %collective-permute-start.7 = (f32[32,4096]{1,0:T(8,128)S(1)}, f32[32,4096]{1,0:T(8,128)S(1)}, u32[]{:S(2)}, u32[]{:S(2)}) collective-permute-start(f32[32,4096]{1,0:T(8,128)S(1)} %get-tuple-element.102), channel_id=1, source_target_pairs={{0,1},{1,0},{2,3},{3,2},{4,5},{5,4},{6,7},{7,6},{8,9},{9,8},{10,11... | collective-permute-start | bytes 1572872 | tf_op jit(solution)/shard_map/ppermute | solution.py:343
  42.3 14.0 %collective-permute-start.10 = (f32[32,4096]{1,0:T(8,128)S(1)}, f32[32,4096]{1,0:T(8,128)S(1)}, u32[]{:S(2)}, u32[]{:S(2)}) collective-permute-start(f32[32,4096]{1,0:T(8,128)S(1)} %add.59.refs_6_), channel_id=1, source_target_pairs={{0,2},{1,3},{2,0},{3,1},{4,6},{5,7},{6,4},{7,5},{8,10},{9,11},{10,... | collective-permute-start | bytes 1572872 | tf_op jit(solution)/shard_map/ppermute | solution.py:346
  43.9 8.5 %collective-permute-start.8 = (f32[32,1536]{1,0:T(8,128)S(1)}, f32[32,1536]{1,0:T(8,128)S(1)}, u32[]{:S(2)}, u32[]{:S(2)}) collective-permute-start(f32[32,1536]{1,0:T(8,128)S(1)} %collective-permute-done.5.refs_2_), channel_id=1, source_target_pairs={{0,4},{4,8},{8,12},{12,0},{1,5},{5,9},{9,13},{13,1},{2,6},{6,10},{... | collective-permute-start | bytes 589832 | tf_op jit(solution)/shard_map/ppermute | solution.py:340
  52.3 12.8 %collective-permute-start.12 = (f32[32,2048]{1,0:T(8,128)S(1)}, f32[32,2048]{1,0:T(8,128)S(1)}, u32[]{:S(2)}, u32[]{:S(2)}) collective-permute-start(f32[32,2048]{1,0:T(8,128)S(1)} %get-tuple-element.127), channel_id=1, source_target_pairs={{0,1},{1,0},{2,3},{3,2},{4,5},{5,4},{6,7},{7,6},{8,9},{9,8},{10,11... | collective-permute-start | bytes 786440 | tf_op jit(solution)/shard_map/ppermute | solution.py:343
  56.4 8.8 %collective-permute-start.11 = (f32[32,2048]{1,0:T(8,128)S(1)}, f32[32,2048]{1,0:T(8,128)S(1)}, u32[]{:S(2)}, u32[]{:S(2)}) collective-permute-start(f32[32,2048]{1,0:T(8,128)S(1)} %add.60.refs_13_), channel_id=1, source_target_pairs={{0,2},{1,3},{2,0},{3,1},{4,6},{5,7},{6,4},{7,5},{8,10},{9,11},{10,... | collective-permute-start | bytes 786440 | tf_op jit(solution)/shard_map/ppermute | solution.py:346
  65.2 2.0 %collective-permute-start.13 = (f32[32,4096]{1,0:T(8,128)S(1)}, f32[32,4096]{1,0:T(8,128)S(1)}, u32[]{:S(2)}, u32[]{:S(2)}) collective-permute-start(f32[32,4096]{1,0:T(8,128)S(1)} %get-tuple-element.132), channel_id=1, source_target_pairs={{0,1},{1,0},{2,3},{3,2},{4,5},{5,4},{6,7},{7,6},{8,9},{9,8},{10,11... | collective-permute-start | bytes 1572872 | tf_op jit(solution)/shard_map/ppermute | solution.py:343
  65.2 16.7 %collective-permute-start.19 = (f32[32,4096]{1,0:T(8,128)S(1)}, f32[32,4096]{1,0:T(8,128)S(1)}, u32[]{:S(2)}, u32[]{:S(2)}) collective-permute-start(f32[32,4096]{1,0:T(8,128)S(1)} %get-tuple-element.150), channel_id=1, source_target_pairs={{0,1},{1,0},{2,3},{3,2},{4,5},{5,4},{6,7},{7,6},{8,9},{9,8},{10,11... | collective-permute-start | bytes 1572872 | tf_op jit(solution)/shard_map/ppermute | solution.py:343
  65.7 16.2 %collective-permute-start.21 = (f32[32,4096]{1,0:T(8,128)S(1)}, f32[32,4096]{1,0:T(8,128)S(1)}, u32[]{:S(2)}, u32[]{:S(2)}) collective-permute-start(f32[32,4096]{1,0:T(8,128)S(1)} %get-tuple-element.152), channel_id=1, source_target_pairs={{0,1},{1,0},{2,3},{3,2},{4,5},{5,4},{6,7},{7,6},{8,9},{9,8},{10,11... | collective-permute-start | bytes 1572872 | tf_op jit(solution)/shard_map/ppermute | solution.py:343
  67.2 14.7 %collective-permute-start.20 = (f32[32,4096]{1,0:T(8,128)S(1)}, f32[32,4096]{1,0:T(8,128)S(1)}, u32[]{:S(2)}, u32[]{:S(2)}) collective-permute-start(f32[32,4096]{1,0:T(8,128)S(1)} %add.61.refs_0_), channel_id=1, source_target_pairs={{0,2},{1,3},{2,0},{3,1},{4,6},{5,7},{6,4},{7,5},{8,10},{9,11},{10,... | collective-permute-start | bytes 1572872 | tf_op jit(solution)/shard_map/ppermute | solution.py:346
  74.9 6.9 %collective-permute-start.15 = (f32[1,6144]{1,0:T(1,128)S(1)}, f32[1,6144]{1,0:T(1,128)S(1)}, u32[]{:S(2)}, u32[]{:S(2)}) collective-permute-start(f32[1,6144]{1,0:T(1,128)S(1)} %add.62), channel_id=1, source_target_pairs={{0,2},{1,3},{2,0},{3,1},{4,6},{5,7},{6,4},{7,5},{8,10},{9,11},{10,... | collective-permute-start | bytes 73736 | tf_op jit(solution)/shard_map/ppermute | solution.py:346
  81.8 1.6 %collective-permute-start.16 = (f32[32,2048]{1,0:T(8,128)S(1)}, f32[32,2048]{1,0:T(8,128)S(1)}, u32[]{:S(2)}, u32[]{:S(2)}) collective-permute-start(f32[32,2048]{1,0:T(8,128)S(1)} %get-tuple-element.145), channel_id=1, source_target_pairs={{0,1},{1,0},{2,3},{3,2},{4,5},{5,4},{6,7},{7,6},{8,9},{9,8},{10,11... | collective-permute-start | bytes 786440 | tf_op jit(solution)/shard_map/ppermute | solution.py:343
  82.5 20.9 %collective-permute-start.23 = (f32[32,4096]{1,0:T(8,128)S(1)}, f32[32,4096]{1,0:T(8,128)S(1)}, u32[]{:S(2)}, u32[]{:S(2)}) collective-permute-start(f32[32,4096]{1,0:T(8,128)S(1)} %get-tuple-element.153.refs_8_.refs_1_), channel_id=1, source_target_pairs={{0,2},{1,3},{2,0},{3,1},{4,6},{5,7},{6,4},{7,5},{8,10},{9,11},{10,... | collective-permute-start | bytes 1572872 | tf_op jit(solution)/shard_map/ppermute | solution.py:346
  83.1 1.8 %collective-permute-start.18 = (f32[32,2048]{1,0:T(8,128)S(1)}, f32[32,2048]{1,0:T(8,128)S(1)}, u32[]{:S(2)}, u32[]{:S(2)}) collective-permute-start(f32[32,2048]{1,0:T(8,128)S(1)} %get-tuple-element.147), channel_id=1, source_target_pairs={{0,1},{1,0},{2,3},{3,2},{4,5},{5,4},{6,7},{7,6},{8,9},{9,8},{10,11... | collective-permute-start | bytes 786440 | tf_op jit(solution)/shard_map/ppermute | solution.py:343
  83.5 19.0 %collective-permute-start.17 = (f32[32,2048]{1,0:T(8,128)S(1)}, f32[32,2048]{1,0:T(8,128)S(1)}, u32[]{:S(2)}, u32[]{:S(2)}) collective-permute-start(f32[32,2048]{1,0:T(8,128)S(1)} %add.64), channel_id=1, source_target_pairs={{0,2},{1,3},{2,0},{3,1},{4,6},{5,7},{6,4},{7,5},{8,10},{9,11},{10,... | collective-permute-start | bytes 786440 | tf_op jit(solution)/shard_map/ppermute | solution.py:346
  84.8 19.3 %collective-permute-start.24 = (f32[32,4096]{1,0:T(8,128)S(1)}, f32[32,4096]{1,0:T(8,128)S(1)}, u32[]{:S(2)}, u32[]{:S(2)}) collective-permute-start(f32[32,4096]{1,0:T(8,128)S(1)} %get-tuple-element.153.refs_8_.refs_1_), channel_id=1, source_target_pairs={{0,1},{1,0},{2,3},{3,2},{4,5},{5,4},{6,7},{7,6},{8,9},{9,8},{10,11... | collective-permute-start | bytes 1572872 | tf_op jit(solution)/shard_map/ppermute | solution.py:343
  103.4 1.9 %collective-permute-start.25 = (f32[32,4096]{1,0:T(8,128)S(1)}, f32[32,4096]{1,0:T(8,128)S(1)}, u32[]{:S(2)}, u32[]{:S(2)}) collective-permute-start(f32[32,4096]{1,0:T(8,128)S(1)} %collective-permute-done.23.refs_2_), channel_id=1, source_target_pairs={{0,1},{1,0},{2,3},{3,2},{4,5},{5,4},{6,7},{7,6},{8,9},{9,8},{10,11... | collective-permute-start | bytes 1572872 | tf_op jit(solution)/shard_map/ppermute | solution.py:343
  103.4 11.1 %collective-permute-start.22 = (f32[32,2176]{1,0:T(8,128)S(1)}, f32[32,2176]{1,0:T(8,128)S(1)}, u32[]{:S(2)}, u32[]{:S(2)}) collective-permute-start(f32[32,2176]{1,0:T(8,128)S(1)} %get-tuple-element.155.refs_1_), channel_id=1, source_target_pairs={{0,2},{1,3},{2,0},{3,1},{4,6},{5,7},{6,4},{7,5},{8,10},{9,11},{10,... | collective-permute-start | bytes 835592 | tf_op jit(solution)/shard_map/ppermute | solution.py:346
  104.0 10.8 %collective-permute-start.26 = (f32[32,2176]{1,0:T(8,128)S(1)}, f32[32,2176]{1,0:T(8,128)S(1)}, u32[]{:S(2)}, u32[]{:S(2)}) collective-permute-start(f32[32,2176]{1,0:T(8,128)S(1)} %get-tuple-element.155.refs_1_), channel_id=1, source_target_pairs={{0,1},{1,0},{2,3},{3,2},{4,5},{5,4},{6,7},{7,6},{8,9},{9,8},{10,11... | collective-permute-start | bytes 835592 | tf_op jit(solution)/shard_map/ppermute | solution.py:343
  114.5 1.6 %collective-permute-start.27 = (f32[32,2176]{1,0:T(8,128)S(1)}, f32[32,2176]{1,0:T(8,128)S(1)}, u32[]{:S(2)}, u32[]{:S(2)}) collective-permute-start(f32[32,2176]{1,0:T(8,128)S(1)} %collective-permute-done.22.refs_2_), channel_id=1, source_target_pairs={{0,1},{1,0},{2,3},{3,2},{4,5},{5,4},{6,7},{7,6},{8,9},{9,8},{10,11... | collective-permute-start | bytes 835592 | tf_op jit(solution)/shard_map/ppermute | solution.py:343
  119.2 10.2 %collective-permute-start.28 = (f32[32,896]{1,0:T(8,128)S(1)}, f32[32,896]{1,0:T(8,128)S(1)}, u32[]{:S(2)}, u32[]{:S(2)}) collective-permute-start(f32[32,896]{1,0:T(8,128)S(1)} %get-tuple-element.167), channel_id=1, source_target_pairs={{0,12},{4,0},{8,4},{12,8},{1,13},{5,1},{9,5},{13,9},{2,14},{6,2},{... | collective-permute-start | bytes 344072 | tf_op jit(solution)/shard_map/ppermute | solution.py:340
  121.2 15.5 %collective-permute-start.29 = (f32[32,896]{1,0:T(8,128)S(1)}, f32[32,896]{1,0:T(8,128)S(1)}, u32[]{:S(2)}, u32[]{:S(2)}) collective-permute-start(f32[32,896]{1,0:T(8,128)S(1)} %get-tuple-element.168), channel_id=1, source_target_pairs={{0,8},{4,12},{8,0},{12,4},{1,9},{5,13},{9,1},{13,5},{2,10},{6,14},... | collective-permute-start | bytes 344072 | tf_op jit(solution)/shard_map/ppermute | solution.py:340
  121.6 15.1 %collective-permute-start.30 = (f32[32,896]{1,0:T(8,128)S(1)}, f32[32,896]{1,0:T(8,128)S(1)}, u32[]{:S(2)}, u32[]{:S(2)}) collective-permute-start(f32[32,896]{1,0:T(8,128)S(1)} %get-tuple-element.169), channel_id=1, source_target_pairs={{0,4},{4,8},{8,12},{12,0},{1,5},{5,9},{9,13},{13,1},{2,6},{6,10},{... | collective-permute-start | bytes 344072 | tf_op jit(solution)/shard_map/ppermute | solution.py:340
  125.0 11.9 %collective-permute-start.31 = (f32[32,768]{1,0:T(8,128)S(1)}, f32[32,768]{1,0:T(8,128)S(1)}, u32[]{:S(2)}, u32[]{:S(2)}) collective-permute-start(f32[32,768]{1,0:T(8,128)S(1)} %get-tuple-element.174), channel_id=1, source_target_pairs={{0,12},{4,0},{8,4},{12,8},{1,13},{5,1},{9,5},{13,9},{2,14},{6,2},{... | collective-permute-start | bytes 294920 | tf_op jit(solution)/shard_map/ppermute | solution.py:340
  128.6 12.0 %collective-permute-start.32 = (f32[32,768]{1,0:T(8,128)S(1)}, f32[32,768]{1,0:T(8,128)S(1)}, u32[]{:S(2)}, u32[]{:S(2)}) collective-permute-start(f32[32,768]{1,0:T(8,128)S(1)} %get-tuple-element.175), channel_id=1, source_target_pairs={{0,8},{4,12},{8,0},{12,4},{1,9},{5,13},{9,1},{13,5},{2,10},{6,14},... | collective-permute-start | bytes 294920 | tf_op jit(solution)/shard_map/ppermute | solution.py:340
  129.4 11.2 %collective-permute-start.33 = (f32[32,768]{1,0:T(8,128)S(1)}, f32[32,768]{1,0:T(8,128)S(1)}, u32[]{:S(2)}, u32[]{:S(2)}) collective-permute-start(f32[32,768]{1,0:T(8,128)S(1)} %get-tuple-element.176), channel_id=1, source_target_pairs={{0,4},{4,8},{8,12},{12,0},{1,5},{5,9},{9,13},{13,1},{2,6},{6,10},{... | collective-permute-start | bytes 294920 | tf_op jit(solution)/shard_map/ppermute | solution.py:340
  (7 other events, 23.0 us)

commit v18 on v14

--- a/solution.py
+++ b/solution.py
@@ -75,20 +75,23 @@
     inv_std_ref[...] = inv_std
 
 
-def slope_kernel(terms, *refs):
+def slope_kernel(terms, earlier, *refs):
     back_refs, pre_refs, (bias_ref, weight_ref) = refs[:terms], refs[terms : 2 * terms], refs[2 * terms : 2 * terms + 2]
-    *sums_refs, act_ref, out_sums_ref = refs[2 * terms + 2 :]
+    sums_refs, act_refs = refs[2 * terms + 2 : 2 * terms + 2 + earlier], refs[2 * terms + 2 + earlier : -1]
+    out_sums_ref = refs[-1]
     hidden = bias_ref.shape[1]
     product = sum(ref[...] for ref in pre_refs)
     act = sum(ref[...] for ref in back_refs) * gelu_slope(product + bias_ref[...])
-    act_ref[:, :hidden] = act
+    width = hidden // len(act_refs)
+    for n, act_ref in enumerate(act_refs):
+        act_ref[:, :width] = act[:, n * width : (n + 1) * width]
     lane = lax.broadcasted_iota(jnp.int32, out_sums_ref.shape, 1)
     first = jnp.sum(act * weight_ref[...], axis=1, keepdims=True)
     second = jnp.sum(act * product, axis=1, keepdims=True)
     sums = jnp.where(lane == 0, first, jnp.where(lane == 1, second, 0.0)) + sum(ref[...] for ref in sums_refs)
     out_sums_ref[...] = sums
-    if act_ref.shape[1] > hidden:
-        act_ref[:, hidden:] = sums
+    if act_refs[-1].shape[1] > width:
+        act_refs[-1][:, width:] = sums
 
 
 def prepare_kernel(rows, columns, block, depth, weight_ref, gain_ref, *refs):
@@ -418,15 +421,14 @@
         passing = next_chip(passing)
         gain_sums = gain_sums + passing
 
-    def slope_product(span, back, pre, sums):
-        width = span.stop - span.start
+    def slope_product(span, back, pre, sums, after):
+        pieces, room = (span.stop - span.start) // third, 128 * len(sums)
+        widths = [third] * (pieces - 1) + [third + room, 128]
         return call(
-            functools.partial(slope_kernel, len(back)),
-            tuple(
-                jax.ShapeDtypeStruct((tokens, n), jnp.float32) for n in (width + 128 * len(sums), 128)
-            ),
+            functools.partial(slope_kernel, len(back), len(sums)),
+            tuple(jax.ShapeDtypeStruct((tokens, n), jnp.float32) for n in widths),
             (*back, *pre, in_bias[None, span], gain_sums[:, span], *sums),
-            (),
+            after,
         )
 
     def spread_out(act):
@@ -446,11 +448,12 @@
 
     half_1 = halved(pre_1, pre_0[0])
     pre_0 = tied(pre_0, half_1[0])[0]
-    act_0, sums_0 = slope_product(slice(0, 2 * third), back_0, pre_0, ())
+    act_0, act_1, sums_0 = slope_product(slice(0, 2 * third), back_0, pre_0, (), ())
     pre_1 = exchanged(half_1)
-    act_1, _ = slope_product(slice(2 * third, hidden), back_1, pre_1, (sums_0,))
-    acts_0, acts_1 = spread_out(act_0), spread_out(act_1)
-    sums = backward(both_cores(acts_0), in_parts[:8], place, (), 0, 1, [])
+    sums = backward(both_cores(spread_out(act_0)), in_parts[:4], place, (), 0, 1, [])
+    act_2, _ = slope_product(slice(2 * third, hidden), back_1, pre_1, (sums_0,), (sums[0],))
+    acts_0, acts_1 = spread_out(act_1), spread_out(act_2)
+    sums = backward(both_cores(acts_0), in_parts[4:8], place, sums, 0, 1, [act_2])
     acts_1[1:], sums = tied(acts_1[1:], sums)
     acts_1 = both_cores(acts_1)
     parts = 2 if depth % 512 == 0 else 1

time: 138 us -> 137 us (level)
  waiting for transfers between devices: 40 us -> 37.6 us
    ppermute x8 -> x9, waiting for transfers between devices: 23.8 us -> 20.5 us  [next_chip(): lax.ppermute(values, 'emb', [(i, (i + 2) % emb_size) for i in range(emb_s...]
    pallas_call x3 -> x4, Pallas kernels: 15.3 us -> 16.7 us  [backward(): pl.pallas_call(lambda *refs: backward_kernel(part * depth, depth, refs[0]...]
    ppermute x14 -> x16, waiting for transfers between devices: 4.44 us -> 5.7 us  [other_core(): return lax.ppermute(values, 'emb', [(i, i ^ 1) for i in range(emb_size)])]
    ppermute x8 -> x9, starting transfers between devices: 8.1 us -> 8.66 us  [next_chip(): lax.ppermute(values, 'emb', [(i, (i + 2) % emb_size) for i in range(emb_s...]
    ppermute x14 -> x16, starting transfers between devices: 2.86 us -> 3 us  [other_core(): return lax.ppermute(values, 'emb', [(i, i ^ 1) for i in range(emb_size)])]
  transfers between devices with their start and end apart: 34 -> 37, of which waited for: 12 -> 14; matrix products, arithmetic and copies ran while one was open for 1% -> 1% of each run, Pallas kernels for 44% -> 45%
where the time goes in v18:
time: 137 us
  Pallas kernels  65.1 us (48%)
  waiting for transfers between devices  37.6 us (27%)
  starting transfers between devices  30.7 us (22%)
  local copies, waits for them, and re-layouts  2.04 us (1%)
    ppermute x9, waiting for transfers between devices, next_chip(): lax.ppermute(values, 'emb', [(i, (i + 2) % emb_size) for i in range(emb_s...  20.5 us
    ppermute x12, starting transfers between devices, along_hid(): lax.ppermute(values, 'hid', [(i, (i + steps) % hid_size) for i in range(h...  19 us
    pallas_call x2, Pallas kernels, stream(): pl.pallas_call(lambda *refs: stream_kernel(first, depth, refs[0], refs[1:...  18.3 us
    pallas_call x3, Pallas kernels, prepare(): pl.pallas_call(lambda weight_ref, gain_ref, *refs: prepare_kernel(rows, c...  17.2 us
    pallas_call x4, Pallas kernels, backward(): pl.pallas_call(lambda *refs: backward_kernel(part * depth, depth, refs[0]...  16.7 us
    ppermute x12, waiting for transfers between devices, along_hid(): lax.ppermute(values, 'hid', [(i, (i + steps) % hid_size) for i in range(h...  11.4 us
    pallas_call x2, Pallas kernels, forward(): pl.pallas_call(lambda *refs: forward_kernel(refs[0], refs[1:ends[0]], ref...  11.2 us
    ppermute x9, starting transfers between devices, next_chip(): lax.ppermute(values, 'emb', [(i, (i + 2) % emb_size) for i in range(emb_s...  8.66 us
  transfers between devices with their start and end apart: 37, of which 14 were waited for; matrix products, arithmetic and copies ran while one was open for 1% of the time, Pallas kernels for 45%

profile of v18, /device:TPU:0, one launch (start us, length us, event | category | flops | bytes accessed | tf_op | source)
XLA Modules:
  0.0 137.1 jit_solution(11156394685140410599)
XLA Ops:
  0.0 3.0 %collective-permute-start.1 = (f32[32,1536]{1,0:T(8,128)}, f32[32,1536]{1,0:T(8,128)S(1)}, u32[]{:S(2)}, u32[]{:S(2)}) collective-permute-start(f32[32,1536]{1,0:T(8,128)} %refs_1_.3), channel_id=1, source_target_pairs={{0,4},{4,8},{8,12},{12,0},{1,5},{5,9},{9,13},{13,1},{2,6},{6,10},{... | collective-permute-start | bytes 589832 | tf_op jit(solution)/shard_map/ppermute | solution.py:342
  3.0 2.6 %collective-permute-start.2 = (f32[32,1536]{1,0:T(8,128)}, f32[32,1536]{1,0:T(8,128)S(1)}, u32[]{:S(2)}, u32[]{:S(2)}) collective-permute-start(f32[32,1536]{1,0:T(8,128)} %refs_1_.3), channel_id=1, source_target_pairs={{0,8},{4,12},{8,0},{12,4},{1,9},{5,13},{9,1},{13,5},{2,10},{6,14},... | collective-permute-start | bytes 589832 | tf_op jit(solution)/shard_map/ppermute | solution.py:342
  5.6 1.3 collective-permute-start.3
  9.1 5.7 %shard_map.65 = (bf16[1536,1024]{1,0:T(8,128)(2,1)S(1)}, bf16[1536,1024]{1,0:T(8,128)(2,1)S(1)}, bf16[1536,1024]{1,0:T(8,128)(2,1)S(1)}, bf16[1536,1024]{1,0:T(8,128)(2,1)S(1)}, f32[1,2048]{1,0:T(1,128)S(1)}) custom-call(f32[1536,6144]{1,0:T(8,128)} %weight_ref.5, f32[1536,1]{1,0:T(8,128)S(1)} %broadcast_in_dim.19.gain_ref, s32[4]{0:T(128)S(1)} %fusion.5.refs_0_, ...), custom_call_target="tpu_custom_call" | custom-call | flops 1048576 | bytes 262144 | tf_op jit(solution)/shard_map/pallas_call | solution.py:135
  14.8 5.7 %shard_map.66 = (bf16[1536,1024]{1,0:T(8,128)(2,1)S(1)}, bf16[1536,1024]{1,0:T(8,128)(2,1)S(1)}, bf16[1536,1024]{1,0:T(8,128)(2,1)S(1)}, bf16[1536,1024]{1,0:T(8,128)(2,1)S(1)}, f32[1,2048]{1,0:T(1,128)S(1)}) custom-call(f32[1536,6144]{1,0:T(8,128)} %weight_ref.5, f32[1536,1]{1,0:T(8,128)S(1)} %broadcast_in_dim.19.gain_ref, ...), custom_call_target="tpu_custom_call" | custom-call | flops 1048576 | bytes 262144 | tf_op jit(solution)/shard_map/pallas_call | solution.py:135
  20.6 1.6 %collective-permute-start.4 = (f32[64,128]{1,0:T(8,128)S(1)}, f32[64,128]{1,0:T(8,128)S(1)}, u32[]{:S(2)}, u32[]{:S(2)}) collective-permute-start(f32[64,128]{1,0:T(8,128)S(1)} %shard_map.67.refs_2_), channel_id=1, source_target_pairs={{0,2},{1,3},{2,0},{3,1},{4,6},{5,7},{6,4},{7,5},{8,10},{9,11},{10,... | collective-permute-start | bytes 98312 | tf_op jit(solution)/shard_map/ppermute | solution.py:348
  22.2 2.4 %collective-permute-done.4.refs_3_ = f32[64,128]{1,0:T(8,128)S(1)} collective-permute-done((f32[64,128]{1,0:T(8,128)S(1)}, f32[64,128]{1,0:T(8,128)S(1)}, u32[]{:S(2)}, u32[]{:S(2)}) %collective-permute-start.4) | collective-permute-done | bytes 32800 | tf_op jit(solution)/shard_map/ppermute | solution.py:348
  24.8 2.8 %collective-permute-start.5 = (f32[32,1536]{1,0:T(8,128)S(1)}, f32[32,1536]{1,0:T(8,128)S(1)}, u32[]{:S(2)}, u32[]{:S(2)}) collective-permute-start(f32[32,1536]{1,0:T(8,128)S(1)} %get-tuple-element.108.refs_6_.refs_1_), channel_id=1, source_target_pairs={{0,4},{4,8},{8,12},{12,0},{1,5},{5,9},{9,13},{13,1},{2,6},{6,10},{... | collective-permute-start | bytes 589832 | tf_op jit(solution)/shard_map/ppermute | solution.py:342
  27.6 1.1 collective-permute-start.6
  28.7 11.5 %shard_map.69 = (f32[32,4096]{1,0:T(8,128)S(1)}, f32[32,4096]{1,0:T(8,128)S(1)}, f32[32,4096]{1,0:T(8,128)S(1)}, f32[32,4096]{1,0:T(8,128)S(1)}) custom-call(s32[4]{0:T(128)S(1)} %fusion.5.refs_0_, f32[32,1536]{1,0:T(8,128)S(1)} %copy-done.2, f32[32,1536]{1,0:T(8,128)S(1)} %collective-permute-done.1.refs_3_.refs_2_, ...), custom_call_target="tpu_custom_call" | custom-call | flops 1048576 | bytes 262144 | tf_op jit(solution)/shard_map/pallas_call | solution.py:254
  40.3 1.9 %collective-permute-done.7 = f32[32,4096]{1,0:T(8,128)S(1)} collective-permute-done((f32[32,4096]{1,0:T(8,128)S(1)}, f32[32,4096]{1,0:T(8,128)S(1)}, u32[]{:S(2)}, u32[]{:S(2)}) %collective-permute-start.7) | collective-permute-done | bytes 524320 | tf_op jit(solution)/shard_map/ppermute | solution.py:345
  42.3 1.6 %collective-permute-start.10 = (f32[32,4096]{1,0:T(8,128)S(1)}, f32[32,4096]{1,0:T(8,128)S(1)}, u32[]{:S(2)}, u32[]{:S(2)}) collective-permute-start(f32[32,4096]{1,0:T(8,128)S(1)} %add.59.refs_6_), channel_id=1, source_target_pairs={{0,2},{1,3},{2,0},{3,1},{4,6},{5,7},{6,4},{7,5},{8,10},{9,11},{10,... | collective-permute-start | bytes 1572872 | tf_op jit(solution)/shard_map/ppermute | solution.py:348
  44.7 6.8 %shard_map.70 = (f32[32,2048]{1,0:T(8,128)S(1)}, f32[32,2048]{1,0:T(8,128)S(1)}, f32[32,2048]{1,0:T(8,128)S(1)}, f32[32,2048]{1,0:T(8,128)S(1)}) custom-call(s32[4]{0:T(128)S(1)} %fusion.5.refs_0_, f32[32,1536]{1,0:T(8,128)S(1)} %copy-done.2, f32[32,1536]{1,0:T(8,128)S(1)} %collective-permute-done.1.refs_3_.refs_2_, ...), custom_call_target="tpu_custom_call" | custom-call | flops 1048576 | bytes 262144 | tf_op jit(solution)/shard_map/pallas_call | solution.py:254
  52.3 7.2 %shard_map.71 = (f32[32,4096]{1,0:T(8,128)S(1)}, f32[32,4096]{1,0:T(8,128)S(1)}, f32[32,4096]{1,0:T(8,128)S(1)}, f32[32,4096]{1,0:T(8,128)S(1)}) custom-call(s32[4]{0:T(128)S(1)} %fusion.5.refs_0_, f32[32,1536]{1,0:T(8,128)S(1)} %get-tuple-element.108.refs_6_.refs_1_, f32[32,1536]{1,0:T(8,128)S(1)} %collective-permute-done.5.refs_2_, ...), custom_call_target="tpu_custom_call" | custom-call | flops 1048576 | bytes 262144 | tf_op jit(solution)/shard_map/pallas_call | solution.py:212
  61.7 1.2 collective-permute-start.15
  62.9 5.7 %shard_map.72 = (bf16[1536,1024]{1,0:T(8,128)(2,1)S(1)}, bf16[1536,1024]{1,0:T(8,128)(2,1)S(1)}, bf16[1536,1024]{1,0:T(8,128)(2,1)S(1)}, bf16[1536,1024]{1,0:T(8,128)(2,1)S(1)}, f32[1,2048]{1,0:T(1,128)S(1)}) custom-call(f32[1536,6144]{1,0:T(8,128)} %weight_ref.5, f32[1536,1]{1,0:T(8,128)S(1)} %broadcast_in_dim.19.gain_ref, ...), custom_call_target="tpu_custom_call" | custom-call | flops 1048576 | bytes 262144 | tf_op jit(solution)/shard_map/pallas_call | solution.py:135
  69.4 3.9 %shard_map.73 = (f32[32,2048]{1,0:T(8,128)S(1)}, f32[32,2048]{1,0:T(8,128)S(1)}, f32[32,2048]{1,0:T(8,128)S(1)}, f32[32,2048]{1,0:T(8,128)S(1)}) custom-call(s32[4]{0:T(128)S(1)} %fusion.5.refs_0_, f32[32,1536]{1,0:T(8,128)S(1)} %get-tuple-element.108.refs_6_.refs_1_, f32[32,1536]{1,0:T(8,128)S(1)} %collective-permute-done.5.refs_2_, ...), custom_call_target="tpu_custom_call" | custom-call | flops 1048576 | bytes 262144 | tf_op jit(solution)/shard_map/pallas_call | solution.py:212
  75.6 4.6 %collective-permute-done.19 = f32[1,6144]{1,0:T(1,128)S(1)} collective-permute-done((f32[1,6144]{1,0:T(1,128)S(1)}, f32[1,6144]{1,0:T(1,128)S(1)}, u32[]{:S(2)}, u32[]{:S(2)}) %collective-permute-start.19) | collective-permute-done | bytes 24608 | tf_op jit(solution)/shard_map/ppermute | solution.py:348
  81.5 6.8 %collective-permute-done.22.refs_2_ = f32[32,2048]{1,0:T(8,128)S(1)} collective-permute-done((f32[32,2048]{1,0:T(8,128)S(1)}, f32[32,2048]{1,0:T(8,128)S(1)}, u32[]{:S(2)}, u32[]{:S(2)}) %collective-permute-start.22) | collective-permute-done | bytes 262176 | tf_op jit(solution)/shard_map/ppermute | solution.py:348
  89.4 1.5 %collective-permute-start.26 = (f32[32,2048]{1,0:T(8,128)S(1)}, f32[32,2048]{1,0:T(8,128)S(1)}, u32[]{:S(2)}, u32[]{:S(2)}) collective-permute-start(f32[32,2048]{1,0:T(8,128)S(1)} %get-tuple-element.147.refs_1_), channel_id=1, source_target_pairs={{0,2},{1,3},{2,0},{3,1},{4,6},{5,7},{6,4},{7,5},{8,10},{9,11},{10,... | collective-permute-start | bytes 786440 | tf_op jit(solution)/shard_map/ppermute | solution.py:348
  90.9 5.3 %shard_map.75 = (f32[32,1536]{1,0:T(8,128)S(1)}, f32[32,1536]{1,0:T(8,128)S(1)}, f32[32,1536]{1,0:T(8,128)S(1)}, f32[32,1536]{1,0:T(8,128)S(1)}) custom-call(s32[4]{0:T(128)S(1)} %fusion.5.refs_0_, f32[32,2048]{1,0:T(8,128)S(1)} %get-tuple-element.144.refs_1_, f32[32,2048]{1,0:T(8,128)S(1)} %collective-permute-done.22.refs_2_, ...), custom_call_target="tpu_custom_call" | custom-call | flops 1048576 | bytes 262144 | tf_op jit(solution)/shard_map/pallas_call | solution.py:309
  96.2 1.7 %collective-permute-done.16.refs_3_ = f32[32,2048]{1,0:T(8,128)S(1)} collective-permute-done((f32[32,2048]{1,0:T(8,128)S(1)}, f32[32,2048]{1,0:T(8,128)S(1)}, u32[]{:S(2)}, u32[]{:S(2)}) %collective-permute-start.16) | collective-permute-done | bytes 262176 | tf_op jit(solution)/shard_map/ppermute | solution.py:348
  99.4 4.2 %collective-permute-done.26.refs_2_ = f32[32,2048]{1,0:T(8,128)S(1)} collective-permute-done((f32[32,2048]{1,0:T(8,128)S(1)}, f32[32,2048]{1,0:T(8,128)S(1)}, u32[]{:S(2)}, u32[]{:S(2)}) %collective-permute-start.26) | collective-permute-done | bytes 262176 | tf_op jit(solution)/shard_map/ppermute | solution.py:348
  105.1 5.3 %shard_map.77 = (f32[32,1536]{1,0:T(8,128)S(1)}, f32[32,1536]{1,0:T(8,128)S(1)}, f32[32,1536]{1,0:T(8,128)S(1)}, f32[32,1536]{1,0:T(8,128)S(1)}) custom-call(s32[4]{0:T(128)S(1)} %fusion.5.refs_0_, f32[32,2048]{1,0:T(8,128)S(1)} %get-tuple-element.147.refs_1_, f32[32,2048]{1,0:T(8,128)S(1)} %collective-permute-done.26.refs_2_, ...), custom_call_target="tpu_custom_call" | custom-call | flops 1048576 | bytes 262144 | tf_op jit(solution)/shard_map/pallas_call | solution.py:309
  110.6 1.4 %collective-permute-done.30.refs_4_ = f32[32,2176]{1,0:T(8,128)S(1)} collective-permute-done((f32[32,2176]{1,0:T(8,128)S(1)}, f32[32,2176]{1,0:T(8,128)S(1)}, u32[]{:S(2)}, u32[]{:S(2)}) %collective-permute-start.30) | collective-permute-done | bytes 278560 | tf_op jit(solution)/shard_map/ppermute | solution.py:345
  112.0 3.1 %shard_map.78 = (f32[32,896]{1,0:T(8,128)S(1)}, f32[32,896]{1,0:T(8,128)S(1)}, f32[32,896]{1,0:T(8,128)S(1)}, f32[32,896]{1,0:T(8,128)S(1)}) custom-call(s32[4]{0:T(128)S(1)} %fusion.5.refs_0_, f32[32,2176]{1,0:T(8,128)S(1)} %get-tuple-element.146.refs_13_.refs_1_, f32[32,2176]{1,0:T(8,128)S(1)} %collective-permute-done.25.refs_2_, ...), custom_call_target="tpu_custom_call" | custom-call | flops 1048576 | bytes 262144 | tf_op jit(solution)/shard_map/pallas_call | solution.py:309
  115.1 2.3 %collective-permute-start.31 = (f32[32,896]{1,0:T(8,128)S(1)}, f32[32,896]{1,0:T(8,128)S(1)}, u32[]{:S(2)}, u32[]{:S(2)}) collective-permute-start(f32[32,896]{1,0:T(8,128)S(1)} %get-tuple-element.161), channel_id=1, source_target_pairs={{0,12},{4,0},{8,4},{12,8},{1,13},{5,1},{9,5},{13,9},{2,14},{6,2},{... | collective-permute-start | bytes 344072 | tf_op jit(solution)/shard_map/ppermute | solution.py:342
  118.2 3.0 %shard_map.79 = (f32[32,768]{1,0:T(8,128)S(1)}, f32[32,768]{1,0:T(8,128)S(1)}, f32[32,768]{1,0:T(8,128)S(1)}, f32[32,768]{1,0:T(8,128)S(1)}) custom-call(s32[4]{0:T(128)S(1)} %fusion.5.refs_0_, f32[32,2176]{1,0:T(8,128)S(1)} %get-tuple-element.146.refs_13_.refs_1_, f32[32,2176]{1,0:T(8,128)S(1)} %collective-permute-done.25.refs_2_, ...), custom_call_target="tpu_custom_call" | custom-call | flops 1048576 | bytes 262144 | tf_op jit(solution)/shard_map/pallas_call | solution.py:309
  121.3 3.2 %collective-permute-start.34 = (f32[32,768]{1,0:T(8,128)S(1)}, f32[32,768]{1,0:T(8,128)S(1)}, u32[]{:S(2)}, u32[]{:S(2)}) collective-permute-start(f32[32,768]{1,0:T(8,128)S(1)} %get-tuple-element.168), channel_id=1, source_target_pairs={{0,12},{4,0},{8,4},{12,8},{1,13},{5,1},{9,5},{13,9},{2,14},{6,2},{... | collective-permute-start | bytes 294920 | tf_op jit(solution)/shard_map/ppermute | solution.py:342
  124.4 1.1 collective-permute-start.35
  125.5 7.0 %collective-permute-done.32 = f32[32,896]{1,0:T(8,128)S(1)} collective-permute-done((f32[32,896]{1,0:T(8,128)S(1)}, f32[32,896]{1,0:T(8,128)S(1)}, u32[]{:S(2)}, u32[]{:S(2)}) %collective-permute-start.32) | collective-permute-done | bytes 114720 | tf_op jit(solution)/shard_map/ppermute | solution.py:342
  132.8 3.5 %collective-permute-done.35 = f32[32,768]{1,0:T(8,128)S(1)} collective-permute-done((f32[32,768]{1,0:T(8,128)S(1)}, f32[32,768]{1,0:T(8,128)S(1)}, u32[]{:S(2)}, u32[]{:S(2)}) %collective-permute-start.35) | collective-permute-done | bytes 98336 | tf_op jit(solution)/shard_map/ppermute | solution.py:342
  (88 shorter events, 16.6 us)
Async XLA Ops:
  0.0 20.6 %collective-permute-start.1 = (f32[32,1536]{1,0:T(8,128)}, f32[32,1536]{1,0:T(8,128)S(1)}, u32[]{:S(2)}, u32[]{:S(2)}) collective-permute-start(f32[32,1536]{1,0:T(8,128)} %refs_1_.3), channel_id=1, source_target_pairs={{0,4},{4,8},{8,12},{12,0},{1,5},{5,9},{9,13},{13,1},{2,6},{6,10},{... | collective-permute-start | bytes 589832 | tf_op jit(solution)/shard_map/ppermute | solution.py:342
  3.0 17.6 %collective-permute-start.2 = (f32[32,1536]{1,0:T(8,128)}, f32[32,1536]{1,0:T(8,128)S(1)}, u32[]{:S(2)}, u32[]{:S(2)}) collective-permute-start(f32[32,1536]{1,0:T(8,128)} %refs_1_.3), channel_id=1, source_target_pairs={{0,8},{4,12},{8,0},{12,4},{1,9},{5,13},{9,1},{13,5},{2,10},{6,14},... | collective-permute-start | bytes 589832 | tf_op jit(solution)/shard_map/ppermute | solution.py:342
  5.6 15.0 %collective-permute-start.3 = (f32[32,1536]{1,0:T(8,128)}, f32[32,1536]{1,0:T(8,128)S(1)}, u32[]{:S(2)}, u32[]{:S(2)}) collective-permute-start(f32[32,1536]{1,0:T(8,128)} %refs_1_.3), channel_id=1, source_target_pairs={{0,12},{4,0},{8,4},{12,8},{1,13},{5,1},{9,5},{13,9},{2,14},{6,2},{... | collective-permute-start | bytes 589832 | tf_op jit(solution)/shard_map/ppermute | solution.py:342
  8.1 12.5 %collective-permute-start = (f32[64,128]{1,0:T(8,128)S(1)}, f32[64,128]{1,0:T(8,128)S(1)}, u32[]{:S(2)}, u32[]{:S(2)}) collective-permute-start(f32[64,128]{1,0:T(8,128)S(1)} %shard_map.64.refs_1_.refs_0_), channel_id=1, source_target_pairs={{0,1},{1,0},{2,3},{3,2},{4,5},{5,4},{6,7},{7,6},{8,9},{9,8},{10,11... | collective-permute-start | bytes 98312 | tf_op jit(solution)/shard_map/ppermute | solution.py:345
  20.6 4.0 %collective-permute-start.4 = (f32[64,128]{1,0:T(8,128)S(1)}, f32[64,128]{1,0:T(8,128)S(1)}, u32[]{:S(2)}, u32[]{:S(2)}) collective-permute-start(f32[64,128]{1,0:T(8,128)S(1)} %shard_map.67.refs_2_), channel_id=1, source_target_pairs={{0,2},{1,3},{2,0},{3,1},{4,6},{5,7},{6,4},{7,5},{8,10},{9,11},{10,... | collective-permute-start | bytes 98312 | tf_op jit(solution)/shard_map/ppermute | solution.py:348
  24.8 15.5 %collective-permute-start.5 = (f32[32,1536]{1,0:T(8,128)S(1)}, f32[32,1536]{1,0:T(8,128)S(1)}, u32[]{:S(2)}, u32[]{:S(2)}) collective-permute-start(f32[32,1536]{1,0:T(8,128)S(1)} %get-tuple-element.108.refs_6_.refs_1_), channel_id=1, source_target_pairs={{0,4},{4,8},{8,12},{12,0},{1,5},{5,9},{9,13},{13,1},{2,6},{6,10},{... | collective-permute-start | bytes 589832 | tf_op jit(solution)/shard_map/ppermute | solution.py:342
  27.6 12.7 %collective-permute-start.6 = (f32[32,1536]{1,0:T(8,128)S(1)}, f32[32,1536]{1,0:T(8,128)S(1)}, u32[]{:S(2)}, u32[]{:S(2)}) collective-permute-start(f32[32,1536]{1,0:T(8,128)S(1)} %get-tuple-element.108.refs_6_.refs_1_), channel_id=1, source_target_pairs={{0,12},{4,0},{8,4},{12,8},{1,13},{5,1},{9,5},{13,9},{2,14},{6,2},{... | collective-permute-start | bytes 589832 | tf_op jit(solution)/shard_map/ppermute | solution.py:342
  42.3 17.8 %collective-permute-start.10 = (f32[32,4096]{1,0:T(8,128)S(1)}, f32[32,4096]{1,0:T(8,128)S(1)}, u32[]{:S(2)}, u32[]{:S(2)}) collective-permute-start(f32[32,4096]{1,0:T(8,128)S(1)} %add.59.refs_6_), channel_id=1, source_target_pairs={{0,2},{1,3},{2,0},{3,1},{4,6},{5,7},{6,4},{7,5},{8,10},{9,11},{10,... | collective-permute-start | bytes 1572872 | tf_op jit(solution)/shard_map/ppermute | solution.py:348
  43.8 8.5 %collective-permute-start.8 = (f32[32,1536]{1,0:T(8,128)S(1)}, f32[32,1536]{1,0:T(8,128)S(1)}, u32[]{:S(2)}, u32[]{:S(2)}) collective-permute-start(f32[32,1536]{1,0:T(8,128)S(1)} %collective-permute-done.5.refs_2_), channel_id=1, source_target_pairs={{0,4},{4,8},{8,12},{12,0},{1,5},{5,9},{9,13},{13,1},{2,6},{6,10},{... | collective-permute-start | bytes 589832 | tf_op jit(solution)/shard_map/ppermute | solution.py:342
  52.3 7.8 %collective-permute-start.9 = (f32[32,2048]{1,0:T(8,128)S(1)}, f32[32,2048]{1,0:T(8,128)S(1)}, u32[]{:S(2)}, u32[]{:S(2)}) collective-permute-start(f32[32,2048]{1,0:T(8,128)S(1)} %get-tuple-element.107), channel_id=1, source_target_pairs={{0,1},{1,0},{2,3},{3,2},{4,5},{5,4},{6,7},{7,6},{8,9},{9,8},{10,11... | collective-permute-start | bytes 786440 | tf_op jit(solution)/shard_map/ppermute | solution.py:345
  60.1 9.2 %collective-permute-start.11 = (f32[32,2048]{1,0:T(8,128)S(1)}, f32[32,2048]{1,0:T(8,128)S(1)}, u32[]{:S(2)}, u32[]{:S(2)}) collective-permute-start(f32[32,2048]{1,0:T(8,128)S(1)} %add.60.refs_1_), channel_id=1, source_target_pairs={{0,2},{1,3},{2,0},{3,1},{4,6},{5,7},{6,4},{7,5},{8,10},{9,11},{10,... | collective-permute-start | bytes 786440 | tf_op jit(solution)/shard_map/ppermute | solution.py:348
  60.8 19.6 %collective-permute-start.20 = (f32[32,4096]{1,0:T(8,128)S(1)}, f32[32,4096]{1,0:T(8,128)S(1)}, u32[]{:S(2)}, u32[]{:S(2)}) collective-permute-start(f32[32,4096]{1,0:T(8,128)S(1)} %get-tuple-element.139), channel_id=1, source_target_pairs={{0,1},{1,0},{2,3},{3,2},{4,5},{5,4},{6,7},{7,6},{8,9},{9,8},{10,11... | collective-permute-start | bytes 1572872 | tf_op jit(solution)/shard_map/ppermute | solution.py:345
  60.8 19.6 %collective-permute-start.21 = (f32[32,4096]{1,0:T(8,128)S(1)}, f32[32,4096]{1,0:T(8,128)S(1)}, u32[]{:S(2)}, u32[]{:S(2)}) collective-permute-start(f32[32,4096]{1,0:T(8,128)S(1)} %get-tuple-element.121), channel_id=1, source_target_pairs={{0,1},{1,0},{2,3},{3,2},{4,5},{5,4},{6,7},{7,6},{8,9},{9,8},{10,11... | collective-permute-start | bytes 1572872 | tf_op jit(solution)/shard_map/ppermute | solution.py:345
  61.7 18.6 %collective-permute-start.15 = (f32[32,4096]{1,0:T(8,128)S(1)}, f32[32,4096]{1,0:T(8,128)S(1)}, u32[]{:S(2)}, u32[]{:S(2)}) collective-permute-start(f32[32,4096]{1,0:T(8,128)S(1)} %add.61.refs_0_.refs_9_), channel_id=1, source_target_pairs={{0,2},{1,3},{2,0},{3,1},{4,6},{5,7},{6,4},{7,5},{8,10},{9,11},{10,... | collective-permute-start | bytes 1572872 | tf_op jit(solution)/shard_map/ppermute | solution.py:348
  73.3 6.9 %collective-permute-start.14 = (f32[32,2048]{1,0:T(8,128)S(1)}, f32[32,2048]{1,0:T(8,128)S(1)}, u32[]{:S(2)}, u32[]{:S(2)}) collective-permute-start(f32[32,2048]{1,0:T(8,128)S(1)} %get-tuple-element.130), channel_id=1, source_target_pairs={{0,1},{1,0},{2,3},{3,2},{4,5},{5,4},{6,7},{7,6},{8,9},{9,8},{10,11... | collective-permute-start | bytes 786440 | tf_op jit(solution)/shard_map/ppermute | solution.py:345
  75.0 5.2 %collective-permute-start.19 = (f32[1,6144]{1,0:T(1,128)S(1)}, f32[1,6144]{1,0:T(1,128)S(1)}, u32[]{:S(2)}, u32[]{:S(2)}) collective-permute-start(f32[1,6144]{1,0:T(1,128)S(1)} %add.63), channel_id=1, source_target_pairs={{0,2},{1,3},{2,0},{3,1},{4,6},{5,7},{6,4},{7,5},{8,10},{9,11},{10,... | collective-permute-start | bytes 73736 | tf_op jit(solution)/shard_map/ppermute | solution.py:348
  80.9 7.4 %collective-permute-start.22 = (f32[32,2048]{1,0:T(8,128)S(1)}, f32[32,2048]{1,0:T(8,128)S(1)}, u32[]{:S(2)}, u32[]{:S(2)}) collective-permute-start(f32[32,2048]{1,0:T(8,128)S(1)} %get-tuple-element.144.refs_1_), channel_id=1, source_target_pairs={{0,2},{1,3},{2,0},{3,1},{4,6},{5,7},{6,4},{7,5},{8,10},{9,11},{10,... | collective-permute-start | bytes 786440 | tf_op jit(solution)/shard_map/ppermute | solution.py:348
  81.5 7.9 %collective-permute-start.23 = (f32[32,2048]{1,0:T(8,128)S(1)}, f32[32,2048]{1,0:T(8,128)S(1)}, u32[]{:S(2)}, u32[]{:S(2)}) collective-permute-start(f32[32,2048]{1,0:T(8,128)S(1)} %get-tuple-element.144.refs_1_), channel_id=1, source_target_pairs={{0,1},{1,0},{2,3},{3,2},{4,5},{5,4},{6,7},{7,6},{8,9},{9,8},{10,11... | collective-permute-start | bytes 786440 | tf_op jit(solution)/shard_map/ppermute | solution.py:345
  88.3 2.6 %collective-permute-start.24 = (f32[32,2048]{1,0:T(8,128)S(1)}, f32[32,2048]{1,0:T(8,128)S(1)}, u32[]{:S(2)}, u32[]{:S(2)}) collective-permute-start(f32[32,2048]{1,0:T(8,128)S(1)} %collective-permute-done.22.refs_2_), channel_id=1, source_target_pairs={{0,1},{1,0},{2,3},{3,2},{4,5},{5,4},{6,7},{7,6},{8,9},{9,8},{10,11... | collective-permute-start | bytes 786440 | tf_op jit(solution)/shard_map/ppermute | solution.py:345
  88.3 7.9 %collective-permute-start.12 = (f32[32,2048]{1,0:T(8,128)S(1)}, f32[32,2048]{1,0:T(8,128)S(1)}, u32[]{:S(2)}, u32[]{:S(2)}) collective-permute-start(f32[32,2048]{1,0:T(8,128)S(1)} %get-tuple-element.124), channel_id=1, source_target_pairs={{0,1},{1,0},{2,3},{3,2},{4,5},{5,4},{6,7},{7,6},{8,9},{9,8},{10,11... | collective-permute-start | bytes 786440 | tf_op jit(solution)/shard_map/ppermute | solution.py:345
  88.8 7.4 %collective-permute-start.17 = (f32[32,2048]{1,0:T(8,128)S(1)}, f32[32,2048]{1,0:T(8,128)S(1)}, u32[]{:S(2)}, u32[]{:S(2)}) collective-permute-start(f32[32,2048]{1,0:T(8,128)S(1)} %get-tuple-element.133), channel_id=1, source_target_pairs={{0,1},{1,0},{2,3},{3,2},{4,5},{5,4},{6,7},{7,6},{8,9},{9,8},{10,11... | collective-permute-start | bytes 786440 | tf_op jit(solution)/shard_map/ppermute | solution.py:345
  88.8 9.1 %collective-permute-start.16 = (f32[32,2048]{1,0:T(8,128)S(1)}, f32[32,2048]{1,0:T(8,128)S(1)}, u32[]{:S(2)}, u32[]{:S(2)}) collective-permute-start(f32[32,2048]{1,0:T(8,128)S(1)} %add.62), channel_id=1, source_target_pairs={{0,2},{1,3},{2,0},{3,1},{4,6},{5,7},{6,4},{7,5},{8,10},{9,11},{10,... | collective-permute-start | bytes 786440 | tf_op jit(solution)/shard_map/ppermute | solution.py:348
  89.4 14.2 %collective-permute-start.26 = (f32[32,2048]{1,0:T(8,128)S(1)}, f32[32,2048]{1,0:T(8,128)S(1)}, u32[]{:S(2)}, u32[]{:S(2)}) collective-permute-start(f32[32,2048]{1,0:T(8,128)S(1)} %get-tuple-element.147.refs_1_), channel_id=1, source_target_pairs={{0,2},{1,3},{2,0},{3,1},{4,6},{5,7},{6,4},{7,5},{8,10},{9,11},{10,... | collective-permute-start | bytes 786440 | tf_op jit(solution)/shard_map/ppermute | solution.py:348
  98.9 11.6 %collective-permute-start.25 = (f32[32,2176]{1,0:T(8,128)S(1)}, f32[32,2176]{1,0:T(8,128)S(1)}, u32[]{:S(2)}, u32[]{:S(2)}) collective-permute-start(f32[32,2176]{1,0:T(8,128)S(1)} %get-tuple-element.146.refs_13_.refs_1_), channel_id=1, source_target_pairs={{0,2},{1,3},{2,0},{3,1},{4,6},{5,7},{6,4},{7,5},{8,10},{9,11},{10,... | collective-permute-start | bytes 835592 | tf_op jit(solution)/shard_map/ppermute | solution.py:348
  99.4 4.7 %collective-permute-start.27 = (f32[32,2048]{1,0:T(8,128)S(1)}, f32[32,2048]{1,0:T(8,128)S(1)}, u32[]{:S(2)}, u32[]{:S(2)}) collective-permute-start(f32[32,2048]{1,0:T(8,128)S(1)} %get-tuple-element.147.refs_1_), channel_id=1, source_target_pairs={{0,1},{1,0},{2,3},{3,2},{4,5},{5,4},{6,7},{7,6},{8,9},{9,8},{10,11... | collective-permute-start | bytes 786440 | tf_op jit(solution)/shard_map/ppermute | solution.py:345
  103.6 7.1 %collective-permute-start.29 = (f32[32,2176]{1,0:T(8,128)S(1)}, f32[32,2176]{1,0:T(8,128)S(1)}, u32[]{:S(2)}, u32[]{:S(2)}) collective-permute-start(f32[32,2176]{1,0:T(8,128)S(1)} %get-tuple-element.146.refs_13_.refs_1_), channel_id=1, source_target_pairs={{0,1},{1,0},{2,3},{3,2},{4,5},{5,4},{6,7},{7,6},{8,9},{9,8},{10,11... | collective-permute-start | bytes 835592 | tf_op jit(solution)/shard_map/ppermute | solution.py:345
  115.1 10.4 %collective-permute-start.31 = (f32[32,896]{1,0:T(8,128)S(1)}, f32[32,896]{1,0:T(8,128)S(1)}, u32[]{:S(2)}, u32[]{:S(2)}) collective-permute-start(f32[32,896]{1,0:T(8,128)S(1)} %get-tuple-element.161), channel_id=1, source_target_pairs={{0,12},{4,0},{8,4},{12,8},{1,13},{5,1},{9,5},{13,9},{2,14},{6,2},{... | collective-permute-start | bytes 344072 | tf_op jit(solution)/shard_map/ppermute | solution.py:342
  117.4 15.2 %collective-permute-start.32 = (f32[32,896]{1,0:T(8,128)S(1)}, f32[32,896]{1,0:T(8,128)S(1)}, u32[]{:S(2)}, u32[]{:S(2)}) collective-permute-start(f32[32,896]{1,0:T(8,128)S(1)} %get-tuple-element.162), channel_id=1, source_target_pairs={{0,8},{4,12},{8,0},{12,4},{1,9},{5,13},{9,1},{13,5},{2,10},{6,14},... | collective-permute-start | bytes 344072 | tf_op jit(solution)/shard_map/ppermute | solution.py:342
  117.4 15.2 %collective-permute-start.33 = (f32[32,896]{1,0:T(8,128)S(1)}, f32[32,896]{1,0:T(8,128)S(1)}, u32[]{:S(2)}, u32[]{:S(2)}) collective-permute-start(f32[32,896]{1,0:T(8,128)S(1)} %get-tuple-element.163), channel_id=1, source_target_pairs={{0,4},{4,8},{8,12},{12,0},{1,5},{5,9},{9,13},{13,1},{2,6},{6,10},{... | collective-permute-start | bytes 344072 | tf_op jit(solution)/shard_map/ppermute | solution.py:342
  121.3 11.6 %collective-permute-start.34 = (f32[32,768]{1,0:T(8,128)S(1)}, f32[32,768]{1,0:T(8,128)S(1)}, u32[]{:S(2)}, u32[]{:S(2)}) collective-permute-start(f32[32,768]{1,0:T(8,128)S(1)} %get-tuple-element.168), channel_id=1, source_target_pairs={{0,12},{4,0},{8,4},{12,8},{1,13},{5,1},{9,5},{13,9},{2,14},{6,2},{... | collective-permute-start | bytes 294920 | tf_op jit(solution)/shard_map/ppermute | solution.py:342
  124.4 11.9 %collective-permute-start.35 = (f32[32,768]{1,0:T(8,128)S(1)}, f32[32,768]{1,0:T(8,128)S(1)}, u32[]{:S(2)}, u32[]{:S(2)}) collective-permute-start(f32[32,768]{1,0:T(8,128)S(1)} %get-tuple-element.169), channel_id=1, source_target_pairs={{0,8},{4,12},{8,0},{12,4},{1,9},{5,13},{9,1},{13,5},{2,10},{6,14},... | collective-permute-start | bytes 294920 | tf_op jit(solution)/shard_map/ppermute | solution.py:342
  125.5 10.8 %collective-permute-start.36 = (f32[32,768]{1,0:T(8,128)S(1)}, f32[32,768]{1,0:T(8,128)S(1)}, u32[]{:S(2)}, u32[]{:S(2)}) collective-permute-start(f32[32,768]{1,0:T(8,128)S(1)} %get-tuple-element.170), channel_id=1, source_target_pairs={{0,4},{4,8},{8,12},{12,0},{1,5},{5,9},{9,13},{13,1},{2,6},{6,10},{... | collective-permute-start | bytes 294920 | tf_op jit(solution)/shard_map/ppermute | solution.py:342
  (10 other events, 29.7 us)

commit v19 on v18

--- a/solution.py
+++ b/solution.py
@@ -299,7 +299,8 @@
 
 
 def backward(acts, weights, place, earlier, part, parts, after):
-    slots, block, hidden = len(acts), acts[0].shape[0], sum(w.shape[1] for w in weights[::2])
+    slots, outs = len(acts), place.shape[0]
+    block, hidden = acts[0].shape[0], sum(w.shape[1] for w in weights[::2])
     riding = acts[0].shape[1] - hidden if part == 0 else 0
     depth = weights[0].shape[0] // parts
     width = divisor(depth, 256, 128)
@@ -314,12 +315,12 @@
             refs[1 : ends[0]],
             refs[ends[0] : ends[1]],
             refs[ends[1] : ends[2]],
-            refs[-3 - slots : -3],
+            refs[-3 - outs : -3],
             *refs[-3:],
         ),
-        out_shape=[out] * slots,
+        out_shape=[out] * outs,
         in_specs=[pl.BlockSpec(memory_space=pltpu.SMEM)] + [inside] * (ends[2] - 1) + [anywhere] * len(after),
-        out_specs=[inside] * slots,
+        out_specs=[inside] * outs,
         scratch_shapes=[
             pltpu.VMEM((2 * block * slots, hidden), jnp.bfloat16),
             pltpu.VMEM((block * slots, width), jnp.float32),
@@ -348,6 +349,8 @@
         return lax.ppermute(values, "emb", [(i, (i + 2) % emb_size) for i in range(emb_size)])
 
     owner = jnp.arange(emb_size, dtype=jnp.int32)
+    if hid_size == 4:
+        owner = jnp.append(owner, jnp.where(lax.axis_index("hid") == 0, 1, 3).astype(jnp.int32))
     place = ((owner % 2) ^ core) * chips + (owner // 2 - chip) % chips
 
     def gathered(values):
@@ -442,8 +445,21 @@
     def both_cores(mine):
         return mine + [other_core(block) for block in mine]
 
+    def handed_on(sums, behind):
+        if hid_size != 4:
+            return sums
+        farthest = tied(lax.ppermute(sums[4], "hid", [(0, 1), (3, 2)]), behind)[0]
+        return [sums[0], sums[1], sums[2] + farthest, sums[3]]
+
     def summed_along_hid(sums, behind=()):
-        arrivals = [along_hid(sums[step], -step) for step in range(1, hid_size)]
+        if hid_size == 4:
+            arrivals = [
+                lax.ppermute(sums[1], "hid", [(1, 0), (2, 1), (3, 2)]),
+                lax.ppermute(sums[3], "hid", [(0, 1), (1, 2), (2, 3)]),
+                along_hid(sums[2], 2),
+            ]
+        else:
+            arrivals = [along_hid(sums[step], -step) for step in range(1, hid_size)]
         return sum(tied(arrivals, behind)[0], start=sums[0])
 
     half_1 = halved(pre_1, pre_0[0])
@@ -460,6 +476,8 @@
     ends = []
     for part in range(parts):
         ends.append(backward(acts_1, in_parts[8:], place, sums, part, parts, [ends[-1][0]] if ends else []))
+    for part in range(parts):
+        ends[part] = handed_on(tied(ends[part], ends[part - 1][2])[0] if part else ends[part], ends[part + 1 :])
     first = summed_along_hid(ends[0])
     others = [summed_along_hid(end, first) for end in ends[1:]]
     width = depth // parts

time: 137 us -> 142 us (1.036)
  starting transfers between devices: 30.7 us -> 40.9 us
  waiting for transfers between devices: 37.6 us -> 31.5 us
    ppermute x0 -> x6, starting transfers between devices: none -> 14.1 us  [the longest x2 8.93 us: summed_along_hid(): lax.ppermute(sums[3], 'hid', [(0, 1), (1, 2), (2, 3)])]
    ppermute x12 -> x8, waiting for transfers between devices: 11.4 us -> 3.61 us  [along_hid(): lax.ppermute(values, 'hid', [(i, (i + steps) % hid_size) for i in range(h...]
    ppermute x12 -> x8, starting transfers between devices: 19 us -> 15.2 us  [along_hid(): lax.ppermute(values, 'hid', [(i, (i + steps) % hid_size) for i in range(h...]
    ppermute x0 -> x6, waiting for transfers between devices: none -> 1.67 us  [the longest x2 1.66 us: handed_on(): farthest = tied(lax.ppermute(sums[4], 'hid', [(0, 1), (3, 2)]), behind)[0]]
  transfers between devices with their start and end apart: 37 -> 39, of which waited for: 14 -> 14; matrix products, arithmetic and copies ran while one was open for 1% -> 1% of each run, Pallas kernels for 45% -> 43%
where the time goes in v19:
time: 142 us
  Pallas kernels  65.2 us (46%)
  starting transfers between devices  40.9 us (29%)
  waiting for transfers between devices  31.5 us (22%)
  local copies, waits for them, and re-layouts  2.04 us (1%)
    ppermute x9, waiting for transfers between devices, next_chip(): lax.ppermute(values, 'emb', [(i, (i + 2) % emb_size) for i in range(emb_s...  20.5 us
    pallas_call x2, Pallas kernels, stream(): pl.pallas_call(lambda *refs: stream_kernel(first, depth, refs[0], refs[1:...  18.3 us
    pallas_call x3, Pallas kernels, prepare(): pl.pallas_call(lambda weight_ref, gain_ref, *refs: prepare_kernel(rows, c...  17.2 us
    pallas_call x4, Pallas kernels, backward(): pl.pallas_call(lambda *refs: backward_kernel(part * depth, depth, refs[0]...  16.8 us
    ppermute x8, starting transfers between devices, along_hid(): lax.ppermute(values, 'hid', [(i, (i + steps) % hid_size) for i in range(h...  15.2 us
    pallas_call x2, Pallas kernels, forward(): pl.pallas_call(lambda *refs: forward_kernel(refs[0], refs[1:ends[0]], ref...  11.2 us
    ppermute x2, starting transfers between devices, summed_along_hid(): lax.ppermute(sums[3], 'hid', [(0, 1), (1, 2), (2, 3)])  8.93 us
    ppermute x9, starting transfers between devices, next_chip(): lax.ppermute(values, 'emb', [(i, (i + 2) % emb_size) for i in range(emb_s...  8.63 us
  transfers between devices with their start and end apart: 39, of which 14 were waited for; matrix products, arithmetic and copies ran while one was open for 1% of the time, Pallas kernels for 43%

profile of v19, /device:TPU:0, one launch (start us, length us, event | category | flops | bytes accessed | tf_op | source)
XLA Modules:
  0.0 141.5 jit_solution(13413048693172537635)
XLA Ops:
  0.0 3.0 %collective-permute-start.1 = (f32[32,1536]{1,0:T(8,128)}, f32[32,1536]{1,0:T(8,128)S(1)}, u32[]{:S(2)}, u32[]{:S(2)}) collective-permute-start(f32[32,1536]{1,0:T(8,128)} %refs_1_.3), channel_id=1, source_target_pairs={{0,4},{4,8},{8,12},{12,0},{1,5},{5,9},{9,13},{13,1},{2,6},{6,10},{... | collective-permute-start | bytes 589832 | tf_op jit(solution)/shard_map/ppermute | solution.py:343
  3.0 2.6 %collective-permute-start.2 = (f32[32,1536]{1,0:T(8,128)}, f32[32,1536]{1,0:T(8,128)S(1)}, u32[]{:S(2)}, u32[]{:S(2)}) collective-permute-start(f32[32,1536]{1,0:T(8,128)} %refs_1_.3), channel_id=1, source_target_pairs={{0,8},{4,12},{8,0},{12,4},{1,9},{5,13},{9,1},{13,5},{2,10},{6,14},... | collective-permute-start | bytes 589832 | tf_op jit(solution)/shard_map/ppermute | solution.py:343
  5.6 1.3 collective-permute-start.3
  9.2 5.7 %shard_map.65 = (bf16[1536,1024]{1,0:T(8,128)(2,1)S(1)}, bf16[1536,1024]{1,0:T(8,128)(2,1)S(1)}, bf16[1536,1024]{1,0:T(8,128)(2,1)S(1)}, bf16[1536,1024]{1,0:T(8,128)(2,1)S(1)}, f32[1,2048]{1,0:T(1,128)S(1)}) custom-call(f32[1536,6144]{1,0:T(8,128)} %weight_ref.5, f32[1536,1]{1,0:T(8,128)S(1)} %broadcast_in_dim.19.gain_ref, s32[5]{0:T(128)S(1)} %fusion.5.refs_0_, ...), custom_call_target="tpu_custom_call" | custom-call | flops 1048576 | bytes 262144 | tf_op jit(solution)/shard_map/pallas_call | solution.py:135
  14.9 5.7 %shard_map.66 = (bf16[1536,1024]{1,0:T(8,128)(2,1)S(1)}, bf16[1536,1024]{1,0:T(8,128)(2,1)S(1)}, bf16[1536,1024]{1,0:T(8,128)(2,1)S(1)}, bf16[1536,1024]{1,0:T(8,128)(2,1)S(1)}, f32[1,2048]{1,0:T(1,128)S(1)}) custom-call(f32[1536,6144]{1,0:T(8,128)} %weight_ref.5, f32[1536,1]{1,0:T(8,128)S(1)} %broadcast_in_dim.19.gain_ref, ...), custom_call_target="tpu_custom_call" | custom-call | flops 1048576 | bytes 262144 | tf_op jit(solution)/shard_map/pallas_call | solution.py:135
  20.7 1.6 %collective-permute-start.4 = (f32[64,128]{1,0:T(8,128)S(1)}, f32[64,128]{1,0:T(8,128)S(1)}, u32[]{:S(2)}, u32[]{:S(2)}) collective-permute-start(f32[64,128]{1,0:T(8,128)S(1)} %shard_map.67.refs_2_), channel_id=1, source_target_pairs={{0,2},{1,3},{2,0},{3,1},{4,6},{5,7},{6,4},{7,5},{8,10},{9,11},{10,... | collective-permute-start | bytes 98312 | tf_op jit(solution)/shard_map/ppermute | solution.py:349
  22.3 2.4 %collective-permute-done.4.refs_3_ = f32[64,128]{1,0:T(8,128)S(1)} collective-permute-done((f32[64,128]{1,0:T(8,128)S(1)}, f32[64,128]{1,0:T(8,128)S(1)}, u32[]{:S(2)}, u32[]{:S(2)}) %collective-permute-start.4) | collective-permute-done | bytes 32800 | tf_op jit(solution)/shard_map/ppermute | solution.py:349
  24.8 2.7 %collective-permute-start.5 = (f32[32,1536]{1,0:T(8,128)S(1)}, f32[32,1536]{1,0:T(8,128)S(1)}, u32[]{:S(2)}, u32[]{:S(2)}) collective-permute-start(f32[32,1536]{1,0:T(8,128)S(1)} %get-tuple-element.119.refs_6_.refs_1_), channel_id=1, source_target_pairs={{0,4},{4,8},{8,12},{12,0},{1,5},{5,9},{9,13},{13,1},{2,6},{6,10},{... | collective-permute-start | bytes 589832 | tf_op jit(solution)/shard_map/ppermute | solution.py:343
  28.7 11.5 %shard_map.69 = (f32[32,4096]{1,0:T(8,128)S(1)}, f32[32,4096]{1,0:T(8,128)S(1)}, f32[32,4096]{1,0:T(8,128)S(1)}, f32[32,4096]{1,0:T(8,128)S(1)}) custom-call(s32[5]{0:T(128)S(1)} %fusion.5.refs_0_, f32[32,1536]{1,0:T(8,128)S(1)} %copy-done.2, f32[32,1536]{1,0:T(8,128)S(1)} %collective-permute-done.1.refs_3_.refs_2_, ...), custom_call_target="tpu_custom_call" | custom-call | flops 1048576 | bytes 262144 | tf_op jit(solution)/shard_map/pallas_call | solution.py:254
  40.4 1.9 %collective-permute-done.7 = f32[32,4096]{1,0:T(8,128)S(1)} collective-permute-done((f32[32,4096]{1,0:T(8,128)S(1)}, f32[32,4096]{1,0:T(8,128)S(1)}, u32[]{:S(2)}, u32[]{:S(2)}) %collective-permute-start.7) | collective-permute-done | bytes 524320 | tf_op jit(solution)/shard_map/ppermute | solution.py:346
  42.3 1.6 %collective-permute-start.10 = (f32[32,4096]{1,0:T(8,128)S(1)}, f32[32,4096]{1,0:T(8,128)S(1)}, u32[]{:S(2)}, u32[]{:S(2)}) collective-permute-start(f32[32,4096]{1,0:T(8,128)S(1)} %add.65.refs_6_), channel_id=1, source_target_pairs={{0,2},{1,3},{2,0},{3,1},{4,6},{5,7},{6,4},{7,5},{8,10},{9,11},{10,... | collective-permute-start | bytes 1572872 | tf_op jit(solution)/shard_map/ppermute | solution.py:349
  44.7 6.8 %shard_map.70 = (f32[32,2048]{1,0:T(8,128)S(1)}, f32[32,2048]{1,0:T(8,128)S(1)}, f32[32,2048]{1,0:T(8,128)S(1)}, f32[32,2048]{1,0:T(8,128)S(1)}) custom-call(s32[5]{0:T(128)S(1)} %fusion.5.refs_0_, f32[32,1536]{1,0:T(8,128)S(1)} %copy-done.2, f32[32,1536]{1,0:T(8,128)S(1)} %collective-permute-done.1.refs_3_.refs_2_, ...), custom_call_target="tpu_custom_call" | custom-call | flops 1048576 | bytes 262144 | tf_op jit(solution)/shard_map/pallas_call | solution.py:254
  52.4 7.2 %shard_map.71 = (f32[32,4096]{1,0:T(8,128)S(1)}, f32[32,4096]{1,0:T(8,128)S(1)}, f32[32,4096]{1,0:T(8,128)S(1)}, f32[32,4096]{1,0:T(8,128)S(1)}) custom-call(s32[5]{0:T(128)S(1)} %fusion.5.refs_0_, f32[32,1536]{1,0:T(8,128)S(1)} %get-tuple-element.119.refs_6_.refs_1_, f32[32,1536]{1,0:T(8,128)S(1)} %collective-permute-done.5.refs_2_, ...), custom_call_target="tpu_custom_call" | custom-call | flops 1048576 | bytes 262144 | tf_op jit(solution)/shard_map/pallas_call | solution.py:212
  62.9 5.7 %shard_map.72 = (bf16[1536,1024]{1,0:T(8,128)(2,1)S(1)}, bf16[1536,1024]{1,0:T(8,128)(2,1)S(1)}, bf16[1536,1024]{1,0:T(8,128)(2,1)S(1)}, bf16[1536,1024]{1,0:T(8,128)(2,1)S(1)}, f32[1,2048]{1,0:T(1,128)S(1)}) custom-call(f32[1536,6144]{1,0:T(8,128)} %weight_ref.5, f32[1536,1]{1,0:T(8,128)S(1)} %broadcast_in_dim.19.gain_ref, ...), custom_call_target="tpu_custom_call" | custom-call | flops 1048576 | bytes 262144 | tf_op jit(solution)/shard_map/pallas_call | solution.py:135
  69.4 3.9 %shard_map.73 = (f32[32,2048]{1,0:T(8,128)S(1)}, f32[32,2048]{1,0:T(8,128)S(1)}, f32[32,2048]{1,0:T(8,128)S(1)}, f32[32,2048]{1,0:T(8,128)S(1)}) custom-call(s32[5]{0:T(128)S(1)} %fusion.5.refs_0_, f32[32,1536]{1,0:T(8,128)S(1)} %get-tuple-element.119.refs_6_.refs_1_, f32[32,1536]{1,0:T(8,128)S(1)} %collective-permute-done.5.refs_2_, ...), custom_call_target="tpu_custom_call" | custom-call | flops 1048576 | bytes 262144 | tf_op jit(solution)/shard_map/pallas_call | solution.py:212
  75.7 4.6 %collective-permute-done.19 = f32[1,6144]{1,0:T(1,128)S(1)} collective-permute-done((f32[1,6144]{1,0:T(1,128)S(1)}, f32[1,6144]{1,0:T(1,128)S(1)}, u32[]{:S(2)}, u32[]{:S(2)}) %collective-permute-start.19) | collective-permute-done | bytes 24608 | tf_op jit(solution)/shard_map/ppermute | solution.py:349
  81.5 6.9 %collective-permute-done.22.refs_2_ = f32[32,2048]{1,0:T(8,128)S(1)} collective-permute-done((f32[32,2048]{1,0:T(8,128)S(1)}, f32[32,2048]{1,0:T(8,128)S(1)}, u32[]{:S(2)}, u32[]{:S(2)}) %collective-permute-start.22) | collective-permute-done | bytes 262176 | tf_op jit(solution)/shard_map/ppermute | solution.py:349
  89.4 1.5 %collective-permute-start.26 = (f32[32,2048]{1,0:T(8,128)S(1)}, f32[32,2048]{1,0:T(8,128)S(1)}, u32[]{:S(2)}, u32[]{:S(2)}) collective-permute-start(f32[32,2048]{1,0:T(8,128)S(1)} %get-tuple-element.158.refs_1_), channel_id=1, source_target_pairs={{0,2},{1,3},{2,0},{3,1},{4,6},{5,7},{6,4},{7,5},{8,10},{9,11},{10,... | collective-permute-start | bytes 786440 | tf_op jit(solution)/shard_map/ppermute | solution.py:349
  90.9 5.3 %shard_map.75 = (f32[32,1536]{1,0:T(8,128)S(1)}, f32[32,1536]{1,0:T(8,128)S(1)}, f32[32,1536]{1,0:T(8,128)S(1)}, f32[32,1536]{1,0:T(8,128)S(1)}, f32[32,1536]{1,0:T(8,128)S(1)}) custom-call(s32[5]{0:T(128)S(1)} %fusion.5.refs_0_, f32[32,2048]{1,0:T(8,128)S(1)} %get-tuple-element.155.refs_1_, f32[32,2048]{1,0:T(8,128)S(1)} %collective-permute-done.22.refs_2_, ...), custom_call_target="tpu_custom_call" | custom-call | flops 1048576 | bytes 262144 | tf_op jit(solution)/shard_map/pallas_call | solution.py:310
  96.3 1.7 %collective-permute-done.16.refs_3_ = f32[32,2048]{1,0:T(8,128)S(1)} collective-permute-done((f32[32,2048]{1,0:T(8,128)S(1)}, f32[32,2048]{1,0:T(8,128)S(1)}, u32[]{:S(2)}, u32[]{:S(2)}) %collective-permute-start.16) | collective-permute-done | bytes 262176 | tf_op jit(solution)/shard_map/ppermute | solution.py:349
  99.5 4.2 %collective-permute-done.26.refs_2_ = f32[32,2048]{1,0:T(8,128)S(1)} collective-permute-done((f32[32,2048]{1,0:T(8,128)S(1)}, f32[32,2048]{1,0:T(8,128)S(1)}, u32[]{:S(2)}, u32[]{:S(2)}) %collective-permute-start.26) | collective-permute-done | bytes 262176 | tf_op jit(solution)/shard_map/ppermute | solution.py:349
  105.2 5.3 %shard_map.77 = (f32[32,1536]{1,0:T(8,128)S(1)}, f32[32,1536]{1,0:T(8,128)S(1)}, f32[32,1536]{1,0:T(8,128)S(1)}, f32[32,1536]{1,0:T(8,128)S(1)}, f32[32,1536]{1,0:T(8,128)S(1)}) custom-call(s32[5]{0:T(128)S(1)} %fusion.5.refs_0_, f32[32,2048]{1,0:T(8,128)S(1)} %get-tuple-element.158.refs_1_, f32[32,2048]{1,0:T(8,128)S(1)} %collective-permute-done.26.refs_2_, ...), custom_call_target="tpu_custom_call" | custom-call | flops 1048576 | bytes 262144 | tf_op jit(solution)/shard_map/pallas_call | solution.py:310
  110.7 1.4 %collective-permute-done.30.refs_4_ = f32[32,2176]{1,0:T(8,128)S(1)} collective-permute-done((f32[32,2176]{1,0:T(8,128)S(1)}, f32[32,2176]{1,0:T(8,128)S(1)}, u32[]{:S(2)}, u32[]{:S(2)}) %collective-permute-start.30) | collective-permute-done | bytes 278560 | tf_op jit(solution)/shard_map/ppermute | solution.py:346
  112.1 3.1 %shard_map.78 = (f32[32,896]{1,0:T(8,128)S(1)}, f32[32,896]{1,0:T(8,128)S(1)}, f32[32,896]{1,0:T(8,128)S(1)}, f32[32,896]{1,0:T(8,128)S(1)}, f32[32,896]{1,0:T(8,128)S(1)}) custom-call(s32[5]{0:T(128)S(1)} %fusion.5.refs_0_, f32[32,2176]{1,0:T(8,128)S(1)} %get-tuple-element.157.refs_14_.refs_1_, f32[32,2176]{1,0:T(8,128)S(1)} %collective-permute-done.25.refs_2_, ...), custom_call_target="tpu_custom_call" | custom-call | flops 1048576 | bytes 262144 | tf_op jit(solution)/shard_map/pallas_call | solution.py:310
  115.2 1.3 collective-permute-start.33
  116.6 1.3 collective-permute-start.31
  117.9 4.6 %collective-permute-start.32 = (f32[32,896]{1,0:T(8,128)S(1)}, f32[32,896]{1,0:T(8,128)S(1)}, u32[]{:S(2)}, u32[]{:S(2)}) collective-permute-start(f32[32,896]{1,0:T(8,128)S(1)} %get-tuple-element.176), channel_id=1, source_target_pairs={{0,4},{4,8},{8,12},{1,5},{5,9},{9,13},{2,6},{6,10},{10,14},{3,7},{... | collective-permute-start | bytes 344072 | tf_op jit(solution)/shard_map/ppermute | solution.py:458
  122.4 3.0 %shard_map.79 = (f32[32,768]{1,0:T(8,128)S(1)}, f32[32,768]{1,0:T(8,128)S(1)}, f32[32,768]{1,0:T(8,128)S(1)}, f32[32,768]{1,0:T(8,128)S(1)}, f32[32,768]{1,0:T(8,128)S(1)}) custom-call(s32[5]{0:T(128)S(1)} %fusion.5.refs_0_, f32[32,2176]{1,0:T(8,128)S(1)} %get-tuple-element.157.refs_14_.refs_1_, f32[32,2176]{1,0:T(8,128)S(1)} %collective-permute-done.25.refs_2_, ...), custom_call_target="tpu_custom_call" | custom-call | flops 1048576 | bytes 262144 | tf_op jit(solution)/shard_map/pallas_call | solution.py:310
  129.1 1.7 %collective-permute-done.37 = f32[32,768]{1,0:T(8,128)S(1)} collective-permute-done((f32[32,768]{1,0:T(8,128)S(1)}, f32[32,768]{1,0:T(8,128)S(1)}, u32[]{:S(2)}, u32[]{:S(2)}) %collective-permute-start.37) | collective-permute-done | bytes 98336 | tf_op jit(solution)/shard_map/ppermute | solution.py:451
  130.7 4.4 %collective-permute-start.36 = (f32[32,768]{1,0:T(8,128)S(1)}, f32[32,768]{1,0:T(8,128)S(1)}, u32[]{:S(2)}, u32[]{:S(2)}) collective-permute-start(f32[32,768]{1,0:T(8,128)S(1)} %get-tuple-element.190), channel_id=1, source_target_pairs={{0,4},{4,8},{8,12},{1,5},{5,9},{9,13},{2,6},{6,10},{10,14},{3,7},{... | collective-permute-start | bytes 294920 | tf_op jit(solution)/shard_map/ppermute | solution.py:458
  135.2 2.6 %collective-permute-start.38 = (f32[32,768]{1,0:T(8,128)S(1)}, f32[32,768]{1,0:T(8,128)S(1)}, u32[]{:S(2)}, u32[]{:S(2)}) collective-permute-start(f32[32,768]{1,0:T(8,128)S(1)} %add.75), channel_id=1, source_target_pairs={{0,8},{4,12},{8,0},{12,4},{1,9},{5,13},{9,1},{13,5},{2,10},{6,14},... | collective-permute-start | bytes 294920 | tf_op jit(solution)/shard_map/ppermute | solution.py:343
  138.0 2.7 %collective-permute-done.38 = f32[32,768]{1,0:T(8,128)S(1)} collective-permute-done((f32[32,768]{1,0:T(8,128)S(1)}, f32[32,768]{1,0:T(8,128)S(1)}, u32[]{:S(2)}, u32[]{:S(2)}) %collective-permute-start.38) | collective-permute-done | bytes 98336 | tf_op jit(solution)/shard_map/ppermute | solution.py:343
  (95 shorter events, 21.8 us)
Async XLA Ops:
  0.0 20.7 %collective-permute-start.1 = (f32[32,1536]{1,0:T(8,128)}, f32[32,1536]{1,0:T(8,128)S(1)}, u32[]{:S(2)}, u32[]{:S(2)}) collective-permute-start(f32[32,1536]{1,0:T(8,128)} %refs_1_.3), channel_id=1, source_target_pairs={{0,4},{4,8},{8,12},{12,0},{1,5},{5,9},{9,13},{13,1},{2,6},{6,10},{... | collective-permute-start | bytes 589832 | tf_op jit(solution)/shard_map/ppermute | solution.py:343
  3.0 17.7 %collective-permute-start.2 = (f32[32,1536]{1,0:T(8,128)}, f32[32,1536]{1,0:T(8,128)S(1)}, u32[]{:S(2)}, u32[]{:S(2)}) collective-permute-start(f32[32,1536]{1,0:T(8,128)} %refs_1_.3), channel_id=1, source_target_pairs={{0,8},{4,12},{8,0},{12,4},{1,9},{5,13},{9,1},{13,5},{2,10},{6,14},... | collective-permute-start | bytes 589832 | tf_op jit(solution)/shard_map/ppermute | solution.py:343
  5.6 15.1 %collective-permute-start.3 = (f32[32,1536]{1,0:T(8,128)}, f32[32,1536]{1,0:T(8,128)S(1)}, u32[]{:S(2)}, u32[]{:S(2)}) collective-permute-start(f32[32,1536]{1,0:T(8,128)} %refs_1_.3), channel_id=1, source_target_pairs={{0,12},{4,0},{8,4},{12,8},{1,13},{5,1},{9,5},{13,9},{2,14},{6,2},{... | collective-permute-start | bytes 589832 | tf_op jit(solution)/shard_map/ppermute | solution.py:343
  8.1 12.6 %collective-permute-start = (f32[64,128]{1,0:T(8,128)S(1)}, f32[64,128]{1,0:T(8,128)S(1)}, u32[]{:S(2)}, u32[]{:S(2)}) collective-permute-start(f32[64,128]{1,0:T(8,128)S(1)} %shard_map.64.refs_1_.refs_0_), channel_id=1, source_target_pairs={{0,1},{1,0},{2,3},{3,2},{4,5},{5,4},{6,7},{7,6},{8,9},{9,8},{10,11... | collective-permute-start | bytes 98312 | tf_op jit(solution)/shard_map/ppermute | solution.py:346
  24.8 15.4 %collective-permute-start.5 = (f32[32,1536]{1,0:T(8,128)S(1)}, f32[32,1536]{1,0:T(8,128)S(1)}, u32[]{:S(2)}, u32[]{:S(2)}) collective-permute-start(f32[32,1536]{1,0:T(8,128)S(1)} %get-tuple-element.119.refs_6_.refs_1_), channel_id=1, source_target_pairs={{0,4},{4,8},{8,12},{12,0},{1,5},{5,9},{9,13},{13,1},{2,6},{6,10},{... | collective-permute-start | bytes 589832 | tf_op jit(solution)/shard_map/ppermute | solution.py:343
  27.6 12.7 %collective-permute-start.6 = (f32[32,1536]{1,0:T(8,128)S(1)}, f32[32,1536]{1,0:T(8,128)S(1)}, u32[]{:S(2)}, u32[]{:S(2)}) collective-permute-start(f32[32,1536]{1,0:T(8,128)S(1)} %get-tuple-element.119.refs_6_.refs_1_), channel_id=1, source_target_pairs={{0,12},{4,0},{8,4},{12,8},{1,13},{5,1},{9,5},{13,9},{2,14},{6,2},{... | collective-permute-start | bytes 589832 | tf_op jit(solution)/shard_map/ppermute | solution.py:343
  42.3 17.8 %collective-permute-start.10 = (f32[32,4096]{1,0:T(8,128)S(1)}, f32[32,4096]{1,0:T(8,128)S(1)}, u32[]{:S(2)}, u32[]{:S(2)}) collective-permute-start(f32[32,4096]{1,0:T(8,128)S(1)} %add.65.refs_6_), channel_id=1, source_target_pairs={{0,2},{1,3},{2,0},{3,1},{4,6},{5,7},{6,4},{7,5},{8,10},{9,11},{10,... | collective-permute-start | bytes 1572872 | tf_op jit(solution)/shard_map/ppermute | solution.py:349
  43.9 8.5 %collective-permute-start.8 = (f32[32,1536]{1,0:T(8,128)S(1)}, f32[32,1536]{1,0:T(8,128)S(1)}, u32[]{:S(2)}, u32[]{:S(2)}) collective-permute-start(f32[32,1536]{1,0:T(8,128)S(1)} %collective-permute-done.5.refs_2_), channel_id=1, source_target_pairs={{0,4},{4,8},{8,12},{12,0},{1,5},{5,9},{9,13},{13,1},{2,6},{6,10},{... | collective-permute-start | bytes 589832 | tf_op jit(solution)/shard_map/ppermute | solution.py:343
  52.4 7.8 %collective-permute-start.9 = (f32[32,2048]{1,0:T(8,128)S(1)}, f32[32,2048]{1,0:T(8,128)S(1)}, u32[]{:S(2)}, u32[]{:S(2)}) collective-permute-start(f32[32,2048]{1,0:T(8,128)S(1)} %get-tuple-element.118), channel_id=1, source_target_pairs={{0,1},{1,0},{2,3},{3,2},{4,5},{5,4},{6,7},{7,6},{8,9},{9,8},{10,11... | collective-permute-start | bytes 786440 | tf_op jit(solution)/shard_map/ppermute | solution.py:346
  60.2 9.2 %collective-permute-start.11 = (f32[32,2048]{1,0:T(8,128)S(1)}, f32[32,2048]{1,0:T(8,128)S(1)}, u32[]{:S(2)}, u32[]{:S(2)}) collective-permute-start(f32[32,2048]{1,0:T(8,128)S(1)} %add.66.refs_1_), channel_id=1, source_target_pairs={{0,2},{1,3},{2,0},{3,1},{4,6},{5,7},{6,4},{7,5},{8,10},{9,11},{10,... | collective-permute-start | bytes 786440 | tf_op jit(solution)/shard_map/ppermute | solution.py:349
  60.8 19.6 %collective-permute-start.20 = (f32[32,4096]{1,0:T(8,128)S(1)}, f32[32,4096]{1,0:T(8,128)S(1)}, u32[]{:S(2)}, u32[]{:S(2)}) collective-permute-start(f32[32,4096]{1,0:T(8,128)S(1)} %get-tuple-element.150), channel_id=1, source_target_pairs={{0,1},{1,0},{2,3},{3,2},{4,5},{5,4},{6,7},{7,6},{8,9},{9,8},{10,11... | collective-permute-start | bytes 1572872 | tf_op jit(solution)/shard_map/ppermute | solution.py:346
  60.8 19.6 %collective-permute-start.21 = (f32[32,4096]{1,0:T(8,128)S(1)}, f32[32,4096]{1,0:T(8,128)S(1)}, u32[]{:S(2)}, u32[]{:S(2)}) collective-permute-start(f32[32,4096]{1,0:T(8,128)S(1)} %get-tuple-element.132), channel_id=1, source_target_pairs={{0,1},{1,0},{2,3},{3,2},{4,5},{5,4},{6,7},{7,6},{8,9},{9,8},{10,11... | collective-permute-start | bytes 1572872 | tf_op jit(solution)/shard_map/ppermute | solution.py:346
  61.7 18.6 %collective-permute-start.15 = (f32[32,4096]{1,0:T(8,128)S(1)}, f32[32,4096]{1,0:T(8,128)S(1)}, u32[]{:S(2)}, u32[]{:S(2)}) collective-permute-start(f32[32,4096]{1,0:T(8,128)S(1)} %add.67.refs_0_.refs_9_), channel_id=1, source_target_pairs={{0,2},{1,3},{2,0},{3,1},{4,6},{5,7},{6,4},{7,5},{8,10},{9,11},{10,... | collective-permute-start | bytes 1572872 | tf_op jit(solution)/shard_map/ppermute | solution.py:349
  73.4 6.9 %collective-permute-start.14 = (f32[32,2048]{1,0:T(8,128)S(1)}, f32[32,2048]{1,0:T(8,128)S(1)}, u32[]{:S(2)}, u32[]{:S(2)}) collective-permute-start(f32[32,2048]{1,0:T(8,128)S(1)} %get-tuple-element.141), channel_id=1, source_target_pairs={{0,1},{1,0},{2,3},{3,2},{4,5},{5,4},{6,7},{7,6},{8,9},{9,8},{10,11... | collective-permute-start | bytes 786440 | tf_op jit(solution)/shard_map/ppermute | solution.py:346
  75.0 5.2 %collective-permute-start.19 = (f32[1,6144]{1,0:T(1,128)S(1)}, f32[1,6144]{1,0:T(1,128)S(1)}, u32[]{:S(2)}, u32[]{:S(2)}) collective-permute-start(f32[1,6144]{1,0:T(1,128)S(1)} %add.69), channel_id=1, source_target_pairs={{0,2},{1,3},{2,0},{3,1},{4,6},{5,7},{6,4},{7,5},{8,10},{9,11},{10,... | collective-permute-start | bytes 73736 | tf_op jit(solution)/shard_map/ppermute | solution.py:349
  81.0 7.4 %collective-permute-start.22 = (f32[32,2048]{1,0:T(8,128)S(1)}, f32[32,2048]{1,0:T(8,128)S(1)}, u32[]{:S(2)}, u32[]{:S(2)}) collective-permute-start(f32[32,2048]{1,0:T(8,128)S(1)} %get-tuple-element.155.refs_1_), channel_id=1, source_target_pairs={{0,2},{1,3},{2,0},{3,1},{4,6},{5,7},{6,4},{7,5},{8,10},{9,11},{10,... | collective-permute-start | bytes 786440 | tf_op jit(solution)/shard_map/ppermute | solution.py:349
  81.5 7.9 %collective-permute-start.23 = (f32[32,2048]{1,0:T(8,128)S(1)}, f32[32,2048]{1,0:T(8,128)S(1)}, u32[]{:S(2)}, u32[]{:S(2)}) collective-permute-start(f32[32,2048]{1,0:T(8,128)S(1)} %get-tuple-element.155.refs_1_), channel_id=1, source_target_pairs={{0,1},{1,0},{2,3},{3,2},{4,5},{5,4},{6,7},{7,6},{8,9},{9,8},{10,11... | collective-permute-start | bytes 786440 | tf_op jit(solution)/shard_map/ppermute | solution.py:346
  88.4 7.9 %collective-permute-start.12 = (f32[32,2048]{1,0:T(8,128)S(1)}, f32[32,2048]{1,0:T(8,128)S(1)}, u32[]{:S(2)}, u32[]{:S(2)}) collective-permute-start(f32[32,2048]{1,0:T(8,128)S(1)} %get-tuple-element.135), channel_id=1, source_target_pairs={{0,1},{1,0},{2,3},{3,2},{4,5},{5,4},{6,7},{7,6},{8,9},{9,8},{10,11... | collective-permute-start | bytes 786440 | tf_op jit(solution)/shard_map/ppermute | solution.py:346
  88.9 7.4 %collective-permute-start.17 = (f32[32,2048]{1,0:T(8,128)S(1)}, f32[32,2048]{1,0:T(8,128)S(1)}, u32[]{:S(2)}, u32[]{:S(2)}) collective-permute-start(f32[32,2048]{1,0:T(8,128)S(1)} %get-tuple-element.144), channel_id=1, source_target_pairs={{0,1},{1,0},{2,3},{3,2},{4,5},{5,4},{6,7},{7,6},{8,9},{9,8},{10,11... | collective-permute-start | bytes 786440 | tf_op jit(solution)/shard_map/ppermute | solution.py:346
  88.9 9.1 %collective-permute-start.16 = (f32[32,2048]{1,0:T(8,128)S(1)}, f32[32,2048]{1,0:T(8,128)S(1)}, u32[]{:S(2)}, u32[]{:S(2)}) collective-permute-start(f32[32,2048]{1,0:T(8,128)S(1)} %add.68), channel_id=1, source_target_pairs={{0,2},{1,3},{2,0},{3,1},{4,6},{5,7},{6,4},{7,5},{8,10},{9,11},{10,... | collective-permute-start | bytes 786440 | tf_op jit(solution)/shard_map/ppermute | solution.py:349
  89.4 14.2 %collective-permute-start.26 = (f32[32,2048]{1,0:T(8,128)S(1)}, f32[32,2048]{1,0:T(8,128)S(1)}, u32[]{:S(2)}, u32[]{:S(2)}) collective-permute-start(f32[32,2048]{1,0:T(8,128)S(1)} %get-tuple-element.158.refs_1_), channel_id=1, source_target_pairs={{0,2},{1,3},{2,0},{3,1},{4,6},{5,7},{6,4},{7,5},{8,10},{9,11},{10,... | collective-permute-start | bytes 786440 | tf_op jit(solution)/shard_map/ppermute | solution.py:349
  98.9 11.6 %collective-permute-start.25 = (f32[32,2176]{1,0:T(8,128)S(1)}, f32[32,2176]{1,0:T(8,128)S(1)}, u32[]{:S(2)}, u32[]{:S(2)}) collective-permute-start(f32[32,2176]{1,0:T(8,128)S(1)} %get-tuple-element.157.refs_14_.refs_1_), channel_id=1, source_target_pairs={{0,2},{1,3},{2,0},{3,1},{4,6},{5,7},{6,4},{7,5},{8,10},{9,11},{10,... | collective-permute-start | bytes 835592 | tf_op jit(solution)/shard_map/ppermute | solution.py:349
  99.5 4.7 %collective-permute-start.27 = (f32[32,2048]{1,0:T(8,128)S(1)}, f32[32,2048]{1,0:T(8,128)S(1)}, u32[]{:S(2)}, u32[]{:S(2)}) collective-permute-start(f32[32,2048]{1,0:T(8,128)S(1)} %get-tuple-element.158.refs_1_), channel_id=1, source_target_pairs={{0,1},{1,0},{2,3},{3,2},{4,5},{5,4},{6,7},{7,6},{8,9},{9,8},{10,11... | collective-permute-start | bytes 786440 | tf_op jit(solution)/shard_map/ppermute | solution.py:346
  103.6 7.1 %collective-permute-start.29 = (f32[32,2176]{1,0:T(8,128)S(1)}, f32[32,2176]{1,0:T(8,128)S(1)}, u32[]{:S(2)}, u32[]{:S(2)}) collective-permute-start(f32[32,2176]{1,0:T(8,128)S(1)} %get-tuple-element.157.refs_14_.refs_1_), channel_id=1, source_target_pairs={{0,1},{1,0},{2,3},{3,2},{4,5},{5,4},{6,7},{7,6},{8,9},{9,8},{10,11... | collective-permute-start | bytes 835592 | tf_op jit(solution)/shard_map/ppermute | solution.py:346
  115.2 10.2 %collective-permute-start.33 = (f32[32,896]{1,0:T(8,128)S(1)}, f32[32,896]{1,0:T(8,128)S(1)}, u32[]{:S(2)}, u32[]{:S(2)}) collective-permute-start(f32[32,896]{1,0:T(8,128)S(1)} %get-tuple-element.178), channel_id=1, source_target_pairs={{0,4},{12,8},{1,5},{13,9},{2,6},{14,10},{3,7},{15,11},{16,20},{28,... | collective-permute-start | bytes 344072 | tf_op jit(solution)/shard_map/ppermute | solution.py:451
  116.6 18.6 %collective-permute-start.31 = (f32[32,896]{1,0:T(8,128)S(1)}, f32[32,896]{1,0:T(8,128)S(1)}, u32[]{:S(2)}, u32[]{:S(2)}) collective-permute-start(f32[32,896]{1,0:T(8,128)S(1)} %get-tuple-element.175), channel_id=1, source_target_pairs={{4,0},{8,4},{12,8},{5,1},{9,5},{13,9},{6,2},{10,6},{14,10},{7,3},{... | collective-permute-start | bytes 344072 | tf_op jit(solution)/shard_map/ppermute | solution.py:457
  117.9 19.9 %collective-permute-start.32 = (f32[32,896]{1,0:T(8,128)S(1)}, f32[32,896]{1,0:T(8,128)S(1)}, u32[]{:S(2)}, u32[]{:S(2)}) collective-permute-start(f32[32,896]{1,0:T(8,128)S(1)} %get-tuple-element.176), channel_id=1, source_target_pairs={{0,4},{4,8},{8,12},{1,5},{5,9},{9,13},{2,6},{6,10},{10,14},{3,7},{... | collective-permute-start | bytes 344072 | tf_op jit(solution)/shard_map/ppermute | solution.py:458
  125.5 12.3 %collective-permute-start.34 = (f32[32,896]{1,0:T(8,128)S(1)}, f32[32,896]{1,0:T(8,128)S(1)}, u32[]{:S(2)}, u32[]{:S(2)}) collective-permute-start(f32[32,896]{1,0:T(8,128)S(1)} %add.71), channel_id=1, source_target_pairs={{0,8},{4,12},{8,0},{12,4},{1,9},{5,13},{9,1},{13,5},{2,10},{6,14},... | collective-permute-start | bytes 344072 | tf_op jit(solution)/shard_map/ppermute | solution.py:343
  126.4 4.4 %collective-permute-start.37 = (f32[32,768]{1,0:T(8,128)S(1)}, f32[32,768]{1,0:T(8,128)S(1)}, u32[]{:S(2)}, u32[]{:S(2)}) collective-permute-start(f32[32,768]{1,0:T(8,128)S(1)} %get-tuple-element.192), channel_id=1, source_target_pairs={{0,4},{12,8},{1,5},{13,9},{2,6},{14,10},{3,7},{15,11},{16,20},{28,... | collective-permute-start | bytes 294920 | tf_op jit(solution)/shard_map/ppermute | solution.py:451
  127.8 10.2 %collective-permute-start.35 = (f32[32,768]{1,0:T(8,128)S(1)}, f32[32,768]{1,0:T(8,128)S(1)}, u32[]{:S(2)}, u32[]{:S(2)}) collective-permute-start(f32[32,768]{1,0:T(8,128)S(1)} %get-tuple-element.189), channel_id=1, source_target_pairs={{4,0},{8,4},{12,8},{5,1},{9,5},{13,9},{6,2},{10,6},{14,10},{7,3},{... | collective-permute-start | bytes 294920 | tf_op jit(solution)/shard_map/ppermute | solution.py:457
  130.7 7.3 %collective-permute-start.36 = (f32[32,768]{1,0:T(8,128)S(1)}, f32[32,768]{1,0:T(8,128)S(1)}, u32[]{:S(2)}, u32[]{:S(2)}) collective-permute-start(f32[32,768]{1,0:T(8,128)S(1)} %get-tuple-element.190), channel_id=1, source_target_pairs={{0,4},{4,8},{8,12},{1,5},{5,9},{9,13},{2,6},{6,10},{10,14},{3,7},{... | collective-permute-start | bytes 294920 | tf_op jit(solution)/shard_map/ppermute | solution.py:458
  135.2 5.6 %collective-permute-start.38 = (f32[32,768]{1,0:T(8,128)S(1)}, f32[32,768]{1,0:T(8,128)S(1)}, u32[]{:S(2)}, u32[]{:S(2)}) collective-permute-start(f32[32,768]{1,0:T(8,128)S(1)} %add.75), channel_id=1, source_target_pairs={{0,8},{4,12},{8,0},{12,4},{1,9},{5,13},{9,1},{13,5},{2,10},{6,14},... | collective-permute-start | bytes 294920 | tf_op jit(solution)/shard_map/ppermute | solution.py:343
  (12 other events, 36.2 us)

commit v20 on v18

--- a/solution.py
+++ b/solution.py
@@ -75,23 +75,27 @@
     inv_std_ref[...] = inv_std
 
 
-def slope_kernel(terms, earlier, *refs):
-    back_refs, pre_refs, (bias_ref, weight_ref) = refs[:terms], refs[terms : 2 * terms], refs[2 * terms : 2 * terms + 2]
-    sums_refs, act_refs = refs[2 * terms + 2 : 2 * terms + 2 + earlier], refs[2 * terms + 2 + earlier : -1]
-    out_sums_ref = refs[-1]
+def slope_kernel(terms, outs, *refs):
+    back_refs, pre_refs, bias_ref = refs[:terms], refs[terms : 2 * terms], refs[2 * terms]
+    others, act_refs, sums_ref = refs[2 * terms + 1 : -1 - outs], refs[-1 - outs : -1], refs[-1]
     hidden = bias_ref.shape[1]
+    width = hidden // outs
     product = sum(ref[...] for ref in pre_refs)
     act = sum(ref[...] for ref in back_refs) * gelu_slope(product + bias_ref[...])
-    width = hidden // len(act_refs)
     for n, act_ref in enumerate(act_refs):
         act_ref[:, :width] = act[:, n * width : (n + 1) * width]
-    lane = lax.broadcasted_iota(jnp.int32, out_sums_ref.shape, 1)
-    first = jnp.sum(act * weight_ref[...], axis=1, keepdims=True)
-    second = jnp.sum(act * product, axis=1, keepdims=True)
-    sums = jnp.where(lane == 0, first, jnp.where(lane == 1, second, 0.0)) + sum(ref[...] for ref in sums_refs)
-    out_sums_ref[...] = sums
-    if act_refs[-1].shape[1] > width:
+    lane = lax.broadcasted_iota(jnp.int32, sums_ref.shape, 1)
+    sums = jnp.where(lane == 1, jnp.sum(act * product, axis=1, keepdims=True), 0.0)
+    if others:
+        weight_ref, earlier_sums_ref, *earlier_refs = others
+        first, column = 0.0, 0
+        for piece in (*[ref[...] for ref in earlier_refs], act):
+            end = column + piece.shape[1]
+            first = first + jnp.sum(piece * weight_ref[:, column:end], axis=1, keepdims=True)
+            column = end
+        sums = sums + earlier_sums_ref[...] + jnp.where(lane == 0, first, 0.0)
         act_refs[-1][:, width:] = sums
+    sums_ref[...] = sums
 
 
 def prepare_kernel(rows, columns, block, depth, weight_ref, gain_ref, *refs):
@@ -421,13 +425,13 @@
         passing = next_chip(passing)
         gain_sums = gain_sums + passing
 
-    def slope_product(span, back, pre, sums, after):
-        pieces, room = (span.stop - span.start) // third, 128 * len(sums)
-        widths = [third] * (pieces - 1) + [third + room, 128]
+    def slope_product(span, back, pre, others, after):
+        pieces = (span.stop - span.start) // third
+        widths = [third] * (pieces - 1) + [third + 128 * bool(others), 128]
         return call(
-            functools.partial(slope_kernel, len(back), len(sums)),
+            functools.partial(slope_kernel, len(back), pieces),
             tuple(jax.ShapeDtypeStruct((tokens, n), jnp.float32) for n in widths),
-            (*back, *pre, in_bias[None, span], gain_sums[:, span], *sums),
+            (*back, *pre, in_bias[None, span], *others),
             after,
         )
 
@@ -451,7 +455,9 @@
     act_0, act_1, sums_0 = slope_product(slice(0, 2 * third), back_0, pre_0, (), ())
     pre_1 = exchanged(half_1)
     sums = backward(both_cores(spread_out(act_0)), in_parts[:4], place, (), 0, 1, [])
-    act_2, _ = slope_product(slice(2 * third, hidden), back_1, pre_1, (sums_0,), (sums[0],))
+    act_2, _ = slope_product(
+        slice(2 * third, hidden), back_1, pre_1, (gain_sums, sums_0, act_0, act_1), (sums[0],)
+    )
     acts_0, acts_1 = spread_out(act_1), spread_out(act_2)
     sums = backward(both_cores(acts_0), in_parts[4:8], place, sums, 0, 1, [act_2])
     acts_1[1:], sums = tied(acts_1[1:], sums)

time: 137 us -> 137 us (level)
  starting transfers between devices: 30.7 us -> 32.5 us
  waiting for transfers between devices: 37.6 us -> 35.9 us
    ppermute x9, waiting for transfers between devices: 20.5 us -> 18 us  [next_chip(): lax.ppermute(values, 'emb', [(i, (i + 2) % emb_size) for i in range(emb_s...]
    ppermute x16, waiting for transfers between devices: 5.7 us -> 7.45 us  [other_core(): return lax.ppermute(values, 'emb', [(i, i ^ 1) for i in range(emb_size)])]
where the time goes in v20:
time: 137 us
  Pallas kernels  65.1 us (48%)
  waiting for transfers between devices  35.9 us (26%)
  starting transfers between devices  32.5 us (24%)
  local copies, waits for them, and re-layouts  2.03 us (1%)
    ppermute x12, starting transfers between devices, along_hid(): lax.ppermute(values, 'hid', [(i, (i + steps) % hid_size) for i in range(h...  19.6 us
    pallas_call x2, Pallas kernels, stream(): pl.pallas_call(lambda *refs: stream_kernel(first, depth, refs[0], refs[1:...  18.3 us
    ppermute x9, waiting for transfers between devices, next_chip(): lax.ppermute(values, 'emb', [(i, (i + 2) % emb_size) for i in range(emb_s...  18 us
    pallas_call x3, Pallas kernels, prepare(): pl.pallas_call(lambda weight_ref, gain_ref, *refs: prepare_kernel(rows, c...  17.2 us
    pallas_call x4, Pallas kernels, backward(): pl.pallas_call(lambda *refs: backward_kernel(part * depth, depth, refs[0]...  16.7 us
    pallas_call x2, Pallas kernels, forward(): pl.pallas_call(lambda *refs: forward_kernel(refs[0], refs[1:ends[0]], ref...  11.2 us
    ppermute x12, waiting for transfers between devices, along_hid(): lax.ppermute(values, 'hid', [(i, (i + steps) % hid_size) for i in range(h...  10.5 us
    ppermute x9, starting transfers between devices, next_chip(): lax.ppermute(values, 'emb', [(i, (i + 2) % emb_size) for i in range(emb_s...  9.93 us
  transfers between devices with their start and end apart: 37, of which 14 were waited for; matrix products, arithmetic and copies ran while one was open for 1% of the time, Pallas kernels for 45%

profile of v20, /device:TPU:0, one launch (start us, length us, event | category | flops | bytes accessed | tf_op | source)
XLA Modules:
  0.0 137.3 jit_solution(3942397512817924599)
XLA Ops:
  0.0 3.0 %collective-permute-start.1 = (f32[32,1536]{1,0:T(8,128)}, f32[32,1536]{1,0:T(8,128)S(1)}, u32[]{:S(2)}, u32[]{:S(2)}) collective-permute-start(f32[32,1536]{1,0:T(8,128)} %refs_1_.3), channel_id=1, source_target_pairs={{0,4},{4,8},{8,12},{12,0},{1,5},{5,9},{9,13},{13,1},{2,6},{6,10},{... | collective-permute-start | bytes 589832 | tf_op jit(solution)/shard_map/ppermute | solution.py:346
  3.0 2.6 %collective-permute-start.2 = (f32[32,1536]{1,0:T(8,128)}, f32[32,1536]{1,0:T(8,128)S(1)}, u32[]{:S(2)}, u32[]{:S(2)}) collective-permute-start(f32[32,1536]{1,0:T(8,128)} %refs_1_.3), channel_id=1, source_target_pairs={{0,8},{4,12},{8,0},{12,4},{1,9},{5,13},{9,1},{13,5},{2,10},{6,14},... | collective-permute-start | bytes 589832 | tf_op jit(solution)/shard_map/ppermute | solution.py:346
  5.6 1.3 collective-permute-start.3
  9.1 5.7 %shard_map.65 = (bf16[1536,1024]{1,0:T(8,128)(2,1)S(1)}, bf16[1536,1024]{1,0:T(8,128)(2,1)S(1)}, bf16[1536,1024]{1,0:T(8,128)(2,1)S(1)}, bf16[1536,1024]{1,0:T(8,128)(2,1)S(1)}, f32[1,2048]{1,0:T(1,128)S(1)}) custom-call(f32[1536,6144]{1,0:T(8,128)} %weight_ref.5, f32[1536,1]{1,0:T(8,128)S(1)} %broadcast_in_dim.19.gain_ref, s32[4]{0:T(128)S(1)} %fusion.5.refs_0_, ...), custom_call_target="tpu_custom_call" | custom-call | flops 1048576 | bytes 262144 | tf_op jit(solution)/shard_map/pallas_call | solution.py:139
  14.8 5.7 %shard_map.66 = (bf16[1536,1024]{1,0:T(8,128)(2,1)S(1)}, bf16[1536,1024]{1,0:T(8,128)(2,1)S(1)}, bf16[1536,1024]{1,0:T(8,128)(2,1)S(1)}, bf16[1536,1024]{1,0:T(8,128)(2,1)S(1)}, f32[1,2048]{1,0:T(1,128)S(1)}) custom-call(f32[1536,6144]{1,0:T(8,128)} %weight_ref.5, f32[1536,1]{1,0:T(8,128)S(1)} %broadcast_in_dim.19.gain_ref, ...), custom_call_target="tpu_custom_call" | custom-call | flops 1048576 | bytes 262144 | tf_op jit(solution)/shard_map/pallas_call | solution.py:139
  20.6 1.6 %collective-permute-start.4 = (f32[64,128]{1,0:T(8,128)S(1)}, f32[64,128]{1,0:T(8,128)S(1)}, u32[]{:S(2)}, u32[]{:S(2)}) collective-permute-start(f32[64,128]{1,0:T(8,128)S(1)} %shard_map.67.refs_2_), channel_id=1, source_target_pairs={{0,2},{1,3},{2,0},{3,1},{4,6},{5,7},{6,4},{7,5},{8,10},{9,11},{10,... | collective-permute-start | bytes 98312 | tf_op jit(solution)/shard_map/ppermute | solution.py:352
  22.2 2.4 %collective-permute-done.4.refs_3_ = f32[64,128]{1,0:T(8,128)S(1)} collective-permute-done((f32[64,128]{1,0:T(8,128)S(1)}, f32[64,128]{1,0:T(8,128)S(1)}, u32[]{:S(2)}, u32[]{:S(2)}) %collective-permute-start.4) | collective-permute-done | bytes 32800 | tf_op jit(solution)/shard_map/ppermute | solution.py:352
  24.8 2.8 %collective-permute-start.5 = (f32[32,1536]{1,0:T(8,128)S(1)}, f32[32,1536]{1,0:T(8,128)S(1)}, u32[]{:S(2)}, u32[]{:S(2)}) collective-permute-start(f32[32,1536]{1,0:T(8,128)S(1)} %get-tuple-element.108.refs_6_.refs_1_), channel_id=1, source_target_pairs={{0,4},{4,8},{8,12},{12,0},{1,5},{5,9},{9,13},{13,1},{2,6},{6,10},{... | collective-permute-start | bytes 589832 | tf_op jit(solution)/shard_map/ppermute | solution.py:346
  28.7 11.5 %shard_map.69 = (f32[32,4096]{1,0:T(8,128)S(1)}, f32[32,4096]{1,0:T(8,128)S(1)}, f32[32,4096]{1,0:T(8,128)S(1)}, f32[32,4096]{1,0:T(8,128)S(1)}) custom-call(s32[4]{0:T(128)S(1)} %fusion.5.refs_0_, f32[32,1536]{1,0:T(8,128)S(1)} %copy-done.2, f32[32,1536]{1,0:T(8,128)S(1)} %collective-permute-done.1.refs_3_.refs_2_, ...), custom_call_target="tpu_custom_call" | custom-call | flops 1048576 | bytes 262144 | tf_op jit(solution)/shard_map/pallas_call | solution.py:258
  42.3 1.6 %collective-permute-start.10 = (f32[32,4096]{1,0:T(8,128)S(1)}, f32[32,4096]{1,0:T(8,128)S(1)}, u32[]{:S(2)}, u32[]{:S(2)}) collective-permute-start(f32[32,4096]{1,0:T(8,128)S(1)} %add.59.refs_6_), channel_id=1, source_target_pairs={{0,2},{1,3},{2,0},{3,1},{4,6},{5,7},{6,4},{7,5},{8,10},{9,11},{10,... | collective-permute-start | bytes 1572872 | tf_op jit(solution)/shard_map/ppermute | solution.py:352
  43.8 6.8 %shard_map.70 = (f32[32,2048]{1,0:T(8,128)S(1)}, f32[32,2048]{1,0:T(8,128)S(1)}, f32[32,2048]{1,0:T(8,128)S(1)}, f32[32,2048]{1,0:T(8,128)S(1)}) custom-call(s32[4]{0:T(128)S(1)} %fusion.5.refs_0_, f32[32,1536]{1,0:T(8,128)S(1)} %copy-done.2, f32[32,1536]{1,0:T(8,128)S(1)} %collective-permute-done.1.refs_3_.refs_2_, ...), custom_call_target="tpu_custom_call" | custom-call | flops 1048576 | bytes 262144 | tf_op jit(solution)/shard_map/pallas_call | solution.py:258
  50.6 7.2 %shard_map.71 = (f32[32,4096]{1,0:T(8,128)S(1)}, f32[32,4096]{1,0:T(8,128)S(1)}, f32[32,4096]{1,0:T(8,128)S(1)}, f32[32,4096]{1,0:T(8,128)S(1)}) custom-call(s32[4]{0:T(128)S(1)} %fusion.5.refs_0_, f32[32,1536]{1,0:T(8,128)S(1)} %get-tuple-element.108.refs_6_.refs_1_, f32[32,1536]{1,0:T(8,128)S(1)} %collective-permute-done.5.refs_2_, ...), custom_call_target="tpu_custom_call" | custom-call | flops 1048576 | bytes 262144 | tf_op jit(solution)/shard_map/pallas_call | solution.py:216
  58.4 1.8 %collective-permute-done.9 = f32[32,2048]{1,0:T(8,128)S(1)} collective-permute-done((f32[32,2048]{1,0:T(8,128)S(1)}, f32[32,2048]{1,0:T(8,128)S(1)}, u32[]{:S(2)}, u32[]{:S(2)}) %collective-permute-start.9) | collective-permute-done | bytes 262176 | tf_op jit(solution)/shard_map/ppermute | solution.py:349
  60.9 1.6 %collective-permute-start.15 = (f32[32,4096]{1,0:T(8,128)S(1)}, f32[32,4096]{1,0:T(8,128)S(1)}, u32[]{:S(2)}, u32[]{:S(2)}) collective-permute-start(f32[32,4096]{1,0:T(8,128)S(1)} %add.61.refs_0_.refs_9_), channel_id=1, source_target_pairs={{0,2},{1,3},{2,0},{3,1},{4,6},{5,7},{6,4},{7,5},{8,10},{9,11},{10,... | collective-permute-start | bytes 1572872 | tf_op jit(solution)/shard_map/ppermute | solution.py:352
  63.0 5.7 %shard_map.72 = (bf16[1536,1024]{1,0:T(8,128)(2,1)S(1)}, bf16[1536,1024]{1,0:T(8,128)(2,1)S(1)}, bf16[1536,1024]{1,0:T(8,128)(2,1)S(1)}, bf16[1536,1024]{1,0:T(8,128)(2,1)S(1)}, f32[1,2048]{1,0:T(1,128)S(1)}) custom-call(f32[1536,6144]{1,0:T(8,128)} %weight_ref.5, f32[1536,1]{1,0:T(8,128)S(1)} %broadcast_in_dim.19.gain_ref, ...), custom_call_target="tpu_custom_call" | custom-call | flops 1048576 | bytes 262144 | tf_op jit(solution)/shard_map/pallas_call | solution.py:139
  69.5 3.9 %shard_map.73 = (f32[32,2048]{1,0:T(8,128)S(1)}, f32[32,2048]{1,0:T(8,128)S(1)}, f32[32,2048]{1,0:T(8,128)S(1)}, f32[32,2048]{1,0:T(8,128)S(1)}) custom-call(s32[4]{0:T(128)S(1)} %fusion.5.refs_0_, f32[32,1536]{1,0:T(8,128)S(1)} %get-tuple-element.108.refs_6_.refs_1_, f32[32,1536]{1,0:T(8,128)S(1)} %collective-permute-done.5.refs_2_, ...), custom_call_target="tpu_custom_call" | custom-call | flops 1048576 | bytes 262144 | tf_op jit(solution)/shard_map/pallas_call | solution.py:216
  73.5 1.5 %collective-permute-done.14 = f32[32,2048]{1,0:T(8,128)S(1)} collective-permute-done((f32[32,2048]{1,0:T(8,128)S(1)}, f32[32,2048]{1,0:T(8,128)S(1)}, u32[]{:S(2)}, u32[]{:S(2)}) %collective-permute-start.14) | collective-permute-done | bytes 262176 | tf_op jit(solution)/shard_map/ppermute | solution.py:349
  75.0 4.9 %collective-permute-done.15.refs_3_ = f32[32,4096]{1,0:T(8,128)S(1)} collective-permute-done((f32[32,4096]{1,0:T(8,128)S(1)}, f32[32,4096]{1,0:T(8,128)S(1)}, u32[]{:S(2)}, u32[]{:S(2)}) %collective-permute-start.15) | collective-permute-done | bytes 524320 | tf_op jit(solution)/shard_map/ppermute | solution.py:352
  82.6 1.6 %collective-permute-start.19 = (f32[1,6144]{1,0:T(1,128)S(1)}, f32[1,6144]{1,0:T(1,128)S(1)}, u32[]{:S(2)}, u32[]{:S(2)}) collective-permute-start(f32[1,6144]{1,0:T(1,128)S(1)} %add.63), channel_id=1, source_target_pairs={{0,2},{1,3},{2,0},{3,1},{4,6},{5,7},{6,4},{7,5},{8,10},{9,11},{10,... | collective-permute-start | bytes 73736 | tf_op jit(solution)/shard_map/ppermute | solution.py:352
  84.2 4.1 %collective-permute-done.22.refs_2_ = f32[32,2048]{1,0:T(8,128)S(1)} collective-permute-done((f32[32,2048]{1,0:T(8,128)S(1)}, f32[32,2048]{1,0:T(8,128)S(1)}, u32[]{:S(2)}, u32[]{:S(2)}) %collective-permute-start.22) | collective-permute-done | bytes 262176 | tf_op jit(solution)/shard_map/ppermute | solution.py:352
  89.3 1.5 %collective-permute-start.26 = (f32[32,2048]{1,0:T(8,128)S(1)}, f32[32,2048]{1,0:T(8,128)S(1)}, u32[]{:S(2)}, u32[]{:S(2)}) collective-permute-start(f32[32,2048]{1,0:T(8,128)S(1)} %get-tuple-element.145.refs_10_.refs_1_), channel_id=1, source_target_pairs={{0,2},{1,3},{2,0},{3,1},{4,6},{5,7},{6,4},{7,5},{8,10},{9,11},{10,... | collective-permute-start | bytes 786440 | tf_op jit(solution)/shard_map/ppermute | solution.py:352
  90.9 5.3 %shard_map.75 = (f32[32,1536]{1,0:T(8,128)S(1)}, f32[32,1536]{1,0:T(8,128)S(1)}, f32[32,1536]{1,0:T(8,128)S(1)}, f32[32,1536]{1,0:T(8,128)S(1)}) custom-call(s32[4]{0:T(128)S(1)} %fusion.5.refs_0_, f32[32,2048]{1,0:T(8,128)S(1)} %get-tuple-element.144.refs_1_.refs_9_, f32[32,2048]{1,0:T(8,128)S(1)} %collective-permute-done.22.refs_2_, ...), custom_call_target="tpu_custom_call" | custom-call | flops 1048576 | bytes 262144 | tf_op jit(solution)/shard_map/pallas_call | solution.py:313
  96.2 1.7 %collective-permute-done.16.refs_3_ = f32[32,2048]{1,0:T(8,128)S(1)} collective-permute-done((f32[32,2048]{1,0:T(8,128)S(1)}, f32[32,2048]{1,0:T(8,128)S(1)}, u32[]{:S(2)}, u32[]{:S(2)}) %collective-permute-start.16) | collective-permute-done | bytes 262176 | tf_op jit(solution)/shard_map/ppermute | solution.py:352
  99.4 4.1 %collective-permute-done.26.refs_2_ = f32[32,2048]{1,0:T(8,128)S(1)} collective-permute-done((f32[32,2048]{1,0:T(8,128)S(1)}, f32[32,2048]{1,0:T(8,128)S(1)}, u32[]{:S(2)}, u32[]{:S(2)}) %collective-permute-start.26) | collective-permute-done | bytes 262176 | tf_op jit(solution)/shard_map/ppermute | solution.py:352
  105.0 5.3 %shard_map.77 = (f32[32,1536]{1,0:T(8,128)S(1)}, f32[32,1536]{1,0:T(8,128)S(1)}, f32[32,1536]{1,0:T(8,128)S(1)}, f32[32,1536]{1,0:T(8,128)S(1)}) custom-call(s32[4]{0:T(128)S(1)} %fusion.5.refs_0_, f32[32,2048]{1,0:T(8,128)S(1)} %get-tuple-element.145.refs_10_.refs_1_, f32[32,2048]{1,0:T(8,128)S(1)} %collective-permute-done.26.refs_2_, ...), custom_call_target="tpu_custom_call" | custom-call | flops 1048576 | bytes 262144 | tf_op jit(solution)/shard_map/pallas_call | solution.py:313
  110.6 1.4 %collective-permute-done.30.refs_4_ = f32[32,2176]{1,0:T(8,128)S(1)} collective-permute-done((f32[32,2176]{1,0:T(8,128)S(1)}, f32[32,2176]{1,0:T(8,128)S(1)}, u32[]{:S(2)}, u32[]{:S(2)}) %collective-permute-start.30) | collective-permute-done | bytes 278560 | tf_op jit(solution)/shard_map/ppermute | solution.py:349
  112.0 3.1 %shard_map.78 = (f32[32,896]{1,0:T(8,128)S(1)}, f32[32,896]{1,0:T(8,128)S(1)}, f32[32,896]{1,0:T(8,128)S(1)}, f32[32,896]{1,0:T(8,128)S(1)}) custom-call(s32[4]{0:T(128)S(1)} %fusion.5.refs_0_, f32[32,2176]{1,0:T(8,128)S(1)} %get-tuple-element.147.refs_13_.refs_1_, f32[32,2176]{1,0:T(8,128)S(1)} %collective-permute-done.25.refs_2_, ...), custom_call_target="tpu_custom_call" | custom-call | flops 1048576 | bytes 262144 | tf_op jit(solution)/shard_map/pallas_call | solution.py:313
  115.1 2.2 %collective-permute-start.31 = (f32[32,896]{1,0:T(8,128)S(1)}, f32[32,896]{1,0:T(8,128)S(1)}, u32[]{:S(2)}, u32[]{:S(2)}) collective-permute-start(f32[32,896]{1,0:T(8,128)S(1)} %get-tuple-element.161), channel_id=1, source_target_pairs={{0,12},{4,0},{8,4},{12,8},{1,13},{5,1},{9,5},{13,9},{2,14},{6,2},{... | collective-permute-start | bytes 344072 | tf_op jit(solution)/shard_map/ppermute | solution.py:346
  118.1 3.0 %shard_map.79 = (f32[32,768]{1,0:T(8,128)S(1)}, f32[32,768]{1,0:T(8,128)S(1)}, f32[32,768]{1,0:T(8,128)S(1)}, f32[32,768]{1,0:T(8,128)S(1)}) custom-call(s32[4]{0:T(128)S(1)} %fusion.5.refs_0_, f32[32,2176]{1,0:T(8,128)S(1)} %get-tuple-element.147.refs_13_.refs_1_, f32[32,2176]{1,0:T(8,128)S(1)} %collective-permute-done.25.refs_2_, ...), custom_call_target="tpu_custom_call" | custom-call | flops 1048576 | bytes 262144 | tf_op jit(solution)/shard_map/pallas_call | solution.py:313
  121.1 3.3 %collective-permute-start.34 = (f32[32,768]{1,0:T(8,128)S(1)}, f32[32,768]{1,0:T(8,128)S(1)}, u32[]{:S(2)}, u32[]{:S(2)}) collective-permute-start(f32[32,768]{1,0:T(8,128)S(1)} %get-tuple-element.168), channel_id=1, source_target_pairs={{0,12},{4,0},{8,4},{12,8},{1,13},{5,1},{9,5},{13,9},{2,14},{6,2},{... | collective-permute-start | bytes 294920 | tf_op jit(solution)/shard_map/ppermute | solution.py:346
  125.8 6.7 %collective-permute-done.32 = f32[32,896]{1,0:T(8,128)S(1)} collective-permute-done((f32[32,896]{1,0:T(8,128)S(1)}, f32[32,896]{1,0:T(8,128)S(1)}, u32[]{:S(2)}, u32[]{:S(2)}) %collective-permute-start.32) | collective-permute-done | bytes 114720 | tf_op jit(solution)/shard_map/ppermute | solution.py:346
  132.7 3.8 %collective-permute-done.35 = f32[32,768]{1,0:T(8,128)S(1)} collective-permute-done((f32[32,768]{1,0:T(8,128)S(1)}, f32[32,768]{1,0:T(8,128)S(1)}, u32[]{:S(2)}, u32[]{:S(2)}) %collective-permute-start.35) | collective-permute-done | bytes 98336 | tf_op jit(solution)/shard_map/ppermute | solution.py:346
  (86 shorter events, 18.1 us)
Async XLA Ops:
  0.0 20.6 %collective-permute-start.1 = (f32[32,1536]{1,0:T(8,128)}, f32[32,1536]{1,0:T(8,128)S(1)}, u32[]{:S(2)}, u32[]{:S(2)}) collective-permute-start(f32[32,1536]{1,0:T(8,128)} %refs_1_.3), channel_id=1, source_target_pairs={{0,4},{4,8},{8,12},{12,0},{1,5},{5,9},{9,13},{13,1},{2,6},{6,10},{... | collective-permute-start | bytes 589832 | tf_op jit(solution)/shard_map/ppermute | solution.py:346
  3.0 17.6 %collective-permute-start.2 = (f32[32,1536]{1,0:T(8,128)}, f32[32,1536]{1,0:T(8,128)S(1)}, u32[]{:S(2)}, u32[]{:S(2)}) collective-permute-start(f32[32,1536]{1,0:T(8,128)} %refs_1_.3), channel_id=1, source_target_pairs={{0,8},{4,12},{8,0},{12,4},{1,9},{5,13},{9,1},{13,5},{2,10},{6,14},... | collective-permute-start | bytes 589832 | tf_op jit(solution)/shard_map/ppermute | solution.py:346
  5.6 15.0 %collective-permute-start.3 = (f32[32,1536]{1,0:T(8,128)}, f32[32,1536]{1,0:T(8,128)S(1)}, u32[]{:S(2)}, u32[]{:S(2)}) collective-permute-start(f32[32,1536]{1,0:T(8,128)} %refs_1_.3), channel_id=1, source_target_pairs={{0,12},{4,0},{8,4},{12,8},{1,13},{5,1},{9,5},{13,9},{2,14},{6,2},{... | collective-permute-start | bytes 589832 | tf_op jit(solution)/shard_map/ppermute | solution.py:346
  8.1 12.5 %collective-permute-start = (f32[64,128]{1,0:T(8,128)S(1)}, f32[64,128]{1,0:T(8,128)S(1)}, u32[]{:S(2)}, u32[]{:S(2)}) collective-permute-start(f32[64,128]{1,0:T(8,128)S(1)} %shard_map.64.refs_1_.refs_0_), channel_id=1, source_target_pairs={{0,1},{1,0},{2,3},{3,2},{4,5},{5,4},{6,7},{7,6},{8,9},{9,8},{10,11... | collective-permute-start | bytes 98312 | tf_op jit(solution)/shard_map/ppermute | solution.py:349
  20.6 4.0 %collective-permute-start.4 = (f32[64,128]{1,0:T(8,128)S(1)}, f32[64,128]{1,0:T(8,128)S(1)}, u32[]{:S(2)}, u32[]{:S(2)}) collective-permute-start(f32[64,128]{1,0:T(8,128)S(1)} %shard_map.67.refs_2_), channel_id=1, source_target_pairs={{0,2},{1,3},{2,0},{3,1},{4,6},{5,7},{6,4},{7,5},{8,10},{9,11},{10,... | collective-permute-start | bytes 98312 | tf_op jit(solution)/shard_map/ppermute | solution.py:352
  24.8 15.5 %collective-permute-start.5 = (f32[32,1536]{1,0:T(8,128)S(1)}, f32[32,1536]{1,0:T(8,128)S(1)}, u32[]{:S(2)}, u32[]{:S(2)}) collective-permute-start(f32[32,1536]{1,0:T(8,128)S(1)} %get-tuple-element.108.refs_6_.refs_1_), channel_id=1, source_target_pairs={{0,4},{4,8},{8,12},{12,0},{1,5},{5,9},{9,13},{13,1},{2,6},{6,10},{... | collective-permute-start | bytes 589832 | tf_op jit(solution)/shard_map/ppermute | solution.py:346
  27.6 12.7 %collective-permute-start.6 = (f32[32,1536]{1,0:T(8,128)S(1)}, f32[32,1536]{1,0:T(8,128)S(1)}, u32[]{:S(2)}, u32[]{:S(2)}) collective-permute-start(f32[32,1536]{1,0:T(8,128)S(1)} %get-tuple-element.108.refs_6_.refs_1_), channel_id=1, source_target_pairs={{0,12},{4,0},{8,4},{12,8},{1,13},{5,1},{9,5},{13,9},{2,14},{6,2},{... | collective-permute-start | bytes 589832 | tf_op jit(solution)/shard_map/ppermute | solution.py:346
  40.3 10.3 %collective-permute-start.8 = (f32[32,1536]{1,0:T(8,128)S(1)}, f32[32,1536]{1,0:T(8,128)S(1)}, u32[]{:S(2)}, u32[]{:S(2)}) collective-permute-start(f32[32,1536]{1,0:T(8,128)S(1)} %collective-permute-done.5.refs_2_), channel_id=1, source_target_pairs={{0,4},{4,8},{8,12},{12,0},{1,5},{5,9},{9,13},{13,1},{2,6},{6,10},{... | collective-permute-start | bytes 589832 | tf_op jit(solution)/shard_map/ppermute | solution.py:346
  42.3 17.9 %collective-permute-start.10 = (f32[32,4096]{1,0:T(8,128)S(1)}, f32[32,4096]{1,0:T(8,128)S(1)}, u32[]{:S(2)}, u32[]{:S(2)}) collective-permute-start(f32[32,4096]{1,0:T(8,128)S(1)} %add.59.refs_6_), channel_id=1, source_target_pairs={{0,2},{1,3},{2,0},{3,1},{4,6},{5,7},{6,4},{7,5},{8,10},{9,11},{10,... | collective-permute-start | bytes 1572872 | tf_op jit(solution)/shard_map/ppermute | solution.py:352
  57.9 3.0 %collective-permute-start.13 = (f32[32,4096]{1,0:T(8,128)S(1)}, f32[32,4096]{1,0:T(8,128)S(1)}, u32[]{:S(2)}, u32[]{:S(2)}) collective-permute-start(f32[32,4096]{1,0:T(8,128)S(1)} %get-tuple-element.122), channel_id=1, source_target_pairs={{0,1},{1,0},{2,3},{3,2},{4,5},{5,4},{6,7},{7,6},{8,9},{9,8},{10,11... | collective-permute-start | bytes 1572872 | tf_op jit(solution)/shard_map/ppermute | solution.py:349
  57.9 2.3 %collective-permute-start.9 = (f32[32,2048]{1,0:T(8,128)S(1)}, f32[32,2048]{1,0:T(8,128)S(1)}, u32[]{:S(2)}, u32[]{:S(2)}) collective-permute-start(f32[32,2048]{1,0:T(8,128)S(1)} %get-tuple-element.107), channel_id=1, source_target_pairs={{0,1},{1,0},{2,3},{3,2},{4,5},{5,4},{6,7},{7,6},{8,9},{9,8},{10,11... | collective-permute-start | bytes 786440 | tf_op jit(solution)/shard_map/ppermute | solution.py:349
  60.2 9.2 %collective-permute-start.11 = (f32[32,2048]{1,0:T(8,128)S(1)}, f32[32,2048]{1,0:T(8,128)S(1)}, u32[]{:S(2)}, u32[]{:S(2)}) collective-permute-start(f32[32,2048]{1,0:T(8,128)S(1)} %add.60.refs_1_), channel_id=1, source_target_pairs={{0,2},{1,3},{2,0},{3,1},{4,6},{5,7},{6,4},{7,5},{8,10},{9,11},{10,... | collective-permute-start | bytes 786440 | tf_op jit(solution)/shard_map/ppermute | solution.py:352
  60.9 19.0 %collective-permute-start.15 = (f32[32,4096]{1,0:T(8,128)S(1)}, f32[32,4096]{1,0:T(8,128)S(1)}, u32[]{:S(2)}, u32[]{:S(2)}) collective-permute-start(f32[32,4096]{1,0:T(8,128)S(1)} %add.61.refs_0_.refs_9_), channel_id=1, source_target_pairs={{0,2},{1,3},{2,0},{3,1},{4,6},{5,7},{6,4},{7,5},{8,10},{9,11},{10,... | collective-permute-start | bytes 1572872 | tf_op jit(solution)/shard_map/ppermute | solution.py:352
  62.5 17.5 %collective-permute-start.21 = (f32[32,4096]{1,0:T(8,128)S(1)}, f32[32,4096]{1,0:T(8,128)S(1)}, u32[]{:S(2)}, u32[]{:S(2)}) collective-permute-start(f32[32,4096]{1,0:T(8,128)S(1)} %get-tuple-element.121), channel_id=1, source_target_pairs={{0,1},{1,0},{2,3},{3,2},{4,5},{5,4},{6,7},{7,6},{8,9},{9,8},{10,11... | collective-permute-start | bytes 1572872 | tf_op jit(solution)/shard_map/ppermute | solution.py:349
  62.5 17.5 %collective-permute-start.20 = (f32[32,4096]{1,0:T(8,128)S(1)}, f32[32,4096]{1,0:T(8,128)S(1)}, u32[]{:S(2)}, u32[]{:S(2)}) collective-permute-start(f32[32,4096]{1,0:T(8,128)S(1)} %get-tuple-element.139), channel_id=1, source_target_pairs={{0,1},{1,0},{2,3},{3,2},{4,5},{5,4},{6,7},{7,6},{8,9},{9,8},{10,11... | collective-permute-start | bytes 1572872 | tf_op jit(solution)/shard_map/ppermute | solution.py:349
  80.5 7.8 %collective-permute-start.22 = (f32[32,2048]{1,0:T(8,128)S(1)}, f32[32,2048]{1,0:T(8,128)S(1)}, u32[]{:S(2)}, u32[]{:S(2)}) collective-permute-start(f32[32,2048]{1,0:T(8,128)S(1)} %get-tuple-element.144.refs_1_.refs_9_), channel_id=1, source_target_pairs={{0,2},{1,3},{2,0},{3,1},{4,6},{5,7},{6,4},{7,5},{8,10},{9,11},{10,... | collective-permute-start | bytes 786440 | tf_op jit(solution)/shard_map/ppermute | solution.py:352
  81.0 8.3 %collective-permute-start.23 = (f32[32,2048]{1,0:T(8,128)S(1)}, f32[32,2048]{1,0:T(8,128)S(1)}, u32[]{:S(2)}, u32[]{:S(2)}) collective-permute-start(f32[32,2048]{1,0:T(8,128)S(1)} %get-tuple-element.144.refs_1_.refs_9_), channel_id=1, source_target_pairs={{0,1},{1,0},{2,3},{3,2},{4,5},{5,4},{6,7},{7,6},{8,9},{9,8},{10,11... | collective-permute-start | bytes 786440 | tf_op jit(solution)/shard_map/ppermute | solution.py:349
  82.6 6.2 %collective-permute-start.19 = (f32[1,6144]{1,0:T(1,128)S(1)}, f32[1,6144]{1,0:T(1,128)S(1)}, u32[]{:S(2)}, u32[]{:S(2)}) collective-permute-start(f32[1,6144]{1,0:T(1,128)S(1)} %add.63), channel_id=1, source_target_pairs={{0,2},{1,3},{2,0},{3,1},{4,6},{5,7},{6,4},{7,5},{8,10},{9,11},{10,... | collective-permute-start | bytes 73736 | tf_op jit(solution)/shard_map/ppermute | solution.py:352
  88.3 2.6 %collective-permute-start.24 = (f32[32,2048]{1,0:T(8,128)S(1)}, f32[32,2048]{1,0:T(8,128)S(1)}, u32[]{:S(2)}, u32[]{:S(2)}) collective-permute-start(f32[32,2048]{1,0:T(8,128)S(1)} %collective-permute-done.22.refs_2_), channel_id=1, source_target_pairs={{0,1},{1,0},{2,3},{3,2},{4,5},{5,4},{6,7},{7,6},{8,9},{9,8},{10,11... | collective-permute-start | bytes 786440 | tf_op jit(solution)/shard_map/ppermute | solution.py:349
  88.3 7.9 %collective-permute-start.12 = (f32[32,2048]{1,0:T(8,128)S(1)}, f32[32,2048]{1,0:T(8,128)S(1)}, u32[]{:S(2)}, u32[]{:S(2)}) collective-permute-start(f32[32,2048]{1,0:T(8,128)S(1)} %get-tuple-element.124), channel_id=1, source_target_pairs={{0,1},{1,0},{2,3},{3,2},{4,5},{5,4},{6,7},{7,6},{8,9},{9,8},{10,11... | collective-permute-start | bytes 786440 | tf_op jit(solution)/shard_map/ppermute | solution.py:349
  88.8 7.4 %collective-permute-start.17 = (f32[32,2048]{1,0:T(8,128)S(1)}, f32[32,2048]{1,0:T(8,128)S(1)}, u32[]{:S(2)}, u32[]{:S(2)}) collective-permute-start(f32[32,2048]{1,0:T(8,128)S(1)} %get-tuple-element.133), channel_id=1, source_target_pairs={{0,1},{1,0},{2,3},{3,2},{4,5},{5,4},{6,7},{7,6},{8,9},{9,8},{10,11... | collective-permute-start | bytes 786440 | tf_op jit(solution)/shard_map/ppermute | solution.py:349
  88.8 9.1 %collective-permute-start.16 = (f32[32,2048]{1,0:T(8,128)S(1)}, f32[32,2048]{1,0:T(8,128)S(1)}, u32[]{:S(2)}, u32[]{:S(2)}) collective-permute-start(f32[32,2048]{1,0:T(8,128)S(1)} %add.62), channel_id=1, source_target_pairs={{0,2},{1,3},{2,0},{3,1},{4,6},{5,7},{6,4},{7,5},{8,10},{9,11},{10,... | collective-permute-start | bytes 786440 | tf_op jit(solution)/shard_map/ppermute | solution.py:352
  89.3 14.2 %collective-permute-start.26 = (f32[32,2048]{1,0:T(8,128)S(1)}, f32[32,2048]{1,0:T(8,128)S(1)}, u32[]{:S(2)}, u32[]{:S(2)}) collective-permute-start(f32[32,2048]{1,0:T(8,128)S(1)} %get-tuple-element.145.refs_10_.refs_1_), channel_id=1, source_target_pairs={{0,2},{1,3},{2,0},{3,1},{4,6},{5,7},{6,4},{7,5},{8,10},{9,11},{10,... | collective-permute-start | bytes 786440 | tf_op jit(solution)/shard_map/ppermute | solution.py:352
  98.8 11.5 %collective-permute-start.25 = (f32[32,2176]{1,0:T(8,128)S(1)}, f32[32,2176]{1,0:T(8,128)S(1)}, u32[]{:S(2)}, u32[]{:S(2)}) collective-permute-start(f32[32,2176]{1,0:T(8,128)S(1)} %get-tuple-element.147.refs_13_.refs_1_), channel_id=1, source_target_pairs={{0,2},{1,3},{2,0},{3,1},{4,6},{5,7},{6,4},{7,5},{8,10},{9,11},{10,... | collective-permute-start | bytes 835592 | tf_op jit(solution)/shard_map/ppermute | solution.py:352
  99.4 4.6 %collective-permute-start.27 = (f32[32,2048]{1,0:T(8,128)S(1)}, f32[32,2048]{1,0:T(8,128)S(1)}, u32[]{:S(2)}, u32[]{:S(2)}) collective-permute-start(f32[32,2048]{1,0:T(8,128)S(1)} %get-tuple-element.145.refs_10_.refs_1_), channel_id=1, source_target_pairs={{0,1},{1,0},{2,3},{3,2},{4,5},{5,4},{6,7},{7,6},{8,9},{9,8},{10,11... | collective-permute-start | bytes 786440 | tf_op jit(solution)/shard_map/ppermute | solution.py:349
  103.5 7.1 %collective-permute-start.29 = (f32[32,2176]{1,0:T(8,128)S(1)}, f32[32,2176]{1,0:T(8,128)S(1)}, u32[]{:S(2)}, u32[]{:S(2)}) collective-permute-start(f32[32,2176]{1,0:T(8,128)S(1)} %get-tuple-element.147.refs_13_.refs_1_), channel_id=1, source_target_pairs={{0,1},{1,0},{2,3},{3,2},{4,5},{5,4},{6,7},{7,6},{8,9},{9,8},{10,11... | collective-permute-start | bytes 835592 | tf_op jit(solution)/shard_map/ppermute | solution.py:349
  115.1 10.4 %collective-permute-start.31 = (f32[32,896]{1,0:T(8,128)S(1)}, f32[32,896]{1,0:T(8,128)S(1)}, u32[]{:S(2)}, u32[]{:S(2)}) collective-permute-start(f32[32,896]{1,0:T(8,128)S(1)} %get-tuple-element.161), channel_id=1, source_target_pairs={{0,12},{4,0},{8,4},{12,8},{1,13},{5,1},{9,5},{13,9},{2,14},{6,2},{... | collective-permute-start | bytes 344072 | tf_op jit(solution)/shard_map/ppermute | solution.py:346
  117.3 15.2 %collective-permute-start.32 = (f32[32,896]{1,0:T(8,128)S(1)}, f32[32,896]{1,0:T(8,128)S(1)}, u32[]{:S(2)}, u32[]{:S(2)}) collective-permute-start(f32[32,896]{1,0:T(8,128)S(1)} %get-tuple-element.162), channel_id=1, source_target_pairs={{0,8},{4,12},{8,0},{12,4},{1,9},{5,13},{9,1},{13,5},{2,10},{6,14},... | collective-permute-start | bytes 344072 | tf_op jit(solution)/shard_map/ppermute | solution.py:346
  117.5 15.0 %collective-permute-start.33 = (f32[32,896]{1,0:T(8,128)S(1)}, f32[32,896]{1,0:T(8,128)S(1)}, u32[]{:S(2)}, u32[]{:S(2)}) collective-permute-start(f32[32,896]{1,0:T(8,128)S(1)} %get-tuple-element.163), channel_id=1, source_target_pairs={{0,4},{4,8},{8,12},{12,0},{1,5},{5,9},{9,13},{13,1},{2,6},{6,10},{... | collective-permute-start | bytes 344072 | tf_op jit(solution)/shard_map/ppermute | solution.py:346
  121.1 11.6 %collective-permute-start.34 = (f32[32,768]{1,0:T(8,128)S(1)}, f32[32,768]{1,0:T(8,128)S(1)}, u32[]{:S(2)}, u32[]{:S(2)}) collective-permute-start(f32[32,768]{1,0:T(8,128)S(1)} %get-tuple-element.168), channel_id=1, source_target_pairs={{0,12},{4,0},{8,4},{12,8},{1,13},{5,1},{9,5},{13,9},{2,14},{6,2},{... | collective-permute-start | bytes 294920 | tf_op jit(solution)/shard_map/ppermute | solution.py:346
  124.5 12.0 %collective-permute-start.35 = (f32[32,768]{1,0:T(8,128)S(1)}, f32[32,768]{1,0:T(8,128)S(1)}, u32[]{:S(2)}, u32[]{:S(2)}) collective-permute-start(f32[32,768]{1,0:T(8,128)S(1)} %get-tuple-element.169), channel_id=1, source_target_pairs={{0,8},{4,12},{8,0},{12,4},{1,9},{5,13},{9,1},{13,5},{2,10},{6,14},... | collective-permute-start | bytes 294920 | tf_op jit(solution)/shard_map/ppermute | solution.py:346
  125.4 11.0 %collective-permute-start.36 = (f32[32,768]{1,0:T(8,128)S(1)}, f32[32,768]{1,0:T(8,128)S(1)}, u32[]{:S(2)}, u32[]{:S(2)}) collective-permute-start(f32[32,768]{1,0:T(8,128)S(1)} %get-tuple-element.170), channel_id=1, source_target_pairs={{0,4},{4,8},{8,12},{12,0},{1,5},{5,9},{9,13},{13,1},{2,6},{6,10},{... | collective-permute-start | bytes 294920 | tf_op jit(solution)/shard_map/ppermute | solution.py:346
  (10 other events, 27.1 us)

commit v21 on v18

--- a/solution.py
+++ b/solution.py
@@ -298,17 +298,16 @@
             out_ref[:, pl.ds(pl.multiple_of(step * width, width), width)] = rows
 
 
-def backward(acts, weights, place, earlier, part, parts, after):
+def backward(acts, weights, place, earlier, first, depth, after):
     slots, block, hidden = len(acts), acts[0].shape[0], sum(w.shape[1] for w in weights[::2])
-    riding = acts[0].shape[1] - hidden if part == 0 else 0
-    depth = weights[0].shape[0] // parts
+    riding = acts[0].shape[1] - hidden if first == 0 else 0
     width = divisor(depth, 256, 128)
     out = jax.ShapeDtypeStruct((block, depth + riding), jnp.float32)
     inside, anywhere = pl.BlockSpec(memory_space=pltpu.VMEM), pl.BlockSpec(memory_space=pl.ANY)
     ends = [1 + slots, 1 + slots + len(weights), 1 + slots + len(weights) + len(earlier)]
     return pl.pallas_call(
         lambda *refs: backward_kernel(
-            part * depth,
+            first,
             depth,
             refs[0],
             refs[1 : ends[0]],
@@ -450,19 +449,19 @@
     pre_0 = tied(pre_0, half_1[0])[0]
     act_0, act_1, sums_0 = slope_product(slice(0, 2 * third), back_0, pre_0, (), ())
     pre_1 = exchanged(half_1)
-    sums = backward(both_cores(spread_out(act_0)), in_parts[:4], place, (), 0, 1, [])
+    sums = backward(both_cores(spread_out(act_0)), in_parts[:4], place, (), 0, depth, [])
     act_2, _ = slope_product(slice(2 * third, hidden), back_1, pre_1, (sums_0,), (sums[0],))
     acts_0, acts_1 = spread_out(act_1), spread_out(act_2)
-    sums = backward(both_cores(acts_0), in_parts[4:8], place, sums, 0, 1, [act_2])
+    sums = backward(both_cores(acts_0), in_parts[4:8], place, sums, 0, depth, [act_2])
     acts_1[1:], sums = tied(acts_1[1:], sums)
     acts_1 = both_cores(acts_1)
-    parts = 2 if depth % 512 == 0 else 1
+    width = depth // 3 if depth % 768 == 0 else depth
     ends = []
-    for part in range(parts):
-        ends.append(backward(acts_1, in_parts[8:], place, sums, part, parts, [ends[-1][0]] if ends else []))
+    for start, extent in ((0, width), (width, depth - width))[: 1 if width == depth else 2]:
+        after = [ends[-1][0]] if ends else []
+        ends.append(backward(acts_1, in_parts[8:], place, sums, start, extent, after))
     first = summed_along_hid(ends[0])
     others = [summed_along_hid(end, first) for end in ends[1:]]
-    width = depth // parts
     normed_grad = jnp.concatenate([first[:, :width], *others], axis=1) * norm_gain
     mean, slope = first[:, width : width + 1] / model_width, first[:, width + 1 : width + 2] / model_width
     return inv_std * (normed_grad - mean - normed * slope)

time: 137 us -> 138 us (level)
  no operation moved by 1% of the time
where the time goes in v21:
time: 138 us; the launch traced here: 137 us
  Pallas kernels  65.1 us (47%)
  waiting for transfers between devices  37.9 us (27%)
  starting transfers between devices  30.7 us (22%)
  local copies, waits for them, and re-layouts  2.03 us (1%)
    ppermute x9, waiting for transfers between devices, next_chip(): lax.ppermute(values, 'emb', [(i, (i + 2) % emb_size) for i in range(emb_s...  20.5 us
    ppermute x12, starting transfers between devices, along_hid(): lax.ppermute(values, 'hid', [(i, (i + steps) % hid_size) for i in range(h...  19 us
    pallas_call x2, Pallas kernels, stream(): pl.pallas_call(lambda *refs: stream_kernel(first, depth, refs[0], refs[1:...  18.3 us
    pallas_call x3, Pallas kernels, prepare(): pl.pallas_call(lambda weight_ref, gain_ref, *refs: prepare_kernel(rows, c...  17.2 us
    pallas_call x4, Pallas kernels, backward(): pl.pallas_call(lambda *refs: backward_kernel(first, depth, refs[0], refs[...  16.7 us
    ppermute x12, waiting for transfers between devices, along_hid(): lax.ppermute(values, 'hid', [(i, (i + steps) % hid_size) for i in range(h...  11.7 us
    pallas_call x2, Pallas kernels, forward(): pl.pallas_call(lambda *refs: forward_kernel(refs[0], refs[1:ends[0]], ref...  11.2 us
    ppermute x9, starting transfers between devices, next_chip(): lax.ppermute(values, 'emb', [(i, (i + 2) % emb_size) for i in range(emb_s...  8.66 us
  transfers between devices with their start and end apart: 37, of which 14 were waited for; matrix products, arithmetic and copies ran while one was open for 1% of the time, Pallas kernels for 45%

profile of v21, /device:TPU:0, one launch (start us, length us, event | category | flops | bytes accessed | tf_op | source)
XLA Modules:
  0.0 137.5 jit_solution(18011493212088342644)
XLA Ops:
  0.0 3.0 %collective-permute-start.1 = (f32[32,1536]{1,0:T(8,128)}, f32[32,1536]{1,0:T(8,128)S(1)}, u32[]{:S(2)}, u32[]{:S(2)}) collective-permute-start(f32[32,1536]{1,0:T(8,128)} %refs_1_.3), channel_id=1, source_target_pairs={{0,4},{4,8},{8,12},{12,0},{1,5},{5,9},{9,13},{13,1},{2,6},{6,10},{... | collective-permute-start | bytes 589832 | tf_op jit(solution)/shard_map/ppermute | solution.py:341
  3.0 2.6 %collective-permute-start.2 = (f32[32,1536]{1,0:T(8,128)}, f32[32,1536]{1,0:T(8,128)S(1)}, u32[]{:S(2)}, u32[]{:S(2)}) collective-permute-start(f32[32,1536]{1,0:T(8,128)} %refs_1_.3), channel_id=1, source_target_pairs={{0,8},{4,12},{8,0},{12,4},{1,9},{5,13},{9,1},{13,5},{2,10},{6,14},... | collective-permute-start | bytes 589832 | tf_op jit(solution)/shard_map/ppermute | solution.py:341
  5.6 1.3 collective-permute-start.3
  9.1 5.7 %shard_map.65 = (bf16[1536,1024]{1,0:T(8,128)(2,1)S(1)}, bf16[1536,1024]{1,0:T(8,128)(2,1)S(1)}, bf16[1536,1024]{1,0:T(8,128)(2,1)S(1)}, bf16[1536,1024]{1,0:T(8,128)(2,1)S(1)}, f32[1,2048]{1,0:T(1,128)S(1)}) custom-call(f32[1536,6144]{1,0:T(8,128)} %weight_ref.5, f32[1536,1]{1,0:T(8,128)S(1)} %broadcast_in_dim.19.gain_ref, s32[4]{0:T(128)S(1)} %fusion.5.refs_0_, ...), custom_call_target="tpu_custom_call" | custom-call | flops 1048576 | bytes 262144 | tf_op jit(solution)/shard_map/pallas_call | solution.py:135
  14.8 5.7 %shard_map.66 = (bf16[1536,1024]{1,0:T(8,128)(2,1)S(1)}, bf16[1536,1024]{1,0:T(8,128)(2,1)S(1)}, bf16[1536,1024]{1,0:T(8,128)(2,1)S(1)}, bf16[1536,1024]{1,0:T(8,128)(2,1)S(1)}, f32[1,2048]{1,0:T(1,128)S(1)}) custom-call(f32[1536,6144]{1,0:T(8,128)} %weight_ref.5, f32[1536,1]{1,0:T(8,128)S(1)} %broadcast_in_dim.19.gain_ref, ...), custom_call_target="tpu_custom_call" | custom-call | flops 1048576 | bytes 262144 | tf_op jit(solution)/shard_map/pallas_call | solution.py:135
  20.6 1.6 %collective-permute-start.4 = (f32[64,128]{1,0:T(8,128)S(1)}, f32[64,128]{1,0:T(8,128)S(1)}, u32[]{:S(2)}, u32[]{:S(2)}) collective-permute-start(f32[64,128]{1,0:T(8,128)S(1)} %shard_map.67.refs_2_), channel_id=1, source_target_pairs={{0,2},{1,3},{2,0},{3,1},{4,6},{5,7},{6,4},{7,5},{8,10},{9,11},{10,... | collective-permute-start | bytes 98312 | tf_op jit(solution)/shard_map/ppermute | solution.py:347
  22.2 2.4 %collective-permute-done.4.refs_3_ = f32[64,128]{1,0:T(8,128)S(1)} collective-permute-done((f32[64,128]{1,0:T(8,128)S(1)}, f32[64,128]{1,0:T(8,128)S(1)}, u32[]{:S(2)}, u32[]{:S(2)}) %collective-permute-start.4) | collective-permute-done | bytes 32800 | tf_op jit(solution)/shard_map/ppermute | solution.py:347
  24.8 2.8 %collective-permute-start.5 = (f32[32,1536]{1,0:T(8,128)S(1)}, f32[32,1536]{1,0:T(8,128)S(1)}, u32[]{:S(2)}, u32[]{:S(2)}) collective-permute-start(f32[32,1536]{1,0:T(8,128)S(1)} %get-tuple-element.108.refs_6_.refs_1_), channel_id=1, source_target_pairs={{0,4},{4,8},{8,12},{12,0},{1,5},{5,9},{9,13},{13,1},{2,6},{6,10},{... | collective-permute-start | bytes 589832 | tf_op jit(solution)/shard_map/ppermute | solution.py:341
  27.6 1.1 collective-permute-start.6
  28.7 11.5 %shard_map.69 = (f32[32,4096]{1,0:T(8,128)S(1)}, f32[32,4096]{1,0:T(8,128)S(1)}, f32[32,4096]{1,0:T(8,128)S(1)}, f32[32,4096]{1,0:T(8,128)S(1)}) custom-call(s32[4]{0:T(128)S(1)} %fusion.5.refs_0_, f32[32,1536]{1,0:T(8,128)S(1)} %copy-done.2, f32[32,1536]{1,0:T(8,128)S(1)} %collective-permute-done.1.refs_3_.refs_2_, ...), custom_call_target="tpu_custom_call" | custom-call | flops 1048576 | bytes 262144 | tf_op jit(solution)/shard_map/pallas_call | solution.py:254
  40.3 1.9 %collective-permute-done.7 = f32[32,4096]{1,0:T(8,128)S(1)} collective-permute-done((f32[32,4096]{1,0:T(8,128)S(1)}, f32[32,4096]{1,0:T(8,128)S(1)}, u32[]{:S(2)}, u32[]{:S(2)}) %collective-permute-start.7) | collective-permute-done | bytes 524320 | tf_op jit(solution)/shard_map/ppermute | solution.py:344
  42.3 1.6 %collective-permute-start.10 = (f32[32,4096]{1,0:T(8,128)S(1)}, f32[32,4096]{1,0:T(8,128)S(1)}, u32[]{:S(2)}, u32[]{:S(2)}) collective-permute-start(f32[32,4096]{1,0:T(8,128)S(1)} %add.59.refs_6_), channel_id=1, source_target_pairs={{0,2},{1,3},{2,0},{3,1},{4,6},{5,7},{6,4},{7,5},{8,10},{9,11},{10,... | collective-permute-start | bytes 1572872 | tf_op jit(solution)/shard_map/ppermute | solution.py:347
  44.7 6.8 %shard_map.70 = (f32[32,2048]{1,0:T(8,128)S(1)}, f32[32,2048]{1,0:T(8,128)S(1)}, f32[32,2048]{1,0:T(8,128)S(1)}, f32[32,2048]{1,0:T(8,128)S(1)}) custom-call(s32[4]{0:T(128)S(1)} %fusion.5.refs_0_, f32[32,1536]{1,0:T(8,128)S(1)} %copy-done.2, f32[32,1536]{1,0:T(8,128)S(1)} %collective-permute-done.1.refs_3_.refs_2_, ...), custom_call_target="tpu_custom_call" | custom-call | flops 1048576 | bytes 262144 | tf_op jit(solution)/shard_map/pallas_call | solution.py:254
  52.3 7.2 %shard_map.71 = (f32[32,4096]{1,0:T(8,128)S(1)}, f32[32,4096]{1,0:T(8,128)S(1)}, f32[32,4096]{1,0:T(8,128)S(1)}, f32[32,4096]{1,0:T(8,128)S(1)}) custom-call(s32[4]{0:T(128)S(1)} %fusion.5.refs_0_, f32[32,1536]{1,0:T(8,128)S(1)} %get-tuple-element.108.refs_6_.refs_1_, f32[32,1536]{1,0:T(8,128)S(1)} %collective-permute-done.5.refs_2_, ...), custom_call_target="tpu_custom_call" | custom-call | flops 1048576 | bytes 262144 | tf_op jit(solution)/shard_map/pallas_call | solution.py:212
  61.7 1.2 collective-permute-start.15
  62.9 5.7 %shard_map.72 = (bf16[1536,1024]{1,0:T(8,128)(2,1)S(1)}, bf16[1536,1024]{1,0:T(8,128)(2,1)S(1)}, bf16[1536,1024]{1,0:T(8,128)(2,1)S(1)}, bf16[1536,1024]{1,0:T(8,128)(2,1)S(1)}, f32[1,2048]{1,0:T(1,128)S(1)}) custom-call(f32[1536,6144]{1,0:T(8,128)} %weight_ref.5, f32[1536,1]{1,0:T(8,128)S(1)} %broadcast_in_dim.19.gain_ref, ...), custom_call_target="tpu_custom_call" | custom-call | flops 1048576 | bytes 262144 | tf_op jit(solution)/shard_map/pallas_call | solution.py:135
  69.4 3.9 %shard_map.73 = (f32[32,2048]{1,0:T(8,128)S(1)}, f32[32,2048]{1,0:T(8,128)S(1)}, f32[32,2048]{1,0:T(8,128)S(1)}, f32[32,2048]{1,0:T(8,128)S(1)}) custom-call(s32[4]{0:T(128)S(1)} %fusion.5.refs_0_, f32[32,1536]{1,0:T(8,128)S(1)} %get-tuple-element.108.refs_6_.refs_1_, f32[32,1536]{1,0:T(8,128)S(1)} %collective-permute-done.5.refs_2_, ...), custom_call_target="tpu_custom_call" | custom-call | flops 1048576 | bytes 262144 | tf_op jit(solution)/shard_map/pallas_call | solution.py:212
  75.6 4.6 %collective-permute-done.19 = f32[1,6144]{1,0:T(1,128)S(1)} collective-permute-done((f32[1,6144]{1,0:T(1,128)S(1)}, f32[1,6144]{1,0:T(1,128)S(1)}, u32[]{:S(2)}, u32[]{:S(2)}) %collective-permute-start.19) | collective-permute-done | bytes 24608 | tf_op jit(solution)/shard_map/ppermute | solution.py:347
  81.5 6.8 %collective-permute-done.22.refs_2_ = f32[32,2048]{1,0:T(8,128)S(1)} collective-permute-done((f32[32,2048]{1,0:T(8,128)S(1)}, f32[32,2048]{1,0:T(8,128)S(1)}, u32[]{:S(2)}, u32[]{:S(2)}) %collective-permute-start.22) | collective-permute-done | bytes 262176 | tf_op jit(solution)/shard_map/ppermute | solution.py:347
  89.4 1.5 %collective-permute-start.26 = (f32[32,2048]{1,0:T(8,128)S(1)}, f32[32,2048]{1,0:T(8,128)S(1)}, u32[]{:S(2)}, u32[]{:S(2)}) collective-permute-start(f32[32,2048]{1,0:T(8,128)S(1)} %get-tuple-element.147.refs_1_), channel_id=1, source_target_pairs={{0,2},{1,3},{2,0},{3,1},{4,6},{5,7},{6,4},{7,5},{8,10},{9,11},{10,... | collective-permute-start | bytes 786440 | tf_op jit(solution)/shard_map/ppermute | solution.py:347
  90.9 5.3 %shard_map.75 = (f32[32,1536]{1,0:T(8,128)S(1)}, f32[32,1536]{1,0:T(8,128)S(1)}, f32[32,1536]{1,0:T(8,128)S(1)}, f32[32,1536]{1,0:T(8,128)S(1)}) custom-call(s32[4]{0:T(128)S(1)} %fusion.5.refs_0_, f32[32,2048]{1,0:T(8,128)S(1)} %get-tuple-element.144.refs_1_, f32[32,2048]{1,0:T(8,128)S(1)} %collective-permute-done.22.refs_2_, ...), custom_call_target="tpu_custom_call" | custom-call | flops 1048576 | bytes 262144 | tf_op jit(solution)/shard_map/pallas_call | solution.py:308
  96.2 1.7 %collective-permute-done.16.refs_3_ = f32[32,2048]{1,0:T(8,128)S(1)} collective-permute-done((f32[32,2048]{1,0:T(8,128)S(1)}, f32[32,2048]{1,0:T(8,128)S(1)}, u32[]{:S(2)}, u32[]{:S(2)}) %collective-permute-start.16) | collective-permute-done | bytes 262176 | tf_op jit(solution)/shard_map/ppermute | solution.py:347
  99.4 4.2 %collective-permute-done.26.refs_2_ = f32[32,2048]{1,0:T(8,128)S(1)} collective-permute-done((f32[32,2048]{1,0:T(8,128)S(1)}, f32[32,2048]{1,0:T(8,128)S(1)}, u32[]{:S(2)}, u32[]{:S(2)}) %collective-permute-start.26) | collective-permute-done | bytes 262176 | tf_op jit(solution)/shard_map/ppermute | solution.py:347
  105.1 5.3 %shard_map.77 = (f32[32,1536]{1,0:T(8,128)S(1)}, f32[32,1536]{1,0:T(8,128)S(1)}, f32[32,1536]{1,0:T(8,128)S(1)}, f32[32,1536]{1,0:T(8,128)S(1)}) custom-call(s32[4]{0:T(128)S(1)} %fusion.5.refs_0_, f32[32,2048]{1,0:T(8,128)S(1)} %get-tuple-element.147.refs_1_, f32[32,2048]{1,0:T(8,128)S(1)} %collective-permute-done.26.refs_2_, ...), custom_call_target="tpu_custom_call" | custom-call | flops 1048576 | bytes 262144 | tf_op jit(solution)/shard_map/pallas_call | solution.py:308
  110.6 1.4 %collective-permute-done.30.refs_4_ = f32[32,2176]{1,0:T(8,128)S(1)} collective-permute-done((f32[32,2176]{1,0:T(8,128)S(1)}, f32[32,2176]{1,0:T(8,128)S(1)}, u32[]{:S(2)}, u32[]{:S(2)}) %collective-permute-start.30) | collective-permute-done | bytes 278560 | tf_op jit(solution)/shard_map/ppermute | solution.py:344
  112.0 2.3 %shard_map.78 = (f32[32,640]{1,0:T(8,128)S(1)}, f32[32,640]{1,0:T(8,128)S(1)}, f32[32,640]{1,0:T(8,128)S(1)}, f32[32,640]{1,0:T(8,128)S(1)}) custom-call(s32[4]{0:T(128)S(1)} %fusion.5.refs_0_, f32[32,2176]{1,0:T(8,128)S(1)} %get-tuple-element.146.refs_13_.refs_1_, f32[32,2176]{1,0:T(8,128)S(1)} %collective-permute-done.25.refs_2_, ...), custom_call_target="tpu_custom_call" | custom-call | flops 1048576 | bytes 262144 | tf_op jit(solution)/shard_map/pallas_call | solution.py:308
  114.4 2.3 %collective-permute-start.31 = (f32[32,640]{1,0:T(8,128)S(1)}, f32[32,640]{1,0:T(8,128)S(1)}, u32[]{:S(2)}, u32[]{:S(2)}) collective-permute-start(f32[32,640]{1,0:T(8,128)S(1)} %get-tuple-element.161), channel_id=1, source_target_pairs={{0,12},{4,0},{8,4},{12,8},{1,13},{5,1},{9,5},{13,9},{2,14},{6,2},{... | collective-permute-start | bytes 245768 | tf_op jit(solution)/shard_map/ppermute | solution.py:341
  117.5 3.8 %shard_map.79 = (f32[32,1024]{1,0:T(8,128)S(1)}, f32[32,1024]{1,0:T(8,128)S(1)}, f32[32,1024]{1,0:T(8,128)S(1)}, f32[32,1024]{1,0:T(8,128)S(1)}) custom-call(s32[4]{0:T(128)S(1)} %fusion.5.refs_0_, f32[32,2176]{1,0:T(8,128)S(1)} %get-tuple-element.146.refs_13_.refs_1_, f32[32,2176]{1,0:T(8,128)S(1)} %collective-permute-done.25.refs_2_, ...), custom_call_target="tpu_custom_call" | custom-call | flops 1048576 | bytes 262144 | tf_op jit(solution)/shard_map/pallas_call | solution.py:308
  121.3 3.1 %collective-permute-start.34 = (f32[32,1024]{1,0:T(8,128)S(1)}, f32[32,1024]{1,0:T(8,128)S(1)}, u32[]{:S(2)}, u32[]{:S(2)}) collective-permute-start(f32[32,1024]{1,0:T(8,128)S(1)} %get-tuple-element.168), channel_id=1, source_target_pairs={{0,12},{4,0},{8,4},{12,8},{1,13},{5,1},{9,5},{13,9},{2,14},{6,2},{... | collective-permute-start | bytes 393224 | tf_op jit(solution)/shard_map/ppermute | solution.py:341
  124.4 1.1 collective-permute-start.35
  125.8 2.6 %collective-permute-done.34 = f32[32,1024]{1,0:T(8,128)S(1)} collective-permute-done((f32[32,1024]{1,0:T(8,128)S(1)}, f32[32,1024]{1,0:T(8,128)S(1)}, u32[]{:S(2)}, u32[]{:S(2)}) %collective-permute-start.34) | collective-permute-done | bytes 131104 | tf_op jit(solution)/shard_map/ppermute | solution.py:341
  128.3 8.3 %collective-permute-done.35 = f32[32,1024]{1,0:T(8,128)S(1)} collective-permute-done((f32[32,1024]{1,0:T(8,128)S(1)}, f32[32,1024]{1,0:T(8,128)S(1)}, u32[]{:S(2)}, u32[]{:S(2)}) %collective-permute-start.35) | collective-permute-done | bytes 131104 | tf_op jit(solution)/shard_map/ppermute | solution.py:341
  (88 shorter events, 16.6 us)
Async XLA Ops:
  0.0 20.6 %collective-permute-start.1 = (f32[32,1536]{1,0:T(8,128)}, f32[32,1536]{1,0:T(8,128)S(1)}, u32[]{:S(2)}, u32[]{:S(2)}) collective-permute-start(f32[32,1536]{1,0:T(8,128)} %refs_1_.3), channel_id=1, source_target_pairs={{0,4},{4,8},{8,12},{12,0},{1,5},{5,9},{9,13},{13,1},{2,6},{6,10},{... | collective-permute-start | bytes 589832 | tf_op jit(solution)/shard_map/ppermute | solution.py:341
  3.0 17.6 %collective-permute-start.2 = (f32[32,1536]{1,0:T(8,128)}, f32[32,1536]{1,0:T(8,128)S(1)}, u32[]{:S(2)}, u32[]{:S(2)}) collective-permute-start(f32[32,1536]{1,0:T(8,128)} %refs_1_.3), channel_id=1, source_target_pairs={{0,8},{4,12},{8,0},{12,4},{1,9},{5,13},{9,1},{13,5},{2,10},{6,14},... | collective-permute-start | bytes 589832 | tf_op jit(solution)/shard_map/ppermute | solution.py:341
  5.6 15.0 %collective-permute-start.3 = (f32[32,1536]{1,0:T(8,128)}, f32[32,1536]{1,0:T(8,128)S(1)}, u32[]{:S(2)}, u32[]{:S(2)}) collective-permute-start(f32[32,1536]{1,0:T(8,128)} %refs_1_.3), channel_id=1, source_target_pairs={{0,12},{4,0},{8,4},{12,8},{1,13},{5,1},{9,5},{13,9},{2,14},{6,2},{... | collective-permute-start | bytes 589832 | tf_op jit(solution)/shard_map/ppermute | solution.py:341
  8.1 12.5 %collective-permute-start = (f32[64,128]{1,0:T(8,128)S(1)}, f32[64,128]{1,0:T(8,128)S(1)}, u32[]{:S(2)}, u32[]{:S(2)}) collective-permute-start(f32[64,128]{1,0:T(8,128)S(1)} %shard_map.64.refs_1_.refs_0_), channel_id=1, source_target_pairs={{0,1},{1,0},{2,3},{3,2},{4,5},{5,4},{6,7},{7,6},{8,9},{9,8},{10,11... | collective-permute-start | bytes 98312 | tf_op jit(solution)/shard_map/ppermute | solution.py:344
  20.6 4.0 %collective-permute-start.4 = (f32[64,128]{1,0:T(8,128)S(1)}, f32[64,128]{1,0:T(8,128)S(1)}, u32[]{:S(2)}, u32[]{:S(2)}) collective-permute-start(f32[64,128]{1,0:T(8,128)S(1)} %shard_map.67.refs_2_), channel_id=1, source_target_pairs={{0,2},{1,3},{2,0},{3,1},{4,6},{5,7},{6,4},{7,5},{8,10},{9,11},{10,... | collective-permute-start | bytes 98312 | tf_op jit(solution)/shard_map/ppermute | solution.py:347
  24.8 15.5 %collective-permute-start.5 = (f32[32,1536]{1,0:T(8,128)S(1)}, f32[32,1536]{1,0:T(8,128)S(1)}, u32[]{:S(2)}, u32[]{:S(2)}) collective-permute-start(f32[32,1536]{1,0:T(8,128)S(1)} %get-tuple-element.108.refs_6_.refs_1_), channel_id=1, source_target_pairs={{0,4},{4,8},{8,12},{12,0},{1,5},{5,9},{9,13},{13,1},{2,6},{6,10},{... | collective-permute-start | bytes 589832 | tf_op jit(solution)/shard_map/ppermute | solution.py:341
  27.6 12.7 %collective-permute-start.6 = (f32[32,1536]{1,0:T(8,128)S(1)}, f32[32,1536]{1,0:T(8,128)S(1)}, u32[]{:S(2)}, u32[]{:S(2)}) collective-permute-start(f32[32,1536]{1,0:T(8,128)S(1)} %get-tuple-element.108.refs_6_.refs_1_), channel_id=1, source_target_pairs={{0,12},{4,0},{8,4},{12,8},{1,13},{5,1},{9,5},{13,9},{2,14},{6,2},{... | collective-permute-start | bytes 589832 | tf_op jit(solution)/shard_map/ppermute | solution.py:341
  42.3 17.8 %collective-permute-start.10 = (f32[32,4096]{1,0:T(8,128)S(1)}, f32[32,4096]{1,0:T(8,128)S(1)}, u32[]{:S(2)}, u32[]{:S(2)}) collective-permute-start(f32[32,4096]{1,0:T(8,128)S(1)} %add.59.refs_6_), channel_id=1, source_target_pairs={{0,2},{1,3},{2,0},{3,1},{4,6},{5,7},{6,4},{7,5},{8,10},{9,11},{10,... | collective-permute-start | bytes 1572872 | tf_op jit(solution)/shard_map/ppermute | solution.py:347
  43.8 8.5 %collective-permute-start.8 = (f32[32,1536]{1,0:T(8,128)S(1)}, f32[32,1536]{1,0:T(8,128)S(1)}, u32[]{:S(2)}, u32[]{:S(2)}) collective-permute-start(f32[32,1536]{1,0:T(8,128)S(1)} %collective-permute-done.5.refs_2_), channel_id=1, source_target_pairs={{0,4},{4,8},{8,12},{12,0},{1,5},{5,9},{9,13},{13,1},{2,6},{6,10},{... | collective-permute-start | bytes 589832 | tf_op jit(solution)/shard_map/ppermute | solution.py:341
  52.3 7.8 %collective-permute-start.9 = (f32[32,2048]{1,0:T(8,128)S(1)}, f32[32,2048]{1,0:T(8,128)S(1)}, u32[]{:S(2)}, u32[]{:S(2)}) collective-permute-start(f32[32,2048]{1,0:T(8,128)S(1)} %get-tuple-element.107), channel_id=1, source_target_pairs={{0,1},{1,0},{2,3},{3,2},{4,5},{5,4},{6,7},{7,6},{8,9},{9,8},{10,11... | collective-permute-start | bytes 786440 | tf_op jit(solution)/shard_map/ppermute | solution.py:344
  60.1 9.2 %collective-permute-start.11 = (f32[32,2048]{1,0:T(8,128)S(1)}, f32[32,2048]{1,0:T(8,128)S(1)}, u32[]{:S(2)}, u32[]{:S(2)}) collective-permute-start(f32[32,2048]{1,0:T(8,128)S(1)} %add.60.refs_1_), channel_id=1, source_target_pairs={{0,2},{1,3},{2,0},{3,1},{4,6},{5,7},{6,4},{7,5},{8,10},{9,11},{10,... | collective-permute-start | bytes 786440 | tf_op jit(solution)/shard_map/ppermute | solution.py:347
  60.8 19.6 %collective-permute-start.20 = (f32[32,4096]{1,0:T(8,128)S(1)}, f32[32,4096]{1,0:T(8,128)S(1)}, u32[]{:S(2)}, u32[]{:S(2)}) collective-permute-start(f32[32,4096]{1,0:T(8,128)S(1)} %get-tuple-element.139), channel_id=1, source_target_pairs={{0,1},{1,0},{2,3},{3,2},{4,5},{5,4},{6,7},{7,6},{8,9},{9,8},{10,11... | collective-permute-start | bytes 1572872 | tf_op jit(solution)/shard_map/ppermute | solution.py:344
  60.8 19.6 %collective-permute-start.21 = (f32[32,4096]{1,0:T(8,128)S(1)}, f32[32,4096]{1,0:T(8,128)S(1)}, u32[]{:S(2)}, u32[]{:S(2)}) collective-permute-start(f32[32,4096]{1,0:T(8,128)S(1)} %get-tuple-element.121), channel_id=1, source_target_pairs={{0,1},{1,0},{2,3},{3,2},{4,5},{5,4},{6,7},{7,6},{8,9},{9,8},{10,11... | collective-permute-start | bytes 1572872 | tf_op jit(solution)/shard_map/ppermute | solution.py:344
  61.7 18.6 %collective-permute-start.15 = (f32[32,4096]{1,0:T(8,128)S(1)}, f32[32,4096]{1,0:T(8,128)S(1)}, u32[]{:S(2)}, u32[]{:S(2)}) collective-permute-start(f32[32,4096]{1,0:T(8,128)S(1)} %add.61.refs_0_.refs_9_), channel_id=1, source_target_pairs={{0,2},{1,3},{2,0},{3,1},{4,6},{5,7},{6,4},{7,5},{8,10},{9,11},{10,... | collective-permute-start | bytes 1572872 | tf_op jit(solution)/shard_map/ppermute | solution.py:347
  73.3 6.9 %collective-permute-start.14 = (f32[32,2048]{1,0:T(8,128)S(1)}, f32[32,2048]{1,0:T(8,128)S(1)}, u32[]{:S(2)}, u32[]{:S(2)}) collective-permute-start(f32[32,2048]{1,0:T(8,128)S(1)} %get-tuple-element.130), channel_id=1, source_target_pairs={{0,1},{1,0},{2,3},{3,2},{4,5},{5,4},{6,7},{7,6},{8,9},{9,8},{10,11... | collective-permute-start | bytes 786440 | tf_op jit(solution)/shard_map/ppermute | solution.py:344
  75.0 5.2 %collective-permute-start.19 = (f32[1,6144]{1,0:T(1,128)S(1)}, f32[1,6144]{1,0:T(1,128)S(1)}, u32[]{:S(2)}, u32[]{:S(2)}) collective-permute-start(f32[1,6144]{1,0:T(1,128)S(1)} %add.63), channel_id=1, source_target_pairs={{0,2},{1,3},{2,0},{3,1},{4,6},{5,7},{6,4},{7,5},{8,10},{9,11},{10,... | collective-permute-start | bytes 73736 | tf_op jit(solution)/shard_map/ppermute | solution.py:347
  80.9 7.4 %collective-permute-start.22 = (f32[32,2048]{1,0:T(8,128)S(1)}, f32[32,2048]{1,0:T(8,128)S(1)}, u32[]{:S(2)}, u32[]{:S(2)}) collective-permute-start(f32[32,2048]{1,0:T(8,128)S(1)} %get-tuple-element.144.refs_1_), channel_id=1, source_target_pairs={{0,2},{1,3},{2,0},{3,1},{4,6},{5,7},{6,4},{7,5},{8,10},{9,11},{10,... | collective-permute-start | bytes 786440 | tf_op jit(solution)/shard_map/ppermute | solution.py:347
  81.5 7.9 %collective-permute-start.23 = (f32[32,2048]{1,0:T(8,128)S(1)}, f32[32,2048]{1,0:T(8,128)S(1)}, u32[]{:S(2)}, u32[]{:S(2)}) collective-permute-start(f32[32,2048]{1,0:T(8,128)S(1)} %get-tuple-element.144.refs_1_), channel_id=1, source_target_pairs={{0,1},{1,0},{2,3},{3,2},{4,5},{5,4},{6,7},{7,6},{8,9},{9,8},{10,11... | collective-permute-start | bytes 786440 | tf_op jit(solution)/shard_map/ppermute | solution.py:344
  88.3 2.6 %collective-permute-start.24 = (f32[32,2048]{1,0:T(8,128)S(1)}, f32[32,2048]{1,0:T(8,128)S(1)}, u32[]{:S(2)}, u32[]{:S(2)}) collective-permute-start(f32[32,2048]{1,0:T(8,128)S(1)} %collective-permute-done.22.refs_2_), channel_id=1, source_target_pairs={{0,1},{1,0},{2,3},{3,2},{4,5},{5,4},{6,7},{7,6},{8,9},{9,8},{10,11... | collective-permute-start | bytes 786440 | tf_op jit(solution)/shard_map/ppermute | solution.py:344
  88.3 7.9 %collective-permute-start.12 = (f32[32,2048]{1,0:T(8,128)S(1)}, f32[32,2048]{1,0:T(8,128)S(1)}, u32[]{:S(2)}, u32[]{:S(2)}) collective-permute-start(f32[32,2048]{1,0:T(8,128)S(1)} %get-tuple-element.124), channel_id=1, source_target_pairs={{0,1},{1,0},{2,3},{3,2},{4,5},{5,4},{6,7},{7,6},{8,9},{9,8},{10,11... | collective-permute-start | bytes 786440 | tf_op jit(solution)/shard_map/ppermute | solution.py:344
  88.8 7.4 %collective-permute-start.17 = (f32[32,2048]{1,0:T(8,128)S(1)}, f32[32,2048]{1,0:T(8,128)S(1)}, u32[]{:S(2)}, u32[]{:S(2)}) collective-permute-start(f32[32,2048]{1,0:T(8,128)S(1)} %get-tuple-element.133), channel_id=1, source_target_pairs={{0,1},{1,0},{2,3},{3,2},{4,5},{5,4},{6,7},{7,6},{8,9},{9,8},{10,11... | collective-permute-start | bytes 786440 | tf_op jit(solution)/shard_map/ppermute | solution.py:344
  88.8 9.1 %collective-permute-start.16 = (f32[32,2048]{1,0:T(8,128)S(1)}, f32[32,2048]{1,0:T(8,128)S(1)}, u32[]{:S(2)}, u32[]{:S(2)}) collective-permute-start(f32[32,2048]{1,0:T(8,128)S(1)} %add.62), channel_id=1, source_target_pairs={{0,2},{1,3},{2,0},{3,1},{4,6},{5,7},{6,4},{7,5},{8,10},{9,11},{10,... | collective-permute-start | bytes 786440 | tf_op jit(solution)/shard_map/ppermute | solution.py:347
  89.4 14.2 %collective-permute-start.26 = (f32[32,2048]{1,0:T(8,128)S(1)}, f32[32,2048]{1,0:T(8,128)S(1)}, u32[]{:S(2)}, u32[]{:S(2)}) collective-permute-start(f32[32,2048]{1,0:T(8,128)S(1)} %get-tuple-element.147.refs_1_), channel_id=1, source_target_pairs={{0,2},{1,3},{2,0},{3,1},{4,6},{5,7},{6,4},{7,5},{8,10},{9,11},{10,... | collective-permute-start | bytes 786440 | tf_op jit(solution)/shard_map/ppermute | solution.py:347
  98.9 11.6 %collective-permute-start.25 = (f32[32,2176]{1,0:T(8,128)S(1)}, f32[32,2176]{1,0:T(8,128)S(1)}, u32[]{:S(2)}, u32[]{:S(2)}) collective-permute-start(f32[32,2176]{1,0:T(8,128)S(1)} %get-tuple-element.146.refs_13_.refs_1_), channel_id=1, source_target_pairs={{0,2},{1,3},{2,0},{3,1},{4,6},{5,7},{6,4},{7,5},{8,10},{9,11},{10,... | collective-permute-start | bytes 835592 | tf_op jit(solution)/shard_map/ppermute | solution.py:347
  99.4 4.7 %collective-permute-start.27 = (f32[32,2048]{1,0:T(8,128)S(1)}, f32[32,2048]{1,0:T(8,128)S(1)}, u32[]{:S(2)}, u32[]{:S(2)}) collective-permute-start(f32[32,2048]{1,0:T(8,128)S(1)} %get-tuple-element.147.refs_1_), channel_id=1, source_target_pairs={{0,1},{1,0},{2,3},{3,2},{4,5},{5,4},{6,7},{7,6},{8,9},{9,8},{10,11... | collective-permute-start | bytes 786440 | tf_op jit(solution)/shard_map/ppermute | solution.py:344
  103.6 7.1 %collective-permute-start.29 = (f32[32,2176]{1,0:T(8,128)S(1)}, f32[32,2176]{1,0:T(8,128)S(1)}, u32[]{:S(2)}, u32[]{:S(2)}) collective-permute-start(f32[32,2176]{1,0:T(8,128)S(1)} %get-tuple-element.146.refs_13_.refs_1_), channel_id=1, source_target_pairs={{0,1},{1,0},{2,3},{3,2},{4,5},{5,4},{6,7},{7,6},{8,9},{9,8},{10,11... | collective-permute-start | bytes 835592 | tf_op jit(solution)/shard_map/ppermute | solution.py:344
  114.4 11.2 %collective-permute-start.31 = (f32[32,640]{1,0:T(8,128)S(1)}, f32[32,640]{1,0:T(8,128)S(1)}, u32[]{:S(2)}, u32[]{:S(2)}) collective-permute-start(f32[32,640]{1,0:T(8,128)S(1)} %get-tuple-element.161), channel_id=1, source_target_pairs={{0,12},{4,0},{8,4},{12,8},{1,13},{5,1},{9,5},{13,9},{2,14},{6,2},{... | collective-permute-start | bytes 245768 | tf_op jit(solution)/shard_map/ppermute | solution.py:341
  116.6 8.9 %collective-permute-start.32 = (f32[32,640]{1,0:T(8,128)S(1)}, f32[32,640]{1,0:T(8,128)S(1)}, u32[]{:S(2)}, u32[]{:S(2)}) collective-permute-start(f32[32,640]{1,0:T(8,128)S(1)} %get-tuple-element.162), channel_id=1, source_target_pairs={{0,8},{4,12},{8,0},{12,4},{1,9},{5,13},{9,1},{13,5},{2,10},{6,14},... | collective-permute-start | bytes 245768 | tf_op jit(solution)/shard_map/ppermute | solution.py:341
  116.6 8.9 %collective-permute-start.33 = (f32[32,640]{1,0:T(8,128)S(1)}, f32[32,640]{1,0:T(8,128)S(1)}, u32[]{:S(2)}, u32[]{:S(2)}) collective-permute-start(f32[32,640]{1,0:T(8,128)S(1)} %get-tuple-element.163), channel_id=1, source_target_pairs={{0,4},{4,8},{8,12},{12,0},{1,5},{5,9},{9,13},{13,1},{2,6},{6,10},{... | collective-permute-start | bytes 245768 | tf_op jit(solution)/shard_map/ppermute | solution.py:341
  121.3 7.1 %collective-permute-start.34 = (f32[32,1024]{1,0:T(8,128)S(1)}, f32[32,1024]{1,0:T(8,128)S(1)}, u32[]{:S(2)}, u32[]{:S(2)}) collective-permute-start(f32[32,1024]{1,0:T(8,128)S(1)} %get-tuple-element.168), channel_id=1, source_target_pairs={{0,12},{4,0},{8,4},{12,8},{1,13},{5,1},{9,5},{13,9},{2,14},{6,2},{... | collective-permute-start | bytes 393224 | tf_op jit(solution)/shard_map/ppermute | solution.py:341
  124.4 12.2 %collective-permute-start.35 = (f32[32,1024]{1,0:T(8,128)S(1)}, f32[32,1024]{1,0:T(8,128)S(1)}, u32[]{:S(2)}, u32[]{:S(2)}) collective-permute-start(f32[32,1024]{1,0:T(8,128)S(1)} %get-tuple-element.169), channel_id=1, source_target_pairs={{0,8},{4,12},{8,0},{12,4},{1,9},{5,13},{9,1},{13,5},{2,10},{6,14},... | collective-permute-start | bytes 393224 | tf_op jit(solution)/shard_map/ppermute | solution.py:341
  125.5 11.1 %collective-permute-start.36 = (f32[32,1024]{1,0:T(8,128)S(1)}, f32[32,1024]{1,0:T(8,128)S(1)}, u32[]{:S(2)}, u32[]{:S(2)}) collective-permute-start(f32[32,1024]{1,0:T(8,128)S(1)} %get-tuple-element.170), channel_id=1, source_target_pairs={{0,4},{4,8},{8,12},{12,0},{1,5},{5,9},{9,13},{13,1},{2,6},{6,10},{... | collective-permute-start | bytes 393224 | tf_op jit(solution)/shard_map/ppermute | solution.py:341
  (10 other events, 29.7 us)
